TPU v7x, 32 devices: a whole 2x2x4 slice. The times are simulated.
32 devices in a mesh: head: 4 (over z), seg: 8 (over y, x, core).
Axes of the slice: x: 2, y: 2, z: 4, core: 2. Of those that a mesh axis runs over, the one named last changes fastest.
Arguments:
- queries: bfloat16 [8, 256, 8192], P('seg', None, 'head'), may hold values from -6 to 6
- key_rows: bfloat16 [8, 256, 8192], P('seg', None, 'head'), may hold values from -6 to 6
- values: bfloat16 [8, 256, 8192], P('seg', None, 'head'), may hold values from -36 to 36
- cotangent: bfloat16 [8, 256, 8192], P('seg', None, 'head'), may hold values from -8 to 8
- out_gain: float32 [8192], P('head'), may hold values from 0.1 to 1.9
- parent: int32 [8], replicated, may hold values from -1 to 7, as said below
- seg_len: int32 [8], P('seg'), may hold values from 64 to 256, as said below
Outputs:
- attended: bfloat16 [8, 256, 8192], P('seg', None, 'head')
- query_grad: bfloat16 [8, 256, 8192], P('seg', None, 'head')
- key_grad: bfloat16 [8, 256, 8192], P('seg', None, 'head')
- value_grad: bfloat16 [8, 256, 8192], P('seg', None, 'head')
Inputs may be any that keep to these rules, and one draw needn't show every extreme that they name: Three levels: a parent is a root or the child of a root; no segment is its own ancestor. `seg_len`: at most 256 live tokens a segment; some segment is full in every draw.
All inputs are finite; a program needn't handle non-finite values.
Results may differ from a plain program's by a relative error of at most 0.013.
Values may be sent and summed in bfloat16 or wider, within the bound.
No kernel may reach another device: no remote copies, remote signals or barrier semaphores. Data moves between devices by JAX's collectives and lax.ppermute only.
A program may use at most 64 MiB of HBM per device.

v0:
```python
import math

import jax
import jax.numpy as jnp
from jax import lax
from jax.sharding import PartitionSpec as P

HEADS = 64
HD = 128


EPSILON = 1e-06


def ancestry_weights(parent, my_index):
    holders = jnp.arange(parent.shape[0], dtype=jnp.int32)
    matches = parent[:, None] == holders[None, :]
    grandparent = jnp.where(
        parent >= 0, jnp.sum(jnp.where(matches, parent[None, :], 0), axis=1), -1
    )
    my_parent = jnp.sum(jnp.where(holders == my_index, parent, 0))
    my_grand = jnp.sum(jnp.where(holders == my_index, grandparent, 0))
    upward = ((holders == my_parent) | (holders == my_grand)).astype(jnp.bfloat16)
    downward = ((parent == my_index) | (grandparent == my_index)).astype(jnp.bfloat16)
    return (upward, downward)


def per_device(queries, key_rows, values, cotangent, out_gain, parent, seg_len):
    seg_rows = queries.shape[1]
    local_heads = queries.shape[2] // HD
    head_shape = (seg_rows, local_heads, HD)
    width = HEADS * HD
    query_seg = queries[0].reshape(head_shape)
    key_seg = key_rows[0].reshape(head_shape)
    value_seg = values[0].reshape(head_shape)
    my_index = lax.axis_index("seg")
    upward, downward = ancestry_weights(parent, my_index)
    length = seg_len[0]
    positions = jnp.arange(seg_rows, dtype=jnp.int32)
    live_rows = positions < length
    live_mask = live_rows.astype(jnp.float32)[:, None, None]
    score_scale = 1.0 / math.sqrt(HD * seg_rows)
    masked_keys = key_seg * live_rows.astype(jnp.bfloat16)[:, None, None]
    own_state = jnp.einsum(
        "thd,the->hde", masked_keys, value_seg, preferred_element_type=jnp.float32
    ).astype(jnp.bfloat16)
    weights = upward
    prefix = jnp.einsum(
        "j,jhde->hde",
        weights,
        lax.all_gather(own_state[None], "seg", axis=0, tiled=True),
        preferred_element_type=jnp.float32,
    ).astype(jnp.bfloat16)
    keep = (positions[None, :] <= positions[:, None]) & (positions[None, :] < length)
    raw_scores = jnp.einsum("thd,uhd->htu", query_seg, key_seg, preferred_element_type=jnp.float32)
    scores = jnp.where(keep[None], raw_scores, 0.0).astype(jnp.bfloat16)
    carried = jnp.einsum("thd,hde->the", query_seg, prefix, preferred_element_type=jnp.float32)
    local_part = jnp.einsum("htu,uhe->the", scores, value_seg, preferred_element_type=jnp.float32)
    attention_out = score_scale * (carried + local_part) * live_mask
    gain = out_gain.reshape(local_heads, HD)
    gain_grad = cotangent[0].reshape(head_shape).astype(jnp.float32) * gain
    square_part = jnp.sum(attention_out * attention_out, axis=(1, 2))
    dot_part = jnp.sum(attention_out * gain_grad, axis=(1, 2))
    total_square, total_dot = lax.psum((square_part, dot_part), "head")
    inverse_rms = lax.rsqrt(total_square / width + EPSILON)[:, None, None]
    normed_dot = inverse_rms * total_dot[:, None, None]
    attended = (attention_out * inverse_rms * gain).astype(jnp.bfloat16)
    grad_out = (
        live_mask * inverse_rms * (gain_grad - attention_out * inverse_rms * normed_dot / width)
    ).astype(jnp.bfloat16)
    state_grad = (
        score_scale
        * jnp.einsum("thd,the->hde", query_seg, grad_out, preferred_element_type=jnp.float32)
    ).astype(jnp.bfloat16)
    upward_float = upward.astype(jnp.float32)
    state_float = state_grad.astype(jnp.float32)
    weights = upward_float
    below = lax.psum_scatter(
        (weights[:, None, None, None] * state_float[None]).astype(jnp.bfloat16),
        "seg",
        scatter_dimension=0,
        tiled=True,
    ).astype(jnp.float32)[0]
    below = below.astype(jnp.bfloat16)
    grad_raw = jnp.einsum("the,uhe->htu", grad_out, value_seg, preferred_element_type=jnp.float32)
    grad_scores = jnp.where(keep[None], grad_raw, 0.0).astype(jnp.bfloat16)
    query_part = score_scale * (
        jnp.einsum("the,hde->thd", grad_out, prefix, preferred_element_type=jnp.float32)
        + jnp.einsum("htu,uhd->thd", grad_scores, key_seg, preferred_element_type=jnp.float32)
    )
    key_part = score_scale * jnp.einsum(
        "htu,thd->uhd", grad_scores, query_seg, preferred_element_type=jnp.float32
    ) + live_mask * jnp.einsum("uhe,hde->uhd", value_seg, below, preferred_element_type=jnp.float32)
    value_part = score_scale * jnp.einsum(
        "htu,the->uhe", scores, grad_out, preferred_element_type=jnp.float32
    ) + live_mask * jnp.einsum("uhd,hde->uhe", key_seg, below, preferred_element_type=jnp.float32)
    flat_shape = (1, seg_rows, local_heads * HD)
    return (
        attended.reshape(flat_shape),
        query_part.astype(jnp.bfloat16).reshape(flat_shape),
        key_part.astype(jnp.bfloat16).reshape(flat_shape),
        value_part.astype(jnp.bfloat16).reshape(flat_shape),
    )


def solution(mesh):
    placed = (
        P("seg", None, "head"),
        P("seg", None, "head"),
        P("seg", None, "head"),
        P("seg", None, "head"),
        P("head"),
        P(),
        P("seg"),
    )
    return jax.shard_map(
        per_device,
        mesh=mesh,
        in_specs=placed,
        out_specs=(
            P("seg", None, "head"),
            P("seg", None, "head"),
            P("seg", None, "head"),
            P("seg", None, "head"),
        ),
        check_vma=False,
    )
```

profile of v0, /device:TPU:0, one launch (start us, length us, event | category | flops | bytes accessed | tf_op | source)
XLA Modules:
  0.0 146.0 jit_solution(14720933102258140987)
XLA Ops:
  7.2 0.0 all-gather.3.cloned.1.call-start
  7.9 0.0 copy-start.18
  7.9 1.5 %copy.81 = bf16[32,8,16,128]{3,2,1,0:T(8,128)(2,1)S(1)} copy(bf16[32,8,16,128]{3,1,2,0:T(8,128)(2,1)} %bitcast.87) | data formatting | bytes 2097152
  9.4 0.0 copy-start.6
  9.4 0.8 copy.53
  10.2 0.0 copy-start.15
  10.2 0.0 copy-done.18
  10.3 0.2 copy.82
  10.5 0.0 copy-done.6
  10.5 0.0 copy-start.3
  10.5 1.0 copy-done.3
  11.6 1.3 convolution_convert_fusion
  12.8 0.0 copy-done.15
  12.8 0.0 all-gather.3.cloned.1.call-update
  12.8 0.0 reduce-scatter.2.cloned.1.call-start
  12.9 0.0 copy-done.19
  12.9 0.2 copy.83
  13.1 0.0 copy-start
  13.2 0.0 copy-start.21
  13.2 1.9 %copy.60 = f32[1,256,2048]{1,2,0:T(8,128)S(1)} copy(bf16[1,256,2048]{2,1,0:T(8,128)(2,1)} %param.10) | data formatting | bytes 3145728 | tf_op jit(solution)/shard_map/convert_element_type | solution.py:61
  15.0 0.0 copy-done.21
  15.1 0.2 select_reduce_fusion
  15.2 0.7 fusion.29
  16.0 1.2 convert_convert_fusion
  17.2 0.0 copy-start.4
  17.3 2.1 %select_convert_fusion.1 = bf16[16,256,256]{2,1,0:T(8,128)(2,1)S(1)} fusion(pred[256,256]{1,0:T(8,128)(4,1)S(1)} %fusion.27, bf16[256,16,128]{2,1,0:T(8,128)(2,1)} %bitcast.78, bf16[256,16,128]{2,1,0:T(8,128)(2,1)S(1)} %bitcast.69), kind=kOutput, calls=%fused_computation.4 | convolution fusion | flops 270532608 | bytes 4259840 | tf_op jit(solution)/shard_map/thd,uhd->htu/dot_general | solution.py:55
  19.3 0.0 copy-start.11
  19.4 1.3 copy-done.11
  20.7 0.0 copy-done.4
  20.7 2.2 %fusion.17 = f32[16,256,128]{1,2,0:T(8,128)} fusion(bf16[16,256,256]{2,1,0:T(8,128)(2,1)S(1)} %select_convert_fusion.1, bf16[256,16,128]{2,1,0:T(8,128)(2,1)S(1)} %bitcast.74), kind=kOutput, calls=%fused_computation.30 | convolution fusion | flops 268435456 | bytes 5242880 | tf_op jit(solution)/shard_map/htu,uhe->the/dot_general | solution.py:58
  22.8 29.6 %all-gather.3.cloned.1.call-done = bf16[128,128,128]{2,1,0:T(8,128)(2,1)} async-done(((bf16[16,128,128]{2,1,0:T(8,128)(2,1)}), bf16[128,128,128]{2,1,0:T(8,128)(2,1)}) %all-gather.3.cloned.1.call-update) | async-done | bytes 4194320 | tf_op jit(solution)/shard_map/all_gather | solution.py:51
  52.4 6.3 %fusion = f32[1,16,128,128]{3,0,2,1:T(1,128)S(1)} fusion(bf16[8,16,128,128]{3,2,1,0:T(8,128)(2,1)} %bitcast.86, s32[]{:T(128)} %get-tuple-element.19, s32[]{:T(128)} %get-tuple-element.18), kind=kOutput, calls=%fused_computation.1 | convolution fusion | flops 4194328 | bytes 5242888 | tf_op jit(solution)/shard_map/j,jhde->hde/dot_general | solution.py:48
  58.8 0.0 copy-done
  58.8 0.0 copy-done.14
  58.8 0.0 copy-done.20
  58.8 2.4 %multiply_reduce_fusion = (f32[256]{0:T(256)S(1)}, f32[256]{0:T(256)S(1)}, f32[256,16,128]{0,2,1:T(8,128)}) fusion(f32[256,16,128]{0,2,1:T(8,128)S(1)} %bitcast.67, f32[16,128]{1,0:T(8,128)S(1)} %bitcast.90, f32[256]{0:T(256)S(1)} %broadcast_select_fusion.1, f32[16,256,128]{1,2,0:T(8,128)S(1)} %copy-done.14, bf16[256,16,128]{2,1,0:T(8,128)(2,1)S(1)} %bitcast.70, ...), kind=kOutput, calls=%fused_computation.14 | convolution fusion | flops 138149376 | bytes 8399872 | tf_op jit(solution)/shard_map/thd,hde->the/dot_general | solution.py:57
  61.2 0.0 copy-done.8
  61.2 11.8 %all-reduce = (f32[256]{0:T(256)S(1)}, f32[256]{0:T(256)S(1)}) all-reduce(f32[256]{0:T(256)S(1)} %get-tuple-element.17, f32[256]{0:T(256)S(1)} %get-tuple-element.16), channel_id=1, replica_groups=mesh['head'=4,'seg'=8] {'head'}, use_global_device_ids=true, to_apply=%region_4.5 | all-reduce | flops 512 | bytes 4096 | tf_op jit(solution)/shard_map/psum | solution.py:64
  73.0 3.3 %multiply_convert_fusion.1 = (bf16[256,16,128]{0,2,1:T(8,128)(2,1)S(1)}, bf16[256,16,128]{0,2,1:T(8,128)(2,1)}) fusion(f32[256,16,128]{0,2,1:T(8,128)S(1)} %bitcast.68, f32[256,16,128]{0,2,1:T(8,128)} %get-tuple-element.27, f32[256]{0:T(256)S(1)} %get-tuple-element.25, f32[256]{0:T(256)S(1)} %get-tuple-element.24, f32[16,128]{1,0:T(8,128)S(1)} %bitcast.91, ...), kind=kLoop, calls=%fused_computation.13 | loop fusion | flops 4718592 | bytes 6302720 | tf_op jit(solution)/shard_map/convert_element_type | solution.py:70
  76.3 0.0 copy-done.1
  76.3 0.5 fusion.8
  76.8 3.1 %multiply_convert_fusion = bf16[8,16,128,128]{2,3,1,0:T(8,128)(2,1)} fusion(f32[16,128,128]{1,2,0:T(8,128)S(1)} %fusion.8, f32[8]{0:T(128)S(1)} %convert_convert_fusion), kind=kLoop, calls=%fused_computation | loop fusion | flops 4194304 | bytes 5242912 | tf_op jit(solution)/shard_map/convert_element_type | solution.py:79
  79.9 0.0 reduce-scatter.2.cloned.1.call-update
  79.9 1.2 copy-done.5
  81.1 0.8 select_convert_fusion
  81.9 0.4 copy-done.16
  82.3 0.8 fusion.34
  83.1 0.5 copy-done.12
  83.6 0.7 copy-done.9
  84.3 1.4 fusion.4
  85.7 2.4 %copy.71 = bf16[1,256,2048]{2,1,0:T(8,128)(2,1)} copy(bf16[1,256,2048]{1,2,0:T(8,128)(2,1)} %bitcast.84) | data formatting | bytes 2097152
  88.2 0.0 copy-done.17
  88.2 1.4 copy.70
  89.6 3.6 %fusion.35 = f32[16,128,256]{2,1,0:T(8,128)} fusion(bf16[256,16,128]{0,2,1:T(8,128)(2,1)S(1)} %get-tuple-element.22, bf16[16,256,256]{2,1,0:T(8,128)(2,1)} %copy-done.11), kind=kOutput, calls=%fused_computation.60 | convolution fusion | flops 268435456 | bytes 5242880 | tf_op jit(solution)/shard_map/htu,the->uhe/dot_general | solution.py:94
  93.2 0.0 copy-done.2
  93.2 0.0 copy-done.13
  93.2 1.9 %fusion.12 = f32[16,256,128]{1,2,0:T(8,128)} fusion(bf16[16,256,256]{2,1,0:T(8,128)(2,1)S(1)} %copy-done.13, bf16[256,16,128]{2,1,0:T(8,128)(2,1)S(1)} %bitcast.72), kind=kOutput, calls=%fused_computation.25 | convolution fusion | flops 268435456 | bytes 5242880 | tf_op jit(solution)/shard_map/htu,thd->uhd/dot_general | solution.py:91
  95.1 33.5 %reduce-scatter.2.cloned.1.call-done = bf16[1,16,128,128]{2,3,1,0:T(8,128)(2,1)} async-done(((bf16[8,16,128,128]{2,3,1,0:T(8,128)(2,1)}), bf16[1,16,128,128]{2,3,1,0:T(8,128)(2,1)}) %reduce-scatter.2.cloned.1.call-update) | async-done | bytes 524304 | tf_op jit(solution)/shard_map/reduce_scatter | solution.py:78
  128.6 0.0 copy-done.7
  128.6 3.3 %add_convert_fusion = bf16[16,128,256]{2,1,0:T(8,128)(2,1)} fusion(f32[16,128,256]{2,1,0:T(8,128)} %fusion.35, f32[256]{0:T(256)S(1)} %fusion.32, bf16[256,16,128]{2,1,0:T(8,128)(2,1)S(1)} %bitcast.79, bf16[1,16,128,128]{2,3,1,0:T(8,128)(2,1)} %reduce-scatter.2.cloned.1.call-done), kind=kOutput, calls=%fused_computation.12 | convolution fusion | flops 136314880 | bytes 4719616 | tf_op jit(solution)/shard_map/uhd,hde->uhe/dot_general | solution.py:96
  131.9 2.4 %copy.73 = bf16[1,256,2048]{2,1,0:T(8,128)(2,1)} copy(bf16[1,256,2048]{1,2,0:T(8,128)(2,1)} %bitcast.85) | data formatting | bytes 2097152
  134.3 0.0 copy-done.10
  134.3 2.6 %fusion.2 = bf16[256,16,128]{0,2,1:T(8,128)(2,1)} fusion(f32[16,256,128]{1,2,0:T(8,128)S(1)} %copy-done.10, f32[256]{0:T(256)S(1)} %fusion.32, bf16[256,16,128]{2,1,0:T(8,128)(2,1)S(1)} %bitcast.76, bf16[1,16,128,128]{2,3,1,0:T(8,128)(2,1)} %reduce-scatter.2.cloned.1.call-done), kind=kOutput, calls=%fused_computation.6 | convolution fusion | flops 136314880 | bytes 4719616 | tf_op jit(solution)/shard_map/uhe,hde->uhd/dot_general | solution.py:93
  136.9 2.3 %copy.72 = bf16[1,256,2048]{2,1,0:T(8,128)(2,1)} copy(bf16[1,256,2048]{1,2,0:T(8,128)(2,1)} %bitcast.83) | data formatting | bytes 2097152
  (20 shorter events, 0.1 us)
Async XLA Ops:
  7.2 45.3 %all-gather.3.cloned.1.call-start = ((), (), s32[]{:S(2)}) async-start(), calls=%async_computation.2 | async-start | bytes 4718592 | tf_op jit(solution)/shard_map/all_gather | solution.py:51
  7.9 2.4 %copy-start.18 = (bf16[1,256,2048]{2,1,0:T(8,128)(2,1)S(1)}, bf16[1,256,2048]{2,1,0:T(8,128)(2,1)}, u32[]{:S(2)}) copy-start(bf16[1,256,2048]{2,1,0:T(8,128)(2,1)} %param.9) | copy-start | bytes 3145732
  9.4 1.1 copy-start.6
  10.2 2.6 %copy-start.15 = (bf16[256,16,128]{0,2,1:T(8,128)(2,1)}, bf16[256,16,128]{0,2,1:T(8,128)(2,1)S(1)}, u32[]{:S(2)}) copy-start(bf16[256,16,128]{0,2,1:T(8,128)(2,1)S(1)} %copy.53) | copy-start | bytes 3145732
  10.5 1.0 copy-start.3
  11.6 1.3 copy-start.19
  12.8 115.8 %reduce-scatter.2.cloned.1.call-start = ((), (), s32[]{:S(2)}) async-start(), calls=%async_computation.1 | async-start | bytes 4718592 | tf_op jit(solution)/shard_map/reduce_scatter | solution.py:78
  13.1 45.6 %copy-start = (bf16[32,8,16,128]{3,2,1,0:T(8,128)(2,1)}, bf16[32,8,16,128]{3,2,1,0:T(8,128)(2,1)S(1)}, u32[]{:S(2)}) copy-start(bf16[32,8,16,128]{3,2,1,0:T(8,128)(2,1)S(1)} %copy.83) | copy-start | bytes 3145732
  13.2 1.9 %copy-start.21 = (s32[8]{0:T(128)S(1)}, s32[8]{0:T(128)}, u32[]{:S(2)}) copy-start(s32[8]{0:T(128)} %param.12) | copy-start | bytes 100
  17.2 3.4 %copy-start.4 = (bf16[32,8,16,128]{3,2,1,0:T(8,128)(2,1)S(1)}, bf16[32,8,16,128]{3,2,1,0:T(8,128)(2,1)}, u32[]{:S(2)}) copy-start(bf16[32,8,16,128]{3,2,1,0:T(8,128)(2,1)} %copy-done.3) | copy-start | bytes 3145732
  19.3 1.3 copy-start.11
  52.4 6.4 %copy-start.14 = (f32[16,256,128]{1,2,0:T(8,128)S(1)}, f32[16,256,128]{1,2,0:T(8,128)}, u32[]{:S(2)}) copy-start(f32[16,256,128]{1,2,0:T(8,128)} %fusion.17) | copy-start | bytes 6291460
  52.4 6.4 %copy-start.20 = (f32[2048]{0:T(1024)S(1)}, f32[2048]{0:T(1024)}, u32[]{:S(2)}) copy-start(f32[2048]{0:T(1024)} %param.11) | copy-start | bytes 24580
  58.8 2.4 %copy-start.8 = (f32[1,16,128,128]{3,0,2,1:T(1,128)}, f32[1,16,128,128]{3,0,2,1:T(1,128)S(1)}, u32[]{:S(2)}) copy-start(f32[1,16,128,128]{3,0,2,1:T(1,128)S(1)} %fusion) | copy-start | bytes 3145732
  73.0 3.3 %copy-start.1 = (bf16[32,8,16,128]{3,2,1,0:T(8,128)(2,1)S(1)}, bf16[32,8,16,128]{3,2,1,0:T(8,128)(2,1)}, u32[]{:S(2)}) copy-start(bf16[32,8,16,128]{3,2,1,0:T(8,128)(2,1)} %copy-done) | copy-start | bytes 3145732
  79.9 1.2 copy-start.5
  81.1 1.2 copy-start.16
  82.3 1.3 copy-start.12
  82.3 2.0 %copy-start.9 = (f32[1,16,128,128]{3,0,2,1:T(1,128)S(1)}, f32[1,16,128,128]{3,0,2,1:T(1,128)}, u32[]{:S(2)}) copy-start(f32[1,16,128,128]{3,0,2,1:T(1,128)} %copy-done.8) | copy-start | bytes 3145732
  85.7 2.4 %copy-start.17 = (bf16[256,16,128]{0,2,1:T(8,128)(2,1)S(1)}, bf16[256,16,128]{0,2,1:T(8,128)(2,1)}, u32[]{:S(2)}) copy-start(bf16[256,16,128]{0,2,1:T(8,128)(2,1)} %get-tuple-element.23) | copy-start | bytes 3145732
  89.6 3.7 %copy-start.2 = (bf16[32,8,16,128]{3,2,1,0:T(8,128)(2,1)S(1)}, bf16[32,8,16,128]{3,2,1,0:T(8,128)(2,1)}, u32[]{:S(2)}) copy-start(bf16[32,8,16,128]{3,2,1,0:T(8,128)(2,1)} %copy-done) | copy-start | bytes 3145732
  89.6 3.7 %copy-start.13 = (bf16[16,256,256]{2,1,0:T(8,128)(2,1)S(1)}, bf16[16,256,256]{2,1,0:T(8,128)(2,1)}, u32[]{:S(2)}) copy-start(bf16[16,256,256]{2,1,0:T(8,128)(2,1)} %copy-done.12) | copy-start | bytes 6291460
  93.2 35.4 %copy-start.7 = (bf16[32,8,16,128]{3,2,1,0:T(8,128)(2,1)S(1)}, bf16[32,8,16,128]{3,2,1,0:T(8,128)(2,1)}, u32[]{:S(2)}) copy-start(bf16[32,8,16,128]{3,2,1,0:T(8,128)(2,1)} %copy-done.6) | copy-start | bytes 3145732
  131.9 2.4 %copy-start.10 = (f32[16,256,128]{1,2,0:T(8,128)S(1)}, f32[16,256,128]{1,2,0:T(8,128)}, u32[]{:S(2)}) copy-start(f32[16,256,128]{1,2,0:T(8,128)} %fusion.12) | copy-start | bytes 6291460
Sparse Core Ops, SparseCore 0:
  13.0 39.4 all-gather.2
  80.0 48.5 reduce-scatter.1
where the time goes:
time: 147 us; the launch traced here: 146 us
  waiting for transfers between devices  63.1 us (43%)
  matrix products  29.2 us (20%)
  local copies, waits for them, and re-layouts  18.3 us (12%)
  between operations  14.9 us (10%)
  blocking collectives  11.8 us (8%)
  other arithmetic  8.54 us (6%)
    reduce_scatter x1, waiting for transfers between devices, per_device(): lax.psum_scatter((weights[:, None, None, None] * state_float[None]).astyp...  33.5 us
    all_gather x1, waiting for transfers between devices, per_device(): lax.all_gather(own_state[None], 'seg', axis=0, tiled=True)  29.6 us
    unnamed x51, local copies, waits for them, and re-layouts  15.7 us
    psum x1, blocking collectives, per_device(): total_square, total_dot = lax.psum((square_part, dot_part), 'head')  11.8 us
    dot_general x1, matrix products, per_device(): jnp.einsum('j,jhde->hde', weights, lax.all_gather(own_state[None], 'seg',...  6.33 us
    dot_general x1, matrix products, per_device(): jnp.einsum('htu,the->uhe', scores, grad_out, preferred_element_type=jnp.f...  3.65 us
    dot_general x1, matrix products, per_device(): jnp.einsum('uhd,hde->uhe', key_seg, below, preferred_element_type=jnp.flo...  3.28 us
    convert_element_type x1, other arithmetic, per_device(): grad_out = (live_mask * inverse_rms * (gain_grad - attention_out * invers...  3.25 us
  transfers between devices with their start and end apart: 2, of which 2 were waited for; matrix products, arithmetic and copies ran while one was open for 14% of the time, Pallas kernels for 0%

commit v1 on v0

v1 whole, which is shorter than its diff:
```python
import functools
import math

import jax
import jax.numpy as jnp
from jax import lax
from jax.experimental import pallas as pl
from jax.experimental.pallas import tpu as pltpu
from jax.sharding import PartitionSpec as P

HEADS = 64
HD = 128
EPSILON = 1e-06
F32 = jnp.float32
BF16 = jnp.bfloat16
VMEM_LIMIT = 24 * 1024 * 1024

VMEM = pl.BlockSpec(memory_space=pltpu.VMEM)
SMEM = pl.BlockSpec(memory_space=pltpu.SMEM)


def dot(a, b, contract):
    return lax.dot_general(a, b, (contract, ((), ())), preferred_element_type=F32)


def nn(a, b):
    return dot(a, b, ((1,), (0,)))


def nt(a, b):
    return dot(a, b, ((1,), (1,)))


def tn(a, b):
    return dot(a, b, ((0,), (0,)))


def head_cols(head):
    return slice(head * HD, (head + 1) * HD)


def split_rows(full, outs, me):
    parts = len(outs)
    rows = full.shape[0] // parts
    for step, out in enumerate(outs):
        place = lax.rem(me + step, parts)
        out[...] = full[pl.ds(pl.multiple_of(place * rows, rows), rows), :]


def join_rows(received, full, me):
    parts = len(received)
    rows = full.shape[0] // parts
    for step, block in enumerate(received):
        place = lax.rem(me + parts - step, parts)
        full[pl.ds(pl.multiple_of(place * rows, rows), rows), :] = block[...]


def state_kernel(heads, seg_len, keys, values, *rest):
    outs, full = rest[:-1], rest[-1]
    rows = keys.shape[0]
    live = lax.broadcasted_iota(jnp.int32, (rows, HD), 0) < seg_len[0]
    for head in range(heads):
        cols = head_cols(head)
        masked = jnp.where(live, keys[:, cols], jnp.zeros((), BF16))
        full[head * HD : (head + 1) * HD, :] = tn(masked, values[:, cols]).astype(BF16)
    split_rows(full, outs, lax.axis_index("seg"))


def mix_kernel(parts, upward, parent, *refs):
    blocks, outs = refs[:parts], refs[parts:]
    me = lax.axis_index("seg")

    def is_ancestor(child, other):
        first = parent[child]
        second = jnp.where(first >= 0, parent[jnp.maximum(first, 0)], -1)
        return jnp.logical_or(other == first, other == second)

    loaded = [block[...].astype(F32) for block in blocks]
    for out_step, out in enumerate(outs):
        target = lax.rem(me + out_step, parts)
        total = jnp.zeros(out.shape, F32)
        for in_step in range(parts):
            source = lax.rem(me + parts - in_step, parts)
            if upward:
                used = is_ancestor(target, source)
            else:
                used = is_ancestor(source, target)
            total = total + jnp.where(used, 1.0, 0.0) * loaded[in_step]
        out[...] = total.astype(BF16)


def keep_mask(rows, length):
    token = lax.broadcasted_iota(jnp.int32, (rows, rows), 0)
    other = lax.broadcasted_iota(jnp.int32, (rows, rows), 1)
    return (other <= token) & (other < length)


def local_kernel(heads, seg_len, queries, keys, values, local):
    rows = keys.shape[0]
    keep = keep_mask(rows, seg_len[0])
    for head in range(heads):
        cols = head_cols(head)
        scores = jnp.where(keep, nt(queries[:, cols], keys[:, cols]), 0.0).astype(BF16)
        local[:, cols] = nn(scores, values[:, cols])


def token_rows(total):
    return jnp.sum(jnp.transpose(total), axis=0, keepdims=True)


def token_columns(row):
    return jnp.transpose(jnp.broadcast_to(row, (HD, row.shape[1])))


def carry_kernel(heads, parts, scale, seg_len, queries, local, cotangent, gain, *rest):
    received, (attention, sums, prefix) = rest[:parts], rest[parts:]
    join_rows(received, prefix, lax.axis_index("seg"))
    rows = queries.shape[0]
    live = lax.broadcasted_iota(jnp.int32, (rows, HD), 0) < seg_len[0]
    factor = jnp.where(live, scale, 0.0)
    squares = jnp.zeros((rows, HD), F32)
    products = jnp.zeros((rows, HD), F32)
    for head in range(heads):
        cols = head_cols(head)
        carried = nn(queries[:, cols], prefix[head * HD : (head + 1) * HD, :])
        out = factor * (carried + local[:, cols])
        attention[:, cols] = out
        squares += out * out
        products += out * (cotangent[:, cols].astype(F32) * gain[:, cols])
    sums[0:1, :] = token_rows(squares)
    sums[1:2, :] = token_rows(products)


def grad_kernel(heads, parts, groups, scale, seg_len, queries, attention, cotangent, gain, *rest):
    all_sums, rest = rest[:groups], rest[groups:]
    attended, grad_out = rest[:2]
    outs, full = rest[2:-1], rest[-1]
    rows = queries.shape[0]
    width = HEADS * HD
    total = all_sums[0][...]
    for other in all_sums[1:]:
        total = total + other[...]
    inverse = lax.rsqrt(total[0:1, :] / width + EPSILON)
    live = lax.broadcasted_iota(jnp.int32, (1, rows), 1) < seg_len[0]
    live_inverse = jnp.where(live, inverse, 0.0)
    shrink = live_inverse * inverse * (inverse * total[1:2, :]) / width
    inverse = token_columns(inverse)
    live_inverse = token_columns(live_inverse)
    shrink = token_columns(shrink)
    for head in range(heads):
        cols = head_cols(head)
        out = attention[:, cols]
        head_gain = gain[:, cols]
        attended[:, cols] = (out * inverse * head_gain).astype(BF16)
        gain_grad = cotangent[:, cols].astype(F32) * head_gain
        grad = (live_inverse * gain_grad - out * shrink).astype(BF16)
        grad_out[:, cols] = grad
        full[head * HD : (head + 1) * HD, :] = (scale * tn(queries[:, cols], grad)).astype(BF16)
    split_rows(full, outs, lax.axis_index("seg"))


def back_kernel(heads, parts, scale, seg_len, queries, keys, values, grad_out, *rest):
    received, (query_grad, key_part, value_part, prefix) = rest[:parts], rest[parts:]
    join_rows(received, prefix, lax.axis_index("seg"))
    rows = queries.shape[0]
    length = seg_len[0]
    keep = keep_mask(rows, length)
    other = lax.broadcasted_iota(jnp.int32, (rows, rows), 0)
    token = lax.broadcasted_iota(jnp.int32, (rows, rows), 1)
    keep_turned = (other <= token) & (other < length)
    for head in range(heads):
        cols = head_cols(head)
        query, key, value, grad = queries[:, cols], keys[:, cols], values[:, cols], grad_out[:, cols]
        grad_scores = jnp.where(keep, nt(grad, value), 0.0).astype(BF16)
        carried = nt(grad, prefix[head * HD : (head + 1) * HD, :])
        query_grad[:, cols] = (scale * (carried + nn(grad_scores, key))).astype(BF16)
        turned = jnp.where(keep_turned, nt(value, grad), 0.0).astype(BF16)
        key_part[:, cols] = scale * nn(turned, query)
        turned = jnp.where(keep_turned, nt(key, query), 0.0).astype(BF16)
        value_part[:, cols] = scale * nn(turned, grad)


def final_kernel(heads, parts, seg_len, keys, values, key_part, value_part, *rest):
    received, (key_grad, value_grad, below) = rest[:parts], rest[parts:]
    join_rows(received, below, lax.axis_index("seg"))
    rows = keys.shape[0]
    live = lax.broadcasted_iota(jnp.int32, (rows, HD), 0) < seg_len[0]
    live = jnp.where(live, 1.0, 0.0)
    for head in range(heads):
        cols = head_cols(head)
        state = below[head * HD : (head + 1) * HD, :]
        key_grad[:, cols] = (key_part[:, cols] + live * nt(values[:, cols], state)).astype(BF16)
        value_grad[:, cols] = (value_part[:, cols] + live * nn(keys[:, cols], state)).astype(BF16)


def call(kernel, out_shape, operands, scalars, scratch=(), flops=0):
    moved = sum(math.prod(x.shape) * x.dtype.itemsize for x in operands)
    moved += sum(math.prod(x.shape) * x.dtype.itemsize for x in out_shape)
    return pl.pallas_call(
        kernel,
        out_shape=out_shape,
        in_specs=[SMEM] * scalars + [VMEM] * (len(operands) - scalars),
        out_specs=[VMEM] * len(out_shape),
        scratch_shapes=list(scratch),
        compiler_params=pltpu.CompilerParams(vmem_limit_bytes=VMEM_LIMIT),
        cost_estimate=pl.CostEstimate(flops=flops, bytes_accessed=moved, transcendentals=0),
    )(*operands)


def send_around(blocks, axis):
    size = len(blocks)
    received = [blocks[0]]
    for step in range(1, size):
        pairs = [(j, (j + step) % size) for j in range(size)]
        received.append(lax.ppermute(blocks[step], axis, pairs))
    return received


def per_device(segs, groups, queries, key_rows, values, cotangent, out_gain, parent, seg_len):
    rows, features = queries.shape[1:]
    heads = features // HD
    scale = 1.0 / math.sqrt(HD * rows)
    query, key, value, cot = queries[0], key_rows[0], values[0], cotangent[0]
    gain = out_gain[None]
    shape = jax.ShapeDtypeStruct
    part_shapes = [shape((features // segs, HD), BF16)] * segs
    state_scratch = pltpu.VMEM((features, HD), BF16)
    unit = 2 * heads * rows * HD

    own = call(
        functools.partial(state_kernel, heads),
        part_shapes, (seg_len, key, value), 1, [state_scratch], unit * HD,
    )
    mixed = call(
        functools.partial(mix_kernel, segs, True), part_shapes, (parent, *send_around(own, "seg")), 1
    )
    (local,) = call(
        functools.partial(local_kernel, heads),
        [shape((rows, features), F32)], (seg_len, query, key, value), 1, (), unit * rows * 2,
    )
    prefix = send_around(mixed, "seg")
    attention, sums = call(
        functools.partial(carry_kernel, heads, segs, scale),
        [shape((rows, features), F32), shape((2, rows), F32)],
        (seg_len, query, local, cot, gain, *prefix), 1, [state_scratch], unit * HD,
    )
    all_sums = send_around([sums] * groups, "head")
    attended, grad_out, *state_grad = call(
        functools.partial(grad_kernel, heads, segs, groups, scale),
        [shape((rows, features), BF16)] * 2 + part_shapes,
        (seg_len, query, attention, cot, gain, *all_sums), 1, [state_scratch], unit * HD,
    )
    mixed = call(
        functools.partial(mix_kernel, segs, False), part_shapes, (parent, *send_around(state_grad, "seg")), 1
    )
    query_grad, key_part, value_part = call(
        functools.partial(back_kernel, heads, segs, scale),
        [shape((rows, features), BF16)] + [shape((rows, features), F32)] * 2,
        (seg_len, query, key, value, grad_out, *prefix), 1, [state_scratch], unit * (6 * rows + HD),
    )
    below = send_around(mixed, "seg")
    key_grad, value_grad = call(
        functools.partial(final_kernel, heads, segs),
        [shape((rows, features), BF16)] * 2,
        (seg_len, key, value, key_part, value_part, *below), 1, [state_scratch], 2 * unit * HD,
    )
    return attended[None], query_grad[None], key_grad[None], value_grad[None]


def solution(mesh):
    split = P("seg", None, "head")
    return jax.shard_map(
        functools.partial(per_device, mesh.shape["seg"], mesh.shape["head"]),
        mesh=mesh,
        in_specs=(split, split, split, split, P("head"), P(), P("seg")),
        out_specs=(split, split, split, split),
        check_vma=False,
    )
```

time: 147 us -> 67.2 us (0.46)
  waiting for transfers between devices: 63.1 us -> 9.44 us
  starting transfers between devices: 0.08 us -> 36.6 us
  matrix products: 29.2 us -> 0 us
  Pallas kernels: 0 us -> 15.7 us
  local copies, waits for them, and re-layouts: 18.3 us -> 3.69 us
  between operations: 14.9 us -> 1.52 us
  blocking collectives: 11.8 us -> 0 us
  other arithmetic: 8.54 us -> 0 us
    ppermute x0 -> x31, starting transfers between devices: none -> 36.6 us  [send_around(): received.append(lax.ppermute(blocks[step], axis, pairs))]
    reduce_scatter x1 -> x0, waiting for transfers between devices: 33.5 us -> none  [per_device(): lax.psum_scatter((weights[:, None, None, None] * state_float[None]).astyp...]
    all_gather x1 -> x0, waiting for transfers between devices: 29.6 us -> none  [per_device(): lax.all_gather(own_state[None], 'seg', axis=0, tiled=True)]
    dot_general x13 -> x0, matrix products: 29.2 us -> none  [the longest x1 6.33 us: per_device(): jnp.einsum('j,jhde->hde', weights, lax.all_gather(own_state[None], 'seg',...]
    pallas_call x0 -> x8, Pallas kernels: none -> 15.7 us  [call(): pl.pallas_call(kernel, out_shape=out_shape, in_specs=[SMEM] * scalars + [...]
    unnamed x51 -> x18, local copies, waits for them, and re-layouts: 15.7 us -> 3.69 us
    psum x1 -> x0, blocking collectives: 11.8 us -> none  [per_device(): total_square, total_dot = lax.psum((square_part, dot_part), 'head')]
    ppermute x0 -> x31, waiting for transfers between devices: none -> 9.44 us  [send_around(): received.append(lax.ppermute(blocks[step], axis, pairs))]
  transfers between devices with their start and end apart: 2 -> 31, of which waited for: 2 -> 11; matrix products, arithmetic and copies ran while one was open for 14% -> 0% of each run, Pallas kernels for 0% -> 11%
where the time goes in v1:
time: 67.2 us; the launch traced here: 67 us
  starting transfers between devices  36.6 us (54%)
  Pallas kernels  15.7 us (23%)
  waiting for transfers between devices  9.44 us (14%)
  local copies, waits for them, and re-layouts  3.69 us (5%)
  between operations  1.52 us (2%)
    ppermute x31, starting transfers between devices, send_around(): received.append(lax.ppermute(blocks[step], axis, pairs))  36.6 us
    pallas_call x8, Pallas kernels, call(): pl.pallas_call(kernel, out_shape=out_shape, in_specs=[SMEM] * scalars + [...  15.7 us
    ppermute x31, waiting for transfers between devices, send_around(): received.append(lax.ppermute(blocks[step], axis, pairs))  9.44 us
    unnamed x18, local copies, waits for them, and re-layouts  3.69 us
  transfers between devices with their start and end apart: 31, of which 11 were waited for; matrix products, arithmetic and copies ran while one was open for 0% of the time, Pallas kernels for 11%

profile of v1, /device:TPU:0, one launch (start us, length us, event | category | flops | bytes accessed | tf_op | source)
XLA Modules:
  0.0 67.0 jit_solution(18402320229714719437)
XLA Ops:
  1.4 1.2 %copy-done.1 = bf16[1,256,2048]{2,1,0:T(8,128)(2,1)S(1)} copy-done((bf16[1,256,2048]{2,1,0:T(8,128)(2,1)S(1)}, bf16[1,256,2048]{2,1,0:T(8,128)(2,1)}, u32[]{:S(2)}) %copy-start.1) | copy-done | bytes 1048600
  2.6 1.2 %copy-done.3 = bf16[1,256,2048]{2,1,0:T(8,128)(2,1)S(1)} copy-done((bf16[1,256,2048]{2,1,0:T(8,128)(2,1)S(1)}, bf16[1,256,2048]{2,1,0:T(8,128)(2,1)}, u32[]{:S(2)}) %copy-start.3) | copy-done | bytes 1048600
  3.8 0.5 shard_map.103
  4.4 0.5 collective-permute-start
  4.9 2.5 %collective-permute-start.1 = (bf16[256,128]{1,0:T(8,128)(2,1)S(1)}, bf16[256,128]{1,0:T(8,128)(2,1)S(1)}, u32[]{:S(2)}, u32[]{:S(2)}) collective-permute-start(bf16[256,128]{1,0:T(8,128)(2,1)S(1)} %get-tuple-element.47), channel_id=1, source_target_pairs={{0,2},{1,3},{2,4},{3,5},{4,6},{5,7},{6,0},{7,1},{8,10},{9,11},{10,... | collective-permute-start | bytes 196616 | tf_op jit(solution)/shard_map/ppermute | solution.py:215
  7.4 2.4 %collective-permute-start.2 = (bf16[256,128]{1,0:T(8,128)(2,1)S(1)}, bf16[256,128]{1,0:T(8,128)(2,1)S(1)}, u32[]{:S(2)}, u32[]{:S(2)}) collective-permute-start(bf16[256,128]{1,0:T(8,128)(2,1)S(1)} %get-tuple-element.48), channel_id=1, source_target_pairs={{0,3},{1,4},{2,5},{3,6},{4,7},{5,0},{6,1},{7,2},{8,11},{9,12},{10,... | collective-permute-start | bytes 196616 | tf_op jit(solution)/shard_map/ppermute | solution.py:215
  9.8 0.5 collective-permute-start.3
  10.3 0.1 collective-permute-start.4
  10.4 0.0 collective-permute-done.refs_1_
  10.4 1.7 %collective-permute-start.5 = (bf16[256,128]{1,0:T(8,128)(2,1)S(1)}, bf16[256,128]{1,0:T(8,128)(2,1)S(1)}, u32[]{:S(2)}, u32[]{:S(2)}) collective-permute-start(bf16[256,128]{1,0:T(8,128)(2,1)S(1)} %get-tuple-element.51), channel_id=1, source_target_pairs={{0,6},{1,7},{2,0},{3,1},{4,2},{5,3},{6,4},{7,5},{8,14},{9,15},{10,... | collective-permute-start | bytes 196616 | tf_op jit(solution)/shard_map/ppermute | solution.py:215
  12.1 0.0 collective-permute-done.1.refs_2_
  12.1 2.0 %collective-permute-start.6 = (bf16[256,128]{1,0:T(8,128)(2,1)S(1)}, bf16[256,128]{1,0:T(8,128)(2,1)S(1)}, u32[]{:S(2)}, u32[]{:S(2)}) collective-permute-start(bf16[256,128]{1,0:T(8,128)(2,1)S(1)} %get-tuple-element.52), channel_id=1, source_target_pairs={{0,7},{1,0},{2,1},{3,2},{4,3},{5,4},{6,5},{7,6},{8,15},{9,8},{10,9... | collective-permute-start | bytes 196616 | tf_op jit(solution)/shard_map/ppermute | solution.py:215
  14.2 0.0 collective-permute-done.2.refs_3_
  14.2 0.0 collective-permute-done.3.refs_4_
  14.2 0.3 collective-permute-done.4.refs_5_
  14.4 0.7 %collective-permute-done.5.refs_6_ = bf16[256,128]{1,0:T(8,128)(2,1)S(1)} collective-permute-done((bf16[256,128]{1,0:T(8,128)(2,1)S(1)}, bf16[256,128]{1,0:T(8,128)(2,1)S(1)}, u32[]{:S(2)}, u32[]{:S(2)}) %collective-permute-start.5) | collective-permute-done | bytes 65568 | tf_op jit(solution)/shard_map/ppermute | solution.py:215
  15.1 1.0 %collective-permute-done.6.refs_7_ = bf16[256,128]{1,0:T(8,128)(2,1)S(1)} collective-permute-done((bf16[256,128]{1,0:T(8,128)(2,1)S(1)}, bf16[256,128]{1,0:T(8,128)(2,1)S(1)}, u32[]{:S(2)}, u32[]{:S(2)}) %collective-permute-start.6) | collective-permute-done | bytes 65568 | tf_op jit(solution)/shard_map/ppermute | solution.py:215
  16.1 1.1 %shard_map.104 = (bf16[256,128]{1,0:T(8,128)(2,1)S(1)}, bf16[256,128]{1,0:T(8,128)(2,1)S(1)}, bf16[256,128]{1,0:T(8,128)(2,1)S(1)}, bf16[256,128]{1,0:T(8,128)(2...) custom-call(s32[8]{0:T(128)S(1)} %copy-done.8, ...), custom_call_target="tpu_custom_call" | custom-call | bytes 1048608 | tf_op jit(solution)/shard_map/pallas_call | solution.py:199
  17.2 0.8 %collective-permute-start.7 = (bf16[256,128]{1,0:T(8,128)(2,1)S(1)}, bf16[256,128]{1,0:T(8,128)(2,1)S(1)}, u32[]{:S(2)}, u32[]{:S(2)}) collective-permute-start(bf16[256,128]{1,0:T(8,128)(2,1)S(1)} %get-tuple-element.54), channel_id=1, source_target_pairs={{0,1},{1,2},{2,3},{3,4},{4,5},{5,6},{6,7},{7,0},{8,9},{9,10},{10,1... | collective-permute-start | bytes 196616 | tf_op jit(solution)/shard_map/ppermute | solution.py:215
  18.0 1.5 %collective-permute-start.8 = (bf16[256,128]{1,0:T(8,128)(2,1)S(1)}, bf16[256,128]{1,0:T(8,128)(2,1)S(1)}, u32[]{:S(2)}, u32[]{:S(2)}) collective-permute-start(bf16[256,128]{1,0:T(8,128)(2,1)S(1)} %get-tuple-element.55), channel_id=1, source_target_pairs={{0,2},{1,3},{2,4},{3,5},{4,6},{5,7},{6,0},{7,1},{8,10},{9,11},{10,... | collective-permute-start | bytes 196616 | tf_op jit(solution)/shard_map/ppermute | solution.py:215
  19.5 0.9 %collective-permute-start.9 = (bf16[256,128]{1,0:T(8,128)(2,1)S(1)}, bf16[256,128]{1,0:T(8,128)(2,1)S(1)}, u32[]{:S(2)}, u32[]{:S(2)}) collective-permute-start(bf16[256,128]{1,0:T(8,128)(2,1)S(1)} %get-tuple-element.56), channel_id=1, source_target_pairs={{0,3},{1,4},{2,5},{3,6},{4,7},{5,0},{6,1},{7,2},{8,11},{9,12},{10,... | collective-permute-start | bytes 196616 | tf_op jit(solution)/shard_map/ppermute | solution.py:215
  20.4 1.3 %collective-permute-start.10 = (bf16[256,128]{1,0:T(8,128)(2,1)S(1)}, bf16[256,128]{1,0:T(8,128)(2,1)S(1)}, u32[]{:S(2)}, u32[]{:S(2)}) collective-permute-start(bf16[256,128]{1,0:T(8,128)(2,1)S(1)} %get-tuple-element.57), channel_id=1, source_target_pairs={{0,4},{1,5},{2,6},{3,7},{4,0},{5,1},{6,2},{7,3},{8,12},{9,13},{10,... | collective-permute-start | bytes 196616 | tf_op jit(solution)/shard_map/ppermute | solution.py:215
  21.8 0.6 collective-permute-start.11
  22.4 0.0 collective-permute-done.7.rest_1_
  22.4 0.9 %collective-permute-start.12 = (bf16[256,128]{1,0:T(8,128)(2,1)S(1)}, bf16[256,128]{1,0:T(8,128)(2,1)S(1)}, u32[]{:S(2)}, u32[]{:S(2)}) collective-permute-start(bf16[256,128]{1,0:T(8,128)(2,1)S(1)} %get-tuple-element.59), channel_id=1, source_target_pairs={{0,6},{1,7},{2,0},{3,1},{4,2},{5,3},{6,4},{7,5},{8,14},{9,15},{10,... | collective-permute-start | bytes 196616 | tf_op jit(solution)/shard_map/ppermute | solution.py:215
  23.3 0.7 collective-permute-done.8.rest_2_
  23.9 0.8 %collective-permute-start.13 = (bf16[256,128]{1,0:T(8,128)(2,1)S(1)}, bf16[256,128]{1,0:T(8,128)(2,1)S(1)}, u32[]{:S(2)}, u32[]{:S(2)}) collective-permute-start(bf16[256,128]{1,0:T(8,128)(2,1)S(1)} %get-tuple-element.60), channel_id=1, source_target_pairs={{0,7},{1,0},{2,1},{3,2},{4,3},{5,4},{6,5},{7,6},{8,15},{9,8},{10,9... | collective-permute-start | bytes 196616 | tf_op jit(solution)/shard_map/ppermute | solution.py:215
  24.8 1.2 %copy-done.4 = bf16[1,256,2048]{2,1,0:T(8,128)(2,1)S(1)} copy-done((bf16[1,256,2048]{2,1,0:T(8,128)(2,1)S(1)}, bf16[1,256,2048]{2,1,0:T(8,128)(2,1)}, u32[]{:S(2)}) %copy-start.4) | copy-done | bytes 1048600
  26.0 1.5 %shard_map.102.local = f32[256,2048]{1,0:T(8,128)S(1)} custom-call(s32[1]{0:T(128)S(6)} %copy.11.seg_len, bf16[256,2048]{1,0:T(8,128)(2,1)S(1)} %bitcast.9, bf16[256,2048]{1,0:T(8,128)(2,1)S(1)} %bitcast.14, bf16[256,2048]{1,0:T(8,128)(2,1)S(1)} %bitcast.18), custom_call_target="tpu_custom_call" | custom-call | flops 536870912 | bytes 5242884 | tf_op jit(solution)/shard_map/pallas_call | solution.py:199
  27.5 0.0 collective-permute-done.10.rest_4_
  27.5 0.0 collective-permute-done.13.rest_7_
  27.5 1.0 %shard_map.105 = (f32[256,2048]{1,0:T(8,128)S(1)}, f32[2,256]{1,0:T(2,128)S(1)}) custom-call(s32[1]{0:T(128)S(6)} %copy.11.seg_len, bf16[256,2048]{1,0:T(8,128)(2,1)S(1)} %bitcast.10, f32[256,2048]{1,0:T(8,128)S(1)} %shard_map.102.local, bf16[256,2048]{1,0:T(8,128)(2,1)S(1)} %bitcast.21, f32[1,2048]{1,0:T(1,128)S(1)} %bitcast.23, ...), custom_call_target="tpu_custom_call" | custom-call | flops 134217728 | bytes 6825988 | tf_op jit(solution)/shard_map/pallas_call | solution.py:199
  28.5 3.7 %collective-permute-start.16 = (f32[2,256]{1,0:T(2,128)S(1)}, f32[2,256]{1,0:T(2,128)S(1)}, u32[]{:S(2)}, u32[]{:S(2)}) collective-permute-start(f32[2,256]{1,0:T(2,128)S(1)} %get-tuple-element.62.rest_0_), channel_id=1, source_target_pairs={{0,24},{8,0},{16,8},{24,16},{1,25},{9,1},{17,9},{25,17},{2,26},{10... | collective-permute-start | bytes 6152 | tf_op jit(solution)/shard_map/ppermute | solution.py:215
  32.2 1.0 %collective-permute-start.14 = (f32[2,256]{1,0:T(2,128)S(1)}, f32[2,256]{1,0:T(2,128)S(1)}, u32[]{:S(2)}, u32[]{:S(2)}) collective-permute-start(f32[2,256]{1,0:T(2,128)S(1)} %get-tuple-element.62.rest_0_), channel_id=1, source_target_pairs={{0,8},{8,16},{16,24},{24,0},{1,9},{9,17},{17,25},{25,1},{2,10},{10... | collective-permute-start | bytes 6152 | tf_op jit(solution)/shard_map/ppermute | solution.py:215
  33.2 0.3 collective-permute-done.16.rest_3_
  33.5 3.2 %collective-permute-done.15.rest_2_ = f32[2,256]{1,0:T(2,128)S(1)} collective-permute-done((f32[2,256]{1,0:T(2,128)S(1)}, f32[2,256]{1,0:T(2,128)S(1)}, u32[]{:S(2)}, u32[]{:S(2)}) %collective-permute-start.15) | collective-permute-done | bytes 2080 | tf_op jit(solution)/shard_map/ppermute | solution.py:215
  36.7 0.9 %collective-permute-done.14.rest_1_ = f32[2,256]{1,0:T(2,128)S(1)} collective-permute-done((f32[2,256]{1,0:T(2,128)S(1)}, f32[2,256]{1,0:T(2,128)S(1)}, u32[]{:S(2)}, u32[]{:S(2)}) %collective-permute-start.14) | collective-permute-done | bytes 2080 | tf_op jit(solution)/shard_map/ppermute | solution.py:215
  37.6 2.1 %shard_map.106 = (bf16[256,2048]{1,0:T(8,128)(2,1)}, bf16[256,2048]{1,0:T(8,128)(2,1)S(1)}, bf16[256,128]{1,0:T(8,128)(2,1)S(1)}, bf16[256,128]{1,0:T(8,128)(2,1...) custom-call(s32[1]{0:T(128)S(6)} %copy.11.seg_len, ...), custom_call_target="tpu_custom_call" | custom-call | flops 134217728 | bytes 6832132 | tf_op jit(solution)/shard_map/pallas_call | solution.py:199
  39.7 0.0 collective-permute-start.17
  39.7 1.3 %collective-permute-start.18 = (bf16[256,128]{1,0:T(8,128)(2,1)S(1)}, bf16[256,128]{1,0:T(8,128)(2,1)S(1)}, u32[]{:S(2)}, u32[]{:S(2)}) collective-permute-start(bf16[256,128]{1,0:T(8,128)(2,1)S(1)} %get-tuple-element.70), channel_id=1, source_target_pairs={{0,2},{1,3},{2,4},{3,5},{4,6},{5,7},{6,0},{7,1},{8,10},{9,11},{10,... | collective-permute-start | bytes 196616 | tf_op jit(solution)/shard_map/ppermute | solution.py:215
  41.1 1.7 %collective-permute-start.19 = (bf16[256,128]{1,0:T(8,128)(2,1)S(1)}, bf16[256,128]{1,0:T(8,128)(2,1)S(1)}, u32[]{:S(2)}, u32[]{:S(2)}) collective-permute-start(bf16[256,128]{1,0:T(8,128)(2,1)S(1)} %get-tuple-element.71), channel_id=1, source_target_pairs={{0,3},{1,4},{2,5},{3,6},{4,7},{5,0},{6,1},{7,2},{8,11},{9,12},{10,... | collective-permute-start | bytes 196616 | tf_op jit(solution)/shard_map/ppermute | solution.py:215
  42.8 1.2 %collective-permute-start.20 = (bf16[256,128]{1,0:T(8,128)(2,1)S(1)}, bf16[256,128]{1,0:T(8,128)(2,1)S(1)}, u32[]{:S(2)}, u32[]{:S(2)}) collective-permute-start(bf16[256,128]{1,0:T(8,128)(2,1)S(1)} %get-tuple-element.72), channel_id=1, source_target_pairs={{0,4},{1,5},{2,6},{3,7},{4,0},{5,1},{6,2},{7,3},{8,12},{9,13},{10,... | collective-permute-start | bytes 196616 | tf_op jit(solution)/shard_map/ppermute | solution.py:215
  44.0 0.5 collective-permute-done.17.refs_1_
  44.5 1.1 %collective-permute-start.22 = (bf16[256,128]{1,0:T(8,128)(2,1)S(1)}, bf16[256,128]{1,0:T(8,128)(2,1)S(1)}, u32[]{:S(2)}, u32[]{:S(2)}) collective-permute-start(bf16[256,128]{1,0:T(8,128)(2,1)S(1)} %get-tuple-element.74), channel_id=1, source_target_pairs={{0,6},{1,7},{2,0},{3,1},{4,2},{5,3},{6,4},{7,5},{8,14},{9,15},{10,... | collective-permute-start | bytes 196616 | tf_op jit(solution)/shard_map/ppermute | solution.py:215
  45.6 2.3 %collective-permute-start.23 = (bf16[256,128]{1,0:T(8,128)(2,1)S(1)}, bf16[256,128]{1,0:T(8,128)(2,1)S(1)}, u32[]{:S(2)}, u32[]{:S(2)}) collective-permute-start(bf16[256,128]{1,0:T(8,128)(2,1)S(1)} %get-tuple-element.75), channel_id=1, source_target_pairs={{0,7},{1,0},{2,1},{3,2},{4,3},{5,4},{6,5},{7,6},{8,15},{9,8},{10,9... | collective-permute-start | bytes 196616 | tf_op jit(solution)/shard_map/ppermute | solution.py:215
  47.9 0.0 collective-permute-done.19.refs_3_
  47.9 0.6 collective-permute-done.20.refs_4_
  48.5 0.0 collective-permute-done.21.refs_5_
  48.5 0.7 %collective-permute-done.22.refs_6_ = bf16[256,128]{1,0:T(8,128)(2,1)S(1)} collective-permute-done((bf16[256,128]{1,0:T(8,128)(2,1)S(1)}, bf16[256,128]{1,0:T(8,128)(2,1)S(1)}, u32[]{:S(2)}, u32[]{:S(2)}) %collective-permute-start.22) | collective-permute-done | bytes 65568 | tf_op jit(solution)/shard_map/ppermute | solution.py:215
  49.2 0.6 collective-permute-done.23.refs_7_
  49.8 1.1 %shard_map.108 = (bf16[256,128]{1,0:T(8,128)(2,1)S(1)}, bf16[256,128]{1,0:T(8,128)(2,1)S(1)}, bf16[256,128]{1,0:T(8,128)(2,1)S(1)}, bf16[256,128]{1,0:T(8,128)(2...) custom-call(s32[8]{0:T(128)S(1)} %copy-done.8, ...), custom_call_target="tpu_custom_call" | custom-call | bytes 1048608 | tf_op jit(solution)/shard_map/pallas_call | solution.py:199
  50.9 0.2 collective-permute-start.24
  51.2 2.1 %collective-permute-start.25 = (bf16[256,128]{1,0:T(8,128)(2,1)S(1)}, bf16[256,128]{1,0:T(8,128)(2,1)S(1)}, u32[]{:S(2)}, u32[]{:S(2)}) collective-permute-start(bf16[256,128]{1,0:T(8,128)(2,1)S(1)} %get-tuple-element.78), channel_id=1, source_target_pairs={{0,2},{1,3},{2,4},{3,5},{4,6},{5,7},{6,0},{7,1},{8,10},{9,11},{10,... | collective-permute-start | bytes 196616 | tf_op jit(solution)/shard_map/ppermute | solution.py:215
  53.2 1.0 %collective-permute-start.26 = (bf16[256,128]{1,0:T(8,128)(2,1)S(1)}, bf16[256,128]{1,0:T(8,128)(2,1)S(1)}, u32[]{:S(2)}, u32[]{:S(2)}) collective-permute-start(bf16[256,128]{1,0:T(8,128)(2,1)S(1)} %get-tuple-element.79), channel_id=1, source_target_pairs={{0,3},{1,4},{2,5},{3,6},{4,7},{5,0},{6,1},{7,2},{8,11},{9,12},{10,... | collective-permute-start | bytes 196616 | tf_op jit(solution)/shard_map/ppermute | solution.py:215
  54.2 1.3 %collective-permute-start.27 = (bf16[256,128]{1,0:T(8,128)(2,1)S(1)}, bf16[256,128]{1,0:T(8,128)(2,1)S(1)}, u32[]{:S(2)}, u32[]{:S(2)}) collective-permute-start(bf16[256,128]{1,0:T(8,128)(2,1)S(1)} %get-tuple-element.80), channel_id=1, source_target_pairs={{0,4},{1,5},{2,6},{3,7},{4,0},{5,1},{6,2},{7,3},{8,12},{9,13},{10,... | collective-permute-start | bytes 196616 | tf_op jit(solution)/shard_map/ppermute | solution.py:215
  55.5 0.6 collective-permute-start.28
  56.1 0.0 collective-permute-done.24.rest_1_
  56.1 0.9 %collective-permute-start.29 = (bf16[256,128]{1,0:T(8,128)(2,1)S(1)}, bf16[256,128]{1,0:T(8,128)(2,1)S(1)}, u32[]{:S(2)}, u32[]{:S(2)}) collective-permute-start(bf16[256,128]{1,0:T(8,128)(2,1)S(1)} %get-tuple-element.82), channel_id=1, source_target_pairs={{0,6},{1,7},{2,0},{3,1},{4,2},{5,3},{6,4},{7,5},{8,14},{9,15},{10,... | collective-permute-start | bytes 196616 | tf_op jit(solution)/shard_map/ppermute | solution.py:215
  57.0 0.0 collective-permute-done.25.rest_2_
  57.0 1.6 %collective-permute-start.30 = (bf16[256,128]{1,0:T(8,128)(2,1)S(1)}, bf16[256,128]{1,0:T(8,128)(2,1)S(1)}, u32[]{:S(2)}, u32[]{:S(2)}) collective-permute-start(bf16[256,128]{1,0:T(8,128)(2,1)S(1)} %get-tuple-element.83), channel_id=1, source_target_pairs={{0,7},{1,0},{2,1},{3,2},{4,3},{5,4},{6,5},{7,6},{8,15},{9,8},{10,9... | collective-permute-start | bytes 196616 | tf_op jit(solution)/shard_map/ppermute | solution.py:215
  58.7 6.1 %shard_map.107 = (bf16[256,2048]{1,0:T(8,128)(2,1)}, f32[256,2048]{1,0:T(8,128)S(1)}, f32[256,2048]{1,0:T(8,128)S(1)}) custom-call(s32[1]{0:T(128)S(6)} %copy.11.seg_len, bf16[256,2048]{1,0:T(8,128)(2,1)S(1)} %bitcast.12, bf16[256,2048]{1,0:T(8,128)(2,1)S(1)} %bitcast.15, bf16[256,2048]{1,0:T(8,128)(2,1)S(1)} %bitcast.19, ...), custom_call_target="tpu_custom_call" | custom-call | flops 1744830464 | bytes 9961476 | tf_op jit(solution)/shard_map/pallas_call | solution.py:199
  64.8 0.0 collective-permute-done.29.rest_6_
  64.8 0.0 collective-permute-done.30.rest_7_
  64.8 2.2 %shard_map.109 = (bf16[256,2048]{1,0:T(8,128)(2,1)}, bf16[256,2048]{1,0:T(8,128)(2,1)}) custom-call(s32[1]{0:T(128)S(6)} %copy.11.seg_len, bf16[256,2048]{1,0:T(8,128)(2,1)S(1)} %bitcast.16, bf16[256,2048]{1,0:T(8,128)(2,1)S(1)} %bitcast.20, f32[256,2048]{1,0:T(8,128)S(1)} %get-tuple-element.66.key_part, f32[256,2048]{1,0:T(8,128)S(1)} %get-tuple-element.67.value_part, ...), custom_call_target="tpu_custom_call" | custom-call | flops 268435456 | bytes 8912900 | tf_op jit(solution)/shard_map/pallas_call | solution.py:199
  (24 shorter events, 0.1 us)
Async XLA Ops:
  0.6 24.1 %copy-start = (bf16[1,256,2048]{2,1,0:T(8,128)(2,1)S(1)}, bf16[1,256,2048]{2,1,0:T(8,128)(2,1)}, u32[]{:S(2)}) copy-start(bf16[1,256,2048]{2,1,0:T(8,128)(2,1)} %param.7) | copy-start | bytes 3145732
  1.4 1.2 %copy-start.1 = (bf16[1,256,2048]{2,1,0:T(8,128)(2,1)S(1)}, bf16[1,256,2048]{2,1,0:T(8,128)(2,1)}, u32[]{:S(2)}) copy-start(bf16[1,256,2048]{2,1,0:T(8,128)(2,1)} %param.8) | copy-start | bytes 3145732
  2.6 1.2 %copy-start.3 = (bf16[1,256,2048]{2,1,0:T(8,128)(2,1)S(1)}, bf16[1,256,2048]{2,1,0:T(8,128)(2,1)}, u32[]{:S(2)}) copy-start(bf16[1,256,2048]{2,1,0:T(8,128)(2,1)} %param.9) | copy-start | bytes 3145732
  3.8 12.2 %copy-start.8 = (s32[8]{0:T(128)S(1)}, s32[8]{0:T(128)}, u32[]{:S(2)}) copy-start(s32[8]{0:T(128)} %parent.3) | copy-start | bytes 100
  3.8 20.9 %copy-start.2 = (bf16[1,256,2048]{2,1,0:T(8,128)(2,1)S(1)}, bf16[1,256,2048]{2,1,0:T(8,128)(2,1)}, u32[]{:S(2)}) copy-start(bf16[1,256,2048]{2,1,0:T(8,128)(2,1)} %param.8) | copy-start | bytes 3145732
  4.4 6.0 %collective-permute-start = (bf16[256,128]{1,0:T(8,128)(2,1)S(1)}, bf16[256,128]{1,0:T(8,128)(2,1)S(1)}, u32[]{:S(2)}, u32[]{:S(2)}) collective-permute-start(bf16[256,128]{1,0:T(8,128)(2,1)S(1)} %get-tuple-element.46), channel_id=1, source_target_pairs={{0,1},{1,2},{2,3},{3,4},{4,5},{5,6},{6,7},{7,0},{8,9},{9,10},{10,1... | collective-permute-start | bytes 196616 | tf_op jit(solution)/shard_map/ppermute | solution.py:215
  4.9 7.2 %collective-permute-start.1 = (bf16[256,128]{1,0:T(8,128)(2,1)S(1)}, bf16[256,128]{1,0:T(8,128)(2,1)S(1)}, u32[]{:S(2)}, u32[]{:S(2)}) collective-permute-start(bf16[256,128]{1,0:T(8,128)(2,1)S(1)} %get-tuple-element.47), channel_id=1, source_target_pairs={{0,2},{1,3},{2,4},{3,5},{4,6},{5,7},{6,0},{7,1},{8,10},{9,11},{10,... | collective-permute-start | bytes 196616 | tf_op jit(solution)/shard_map/ppermute | solution.py:215
  7.4 6.7 %collective-permute-start.2 = (bf16[256,128]{1,0:T(8,128)(2,1)S(1)}, bf16[256,128]{1,0:T(8,128)(2,1)S(1)}, u32[]{:S(2)}, u32[]{:S(2)}) collective-permute-start(bf16[256,128]{1,0:T(8,128)(2,1)S(1)} %get-tuple-element.48), channel_id=1, source_target_pairs={{0,3},{1,4},{2,5},{3,6},{4,7},{5,0},{6,1},{7,2},{8,11},{9,12},{10,... | collective-permute-start | bytes 196616 | tf_op jit(solution)/shard_map/ppermute | solution.py:215
  9.8 4.4 %collective-permute-start.3 = (bf16[256,128]{1,0:T(8,128)(2,1)S(1)}, bf16[256,128]{1,0:T(8,128)(2,1)S(1)}, u32[]{:S(2)}, u32[]{:S(2)}) collective-permute-start(bf16[256,128]{1,0:T(8,128)(2,1)S(1)} %get-tuple-element.49), channel_id=1, source_target_pairs={{0,4},{1,5},{2,6},{3,7},{4,0},{5,1},{6,2},{7,3},{8,12},{9,13},{10,... | collective-permute-start | bytes 196616 | tf_op jit(solution)/shard_map/ppermute | solution.py:215
  10.3 4.1 %collective-permute-start.4 = (bf16[256,128]{1,0:T(8,128)(2,1)S(1)}, bf16[256,128]{1,0:T(8,128)(2,1)S(1)}, u32[]{:S(2)}, u32[]{:S(2)}) collective-permute-start(bf16[256,128]{1,0:T(8,128)(2,1)S(1)} %get-tuple-element.50), channel_id=1, source_target_pairs={{0,5},{1,6},{2,7},{3,0},{4,1},{5,2},{6,3},{7,4},{8,13},{9,14},{10,... | collective-permute-start | bytes 196616 | tf_op jit(solution)/shard_map/ppermute | solution.py:215
  10.4 4.7 %collective-permute-start.5 = (bf16[256,128]{1,0:T(8,128)(2,1)S(1)}, bf16[256,128]{1,0:T(8,128)(2,1)S(1)}, u32[]{:S(2)}, u32[]{:S(2)}) collective-permute-start(bf16[256,128]{1,0:T(8,128)(2,1)S(1)} %get-tuple-element.51), channel_id=1, source_target_pairs={{0,6},{1,7},{2,0},{3,1},{4,2},{5,3},{6,4},{7,5},{8,14},{9,15},{10,... | collective-permute-start | bytes 196616 | tf_op jit(solution)/shard_map/ppermute | solution.py:215
  12.1 3.9 %collective-permute-start.6 = (bf16[256,128]{1,0:T(8,128)(2,1)S(1)}, bf16[256,128]{1,0:T(8,128)(2,1)S(1)}, u32[]{:S(2)}, u32[]{:S(2)}) collective-permute-start(bf16[256,128]{1,0:T(8,128)(2,1)S(1)} %get-tuple-element.52), channel_id=1, source_target_pairs={{0,7},{1,0},{2,1},{3,2},{4,3},{5,4},{6,5},{7,6},{8,15},{9,8},{10,9... | collective-permute-start | bytes 196616 | tf_op jit(solution)/shard_map/ppermute | solution.py:215
  17.2 5.2 %collective-permute-start.7 = (bf16[256,128]{1,0:T(8,128)(2,1)S(1)}, bf16[256,128]{1,0:T(8,128)(2,1)S(1)}, u32[]{:S(2)}, u32[]{:S(2)}) collective-permute-start(bf16[256,128]{1,0:T(8,128)(2,1)S(1)} %get-tuple-element.54), channel_id=1, source_target_pairs={{0,1},{1,2},{2,3},{3,4},{4,5},{5,6},{6,7},{7,0},{8,9},{9,10},{10,1... | collective-permute-start | bytes 196616 | tf_op jit(solution)/shard_map/ppermute | solution.py:215
  18.0 5.9 %collective-permute-start.8 = (bf16[256,128]{1,0:T(8,128)(2,1)S(1)}, bf16[256,128]{1,0:T(8,128)(2,1)S(1)}, u32[]{:S(2)}, u32[]{:S(2)}) collective-permute-start(bf16[256,128]{1,0:T(8,128)(2,1)S(1)} %get-tuple-element.55), channel_id=1, source_target_pairs={{0,2},{1,3},{2,4},{3,5},{4,6},{5,7},{6,0},{7,1},{8,10},{9,11},{10,... | collective-permute-start | bytes 196616 | tf_op jit(solution)/shard_map/ppermute | solution.py:215
  19.5 8.0 %collective-permute-start.9 = (bf16[256,128]{1,0:T(8,128)(2,1)S(1)}, bf16[256,128]{1,0:T(8,128)(2,1)S(1)}, u32[]{:S(2)}, u32[]{:S(2)}) collective-permute-start(bf16[256,128]{1,0:T(8,128)(2,1)S(1)} %get-tuple-element.56), channel_id=1, source_target_pairs={{0,3},{1,4},{2,5},{3,6},{4,7},{5,0},{6,1},{7,2},{8,11},{9,12},{10,... | collective-permute-start | bytes 196616 | tf_op jit(solution)/shard_map/ppermute | solution.py:215
  20.4 7.1 %collective-permute-start.10 = (bf16[256,128]{1,0:T(8,128)(2,1)S(1)}, bf16[256,128]{1,0:T(8,128)(2,1)S(1)}, u32[]{:S(2)}, u32[]{:S(2)}) collective-permute-start(bf16[256,128]{1,0:T(8,128)(2,1)S(1)} %get-tuple-element.57), channel_id=1, source_target_pairs={{0,4},{1,5},{2,6},{3,7},{4,0},{5,1},{6,2},{7,3},{8,12},{9,13},{10,... | collective-permute-start | bytes 196616 | tf_op jit(solution)/shard_map/ppermute | solution.py:215
  21.8 5.7 %collective-permute-start.11 = (bf16[256,128]{1,0:T(8,128)(2,1)S(1)}, bf16[256,128]{1,0:T(8,128)(2,1)S(1)}, u32[]{:S(2)}, u32[]{:S(2)}) collective-permute-start(bf16[256,128]{1,0:T(8,128)(2,1)S(1)} %get-tuple-element.58), channel_id=1, source_target_pairs={{0,5},{1,6},{2,7},{3,0},{4,1},{5,2},{6,3},{7,4},{8,13},{9,14},{10,... | collective-permute-start | bytes 196616 | tf_op jit(solution)/shard_map/ppermute | solution.py:215
  22.4 5.1 %collective-permute-start.12 = (bf16[256,128]{1,0:T(8,128)(2,1)S(1)}, bf16[256,128]{1,0:T(8,128)(2,1)S(1)}, u32[]{:S(2)}, u32[]{:S(2)}) collective-permute-start(bf16[256,128]{1,0:T(8,128)(2,1)S(1)} %get-tuple-element.59), channel_id=1, source_target_pairs={{0,6},{1,7},{2,0},{3,1},{4,2},{5,3},{6,4},{7,5},{8,14},{9,15},{10,... | collective-permute-start | bytes 196616 | tf_op jit(solution)/shard_map/ppermute | solution.py:215
  23.9 3.6 %collective-permute-start.13 = (bf16[256,128]{1,0:T(8,128)(2,1)S(1)}, bf16[256,128]{1,0:T(8,128)(2,1)S(1)}, u32[]{:S(2)}, u32[]{:S(2)}) collective-permute-start(bf16[256,128]{1,0:T(8,128)(2,1)S(1)} %get-tuple-element.60), channel_id=1, source_target_pairs={{0,7},{1,0},{2,1},{3,2},{4,3},{5,4},{6,5},{7,6},{8,15},{9,8},{10,9... | collective-permute-start | bytes 196616 | tf_op jit(solution)/shard_map/ppermute | solution.py:215
  24.8 1.2 %copy-start.4 = (bf16[1,256,2048]{2,1,0:T(8,128)(2,1)S(1)}, bf16[1,256,2048]{2,1,0:T(8,128)(2,1)}, u32[]{:S(2)}) copy-start(bf16[1,256,2048]{2,1,0:T(8,128)(2,1)} %param.9) | copy-start | bytes 3145732
  26.0 1.5 %copy-start.6 = (bf16[1,256,2048]{2,1,0:T(8,128)(2,1)S(1)}, bf16[1,256,2048]{2,1,0:T(8,128)(2,1)}, u32[]{:S(2)}) copy-start(bf16[1,256,2048]{2,1,0:T(8,128)(2,1)} %param.10) | copy-start | bytes 3145732
  26.0 1.5 %copy-start.7 = (f32[2048]{0:T(1024)S(1)}, f32[2048]{0:T(1024)}, u32[]{:S(2)}) copy-start(f32[2048]{0:T(1024)} %param.11) | copy-start | bytes 24580
  28.5 5.0 %collective-permute-start.16 = (f32[2,256]{1,0:T(2,128)S(1)}, f32[2,256]{1,0:T(2,128)S(1)}, u32[]{:S(2)}, u32[]{:S(2)}) collective-permute-start(f32[2,256]{1,0:T(2,128)S(1)} %get-tuple-element.62.rest_0_), channel_id=1, source_target_pairs={{0,24},{8,0},{16,8},{24,16},{1,25},{9,1},{17,9},{25,17},{2,26},{10... | collective-permute-start | bytes 6152 | tf_op jit(solution)/shard_map/ppermute | solution.py:215
  32.2 4.5 %collective-permute-start.15 = (f32[2,256]{1,0:T(2,128)S(1)}, f32[2,256]{1,0:T(2,128)S(1)}, u32[]{:S(2)}, u32[]{:S(2)}) collective-permute-start(f32[2,256]{1,0:T(2,128)S(1)} %get-tuple-element.62.rest_0_), channel_id=1, source_target_pairs={{0,16},{8,24},{16,0},{24,8},{1,17},{9,25},{17,1},{25,9},{2,18},{10... | collective-permute-start | bytes 6152 | tf_op jit(solution)/shard_map/ppermute | solution.py:215
  32.2 5.4 %collective-permute-start.14 = (f32[2,256]{1,0:T(2,128)S(1)}, f32[2,256]{1,0:T(2,128)S(1)}, u32[]{:S(2)}, u32[]{:S(2)}) collective-permute-start(f32[2,256]{1,0:T(2,128)S(1)} %get-tuple-element.62.rest_0_), channel_id=1, source_target_pairs={{0,8},{8,16},{16,24},{24,0},{1,9},{9,17},{17,25},{25,1},{2,10},{10... | collective-permute-start | bytes 6152 | tf_op jit(solution)/shard_map/ppermute | solution.py:215
  37.6 21.1 %copy-start.5 = (bf16[1,256,2048]{2,1,0:T(8,128)(2,1)S(1)}, bf16[1,256,2048]{2,1,0:T(8,128)(2,1)}, u32[]{:S(2)}) copy-start(bf16[1,256,2048]{2,1,0:T(8,128)(2,1)} %param.9) | copy-start | bytes 3145732
  39.7 4.8 %collective-permute-start.17 = (bf16[256,128]{1,0:T(8,128)(2,1)S(1)}, bf16[256,128]{1,0:T(8,128)(2,1)S(1)}, u32[]{:S(2)}, u32[]{:S(2)}) collective-permute-start(bf16[256,128]{1,0:T(8,128)(2,1)S(1)} %get-tuple-element.69), channel_id=1, source_target_pairs={{0,1},{1,2},{2,3},{3,4},{4,5},{5,6},{6,7},{7,0},{8,9},{9,10},{10,1... | collective-permute-start | bytes 196616 | tf_op jit(solution)/shard_map/ppermute | solution.py:215
  39.7 5.9 %collective-permute-start.18 = (bf16[256,128]{1,0:T(8,128)(2,1)S(1)}, bf16[256,128]{1,0:T(8,128)(2,1)S(1)}, u32[]{:S(2)}, u32[]{:S(2)}) collective-permute-start(bf16[256,128]{1,0:T(8,128)(2,1)S(1)} %get-tuple-element.70), channel_id=1, source_target_pairs={{0,2},{1,3},{2,4},{3,5},{4,6},{5,7},{6,0},{7,1},{8,10},{9,11},{10,... | collective-permute-start | bytes 196616 | tf_op jit(solution)/shard_map/ppermute | solution.py:215
  41.1 6.8 %collective-permute-start.19 = (bf16[256,128]{1,0:T(8,128)(2,1)S(1)}, bf16[256,128]{1,0:T(8,128)(2,1)S(1)}, u32[]{:S(2)}, u32[]{:S(2)}) collective-permute-start(bf16[256,128]{1,0:T(8,128)(2,1)S(1)} %get-tuple-element.71), channel_id=1, source_target_pairs={{0,3},{1,4},{2,5},{3,6},{4,7},{5,0},{6,1},{7,2},{8,11},{9,12},{10,... | collective-permute-start | bytes 196616 | tf_op jit(solution)/shard_map/ppermute | solution.py:215
  42.8 5.7 %collective-permute-start.20 = (bf16[256,128]{1,0:T(8,128)(2,1)S(1)}, bf16[256,128]{1,0:T(8,128)(2,1)S(1)}, u32[]{:S(2)}, u32[]{:S(2)}) collective-permute-start(bf16[256,128]{1,0:T(8,128)(2,1)S(1)} %get-tuple-element.72), channel_id=1, source_target_pairs={{0,4},{1,5},{2,6},{3,7},{4,0},{5,1},{6,2},{7,3},{8,12},{9,13},{10,... | collective-permute-start | bytes 196616 | tf_op jit(solution)/shard_map/ppermute | solution.py:215
  44.0 4.5 %collective-permute-start.21 = (bf16[256,128]{1,0:T(8,128)(2,1)S(1)}, bf16[256,128]{1,0:T(8,128)(2,1)S(1)}, u32[]{:S(2)}, u32[]{:S(2)}) collective-permute-start(bf16[256,128]{1,0:T(8,128)(2,1)S(1)} %get-tuple-element.73), channel_id=1, source_target_pairs={{0,5},{1,6},{2,7},{3,0},{4,1},{5,2},{6,3},{7,4},{8,13},{9,14},{10,... | collective-permute-start | bytes 196616 | tf_op jit(solution)/shard_map/ppermute | solution.py:215
  44.5 4.7 %collective-permute-start.22 = (bf16[256,128]{1,0:T(8,128)(2,1)S(1)}, bf16[256,128]{1,0:T(8,128)(2,1)S(1)}, u32[]{:S(2)}, u32[]{:S(2)}) collective-permute-start(bf16[256,128]{1,0:T(8,128)(2,1)S(1)} %get-tuple-element.74), channel_id=1, source_target_pairs={{0,6},{1,7},{2,0},{3,1},{4,2},{5,3},{6,4},{7,5},{8,14},{9,15},{10,... | collective-permute-start | bytes 196616 | tf_op jit(solution)/shard_map/ppermute | solution.py:215
  45.6 4.2 %collective-permute-start.23 = (bf16[256,128]{1,0:T(8,128)(2,1)S(1)}, bf16[256,128]{1,0:T(8,128)(2,1)S(1)}, u32[]{:S(2)}, u32[]{:S(2)}) collective-permute-start(bf16[256,128]{1,0:T(8,128)(2,1)S(1)} %get-tuple-element.75), channel_id=1, source_target_pairs={{0,7},{1,0},{2,1},{3,2},{4,3},{5,4},{6,5},{7,6},{8,15},{9,8},{10,9... | collective-permute-start | bytes 196616 | tf_op jit(solution)/shard_map/ppermute | solution.py:215
  50.9 5.2 %collective-permute-start.24 = (bf16[256,128]{1,0:T(8,128)(2,1)S(1)}, bf16[256,128]{1,0:T(8,128)(2,1)S(1)}, u32[]{:S(2)}, u32[]{:S(2)}) collective-permute-start(bf16[256,128]{1,0:T(8,128)(2,1)S(1)} %get-tuple-element.77), channel_id=1, source_target_pairs={{0,1},{1,2},{2,3},{3,4},{4,5},{5,6},{6,7},{7,0},{8,9},{9,10},{10,1... | collective-permute-start | bytes 196616 | tf_op jit(solution)/shard_map/ppermute | solution.py:215
  51.2 5.8 %collective-permute-start.25 = (bf16[256,128]{1,0:T(8,128)(2,1)S(1)}, bf16[256,128]{1,0:T(8,128)(2,1)S(1)}, u32[]{:S(2)}, u32[]{:S(2)}) collective-permute-start(bf16[256,128]{1,0:T(8,128)(2,1)S(1)} %get-tuple-element.78), channel_id=1, source_target_pairs={{0,2},{1,3},{2,4},{3,5},{4,6},{5,7},{6,0},{7,1},{8,10},{9,11},{10,... | collective-permute-start | bytes 196616 | tf_op jit(solution)/shard_map/ppermute | solution.py:215
  53.2 11.5 %collective-permute-start.26 = (bf16[256,128]{1,0:T(8,128)(2,1)S(1)}, bf16[256,128]{1,0:T(8,128)(2,1)S(1)}, u32[]{:S(2)}, u32[]{:S(2)}) collective-permute-start(bf16[256,128]{1,0:T(8,128)(2,1)S(1)} %get-tuple-element.79), channel_id=1, source_target_pairs={{0,3},{1,4},{2,5},{3,6},{4,7},{5,0},{6,1},{7,2},{8,11},{9,12},{10,... | collective-permute-start | bytes 196616 | tf_op jit(solution)/shard_map/ppermute | solution.py:215
  54.2 10.5 %collective-permute-start.27 = (bf16[256,128]{1,0:T(8,128)(2,1)S(1)}, bf16[256,128]{1,0:T(8,128)(2,1)S(1)}, u32[]{:S(2)}, u32[]{:S(2)}) collective-permute-start(bf16[256,128]{1,0:T(8,128)(2,1)S(1)} %get-tuple-element.80), channel_id=1, source_target_pairs={{0,4},{1,5},{2,6},{3,7},{4,0},{5,1},{6,2},{7,3},{8,12},{9,13},{10,... | collective-permute-start | bytes 196616 | tf_op jit(solution)/shard_map/ppermute | solution.py:215
  55.5 9.3 %collective-permute-start.28 = (bf16[256,128]{1,0:T(8,128)(2,1)S(1)}, bf16[256,128]{1,0:T(8,128)(2,1)S(1)}, u32[]{:S(2)}, u32[]{:S(2)}) collective-permute-start(bf16[256,128]{1,0:T(8,128)(2,1)S(1)} %get-tuple-element.81), channel_id=1, source_target_pairs={{0,5},{1,6},{2,7},{3,0},{4,1},{5,2},{6,3},{7,4},{8,13},{9,14},{10,... | collective-permute-start | bytes 196616 | tf_op jit(solution)/shard_map/ppermute | solution.py:215
  56.1 8.6 %collective-permute-start.29 = (bf16[256,128]{1,0:T(8,128)(2,1)S(1)}, bf16[256,128]{1,0:T(8,128)(2,1)S(1)}, u32[]{:S(2)}, u32[]{:S(2)}) collective-permute-start(bf16[256,128]{1,0:T(8,128)(2,1)S(1)} %get-tuple-element.82), channel_id=1, source_target_pairs={{0,6},{1,7},{2,0},{3,1},{4,2},{5,3},{6,4},{7,5},{8,14},{9,15},{10,... | collective-permute-start | bytes 196616 | tf_op jit(solution)/shard_map/ppermute | solution.py:215
  57.0 7.8 %collective-permute-start.30 = (bf16[256,128]{1,0:T(8,128)(2,1)S(1)}, bf16[256,128]{1,0:T(8,128)(2,1)S(1)}, u32[]{:S(2)}, u32[]{:S(2)}) collective-permute-start(bf16[256,128]{1,0:T(8,128)(2,1)S(1)} %get-tuple-element.83), channel_id=1, source_target_pairs={{0,7},{1,0},{2,1},{3,2},{4,3},{5,4},{6,5},{7,6},{8,15},{9,8},{10,9... | collective-permute-start | bytes 196616 | tf_op jit(solution)/shard_map/ppermute | solution.py:215

commit v2 on v1

v2 whole, which is shorter than its diff:
```python
import functools
import math

import jax
import jax.numpy as jnp
from jax import lax
from jax.experimental import pallas as pl
from jax.experimental.pallas import tpu as pltpu
from jax.sharding import PartitionSpec as P

HEADS = 64
HD = 128
EPSILON = 1e-06
F32 = jnp.float32
BF16 = jnp.bfloat16
VMEM_LIMIT = 24 * 1024 * 1024

VMEM = pl.BlockSpec(memory_space=pltpu.VMEM)
SMEM = pl.BlockSpec(memory_space=pltpu.SMEM)


def dot(a, b, contract):
    return lax.dot_general(a, b, (contract, ((), ())), preferred_element_type=F32)


def nn(a, b):
    return dot(a, b, ((1,), (0,)))


def nt(a, b):
    return dot(a, b, ((1,), (1,)))


def tn(a, b):
    return dot(a, b, ((0,), (0,)))


def head_cols(head):
    return slice(head * HD, (head + 1) * HD)


def state_kernel(heads, seg_len, keys, values, full):
    rows = keys.shape[0]
    live = lax.broadcasted_iota(jnp.int32, (rows, HD), 0) < seg_len[0]
    for head in range(heads):
        cols = head_cols(head)
        masked = jnp.where(live, keys[:, cols], jnp.zeros((), BF16))
        full[head * HD : (head + 1) * HD, :] = tn(masked, values[:, cols]).astype(BF16)


def mix_kernel(parts, upward, parent, blocks, outs):
    def is_ancestor(child, other):
        first = parent[child]
        second = jnp.where(first >= 0, parent[jnp.maximum(first, 0)], -1)
        return jnp.logical_or(other == first, other == second)

    rows = blocks.shape[0] // parts
    loaded = [blocks[j * rows : (j + 1) * rows, :].astype(F32) for j in range(parts)]
    for target in range(parts):
        total = jnp.zeros((rows, HD), F32)
        for source in range(parts):
            used = is_ancestor(target, source) if upward else is_ancestor(source, target)
            total = total + jnp.where(used, 1.0, 0.0) * loaded[source]
        outs[target * rows : (target + 1) * rows, :] = total.astype(BF16)


def keep_mask(rows, length):
    token = lax.broadcasted_iota(jnp.int32, (rows, rows), 0)
    other = lax.broadcasted_iota(jnp.int32, (rows, rows), 1)
    return (other <= token) & (other < length)


def local_kernel(heads, seg_len, queries, keys, values, local):
    rows = keys.shape[0]
    keep = keep_mask(rows, seg_len[0])
    for head in range(heads):
        cols = head_cols(head)
        scores = jnp.where(keep, nt(queries[:, cols], keys[:, cols]), 0.0).astype(BF16)
        local[:, cols] = nn(scores, values[:, cols])


def token_rows(total):
    return jnp.sum(jnp.transpose(total), axis=0, keepdims=True)


def token_columns(row):
    return jnp.transpose(jnp.broadcast_to(row, (HD, row.shape[1])))


def carry_kernel(heads, scale, seg_len, queries, local, cotangent, gain, prefix, attention, sums):
    rows = queries.shape[0]
    live = lax.broadcasted_iota(jnp.int32, (rows, HD), 0) < seg_len[0]
    factor = jnp.where(live, scale, 0.0)
    squares = jnp.zeros((rows, HD), F32)
    products = jnp.zeros((rows, HD), F32)
    for head in range(heads):
        cols = head_cols(head)
        carried = nn(queries[:, cols], prefix[head * HD : (head + 1) * HD, :])
        out = factor * (carried + local[:, cols])
        attention[:, cols] = out
        squares += out * out
        products += out * (cotangent[:, cols].astype(F32) * gain[:, cols])
    sums[0:1, :] = token_rows(squares)
    sums[1:2, :] = token_rows(products)


def grad_kernel(
    heads, scale, seg_len, queries, attention, cotangent, gain, all_sums, attended, grad_out, full
):
    rows = queries.shape[0]
    width = HEADS * HD
    total = all_sums[0]
    for other in range(1, all_sums.shape[0]):
        total = total + all_sums[other]
    inverse = lax.rsqrt(total[0:1, :] / width + EPSILON)
    live = lax.broadcasted_iota(jnp.int32, (1, rows), 1) < seg_len[0]
    live_inverse = jnp.where(live, inverse, 0.0)
    shrink = live_inverse * inverse * (inverse * total[1:2, :]) / width
    inverse = token_columns(inverse)
    live_inverse = token_columns(live_inverse)
    shrink = token_columns(shrink)
    for head in range(heads):
        cols = head_cols(head)
        out = attention[:, cols]
        head_gain = gain[:, cols]
        attended[:, cols] = (out * inverse * head_gain).astype(BF16)
        gain_grad = cotangent[:, cols].astype(F32) * head_gain
        grad = (live_inverse * gain_grad - out * shrink).astype(BF16)
        grad_out[:, cols] = grad
        full[head * HD : (head + 1) * HD, :] = (scale * tn(queries[:, cols], grad)).astype(BF16)


def back_kernel(
    heads, scale, seg_len, queries, keys, values, grad_out, prefix, query_grad, key_part, value_part
):
    rows = queries.shape[0]
    length = seg_len[0]
    keep = keep_mask(rows, length)
    other = lax.broadcasted_iota(jnp.int32, (rows, rows), 0)
    token = lax.broadcasted_iota(jnp.int32, (rows, rows), 1)
    keep_turned = (other <= token) & (other < length)
    for head in range(heads):
        cols = head_cols(head)
        query, key, value, grad = queries[:, cols], keys[:, cols], values[:, cols], grad_out[:, cols]
        grad_scores = jnp.where(keep, nt(grad, value), 0.0).astype(BF16)
        carried = nt(grad, prefix[head * HD : (head + 1) * HD, :])
        query_grad[:, cols] = (scale * (carried + nn(grad_scores, key))).astype(BF16)
        turned = jnp.where(keep_turned, nt(value, grad), 0.0).astype(BF16)
        key_part[:, cols] = scale * nn(turned, query)
        turned = jnp.where(keep_turned, nt(key, query), 0.0).astype(BF16)
        value_part[:, cols] = scale * nn(turned, grad)


def final_kernel(heads, seg_len, keys, values, key_part, value_part, below, key_grad, value_grad):
    rows = keys.shape[0]
    live = lax.broadcasted_iota(jnp.int32, (rows, HD), 0) < seg_len[0]
    live = jnp.where(live, 1.0, 0.0)
    for head in range(heads):
        cols = head_cols(head)
        state = below[head * HD : (head + 1) * HD, :]
        key_grad[:, cols] = (key_part[:, cols] + live * nt(values[:, cols], state)).astype(BF16)
        value_grad[:, cols] = (value_part[:, cols] + live * nn(keys[:, cols], state)).astype(BF16)


def call(kernel, out_shape, operands, scalars, scratch=(), flops=0):
    moved = sum(math.prod(x.shape) * x.dtype.itemsize for x in operands)
    moved += sum(math.prod(x.shape) * x.dtype.itemsize for x in out_shape)
    return pl.pallas_call(
        kernel,
        out_shape=out_shape,
        in_specs=[SMEM] * scalars + [VMEM] * (len(operands) - scalars),
        out_specs=[VMEM] * len(out_shape),
        scratch_shapes=list(scratch),
        compiler_params=pltpu.CompilerParams(vmem_limit_bytes=VMEM_LIMIT),
        cost_estimate=pl.CostEstimate(flops=flops, bytes_accessed=moved, transcendentals=0),
    )(*operands)


def exchange(rows, axis):
    return lax.all_to_all(rows, axis, split_axis=0, concat_axis=0, tiled=True)


def per_device(segs, groups, queries, key_rows, values, cotangent, out_gain, parent, seg_len):
    rows, features = queries.shape[1:]
    heads = features // HD
    scale = 1.0 / math.sqrt(HD * rows)
    query, key, value, cot = queries[0], key_rows[0], values[0], cotangent[0]
    gain = out_gain[None]
    shape = jax.ShapeDtypeStruct
    state = shape((features, HD), BF16)
    narrow = shape((rows, features), BF16)
    wide = shape((rows, features), F32)
    unit = 2 * heads * rows * HD

    (own,) = call(
        functools.partial(state_kernel, heads), [state], (seg_len, key, value), 1, (), unit * HD
    )
    (mixed,) = call(
        functools.partial(mix_kernel, segs, True), [state], (parent, exchange(own, "seg")), 1
    )
    (local,) = call(
        functools.partial(local_kernel, heads),
        [wide], (seg_len, query, key, value), 1, (), unit * rows * 2,
    )
    prefix = exchange(mixed, "seg")
    attention, sums = call(
        functools.partial(carry_kernel, heads, scale),
        [wide, shape((2, rows), F32)],
        (seg_len, query, local, cot, gain, prefix), 1, (), unit * HD,
    )
    all_sums = exchange(jnp.broadcast_to(sums[None], (groups, 2, rows)), "head")
    attended, grad_out, state_grad = call(
        functools.partial(grad_kernel, heads, scale),
        [narrow, narrow, state],
        (seg_len, query, attention, cot, gain, all_sums), 1, (), unit * HD,
    )
    (mixed,) = call(
        functools.partial(mix_kernel, segs, False), [state], (parent, exchange(state_grad, "seg")), 1
    )
    query_grad, key_part, value_part = call(
        functools.partial(back_kernel, heads, scale),
        [narrow, wide, wide],
        (seg_len, query, key, value, grad_out, prefix), 1, (), unit * (6 * rows + HD),
    )
    below = exchange(mixed, "seg")
    key_grad, value_grad = call(
        functools.partial(final_kernel, heads),
        [narrow, narrow],
        (seg_len, key, value, key_part, value_part, below), 1, (), 2 * unit * HD,
    )
    return attended[None], query_grad[None], key_grad[None], value_grad[None]


def solution(mesh):
    split = P("seg", None, "head")
    return jax.shard_map(
        functools.partial(per_device, mesh.shape["seg"], mesh.shape["head"]),
        mesh=mesh,
        in_specs=(split, split, split, split, P("head"), P(), P("seg")),
        out_specs=(split, split, split, split),
        check_vma=False,
    )
```

time: 67.2 us -> 88.9 us (1.32)
  blocking collectives: 0 us -> 37.4 us
  starting transfers between devices: 36.6 us -> 8.5 us
  local copies, waits for them, and re-layouts: 3.69 us -> 15.2 us
  Pallas kernels: 15.7 us -> 18.6 us
  waiting for transfers between devices: 9.44 us -> 6.9 us
    all_to_all x0 -> x3, blocking collectives: none -> 37.4 us  [exchange(): return lax.all_to_all(rows, axis, split_axis=0, concat_axis=0, tiled=True)]
    ppermute x31 -> x0, starting transfers between devices: 36.6 us -> none  [send_around(): received.append(lax.ppermute(blocks[step], axis, pairs))]
    unnamed x18 -> x38, local copies, waits for them, and re-layouts: 3.69 us -> 15.2 us
    ppermute x31 -> x0, waiting for transfers between devices: 9.44 us -> none  [send_around(): received.append(lax.ppermute(blocks[step], axis, pairs))]
    all_to_all x0 -> x2, starting transfers between devices: none -> 8.5 us  [exchange(): return lax.all_to_all(rows, axis, split_axis=0, concat_axis=0, tiled=True)]
    all_to_all x0 -> x2, waiting for transfers between devices: none -> 6.9 us  [exchange(): return lax.all_to_all(rows, axis, split_axis=0, concat_axis=0, tiled=True)]
    pallas_call x8, Pallas kernels: 15.7 us -> 18.6 us  [call(): pl.pallas_call(kernel, out_shape=out_shape, in_specs=[SMEM] * scalars + [...]
  transfers between devices with their start and end apart: 31 -> 2, of which waited for: 11 -> 1; matrix products, arithmetic and copies ran while one was open for 0% -> 0% of each run, Pallas kernels for 11% -> 10%
where the time goes in v2:
time: 88.9 us; the launch traced here: 88.1 us
  blocking collectives  37.4 us (42%)
  Pallas kernels  18.6 us (21%)
  local copies, waits for them, and re-layouts  15.2 us (17%)
  starting transfers between devices  8.5 us (10%)
  waiting for transfers between devices  6.9 us (8%)
  between operations  1.47 us (2%)
    all_to_all x3, blocking collectives, exchange(): return lax.all_to_all(rows, axis, split_axis=0, concat_axis=0, tiled=True)  37.4 us
    pallas_call x8, Pallas kernels, call(): pl.pallas_call(kernel, out_shape=out_shape, in_specs=[SMEM] * scalars + [...  18.6 us
    unnamed x38, local copies, waits for them, and re-layouts  15.2 us
    all_to_all x2, starting transfers between devices, exchange(): return lax.all_to_all(rows, axis, split_axis=0, concat_axis=0, tiled=True)  8.5 us
    all_to_all x2, waiting for transfers between devices, exchange(): return lax.all_to_all(rows, axis, split_axis=0, concat_axis=0, tiled=True)  6.9 us
  transfers between devices with their start and end apart: 2, of which 1 were waited for; matrix products, arithmetic and copies ran while one was open for 0% of the time, Pallas kernels for 10%

profile of v2, /device:TPU:0, one launch (start us, length us, event | category | flops | bytes accessed | tf_op | source)
XLA Modules:
  0.0 88.1 jit_solution(18044067357338170426)
XLA Ops:
  0.6 0.0 copy-start.16
  1.3 0.0 copy-start.1
  1.3 1.2 %copy-done.1 = bf16[1,256,2048]{2,1,0:T(8,128)(2,1)S(1)} copy-done((bf16[1,256,2048]{2,1,0:T(8,128)(2,1)S(1)}, bf16[1,256,2048]{2,1,0:T(8,128)(2,1)}, u32[]{:S(2)}) %copy-start.1) | copy-done | bytes 1048600
  2.5 0.0 copy-start.3
  2.5 1.2 %copy-done.3 = bf16[1,256,2048]{2,1,0:T(8,128)(2,1)S(1)} copy-done((bf16[1,256,2048]{2,1,0:T(8,128)(2,1)S(1)}, bf16[1,256,2048]{2,1,0:T(8,128)(2,1)}, u32[]{:S(2)}) %copy-start.3) | copy-done | bytes 1048600
  3.8 0.5 shard_map.103
  4.3 0.0 copy-start
  4.3 0.0 copy-start.2
  4.3 0.0 copy-start.4
  4.3 15.0 %all_to_all.49 = bf16[8,256,128]{2,1,0:T(8,128)(2,1)S(1)} all-to-all(bf16[8,256,128]{2,1,0:T(8,128)(2,1)S(1)} %bitcast.35), channel_id=1, replica_groups=mesh['head'=4,'seg'=8] {'seg'}, dimensions={0} | all-to-all | bytes 1048576 | tf_op jit(solution)/shard_map/all_to_all | solution.py:180
  19.3 0.0 copy-done.16
  19.3 1.1 %shard_map.104 = bf16[2048,128]{1,0:T(8,128)(2,1)S(1)} custom-call(s32[8]{0:T(128)S(1)} %copy-done.16, bf16[2048,128]{1,0:T(8,128)(2,1)S(1)} %bitcast.33), custom_call_target="tpu_custom_call" | custom-call | bytes 1048608 | tf_op jit(solution)/shard_map/pallas_call | solution.py:168
  20.4 0.0 copy-start.14
  20.4 0.8 copy-done.14
  21.2 4.2 %all-to-all-start.1 = ((bf16[8,256,128]{2,1,0:T(8,128)(2,1)}), bf16[8,256,128]{2,1,0:T(8,128)(2,1)}, u32[]{:S(2)}, u32[]{:S(2)}) async-start(bf16[8,256,128]{2,1,0:T(8,128)(2,1)} %bitcast.32), calls=%async_computation.1 | async-start | bytes 1048576 | tf_op jit(solution)/shard_map/all_to_all | solution.py:180
  25.4 0.0 copy-done
  25.4 0.0 copy-done.2
  25.4 0.0 copy-done.4
  25.4 0.0 copy-start.15
  25.4 1.5 %shard_map.102.local = f32[256,2048]{1,0:T(8,128)S(1)} custom-call(s32[1]{0:T(128)S(6)} %copy.11.seg_len, bf16[256,2048]{1,0:T(8,128)(2,1)S(1)} %bitcast.17, bf16[256,2048]{1,0:T(8,128)(2,1)S(1)} %bitcast.22, bf16[256,2048]{1,0:T(8,128)(2,1)S(1)} %bitcast.26), custom_call_target="tpu_custom_call" | custom-call | flops 536870912 | bytes 5242884 | tf_op jit(solution)/shard_map/pallas_call | solution.py:168
  26.9 0.0 copy-start.5
  26.9 1.3 %copy-done.5 = f32[256,2048]{1,0:T(8,128)} copy-done((f32[256,2048]{1,0:T(8,128)}, f32[256,2048]{1,0:T(8,128)S(1)}, u32[]{:S(2)}) %copy-start.5) | copy-done | bytes 2097176
  28.2 6.9 %all-to-all-done.1 = bf16[8,256,128]{2,1,0:T(8,128)(2,1)} async-done(((bf16[8,256,128]{2,1,0:T(8,128)(2,1)}), bf16[8,256,128]{2,1,0:T(8,128)(2,1)}, u32[]{:S(2)}, u32[]{:S(2)}) %all-to-all-start.1) | async-done | bytes 524320 | tf_op jit(solution)/shard_map/all_to_all | solution.py:180
  35.1 0.0 copy-done.15
  35.1 0.0 copy-start.6
  35.1 1.6 %copy-done.6 = f32[256,2048]{1,0:T(8,128)S(1)} copy-done((f32[256,2048]{1,0:T(8,128)S(1)}, f32[256,2048]{1,0:T(8,128)}, u32[]{:S(2)}) %copy-start.6) | copy-done | bytes 2097176
  36.7 0.0 copy-start.7
  36.7 1.2 %copy-done.7 = bf16[1,256,2048]{2,1,0:T(8,128)(2,1)S(1)} copy-done((bf16[1,256,2048]{2,1,0:T(8,128)(2,1)S(1)}, bf16[1,256,2048]{2,1,0:T(8,128)(2,1)}, u32[]{:S(2)}) %copy-start.7) | copy-done | bytes 1048600
  37.9 0.0 copy-start.8
  37.9 2.0 %shard_map.105 = (f32[256,2048]{1,0:T(8,128)S(1)}, f32[2,256]{1,0:T(2,128)S(1)}) custom-call(s32[1]{0:T(128)S(6)} %copy.11.seg_len, bf16[256,2048]{1,0:T(8,128)(2,1)S(1)} %bitcast.18, f32[256,2048]{1,0:T(8,128)S(1)} %copy-done.6, bf16[256,2048]{1,0:T(8,128)(2,1)S(1)} %bitcast.29, f32[1,2048]{1,0:T(1,128)S(1)} %bitcast.37, bf16[2048,128]{1,0:T(8,128)(2,1)} %bitcast.8.prefix), custom_call_target="tpu_custom_call" | custom-call | flops 134217728 | bytes 6825988 | tf_op jit(solution)/shard_map/pallas_call | solution.py:168
  39.9 10.3 %all_to_all.50.all_sums = f32[4,2,256]{2,1,0:T(2,128)S(1)} all-to-all(f32[4,2,256]{2,1,0:T(2,128)S(1)} %broadcast_in_dim.22), channel_id=1, replica_groups=mesh['head'=4,'seg'=8] {'head'}, dimensions={0} | all-to-all | bytes 16384 | tf_op jit(solution)/shard_map/all_to_all | solution.py:180
  50.2 0.0 copy-done.8
  50.2 2.1 %shard_map.106 = (bf16[256,2048]{1,0:T(8,128)(2,1)}, bf16[256,2048]{1,0:T(8,128)(2,1)S(1)}, bf16[2048,128]{1,0:T(8,128)(2,1)S(1)}) custom-call(s32[1]{0:T(128)S(6)} %copy.11.seg_len, bf16[256,2048]{1,0:T(8,128)(2,1)S(1)} %bitcast.19, f32[256,2048]{1,0:T(8,128)S(1)} %get-tuple-element.14.attention, bf16[256,2048]{1,0:T(8,128)(2,1)S(1)} %bitcast.30, ...), custom_call_target="tpu_custom_call" | custom-call | flops 134217728 | bytes 6832132 | tf_op jit(solution)/shard_map/pallas_call | solution.py:168
  52.3 0.0 copy-start.17
  52.3 12.1 %all_to_all.51 = bf16[8,256,128]{2,1,0:T(8,128)(2,1)S(1)} all-to-all(bf16[8,256,128]{2,1,0:T(8,128)(2,1)S(1)} %bitcast.36), channel_id=1, replica_groups=mesh['head'=4,'seg'=8] {'seg'}, dimensions={0} | all-to-all | bytes 1048576 | tf_op jit(solution)/shard_map/all_to_all | solution.py:180
  64.4 1.1 %shard_map.108 = bf16[2048,128]{1,0:T(8,128)(2,1)S(1)} custom-call(s32[8]{0:T(128)S(1)} %copy-done.16, bf16[2048,128]{1,0:T(8,128)(2,1)S(1)} %bitcast.34), custom_call_target="tpu_custom_call" | custom-call | bytes 1048608 | tf_op jit(solution)/shard_map/pallas_call | solution.py:168
  65.6 0.0 copy-done.17
  65.6 0.0 copy-start.13
  65.6 0.8 copy-done.13
  66.4 4.3 %all-to-all-start.4 = ((bf16[8,256,128]{2,1,0:T(8,128)(2,1)}), bf16[8,256,128]{2,1,0:T(8,128)(2,1)}, u32[]{:S(2)}, u32[]{:S(2)}) async-start(bf16[8,256,128]{2,1,0:T(8,128)(2,1)} %bitcast.31), calls=%async_computation.4 | async-start | bytes 1048576 | tf_op jit(solution)/shard_map/all_to_all | solution.py:180
  70.7 0.0 copy-start.18
  70.7 1.2 %copy-done.18 = bf16[256,2048]{1,0:T(8,128)(2,1)S(1)} copy-done((bf16[256,2048]{1,0:T(8,128)(2,1)S(1)}, bf16[256,2048]{1,0:T(8,128)(2,1)}, u32[]{:S(2)}) %copy-start.18) | copy-done | bytes 1048600
  71.9 7.1 %shard_map.107 = (bf16[256,2048]{1,0:T(8,128)(2,1)}, f32[256,2048]{1,0:T(8,128)S(1)}, f32[256,2048]{1,0:T(8,128)S(1)}) custom-call(s32[1]{0:T(128)S(6)} %copy.11.seg_len, bf16[256,2048]{1,0:T(8,128)(2,1)S(1)} %bitcast.20, bf16[256,2048]{1,0:T(8,128)(2,1)S(1)} %bitcast.23, bf16[256,2048]{1,0:T(8,128)(2,1)S(1)} %bitcast.27, bf16[256,2048]{1,0:T(8,128)(2,1)S(1)} %copy-done.18, ...), custom_call_target="tpu_custom_call" | custom-call | flops 1744830464 | bytes 9961476 | tf_op jit(solution)/shard_map/pallas_call | solution.py:168
  79.1 0.0 copy-start.9
  79.1 1.3 %copy-done.9 = f32[256,2048]{1,0:T(8,128)} copy-done((f32[256,2048]{1,0:T(8,128)}, f32[256,2048]{1,0:T(8,128)S(1)}, u32[]{:S(2)}) %copy-start.9) | copy-done | bytes 2097176
  80.4 0.0 copy-start.11
  80.4 1.3 %copy-done.11 = f32[256,2048]{1,0:T(8,128)} copy-done((f32[256,2048]{1,0:T(8,128)}, f32[256,2048]{1,0:T(8,128)S(1)}, u32[]{:S(2)}) %copy-start.11) | copy-done | bytes 2097176
  81.7 0.0 all-to-all-done.4
  81.7 0.0 copy-start.10
  81.7 1.6 %copy-done.10 = f32[256,2048]{1,0:T(8,128)S(1)} copy-done((f32[256,2048]{1,0:T(8,128)S(1)}, f32[256,2048]{1,0:T(8,128)}, u32[]{:S(2)}) %copy-start.10) | copy-done | bytes 2097176
  83.3 0.0 copy-start.12
  83.3 1.6 %copy-done.12 = f32[256,2048]{1,0:T(8,128)S(1)} copy-done((f32[256,2048]{1,0:T(8,128)S(1)}, f32[256,2048]{1,0:T(8,128)}, u32[]{:S(2)}) %copy-start.12) | copy-done | bytes 2097176
  84.9 3.2 %shard_map.109 = (bf16[256,2048]{1,0:T(8,128)(2,1)}, bf16[256,2048]{1,0:T(8,128)(2,1)}) custom-call(s32[1]{0:T(128)S(6)} %copy.11.seg_len, bf16[256,2048]{1,0:T(8,128)(2,1)S(1)} %bitcast.24, bf16[256,2048]{1,0:T(8,128)(2,1)S(1)} %bitcast.28, f32[256,2048]{1,0:T(8,128)S(1)} %copy-done.10, f32[256,2048]{1,0:T(8,128)S(1)} %copy-done.12, ...), custom_call_target="tpu_custom_call" | custom-call | flops 268435456 | bytes 8912900 | tf_op jit(solution)/shard_map/pallas_call | solution.py:168
  (1 shorter events, 0.0 us)
Async XLA Ops:
  0.6 18.6 %copy-start.16 = (s32[8]{0:T(128)S(1)}, s32[8]{0:T(128)}, u32[]{:S(2)}) copy-start(s32[8]{0:T(128)} %parent.3) | copy-start | bytes 100
  1.3 1.2 %copy-start.1 = (bf16[1,256,2048]{2,1,0:T(8,128)(2,1)S(1)}, bf16[1,256,2048]{2,1,0:T(8,128)(2,1)}, u32[]{:S(2)}) copy-start(bf16[1,256,2048]{2,1,0:T(8,128)(2,1)} %param.8) | copy-start | bytes 3145732
  2.5 1.2 %copy-start.3 = (bf16[1,256,2048]{2,1,0:T(8,128)(2,1)S(1)}, bf16[1,256,2048]{2,1,0:T(8,128)(2,1)}, u32[]{:S(2)}) copy-start(bf16[1,256,2048]{2,1,0:T(8,128)(2,1)} %param.9) | copy-start | bytes 3145732
  4.3 21.1 %copy-start = (bf16[1,256,2048]{2,1,0:T(8,128)(2,1)S(1)}, bf16[1,256,2048]{2,1,0:T(8,128)(2,1)}, u32[]{:S(2)}) copy-start(bf16[1,256,2048]{2,1,0:T(8,128)(2,1)} %param.7) | copy-start | bytes 3145732
  4.3 21.1 %copy-start.2 = (bf16[1,256,2048]{2,1,0:T(8,128)(2,1)S(1)}, bf16[1,256,2048]{2,1,0:T(8,128)(2,1)}, u32[]{:S(2)}) copy-start(bf16[1,256,2048]{2,1,0:T(8,128)(2,1)} %param.8) | copy-start | bytes 3145732
  4.3 21.1 %copy-start.4 = (bf16[1,256,2048]{2,1,0:T(8,128)(2,1)S(1)}, bf16[1,256,2048]{2,1,0:T(8,128)(2,1)}, u32[]{:S(2)}) copy-start(bf16[1,256,2048]{2,1,0:T(8,128)(2,1)} %param.9) | copy-start | bytes 3145732
  20.4 0.8 copy-start.14
  21.2 13.9 %all-to-all-start.1 = ((bf16[8,256,128]{2,1,0:T(8,128)(2,1)}), bf16[8,256,128]{2,1,0:T(8,128)(2,1)}, u32[]{:S(2)}, u32[]{:S(2)}) async-start(bf16[8,256,128]{2,1,0:T(8,128)(2,1)} %bitcast.32), calls=%async_computation.1 | async-start | bytes 1048576 | tf_op jit(solution)/shard_map/all_to_all | solution.py:180
  25.4 9.7 %copy-start.15 = (f32[2048]{0:T(1024)S(1)}, f32[2048]{0:T(1024)}, u32[]{:S(2)}) copy-start(f32[2048]{0:T(1024)} %param.11) | copy-start | bytes 24580
  26.9 1.3 %copy-start.5 = (f32[256,2048]{1,0:T(8,128)}, f32[256,2048]{1,0:T(8,128)S(1)}, u32[]{:S(2)}) copy-start(f32[256,2048]{1,0:T(8,128)S(1)} %shard_map.102.local) | copy-start | bytes 6291460
  35.1 1.6 %copy-start.6 = (f32[256,2048]{1,0:T(8,128)S(1)}, f32[256,2048]{1,0:T(8,128)}, u32[]{:S(2)}) copy-start(f32[256,2048]{1,0:T(8,128)} %copy-done.5) | copy-start | bytes 6291460
  36.7 1.2 %copy-start.7 = (bf16[1,256,2048]{2,1,0:T(8,128)(2,1)S(1)}, bf16[1,256,2048]{2,1,0:T(8,128)(2,1)}, u32[]{:S(2)}) copy-start(bf16[1,256,2048]{2,1,0:T(8,128)(2,1)} %param.10) | copy-start | bytes 3145732
  37.9 12.3 %copy-start.8 = (bf16[1,256,2048]{2,1,0:T(8,128)(2,1)S(1)}, bf16[1,256,2048]{2,1,0:T(8,128)(2,1)}, u32[]{:S(2)}) copy-start(bf16[1,256,2048]{2,1,0:T(8,128)(2,1)} %param.10) | copy-start | bytes 3145732
  52.3 13.3 %copy-start.17 = (bf16[256,2048]{1,0:T(8,128)(2,1)}, bf16[256,2048]{1,0:T(8,128)(2,1)S(1)}, u32[]{:S(2)}) copy-start(bf16[256,2048]{1,0:T(8,128)(2,1)S(1)} %get-tuple-element.17.grad_out) | copy-start | bytes 3145732
  65.6 0.8 copy-start.13
  66.4 15.3 %all-to-all-start.4 = ((bf16[8,256,128]{2,1,0:T(8,128)(2,1)}), bf16[8,256,128]{2,1,0:T(8,128)(2,1)}, u32[]{:S(2)}, u32[]{:S(2)}) async-start(bf16[8,256,128]{2,1,0:T(8,128)(2,1)} %bitcast.31), calls=%async_computation.4 | async-start | bytes 1048576 | tf_op jit(solution)/shard_map/all_to_all | solution.py:180
  70.7 1.2 %copy-start.18 = (bf16[256,2048]{1,0:T(8,128)(2,1)S(1)}, bf16[256,2048]{1,0:T(8,128)(2,1)}, u32[]{:S(2)}) copy-start(bf16[256,2048]{1,0:T(8,128)(2,1)} %copy-done.17) | copy-start | bytes 3145732
  79.1 1.3 %copy-start.9 = (f32[256,2048]{1,0:T(8,128)}, f32[256,2048]{1,0:T(8,128)S(1)}, u32[]{:S(2)}) copy-start(f32[256,2048]{1,0:T(8,128)S(1)} %get-tuple-element.19.key_part) | copy-start | bytes 6291460
  80.4 1.3 %copy-start.11 = (f32[256,2048]{1,0:T(8,128)}, f32[256,2048]{1,0:T(8,128)S(1)}, u32[]{:S(2)}) copy-start(f32[256,2048]{1,0:T(8,128)S(1)} %get-tuple-element.20.value_part) | copy-start | bytes 6291460
  81.7 1.6 %copy-start.10 = (f32[256,2048]{1,0:T(8,128)S(1)}, f32[256,2048]{1,0:T(8,128)}, u32[]{:S(2)}) copy-start(f32[256,2048]{1,0:T(8,128)} %copy-done.9) | copy-start | bytes 6291460
  83.3 1.6 %copy-start.12 = (f32[256,2048]{1,0:T(8,128)S(1)}, f32[256,2048]{1,0:T(8,128)}, u32[]{:S(2)}) copy-start(f32[256,2048]{1,0:T(8,128)} %copy-done.11) | copy-start | bytes 6291460

commit v3 on v2

v3 whole, which is shorter than its diff:
```python
import functools
import math

import jax
import jax.numpy as jnp
from jax import lax
from jax.experimental import pallas as pl
from jax.experimental.pallas import tpu as pltpu
from jax.sharding import PartitionSpec as P

HEADS = 64
HD = 128
EPSILON = 1e-06
F32 = jnp.float32
BF16 = jnp.bfloat16
VMEM_LIMIT = 24 * 1024 * 1024

VMEM = pl.BlockSpec(memory_space=pltpu.VMEM)
SMEM = pl.BlockSpec(memory_space=pltpu.SMEM)
HBM = pl.BlockSpec(memory_space=pltpu.HBM)


def dot(a, b, contract):
    return lax.dot_general(a, b, (contract, ((), ())), preferred_element_type=F32)


def nn(a, b):
    return dot(a, b, ((1,), (0,)))


def nt(a, b):
    return dot(a, b, ((1,), (1,)))


def tn(a, b):
    return dot(a, b, ((0,), (0,)))


def head_cols(head):
    return slice(head * HD, (head + 1) * HD)


def target_of(place, step, size):
    if size & (size - 1) == 0:
        return place ^ step
    return (place + step) % size


def source_of(place, step, size):
    if size & (size - 1) == 0:
        return place ^ step
    return (place + size - step) % size


def my_chip(pair):
    me = lax.axis_index("seg")
    return lax.div(me, pair), lax.rem(me, pair)


def split_rows(full, outs, chip):
    chips = len(outs)
    rows = full.shape[0] // chips
    for step, out in enumerate(outs):
        place = target_of(chip, step, chips)
        out[...] = full[pl.ds(pl.multiple_of(place * rows, rows), rows), :]


def join_rows(received, full, chip):
    chips = len(received)
    rows = full.shape[0] // chips
    for step, block in enumerate(received):
        place = source_of(chip, step, chips)
        full[pl.ds(pl.multiple_of(place * rows, rows), rows), :] = block[...]


def state_kernel(heads, pair, seg_len, keys_hbm, values_hbm, keys, values, *rest):
    outs, full, sems = rest[:-2], rest[-2], rest[-1]
    rows, features = keys.shape
    group = 2 * HD if heads % 2 == 0 else HD
    steps = features // group
    copies = []
    for step in range(steps):
        cols = slice(step * group, (step + 1) * group)
        pieces = ((keys_hbm, keys), (values_hbm, values))
        copies.append(
            [
                pltpu.make_async_copy(src.at[:, cols], dst.at[:, cols], sems.at[j, step])
                for j, (src, dst) in enumerate(pieces)
            ]
        )
    for step in copies:
        for copy in step:
            copy.start()
    live = lax.broadcasted_iota(jnp.int32, (rows, HD), 0) < seg_len[0]
    for step in range(steps):
        for copy in copies[step]:
            copy.wait()
        for head in range(step * group // HD, (step + 1) * group // HD):
            cols = head_cols(head)
            masked = jnp.where(live, keys[:, cols], jnp.zeros((), BF16))
            full[head * HD : (head + 1) * HD, :] = tn(masked, values[:, cols]).astype(BF16)
    split_rows(full, outs, my_chip(pair)[0])


def mix_kernel(chips, pair, upward, parent, *refs):
    blocks, outs, total = refs[: chips * pair], refs[chips * pair : -1], refs[-1]
    chip, core = my_chip(pair)

    def is_ancestor(child, other):
        first = parent[child]
        second = jnp.where(first >= 0, parent[jnp.maximum(first, 0)], -1)
        return jnp.logical_or(other == first, other == second)

    for out_step, out in enumerate(outs):
        target = target_of(chip, out_step, chips) * pair + core
        total[...] = jnp.zeros_like(total)
        for flip in range(pair):
            for in_step in range(chips):
                source = source_of(chip, in_step, chips) * pair + (core ^ flip)
                block = blocks[flip * chips + in_step]
                used = is_ancestor(target, source) if upward else is_ancestor(source, target)

                @pl.when(used)
                def _():
                    total[...] += block[...].astype(F32)

        out[...] = total[...].astype(BF16)


def keep_mask(rows, length):
    token = lax.broadcasted_iota(jnp.int32, (rows, rows), 0)
    other = lax.broadcasted_iota(jnp.int32, (rows, rows), 1)
    return (other <= token) & (other < length)


def local_kernel(heads, seg_len, queries, keys, values, local):
    rows = keys.shape[0]
    keep = keep_mask(rows, seg_len[0])
    for head in range(heads):
        cols = head_cols(head)
        scores = jnp.where(keep, nt(queries[:, cols], keys[:, cols]), 0.0).astype(BF16)
        local[:, cols] = nn(scores, values[:, cols])


def token_rows(total):
    return jnp.sum(jnp.transpose(total), axis=0, keepdims=True)


def token_columns(row):
    return jnp.transpose(jnp.broadcast_to(row, (HD, row.shape[1])))


def carry_kernel(heads, chips, pair, scale, seg_len, queries, local, cotangent, gain, *rest):
    received, (attention, sums, prefix) = rest[:chips], rest[chips:]
    join_rows(received, prefix, my_chip(pair)[0])
    rows = queries.shape[0]
    live = lax.broadcasted_iota(jnp.int32, (rows, HD), 0) < seg_len[0]
    factor = jnp.where(live, scale, 0.0)
    squares = jnp.zeros((rows, HD), F32)
    products = jnp.zeros((rows, HD), F32)
    for head in range(heads):
        cols = head_cols(head)
        carried = nn(queries[:, cols], prefix[head * HD : (head + 1) * HD, :])
        out = factor * (carried + local[:, cols])
        attention[:, cols] = out
        squares += out * out
        products += out * (cotangent[:, cols].astype(F32) * gain[:, cols])
    sums[0:1, :] = token_rows(squares)
    sums[1:2, :] = token_rows(products)


def grad_kernel(heads, groups, pair, scale, seg_len, queries, attention, cotangent, gain, *rest):
    all_sums, (grad_out, inverse_rms), outs, full = (
        rest[:groups], rest[groups : groups + 2], rest[groups + 2 : -1], rest[-1]
    )
    rows = queries.shape[0]
    width = HEADS * HD
    total = all_sums[0][...]
    for other in all_sums[1:]:
        total = total + other[...]
    inverse = lax.rsqrt(total[0:1, :] / width + EPSILON)
    inverse_rms[...] = inverse
    live = lax.broadcasted_iota(jnp.int32, (1, rows), 1) < seg_len[0]
    live_inverse = jnp.where(live, inverse, 0.0)
    shrink = live_inverse * inverse * (inverse * total[1:2, :]) / width
    live_inverse = token_columns(live_inverse)
    shrink = token_columns(shrink)
    for head in range(heads):
        cols = head_cols(head)
        gain_grad = cotangent[:, cols].astype(F32) * gain[:, cols]
        grad = (live_inverse * gain_grad - attention[:, cols] * shrink).astype(BF16)
        grad_out[:, cols] = grad
        full[head * HD : (head + 1) * HD, :] = (scale * tn(queries[:, cols], grad)).astype(BF16)
    split_rows(full, outs, my_chip(pair)[0])


def query_kernel(
    heads, chips, pair, scale, seg_len, keys, values, grad_out, attention, inverse_rms, gain, *rest
):
    received, (attended, query_grad, prefix) = rest[:chips], rest[chips:]
    join_rows(received, prefix, my_chip(pair)[0])
    keep = keep_mask(keys.shape[0], seg_len[0])
    inverse = token_columns(inverse_rms[...])
    for head in range(heads):
        cols = head_cols(head)
        grad = grad_out[:, cols]
        grad_scores = jnp.where(keep, nt(grad, values[:, cols]), 0.0).astype(BF16)
        carried = nt(grad, prefix[head * HD : (head + 1) * HD, :])
        query_grad[:, cols] = (scale * (carried + nn(grad_scores, keys[:, cols]))).astype(BF16)
        attended[:, cols] = (attention[:, cols] * inverse * gain[:, cols]).astype(BF16)


def back_kernel(heads, scale, seg_len, queries, keys, values, grad_out, key_part, value_part):
    rows = queries.shape[0]
    other = lax.broadcasted_iota(jnp.int32, (rows, rows), 0)
    token = lax.broadcasted_iota(jnp.int32, (rows, rows), 1)
    keep = (other <= token) & (other < seg_len[0])
    for head in range(heads):
        cols = head_cols(head)
        query, grad = queries[:, cols], grad_out[:, cols]
        turned = jnp.where(keep, nt(values[:, cols], grad), 0.0).astype(BF16)
        key_part[:, cols] = scale * nn(turned, query)
        turned = jnp.where(keep, nt(keys[:, cols], query), 0.0).astype(BF16)
        value_part[:, cols] = scale * nn(turned, grad)


def final_kernel(heads, chips, pair, seg_len, keys, values, key_part, value_part, *rest):
    received, (key_grad, value_grad, below) = rest[:chips], rest[chips:]
    join_rows(received, below, my_chip(pair)[0])
    rows = keys.shape[0]
    live = lax.broadcasted_iota(jnp.int32, (rows, HD), 0) < seg_len[0]
    live = jnp.where(live, 1.0, 0.0)
    for head in range(heads):
        cols = head_cols(head)
        state = below[head * HD : (head + 1) * HD, :]
        key_grad[:, cols] = (key_part[:, cols] + live * nt(values[:, cols], state)).astype(BF16)
        value_grad[:, cols] = (value_part[:, cols] + live * nn(keys[:, cols], state)).astype(BF16)


def call(kernel, out_shape, operands, scalars, scratch=(), flops=0, stream=0):
    moved = sum(math.prod(x.shape) * x.dtype.itemsize for x in operands)
    moved += sum(math.prod(x.shape) * x.dtype.itemsize for x in out_shape)
    return pl.pallas_call(
        kernel,
        out_shape=out_shape,
        in_specs=[SMEM] * scalars + [HBM] * stream + [VMEM] * (len(operands) - scalars - stream),
        out_specs=[VMEM] * len(out_shape),
        scratch_shapes=list(scratch),
        compiler_params=pltpu.CompilerParams(vmem_limit_bytes=VMEM_LIMIT),
        cost_estimate=pl.CostEstimate(flops=flops, bytes_accessed=moved, transcendentals=0),
    )(*operands)


def chip_sends(blocks, pair):
    chips = len(blocks)
    received = [blocks[0]]
    for step in range(1, chips):
        moves = [
            (c * pair + k, target_of(c, step, chips) * pair + k) for c in range(chips) for k in range(pair)
        ]
        received.append(lax.ppermute(blocks[step], "seg", moves))
    return received


def core_swap(blocks, pair):
    if pair == 1:
        return []
    moves = [(j, j ^ 1) for j in range(len(blocks) * pair)]
    return [lax.ppermute(block, "seg", moves) for block in blocks]


def group_sends(sums, groups):
    received = [sums]
    for step in range(1, groups):
        moves = [(j, target_of(j, step, groups)) for j in range(groups)]
        received.append(lax.ppermute(sums, "head", moves))
    return received


def per_device(segs, groups, queries, key_rows, values, cotangent, out_gain, parent, seg_len):
    rows, features = queries.shape[1:]
    heads = features // HD
    pair = 2 if segs % 2 == 0 else 1
    chips = segs // pair
    scale = 1.0 / math.sqrt(HD * rows)
    query, cot = queries[0], cotangent[0]
    gain = out_gain[None]
    shape = jax.ShapeDtypeStruct
    narrow = shape((rows, features), BF16)
    wide = shape((rows, features), F32)
    part_shapes = [shape((features // chips, HD), BF16)] * chips
    state_scratch = pltpu.VMEM((features, HD), BF16)
    mix_scratch = pltpu.VMEM((features // chips, HD), F32)
    unit = 2 * heads * rows * HD

    def exchange(parts, upward):
        arrived = chip_sends(parts, pair)
        arrived = arrived + core_swap(arrived, pair)
        mixed = call(
            functools.partial(mix_kernel, chips, pair, upward),
            part_shapes, (parent, *arrived), 1, [mix_scratch],
        )
        return chip_sends(mixed, pair)

    key, value, *own = call(
        functools.partial(state_kernel, heads, pair),
        [narrow, narrow] + part_shapes, (seg_len, key_rows[0], values[0]), 1,
        [state_scratch, pltpu.SemaphoreType.DMA((2, heads))], unit * HD, 2,
    )
    prefix = exchange(own, True)
    (local,) = call(
        functools.partial(local_kernel, heads),
        [wide], (seg_len, query, key, value), 1, (), unit * rows * 2,
    )
    attention, sums = call(
        functools.partial(carry_kernel, heads, chips, pair, scale),
        [wide, shape((2, rows), F32)],
        (seg_len, query, local, cot, gain, *prefix), 1, [state_scratch], unit * HD,
    )
    grad_out, inverse_rms, *state_grad = call(
        functools.partial(grad_kernel, heads, groups, pair, scale),
        [narrow, shape((1, rows), F32)] + part_shapes,
        (seg_len, query, attention, cot, gain, *group_sends(sums, groups)), 1, [state_scratch], unit * HD,
    )
    below = exchange(state_grad, False)
    attended, query_grad = call(
        functools.partial(query_kernel, heads, chips, pair, scale),
        [narrow, narrow],
        (seg_len, key, value, grad_out, attention, inverse_rms, gain, *prefix), 1,
        [state_scratch], unit * (2 * rows + HD),
    )
    key_part, value_part = call(
        functools.partial(back_kernel, heads, scale),
        [wide, wide], (seg_len, query, key, value, grad_out), 1, (), unit * 4 * rows,
    )
    key_grad, value_grad = call(
        functools.partial(final_kernel, heads, chips, pair),
        [narrow, narrow],
        (seg_len, key, value, key_part, value_part, *below), 1, [state_scratch], 2 * unit * HD,
    )
    return attended[None], query_grad[None], key_grad[None], value_grad[None]


def solution(mesh):
    split = P("seg", None, "head")
    return jax.shard_map(
        functools.partial(per_device, mesh.shape["seg"], mesh.shape["head"]),
        mesh=mesh,
        in_specs=(split, split, split, split, P("head"), P(), P("seg")),
        out_specs=(split, split, split, split),
        check_vma=False,
    )
```

time: 88.9 us -> 63.7 us (0.72)
  blocking collectives: 37.4 us -> 0 us
  waiting for transfers between devices: 6.9 us -> 21.4 us
  local copies, waits for them, and re-layouts: 15.2 us -> 2.46 us
  starting transfers between devices: 8.5 us -> 20.2 us
    all_to_all x3 -> x0, blocking collectives: 37.4 us -> none  [exchange(): return lax.all_to_all(rows, axis, split_axis=0, concat_axis=0, tiled=True)]
    ppermute x0 -> x23, waiting for transfers between devices: none -> 21.4 us  [the longest x12 15.4 us: chip_sends(): received.append(lax.ppermute(blocks[step], 'seg', moves))]
    ppermute x0 -> x23, starting transfers between devices: none -> 20.2 us  [the longest x12 15.2 us: chip_sends(): received.append(lax.ppermute(blocks[step], 'seg', moves))]
    unnamed x38 -> x12, local copies, waits for them, and re-layouts: 15.2 us -> 2.46 us
    all_to_all x2 -> x0, starting transfers between devices: 8.5 us -> none  [exchange(): return lax.all_to_all(rows, axis, split_axis=0, concat_axis=0, tiled=True)]
    all_to_all x2 -> x0, waiting for transfers between devices: 6.9 us -> none  [exchange(): return lax.all_to_all(rows, axis, split_axis=0, concat_axis=0, tiled=True)]
    pallas_call x8 -> x9, Pallas kernels: 18.6 us -> 17.9 us  [call(): pl.pallas_call(kernel, out_shape=out_shape, in_specs=[SMEM] * scalars + [...]
  transfers between devices with their start and end apart: 2 -> 23, of which waited for: 1 -> 13; matrix products, arithmetic and copies ran while one was open for 0% -> 0% of each run, Pallas kernels for 10% -> 13%
where the time goes in v3:
time: 63.7 us; the launch traced here: 63.4 us
  waiting for transfers between devices  21.4 us (34%)
  starting transfers between devices  20.2 us (32%)
  Pallas kernels  17.9 us (28%)
  local copies, waits for them, and re-layouts  2.46 us (4%)
  between operations  1.49 us (2%)
    pallas_call x9, Pallas kernels, call(): pl.pallas_call(kernel, out_shape=out_shape, in_specs=[SMEM] * scalars + [...  17.9 us
    ppermute x12, waiting for transfers between devices, chip_sends(): received.append(lax.ppermute(blocks[step], 'seg', moves))  15.4 us
    ppermute x12, starting transfers between devices, chip_sends(): received.append(lax.ppermute(blocks[step], 'seg', moves))  15.2 us
    ppermute x3, starting transfers between devices, group_sends(): received.append(lax.ppermute(sums, 'head', moves))  4.45 us
    ppermute x3, waiting for transfers between devices, group_sends(): received.append(lax.ppermute(sums, 'head', moves))  3.7 us
    unnamed x12, local copies, waits for them, and re-layouts  2.46 us
    ppermute x8, waiting for transfers between devices, core_swap(): return [lax.ppermute(block, 'seg', moves) for block in blocks]  2.35 us
  transfers between devices with their start and end apart: 23, of which 13 were waited for; matrix products, arithmetic and copies ran while one was open for 0% of the time, Pallas kernels for 13%

profile of v3, /device:TPU:0, one launch (start us, length us, event | category | flops | bytes accessed | tf_op | source)
XLA Modules:
  0.0 63.4 jit_solution(14162935987057763296)
XLA Ops:
  0.6 0.0 copy-start
  1.4 0.0 copy-start.2
  1.4 1.2 %copy-done.2 = bf16[1,256,2048]{2,1,0:T(8,128)(2,1)S(1)} copy-done((bf16[1,256,2048]{2,1,0:T(8,128)(2,1)S(1)}, bf16[1,256,2048]{2,1,0:T(8,128)(2,1)}, u32[]{:S(2)}) %copy-start.2) | copy-done | bytes 1048600
  2.6 0.0 copy-start.3
  2.6 1.2 %copy-done.3 = bf16[1,256,2048]{2,1,0:T(8,128)(2,1)S(1)} copy-done((bf16[1,256,2048]{2,1,0:T(8,128)(2,1)S(1)}, bf16[1,256,2048]{2,1,0:T(8,128)(2,1)}, u32[]{:S(2)}) %copy-start.3) | copy-done | bytes 1048600
  3.8 2.7 %shard_map.102 = (bf16[256,2048]{1,0:T(8,128)(2,1)S(1)}, bf16[256,2048]{1,0:T(8,128)(2,1)S(1)}, bf16[512,128]{1,0:T(8,128)(2,1)S(1)}, bf16[512,128]{1,0:T(8,128)...) custom-call(s32[1]{0:T(128)S(6)} %copy.11.seg_len, bf16[256,2048]{1,0:T(8,128)(2,1)S(1)} %bitcast.15, ...), custom_call_target="tpu_custom_call" | custom-call | flops 134217728 | bytes 4718596 | tf_op jit(solution)/shard_map/pallas_call | solution.py:243
  6.5 3.0 %collective-permute-start = (bf16[512,128]{1,0:T(8,128)(2,1)S(1)}, bf16[512,128]{1,0:T(8,128)(2,1)S(1)}, u32[]{:S(2)}, u32[]{:S(2)}) collective-permute-start(bf16[512,128]{1,0:T(8,128)(2,1)S(1)} %get-tuple-element.35), channel_id=1, source_target_pairs={{0,2},{1,3},{2,0},{3,1},{4,6},{5,7},{6,4},{7,5},{8,10},{9,11},{10,... | collective-permute-start | bytes 393224 | tf_op jit(solution)/shard_map/ppermute | solution.py:261
  9.6 1.5 %collective-permute-start.1 = (bf16[512,128]{1,0:T(8,128)(2,1)S(1)}, bf16[512,128]{1,0:T(8,128)(2,1)S(1)}, u32[]{:S(2)}, u32[]{:S(2)}) collective-permute-start(bf16[512,128]{1,0:T(8,128)(2,1)S(1)} %get-tuple-element.36), channel_id=1, source_target_pairs={{0,4},{1,5},{2,6},{3,7},{4,0},{5,1},{6,2},{7,3},{8,12},{9,13},{10,... | collective-permute-start | bytes 393224 | tf_op jit(solution)/shard_map/ppermute | solution.py:261
  11.1 0.0 collective-permute-start.2
  11.1 0.0 collective-permute-start.3
  11.1 2.4 %collective-permute-done.refs_1_ = bf16[512,128]{1,0:T(8,128)(2,1)S(1)} collective-permute-done((bf16[512,128]{1,0:T(8,128)(2,1)S(1)}, bf16[512,128]{1,0:T(8,128)(2,1)S(1)}, u32[]{:S(2)}, u32[]{:S(2)}) %collective-permute-start) | collective-permute-done | bytes 131104 | tf_op jit(solution)/shard_map/ppermute | solution.py:261
  13.5 0.0 collective-permute-start.4
  13.5 3.9 %collective-permute-done.1.refs_2_ = bf16[512,128]{1,0:T(8,128)(2,1)S(1)} collective-permute-done((bf16[512,128]{1,0:T(8,128)(2,1)S(1)}, bf16[512,128]{1,0:T(8,128)(2,1)S(1)}, u32[]{:S(2)}, u32[]{:S(2)}) %collective-permute-start.1) | collective-permute-done | bytes 131104 | tf_op jit(solution)/shard_map/ppermute | solution.py:261
  17.3 0.0 collective-permute-start.5
  17.3 0.0 collective-permute-done.2.refs_3_
  17.3 0.5 collective-permute-start.6
  17.8 0.0 collective-permute-done.3.refs_4_
  17.8 0.0 collective-permute-done.4.refs_5_
  17.9 0.8 %collective-permute-done.5.refs_6_ = bf16[512,128]{1,0:T(8,128)(2,1)S(1)} collective-permute-done((bf16[512,128]{1,0:T(8,128)(2,1)S(1)}, bf16[512,128]{1,0:T(8,128)(2,1)S(1)}, u32[]{:S(2)}, u32[]{:S(2)}) %collective-permute-start.5) | collective-permute-done | bytes 131104 | tf_op jit(solution)/shard_map/ppermute | solution.py:269
  18.7 0.2 collective-permute-done.6.refs_7_
  18.9 0.0 copy-done.5
  18.9 1.2 %shard_map.104 = (bf16[512,128]{1,0:T(8,128)(2,1)S(1)}, bf16[512,128]{1,0:T(8,128)(2,1)S(1)}, bf16[512,128]{1,0:T(8,128)(2,1)S(1)}, bf16[512,128]{1,0:T(8,128)(2,1)S(1)}) custom-call(s32[8]{0:T(128)S(1)} %copy-done.5, bf16[512,128]{1,0:T(8,128)(2,1)S(1)} %get-tuple-element.34.refs_0_, bf16[512,128]{1,0:T(8,128)(2,1)S(1)} %collective-permute-done.refs_1_, ...), custom_call_target="tpu_custom_call" | custom-call | bytes 1572896 | tf_op jit(solution)/shard_map/pallas_call | solution.py:243
  20.0 1.1 %collective-permute-start.7 = (bf16[512,128]{1,0:T(8,128)(2,1)S(1)}, bf16[512,128]{1,0:T(8,128)(2,1)S(1)}, u32[]{:S(2)}, u32[]{:S(2)}) collective-permute-start(bf16[512,128]{1,0:T(8,128)(2,1)S(1)} %get-tuple-element.39), channel_id=1, source_target_pairs={{0,2},{1,3},{2,0},{3,1},{4,6},{5,7},{6,4},{7,5},{8,10},{9,11},{10,... | collective-permute-start | bytes 393224 | tf_op jit(solution)/shard_map/ppermute | solution.py:261
  21.1 1.0 %collective-permute-start.8 = (bf16[512,128]{1,0:T(8,128)(2,1)S(1)}, bf16[512,128]{1,0:T(8,128)(2,1)S(1)}, u32[]{:S(2)}, u32[]{:S(2)}) collective-permute-start(bf16[512,128]{1,0:T(8,128)(2,1)S(1)} %get-tuple-element.40), channel_id=1, source_target_pairs={{0,4},{1,5},{2,6},{3,7},{4,0},{5,1},{6,2},{7,3},{8,12},{9,13},{10,... | collective-permute-start | bytes 393224 | tf_op jit(solution)/shard_map/ppermute | solution.py:261
  22.1 1.4 %collective-permute-start.9 = (bf16[512,128]{1,0:T(8,128)(2,1)S(1)}, bf16[512,128]{1,0:T(8,128)(2,1)S(1)}, u32[]{:S(2)}, u32[]{:S(2)}) collective-permute-start(bf16[512,128]{1,0:T(8,128)(2,1)S(1)} %get-tuple-element.41), channel_id=1, source_target_pairs={{0,6},{1,7},{2,4},{3,5},{4,2},{5,3},{6,0},{7,1},{8,14},{9,15},{10,... | collective-permute-start | bytes 393224 | tf_op jit(solution)/shard_map/ppermute | solution.py:261
  23.6 0.0 copy-done
  23.6 1.5 %shard_map.103.local = f32[256,2048]{1,0:T(8,128)S(1)} custom-call(s32[1]{0:T(128)S(6)} %copy.11.seg_len, bf16[256,2048]{1,0:T(8,128)(2,1)S(1)} %bitcast.9, bf16[256,2048]{1,0:T(8,128)(2,1)S(1)} %get-tuple-element.32.keys, bf16[256,2048]{1,0:T(8,128)(2,1)S(1)} %get-tuple-element.33.values), custom_call_target="tpu_custom_call" | custom-call | flops 536870912 | bytes 5242884 | tf_op jit(solution)/shard_map/pallas_call | solution.py:243
  25.1 1.3 %collective-permute-done.7.rest_1_ = bf16[512,128]{1,0:T(8,128)(2,1)S(1)} collective-permute-done((bf16[512,128]{1,0:T(8,128)(2,1)S(1)}, bf16[512,128]{1,0:T(8,128)(2,1)S(1)}, u32[]{:S(2)}, u32[]{:S(2)}) %collective-permute-start.7) | collective-permute-done | bytes 131104 | tf_op jit(solution)/shard_map/ppermute | solution.py:261
  26.4 1.5 %collective-permute-done.8.rest_2_ = bf16[512,128]{1,0:T(8,128)(2,1)S(1)} collective-permute-done((bf16[512,128]{1,0:T(8,128)(2,1)S(1)}, bf16[512,128]{1,0:T(8,128)(2,1)S(1)}, u32[]{:S(2)}, u32[]{:S(2)}) %collective-permute-start.8) | collective-permute-done | bytes 131104 | tf_op jit(solution)/shard_map/ppermute | solution.py:261
  27.9 1.6 %collective-permute-done.9.rest_3_ = bf16[512,128]{1,0:T(8,128)(2,1)S(1)} collective-permute-done((bf16[512,128]{1,0:T(8,128)(2,1)S(1)}, bf16[512,128]{1,0:T(8,128)(2,1)S(1)}, u32[]{:S(2)}, u32[]{:S(2)}) %collective-permute-start.9) | collective-permute-done | bytes 131104 | tf_op jit(solution)/shard_map/ppermute | solution.py:261
  29.5 0.0 copy-done.1
  29.5 0.0 copy-done.4
  29.5 1.0 %shard_map.105 = (f32[256,2048]{1,0:T(8,128)S(1)}, f32[2,256]{1,0:T(2,128)S(1)}) custom-call(s32[1]{0:T(128)S(6)} %copy.11.seg_len, bf16[256,2048]{1,0:T(8,128)(2,1)S(1)} %bitcast.10, f32[256,2048]{1,0:T(8,128)S(1)} %shard_map.103.local, bf16[256,2048]{1,0:T(8,128)(2,1)S(1)} %bitcast.13, f32[1,2048]{1,0:T(1,128)S(1)} %bitcast.17, ...), custom_call_target="tpu_custom_call" | custom-call | flops 134217728 | bytes 6825988 | tf_op jit(solution)/shard_map/pallas_call | solution.py:243
  30.5 3.7 %collective-permute-start.12 = (f32[2,256]{1,0:T(2,128)S(1)}, f32[2,256]{1,0:T(2,128)S(1)}, u32[]{:S(2)}, u32[]{:S(2)}) collective-permute-start(f32[2,256]{1,0:T(2,128)S(1)} %get-tuple-element.43.rest_0_), channel_id=1, source_target_pairs={{0,24},{8,16},{16,8},{24,0},{1,25},{9,17},{17,9},{25,1},{2,26},{10... | collective-permute-start | bytes 6152 | tf_op jit(solution)/shard_map/ppermute | solution.py:276
  34.2 0.0 collective-permute-start.11
  34.2 0.8 %collective-permute-start.10 = (f32[2,256]{1,0:T(2,128)S(1)}, f32[2,256]{1,0:T(2,128)S(1)}, u32[]{:S(2)}, u32[]{:S(2)}) collective-permute-start(f32[2,256]{1,0:T(2,128)S(1)} %get-tuple-element.43.rest_0_), channel_id=1, source_target_pairs={{0,8},{8,0},{16,24},{24,16},{1,9},{9,1},{17,25},{25,17},{2,10},{10... | collective-permute-start | bytes 6152 | tf_op jit(solution)/shard_map/ppermute | solution.py:276
  35.0 1.0 %collective-permute-done.12.rest_3_ = f32[2,256]{1,0:T(2,128)S(1)} collective-permute-done((f32[2,256]{1,0:T(2,128)S(1)}, f32[2,256]{1,0:T(2,128)S(1)}, u32[]{:S(2)}, u32[]{:S(2)}) %collective-permute-start.12) | collective-permute-done | bytes 2080 | tf_op jit(solution)/shard_map/ppermute | solution.py:276
  36.0 2.7 %collective-permute-done.11.rest_2_ = f32[2,256]{1,0:T(2,128)S(1)} collective-permute-done((f32[2,256]{1,0:T(2,128)S(1)}, f32[2,256]{1,0:T(2,128)S(1)}, u32[]{:S(2)}, u32[]{:S(2)}) %collective-permute-start.11) | collective-permute-done | bytes 2080 | tf_op jit(solution)/shard_map/ppermute | solution.py:276
  38.7 0.0 collective-permute-done.10.rest_1_
  38.7 1.0 %shard_map.106 = (bf16[256,2048]{1,0:T(8,128)(2,1)S(1)}, f32[1,256]{1,0:T(1,128)S(1)}, bf16[512,128]{1,0:T(8,128)(2,1)S(1)}, bf16[512,128]{1,0:T(8,128)(2,1)S(1)...) custom-call(s32[1]{0:T(128)S(6)} %copy.11.seg_len, bf16[256,2048]{1,0:T(8,128)(2,1)S(1)} %bitcast.11, ...), custom_call_target="tpu_custom_call" | custom-call | flops 134217728 | bytes 5784580 | tf_op jit(solution)/shard_map/pallas_call | solution.py:243
  39.7 0.9 %collective-permute-start.13 = (bf16[512,128]{1,0:T(8,128)(2,1)S(1)}, bf16[512,128]{1,0:T(8,128)(2,1)S(1)}, u32[]{:S(2)}, u32[]{:S(2)}) collective-permute-start(bf16[512,128]{1,0:T(8,128)(2,1)S(1)} %get-tuple-element.51), channel_id=1, source_target_pairs={{0,2},{1,3},{2,0},{3,1},{4,6},{5,7},{6,4},{7,5},{8,10},{9,11},{10,... | collective-permute-start | bytes 393224 | tf_op jit(solution)/shard_map/ppermute | solution.py:261
  40.5 1.5 %collective-permute-start.14 = (bf16[512,128]{1,0:T(8,128)(2,1)S(1)}, bf16[512,128]{1,0:T(8,128)(2,1)S(1)}, u32[]{:S(2)}, u32[]{:S(2)}) collective-permute-start(bf16[512,128]{1,0:T(8,128)(2,1)S(1)} %get-tuple-element.52), channel_id=1, source_target_pairs={{0,4},{1,5},{2,6},{3,7},{4,0},{5,1},{6,2},{7,3},{8,12},{9,13},{10,... | collective-permute-start | bytes 393224 | tf_op jit(solution)/shard_map/ppermute | solution.py:261
  42.0 1.2 %collective-permute-start.15 = (bf16[512,128]{1,0:T(8,128)(2,1)S(1)}, bf16[512,128]{1,0:T(8,128)(2,1)S(1)}, u32[]{:S(2)}, u32[]{:S(2)}) collective-permute-start(bf16[512,128]{1,0:T(8,128)(2,1)S(1)} %get-tuple-element.53), channel_id=1, source_target_pairs={{0,6},{1,7},{2,4},{3,5},{4,2},{5,3},{6,0},{7,1},{8,14},{9,15},{10,... | collective-permute-start | bytes 393224 | tf_op jit(solution)/shard_map/ppermute | solution.py:261
  43.2 0.0 collective-permute-start.16
  43.2 1.5 %collective-permute-done.13.refs_1_ = bf16[512,128]{1,0:T(8,128)(2,1)S(1)} collective-permute-done((bf16[512,128]{1,0:T(8,128)(2,1)S(1)}, bf16[512,128]{1,0:T(8,128)(2,1)S(1)}, u32[]{:S(2)}, u32[]{:S(2)}) %collective-permute-start.13) | collective-permute-done | bytes 131104 | tf_op jit(solution)/shard_map/ppermute | solution.py:261
  44.7 0.0 collective-permute-start.17
  44.7 0.8 %collective-permute-done.14.refs_2_ = bf16[512,128]{1,0:T(8,128)(2,1)S(1)} collective-permute-done((bf16[512,128]{1,0:T(8,128)(2,1)S(1)}, bf16[512,128]{1,0:T(8,128)(2,1)S(1)}, u32[]{:S(2)}, u32[]{:S(2)}) %collective-permute-start.14) | collective-permute-done | bytes 131104 | tf_op jit(solution)/shard_map/ppermute | solution.py:261
  45.5 0.0 collective-permute-start.18
  45.5 2.4 %collective-permute-done.15.refs_3_ = bf16[512,128]{1,0:T(8,128)(2,1)S(1)} collective-permute-done((bf16[512,128]{1,0:T(8,128)(2,1)S(1)}, bf16[512,128]{1,0:T(8,128)(2,1)S(1)}, u32[]{:S(2)}, u32[]{:S(2)}) %collective-permute-start.15) | collective-permute-done | bytes 131104 | tf_op jit(solution)/shard_map/ppermute | solution.py:261
  47.9 0.0 collective-permute-start.19
  47.9 0.0 collective-permute-done.16.refs_4_
  47.9 0.0 collective-permute-done.17.refs_5_
  47.9 0.0 collective-permute-done.18.refs_6_
  47.9 1.3 %collective-permute-done.19.refs_7_ = bf16[512,128]{1,0:T(8,128)(2,1)S(1)} collective-permute-done((bf16[512,128]{1,0:T(8,128)(2,1)S(1)}, bf16[512,128]{1,0:T(8,128)(2,1)S(1)}, u32[]{:S(2)}, u32[]{:S(2)}) %collective-permute-start.19) | collective-permute-done | bytes 131104 | tf_op jit(solution)/shard_map/ppermute | solution.py:269
  49.3 1.2 %shard_map.109 = (bf16[512,128]{1,0:T(8,128)(2,1)S(1)}, bf16[512,128]{1,0:T(8,128)(2,1)S(1)}, bf16[512,128]{1,0:T(8,128)(2,1)S(1)}, bf16[512,128]{1,0:T(8,128)(2,1)S(1)}) custom-call(s32[8]{0:T(128)S(1)} %copy-done.5, bf16[512,128]{1,0:T(8,128)(2,1)S(1)} %get-tuple-element.50.refs_0_, bf16[512,128]{1,0:T(8,128)(2,1)S(1)} %collective-permute-done.13.refs_1_, ...), custom_call_target="tpu_custom_call" | custom-call | bytes 1572896 | tf_op jit(solution)/shard_map/pallas_call | solution.py:243
  50.5 0.6 collective-permute-start.20
  51.1 1.2 %collective-permute-start.21 = (bf16[512,128]{1,0:T(8,128)(2,1)S(1)}, bf16[512,128]{1,0:T(8,128)(2,1)S(1)}, u32[]{:S(2)}, u32[]{:S(2)}) collective-permute-start(bf16[512,128]{1,0:T(8,128)(2,1)S(1)} %get-tuple-element.56), channel_id=1, source_target_pairs={{0,4},{1,5},{2,6},{3,7},{4,0},{5,1},{6,2},{7,3},{8,12},{9,13},{10,... | collective-permute-start | bytes 393224 | tf_op jit(solution)/shard_map/ppermute | solution.py:261
  52.3 1.8 %collective-permute-start.22 = (bf16[512,128]{1,0:T(8,128)(2,1)S(1)}, bf16[512,128]{1,0:T(8,128)(2,1)S(1)}, u32[]{:S(2)}, u32[]{:S(2)}) collective-permute-start(bf16[512,128]{1,0:T(8,128)(2,1)S(1)} %get-tuple-element.57), channel_id=1, source_target_pairs={{0,6},{1,7},{2,4},{3,5},{4,2},{5,3},{6,0},{7,1},{8,14},{9,15},{10,... | collective-permute-start | bytes 393224 | tf_op jit(solution)/shard_map/ppermute | solution.py:261
  54.1 4.5 %shard_map.107 = (bf16[256,2048]{1,0:T(8,128)(2,1)}, bf16[256,2048]{1,0:T(8,128)(2,1)}) custom-call(s32[1]{0:T(128)S(6)} %copy.11.seg_len, bf16[256,2048]{1,0:T(8,128)(2,1)S(1)} %get-tuple-element.32.keys, bf16[256,2048]{1,0:T(8,128)(2,1)S(1)} %get-tuple-element.33.values, bf16[256,2048]{1,0:T(8,128)(2,1)S(1)} %get-tuple-element.44.grad_out, ...), custom_call_target="tpu_custom_call" | custom-call | flops 671088640 | bytes 7873540 | tf_op jit(solution)/shard_map/pallas_call | solution.py:243
  58.6 2.6 %shard_map.108 = (f32[256,2048]{1,0:T(8,128)S(1)}, f32[256,2048]{1,0:T(8,128)S(1)}) custom-call(s32[1]{0:T(128)S(6)} %copy.11.seg_len, bf16[256,2048]{1,0:T(8,128)(2,1)S(1)} %bitcast.12, bf16[256,2048]{1,0:T(8,128)(2,1)S(1)} %get-tuple-element.32.keys, bf16[256,2048]{1,0:T(8,128)(2,1)S(1)} %get-tuple-element.33.values, ...), custom_call_target="tpu_custom_call" | custom-call | flops 1073741824 | bytes 8388612 | tf_op jit(solution)/shard_map/pallas_call | solution.py:243
  61.2 0.0 collective-permute-done.20.rest_1_
  61.2 0.0 collective-permute-done.21.rest_2_
  61.2 0.0 collective-permute-done.22.rest_3_
  61.2 2.2 %shard_map.110 = (bf16[256,2048]{1,0:T(8,128)(2,1)}, bf16[256,2048]{1,0:T(8,128)(2,1)}) custom-call(s32[1]{0:T(128)S(6)} %copy.11.seg_len, bf16[256,2048]{1,0:T(8,128)(2,1)S(1)} %get-tuple-element.32.keys, bf16[256,2048]{1,0:T(8,128)(2,1)S(1)} %get-tuple-element.33.values, f32[256,2048]{1,0:T(8,128)S(1)} %get-tuple-element.48.key_part, ...), custom_call_target="tpu_custom_call" | custom-call | flops 268435456 | bytes 8912900 | tf_op jit(solution)/shard_map/pallas_call | solution.py:243
  (3 shorter events, 0.0 us)
Async XLA Ops:
  0.6 23.0 %copy-start = (bf16[1,256,2048]{2,1,0:T(8,128)(2,1)S(1)}, bf16[1,256,2048]{2,1,0:T(8,128)(2,1)}, u32[]{:S(2)}) copy-start(bf16[1,256,2048]{2,1,0:T(8,128)(2,1)} %param.7) | copy-start | bytes 3145732
  1.4 1.2 %copy-start.2 = (bf16[1,256,2048]{2,1,0:T(8,128)(2,1)S(1)}, bf16[1,256,2048]{2,1,0:T(8,128)(2,1)}, u32[]{:S(2)}) copy-start(bf16[1,256,2048]{2,1,0:T(8,128)(2,1)} %param.8) | copy-start | bytes 3145732
  2.6 1.2 %copy-start.3 = (bf16[1,256,2048]{2,1,0:T(8,128)(2,1)S(1)}, bf16[1,256,2048]{2,1,0:T(8,128)(2,1)}, u32[]{:S(2)}) copy-start(bf16[1,256,2048]{2,1,0:T(8,128)(2,1)} %param.9) | copy-start | bytes 3145732
  3.8 15.0 %copy-start.5 = (s32[8]{0:T(128)S(1)}, s32[8]{0:T(128)}, u32[]{:S(2)}) copy-start(s32[8]{0:T(128)} %parent.3) | copy-start | bytes 100
  6.5 6.9 %collective-permute-start = (bf16[512,128]{1,0:T(8,128)(2,1)S(1)}, bf16[512,128]{1,0:T(8,128)(2,1)S(1)}, u32[]{:S(2)}, u32[]{:S(2)}) collective-permute-start(bf16[512,128]{1,0:T(8,128)(2,1)S(1)} %get-tuple-element.35), channel_id=1, source_target_pairs={{0,2},{1,3},{2,0},{3,1},{4,6},{5,7},{6,4},{7,5},{8,10},{9,11},{10,... | collective-permute-start | bytes 393224 | tf_op jit(solution)/shard_map/ppermute | solution.py:261
  9.6 7.8 %collective-permute-start.1 = (bf16[512,128]{1,0:T(8,128)(2,1)S(1)}, bf16[512,128]{1,0:T(8,128)(2,1)S(1)}, u32[]{:S(2)}, u32[]{:S(2)}) collective-permute-start(bf16[512,128]{1,0:T(8,128)(2,1)S(1)} %get-tuple-element.36), channel_id=1, source_target_pairs={{0,4},{1,5},{2,6},{3,7},{4,0},{5,1},{6,2},{7,3},{8,12},{9,13},{10,... | collective-permute-start | bytes 393224 | tf_op jit(solution)/shard_map/ppermute | solution.py:261
  11.1 6.3 %collective-permute-start.2 = (bf16[512,128]{1,0:T(8,128)(2,1)S(1)}, bf16[512,128]{1,0:T(8,128)(2,1)S(1)}, u32[]{:S(2)}, u32[]{:S(2)}) collective-permute-start(bf16[512,128]{1,0:T(8,128)(2,1)S(1)} %get-tuple-element.37), channel_id=1, source_target_pairs={{0,6},{1,7},{2,4},{3,5},{4,2},{5,3},{6,0},{7,1},{8,14},{9,15},{10,... | collective-permute-start | bytes 393224 | tf_op jit(solution)/shard_map/ppermute | solution.py:261
  11.1 6.8 %collective-permute-start.3 = (bf16[512,128]{1,0:T(8,128)(2,1)S(1)}, bf16[512,128]{1,0:T(8,128)(2,1)S(1)}, u32[]{:S(2)}, u32[]{:S(2)}) collective-permute-start(bf16[512,128]{1,0:T(8,128)(2,1)S(1)} %get-tuple-element.34.refs_0_), channel_id=1, source_target_pairs={{0,1},{1,0},{2,3},{3,2},{4,5},{5,4},{6,7},{7,6},{8,9},{9,8},{10,11... | collective-permute-start | bytes 393224 | tf_op jit(solution)/shard_map/ppermute | solution.py:269
  13.5 4.4 %collective-permute-start.4 = (bf16[512,128]{1,0:T(8,128)(2,1)S(1)}, bf16[512,128]{1,0:T(8,128)(2,1)S(1)}, u32[]{:S(2)}, u32[]{:S(2)}) collective-permute-start(bf16[512,128]{1,0:T(8,128)(2,1)S(1)} %collective-permute-done.refs_1_), channel_id=1, source_target_pairs={{0,1},{1,0},{2,3},{3,2},{4,5},{5,4},{6,7},{7,6},{8,9},{9,8},{10,11... | collective-permute-start | bytes 393224 | tf_op jit(solution)/shard_map/ppermute | solution.py:269
  17.3 1.3 %collective-permute-start.5 = (bf16[512,128]{1,0:T(8,128)(2,1)S(1)}, bf16[512,128]{1,0:T(8,128)(2,1)S(1)}, u32[]{:S(2)}, u32[]{:S(2)}) collective-permute-start(bf16[512,128]{1,0:T(8,128)(2,1)S(1)} %collective-permute-done.1.refs_2_), channel_id=1, source_target_pairs={{0,1},{1,0},{2,3},{3,2},{4,5},{5,4},{6,7},{7,6},{8,9},{9,8},{10,11... | collective-permute-start | bytes 393224 | tf_op jit(solution)/shard_map/ppermute | solution.py:269
  17.3 1.5 %collective-permute-start.6 = (bf16[512,128]{1,0:T(8,128)(2,1)S(1)}, bf16[512,128]{1,0:T(8,128)(2,1)S(1)}, u32[]{:S(2)}, u32[]{:S(2)}) collective-permute-start(bf16[512,128]{1,0:T(8,128)(2,1)S(1)} %collective-permute-done.2.refs_3_), channel_id=1, source_target_pairs={{0,1},{1,0},{2,3},{3,2},{4,5},{5,4},{6,7},{7,6},{8,9},{9,8},{10,11... | collective-permute-start | bytes 393224 | tf_op jit(solution)/shard_map/ppermute | solution.py:269
  20.0 6.4 %collective-permute-start.7 = (bf16[512,128]{1,0:T(8,128)(2,1)S(1)}, bf16[512,128]{1,0:T(8,128)(2,1)S(1)}, u32[]{:S(2)}, u32[]{:S(2)}) collective-permute-start(bf16[512,128]{1,0:T(8,128)(2,1)S(1)} %get-tuple-element.39), channel_id=1, source_target_pairs={{0,2},{1,3},{2,0},{3,1},{4,6},{5,7},{6,4},{7,5},{8,10},{9,11},{10,... | collective-permute-start | bytes 393224 | tf_op jit(solution)/shard_map/ppermute | solution.py:261
  21.1 6.8 %collective-permute-start.8 = (bf16[512,128]{1,0:T(8,128)(2,1)S(1)}, bf16[512,128]{1,0:T(8,128)(2,1)S(1)}, u32[]{:S(2)}, u32[]{:S(2)}) collective-permute-start(bf16[512,128]{1,0:T(8,128)(2,1)S(1)} %get-tuple-element.40), channel_id=1, source_target_pairs={{0,4},{1,5},{2,6},{3,7},{4,0},{5,1},{6,2},{7,3},{8,12},{9,13},{10,... | collective-permute-start | bytes 393224 | tf_op jit(solution)/shard_map/ppermute | solution.py:261
  22.1 7.4 %collective-permute-start.9 = (bf16[512,128]{1,0:T(8,128)(2,1)S(1)}, bf16[512,128]{1,0:T(8,128)(2,1)S(1)}, u32[]{:S(2)}, u32[]{:S(2)}) collective-permute-start(bf16[512,128]{1,0:T(8,128)(2,1)S(1)} %get-tuple-element.41), channel_id=1, source_target_pairs={{0,6},{1,7},{2,4},{3,5},{4,2},{5,3},{6,0},{7,1},{8,14},{9,15},{10,... | collective-permute-start | bytes 393224 | tf_op jit(solution)/shard_map/ppermute | solution.py:261
  23.6 5.9 %copy-start.1 = (bf16[1,256,2048]{2,1,0:T(8,128)(2,1)S(1)}, bf16[1,256,2048]{2,1,0:T(8,128)(2,1)}, u32[]{:S(2)}) copy-start(bf16[1,256,2048]{2,1,0:T(8,128)(2,1)} %param.10) | copy-start | bytes 3145732
  23.6 5.9 %copy-start.4 = (f32[2048]{0:T(1024)S(1)}, f32[2048]{0:T(1024)}, u32[]{:S(2)}) copy-start(f32[2048]{0:T(1024)} %param.11) | copy-start | bytes 24580
  30.5 5.4 %collective-permute-start.12 = (f32[2,256]{1,0:T(2,128)S(1)}, f32[2,256]{1,0:T(2,128)S(1)}, u32[]{:S(2)}, u32[]{:S(2)}) collective-permute-start(f32[2,256]{1,0:T(2,128)S(1)} %get-tuple-element.43.rest_0_), channel_id=1, source_target_pairs={{0,24},{8,16},{16,8},{24,0},{1,25},{9,17},{17,9},{25,1},{2,26},{10... | collective-permute-start | bytes 6152 | tf_op jit(solution)/shard_map/ppermute | solution.py:276
  34.2 4.5 %collective-permute-start.11 = (f32[2,256]{1,0:T(2,128)S(1)}, f32[2,256]{1,0:T(2,128)S(1)}, u32[]{:S(2)}, u32[]{:S(2)}) collective-permute-start(f32[2,256]{1,0:T(2,128)S(1)} %get-tuple-element.43.rest_0_), channel_id=1, source_target_pairs={{0,16},{8,24},{16,0},{24,8},{1,17},{9,25},{17,1},{25,9},{2,18},{10... | collective-permute-start | bytes 6152 | tf_op jit(solution)/shard_map/ppermute | solution.py:276
  34.2 4.5 %collective-permute-start.10 = (f32[2,256]{1,0:T(2,128)S(1)}, f32[2,256]{1,0:T(2,128)S(1)}, u32[]{:S(2)}, u32[]{:S(2)}) collective-permute-start(f32[2,256]{1,0:T(2,128)S(1)} %get-tuple-element.43.rest_0_), channel_id=1, source_target_pairs={{0,8},{8,0},{16,24},{24,16},{1,9},{9,1},{17,25},{25,17},{2,10},{10... | collective-permute-start | bytes 6152 | tf_op jit(solution)/shard_map/ppermute | solution.py:276
  39.7 5.0 %collective-permute-start.13 = (bf16[512,128]{1,0:T(8,128)(2,1)S(1)}, bf16[512,128]{1,0:T(8,128)(2,1)S(1)}, u32[]{:S(2)}, u32[]{:S(2)}) collective-permute-start(bf16[512,128]{1,0:T(8,128)(2,1)S(1)} %get-tuple-element.51), channel_id=1, source_target_pairs={{0,2},{1,3},{2,0},{3,1},{4,6},{5,7},{6,4},{7,5},{8,10},{9,11},{10,... | collective-permute-start | bytes 393224 | tf_op jit(solution)/shard_map/ppermute | solution.py:261
  40.5 5.0 %collective-permute-start.14 = (bf16[512,128]{1,0:T(8,128)(2,1)S(1)}, bf16[512,128]{1,0:T(8,128)(2,1)S(1)}, u32[]{:S(2)}, u32[]{:S(2)}) collective-permute-start(bf16[512,128]{1,0:T(8,128)(2,1)S(1)} %get-tuple-element.52), channel_id=1, source_target_pairs={{0,4},{1,5},{2,6},{3,7},{4,0},{5,1},{6,2},{7,3},{8,12},{9,13},{10,... | collective-permute-start | bytes 393224 | tf_op jit(solution)/shard_map/ppermute | solution.py:261
  42.0 5.9 %collective-permute-start.15 = (bf16[512,128]{1,0:T(8,128)(2,1)S(1)}, bf16[512,128]{1,0:T(8,128)(2,1)S(1)}, u32[]{:S(2)}, u32[]{:S(2)}) collective-permute-start(bf16[512,128]{1,0:T(8,128)(2,1)S(1)} %get-tuple-element.53), channel_id=1, source_target_pairs={{0,6},{1,7},{2,4},{3,5},{4,2},{5,3},{6,0},{7,1},{8,14},{9,15},{10,... | collective-permute-start | bytes 393224 | tf_op jit(solution)/shard_map/ppermute | solution.py:261
  43.2 4.7 %collective-permute-start.16 = (bf16[512,128]{1,0:T(8,128)(2,1)S(1)}, bf16[512,128]{1,0:T(8,128)(2,1)S(1)}, u32[]{:S(2)}, u32[]{:S(2)}) collective-permute-start(bf16[512,128]{1,0:T(8,128)(2,1)S(1)} %get-tuple-element.50.refs_0_), channel_id=1, source_target_pairs={{0,1},{1,0},{2,3},{3,2},{4,5},{5,4},{6,7},{7,6},{8,9},{9,8},{10,11... | collective-permute-start | bytes 393224 | tf_op jit(solution)/shard_map/ppermute | solution.py:269
  44.7 3.2 %collective-permute-start.17 = (bf16[512,128]{1,0:T(8,128)(2,1)S(1)}, bf16[512,128]{1,0:T(8,128)(2,1)S(1)}, u32[]{:S(2)}, u32[]{:S(2)}) collective-permute-start(bf16[512,128]{1,0:T(8,128)(2,1)S(1)} %collective-permute-done.13.refs_1_), channel_id=1, source_target_pairs={{0,1},{1,0},{2,3},{3,2},{4,5},{5,4},{6,7},{7,6},{8,9},{9,8},{10,11... | collective-permute-start | bytes 393224 | tf_op jit(solution)/shard_map/ppermute | solution.py:269
  45.5 2.4 %collective-permute-start.18 = (bf16[512,128]{1,0:T(8,128)(2,1)S(1)}, bf16[512,128]{1,0:T(8,128)(2,1)S(1)}, u32[]{:S(2)}, u32[]{:S(2)}) collective-permute-start(bf16[512,128]{1,0:T(8,128)(2,1)S(1)} %collective-permute-done.14.refs_2_), channel_id=1, source_target_pairs={{0,1},{1,0},{2,3},{3,2},{4,5},{5,4},{6,7},{7,6},{8,9},{9,8},{10,11... | collective-permute-start | bytes 393224 | tf_op jit(solution)/shard_map/ppermute | solution.py:269
  47.9 1.3 %collective-permute-start.19 = (bf16[512,128]{1,0:T(8,128)(2,1)S(1)}, bf16[512,128]{1,0:T(8,128)(2,1)S(1)}, u32[]{:S(2)}, u32[]{:S(2)}) collective-permute-start(bf16[512,128]{1,0:T(8,128)(2,1)S(1)} %collective-permute-done.15.refs_3_), channel_id=1, source_target_pairs={{0,1},{1,0},{2,3},{3,2},{4,5},{5,4},{6,7},{7,6},{8,9},{9,8},{10,11... | collective-permute-start | bytes 393224 | tf_op jit(solution)/shard_map/ppermute | solution.py:269
  50.5 10.6 %collective-permute-start.20 = (bf16[512,128]{1,0:T(8,128)(2,1)S(1)}, bf16[512,128]{1,0:T(8,128)(2,1)S(1)}, u32[]{:S(2)}, u32[]{:S(2)}) collective-permute-start(bf16[512,128]{1,0:T(8,128)(2,1)S(1)} %get-tuple-element.55), channel_id=1, source_target_pairs={{0,2},{1,3},{2,0},{3,1},{4,6},{5,7},{6,4},{7,5},{8,10},{9,11},{10,... | collective-permute-start | bytes 393224 | tf_op jit(solution)/shard_map/ppermute | solution.py:261
  51.1 10.0 %collective-permute-start.21 = (bf16[512,128]{1,0:T(8,128)(2,1)S(1)}, bf16[512,128]{1,0:T(8,128)(2,1)S(1)}, u32[]{:S(2)}, u32[]{:S(2)}) collective-permute-start(bf16[512,128]{1,0:T(8,128)(2,1)S(1)} %get-tuple-element.56), channel_id=1, source_target_pairs={{0,4},{1,5},{2,6},{3,7},{4,0},{5,1},{6,2},{7,3},{8,12},{9,13},{10,... | collective-permute-start | bytes 393224 | tf_op jit(solution)/shard_map/ppermute | solution.py:261
  52.3 8.9 %collective-permute-start.22 = (bf16[512,128]{1,0:T(8,128)(2,1)S(1)}, bf16[512,128]{1,0:T(8,128)(2,1)S(1)}, u32[]{:S(2)}, u32[]{:S(2)}) collective-permute-start(bf16[512,128]{1,0:T(8,128)(2,1)S(1)} %get-tuple-element.57), channel_id=1, source_target_pairs={{0,6},{1,7},{2,4},{3,5},{4,2},{5,3},{6,0},{7,1},{8,14},{9,15},{10,... | collective-permute-start | bytes 393224 | tf_op jit(solution)/shard_map/ppermute | solution.py:261

commit v4 on v3

v4 whole, which is shorter than its diff:
```python
import functools
import math

import jax
import jax.numpy as jnp
from jax import lax
from jax.experimental import pallas as pl
from jax.experimental.pallas import tpu as pltpu
from jax.sharding import PartitionSpec as P

HEADS = 64
HD = 128
EPSILON = 1e-06
F32 = jnp.float32
BF16 = jnp.bfloat16
VMEM_LIMIT = 24 * 1024 * 1024

VMEM = pl.BlockSpec(memory_space=pltpu.VMEM)
SMEM = pl.BlockSpec(memory_space=pltpu.SMEM)
HBM = pl.BlockSpec(memory_space=pltpu.HBM)


def dot(a, b, contract):
    return lax.dot_general(a, b, (contract, ((), ())), preferred_element_type=F32)


def nn(a, b):
    return dot(a, b, ((1,), (0,)))


def nt(a, b):
    return dot(a, b, ((1,), (1,)))


def tn(a, b):
    return dot(a, b, ((0,), (0,)))


def head_cols(head):
    return slice(head * HD, (head + 1) * HD)


def target_of(place, step, size):
    if size & (size - 1) == 0:
        return place ^ step
    return (place + step) % size


def source_of(place, step, size):
    if size & (size - 1) == 0:
        return place ^ step
    return (place + size - step) % size


def grid_of(segs):
    pair = 2 if segs % 2 == 0 else 1
    chips = segs // pair
    columns = next(c for c in range(1, chips + 1) if chips % c == 0 and c * c >= chips)
    return chips // columns, columns, pair


def member(grid, row, column, core):
    return (row * grid[1] + column) * grid[2] + core


def place_of(grid, device):
    chip = device // grid[2]
    return chip // grid[1], chip % grid[1], device % grid[2]


def along(grid, place, step, gather, ahead):
    row, column, core = place
    shift = target_of if ahead else source_of
    by_row = (core == 0) if gather else (core != 0)
    valid_column = step < grid[1]
    valid_row = step < grid[0]
    if isinstance(core, int):
        if by_row:
            return row, shift(column, step, grid[1]), valid_column
        return shift(row, step, grid[0]), column, valid_row
    moved_column = shift(column, min(step, grid[1] - 1), grid[1])
    moved_row = shift(row, min(step, grid[0] - 1), grid[0])
    return (
        jnp.where(by_row, row, moved_row),
        jnp.where(by_row, moved_column, column),
        jnp.where(by_row, valid_column, valid_row),
    )


def my_place(grid):
    me = lax.axis_index("seg")
    chip = lax.div(me, grid[2])
    return lax.div(chip, grid[1]), lax.rem(chip, grid[1]), lax.rem(me, grid[2])


def row_halves(full, core, pair):
    half = full.shape[0] // pair
    return [full.at[pl.ds(pl.multiple_of((core ^ j) * half, half), half), :] for j in range(pair)]


def join_halves(parts, full, core, pair):
    for half, terms in zip(row_halves(full, core, pair), parts):
        total = terms[0][...].astype(F32)
        for term in terms[1:]:
            total += term[...].astype(F32)
        half[...] = total.astype(BF16)


def state_kernel(heads, grid, seg_len, keys_hbm, values_hbm, keys, values, *rest):
    outs, full, sems = rest[:-2], rest[-2], rest[-1]
    rows, features = keys.shape
    group = 2 * HD if heads % 2 == 0 else HD
    steps = features // group
    copies = []
    for step in range(steps):
        cols = slice(step * group, (step + 1) * group)
        pieces = ((keys_hbm, keys), (values_hbm, values))
        copies.append(
            [
                pltpu.make_async_copy(src.at[:, cols], dst.at[:, cols], sems.at[j, step])
                for j, (src, dst) in enumerate(pieces)
            ]
        )
    for step in copies:
        for copy in step:
            copy.start()
    live = lax.broadcasted_iota(jnp.int32, (rows, HD), 0) < seg_len[0]
    for step in range(steps):
        for copy in copies[step]:
            copy.wait()
        for head in range(step * group // HD, (step + 1) * group // HD):
            cols = head_cols(head)
            masked = jnp.where(live, keys[:, cols], jnp.zeros((), BF16))
            full[head * HD : (head + 1) * HD, :] = tn(masked, values[:, cols]).astype(BF16)
    for half, out in zip(row_halves(full, my_place(grid)[2], grid[2]), outs):
        out[...] = half[...]


def mix_kernel(grid, upward, sources, parent, *refs):
    blocks, outs = refs[:sources], refs[-line_length(grid) * grid[2] :]
    place = my_place(grid)
    pair = grid[2]

    def is_ancestor(child, other):
        first = parent[child]
        second = jnp.where(first >= 0, parent[jnp.maximum(first, 0)], -1)
        return jnp.logical_or(other == first, other == second)

    weights = []
    for out_step in range(len(outs)):
        row, column, _ = along(grid, place, out_step // pair, False, True)
        target = member(grid, row, column, place[2] ^ (out_step % pair))
        for in_step in range(sources):
            row, column, valid = along(grid, place, in_step // pair, True, False)
            source = member(grid, row, column, place[2] ^ (in_step % pair))
            used = is_ancestor(target, source) if upward else is_ancestor(source, target)
            weights.append(jnp.where(jnp.logical_and(used, valid), 1.0, 0.0))
    rows = blocks[0].shape[0]
    chunk = min(rows, 64)
    for start in range(0, rows, chunk):
        part = slice(start, start + chunk)
        loaded = [block[part, :].astype(F32) for block in blocks]
        for out_step, out in enumerate(outs):
            total = weights[out_step * sources] * loaded[0]
            for in_step in range(1, sources):
                total += weights[out_step * sources + in_step] * loaded[in_step]
            out[part, :] = total.astype(BF16)


def line_length(grid):
    return max(grid[0], grid[1])


def keep_mask(rows, length):
    token = lax.broadcasted_iota(jnp.int32, (rows, rows), 0)
    other = lax.broadcasted_iota(jnp.int32, (rows, rows), 1)
    return (other <= token) & (other < length)


def local_kernel(heads, seg_len, queries, keys, values, local):
    rows = keys.shape[0]
    keep = keep_mask(rows, seg_len[0])
    for head in range(heads):
        cols = head_cols(head)
        scores = jnp.where(keep, nt(queries[:, cols], keys[:, cols]), 0.0).astype(BF16)
        local[:, cols] = nn(scores, values[:, cols])


def token_rows(total):
    return jnp.sum(jnp.transpose(total), axis=0, keepdims=True)


def token_columns(row):
    return jnp.transpose(jnp.broadcast_to(row, (HD, row.shape[1])))


def carry_kernel(heads, grid, counts, scale, seg_len, queries, local, cotangent, gain, *rest):
    received, (attention, sums, prefix) = rest[: sum(counts)], rest[sum(counts) :]
    join_halves(by_half(received, counts), prefix, my_place(grid)[2], grid[2])
    rows = queries.shape[0]
    live = lax.broadcasted_iota(jnp.int32, (rows, HD), 0) < seg_len[0]
    factor = jnp.where(live, scale, 0.0)
    squares = jnp.zeros((rows, HD), F32)
    products = jnp.zeros((rows, HD), F32)
    for head in range(heads):
        cols = head_cols(head)
        carried = nn(queries[:, cols], prefix[head * HD : (head + 1) * HD, :])
        out = factor * (carried + local[:, cols])
        attention[:, cols] = out
        squares += out * out
        products += out * (cotangent[:, cols].astype(F32) * gain[:, cols])
    sums[0:1, :] = token_rows(squares)
    sums[1:2, :] = token_rows(products)


def grad_kernel(heads, groups, grid, scale, seg_len, queries, attention, cotangent, gain, *rest):
    all_sums, (grad_out, inverse_rms), outs, full = (
        rest[:groups], rest[groups : groups + 2], rest[groups + 2 : -1], rest[-1]
    )
    rows = queries.shape[0]
    width = HEADS * HD
    total = all_sums[0][...]
    for other in all_sums[1:]:
        total = total + other[...]
    inverse = lax.rsqrt(total[0:1, :] / width + EPSILON)
    inverse_rms[...] = inverse
    live = lax.broadcasted_iota(jnp.int32, (1, rows), 1) < seg_len[0]
    live_inverse = jnp.where(live, inverse, 0.0)
    shrink = live_inverse * inverse * (inverse * total[1:2, :]) / width
    live_inverse = token_columns(live_inverse)
    shrink = token_columns(shrink)
    for head in range(heads):
        cols = head_cols(head)
        gain_grad = cotangent[:, cols].astype(F32) * gain[:, cols]
        grad = (live_inverse * gain_grad - attention[:, cols] * shrink).astype(BF16)
        grad_out[:, cols] = grad
        full[head * HD : (head + 1) * HD, :] = (scale * tn(queries[:, cols], grad)).astype(BF16)
    for half, out in zip(row_halves(full, my_place(grid)[2], grid[2]), outs):
        out[...] = half[...]


def query_kernel(
    heads, scale, seg_len, keys, values, grad_out, attention, inverse_rms, gain, prefix, attended, query_grad
):
    keep = keep_mask(keys.shape[0], seg_len[0])
    inverse = token_columns(inverse_rms[...])
    for head in range(heads):
        cols = head_cols(head)
        grad = grad_out[:, cols]
        grad_scores = jnp.where(keep, nt(grad, values[:, cols]), 0.0).astype(BF16)
        carried = nt(grad, prefix[head * HD : (head + 1) * HD, :])
        query_grad[:, cols] = (scale * (carried + nn(grad_scores, keys[:, cols]))).astype(BF16)
        attended[:, cols] = (attention[:, cols] * inverse * gain[:, cols]).astype(BF16)


def back_kernel(heads, scale, seg_len, queries, keys, values, grad_out, key_part, value_part):
    rows = queries.shape[0]
    other = lax.broadcasted_iota(jnp.int32, (rows, rows), 0)
    token = lax.broadcasted_iota(jnp.int32, (rows, rows), 1)
    keep = (other <= token) & (other < seg_len[0])
    for head in range(heads):
        cols = head_cols(head)
        query, grad = queries[:, cols], grad_out[:, cols]
        turned = jnp.where(keep, nt(values[:, cols], grad), 0.0).astype(BF16)
        key_part[:, cols] = scale * nn(turned, query)
        turned = jnp.where(keep, nt(keys[:, cols], query), 0.0).astype(BF16)
        value_part[:, cols] = scale * nn(turned, grad)


def final_kernel(heads, grid, counts, seg_len, keys, values, key_part, value_part, *rest):
    received, (key_hbm, value_hbm, key_grad, value_grad, below, sems) = rest[: sum(counts)], rest[sum(counts) :]
    join_halves(by_half(received, counts), below, my_place(grid)[2], grid[2])
    rows = keys.shape[0]
    live = lax.broadcasted_iota(jnp.int32, (rows, HD), 0) < seg_len[0]
    live = jnp.where(live, 1.0, 0.0)
    group = 2 if heads % 2 == 0 else 1
    copies = []
    for head in range(heads):
        cols = head_cols(head)
        state = below[head * HD : (head + 1) * HD, :]
        key_grad[:, cols] = (key_part[:, cols] + live * nt(values[:, cols], state)).astype(BF16)
        value_grad[:, cols] = (value_part[:, cols] + live * nn(keys[:, cols], state)).astype(BF16)
        if (head + 1) % group == 0:
            done = slice((head + 1 - group) * HD, (head + 1) * HD)
            for j, (src, dst) in enumerate(((key_grad, key_hbm), (value_grad, value_hbm))):
                copy = pltpu.make_async_copy(src.at[:, done], dst.at[:, done], sems.at[j, head // group])
                copy.start()
                copies.append(copy)
    for copy in copies:
        copy.wait()


def call(kernel, out_shape, operands, scalars, scratch=(), flops=0, stream=0, after=(), out_specs=None):
    moved = sum(math.prod(x.shape) * x.dtype.itemsize for x in operands)
    moved += sum(math.prod(x.shape) * x.dtype.itemsize for x in out_shape)
    in_vmem = len(operands) - scalars - stream
    specs = [SMEM] * scalars + [HBM] * stream + [VMEM] * in_vmem
    return pl.pallas_call(
        kernel,
        out_shape=out_shape,
        in_specs=specs + [HBM] * len(after),
        out_specs=out_specs or [VMEM] * len(out_shape),
        scratch_shapes=list(scratch),
        compiler_params=pltpu.CompilerParams(vmem_limit_bytes=VMEM_LIMIT),
        cost_estimate=pl.CostEstimate(flops=flops, bytes_accessed=moved, transcendentals=0),
    )(*operands, *after)


def line_send(block, grid, step, flip, gather):
    moves = []
    for device in range(grid[0] * grid[1] * grid[2]):
        place = place_of(grid, device)
        if gather and flip:
            row, column, valid = along(grid, (place[0], place[1], place[2] ^ 1), step, True, True)
        else:
            row, column, valid = along(grid, place, step, gather, True)
        if valid:
            moves.append((device, member(grid, row, column, place[2] ^ flip)))
    return lax.ppermute(block, "seg", moves)


def gather_line(halves, grid):
    arrived = []
    for step in range(line_length(grid)):
        for flip in range(grid[2]):
            if step == 0 and flip == 0:
                arrived.append(halves[0])
            else:
                arrived.append(line_send(halves[flip], grid, step, flip, True))
    return arrived


def scatter_line(sums, grid):
    pair = grid[2]
    parts = [[] for _ in range(pair)]
    for step in range(line_length(grid)):
        for flip in range(pair):
            block = sums[step * pair + flip]
            if step == 0 and flip == 0:
                parts[0].append(block)
            else:
                parts[flip].append(line_send(block, grid, step, flip, False))
    return parts


def by_half(refs, counts):
    parts, at = [], 0
    for count in counts:
        parts.append(refs[at : at + count])
        at += count
    return parts


def group_sends(sums, groups):
    received = [sums]
    for step in range(1, groups):
        moves = [(j, target_of(j, step, groups)) for j in range(groups)]
        received.append(lax.ppermute(sums, "head", moves))
    return received


def per_device(segs, groups, queries, key_rows, values, cotangent, out_gain, parent, seg_len):
    rows, features = queries.shape[1:]
    heads = features // HD
    grid = grid_of(segs)
    scale = 1.0 / math.sqrt(HD * rows)
    query, cot = queries[0], cotangent[0]
    gain = out_gain[None]
    shape = jax.ShapeDtypeStruct
    narrow = shape((rows, features), BF16)
    wide = shape((rows, features), F32)
    state = shape((features, HD), BF16)
    half = shape((features // grid[2], HD), BF16)
    state_scratch = pltpu.VMEM(state.shape, BF16)
    narrow_scratch = pltpu.VMEM(narrow.shape, BF16)
    sems = pltpu.SemaphoreType.DMA((2, heads))
    members = line_length(grid) * grid[2]
    counts = [line_length(grid)] * grid[2]
    unit = 2 * heads * rows * HD

    def mix(halves, upward, after=()):
        arrived = gather_line(halves, grid)
        return call(
            functools.partial(mix_kernel, grid, upward, members),
            [half] * members, (parent, *arrived), 1, after=after,
        )

    def sums_of(parts):
        return [block for part in parts for block in part]

    key_hbm = pltpu.with_memory_space_constraint(key_rows[0], pltpu.HBM)
    value_hbm = pltpu.with_memory_space_constraint(values[0], pltpu.HBM)
    key, value, *own = call(
        functools.partial(state_kernel, heads, grid),
        [narrow, narrow] + [half] * grid[2], (seg_len, key_hbm, value_hbm), 1,
        [state_scratch, sems], unit * HD, 2,
    )
    mixed = mix(own, True)
    (local,) = call(
        functools.partial(local_kernel, heads),
        [wide], (seg_len, query, key, value), 1, (), unit * rows * 2,
    )
    attention, sums, prefix = call(
        functools.partial(carry_kernel, heads, grid, counts, scale),
        [wide, shape((2, rows), F32), state],
        (seg_len, query, local, cot, gain, *sums_of(scatter_line(mixed, grid))), 1, (), unit * HD,
    )
    grad_out, inverse_rms, *state_grad = call(
        functools.partial(grad_kernel, heads, groups, grid, scale),
        [narrow, shape((1, rows), F32)] + [half] * grid[2],
        (seg_len, query, attention, cot, gain, *group_sends(sums, groups)), 1, [state_scratch], unit * HD,
    )
    attended, query_grad = call(
        functools.partial(query_kernel, heads, scale),
        [narrow, narrow],
        (seg_len, key, value, grad_out, attention, inverse_rms, gain, prefix), 1, (),
        unit * (2 * rows + HD),
    )
    mixed = mix(state_grad, False, (pltpu.with_memory_space_constraint(attended, pltpu.HBM),))
    key_part, value_part = call(
        functools.partial(back_kernel, heads, scale),
        [wide, wide], (seg_len, query, key, value, grad_out), 1, (), unit * 4 * rows,
    )
    key_grad, value_grad = call(
        functools.partial(final_kernel, heads, grid, counts),
        [narrow, narrow],
        (seg_len, key, value, key_part, value_part, *sums_of(scatter_line(mixed, grid))), 1,
        [narrow_scratch, narrow_scratch, state_scratch, sems], 2 * unit * HD, out_specs=[HBM, HBM],
    )
    return attended[None], query_grad[None], key_grad[None], value_grad[None]


def solution(mesh):
    split = P("seg", None, "head")
    return jax.shard_map(
        functools.partial(per_device, mesh.shape["seg"], mesh.shape["head"]),
        mesh=mesh,
        in_specs=(split, split, split, split, P("head"), P(), P("seg")),
        out_specs=(split, split, split, split),
        check_vma=False,
    )
```

time: 63.7 us -> 56.4 us (0.89)
  the two profiles are of different devices: /device:TPU:0 before, /device:TPU:1 now
where the time goes in v4:
time: 56.4 us; the launch traced here: 56.2 us
  waiting for transfers between devices  18.7 us (33%)
  Pallas kernels  18.2 us (32%)
  starting transfers between devices  17.6 us (31%)
  between operations  1.62 us (3%)
    pallas_call x9, Pallas kernels, call(): pl.pallas_call(kernel, out_shape=out_shape, in_specs=specs + [HBM] * len(...  18.2 us
    ppermute x12, waiting for transfers between devices, line_send(): return lax.ppermute(block, 'seg', moves)  15.8 us
    ppermute x12, starting transfers between devices, line_send(): return lax.ppermute(block, 'seg', moves)  13.4 us
    ppermute x3, starting transfers between devices, group_sends(): received.append(lax.ppermute(sums, 'head', moves))  4.25 us
    ppermute x3, waiting for transfers between devices, group_sends(): received.append(lax.ppermute(sums, 'head', moves))  2.97 us
  transfers between devices with their start and end apart: 15, of which 7 were waited for; matrix products, arithmetic and copies ran while one was open for 0% of the time, Pallas kernels for 15%

profile of v4, /device:TPU:1, one launch (start us, length us, event | category | flops | bytes accessed | tf_op | source)
XLA Modules:
  0.0 56.2 jit_solution(17715987895226639617)
XLA Ops:
  0.6 0.0 copy-start.3
  0.6 0.0 copy-start
  1.4 3.2 %shard_map.102 = (bf16[256,2048]{1,0:T(8,128)(2,1)S(1)}, bf16[256,2048]{1,0:T(8,128)(2,1)S(1)}, bf16[1024,128]{1,0:T(8,128)(2,1)S(1)}, bf16[1024,128]{1,0:T(8,128)(2,1)S(1)}) custom-call(s32[1]{0:T(128)S(6)} %copy.11.seg_len, bf16[256,2048]{1,0:T(8,128)(2,1)} %bitcast.18, bf16[256,2048]{1,0:T(8,128)(2,1)} %bitcast.19), custom_call_target="tpu_custom_call" | custom-call | flops 134217728 | bytes 4718596 | tf_op jit(solution)/shard_map/pallas_call | solution.py:298
  4.6 2.1 %collective-permute-start.1 = (bf16[1024,128]{1,0:T(8,128)(2,1)S(1)}, bf16[1024,128]{1,0:T(8,128)(2,1)S(1)}, u32[]{:S(2)}, u32[]{:S(2)}) collective-permute-start(bf16[1024,128]{1,0:T(8,128)(2,1)S(1)} %get-tuple-element.31.refs_0_), channel_id=1, source_target_pairs={{0,2},{1,5},{2,0},{3,7},{4,6},{5,1},{6,4},{7,3},{8,10},{9,13},{10,... | collective-permute-start | bytes 786440 | tf_op jit(solution)/shard_map/ppermute | solution.py:319
  6.7 0.6 %collective-permute-start.2 = (bf16[1024,128]{1,0:T(8,128)(2,1)S(1)}, bf16[1024,128]{1,0:T(8,128)(2,1)S(1)}, u32[]{:S(2)}, u32[]{:S(2)}) collective-permute-start(bf16[1024,128]{1,0:T(8,128)(2,1)S(1)} %get-tuple-element.32), channel_id=1, source_target_pairs={{0,5},{1,2},{2,7},{3,0},{4,1},{5,6},{6,3},{7,4},{8,13},{9,10},{10,... | collective-permute-start | bytes 786440 | tf_op jit(solution)/shard_map/ppermute | solution.py:319
  7.3 0.3 collective-permute-start
  7.6 4.1 %collective-permute-done.1.refs_2_ = bf16[1024,128]{1,0:T(8,128)(2,1)S(1)} collective-permute-done((bf16[1024,128]{1,0:T(8,128)(2,1)S(1)}, bf16[1024,128]{1,0:T(8,128)(2,1)S(1)}, u32[]{:S(2)}, u32[]{:S(2)}) %collective-permute-start.1) | collective-permute-done | bytes 262176 | tf_op jit(solution)/shard_map/ppermute | solution.py:319
  11.7 1.8 %collective-permute-done.2.refs_3_ = bf16[1024,128]{1,0:T(8,128)(2,1)S(1)} collective-permute-done((bf16[1024,128]{1,0:T(8,128)(2,1)S(1)}, bf16[1024,128]{1,0:T(8,128)(2,1)S(1)}, u32[]{:S(2)}, u32[]{:S(2)}) %collective-permute-start.2) | collective-permute-done | bytes 262176 | tf_op jit(solution)/shard_map/ppermute | solution.py:319
  13.6 0.0 collective-permute-done.refs_1_
  13.6 0.0 copy-done.3
  13.6 1.1 %shard_map.104 = (bf16[1024,128]{1,0:T(8,128)(2,1)S(1)}, bf16[1024,128]{1,0:T(8,128)(2,1)S(1)}, bf16[1024,128]{1,0:T(8,128)(2,1)S(1)}, bf16[1024,128]{1,0:T(8,128)(2,1)S(1)}) custom-call(s32[8]{0:T(128)S(1)} %copy-done.3, bf16[1024,128]{1,0:T(8,128)(2,1)S(1)} %get-tuple-element.31.refs_0_, bf16[1024,128]{1,0:T(8,128)(2,1)S(1)} %collective-permute-done.refs_1_, ...), custom_call_target="tpu_custom_call" | custom-call | bytes 2097184 | tf_op jit(solution)/shard_map/pallas_call | solution.py:298
  14.7 1.5 %collective-permute-start.3 = (bf16[1024,128]{1,0:T(8,128)(2,1)S(1)}, bf16[1024,128]{1,0:T(8,128)(2,1)S(1)}, u32[]{:S(2)}, u32[]{:S(2)}) collective-permute-start(bf16[1024,128]{1,0:T(8,128)(2,1)S(1)} %get-tuple-element.34), channel_id=1, source_target_pairs={{0,4},{1,3},{2,6},{3,1},{4,0},{5,7},{6,2},{7,5},{8,12},{9,11},{10,... | collective-permute-start | bytes 786440 | tf_op jit(solution)/shard_map/ppermute | solution.py:319
  16.2 1.8 %collective-permute-start.4 = (bf16[1024,128]{1,0:T(8,128)(2,1)S(1)}, bf16[1024,128]{1,0:T(8,128)(2,1)S(1)}, u32[]{:S(2)}, u32[]{:S(2)}) collective-permute-start(bf16[1024,128]{1,0:T(8,128)(2,1)S(1)} %get-tuple-element.35), channel_id=1, source_target_pairs={{0,1},{1,0},{2,3},{3,2},{4,5},{5,4},{6,7},{7,6},{8,9},{9,8},{10,11... | collective-permute-start | bytes 786440 | tf_op jit(solution)/shard_map/ppermute | solution.py:319
  18.0 1.1 %collective-permute-start.5 = (bf16[1024,128]{1,0:T(8,128)(2,1)S(1)}, bf16[1024,128]{1,0:T(8,128)(2,1)S(1)}, u32[]{:S(2)}, u32[]{:S(2)}) collective-permute-start(bf16[1024,128]{1,0:T(8,128)(2,1)S(1)} %get-tuple-element.36), channel_id=1, source_target_pairs={{0,5},{1,2},{2,7},{3,0},{4,1},{5,6},{6,3},{7,4},{8,13},{9,10},{10,... | collective-permute-start | bytes 786440 | tf_op jit(solution)/shard_map/ppermute | solution.py:319
  19.1 0.0 copy-done
  19.1 0.0 copy-start.1
  19.1 0.0 copy-start.2
  19.1 1.5 %shard_map.103.local = f32[256,2048]{1,0:T(8,128)S(1)} custom-call(s32[1]{0:T(128)S(6)} %copy.11.seg_len, bf16[256,2048]{1,0:T(8,128)(2,1)S(1)} %bitcast.9, bf16[256,2048]{1,0:T(8,128)(2,1)S(1)} %get-tuple-element.29.keys, bf16[256,2048]{1,0:T(8,128)(2,1)S(1)} %get-tuple-element.30.values), custom_call_target="tpu_custom_call" | custom-call | flops 536870912 | bytes 5242884 | tf_op jit(solution)/shard_map/pallas_call | solution.py:298
  20.6 0.0 collective-permute-done.3.rest_1_
  20.6 0.0 collective-permute-done.4.rest_2_
  20.6 3.9 %collective-permute-done.5.rest_3_ = bf16[1024,128]{1,0:T(8,128)(2,1)S(1)} collective-permute-done((bf16[1024,128]{1,0:T(8,128)(2,1)S(1)}, bf16[1024,128]{1,0:T(8,128)(2,1)S(1)}, u32[]{:S(2)}, u32[]{:S(2)}) %collective-permute-start.5) | collective-permute-done | bytes 262176 | tf_op jit(solution)/shard_map/ppermute | solution.py:319
  24.5 0.0 copy-done.1
  24.5 0.0 copy-done.2
  24.5 1.1 %shard_map.105 = (f32[256,2048]{1,0:T(8,128)S(1)}, f32[2,256]{1,0:T(2,128)S(1)}, bf16[2048,128]{1,0:T(8,128)(2,1)S(1)}) custom-call(s32[1]{0:T(128)S(6)} %copy.11.seg_len, bf16[256,2048]{1,0:T(8,128)(2,1)S(1)} %bitcast.10, f32[256,2048]{1,0:T(8,128)S(1)} %shard_map.103.local, bf16[256,2048]{1,0:T(8,128)(2,1)S(1)} %bitcast.13, f32[1,2048]{1,0:T(1,128)S(1)} %bitcast.15, ...), custom_call_target="tpu_custom_call" | custom-call | flops 134217728 | bytes 7874564 | tf_op jit(solution)/shard_map/pallas_call | solution.py:298
  25.7 3.9 %collective-permute-start.8 = (f32[2,256]{1,0:T(2,128)S(1)}, f32[2,256]{1,0:T(2,128)S(1)}, u32[]{:S(2)}, u32[]{:S(2)}) collective-permute-start(f32[2,256]{1,0:T(2,128)S(1)} %get-tuple-element.38.rest_0_), channel_id=1, source_target_pairs={{0,24},{8,16},{16,8},{24,0},{1,25},{9,17},{17,9},{25,1},{2,26},{10... | collective-permute-start | bytes 6152 | tf_op jit(solution)/shard_map/ppermute | solution.py:358
  29.5 0.0 collective-permute-start.7
  29.6 0.4 collective-permute-start.6
  29.9 0.6 %collective-permute-done.8.rest_3_ = f32[2,256]{1,0:T(2,128)S(1)} collective-permute-done((f32[2,256]{1,0:T(2,128)S(1)}, f32[2,256]{1,0:T(2,128)S(1)}, u32[]{:S(2)}, u32[]{:S(2)}) %collective-permute-start.8) | collective-permute-done | bytes 2080 | tf_op jit(solution)/shard_map/ppermute | solution.py:358
  30.5 2.4 %collective-permute-done.7.rest_2_ = f32[2,256]{1,0:T(2,128)S(1)} collective-permute-done((f32[2,256]{1,0:T(2,128)S(1)}, f32[2,256]{1,0:T(2,128)S(1)}, u32[]{:S(2)}, u32[]{:S(2)}) %collective-permute-start.7) | collective-permute-done | bytes 2080 | tf_op jit(solution)/shard_map/ppermute | solution.py:358
  32.9 0.0 collective-permute-done.6.rest_1_
  32.9 1.0 %shard_map.106 = (bf16[256,2048]{1,0:T(8,128)(2,1)S(1)}, f32[1,256]{1,0:T(1,128)S(1)}, bf16[1024,128]{1,0:T(8,128)(2,1)S(1)}, bf16[1024,128]{1,0:T(8,128)(2,1)S(1)}) custom-call(s32[1]{0:T(128)S(6)} %copy.11.seg_len, bf16[256,2048]{1,0:T(8,128)(2,1)S(1)} %bitcast.11, f32[256,2048]{1,0:T(8,128)S(1)} %get-tuple-element.37.attention, ...), custom_call_target="tpu_custom_call" | custom-call | flops 134217728 | bytes 5784580 | tf_op jit(solution)/shard_map/pallas_call | solution.py:298
  33.9 1.3 %collective-permute-start.10 = (bf16[1024,128]{1,0:T(8,128)(2,1)S(1)}, bf16[1024,128]{1,0:T(8,128)(2,1)S(1)}, u32[]{:S(2)}, u32[]{:S(2)}) collective-permute-start(bf16[1024,128]{1,0:T(8,128)(2,1)S(1)} %get-tuple-element.46.refs_0_), channel_id=1, source_target_pairs={{0,2},{1,5},{2,0},{3,7},{4,6},{5,1},{6,4},{7,3},{8,10},{9,13},{10,... | collective-permute-start | bytes 786440 | tf_op jit(solution)/shard_map/ppermute | solution.py:319
  35.2 1.5 %collective-permute-start.11 = (bf16[1024,128]{1,0:T(8,128)(2,1)S(1)}, bf16[1024,128]{1,0:T(8,128)(2,1)S(1)}, u32[]{:S(2)}, u32[]{:S(2)}) collective-permute-start(bf16[1024,128]{1,0:T(8,128)(2,1)S(1)} %get-tuple-element.47), channel_id=1, source_target_pairs={{0,5},{1,2},{2,7},{3,0},{4,1},{5,6},{6,3},{7,4},{8,13},{9,10},{10,... | collective-permute-start | bytes 786440 | tf_op jit(solution)/shard_map/ppermute | solution.py:319
  36.7 0.0 collective-permute-start.9
  36.7 4.5 %shard_map.107 = (bf16[256,2048]{1,0:T(8,128)(2,1)}, bf16[256,2048]{1,0:T(8,128)(2,1)}) custom-call(s32[1]{0:T(128)S(6)} %copy.11.seg_len, bf16[256,2048]{1,0:T(8,128)(2,1)S(1)} %get-tuple-element.29.keys, bf16[256,2048]{1,0:T(8,128)(2,1)S(1)} %get-tuple-element.30.values, bf16[256,2048]{1,0:T(8,128)(2,1)S(1)} %get-tuple-element.39.grad_out, ...), custom_call_target="tpu_custom_call" | custom-call | flops 671088640 | bytes 7873540 | tf_op jit(solution)/shard_map/pallas_call | solution.py:298
  41.2 0.0 collective-permute-done.10.refs_2_
  41.2 1.6 %collective-permute-done.11.refs_3_ = bf16[1024,128]{1,0:T(8,128)(2,1)S(1)} collective-permute-done((bf16[1024,128]{1,0:T(8,128)(2,1)S(1)}, bf16[1024,128]{1,0:T(8,128)(2,1)S(1)}, u32[]{:S(2)}, u32[]{:S(2)}) %collective-permute-start.11) | collective-permute-done | bytes 262176 | tf_op jit(solution)/shard_map/ppermute | solution.py:319
  42.9 0.0 collective-permute-done.9.refs_1_
  42.9 1.1 %shard_map.109 = (bf16[1024,128]{1,0:T(8,128)(2,1)S(1)}, bf16[1024,128]{1,0:T(8,128)(2,1)S(1)}, bf16[1024,128]{1,0:T(8,128)(2,1)S(1)}, bf16[1024,128]{1,0:T(8,128)(2,1)S(1)}) custom-call(s32[8]{0:T(128)S(1)} %copy-done.3, bf16[1024,128]{1,0:T(8,128)(2,1)S(1)} %get-tuple-element.46.refs_0_, bf16[1024,128]{1,0:T(8,128)(2,1)S(1)} %collective-permute-done.9.refs_1_, ...), custom_call_target="tpu_custom_call" | custom-call | bytes 2097184 | tf_op jit(solution)/shard_map/pallas_call | solution.py:298
  44.0 0.7 %collective-permute-start.12 = (bf16[1024,128]{1,0:T(8,128)(2,1)S(1)}, bf16[1024,128]{1,0:T(8,128)(2,1)S(1)}, u32[]{:S(2)}, u32[]{:S(2)}) collective-permute-start(bf16[1024,128]{1,0:T(8,128)(2,1)S(1)} %get-tuple-element.49), channel_id=1, source_target_pairs={{0,4},{1,3},{2,6},{3,1},{4,0},{5,7},{6,2},{7,5},{8,12},{9,11},{10,... | collective-permute-start | bytes 786440 | tf_op jit(solution)/shard_map/ppermute | solution.py:319
  44.7 1.4 %collective-permute-start.13 = (bf16[1024,128]{1,0:T(8,128)(2,1)S(1)}, bf16[1024,128]{1,0:T(8,128)(2,1)S(1)}, u32[]{:S(2)}, u32[]{:S(2)}) collective-permute-start(bf16[1024,128]{1,0:T(8,128)(2,1)S(1)} %get-tuple-element.50), channel_id=1, source_target_pairs={{0,1},{1,0},{2,3},{3,2},{4,5},{5,4},{6,7},{7,6},{8,9},{9,8},{10,11... | collective-permute-start | bytes 786440 | tf_op jit(solution)/shard_map/ppermute | solution.py:319
  46.0 1.1 %collective-permute-start.14 = (bf16[1024,128]{1,0:T(8,128)(2,1)S(1)}, bf16[1024,128]{1,0:T(8,128)(2,1)S(1)}, u32[]{:S(2)}, u32[]{:S(2)}) collective-permute-start(bf16[1024,128]{1,0:T(8,128)(2,1)S(1)} %get-tuple-element.51), channel_id=1, source_target_pairs={{0,5},{1,2},{2,7},{3,0},{4,1},{5,6},{6,3},{7,4},{8,13},{9,10},{10,... | collective-permute-start | bytes 786440 | tf_op jit(solution)/shard_map/ppermute | solution.py:319
  47.1 2.6 %shard_map.108 = (f32[256,2048]{1,0:T(8,128)S(1)}, f32[256,2048]{1,0:T(8,128)S(1)}) custom-call(s32[1]{0:T(128)S(6)} %copy.11.seg_len, bf16[256,2048]{1,0:T(8,128)(2,1)S(1)} %bitcast.12, bf16[256,2048]{1,0:T(8,128)(2,1)S(1)} %get-tuple-element.29.keys, bf16[256,2048]{1,0:T(8,128)(2,1)S(1)} %get-tuple-element.30.values, ...), custom_call_target="tpu_custom_call" | custom-call | flops 1073741824 | bytes 8388612 | tf_op jit(solution)/shard_map/pallas_call | solution.py:298
  49.7 0.0 collective-permute-done.12.rest_1_
  49.7 0.0 collective-permute-done.13.rest_2_
  49.7 4.3 %collective-permute-done.14.rest_3_ = bf16[1024,128]{1,0:T(8,128)(2,1)S(1)} collective-permute-done((bf16[1024,128]{1,0:T(8,128)(2,1)S(1)}, bf16[1024,128]{1,0:T(8,128)(2,1)S(1)}, u32[]{:S(2)}, u32[]{:S(2)}) %collective-permute-start.14) | collective-permute-done | bytes 262176 | tf_op jit(solution)/shard_map/ppermute | solution.py:319
  54.0 2.1 %shard_map.110 = (bf16[256,2048]{1,0:T(8,128)(2,1)}, bf16[256,2048]{1,0:T(8,128)(2,1)}) custom-call(s32[1]{0:T(128)S(6)} %copy.11.seg_len, bf16[256,2048]{1,0:T(8,128)(2,1)S(1)} %get-tuple-element.29.keys, bf16[256,2048]{1,0:T(8,128)(2,1)S(1)} %get-tuple-element.30.values, f32[256,2048]{1,0:T(8,128)S(1)} %get-tuple-element.44.key_part, ...), custom_call_target="tpu_custom_call" | custom-call | flops 268435456 | bytes 9437188 | tf_op jit(solution)/shard_map/pallas_call | solution.py:298
Async XLA Ops:
  0.6 12.9 %copy-start.3 = (s32[8]{0:T(128)S(1)}, s32[8]{0:T(128)}, u32[]{:S(2)}) copy-start(s32[8]{0:T(128)} %parent.3) | copy-start | bytes 100
  0.6 18.5 %copy-start = (bf16[1,256,2048]{2,1,0:T(8,128)(2,1)S(1)}, bf16[1,256,2048]{2,1,0:T(8,128)(2,1)}, u32[]{:S(2)}) copy-start(bf16[1,256,2048]{2,1,0:T(8,128)(2,1)} %param.7) | copy-start | bytes 3145732
  4.6 7.2 %collective-permute-start.1 = (bf16[1024,128]{1,0:T(8,128)(2,1)S(1)}, bf16[1024,128]{1,0:T(8,128)(2,1)S(1)}, u32[]{:S(2)}, u32[]{:S(2)}) collective-permute-start(bf16[1024,128]{1,0:T(8,128)(2,1)S(1)} %get-tuple-element.31.refs_0_), channel_id=1, source_target_pairs={{0,2},{1,5},{2,0},{3,7},{4,6},{5,1},{6,4},{7,3},{8,10},{9,13},{10,... | collective-permute-start | bytes 786440 | tf_op jit(solution)/shard_map/ppermute | solution.py:319
  6.7 6.9 %collective-permute-start.2 = (bf16[1024,128]{1,0:T(8,128)(2,1)S(1)}, bf16[1024,128]{1,0:T(8,128)(2,1)S(1)}, u32[]{:S(2)}, u32[]{:S(2)}) collective-permute-start(bf16[1024,128]{1,0:T(8,128)(2,1)S(1)} %get-tuple-element.32), channel_id=1, source_target_pairs={{0,5},{1,2},{2,7},{3,0},{4,1},{5,6},{6,3},{7,4},{8,13},{9,10},{10,... | collective-permute-start | bytes 786440 | tf_op jit(solution)/shard_map/ppermute | solution.py:319
  7.3 6.3 %collective-permute-start = (bf16[1024,128]{1,0:T(8,128)(2,1)S(1)}, bf16[1024,128]{1,0:T(8,128)(2,1)S(1)}, u32[]{:S(2)}, u32[]{:S(2)}) collective-permute-start(bf16[1024,128]{1,0:T(8,128)(2,1)S(1)} %get-tuple-element.32), channel_id=1, source_target_pairs={{0,1},{1,0},{2,3},{3,2},{4,5},{5,4},{6,7},{7,6},{8,9},{9,8},{10,11... | collective-permute-start | bytes 786440 | tf_op jit(solution)/shard_map/ppermute | solution.py:319
  14.7 5.9 %collective-permute-start.3 = (bf16[1024,128]{1,0:T(8,128)(2,1)S(1)}, bf16[1024,128]{1,0:T(8,128)(2,1)S(1)}, u32[]{:S(2)}, u32[]{:S(2)}) collective-permute-start(bf16[1024,128]{1,0:T(8,128)(2,1)S(1)} %get-tuple-element.34), channel_id=1, source_target_pairs={{0,4},{1,3},{2,6},{3,1},{4,0},{5,7},{6,2},{7,5},{8,12},{9,11},{10,... | collective-permute-start | bytes 786440 | tf_op jit(solution)/shard_map/ppermute | solution.py:319
  16.2 4.4 %collective-permute-start.4 = (bf16[1024,128]{1,0:T(8,128)(2,1)S(1)}, bf16[1024,128]{1,0:T(8,128)(2,1)S(1)}, u32[]{:S(2)}, u32[]{:S(2)}) collective-permute-start(bf16[1024,128]{1,0:T(8,128)(2,1)S(1)} %get-tuple-element.35), channel_id=1, source_target_pairs={{0,1},{1,0},{2,3},{3,2},{4,5},{5,4},{6,7},{7,6},{8,9},{9,8},{10,11... | collective-permute-start | bytes 786440 | tf_op jit(solution)/shard_map/ppermute | solution.py:319
  18.0 6.5 %collective-permute-start.5 = (bf16[1024,128]{1,0:T(8,128)(2,1)S(1)}, bf16[1024,128]{1,0:T(8,128)(2,1)S(1)}, u32[]{:S(2)}, u32[]{:S(2)}) collective-permute-start(bf16[1024,128]{1,0:T(8,128)(2,1)S(1)} %get-tuple-element.36), channel_id=1, source_target_pairs={{0,5},{1,2},{2,7},{3,0},{4,1},{5,6},{6,3},{7,4},{8,13},{9,10},{10,... | collective-permute-start | bytes 786440 | tf_op jit(solution)/shard_map/ppermute | solution.py:319
  19.1 5.4 %copy-start.1 = (bf16[1,256,2048]{2,1,0:T(8,128)(2,1)S(1)}, bf16[1,256,2048]{2,1,0:T(8,128)(2,1)}, u32[]{:S(2)}) copy-start(bf16[1,256,2048]{2,1,0:T(8,128)(2,1)} %param.10) | copy-start | bytes 3145732
  19.1 5.4 %copy-start.2 = (f32[2048]{0:T(1024)S(1)}, f32[2048]{0:T(1024)}, u32[]{:S(2)}) copy-start(f32[2048]{0:T(1024)} %param.11) | copy-start | bytes 24580
  25.7 4.9 %collective-permute-start.8 = (f32[2,256]{1,0:T(2,128)S(1)}, f32[2,256]{1,0:T(2,128)S(1)}, u32[]{:S(2)}, u32[]{:S(2)}) collective-permute-start(f32[2,256]{1,0:T(2,128)S(1)} %get-tuple-element.38.rest_0_), channel_id=1, source_target_pairs={{0,24},{8,16},{16,8},{24,0},{1,25},{9,17},{17,9},{25,1},{2,26},{10... | collective-permute-start | bytes 6152 | tf_op jit(solution)/shard_map/ppermute | solution.py:358
  29.5 3.3 %collective-permute-start.7 = (f32[2,256]{1,0:T(2,128)S(1)}, f32[2,256]{1,0:T(2,128)S(1)}, u32[]{:S(2)}, u32[]{:S(2)}) collective-permute-start(f32[2,256]{1,0:T(2,128)S(1)} %get-tuple-element.38.rest_0_), channel_id=1, source_target_pairs={{0,16},{8,24},{16,0},{24,8},{1,17},{9,25},{17,1},{25,9},{2,18},{10... | collective-permute-start | bytes 6152 | tf_op jit(solution)/shard_map/ppermute | solution.py:358
  29.6 3.3 %collective-permute-start.6 = (f32[2,256]{1,0:T(2,128)S(1)}, f32[2,256]{1,0:T(2,128)S(1)}, u32[]{:S(2)}, u32[]{:S(2)}) collective-permute-start(f32[2,256]{1,0:T(2,128)S(1)} %get-tuple-element.38.rest_0_), channel_id=1, source_target_pairs={{0,8},{8,0},{16,24},{24,16},{1,9},{9,1},{17,25},{25,17},{2,10},{10... | collective-permute-start | bytes 6152 | tf_op jit(solution)/shard_map/ppermute | solution.py:358
  33.9 7.4 %collective-permute-start.10 = (bf16[1024,128]{1,0:T(8,128)(2,1)S(1)}, bf16[1024,128]{1,0:T(8,128)(2,1)S(1)}, u32[]{:S(2)}, u32[]{:S(2)}) collective-permute-start(bf16[1024,128]{1,0:T(8,128)(2,1)S(1)} %get-tuple-element.46.refs_0_), channel_id=1, source_target_pairs={{0,2},{1,5},{2,0},{3,7},{4,6},{5,1},{6,4},{7,3},{8,10},{9,13},{10,... | collective-permute-start | bytes 786440 | tf_op jit(solution)/shard_map/ppermute | solution.py:319
  35.2 7.7 %collective-permute-start.11 = (bf16[1024,128]{1,0:T(8,128)(2,1)S(1)}, bf16[1024,128]{1,0:T(8,128)(2,1)S(1)}, u32[]{:S(2)}, u32[]{:S(2)}) collective-permute-start(bf16[1024,128]{1,0:T(8,128)(2,1)S(1)} %get-tuple-element.47), channel_id=1, source_target_pairs={{0,5},{1,2},{2,7},{3,0},{4,1},{5,6},{6,3},{7,4},{8,13},{9,10},{10,... | collective-permute-start | bytes 786440 | tf_op jit(solution)/shard_map/ppermute | solution.py:319
  36.7 6.1 %collective-permute-start.9 = (bf16[1024,128]{1,0:T(8,128)(2,1)S(1)}, bf16[1024,128]{1,0:T(8,128)(2,1)S(1)}, u32[]{:S(2)}, u32[]{:S(2)}) collective-permute-start(bf16[1024,128]{1,0:T(8,128)(2,1)S(1)} %get-tuple-element.47), channel_id=1, source_target_pairs={{0,1},{1,0},{2,3},{3,2},{4,5},{5,4},{6,7},{7,6},{8,9},{9,8},{10,11... | collective-permute-start | bytes 786440 | tf_op jit(solution)/shard_map/ppermute | solution.py:319
  44.0 5.7 %collective-permute-start.12 = (bf16[1024,128]{1,0:T(8,128)(2,1)S(1)}, bf16[1024,128]{1,0:T(8,128)(2,1)S(1)}, u32[]{:S(2)}, u32[]{:S(2)}) collective-permute-start(bf16[1024,128]{1,0:T(8,128)(2,1)S(1)} %get-tuple-element.49), channel_id=1, source_target_pairs={{0,4},{1,3},{2,6},{3,1},{4,0},{5,7},{6,2},{7,5},{8,12},{9,11},{10,... | collective-permute-start | bytes 786440 | tf_op jit(solution)/shard_map/ppermute | solution.py:319
  44.7 5.0 %collective-permute-start.13 = (bf16[1024,128]{1,0:T(8,128)(2,1)S(1)}, bf16[1024,128]{1,0:T(8,128)(2,1)S(1)}, u32[]{:S(2)}, u32[]{:S(2)}) collective-permute-start(bf16[1024,128]{1,0:T(8,128)(2,1)S(1)} %get-tuple-element.50), channel_id=1, source_target_pairs={{0,1},{1,0},{2,3},{3,2},{4,5},{5,4},{6,7},{7,6},{8,9},{9,8},{10,11... | collective-permute-start | bytes 786440 | tf_op jit(solution)/shard_map/ppermute | solution.py:319
  46.0 7.9 %collective-permute-start.14 = (bf16[1024,128]{1,0:T(8,128)(2,1)S(1)}, bf16[1024,128]{1,0:T(8,128)(2,1)S(1)}, u32[]{:S(2)}, u32[]{:S(2)}) collective-permute-start(bf16[1024,128]{1,0:T(8,128)(2,1)S(1)} %get-tuple-element.51), channel_id=1, source_target_pairs={{0,5},{1,2},{2,7},{3,0},{4,1},{5,6},{6,3},{7,4},{8,13},{9,10},{10,... | collective-permute-start | bytes 786440 | tf_op jit(solution)/shard_map/ppermute | solution.py:319

commit v5 on v4

v5 whole, which is shorter than its diff:
```python
import functools
import math

import jax
import jax.numpy as jnp
from jax import lax
from jax.experimental import pallas as pl
from jax.experimental.pallas import tpu as pltpu
from jax.sharding import PartitionSpec as P

HEADS = 64
HD = 128
EPSILON = 1e-06
F32 = jnp.float32
BF16 = jnp.bfloat16
VMEM_LIMIT = 24 * 1024 * 1024
PIECES = 2

VMEM = pl.BlockSpec(memory_space=pltpu.VMEM)
SMEM = pl.BlockSpec(memory_space=pltpu.SMEM)
HBM = pl.BlockSpec(memory_space=pltpu.HBM)
ANY = pl.BlockSpec(memory_space=pl.ANY)


def dot(a, b, contract):
    return lax.dot_general(a, b, (contract, ((), ())), preferred_element_type=F32)


def nn(a, b):
    return dot(a, b, ((1,), (0,)))


def nt(a, b):
    return dot(a, b, ((1,), (1,)))


def tn(a, b):
    return dot(a, b, ((0,), (0,)))


def head_cols(head):
    return slice(head * HD, (head + 1) * HD)


def target_of(place, step, size):
    if size & (size - 1) == 0:
        return place ^ step
    return (place + step) % size


def source_of(place, step, size):
    if size & (size - 1) == 0:
        return place ^ step
    return (place + size - step) % size


def grid_of(segs):
    pair = 2 if segs % 2 == 0 else 1
    chips = segs // pair
    columns = next(c for c in range(1, chips + 1) if chips % c == 0 and c * c >= chips)
    return chips // columns, columns, pair


def member(grid, row, column, core):
    return (row * grid[1] + column) * grid[2] + core


def place_of(grid, device):
    chip = device // grid[2]
    return chip // grid[1], chip % grid[1], device % grid[2]


def along(grid, place, step, gather, ahead):
    row, column, core = place
    shift = target_of if ahead else source_of
    by_row = (core == 0) if gather else (core != 0)
    valid_column = step < grid[1]
    valid_row = step < grid[0]
    if isinstance(core, int):
        if by_row:
            return row, shift(column, step, grid[1]), valid_column
        return shift(row, step, grid[0]), column, valid_row
    moved_column = shift(column, min(step, grid[1] - 1), grid[1])
    moved_row = shift(row, min(step, grid[0] - 1), grid[0])
    return (
        jnp.where(by_row, row, moved_row),
        jnp.where(by_row, moved_column, column),
        jnp.where(by_row, valid_column, valid_row),
    )


def my_place(grid):
    me = lax.axis_index("seg")
    chip = lax.div(me, grid[2])
    return lax.div(chip, grid[1]), lax.rem(chip, grid[1]), lax.rem(me, grid[2])


def row_halves(full, core, pair):
    half = full.shape[0] // pair
    return [full.at[pl.ds(pl.multiple_of((core ^ j) * half, half), half), :] for j in range(pair)]


def join_halves(parts, full, core, pair):
    for half, terms in zip(row_halves(full, core, pair), parts):
        total = terms[0][...].astype(F32)
        for term in terms[1:]:
            total += term[...].astype(F32)
        half[...] = total.astype(BF16)


def line_length(grid):
    return max(grid[0], grid[1])


def write_weights(grid, parent, up, down):
    place = my_place(grid)
    pair = grid[2]
    count = line_length(grid) * pair

    def is_ancestor(child, other):
        first = parent[0, child]
        second = jnp.where(first >= 0, parent[0, jnp.maximum(first, 0)], -1)
        return jnp.logical_or(other == first, other == second)

    for out_step in range(count):
        row, column, _ = along(grid, place, out_step // pair, False, True)
        target = member(grid, row, column, place[2] ^ (out_step % pair))
        for in_step in range(count):
            row, column, valid = along(grid, place, in_step // pair, True, False)
            source = member(grid, row, column, place[2] ^ (in_step % pair))
            at = out_step * count + in_step
            for rows, used in ((up, is_ancestor(target, source)), (down, is_ancestor(source, target))):
                weight = jnp.where(jnp.logical_and(used, valid), 1.0, 0.0)
                rows[at : at + 1, :] = jnp.full((1, HD), weight, F32)


def state_kernel(piece, grid, *rest):
    pair = grid[2]
    first, last = piece == 0, piece == PIECES - 1
    keys_hbm, values_hbm, seg_len = rest[:3]
    parent_hbm, rest = (rest[3], rest[4:]) if last else (None, rest[3:])
    (keys, values), halves, rest = rest[:2], rest[2 : 2 + pair], rest[2 + pair :]
    outs, (full, sems, parent, parent_sem) = rest[:-4], rest[-4:]
    rows, width = keys.shape
    chunk = rows // 4 if rows % 64 == 0 else rows
    cols = slice(piece * width, (piece + 1) * width)
    copies = []
    for step in range(rows // chunk):
        part = slice(step * chunk, (step + 1) * chunk)
        for j, (src, dst) in enumerate(((keys_hbm, keys), (values_hbm, values))):
            copies.append(pltpu.make_async_copy(src.at[part, cols], dst.at[part, :], sems.at[j, step]))
    for copy in copies:
        copy.start()
    if first:
        outs[0][...] = jnp.full(outs[0].shape, seg_len[0], jnp.int32)
    if last:
        copy = pltpu.make_async_copy(parent_hbm, parent, parent_sem)
        copy.start()
        copy.wait()
        write_weights(grid, parent, *outs[-2:])
    live = lax.broadcasted_iota(jnp.int32, (rows, HD), 0) < seg_len[0]
    for copy in copies:
        copy.wait()
    for head in range(width // HD):
        cols = head_cols(head)
        masked = jnp.where(live, keys[:, cols], jnp.zeros((), BF16))
        full[head * HD : (head + 1) * HD, :] = tn(masked, values[:, cols]).astype(BF16)
    for half, out in zip(row_halves(full, my_place(grid)[2], pair), halves):
        out[...] = half[...]


def mix_kernel(sources, weights, *refs):
    blocks, outs = refs[:sources], refs[-sources:]
    rows = blocks[0].shape[0]
    chunk = min(rows, 64)
    for start in range(0, rows, chunk):
        part = slice(start, start + chunk)
        loaded = [block[part, :].astype(F32) for block in blocks]
        for out_step, out in enumerate(outs):
            at = out_step * sources
            total = weights[at : at + 1, :] * loaded[0]
            for in_step in range(1, sources):
                total += weights[at + in_step : at + in_step + 1, :] * loaded[in_step]
            out[part, :] = total.astype(BF16)


def live_rows(length, rows):
    return lax.broadcasted_iota(jnp.int32, (rows, HD), 0) < length[:, :HD]


def keep_mask(length, turned):
    rows = length.shape[1]
    first = lax.broadcasted_iota(jnp.int32, (rows, rows), 0)
    second = lax.broadcasted_iota(jnp.int32, (rows, rows), 1)
    if turned:
        return (first <= second) & (first < length[...])
    return (second <= first) & (second < length[...])


def split_refs(refs, *counts):
    parts, at = [], 0
    for count in counts:
        parts.append(refs[at : at + count])
        at += count
    return parts


def head_of(pieces, head):
    per_piece = pieces[0].shape[1] // HD
    return pieces[head // per_piece], head_cols(head % per_piece)


def local_kernel(heads, length, queries_hbm, *rest):
    keys, values, rest = rest[:PIECES], rest[PIECES : 2 * PIECES], rest[2 * PIECES :]
    queries, local, turned, sems = rest[-4:]
    rows = length.shape[1]
    group = 4 if heads % 4 == 0 else 1
    copies = []
    for at in range(0, heads, group):
        cols = slice(at * HD, (at + group) * HD)
        copies.append(pltpu.make_async_copy(queries_hbm.at[:, cols], queries.at[:, cols], sems.at[at // group]))
    for copy in copies:
        copy.start()
    keep = keep_mask(length, False)
    keep_turned = keep_mask(length, True)
    for head in range(heads):
        if head % group == 0:
            copies[head // group].wait()
        cols = head_cols(head)
        key_piece, at = head_of(keys, head)
        key = key_piece[:, at]
        value_piece, _ = head_of(values, head)
        query = queries[:, cols]
        scores = jnp.where(keep, nt(query, key), 0.0).astype(BF16)
        local[:, cols] = nn(scores, value_piece[:, at])
        turned[head] = jnp.where(keep_turned, nt(key, query), 0.0).astype(BF16)


def token_rows(total):
    return jnp.sum(jnp.transpose(total), axis=0, keepdims=True)


def token_columns(row):
    return jnp.transpose(jnp.broadcast_to(row, (HD, row.shape[1])))


def carry_kernel(piece, grid, counts, scale, length, queries, local, cotangent, gain, *rest):
    received, rest = rest[: sum(counts)], rest[sum(counts) :]
    before, (attention, sums, prefix) = rest[:-3], rest[-3:]
    join_halves(split_refs(received, *counts), prefix, my_place(grid)[2], grid[2])
    rows, width = attention.shape
    factor = jnp.where(live_rows(length, rows), scale, 0.0)
    squares = jnp.zeros((rows, HD), F32)
    products = jnp.zeros((rows, HD), F32)
    for head in range(width // HD):
        cols = head_cols(head)
        whole = head_cols(piece * width // HD + head)
        carried = nn(queries[:, whole], prefix[head * HD : (head + 1) * HD, :])
        out = factor * (carried + local[:, whole])
        attention[:, cols] = out
        squares += out * out
        products += out * (cotangent[:, whole].astype(F32) * gain[:, whole])
    both = jnp.concatenate([token_rows(squares), token_rows(products)], axis=0)
    for other in before:
        both += other[...]
    sums[...] = both


def grad_kernel(piece, groups, grid, scale, length, queries, attention, cotangent, gain, *rest):
    all_sums, rest = rest[:groups], rest[groups:]
    (grad_out, inverse_rms), halves, full = rest[:2], rest[2:-1], rest[-1]
    rows, width = attention.shape
    features = HEADS * HD
    total = all_sums[0][...]
    for other in all_sums[1:]:
        total = total + other[...]
    inverse = lax.rsqrt(total[0:1, :] / features + EPSILON)
    inverse_rms[...] = inverse
    live = lax.broadcasted_iota(jnp.int32, (1, rows), 1) < length[...]
    live_inverse = jnp.where(live, inverse, 0.0)
    shrink = live_inverse * inverse * (inverse * total[1:2, :]) / features
    live_inverse = token_columns(live_inverse)
    shrink = token_columns(shrink)
    for head in range(width // HD):
        cols = head_cols(head)
        whole = head_cols(piece * width // HD + head)
        gain_grad = cotangent[:, whole].astype(F32) * gain[:, whole]
        grad = (live_inverse * gain_grad - attention[:, cols] * shrink).astype(BF16)
        grad_out[:, cols] = grad
        full[head * HD : (head + 1) * HD, :] = (scale * tn(queries[:, whole], grad)).astype(BF16)
    for half, out in zip(row_halves(full, my_place(grid)[2], grid[2]), halves):
        out[...] = half[...]


def query_kernel(heads, scale, length, inverse_rms, gain, *rest):
    keys, values, grads, attention, prefix, rest = split_refs(rest, *[PIECES] * 5, len(rest) - 5 * PIECES)
    attended_hbm, query_hbm, token, attended, query_grad, sems = rest[-6:]
    token[...] = jnp.zeros_like(token)
    keep = keep_mask(length, False)
    inverse = token_columns(inverse_rms[...])
    group = 4 if heads % 4 == 0 else 1
    copies = []
    for head in range(heads):
        cols = head_cols(head)
        key_piece, at = head_of(keys, head)
        value_piece, _ = head_of(values, head)
        grad_piece, _ = head_of(grads, head)
        out_piece, _ = head_of(attention, head)
        prefix_piece, state = prefix[head // (heads // PIECES)], head % (heads // PIECES)
        grad = grad_piece[:, at]
        grad_scores = jnp.where(keep, nt(grad, value_piece[:, at]), 0.0).astype(BF16)
        carried = nt(grad, prefix_piece[state * HD : (state + 1) * HD, :])
        query_grad[:, cols] = (scale * (carried + nn(grad_scores, key_piece[:, at]))).astype(BF16)
        attended[:, cols] = (out_piece[:, at] * inverse * gain[:, cols]).astype(BF16)
        if (head + 1) % group == 0:
            done = slice((head + 1 - group) * HD, (head + 1) * HD)
            for j, (src, dst) in enumerate(((attended, attended_hbm), (query_grad, query_hbm))):
                copy = pltpu.make_async_copy(src.at[:, done], dst.at[:, done], sems.at[j, head // group])
                copy.start()
                copies.append(copy)
    for copy in copies:
        copy.wait()


def back_kernel(heads, scale, length, queries, turned, *rest):
    values, grads, rest = split_refs(rest, PIECES, PIECES, len(rest) - 2 * PIECES)
    key_part, value_part = rest[-2:]
    keep = keep_mask(length, True)
    for head in range(heads):
        cols = head_cols(head)
        value_piece, at = head_of(values, head)
        grad_piece, _ = head_of(grads, head)
        grad = grad_piece[:, at]
        grad_scores = jnp.where(keep, nt(value_piece[:, at], grad), 0.0).astype(BF16)
        key_part[:, cols] = scale * nn(grad_scores, queries[:, cols])
        value_part[:, cols] = scale * nn(turned[head], grad)


def final_kernel(piece, grid, counts, length, keys, values, key_part, value_part, *rest):
    received, rest = rest[: sum(counts)], rest[sum(counts) :]
    key_hbm, value_hbm, key_grad, value_grad, below, sems = rest[-6:]
    join_halves(split_refs(received, *counts), below, my_place(grid)[2], grid[2])
    rows, width = keys.shape
    live = jnp.where(live_rows(length, rows), 1.0, 0.0)
    heads = width // HD
    group = 2 if heads % 2 == 0 else 1
    copies = []
    for head in range(heads):
        cols = head_cols(head)
        whole = head_cols(piece * heads + head)
        state = below[head * HD : (head + 1) * HD, :]
        key_grad[:, cols] = (key_part[:, whole] + live * nt(values[:, cols], state)).astype(BF16)
        value_grad[:, cols] = (value_part[:, whole] + live * nn(keys[:, cols], state)).astype(BF16)
        if (head + 1) % group == 0:
            done = slice((head + 1 - group) * HD, (head + 1) * HD)
            there = slice(piece * width + done.start, piece * width + done.stop)
            for j, (src, dst) in enumerate(((key_grad, key_hbm), (value_grad, value_hbm))):
                copy = pltpu.make_async_copy(src.at[:, done], dst.at[:, there], sems.at[j, head // group])
                copy.start()
                copies.append(copy)
    for copy in copies:
        copy.wait()


def in_hbm(x):
    return pltpu.with_memory_space_constraint(x, pltpu.HBM)


def call(kernel, out_shape, operands, scratch=(), flops=0, stream=(), scalars=(), after=(), out_specs=None, aliases=None):
    moved = sum(math.prod(x.shape) * x.dtype.itemsize for x in operands)
    moved += sum(math.prod(x.shape) * x.dtype.itemsize for x in out_shape)
    specs = [SMEM if j in scalars else HBM if j in stream else VMEM for j in range(len(operands))]
    operands = [in_hbm(x) if j in stream else x for j, x in enumerate(operands)]
    return pl.pallas_call(
        kernel,
        out_shape=out_shape,
        in_specs=specs + [ANY] * len(after),
        out_specs=out_specs or [VMEM] * len(out_shape),
        scratch_shapes=list(scratch),
        input_output_aliases=aliases or {},
        compiler_params=pltpu.CompilerParams(vmem_limit_bytes=VMEM_LIMIT),
        cost_estimate=pl.CostEstimate(flops=flops, bytes_accessed=moved, transcendentals=0),
    )(*operands, *after)


def line_send(block, grid, step, flip, gather):
    moves = []
    for device in range(grid[0] * grid[1] * grid[2]):
        place = place_of(grid, device)
        if gather and flip:
            row, column, valid = along(grid, (place[0], place[1], place[2] ^ 1), step, True, True)
        else:
            row, column, valid = along(grid, place, step, gather, True)
        if valid:
            moves.append((device, member(grid, row, column, place[2] ^ flip)))
    return lax.ppermute(block, "seg", moves)


def gather_line(halves, grid):
    arrived = []
    for step in range(line_length(grid)):
        for flip in range(grid[2]):
            if step == 0 and flip == 0:
                arrived.append(halves[0])
            else:
                arrived.append(line_send(halves[flip], grid, step, flip, True))
    return arrived


def scatter_line(sums, grid):
    pair = grid[2]
    parts = [[] for _ in range(pair)]
    for step in range(line_length(grid)):
        for flip in range(pair):
            block = sums[step * pair + flip]
            if step == 0 and flip == 0:
                parts[0].append(block)
            else:
                parts[flip].append(line_send(block, grid, step, flip, False))
    return parts


def token_sums(sums, groups):
    if groups & (groups - 1):
        moves = [[(j, (j + step) % groups) for j in range(groups)] for step in range(1, groups)]
        return [sums] + [lax.ppermute(sums, "head", pairs) for pairs in moves]
    parts = [sums]
    step = 1
    while step < groups:
        sums = parts[0] if len(parts) == 1 else parts[0] + parts[1]
        parts = [sums, lax.ppermute(sums, "head", [(j, j ^ step) for j in range(groups)])]
        step *= 2
    return parts


def per_device(segs, groups, queries, key_rows, values, cotangent, out_gain, parent, seg_len):
    rows, features = queries.shape[1:]
    heads = features // HD
    grid = grid_of(segs)
    pair = grid[2]
    scale = 1.0 / math.sqrt(HD * rows)
    cot = cotangent[0]
    gain = out_gain[None]
    shape = jax.ShapeDtypeStruct
    width = features // PIECES
    narrow = shape((rows, features), BF16)
    wide = shape((rows, features), F32)
    narrow_piece = shape((rows, width), BF16)
    wide_piece = shape((rows, width), F32)
    state = shape((width, HD), BF16)
    half = shape((width // pair, HD), BF16)
    row = shape((1, rows), F32)
    members = line_length(grid) * pair
    weight_rows = shape((members * members, HD), F32)
    state_scratch = pltpu.VMEM(state.shape, BF16)
    sems = pltpu.SemaphoreType.DMA((2, heads))
    counts = [line_length(grid)] * pair
    unit = 2 * heads * rows * HD
    every = range(PIECES)

    def mix(arrived, weights, after=()):
        return call(functools.partial(mix_kernel, members), [half] * members, (weights, *arrived), after=after)

    def flat(parts):
        return [block for part in parts for block in part]

    keys, vals, own = [], [], []
    for piece in every:
        extra = [shape((1, rows), jnp.int32)] if piece == 0 else []
        extra += [weight_rows] * 2 if piece == PIECES - 1 else []
        key, value, *rest = call(
            functools.partial(state_kernel, piece, grid),
            [narrow_piece] * 2 + [half] * pair + extra,
            (key_rows[0], values[0], seg_len) + ((parent[None],) if piece == PIECES - 1 else ()),
            [state_scratch, sems, pltpu.SMEM((1, segs), jnp.int32), pltpu.SemaphoreType.DMA(())],
            unit * HD // PIECES, (0, 1, 3), (2,),
        )
        keys.append(key)
        vals.append(value)
        own.append(rest[:pair])
        if piece == 0:
            length = rest[pair]
    up, down = rest[-2:]
    mixed = [mix(gather_line(own[piece], grid), up) for piece in every]
    query, local, turned = call(
        functools.partial(local_kernel, heads),
        [narrow, wide, shape((heads, rows, rows), BF16)],
        (length, queries[0], *keys, *vals), [pltpu.SemaphoreType.DMA((heads,))], unit * rows * 3, (1,), after=(mixed[0][0],),
    )
    attention, prefix, sums = [], [], []
    for piece in every:
        out, total, joined = call(
            functools.partial(carry_kernel, piece, grid, counts, scale),
            [wide_piece, shape((2, rows), F32), state],
            (length, query, local, cot, gain, *flat(scatter_line(mixed[piece], grid)), *sums),
            (), unit * HD // PIECES,
        )
        attention.append(out)
        prefix.append(joined)
        sums = [total]
    sums = token_sums(sums[0], groups)
    grads, state_grad = [], []
    for piece in every:
        grad_out, inverse_rms, *halves = call(
            functools.partial(grad_kernel, piece, len(sums), grid, scale),
            [narrow_piece, row] + [half] * pair,
            (length, query, attention[piece], cot, gain, *sums), [state_scratch], unit * HD // PIECES,
        )
        grads.append(grad_out)
        state_grad.append(halves)
    mixed = []
    for piece in every:
        mixed.append(mix(gather_line(state_grad[piece], grid), down, () if piece == 0 else (token,)))
        if piece == 0:
            attended, query_grad, token = call(
                functools.partial(query_kernel, heads, scale),
                [narrow, narrow, shape((8, HD), F32)],
                (length, inverse_rms, gain, *keys, *vals, *grads, *attention, *prefix),
                [pltpu.VMEM(narrow.shape, BF16)] * 2 + [sems], unit * (2 * rows + HD),
                after=(mixed[0][0],), out_specs=[HBM, HBM, VMEM],
            )
    key_part, value_part = call(
        functools.partial(back_kernel, heads, scale),
        [wide, wide], (length, query, turned, *vals, *grads), (), unit * 3 * rows, after=(mixed[-1][0],),
    )
    results = []
    for piece in every:
        below = flat(scatter_line(mixed[piece], grid))
        operands = (length, keys[piece], vals[piece], key_part, value_part, *below, *results)
        first = len(operands) - len(results)
        results = call(
            functools.partial(final_kernel, piece, grid, counts),
            [narrow, narrow], operands,
            [pltpu.VMEM(narrow_piece.shape, BF16)] * 2 + [state_scratch, sems], 2 * unit * HD // PIECES,
            range(first, len(operands)), out_specs=[HBM, HBM],
            aliases={first + j: j for j in range(len(results))},
        )
    key_grad, value_grad = results
    return attended[None], query_grad[None], key_grad[None], value_grad[None]


def solution(mesh):
    split = P("seg", None, "head")
    return jax.shard_map(
        functools.partial(per_device, mesh.shape["seg"], mesh.shape["head"]),
        mesh=mesh,
        in_specs=(split, split, split, split, P("head"), P(), P("seg")),
        out_specs=(split, split, split, split),
        check_vma=False,
    )
```

time: 56.4 us -> 57.5 us (1.020)
  the two profiles are of different devices: /device:TPU:1 before, /device:TPU:0 now
where the time goes in v5:
time: 57.5 us; the launch traced here: 56.5 us
  starting transfers between devices  24.1 us (42%)
  Pallas kernels  23.4 us (41%)
  waiting for transfers between devices  7.29 us (13%)
  between operations  1.64 us (3%)
    pallas_call x15, Pallas kernels, call(): pl.pallas_call(kernel, out_shape=out_shape, in_specs=specs + [ANY] * len(...  23.4 us
    ppermute x24, starting transfers between devices, line_send(): return lax.ppermute(block, 'seg', moves)  19.9 us
    ppermute x2, starting transfers between devices, token_sums(): lax.ppermute(sums, 'head', [(j, j ^ step) for j in range(groups)])  4.24 us
    ppermute x2, waiting for transfers between devices, token_sums(): lax.ppermute(sums, 'head', [(j, j ^ step) for j in range(groups)])  3.89 us
    ppermute x24, waiting for transfers between devices, line_send(): return lax.ppermute(block, 'seg', moves)  3.39 us
  transfers between devices with their start and end apart: 26, of which 6 were waited for; matrix products, arithmetic and copies ran while one was open for 0% of the time, Pallas kernels for 32%

profile of v5, /device:TPU:0, one launch (start us, length us, event | category | flops | bytes accessed | tf_op | source)
XLA Modules:
  0.0 56.5 jit_solution(18300070532833486358)
XLA Ops:
  1.3 2.0 %shard_map.102 = (bf16[256,1024]{1,0:T(8,128)(2,1)S(1)}, bf16[256,1024]{1,0:T(8,128)(2,1)S(1)}, bf16[512,128]{1,0:T(8,128)(2,1)S(1)}, bf16[512,128]{1,0:T(8,128)(2,1)S(1)}, s32[1,256]{1,0:T(1,128)S(1)}) custom-call(bf16[256,2048]{1,0:T(8,128)(2,1)} %bitcast.19, bf16[256,2048]{1,0:T(8,128)(2,1)} %bitcast.21, s32[1]{0:T(128)S(6)} %copy.15.rest_2_), custom_call_target="tpu_custom_call" | custom-call | flops 67108864 | bytes 3408900 | tf_op jit(solution)/shard_map/pallas_call | solution.py:374
  3.2 3.0 %collective-permute-start.1 = (bf16[512,128]{1,0:T(8,128)(2,1)S(1)}, bf16[512,128]{1,0:T(8,128)(2,1)S(1)}, u32[]{:S(2)}, u32[]{:S(2)}) collective-permute-start(bf16[512,128]{1,0:T(8,128)(2,1)S(1)} %get-tuple-element.62.refs_0_), channel_id=1, source_target_pairs={{0,2},{1,5},{2,0},{3,7},{4,6},{5,1},{6,4},{7,3},{8,10},{9,13},{10,... | collective-permute-start | bytes 393224 | tf_op jit(solution)/shard_map/ppermute | solution.py:396
  6.2 0.0 collective-permute-start.2
  6.2 0.2 collective-permute-start
  6.4 1.9 %shard_map.103 = (bf16[256,1024]{1,0:T(8,128)(2,1)S(1)}, bf16[256,1024]{1,0:T(8,128)(2,1)S(1)}, bf16[512,128]{1,0:T(8,128)(2,1)S(1)}, bf16[512,128]{1,0:T(8,128)...) custom-call(bf16[256,2048]{1,0:T(8,128)(2,1)} %bitcast.20, bf16[256,2048]{1,0:T(8,128)(2,1)} %bitcast.22, ...), custom_call_target="tpu_custom_call" | custom-call | flops 67108864 | bytes 3424292 | tf_op jit(solution)/shard_map/pallas_call | solution.py:374
  8.4 2.0 %collective-permute-start.4 = (bf16[512,128]{1,0:T(8,128)(2,1)S(1)}, bf16[512,128]{1,0:T(8,128)(2,1)S(1)}, u32[]{:S(2)}, u32[]{:S(2)}) collective-permute-start(bf16[512,128]{1,0:T(8,128)(2,1)S(1)} %get-tuple-element.67.refs_0_), channel_id=1, source_target_pairs={{0,2},{1,5},{2,0},{3,7},{4,6},{5,1},{6,4},{7,3},{8,10},{9,13},{10,... | collective-permute-start | bytes 393224 | tf_op jit(solution)/shard_map/ppermute | solution.py:396
  10.4 0.0 collective-permute-start.5
  10.4 0.0 collective-permute-done.1.refs_2_
  10.4 0.2 collective-permute-start.3
  10.6 0.0 collective-permute-done.2.refs_3_
  10.6 0.0 collective-permute-done.refs_1_
  10.6 0.3 shard_map.104
  10.9 2.1 %collective-permute-start.9 = (bf16[512,128]{1,0:T(8,128)(2,1)S(1)}, bf16[512,128]{1,0:T(8,128)(2,1)S(1)}, u32[]{:S(2)}, u32[]{:S(2)}) collective-permute-start(bf16[512,128]{1,0:T(8,128)(2,1)S(1)} %get-tuple-element.73), channel_id=1, source_target_pairs={{0,4},{1,3},{2,6},{3,1},{4,0},{5,7},{6,2},{7,5},{8,12},{9,11},{10,... | collective-permute-start | bytes 393224 | tf_op jit(solution)/shard_map/ppermute | solution.py:396
  13.0 0.0 collective-permute-start.10
  13.0 1.2 %collective-permute-done.4.refs_2_ = bf16[512,128]{1,0:T(8,128)(2,1)S(1)} collective-permute-done((bf16[512,128]{1,0:T(8,128)(2,1)S(1)}, bf16[512,128]{1,0:T(8,128)(2,1)S(1)}, u32[]{:S(2)}, u32[]{:S(2)}) %collective-permute-start.4) | collective-permute-done | bytes 131104 | tf_op jit(solution)/shard_map/ppermute | solution.py:396
  14.2 0.5 collective-permute-start.11
  14.7 0.1 collective-permute-done.5.refs_3_
  14.8 0.0 collective-permute-done.3.refs_1_
  14.8 0.3 shard_map.106
  15.1 2.1 %collective-permute-start.6 = (bf16[512,128]{1,0:T(8,128)(2,1)S(1)}, bf16[512,128]{1,0:T(8,128)(2,1)S(1)}, u32[]{:S(2)}, u32[]{:S(2)}) collective-permute-start(bf16[512,128]{1,0:T(8,128)(2,1)S(1)} %get-tuple-element.70), channel_id=1, source_target_pairs={{0,4},{1,3},{2,6},{3,1},{4,0},{5,7},{6,2},{7,5},{8,12},{9,11},{10,... | collective-permute-start | bytes 393224 | tf_op jit(solution)/shard_map/ppermute | solution.py:396
  17.2 0.1 collective-permute-start.7
  17.3 0.0 collective-permute-done.9.rest_1_
  17.3 1.3 %collective-permute-start.8 = (bf16[512,128]{1,0:T(8,128)(2,1)S(1)}, bf16[512,128]{1,0:T(8,128)(2,1)S(1)}, u32[]{:S(2)}, u32[]{:S(2)}) collective-permute-start(bf16[512,128]{1,0:T(8,128)(2,1)S(1)} %get-tuple-element.72), channel_id=1, source_target_pairs={{0,5},{1,2},{2,7},{3,0},{4,1},{5,6},{6,3},{7,4},{8,13},{9,10},{10,... | collective-permute-start | bytes 393224 | tf_op jit(solution)/shard_map/ppermute | solution.py:396
  18.5 4.7 %shard_map.105 = (bf16[256,2048]{1,0:T(8,128)(2,1)S(1)}, f32[256,2048]{1,0:T(8,128)S(1)}, bf16[16,256,256]{2,1,0:T(8,128)(2,1)S(1)}) custom-call(s32[1,256]{1,0:T(1,128)S(1)} %get-tuple-element.56.length, bf16[256,2048]{1,0:T(8,128)(2,1)} %bitcast.25, bf16[256,1024]{1,0:T(8,128)(2,1)S(1)} %get-tuple-element.57.rest_0_.keys, ...), custom_call_target="tpu_custom_call" | custom-call | flops 805306368 | bytes 8389632 | tf_op jit(solution)/shard_map/pallas_call | solution.py:374
  23.2 0.0 collective-permute-done.10.rest_2_
  23.2 0.0 collective-permute-done.11.rest_3_
  23.3 0.7 %shard_map.107 = (f32[256,1024]{1,0:T(8,128)S(1)}, f32[2,256]{1,0:T(2,128)S(1)}, bf16[1024,128]{1,0:T(8,128)(2,1)S(1)}) custom-call(s32[1,256]{1,0:T(1,128)S(1)} %get-tuple-element.56.length, bf16[256,2048]{1,0:T(8,128)(2,1)S(1)} %get-tuple-element.65.queries, f32[256,2048]{1,0:T(8,128)S(1)} %get-tuple-element.66.local, bf16[256,2048]{1,0:T(8,128)(2,1)S(1)} %bitcast.10, ...), custom_call_target="tpu_custom_call" | custom-call | flops 67108864 | bytes 6040576 | tf_op jit(solution)/shard_map/pallas_call | solution.py:374
  23.9 0.0 collective-permute-done.6.rest_1_
  23.9 0.0 collective-permute-done.7.rest_2_
  23.9 0.0 collective-permute-done.8.rest_3_
  24.0 0.7 %shard_map.108 = (f32[256,1024]{1,0:T(8,128)S(1)}, f32[2,256]{1,0:T(2,128)S(1)}, bf16[1024,128]{1,0:T(8,128)(2,1)S(1)}) custom-call(s32[1,256]{1,0:T(1,128)S(1)} %get-tuple-element.56.length, bf16[256,2048]{1,0:T(8,128)(2,1)S(1)} %get-tuple-element.65.queries, f32[256,2048]{1,0:T(8,128)S(1)} %get-tuple-element.66.local, bf16[256,2048]{1,0:T(8,128)(2,1)S(1)} %bitcast.11, ...), custom_call_target="tpu_custom_call" | custom-call | flops 67108864 | bytes 6042624 | tf_op jit(solution)/shard_map/pallas_call | solution.py:374
  24.6 1.6 %collective-permute-start.12 = (f32[2,256]{1,0:T(2,128)S(1)}, f32[2,256]{1,0:T(2,128)S(1)}, u32[]{:S(2)}, u32[]{:S(2)}) collective-permute-start(f32[2,256]{1,0:T(2,128)S(1)} %get-tuple-element.78), channel_id=1, source_target_pairs={{0,8},{8,0},{16,24},{24,16},{1,9},{9,1},{17,25},{25,17},{2,10},{10... | collective-permute-start | bytes 6152 | tf_op jit(solution)/shard_map/ppermute | solution.py:431
  26.3 2.0 %collective-permute-done.12 = f32[2,256]{1,0:T(2,128)S(1)} collective-permute-done((f32[2,256]{1,0:T(2,128)S(1)}, f32[2,256]{1,0:T(2,128)S(1)}, u32[]{:S(2)}, u32[]{:S(2)}) %collective-permute-start.12) | collective-permute-done | bytes 2080 | tf_op jit(solution)/shard_map/ppermute | solution.py:431
  28.3 2.6 %collective-permute-start.13 = (f32[2,256]{1,0:T(2,128)S(1)}, f32[2,256]{1,0:T(2,128)S(1)}, u32[]{:S(2)}, u32[]{:S(2)}) collective-permute-start(f32[2,256]{1,0:T(2,128)S(1)} %add.3.rest_0_), channel_id=1, source_target_pairs={{0,16},{8,24},{16,0},{24,8},{1,17},{9,25},{17,1},{25,9},{2,18},{10... | collective-permute-start | bytes 6152 | tf_op jit(solution)/shard_map/ppermute | solution.py:431
  30.9 1.9 %collective-permute-done.13.rest_1_ = f32[2,256]{1,0:T(2,128)S(1)} collective-permute-done((f32[2,256]{1,0:T(2,128)S(1)}, f32[2,256]{1,0:T(2,128)S(1)}, u32[]{:S(2)}, u32[]{:S(2)}) %collective-permute-start.13) | collective-permute-done | bytes 2080 | tf_op jit(solution)/shard_map/ppermute | solution.py:431
  32.8 1.1 %shard_map.110 = (bf16[256,1024]{1,0:T(8,128)(2,1)S(1)}, f32[1,256]{1,0:T(1,128)}, bf16[512,128]{1,0:T(8,128)(2,1)S(1)}, bf16[512,128]{1,0:T(8,128)(2,1)S(1)}) custom-call(s32[1,256]{1,0:T(1,128)S(1)} %get-tuple-element.56.length, bf16[256,2048]{1,0:T(8,128)(2,1)S(1)} %get-tuple-element.65.queries, f32[256,1024]{1,0:T(8,128)S(1)} %get-tuple-element.80.attention.rest_6_, ...), custom_call_target="tpu_custom_call" | custom-call | flops 67108864 | bytes 3946496 | tf_op jit(solution)/shard_map/pallas_call | solution.py:374
  33.8 1.6 %collective-permute-start.15 = (bf16[512,128]{1,0:T(8,128)(2,1)S(1)}, bf16[512,128]{1,0:T(8,128)(2,1)S(1)}, u32[]{:S(2)}, u32[]{:S(2)}) collective-permute-start(bf16[512,128]{1,0:T(8,128)(2,1)S(1)} %get-tuple-element.86.refs_0_), channel_id=1, source_target_pairs={{0,2},{1,5},{2,0},{3,7},{4,6},{5,1},{6,4},{7,3},{8,10},{9,13},{10,... | collective-permute-start | bytes 393224 | tf_op jit(solution)/shard_map/ppermute | solution.py:396
  35.4 0.0 collective-permute-start.16
  35.4 0.5 collective-permute-start.14
  36.0 0.6 %shard_map.109 = (bf16[256,1024]{1,0:T(8,128)(2,1)S(1)}, f32[1,256]{1,0:T(1,128)S(1)}, bf16[512,128]{1,0:T(8,128)(2,1)S(1)}, bf16[512,128]{1,0:T(8,128)(2,1)S(1)}) custom-call(s32[1,256]{1,0:T(1,128)S(1)} %get-tuple-element.56.length, bf16[256,2048]{1,0:T(8,128)(2,1)S(1)} %get-tuple-element.65.queries, f32[256,1024]{1,0:T(8,128)S(1)} %get-tuple-element.77.attention.rest_7_, ...), custom_call_target="tpu_custom_call" | custom-call | flops 67108864 | bytes 3946496 | tf_op jit(solution)/shard_map/pallas_call | solution.py:374
  36.6 1.7 %collective-permute-start.18 = (bf16[512,128]{1,0:T(8,128)(2,1)S(1)}, bf16[512,128]{1,0:T(8,128)(2,1)S(1)}, u32[]{:S(2)}, u32[]{:S(2)}) collective-permute-start(bf16[512,128]{1,0:T(8,128)(2,1)S(1)} %get-tuple-element.92.refs_0_), channel_id=1, source_target_pairs={{0,2},{1,5},{2,0},{3,7},{4,6},{5,1},{6,4},{7,3},{8,10},{9,13},{10,... | collective-permute-start | bytes 393224 | tf_op jit(solution)/shard_map/ppermute | solution.py:396
  38.2 0.0 collective-permute-start.19
  38.2 0.9 %collective-permute-done.15.refs_2_ = bf16[512,128]{1,0:T(8,128)(2,1)S(1)} collective-permute-done((bf16[512,128]{1,0:T(8,128)(2,1)S(1)}, bf16[512,128]{1,0:T(8,128)(2,1)S(1)}, u32[]{:S(2)}, u32[]{:S(2)}) %collective-permute-start.15) | collective-permute-done | bytes 131104 | tf_op jit(solution)/shard_map/ppermute | solution.py:396
  39.2 0.0 collective-permute-start.17
  39.2 1.0 %collective-permute-done.16.refs_3_ = bf16[512,128]{1,0:T(8,128)(2,1)S(1)} collective-permute-done((bf16[512,128]{1,0:T(8,128)(2,1)S(1)}, bf16[512,128]{1,0:T(8,128)(2,1)S(1)}, u32[]{:S(2)}, u32[]{:S(2)}) %collective-permute-start.16) | collective-permute-done | bytes 131104 | tf_op jit(solution)/shard_map/ppermute | solution.py:396
  40.2 0.0 collective-permute-done.14.refs_1_
  40.2 0.3 shard_map.111
  40.5 0.8 %collective-permute-start.23 = (bf16[512,128]{1,0:T(8,128)(2,1)S(1)}, bf16[512,128]{1,0:T(8,128)(2,1)S(1)}, u32[]{:S(2)}, u32[]{:S(2)}) collective-permute-start(bf16[512,128]{1,0:T(8,128)(2,1)S(1)} %get-tuple-element.101), channel_id=1, source_target_pairs={{0,4},{1,3},{2,6},{3,1},{4,0},{5,7},{6,2},{7,5},{8,12},{9,11},{10,... | collective-permute-start | bytes 393224 | tf_op jit(solution)/shard_map/ppermute | solution.py:396
  41.4 0.9 %collective-permute-start.24 = (bf16[512,128]{1,0:T(8,128)(2,1)S(1)}, bf16[512,128]{1,0:T(8,128)(2,1)S(1)}, u32[]{:S(2)}, u32[]{:S(2)}) collective-permute-start(bf16[512,128]{1,0:T(8,128)(2,1)S(1)} %get-tuple-element.102), channel_id=1, source_target_pairs={{0,1},{1,0},{2,3},{3,2},{4,5},{5,4},{6,7},{7,6},{8,9},{9,8},{10,11... | collective-permute-start | bytes 393224 | tf_op jit(solution)/shard_map/ppermute | solution.py:396
  42.3 0.0 collective-permute-done.18.refs_2_
  42.3 0.5 collective-permute-start.25
  42.7 4.3 %shard_map.112 = (bf16[256,2048]{1,0:T(8,128)(2,1)}, bf16[256,2048]{1,0:T(8,128)(2,1)}, f32[8,128]{1,0:T(8,128)S(1)}) custom-call(s32[1,256]{1,0:T(1,128)S(1)} %get-tuple-element.56.length, f32[1,256]{1,0:T(1,128)S(1)} %get-tuple-element.79.inverse_rms, f32[1,2048]{1,0:T(1,128)S(1)} %bitcast.18, bf16[256,1024]{1,0:T(8,128)(2,1)S(1)} %get-tuple-element.57.rest_0_.keys, ...), custom_call_target="tpu_custom_call" | custom-call | flops 671088640 | bytes 7878656 | tf_op jit(solution)/shard_map/pallas_call | solution.py:374
  47.1 0.0 collective-permute-done.19.refs_3_
  47.1 0.0 collective-permute-done.17.refs_1_
  47.1 0.3 shard_map.113
  47.4 1.2 %collective-permute-start.20 = (bf16[512,128]{1,0:T(8,128)(2,1)S(1)}, bf16[512,128]{1,0:T(8,128)(2,1)S(1)}, u32[]{:S(2)}, u32[]{:S(2)}) collective-permute-start(bf16[512,128]{1,0:T(8,128)(2,1)S(1)} %get-tuple-element.98), channel_id=1, source_target_pairs={{0,4},{1,3},{2,6},{3,1},{4,0},{5,7},{6,2},{7,5},{8,12},{9,11},{10,... | collective-permute-start | bytes 393224 | tf_op jit(solution)/shard_map/ppermute | solution.py:396
  48.6 0.8 %collective-permute-start.21 = (bf16[512,128]{1,0:T(8,128)(2,1)S(1)}, bf16[512,128]{1,0:T(8,128)(2,1)S(1)}, u32[]{:S(2)}, u32[]{:S(2)}) collective-permute-start(bf16[512,128]{1,0:T(8,128)(2,1)S(1)} %get-tuple-element.99), channel_id=1, source_target_pairs={{0,1},{1,0},{2,3},{3,2},{4,5},{5,4},{6,7},{7,6},{8,9},{9,8},{10,11... | collective-permute-start | bytes 393224 | tf_op jit(solution)/shard_map/ppermute | solution.py:396
  49.4 0.5 collective-permute-start.22
  49.9 3.2 %shard_map.114 = (f32[256,2048]{1,0:T(8,128)S(1)}, f32[256,2048]{1,0:T(8,128)S(1)}) custom-call(s32[1,256]{1,0:T(1,128)S(1)} %get-tuple-element.56.length, bf16[256,2048]{1,0:T(8,128)(2,1)S(1)} %get-tuple-element.65.queries, bf16[16,256,256]{2,1,0:T(8,128)(2,1)S(1)} %get-tuple-element.91.turned, ...), custom_call_target="tpu_custom_call" | custom-call | flops 805306368 | bytes 9438208 | tf_op jit(solution)/shard_map/pallas_call | solution.py:374
  53.0 0.0 collective-permute-done.24.rest_2_
  53.1 1.6 %shard_map.115 = (bf16[256,2048]{1,0:T(8,128)(2,1)}, bf16[256,2048]{1,0:T(8,128)(2,1)}) custom-call(s32[1,256]{1,0:T(1,128)S(1)} %get-tuple-element.56.length, bf16[256,1024]{1,0:T(8,128)(2,1)S(1)} %get-tuple-element.57.rest_0_.keys, bf16[256,1024]{1,0:T(8,128)(2,1)S(1)} %get-tuple-element.59.rest_2_.rest_0_.values, ...), custom_call_target="tpu_custom_call" | custom-call | flops 134217728 | bytes 7865344 | tf_op jit(solution)/shard_map/pallas_call | solution.py:374
  54.7 0.0 collective-permute-done.20.rest_1_
  54.7 0.0 collective-permute-done.22.rest_3_
  54.7 1.6 %shard_map.116 = (bf16[256,2048]{1,0:T(8,128)(2,1)}, bf16[256,2048]{1,0:T(8,128)(2,1)}) custom-call(s32[1,256]{1,0:T(1,128)S(1)} %get-tuple-element.56.length, bf16[256,1024]{1,0:T(8,128)(2,1)S(1)} %get-tuple-element.58.rest_1_.keys, bf16[256,1024]{1,0:T(8,128)(2,1)S(1)} %get-tuple-element.60.rest_3_.rest_1_.values, ...), custom_call_target="tpu_custom_call", output_to_operand_aliasing={{0}: (9, {}), {1}: (10, {})} | custom-call | flops 134217728 | bytes 9962496 | tf_op jit(solution)/shard_map/pallas_call | solution.py:374
  (8 shorter events, 0.0 us)
Async XLA Ops:
  3.2 7.2 %collective-permute-start.1 = (bf16[512,128]{1,0:T(8,128)(2,1)S(1)}, bf16[512,128]{1,0:T(8,128)(2,1)S(1)}, u32[]{:S(2)}, u32[]{:S(2)}) collective-permute-start(bf16[512,128]{1,0:T(8,128)(2,1)S(1)} %get-tuple-element.62.refs_0_), channel_id=1, source_target_pairs={{0,2},{1,5},{2,0},{3,7},{4,6},{5,1},{6,4},{7,3},{8,10},{9,13},{10,... | collective-permute-start | bytes 393224 | tf_op jit(solution)/shard_map/ppermute | solution.py:396
  6.2 4.4 %collective-permute-start.2 = (bf16[512,128]{1,0:T(8,128)(2,1)S(1)}, bf16[512,128]{1,0:T(8,128)(2,1)S(1)}, u32[]{:S(2)}, u32[]{:S(2)}) collective-permute-start(bf16[512,128]{1,0:T(8,128)(2,1)S(1)} %get-tuple-element.63), channel_id=1, source_target_pairs={{0,5},{1,2},{2,7},{3,0},{4,1},{5,6},{6,3},{7,4},{8,13},{9,10},{10,... | collective-permute-start | bytes 393224 | tf_op jit(solution)/shard_map/ppermute | solution.py:396
  6.2 4.4 %collective-permute-start = (bf16[512,128]{1,0:T(8,128)(2,1)S(1)}, bf16[512,128]{1,0:T(8,128)(2,1)S(1)}, u32[]{:S(2)}, u32[]{:S(2)}) collective-permute-start(bf16[512,128]{1,0:T(8,128)(2,1)S(1)} %get-tuple-element.63), channel_id=1, source_target_pairs={{0,1},{1,0},{2,3},{3,2},{4,5},{5,4},{6,7},{7,6},{8,9},{9,8},{10,11... | collective-permute-start | bytes 393224 | tf_op jit(solution)/shard_map/ppermute | solution.py:396
  8.4 5.8 %collective-permute-start.4 = (bf16[512,128]{1,0:T(8,128)(2,1)S(1)}, bf16[512,128]{1,0:T(8,128)(2,1)S(1)}, u32[]{:S(2)}, u32[]{:S(2)}) collective-permute-start(bf16[512,128]{1,0:T(8,128)(2,1)S(1)} %get-tuple-element.67.refs_0_), channel_id=1, source_target_pairs={{0,2},{1,5},{2,0},{3,7},{4,6},{5,1},{6,4},{7,3},{8,10},{9,13},{10,... | collective-permute-start | bytes 393224 | tf_op jit(solution)/shard_map/ppermute | solution.py:396
  10.4 4.4 %collective-permute-start.5 = (bf16[512,128]{1,0:T(8,128)(2,1)S(1)}, bf16[512,128]{1,0:T(8,128)(2,1)S(1)}, u32[]{:S(2)}, u32[]{:S(2)}) collective-permute-start(bf16[512,128]{1,0:T(8,128)(2,1)S(1)} %get-tuple-element.68), channel_id=1, source_target_pairs={{0,5},{1,2},{2,7},{3,0},{4,1},{5,6},{6,3},{7,4},{8,13},{9,10},{10,... | collective-permute-start | bytes 393224 | tf_op jit(solution)/shard_map/ppermute | solution.py:396
  10.4 4.4 %collective-permute-start.3 = (bf16[512,128]{1,0:T(8,128)(2,1)S(1)}, bf16[512,128]{1,0:T(8,128)(2,1)S(1)}, u32[]{:S(2)}, u32[]{:S(2)}) collective-permute-start(bf16[512,128]{1,0:T(8,128)(2,1)S(1)} %get-tuple-element.68), channel_id=1, source_target_pairs={{0,1},{1,0},{2,3},{3,2},{4,5},{5,4},{6,7},{7,6},{8,9},{9,8},{10,11... | collective-permute-start | bytes 393224 | tf_op jit(solution)/shard_map/ppermute | solution.py:396
  10.6 12.6 %copy-start = (bf16[1,256,2048]{2,1,0:T(8,128)(2,1)S(1)}, bf16[1,256,2048]{2,1,0:T(8,128)(2,1)}, u32[]{:S(2)}) copy-start(bf16[1,256,2048]{2,1,0:T(8,128)(2,1)} %param.10) | copy-start | bytes 3145732
  10.6 12.6 %copy-start.1 = (f32[2048]{0:T(1024)S(1)}, f32[2048]{0:T(1024)}, u32[]{:S(2)}) copy-start(f32[2048]{0:T(1024)} %param.11) | copy-start | bytes 24580
  10.9 6.3 %collective-permute-start.9 = (bf16[512,128]{1,0:T(8,128)(2,1)S(1)}, bf16[512,128]{1,0:T(8,128)(2,1)S(1)}, u32[]{:S(2)}, u32[]{:S(2)}) collective-permute-start(bf16[512,128]{1,0:T(8,128)(2,1)S(1)} %get-tuple-element.73), channel_id=1, source_target_pairs={{0,4},{1,3},{2,6},{3,1},{4,0},{5,7},{6,2},{7,5},{8,12},{9,11},{10,... | collective-permute-start | bytes 393224 | tf_op jit(solution)/shard_map/ppermute | solution.py:396
  13.0 10.2 %collective-permute-start.10 = (bf16[512,128]{1,0:T(8,128)(2,1)S(1)}, bf16[512,128]{1,0:T(8,128)(2,1)S(1)}, u32[]{:S(2)}, u32[]{:S(2)}) collective-permute-start(bf16[512,128]{1,0:T(8,128)(2,1)S(1)} %get-tuple-element.74), channel_id=1, source_target_pairs={{0,1},{1,0},{2,3},{3,2},{4,5},{5,4},{6,7},{7,6},{8,9},{9,8},{10,11... | collective-permute-start | bytes 393224 | tf_op jit(solution)/shard_map/ppermute | solution.py:396
  14.2 9.0 %collective-permute-start.11 = (bf16[512,128]{1,0:T(8,128)(2,1)S(1)}, bf16[512,128]{1,0:T(8,128)(2,1)S(1)}, u32[]{:S(2)}, u32[]{:S(2)}) collective-permute-start(bf16[512,128]{1,0:T(8,128)(2,1)S(1)} %get-tuple-element.75), channel_id=1, source_target_pairs={{0,5},{1,2},{2,7},{3,0},{4,1},{5,6},{6,3},{7,4},{8,13},{9,10},{10,... | collective-permute-start | bytes 393224 | tf_op jit(solution)/shard_map/ppermute | solution.py:396
  15.1 8.8 %collective-permute-start.6 = (bf16[512,128]{1,0:T(8,128)(2,1)S(1)}, bf16[512,128]{1,0:T(8,128)(2,1)S(1)}, u32[]{:S(2)}, u32[]{:S(2)}) collective-permute-start(bf16[512,128]{1,0:T(8,128)(2,1)S(1)} %get-tuple-element.70), channel_id=1, source_target_pairs={{0,4},{1,3},{2,6},{3,1},{4,0},{5,7},{6,2},{7,5},{8,12},{9,11},{10,... | collective-permute-start | bytes 393224 | tf_op jit(solution)/shard_map/ppermute | solution.py:396
  17.2 6.8 %collective-permute-start.7 = (bf16[512,128]{1,0:T(8,128)(2,1)S(1)}, bf16[512,128]{1,0:T(8,128)(2,1)S(1)}, u32[]{:S(2)}, u32[]{:S(2)}) collective-permute-start(bf16[512,128]{1,0:T(8,128)(2,1)S(1)} %get-tuple-element.71), channel_id=1, source_target_pairs={{0,1},{1,0},{2,3},{3,2},{4,5},{5,4},{6,7},{7,6},{8,9},{9,8},{10,11... | collective-permute-start | bytes 393224 | tf_op jit(solution)/shard_map/ppermute | solution.py:396
  17.3 6.7 %collective-permute-start.8 = (bf16[512,128]{1,0:T(8,128)(2,1)S(1)}, bf16[512,128]{1,0:T(8,128)(2,1)S(1)}, u32[]{:S(2)}, u32[]{:S(2)}) collective-permute-start(bf16[512,128]{1,0:T(8,128)(2,1)S(1)} %get-tuple-element.72), channel_id=1, source_target_pairs={{0,5},{1,2},{2,7},{3,0},{4,1},{5,6},{6,3},{7,4},{8,13},{9,10},{10,... | collective-permute-start | bytes 393224 | tf_op jit(solution)/shard_map/ppermute | solution.py:396
  24.6 3.6 %collective-permute-start.12 = (f32[2,256]{1,0:T(2,128)S(1)}, f32[2,256]{1,0:T(2,128)S(1)}, u32[]{:S(2)}, u32[]{:S(2)}) collective-permute-start(f32[2,256]{1,0:T(2,128)S(1)} %get-tuple-element.78), channel_id=1, source_target_pairs={{0,8},{8,0},{16,24},{24,16},{1,9},{9,1},{17,25},{25,17},{2,10},{10... | collective-permute-start | bytes 6152 | tf_op jit(solution)/shard_map/ppermute | solution.py:431
  28.3 4.5 %collective-permute-start.13 = (f32[2,256]{1,0:T(2,128)S(1)}, f32[2,256]{1,0:T(2,128)S(1)}, u32[]{:S(2)}, u32[]{:S(2)}) collective-permute-start(f32[2,256]{1,0:T(2,128)S(1)} %add.3.rest_0_), channel_id=1, source_target_pairs={{0,16},{8,24},{16,0},{24,8},{1,17},{9,25},{17,1},{25,9},{2,18},{10... | collective-permute-start | bytes 6152 | tf_op jit(solution)/shard_map/ppermute | solution.py:431
  33.8 5.3 %collective-permute-start.15 = (bf16[512,128]{1,0:T(8,128)(2,1)S(1)}, bf16[512,128]{1,0:T(8,128)(2,1)S(1)}, u32[]{:S(2)}, u32[]{:S(2)}) collective-permute-start(bf16[512,128]{1,0:T(8,128)(2,1)S(1)} %get-tuple-element.86.refs_0_), channel_id=1, source_target_pairs={{0,2},{1,5},{2,0},{3,7},{4,6},{5,1},{6,4},{7,3},{8,10},{9,13},{10,... | collective-permute-start | bytes 393224 | tf_op jit(solution)/shard_map/ppermute | solution.py:396
  35.4 4.8 %collective-permute-start.16 = (bf16[512,128]{1,0:T(8,128)(2,1)S(1)}, bf16[512,128]{1,0:T(8,128)(2,1)S(1)}, u32[]{:S(2)}, u32[]{:S(2)}) collective-permute-start(bf16[512,128]{1,0:T(8,128)(2,1)S(1)} %get-tuple-element.87), channel_id=1, source_target_pairs={{0,5},{1,2},{2,7},{3,0},{4,1},{5,6},{6,3},{7,4},{8,13},{9,10},{10,... | collective-permute-start | bytes 393224 | tf_op jit(solution)/shard_map/ppermute | solution.py:396
  35.4 4.8 %collective-permute-start.14 = (bf16[512,128]{1,0:T(8,128)(2,1)S(1)}, bf16[512,128]{1,0:T(8,128)(2,1)S(1)}, u32[]{:S(2)}, u32[]{:S(2)}) collective-permute-start(bf16[512,128]{1,0:T(8,128)(2,1)S(1)} %get-tuple-element.87), channel_id=1, source_target_pairs={{0,1},{1,0},{2,3},{3,2},{4,5},{5,4},{6,7},{7,6},{8,9},{9,8},{10,11... | collective-permute-start | bytes 393224 | tf_op jit(solution)/shard_map/ppermute | solution.py:396
  36.6 5.7 %collective-permute-start.18 = (bf16[512,128]{1,0:T(8,128)(2,1)S(1)}, bf16[512,128]{1,0:T(8,128)(2,1)S(1)}, u32[]{:S(2)}, u32[]{:S(2)}) collective-permute-start(bf16[512,128]{1,0:T(8,128)(2,1)S(1)} %get-tuple-element.92.refs_0_), channel_id=1, source_target_pairs={{0,2},{1,5},{2,0},{3,7},{4,6},{5,1},{6,4},{7,3},{8,10},{9,13},{10,... | collective-permute-start | bytes 393224 | tf_op jit(solution)/shard_map/ppermute | solution.py:396
  38.2 8.8 %collective-permute-start.19 = (bf16[512,128]{1,0:T(8,128)(2,1)S(1)}, bf16[512,128]{1,0:T(8,128)(2,1)S(1)}, u32[]{:S(2)}, u32[]{:S(2)}) collective-permute-start(bf16[512,128]{1,0:T(8,128)(2,1)S(1)} %get-tuple-element.93), channel_id=1, source_target_pairs={{0,5},{1,2},{2,7},{3,0},{4,1},{5,6},{6,3},{7,4},{8,13},{9,10},{10,... | collective-permute-start | bytes 393224 | tf_op jit(solution)/shard_map/ppermute | solution.py:396
  39.2 7.9 %collective-permute-start.17 = (bf16[512,128]{1,0:T(8,128)(2,1)S(1)}, bf16[512,128]{1,0:T(8,128)(2,1)S(1)}, u32[]{:S(2)}, u32[]{:S(2)}) collective-permute-start(bf16[512,128]{1,0:T(8,128)(2,1)S(1)} %get-tuple-element.93), channel_id=1, source_target_pairs={{0,1},{1,0},{2,3},{3,2},{4,5},{5,4},{6,7},{7,6},{8,9},{9,8},{10,11... | collective-permute-start | bytes 393224 | tf_op jit(solution)/shard_map/ppermute | solution.py:396
  40.5 8.9 %collective-permute-start.23 = (bf16[512,128]{1,0:T(8,128)(2,1)S(1)}, bf16[512,128]{1,0:T(8,128)(2,1)S(1)}, u32[]{:S(2)}, u32[]{:S(2)}) collective-permute-start(bf16[512,128]{1,0:T(8,128)(2,1)S(1)} %get-tuple-element.101), channel_id=1, source_target_pairs={{0,4},{1,3},{2,6},{3,1},{4,0},{5,7},{6,2},{7,5},{8,12},{9,11},{10,... | collective-permute-start | bytes 393224 | tf_op jit(solution)/shard_map/ppermute | solution.py:396
  41.4 11.7 %collective-permute-start.24 = (bf16[512,128]{1,0:T(8,128)(2,1)S(1)}, bf16[512,128]{1,0:T(8,128)(2,1)S(1)}, u32[]{:S(2)}, u32[]{:S(2)}) collective-permute-start(bf16[512,128]{1,0:T(8,128)(2,1)S(1)} %get-tuple-element.102), channel_id=1, source_target_pairs={{0,1},{1,0},{2,3},{3,2},{4,5},{5,4},{6,7},{7,6},{8,9},{9,8},{10,11... | collective-permute-start | bytes 393224 | tf_op jit(solution)/shard_map/ppermute | solution.py:396
  42.3 10.8 %collective-permute-start.25 = (bf16[512,128]{1,0:T(8,128)(2,1)S(1)}, bf16[512,128]{1,0:T(8,128)(2,1)S(1)}, u32[]{:S(2)}, u32[]{:S(2)}) collective-permute-start(bf16[512,128]{1,0:T(8,128)(2,1)S(1)} %get-tuple-element.103), channel_id=1, source_target_pairs={{0,5},{1,2},{2,7},{3,0},{4,1},{5,6},{6,3},{7,4},{8,13},{9,10},{10,... | collective-permute-start | bytes 393224 | tf_op jit(solution)/shard_map/ppermute | solution.py:396
  47.4 7.3 %collective-permute-start.20 = (bf16[512,128]{1,0:T(8,128)(2,1)S(1)}, bf16[512,128]{1,0:T(8,128)(2,1)S(1)}, u32[]{:S(2)}, u32[]{:S(2)}) collective-permute-start(bf16[512,128]{1,0:T(8,128)(2,1)S(1)} %get-tuple-element.98), channel_id=1, source_target_pairs={{0,4},{1,3},{2,6},{3,1},{4,0},{5,7},{6,2},{7,5},{8,12},{9,11},{10,... | collective-permute-start | bytes 393224 | tf_op jit(solution)/shard_map/ppermute | solution.py:396
  48.6 6.1 %collective-permute-start.21 = (bf16[512,128]{1,0:T(8,128)(2,1)S(1)}, bf16[512,128]{1,0:T(8,128)(2,1)S(1)}, u32[]{:S(2)}, u32[]{:S(2)}) collective-permute-start(bf16[512,128]{1,0:T(8,128)(2,1)S(1)} %get-tuple-element.99), channel_id=1, source_target_pairs={{0,1},{1,0},{2,3},{3,2},{4,5},{5,4},{6,7},{7,6},{8,9},{9,8},{10,11... | collective-permute-start | bytes 393224 | tf_op jit(solution)/shard_map/ppermute | solution.py:396
  49.4 5.3 %collective-permute-start.22 = (bf16[512,128]{1,0:T(8,128)(2,1)S(1)}, bf16[512,128]{1,0:T(8,128)(2,1)S(1)}, u32[]{:S(2)}, u32[]{:S(2)}) collective-permute-start(bf16[512,128]{1,0:T(8,128)(2,1)S(1)} %get-tuple-element.100), channel_id=1, source_target_pairs={{0,5},{1,2},{2,7},{3,0},{4,1},{5,6},{6,3},{7,4},{8,13},{9,10},{10,... | collective-permute-start | bytes 393224 | tf_op jit(solution)/shard_map/ppermute | solution.py:396

commit v6 on v5

--- a/solution.py
+++ b/solution.py
@@ -14,7 +14,8 @@
 F32 = jnp.float32
 BF16 = jnp.bfloat16
 VMEM_LIMIT = 24 * 1024 * 1024
-PIECES = 2
+FORWARD_PIECES = 2
+BACKWARD_PIECES = 1
 
 VMEM = pl.BlockSpec(memory_space=pltpu.VMEM)
 SMEM = pl.BlockSpec(memory_space=pltpu.SMEM)
@@ -134,30 +135,30 @@
                 rows[at : at + 1, :] = jnp.full((1, HD), weight, F32)
 
 
-def state_kernel(piece, grid, *rest):
-    pair = grid[2]
-    first, last = piece == 0, piece == PIECES - 1
-    keys_hbm, values_hbm, seg_len = rest[:3]
-    parent_hbm, rest = (rest[3], rest[4:]) if last else (None, rest[3:])
-    (keys, values), halves, rest = rest[:2], rest[2 : 2 + pair], rest[2 + pair :]
+def write_halves(full, outs, core, pair):
+    rows = full.shape[0] * pair // len(outs)
+    for piece in range(len(outs) // pair):
+        halves = row_halves(full.at[pl.ds(piece * rows, rows), :], core, pair)
+        for half, out in zip(halves, outs[piece * pair : (piece + 1) * pair]):
+            out[...] = half[...]
+
+
+def state_kernel(grid, seg_len, keys_hbm, values_hbm, parent_hbm, keys, values, length, up, down, *rest):
     outs, (full, sems, parent, parent_sem) = rest[:-4], rest[-4:]
     rows, width = keys.shape
     chunk = rows // 4 if rows % 64 == 0 else rows
-    cols = slice(piece * width, (piece + 1) * width)
     copies = []
     for step in range(rows // chunk):
         part = slice(step * chunk, (step + 1) * chunk)
         for j, (src, dst) in enumerate(((keys_hbm, keys), (values_hbm, values))):
-            copies.append(pltpu.make_async_copy(src.at[part, cols], dst.at[part, :], sems.at[j, step]))
+            copies.append(pltpu.make_async_copy(src.at[part, :], dst.at[part, :], sems.at[j, step]))
+    few = pltpu.make_async_copy(parent_hbm, parent, parent_sem)
+    few.start()
     for copy in copies:
         copy.start()
-    if first:
-        outs[0][...] = jnp.full(outs[0].shape, seg_len[0], jnp.int32)
-    if last:
-        copy = pltpu.make_async_copy(parent_hbm, parent, parent_sem)
-        copy.start()
-        copy.wait()
-        write_weights(grid, parent, *outs[-2:])
+    length[...] = jnp.full(length.shape, seg_len[0], jnp.int32)
+    few.wait()
+    write_weights(grid, parent, up, down)
     live = lax.broadcasted_iota(jnp.int32, (rows, HD), 0) < seg_len[0]
     for copy in copies:
         copy.wait()
@@ -165,8 +166,7 @@
         cols = head_cols(head)
         masked = jnp.where(live, keys[:, cols], jnp.zeros((), BF16))
         full[head * HD : (head + 1) * HD, :] = tn(masked, values[:, cols]).astype(BF16)
-    for half, out in zip(row_halves(full, my_place(grid)[2], pair), halves):
-        out[...] = half[...]
+    write_halves(full, outs, my_place(grid)[2], grid[2])
 
 
 def mix_kernel(sources, weights, *refs):
@@ -210,10 +210,8 @@
     return pieces[head // per_piece], head_cols(head % per_piece)
 
 
-def local_kernel(heads, length, queries_hbm, *rest):
-    keys, values, rest = rest[:PIECES], rest[PIECES : 2 * PIECES], rest[2 * PIECES :]
-    queries, local, turned, sems = rest[-4:]
-    rows = length.shape[1]
+def local_kernel(heads, length, queries_hbm, keys, values, *rest):
+    queries, local, sems = rest[-3:]
     group = 4 if heads % 4 == 0 else 1
     copies = []
     for at in range(0, heads, group):
@@ -222,18 +220,12 @@
     for copy in copies:
         copy.start()
     keep = keep_mask(length, False)
-    keep_turned = keep_mask(length, True)
     for head in range(heads):
         if head % group == 0:
             copies[head // group].wait()
         cols = head_cols(head)
-        key_piece, at = head_of(keys, head)
-        key = key_piece[:, at]
-        value_piece, _ = head_of(values, head)
-        query = queries[:, cols]
-        scores = jnp.where(keep, nt(query, key), 0.0).astype(BF16)
-        local[:, cols] = nn(scores, value_piece[:, at])
-        turned[head] = jnp.where(keep_turned, nt(key, query), 0.0).astype(BF16)
+        scores = jnp.where(keep, nt(queries[:, cols], keys[:, cols]), 0.0).astype(BF16)
+        local[:, cols] = nn(scores, values[:, cols])
 
 
 def token_rows(total):
@@ -266,10 +258,10 @@
     sums[...] = both
 
 
-def grad_kernel(piece, groups, grid, scale, length, queries, attention, cotangent, gain, *rest):
-    all_sums, rest = rest[:groups], rest[groups:]
+def grad_kernel(piece, groups, grid, scale, length, queries, cotangent, gain, *rest):
+    all_sums, attention, rest = split_refs(rest, groups, FORWARD_PIECES, len(rest) - groups - FORWARD_PIECES)
     (grad_out, inverse_rms), halves, full = rest[:2], rest[2:-1], rest[-1]
-    rows, width = attention.shape
+    rows, width = grad_out.shape
     features = HEADS * HD
     total = all_sums[0][...]
     for other in all_sums[1:]:
@@ -283,34 +275,35 @@
     shrink = token_columns(shrink)
     for head in range(width // HD):
         cols = head_cols(head)
-        whole = head_cols(piece * width // HD + head)
+        place = piece * width // HD + head
+        whole = head_cols(place)
+        out_piece, at = head_of(attention, place)
         gain_grad = cotangent[:, whole].astype(F32) * gain[:, whole]
-        grad = (live_inverse * gain_grad - attention[:, cols] * shrink).astype(BF16)
+        grad = (live_inverse * gain_grad - out_piece[:, at] * shrink).astype(BF16)
         grad_out[:, cols] = grad
         full[head * HD : (head + 1) * HD, :] = (scale * tn(queries[:, whole], grad)).astype(BF16)
-    for half, out in zip(row_halves(full, my_place(grid)[2], grid[2]), halves):
-        out[...] = half[...]
-
-
-def query_kernel(heads, scale, length, inverse_rms, gain, *rest):
-    keys, values, grads, attention, prefix, rest = split_refs(rest, *[PIECES] * 5, len(rest) - 5 * PIECES)
+    write_halves(full, halves, my_place(grid)[2], grid[2])
+
+
+def query_kernel(heads, scale, length, inverse_rms, gain, keys, values, *rest):
+    sizes = (BACKWARD_PIECES, FORWARD_PIECES, FORWARD_PIECES)
+    grads, attention, prefix, rest = split_refs(rest, *sizes, len(rest) - sum(sizes))
     attended_hbm, query_hbm, token, attended, query_grad, sems = rest[-6:]
     token[...] = jnp.zeros_like(token)
     keep = keep_mask(length, False)
     inverse = token_columns(inverse_rms[...])
-    group = 4 if heads % 4 == 0 else 1
+    group = 8 if heads % 8 == 0 else 1
     copies = []
     for head in range(heads):
         cols = head_cols(head)
-        key_piece, at = head_of(keys, head)
-        value_piece, _ = head_of(values, head)
-        grad_piece, _ = head_of(grads, head)
-        out_piece, _ = head_of(attention, head)
-        prefix_piece, state = prefix[head // (heads // PIECES)], head % (heads // PIECES)
+        grad_piece, at = head_of(grads, head)
         grad = grad_piece[:, at]
-        grad_scores = jnp.where(keep, nt(grad, value_piece[:, at]), 0.0).astype(BF16)
+        out_piece, at = head_of(attention, head)
+        per_piece = heads // FORWARD_PIECES
+        prefix_piece, state = prefix[head // per_piece], head % per_piece
+        grad_scores = jnp.where(keep, nt(grad, values[:, cols]), 0.0).astype(BF16)
         carried = nt(grad, prefix_piece[state * HD : (state + 1) * HD, :])
-        query_grad[:, cols] = (scale * (carried + nn(grad_scores, key_piece[:, at]))).astype(BF16)
+        query_grad[:, cols] = (scale * (carried + nn(grad_scores, keys[:, cols]))).astype(BF16)
         attended[:, cols] = (out_piece[:, at] * inverse * gain[:, cols]).astype(BF16)
         if (head + 1) % group == 0:
             done = slice((head + 1 - group) * HD, (head + 1) * HD)
@@ -322,25 +315,24 @@
         copy.wait()
 
 
-def back_kernel(heads, scale, length, queries, turned, *rest):
-    values, grads, rest = split_refs(rest, PIECES, PIECES, len(rest) - 2 * PIECES)
-    key_part, value_part = rest[-2:]
+def back_kernel(heads, scale, length, queries, keys, values, *rest):
+    grads, (key_part, value_part) = rest[:BACKWARD_PIECES], rest[-2:]
     keep = keep_mask(length, True)
     for head in range(heads):
         cols = head_cols(head)
-        value_piece, at = head_of(values, head)
-        grad_piece, _ = head_of(grads, head)
-        grad = grad_piece[:, at]
-        grad_scores = jnp.where(keep, nt(value_piece[:, at], grad), 0.0).astype(BF16)
-        key_part[:, cols] = scale * nn(grad_scores, queries[:, cols])
-        value_part[:, cols] = scale * nn(turned[head], grad)
+        grad_piece, at = head_of(grads, head)
+        query, grad = queries[:, cols], grad_piece[:, at]
+        turned = jnp.where(keep, nt(values[:, cols], grad), 0.0).astype(BF16)
+        key_part[:, cols] = scale * nn(turned, query)
+        turned = jnp.where(keep, nt(keys[:, cols], query), 0.0).astype(BF16)
+        value_part[:, cols] = scale * nn(turned, grad)
 
 
 def final_kernel(piece, grid, counts, length, keys, values, key_part, value_part, *rest):
     received, rest = rest[: sum(counts)], rest[sum(counts) :]
     key_hbm, value_hbm, key_grad, value_grad, below, sems = rest[-6:]
     join_halves(split_refs(received, *counts), below, my_place(grid)[2], grid[2])
-    rows, width = keys.shape
+    rows, width = key_grad.shape
     live = jnp.where(live_rows(length, rows), 1.0, 0.0)
     heads = width // HD
     group = 2 if heads % 2 == 0 else 1
@@ -349,8 +341,8 @@
         cols = head_cols(head)
         whole = head_cols(piece * heads + head)
         state = below[head * HD : (head + 1) * HD, :]
-        key_grad[:, cols] = (key_part[:, whole] + live * nt(values[:, cols], state)).astype(BF16)
-        value_grad[:, cols] = (value_part[:, whole] + live * nn(keys[:, cols], state)).astype(BF16)
+        key_grad[:, cols] = (key_part[:, whole] + live * nt(values[:, whole], state)).astype(BF16)
+        value_grad[:, cols] = (value_part[:, whole] + live * nn(keys[:, whole], state)).astype(BF16)
         if (head + 1) % group == 0:
             done = slice((head + 1 - group) * HD, (head + 1) * HD)
             there = slice(piece * width + done.start, piece * width + done.stop)
@@ -421,15 +413,10 @@
 
 
 def token_sums(sums, groups):
-    if groups & (groups - 1):
-        moves = [[(j, (j + step) % groups) for j in range(groups)] for step in range(1, groups)]
-        return [sums] + [lax.ppermute(sums, "head", pairs) for pairs in moves]
     parts = [sums]
-    step = 1
-    while step < groups:
-        sums = parts[0] if len(parts) == 1 else parts[0] + parts[1]
-        parts = [sums, lax.ppermute(sums, "head", [(j, j ^ step) for j in range(groups)])]
-        step *= 2
+    for step in range(1, groups):
+        moves = [(j, target_of(j, step, groups)) for j in range(groups)]
+        parts.append(lax.ppermute(sums, "head", moves))
     return parts
 
 
@@ -442,96 +429,87 @@
     cot = cotangent[0]
     gain = out_gain[None]
     shape = jax.ShapeDtypeStruct
-    width = features // PIECES
     narrow = shape((rows, features), BF16)
     wide = shape((rows, features), F32)
-    narrow_piece = shape((rows, width), BF16)
-    wide_piece = shape((rows, width), F32)
-    state = shape((width, HD), BF16)
-    half = shape((width // pair, HD), BF16)
     row = shape((1, rows), F32)
     members = line_length(grid) * pair
     weight_rows = shape((members * members, HD), F32)
-    state_scratch = pltpu.VMEM(state.shape, BF16)
     sems = pltpu.SemaphoreType.DMA((2, heads))
     counts = [line_length(grid)] * pair
     unit = 2 * heads * rows * HD
-    every = range(PIECES)
+
+    def halves(pieces):
+        return [shape((features // (pair * pieces), HD), BF16)] * pair
 
     def mix(arrived, weights, after=()):
-        return call(functools.partial(mix_kernel, members), [half] * members, (weights, *arrived), after=after)
+        like = [shape(arrived[0].shape, BF16)] * members
+        return call(functools.partial(mix_kernel, members), like, (weights, *arrived), after=after)
 
     def flat(parts):
         return [block for part in parts for block in part]
 
-    keys, vals, own = [], [], []
-    for piece in every:
-        extra = [shape((1, rows), jnp.int32)] if piece == 0 else []
-        extra += [weight_rows] * 2 if piece == PIECES - 1 else []
-        key, value, *rest = call(
-            functools.partial(state_kernel, piece, grid),
-            [narrow_piece] * 2 + [half] * pair + extra,
-            (key_rows[0], values[0], seg_len) + ((parent[None],) if piece == PIECES - 1 else ()),
-            [state_scratch, sems, pltpu.SMEM((1, segs), jnp.int32), pltpu.SemaphoreType.DMA(())],
-            unit * HD // PIECES, (0, 1, 3), (2,),
-        )
-        keys.append(key)
-        vals.append(value)
-        own.append(rest[:pair])
-        if piece == 0:
-            length = rest[pair]
-    up, down = rest[-2:]
-    mixed = [mix(gather_line(own[piece], grid), up) for piece in every]
-    query, local, turned = call(
+    key, value, length, up, down, *own = call(
+        functools.partial(state_kernel, grid),
+        [narrow, narrow, shape((1, rows), jnp.int32), weight_rows, weight_rows] + halves(FORWARD_PIECES) * FORWARD_PIECES,
+        (seg_len, key_rows[0], values[0], parent[None]),
+        [pltpu.VMEM((features, HD), BF16), sems, pltpu.SMEM((1, segs), jnp.int32), pltpu.SemaphoreType.DMA(())],
+        unit * HD, (1, 2, 3), (0,),
+    )
+    mixed = [mix(gather_line(part, grid), up) for part in split_refs(own, *[pair] * FORWARD_PIECES)]
+    query, local = call(
         functools.partial(local_kernel, heads),
-        [narrow, wide, shape((heads, rows, rows), BF16)],
-        (length, queries[0], *keys, *vals), [pltpu.SemaphoreType.DMA((heads,))], unit * rows * 3, (1,), after=(mixed[0][0],),
+        [narrow, wide],
+        (length, queries[0], key, value), [pltpu.SemaphoreType.DMA((heads,))], unit * rows * 2, (1,),
+        after=(mixed[0][0],),
     )
     attention, prefix, sums = [], [], []
-    for piece in every:
+    width = features // FORWARD_PIECES
+    for piece in range(FORWARD_PIECES):
         out, total, joined = call(
             functools.partial(carry_kernel, piece, grid, counts, scale),
-            [wide_piece, shape((2, rows), F32), state],
+            [shape((rows, width), F32), shape((2, rows), F32), shape((width, HD), BF16)],
             (length, query, local, cot, gain, *flat(scatter_line(mixed[piece], grid)), *sums),
-            (), unit * HD // PIECES,
+            (), unit * HD // FORWARD_PIECES,
         )
         attention.append(out)
         prefix.append(joined)
         sums = [total]
     sums = token_sums(sums[0], groups)
     grads, state_grad = [], []
-    for piece in every:
-        grad_out, inverse_rms, *halves = call(
+    width = features // BACKWARD_PIECES
+    for piece in range(BACKWARD_PIECES):
+        grad_out, inverse_rms, *parts = call(
             functools.partial(grad_kernel, piece, len(sums), grid, scale),
-            [narrow_piece, row] + [half] * pair,
-            (length, query, attention[piece], cot, gain, *sums), [state_scratch], unit * HD // PIECES,
+            [shape((rows, width), BF16), row] + halves(BACKWARD_PIECES),
+            (length, query, cot, gain, *sums, *attention), [pltpu.VMEM((width, HD), BF16)],
+            unit * HD // BACKWARD_PIECES,
         )
         grads.append(grad_out)
-        state_grad.append(halves)
+        state_grad.append(parts)
+    attended, query_grad, token = call(
+        functools.partial(query_kernel, heads, scale),
+        [narrow, narrow, shape((8, HD), F32)],
+        (length, inverse_rms, gain, key, value, *grads, *attention, *prefix),
+        [pltpu.VMEM(narrow.shape, BF16)] * 2 + [sems], unit * (2 * rows + HD),
+        out_specs=[HBM, HBM, VMEM],
+    )
     mixed = []
-    for piece in every:
-        mixed.append(mix(gather_line(state_grad[piece], grid), down, () if piece == 0 else (token,)))
-        if piece == 0:
-            attended, query_grad, token = call(
-                functools.partial(query_kernel, heads, scale),
-                [narrow, narrow, shape((8, HD), F32)],
-                (length, inverse_rms, gain, *keys, *vals, *grads, *attention, *prefix),
-                [pltpu.VMEM(narrow.shape, BF16)] * 2 + [sems], unit * (2 * rows + HD),
-                after=(mixed[0][0],), out_specs=[HBM, HBM, VMEM],
-            )
+    for part in state_grad:
+        mixed.append(mix(gather_line(part, grid), down, (token,) if len(mixed) == BACKWARD_PIECES - 1 else ()))
     key_part, value_part = call(
         functools.partial(back_kernel, heads, scale),
-        [wide, wide], (length, query, turned, *vals, *grads), (), unit * 3 * rows, after=(mixed[-1][0],),
+        [wide, wide], (length, query, key, value, *grads), (), unit * 4 * rows, after=(mixed[-1][0],),
     )
     results = []
-    for piece in every:
+    for piece in range(BACKWARD_PIECES):
         below = flat(scatter_line(mixed[piece], grid))
-        operands = (length, keys[piece], vals[piece], key_part, value_part, *below, *results)
+        operands = (length, key, value, key_part, value_part, *below, *results)
         first = len(operands) - len(results)
         results = call(
             functools.partial(final_kernel, piece, grid, counts),
             [narrow, narrow], operands,
-            [pltpu.VMEM(narrow_piece.shape, BF16)] * 2 + [state_scratch, sems], 2 * unit * HD // PIECES,
+            [pltpu.VMEM((rows, width), BF16)] * 2 + [pltpu.VMEM((width, HD), BF16), sems],
+            2 * unit * HD // BACKWARD_PIECES,
             range(first, len(operands)), out_specs=[HBM, HBM],
             aliases={first + j: j for j in range(len(results))},
         )

time: 57.5 us -> 52.7 us (0.917)
  waiting for transfers between devices: 7.29 us -> 13.4 us
  starting transfers between devices: 24.1 us -> 18.8 us
  Pallas kernels: 23.4 us -> 18.4 us
    ppermute x24 -> x18, waiting for transfers between devices: 3.39 us -> 9.58 us  [line_send(): return lax.ppermute(block, 'seg', moves)]
    ppermute x24 -> x18, starting transfers between devices: 19.9 us -> 14.3 us  [line_send(): return lax.ppermute(block, 'seg', moves)]
    pallas_call x15 -> x11, Pallas kernels: 23.4 us -> 18.4 us  [call(): pl.pallas_call(kernel, out_shape=out_shape, in_specs=specs + [ANY] * len(...]
    ppermute x2 -> x3, starting transfers between devices: 4.24 us -> 4.5 us  [token_sums(): parts.append(lax.ppermute(sums, 'head', moves))]
    ppermute x2 -> x3, waiting for transfers between devices: 3.89 us -> 3.84 us  [token_sums(): parts.append(lax.ppermute(sums, 'head', moves))]
  transfers between devices with their start and end apart: 26 -> 21, of which waited for: 6 -> 9; matrix products, arithmetic and copies ran while one was open for 0% -> 0% of each run, Pallas kernels for 32% -> 22%
where the time goes in v6:
time: 52.7 us; the launch traced here: 52.2 us
  starting transfers between devices  18.8 us (36%)
  Pallas kernels  18.4 us (35%)
  waiting for transfers between devices  13.4 us (25%)
  between operations  1.57 us (3%)
    pallas_call x11, Pallas kernels, call(): pl.pallas_call(kernel, out_shape=out_shape, in_specs=specs + [ANY] * len(...  18.4 us
    ppermute x18, starting transfers between devices, line_send(): return lax.ppermute(block, 'seg', moves)  14.3 us
    ppermute x18, waiting for transfers between devices, line_send(): return lax.ppermute(block, 'seg', moves)  9.58 us
    ppermute x3, starting transfers between devices, token_sums(): parts.append(lax.ppermute(sums, 'head', moves))  4.5 us
    ppermute x3, waiting for transfers between devices, token_sums(): parts.append(lax.ppermute(sums, 'head', moves))  3.84 us
  transfers between devices with their start and end apart: 21, of which 9 were waited for; matrix products, arithmetic and copies ran while one was open for 0% of the time, Pallas kernels for 22%

profile of v6, /device:TPU:0, one launch (start us, length us, event | category | flops | bytes accessed | tf_op | source)
XLA Modules:
  0.0 52.2 jit_solution(11544141755240317375)
XLA Ops:
  1.3 2.3 %shard_map.102 = (bf16[256,2048]{1,0:T(8,128)(2,1)S(1)}, bf16[256,2048]{1,0:T(8,128)(2,1)S(1)}, s32[1,256]{1,0:T(1,128)S(1)}, f32[16,128]{1,0:T(8,128)S(1)}, f32...) custom-call(s32[1]{0:T(128)S(6)} %copy.11.seg_len, ...), custom_call_target="tpu_custom_call" | custom-call | flops 134217728 | bytes 4736036 | tf_op jit(solution)/shard_map/pallas_call | solution.py:366
  3.6 3.0 %collective-permute-start.1 = (bf16[512,128]{1,0:T(8,128)(2,1)S(1)}, bf16[512,128]{1,0:T(8,128)(2,1)S(1)}, u32[]{:S(2)}, u32[]{:S(2)}) collective-permute-start(bf16[512,128]{1,0:T(8,128)(2,1)S(1)} %get-tuple-element.48.refs_0_), channel_id=1, source_target_pairs={{0,2},{1,5},{2,0},{3,7},{4,6},{5,1},{6,4},{7,3},{8,10},{9,13},{10,... | collective-permute-start | bytes 393224 | tf_op jit(solution)/shard_map/ppermute | solution.py:388
  6.6 0.0 collective-permute-start.2
  6.6 0.2 collective-permute-start
  6.8 2.0 %collective-permute-start.4 = (bf16[512,128]{1,0:T(8,128)(2,1)S(1)}, bf16[512,128]{1,0:T(8,128)(2,1)S(1)}, u32[]{:S(2)}, u32[]{:S(2)}) collective-permute-start(bf16[512,128]{1,0:T(8,128)(2,1)S(1)} %get-tuple-element.53.refs_0_), channel_id=1, source_target_pairs={{0,2},{1,5},{2,0},{3,7},{4,6},{5,1},{6,4},{7,3},{8,10},{9,13},{10,... | collective-permute-start | bytes 393224 | tf_op jit(solution)/shard_map/ppermute | solution.py:388
  8.8 0.0 collective-permute-start.5
  8.8 1.7 %collective-permute-done.1.refs_2_ = bf16[512,128]{1,0:T(8,128)(2,1)S(1)} collective-permute-done((bf16[512,128]{1,0:T(8,128)(2,1)S(1)}, bf16[512,128]{1,0:T(8,128)(2,1)S(1)}, u32[]{:S(2)}, u32[]{:S(2)}) %collective-permute-start.1) | collective-permute-done | bytes 131104 | tf_op jit(solution)/shard_map/ppermute | solution.py:388
  10.4 0.0 collective-permute-start.3
  10.4 1.3 %collective-permute-done.2.refs_3_ = bf16[512,128]{1,0:T(8,128)(2,1)S(1)} collective-permute-done((bf16[512,128]{1,0:T(8,128)(2,1)S(1)}, bf16[512,128]{1,0:T(8,128)(2,1)S(1)}, u32[]{:S(2)}, u32[]{:S(2)}) %collective-permute-start.2) | collective-permute-done | bytes 131104 | tf_op jit(solution)/shard_map/ppermute | solution.py:388
  11.7 0.0 collective-permute-done.refs_1_
  11.7 0.0 copy-start
  11.7 0.0 copy-start.1
  11.7 0.3 shard_map.103
  12.0 2.0 %collective-permute-start.9 = (bf16[512,128]{1,0:T(8,128)(2,1)S(1)}, bf16[512,128]{1,0:T(8,128)(2,1)S(1)}, u32[]{:S(2)}, u32[]{:S(2)}) collective-permute-start(bf16[512,128]{1,0:T(8,128)(2,1)S(1)} %get-tuple-element.59), channel_id=1, source_target_pairs={{0,4},{1,3},{2,6},{3,1},{4,0},{5,7},{6,2},{7,5},{8,12},{9,11},{10,... | collective-permute-start | bytes 393224 | tf_op jit(solution)/shard_map/ppermute | solution.py:388
  14.0 0.0 collective-permute-start.10
  14.0 0.0 collective-permute-done.4.refs_2_
  14.0 0.7 %collective-permute-start.11 = (bf16[512,128]{1,0:T(8,128)(2,1)S(1)}, bf16[512,128]{1,0:T(8,128)(2,1)S(1)}, u32[]{:S(2)}, u32[]{:S(2)}) collective-permute-start(bf16[512,128]{1,0:T(8,128)(2,1)S(1)} %get-tuple-element.61), channel_id=1, source_target_pairs={{0,5},{1,2},{2,7},{3,0},{4,1},{5,6},{6,3},{7,4},{8,13},{9,10},{10,... | collective-permute-start | bytes 393224 | tf_op jit(solution)/shard_map/ppermute | solution.py:388
  14.7 0.0 collective-permute-done.5.refs_3_
  14.7 0.0 collective-permute-done.3.refs_1_
  14.8 0.3 shard_map.105
  15.0 1.5 %collective-permute-start.6 = (bf16[512,128]{1,0:T(8,128)(2,1)S(1)}, bf16[512,128]{1,0:T(8,128)(2,1)S(1)}, u32[]{:S(2)}, u32[]{:S(2)}) collective-permute-start(bf16[512,128]{1,0:T(8,128)(2,1)S(1)} %get-tuple-element.56), channel_id=1, source_target_pairs={{0,4},{1,3},{2,6},{3,1},{4,0},{5,7},{6,2},{7,5},{8,12},{9,11},{10,... | collective-permute-start | bytes 393224 | tf_op jit(solution)/shard_map/ppermute | solution.py:388
  16.5 0.0 collective-permute-start.7
  16.6 0.5 collective-permute-done.9.rest_1_
  17.0 0.5 collective-permute-start.8
  17.5 3.4 %shard_map.104 = (bf16[256,2048]{1,0:T(8,128)(2,1)S(1)}, f32[256,2048]{1,0:T(8,128)S(1)}) custom-call(s32[1,256]{1,0:T(1,128)S(1)} %get-tuple-element.44.length, bf16[256,2048]{1,0:T(8,128)(2,1)} %bitcast.17, bf16[256,2048]{1,0:T(8,128)(2,1)S(1)} %get-tuple-element.45.keys, bf16[256,2048]{1,0:T(8,128)(2,1)S(1)} %get-tuple-element.46.values, ...), custom_call_target="tpu_custom_call" | custom-call | flops 536870912 | bytes 6292480 | tf_op jit(solution)/shard_map/pallas_call | solution.py:366
  20.9 0.0 collective-permute-done.10.rest_2_
  20.9 0.0 collective-permute-done.11.rest_3_
  20.9 0.0 copy-done
  21.0 0.0 copy-done.1
  21.0 0.7 %shard_map.106 = (f32[256,1024]{1,0:T(8,128)S(1)}, f32[2,256]{1,0:T(2,128)S(1)}, bf16[1024,128]{1,0:T(8,128)(2,1)S(1)}) custom-call(s32[1,256]{1,0:T(1,128)S(1)} %get-tuple-element.44.length, bf16[256,2048]{1,0:T(8,128)(2,1)S(1)} %get-tuple-element.51.queries, f32[256,2048]{1,0:T(8,128)S(1)} %get-tuple-element.52.local, bf16[256,2048]{1,0:T(8,128)(2,1)S(1)} %bitcast.10, ...), custom_call_target="tpu_custom_call" | custom-call | flops 67108864 | bytes 6040576 | tf_op jit(solution)/shard_map/pallas_call | solution.py:366
  21.6 0.0 collective-permute-done.6.rest_1_
  21.7 0.0 collective-permute-done.7.rest_2_
  21.7 0.0 collective-permute-done.8.rest_3_
  21.7 0.7 %shard_map.107 = (f32[256,1024]{1,0:T(8,128)S(1)}, f32[2,256]{1,0:T(2,128)S(1)}, bf16[1024,128]{1,0:T(8,128)(2,1)S(1)}) custom-call(s32[1,256]{1,0:T(1,128)S(1)} %get-tuple-element.44.length, bf16[256,2048]{1,0:T(8,128)(2,1)S(1)} %get-tuple-element.51.queries, f32[256,2048]{1,0:T(8,128)S(1)} %get-tuple-element.52.local, bf16[256,2048]{1,0:T(8,128)(2,1)S(1)} %bitcast.11, ...), custom_call_target="tpu_custom_call" | custom-call | flops 67108864 | bytes 6042624 | tf_op jit(solution)/shard_map/pallas_call | solution.py:366
  22.3 3.9 %collective-permute-start.14 = (f32[2,256]{1,0:T(2,128)S(1)}, f32[2,256]{1,0:T(2,128)S(1)}, u32[]{:S(2)}, u32[]{:S(2)}) collective-permute-start(f32[2,256]{1,0:T(2,128)S(1)} %get-tuple-element.63.rest_0_), channel_id=1, source_target_pairs={{0,24},{8,16},{16,8},{24,0},{1,25},{9,17},{17,9},{25,1},{2,26},{10... | collective-permute-start | bytes 6152 | tf_op jit(solution)/shard_map/ppermute | solution.py:419
  26.2 0.0 collective-permute-start.13
  26.2 0.6 %collective-permute-start.12 = (f32[2,256]{1,0:T(2,128)S(1)}, f32[2,256]{1,0:T(2,128)S(1)}, u32[]{:S(2)}, u32[]{:S(2)}) collective-permute-start(f32[2,256]{1,0:T(2,128)S(1)} %get-tuple-element.63.rest_0_), channel_id=1, source_target_pairs={{0,8},{8,0},{16,24},{24,16},{1,9},{9,1},{17,25},{25,17},{2,10},{10... | collective-permute-start | bytes 6152 | tf_op jit(solution)/shard_map/ppermute | solution.py:419
  26.9 0.9 %collective-permute-done.14.rest_3_ = f32[2,256]{1,0:T(2,128)S(1)} collective-permute-done((f32[2,256]{1,0:T(2,128)S(1)}, f32[2,256]{1,0:T(2,128)S(1)}, u32[]{:S(2)}, u32[]{:S(2)}) %collective-permute-start.14) | collective-permute-done | bytes 2080 | tf_op jit(solution)/shard_map/ppermute | solution.py:419
  27.8 2.9 %collective-permute-done.13.rest_2_ = f32[2,256]{1,0:T(2,128)S(1)} collective-permute-done((f32[2,256]{1,0:T(2,128)S(1)}, f32[2,256]{1,0:T(2,128)S(1)}, u32[]{:S(2)}, u32[]{:S(2)}) %collective-permute-start.13) | collective-permute-done | bytes 2080 | tf_op jit(solution)/shard_map/ppermute | solution.py:419
  30.7 0.0 collective-permute-done.12.rest_1_
  30.7 1.0 %shard_map.108 = (bf16[256,2048]{1,0:T(8,128)(2,1)S(1)}, f32[1,256]{1,0:T(1,128)S(1)}, bf16[1024,128]{1,0:T(8,128)(2,1)S(1)}, bf16[1024,128]{1,0:T(8,128)(2,1)S(1)}) custom-call(s32[1,256]{1,0:T(1,128)S(1)} %get-tuple-element.44.length, bf16[256,2048]{1,0:T(8,128)(2,1)S(1)} %get-tuple-element.51.queries, bf16[256,2048]{1,0:T(8,128)(2,1)S(1)} %bitcast.12, ...), custom_call_target="tpu_custom_call" | custom-call | flops 134217728 | bytes 5785600 | tf_op jit(solution)/shard_map/pallas_call | solution.py:366
  31.7 1.5 %collective-permute-start.16 = (bf16[1024,128]{1,0:T(8,128)(2,1)S(1)}, bf16[1024,128]{1,0:T(8,128)(2,1)S(1)}, u32[]{:S(2)}, u32[]{:S(2)}) collective-permute-start(bf16[1024,128]{1,0:T(8,128)(2,1)S(1)} %get-tuple-element.73.refs_0_), channel_id=1, source_target_pairs={{0,2},{1,5},{2,0},{3,7},{4,6},{5,1},{6,4},{7,3},{8,10},{9,13},{10,... | collective-permute-start | bytes 786440 | tf_op jit(solution)/shard_map/ppermute | solution.py:388
  33.2 0.0 collective-permute-start.17
  33.2 0.7 %collective-permute-start.15 = (bf16[1024,128]{1,0:T(8,128)(2,1)S(1)}, bf16[1024,128]{1,0:T(8,128)(2,1)S(1)}, u32[]{:S(2)}, u32[]{:S(2)}) collective-permute-start(bf16[1024,128]{1,0:T(8,128)(2,1)S(1)} %get-tuple-element.74), channel_id=1, source_target_pairs={{0,1},{1,0},{2,3},{3,2},{4,5},{5,4},{6,7},{7,6},{8,9},{9,8},{10,11... | collective-permute-start | bytes 786440 | tf_op jit(solution)/shard_map/ppermute | solution.py:388
  34.0 4.4 %shard_map.109 = (bf16[256,2048]{1,0:T(8,128)(2,1)}, bf16[256,2048]{1,0:T(8,128)(2,1)}, f32[8,128]{1,0:T(8,128)S(1)}) custom-call(s32[1,256]{1,0:T(1,128)S(1)} %get-tuple-element.44.length, f32[1,256]{1,0:T(1,128)S(1)} %get-tuple-element.66.inverse_rms, f32[1,2048]{1,0:T(1,128)S(1)} %bitcast.16, bf16[256,2048]{1,0:T(8,128)(2,1)S(1)} %get-tuple-element.45.keys, ...), custom_call_target="tpu_custom_call" | custom-call | flops 671088640 | bytes 7878656 | tf_op jit(solution)/shard_map/pallas_call | solution.py:366
  38.4 1.8 %collective-permute-done.16.refs_2_ = bf16[1024,128]{1,0:T(8,128)(2,1)S(1)} collective-permute-done((bf16[1024,128]{1,0:T(8,128)(2,1)S(1)}, bf16[1024,128]{1,0:T(8,128)(2,1)S(1)}, u32[]{:S(2)}, u32[]{:S(2)}) %collective-permute-start.16) | collective-permute-done | bytes 262176 | tf_op jit(solution)/shard_map/ppermute | solution.py:388
  40.2 0.8 %collective-permute-done.17.refs_3_ = bf16[1024,128]{1,0:T(8,128)(2,1)S(1)} collective-permute-done((bf16[1024,128]{1,0:T(8,128)(2,1)S(1)}, bf16[1024,128]{1,0:T(8,128)(2,1)S(1)}, u32[]{:S(2)}, u32[]{:S(2)}) %collective-permute-start.17) | collective-permute-done | bytes 262176 | tf_op jit(solution)/shard_map/ppermute | solution.py:388
  41.0 0.0 collective-permute-done.15.refs_1_
  41.0 0.6 %shard_map.110 = (bf16[1024,128]{1,0:T(8,128)(2,1)S(1)}, bf16[1024,128]{1,0:T(8,128)(2,1)S(1)}, bf16[1024,128]{1,0:T(8,128)(2,1)S(1)}, bf16[1024,128]{1,0:T(8,128)(2,1)S(1)}) custom-call(f32[16,128]{1,0:T(8,128)S(1)} %get-tuple-element.72.weights, bf16[1024,128]{1,0:T(8,128)(2,1)S(1)} %get-tuple-element.73.refs_0_, ...), custom_call_target="tpu_custom_call" | custom-call | bytes 2105344 | tf_op jit(solution)/shard_map/pallas_call | solution.py:366
  41.6 1.6 %collective-permute-start.18 = (bf16[1024,128]{1,0:T(8,128)(2,1)S(1)}, bf16[1024,128]{1,0:T(8,128)(2,1)S(1)}, u32[]{:S(2)}, u32[]{:S(2)}) collective-permute-start(bf16[1024,128]{1,0:T(8,128)(2,1)S(1)} %get-tuple-element.79), channel_id=1, source_target_pairs={{0,4},{1,3},{2,6},{3,1},{4,0},{5,7},{6,2},{7,5},{8,12},{9,11},{10,... | collective-permute-start | bytes 786440 | tf_op jit(solution)/shard_map/ppermute | solution.py:388
  43.2 0.0 collective-permute-start.19
  43.2 0.6 %collective-permute-start.20 = (bf16[1024,128]{1,0:T(8,128)(2,1)S(1)}, bf16[1024,128]{1,0:T(8,128)(2,1)S(1)}, u32[]{:S(2)}, u32[]{:S(2)}) collective-permute-start(bf16[1024,128]{1,0:T(8,128)(2,1)S(1)} %get-tuple-element.81), channel_id=1, source_target_pairs={{0,5},{1,2},{2,7},{3,0},{4,1},{5,6},{6,3},{7,4},{8,13},{9,10},{10,... | collective-permute-start | bytes 786440 | tf_op jit(solution)/shard_map/ppermute | solution.py:388
  43.8 2.6 %shard_map.111 = (f32[256,2048]{1,0:T(8,128)S(1)}, f32[256,2048]{1,0:T(8,128)S(1)}) custom-call(s32[1,256]{1,0:T(1,128)S(1)} %get-tuple-element.44.length, bf16[256,2048]{1,0:T(8,128)(2,1)S(1)} %get-tuple-element.51.queries, bf16[256,2048]{1,0:T(8,128)(2,1)S(1)} %get-tuple-element.45.keys, bf16[256,2048]{1,0:T(8,128)(2,1)S(1)} %get-tuple-element.46.values, ...), custom_call_target="tpu_custom_call" | custom-call | flops 1073741824 | bytes 8389632 | tf_op jit(solution)/shard_map/pallas_call | solution.py:366
  46.4 1.6 %collective-permute-done.18.rest_1_ = bf16[1024,128]{1,0:T(8,128)(2,1)S(1)} collective-permute-done((bf16[1024,128]{1,0:T(8,128)(2,1)S(1)}, bf16[1024,128]{1,0:T(8,128)(2,1)S(1)}, u32[]{:S(2)}, u32[]{:S(2)}) %collective-permute-start.18) | collective-permute-done | bytes 262176 | tf_op jit(solution)/shard_map/ppermute | solution.py:388
  48.0 0.0 collective-permute-done.19.rest_2_
  48.0 1.8 %collective-permute-done.20.rest_3_ = bf16[1024,128]{1,0:T(8,128)(2,1)S(1)} collective-permute-done((bf16[1024,128]{1,0:T(8,128)(2,1)S(1)}, bf16[1024,128]{1,0:T(8,128)(2,1)S(1)}, u32[]{:S(2)}, u32[]{:S(2)}) %collective-permute-start.20) | collective-permute-done | bytes 262176 | tf_op jit(solution)/shard_map/ppermute | solution.py:388
  49.9 2.2 %shard_map.112 = (bf16[256,2048]{1,0:T(8,128)(2,1)}, bf16[256,2048]{1,0:T(8,128)(2,1)}) custom-call(s32[1,256]{1,0:T(1,128)S(1)} %get-tuple-element.44.length, bf16[256,2048]{1,0:T(8,128)(2,1)S(1)} %get-tuple-element.45.keys, bf16[256,2048]{1,0:T(8,128)(2,1)S(1)} %get-tuple-element.46.values, f32[256,2048]{1,0:T(8,128)S(1)} %get-tuple-element.77.key_part, ...), custom_call_target="tpu_custom_call" | custom-call | flops 268435456 | bytes 9438208 | tf_op jit(solution)/shard_map/pallas_call | solution.py:366
Async XLA Ops:
  3.6 6.8 %collective-permute-start.1 = (bf16[512,128]{1,0:T(8,128)(2,1)S(1)}, bf16[512,128]{1,0:T(8,128)(2,1)S(1)}, u32[]{:S(2)}, u32[]{:S(2)}) collective-permute-start(bf16[512,128]{1,0:T(8,128)(2,1)S(1)} %get-tuple-element.48.refs_0_), channel_id=1, source_target_pairs={{0,2},{1,5},{2,0},{3,7},{4,6},{5,1},{6,4},{7,3},{8,10},{9,13},{10,... | collective-permute-start | bytes 393224 | tf_op jit(solution)/shard_map/ppermute | solution.py:388
  6.6 5.1 %collective-permute-start.2 = (bf16[512,128]{1,0:T(8,128)(2,1)S(1)}, bf16[512,128]{1,0:T(8,128)(2,1)S(1)}, u32[]{:S(2)}, u32[]{:S(2)}) collective-permute-start(bf16[512,128]{1,0:T(8,128)(2,1)S(1)} %get-tuple-element.49), channel_id=1, source_target_pairs={{0,5},{1,2},{2,7},{3,0},{4,1},{5,6},{6,3},{7,4},{8,13},{9,10},{10,... | collective-permute-start | bytes 393224 | tf_op jit(solution)/shard_map/ppermute | solution.py:388
  6.6 5.1 %collective-permute-start = (bf16[512,128]{1,0:T(8,128)(2,1)S(1)}, bf16[512,128]{1,0:T(8,128)(2,1)S(1)}, u32[]{:S(2)}, u32[]{:S(2)}) collective-permute-start(bf16[512,128]{1,0:T(8,128)(2,1)S(1)} %get-tuple-element.49), channel_id=1, source_target_pairs={{0,1},{1,0},{2,3},{3,2},{4,5},{5,4},{6,7},{7,6},{8,9},{9,8},{10,11... | collective-permute-start | bytes 393224 | tf_op jit(solution)/shard_map/ppermute | solution.py:388
  6.8 7.2 %collective-permute-start.4 = (bf16[512,128]{1,0:T(8,128)(2,1)S(1)}, bf16[512,128]{1,0:T(8,128)(2,1)S(1)}, u32[]{:S(2)}, u32[]{:S(2)}) collective-permute-start(bf16[512,128]{1,0:T(8,128)(2,1)S(1)} %get-tuple-element.53.refs_0_), channel_id=1, source_target_pairs={{0,2},{1,5},{2,0},{3,7},{4,6},{5,1},{6,4},{7,3},{8,10},{9,13},{10,... | collective-permute-start | bytes 393224 | tf_op jit(solution)/shard_map/ppermute | solution.py:388
  8.8 6.0 %collective-permute-start.5 = (bf16[512,128]{1,0:T(8,128)(2,1)S(1)}, bf16[512,128]{1,0:T(8,128)(2,1)S(1)}, u32[]{:S(2)}, u32[]{:S(2)}) collective-permute-start(bf16[512,128]{1,0:T(8,128)(2,1)S(1)} %get-tuple-element.54), channel_id=1, source_target_pairs={{0,5},{1,2},{2,7},{3,0},{4,1},{5,6},{6,3},{7,4},{8,13},{9,10},{10,... | collective-permute-start | bytes 393224 | tf_op jit(solution)/shard_map/ppermute | solution.py:388
  10.4 4.3 %collective-permute-start.3 = (bf16[512,128]{1,0:T(8,128)(2,1)S(1)}, bf16[512,128]{1,0:T(8,128)(2,1)S(1)}, u32[]{:S(2)}, u32[]{:S(2)}) collective-permute-start(bf16[512,128]{1,0:T(8,128)(2,1)S(1)} %get-tuple-element.54), channel_id=1, source_target_pairs={{0,1},{1,0},{2,3},{3,2},{4,5},{5,4},{6,7},{7,6},{8,9},{9,8},{10,11... | collective-permute-start | bytes 393224 | tf_op jit(solution)/shard_map/ppermute | solution.py:388
  11.7 9.2 %copy-start = (bf16[1,256,2048]{2,1,0:T(8,128)(2,1)S(1)}, bf16[1,256,2048]{2,1,0:T(8,128)(2,1)}, u32[]{:S(2)}) copy-start(bf16[1,256,2048]{2,1,0:T(8,128)(2,1)} %param.10) | copy-start | bytes 3145732
  11.7 9.2 %copy-start.1 = (f32[2048]{0:T(1024)S(1)}, f32[2048]{0:T(1024)}, u32[]{:S(2)}) copy-start(f32[2048]{0:T(1024)} %param.11) | copy-start | bytes 24580
  12.0 5.0 %collective-permute-start.9 = (bf16[512,128]{1,0:T(8,128)(2,1)S(1)}, bf16[512,128]{1,0:T(8,128)(2,1)S(1)}, u32[]{:S(2)}, u32[]{:S(2)}) collective-permute-start(bf16[512,128]{1,0:T(8,128)(2,1)S(1)} %get-tuple-element.59), channel_id=1, source_target_pairs={{0,4},{1,3},{2,6},{3,1},{4,0},{5,7},{6,2},{7,5},{8,12},{9,11},{10,... | collective-permute-start | bytes 393224 | tf_op jit(solution)/shard_map/ppermute | solution.py:388
  14.0 6.9 %collective-permute-start.10 = (bf16[512,128]{1,0:T(8,128)(2,1)S(1)}, bf16[512,128]{1,0:T(8,128)(2,1)S(1)}, u32[]{:S(2)}, u32[]{:S(2)}) collective-permute-start(bf16[512,128]{1,0:T(8,128)(2,1)S(1)} %get-tuple-element.60), channel_id=1, source_target_pairs={{0,1},{1,0},{2,3},{3,2},{4,5},{5,4},{6,7},{7,6},{8,9},{9,8},{10,11... | collective-permute-start | bytes 393224 | tf_op jit(solution)/shard_map/ppermute | solution.py:388
  14.0 6.9 %collective-permute-start.11 = (bf16[512,128]{1,0:T(8,128)(2,1)S(1)}, bf16[512,128]{1,0:T(8,128)(2,1)S(1)}, u32[]{:S(2)}, u32[]{:S(2)}) collective-permute-start(bf16[512,128]{1,0:T(8,128)(2,1)S(1)} %get-tuple-element.61), channel_id=1, source_target_pairs={{0,5},{1,2},{2,7},{3,0},{4,1},{5,6},{6,3},{7,4},{8,13},{9,10},{10,... | collective-permute-start | bytes 393224 | tf_op jit(solution)/shard_map/ppermute | solution.py:388
  15.0 6.6 %collective-permute-start.6 = (bf16[512,128]{1,0:T(8,128)(2,1)S(1)}, bf16[512,128]{1,0:T(8,128)(2,1)S(1)}, u32[]{:S(2)}, u32[]{:S(2)}) collective-permute-start(bf16[512,128]{1,0:T(8,128)(2,1)S(1)} %get-tuple-element.56), channel_id=1, source_target_pairs={{0,4},{1,3},{2,6},{3,1},{4,0},{5,7},{6,2},{7,5},{8,12},{9,11},{10,... | collective-permute-start | bytes 393224 | tf_op jit(solution)/shard_map/ppermute | solution.py:388
  16.5 5.1 %collective-permute-start.7 = (bf16[512,128]{1,0:T(8,128)(2,1)S(1)}, bf16[512,128]{1,0:T(8,128)(2,1)S(1)}, u32[]{:S(2)}, u32[]{:S(2)}) collective-permute-start(bf16[512,128]{1,0:T(8,128)(2,1)S(1)} %get-tuple-element.57), channel_id=1, source_target_pairs={{0,1},{1,0},{2,3},{3,2},{4,5},{5,4},{6,7},{7,6},{8,9},{9,8},{10,11... | collective-permute-start | bytes 393224 | tf_op jit(solution)/shard_map/ppermute | solution.py:388
  17.0 4.6 %collective-permute-start.8 = (bf16[512,128]{1,0:T(8,128)(2,1)S(1)}, bf16[512,128]{1,0:T(8,128)(2,1)S(1)}, u32[]{:S(2)}, u32[]{:S(2)}) collective-permute-start(bf16[512,128]{1,0:T(8,128)(2,1)S(1)} %get-tuple-element.58), channel_id=1, source_target_pairs={{0,5},{1,2},{2,7},{3,0},{4,1},{5,6},{6,3},{7,4},{8,13},{9,10},{10,... | collective-permute-start | bytes 393224 | tf_op jit(solution)/shard_map/ppermute | solution.py:388
  22.3 5.4 %collective-permute-start.14 = (f32[2,256]{1,0:T(2,128)S(1)}, f32[2,256]{1,0:T(2,128)S(1)}, u32[]{:S(2)}, u32[]{:S(2)}) collective-permute-start(f32[2,256]{1,0:T(2,128)S(1)} %get-tuple-element.63.rest_0_), channel_id=1, source_target_pairs={{0,24},{8,16},{16,8},{24,0},{1,25},{9,17},{17,9},{25,1},{2,26},{10... | collective-permute-start | bytes 6152 | tf_op jit(solution)/shard_map/ppermute | solution.py:419
  26.2 4.5 %collective-permute-start.13 = (f32[2,256]{1,0:T(2,128)S(1)}, f32[2,256]{1,0:T(2,128)S(1)}, u32[]{:S(2)}, u32[]{:S(2)}) collective-permute-start(f32[2,256]{1,0:T(2,128)S(1)} %get-tuple-element.63.rest_0_), channel_id=1, source_target_pairs={{0,16},{8,24},{16,0},{24,8},{1,17},{9,25},{17,1},{25,9},{2,18},{10... | collective-permute-start | bytes 6152 | tf_op jit(solution)/shard_map/ppermute | solution.py:419
  26.2 4.5 %collective-permute-start.12 = (f32[2,256]{1,0:T(2,128)S(1)}, f32[2,256]{1,0:T(2,128)S(1)}, u32[]{:S(2)}, u32[]{:S(2)}) collective-permute-start(f32[2,256]{1,0:T(2,128)S(1)} %get-tuple-element.63.rest_0_), channel_id=1, source_target_pairs={{0,8},{8,0},{16,24},{24,16},{1,9},{9,1},{17,25},{25,17},{2,10},{10... | collective-permute-start | bytes 6152 | tf_op jit(solution)/shard_map/ppermute | solution.py:419
  31.7 8.4 %collective-permute-start.16 = (bf16[1024,128]{1,0:T(8,128)(2,1)S(1)}, bf16[1024,128]{1,0:T(8,128)(2,1)S(1)}, u32[]{:S(2)}, u32[]{:S(2)}) collective-permute-start(bf16[1024,128]{1,0:T(8,128)(2,1)S(1)} %get-tuple-element.73.refs_0_), channel_id=1, source_target_pairs={{0,2},{1,5},{2,0},{3,7},{4,6},{5,1},{6,4},{7,3},{8,10},{9,13},{10,... | collective-permute-start | bytes 786440 | tf_op jit(solution)/shard_map/ppermute | solution.py:388
  33.2 7.8 %collective-permute-start.17 = (bf16[1024,128]{1,0:T(8,128)(2,1)S(1)}, bf16[1024,128]{1,0:T(8,128)(2,1)S(1)}, u32[]{:S(2)}, u32[]{:S(2)}) collective-permute-start(bf16[1024,128]{1,0:T(8,128)(2,1)S(1)} %get-tuple-element.74), channel_id=1, source_target_pairs={{0,5},{1,2},{2,7},{3,0},{4,1},{5,6},{6,3},{7,4},{8,13},{9,10},{10,... | collective-permute-start | bytes 786440 | tf_op jit(solution)/shard_map/ppermute | solution.py:388
  33.2 7.8 %collective-permute-start.15 = (bf16[1024,128]{1,0:T(8,128)(2,1)S(1)}, bf16[1024,128]{1,0:T(8,128)(2,1)S(1)}, u32[]{:S(2)}, u32[]{:S(2)}) collective-permute-start(bf16[1024,128]{1,0:T(8,128)(2,1)S(1)} %get-tuple-element.74), channel_id=1, source_target_pairs={{0,1},{1,0},{2,3},{3,2},{4,5},{5,4},{6,7},{7,6},{8,9},{9,8},{10,11... | collective-permute-start | bytes 786440 | tf_op jit(solution)/shard_map/ppermute | solution.py:388
  41.6 6.4 %collective-permute-start.18 = (bf16[1024,128]{1,0:T(8,128)(2,1)S(1)}, bf16[1024,128]{1,0:T(8,128)(2,1)S(1)}, u32[]{:S(2)}, u32[]{:S(2)}) collective-permute-start(bf16[1024,128]{1,0:T(8,128)(2,1)S(1)} %get-tuple-element.79), channel_id=1, source_target_pairs={{0,4},{1,3},{2,6},{3,1},{4,0},{5,7},{6,2},{7,5},{8,12},{9,11},{10,... | collective-permute-start | bytes 786440 | tf_op jit(solution)/shard_map/ppermute | solution.py:388
  43.2 4.9 %collective-permute-start.19 = (bf16[1024,128]{1,0:T(8,128)(2,1)S(1)}, bf16[1024,128]{1,0:T(8,128)(2,1)S(1)}, u32[]{:S(2)}, u32[]{:S(2)}) collective-permute-start(bf16[1024,128]{1,0:T(8,128)(2,1)S(1)} %get-tuple-element.80), channel_id=1, source_target_pairs={{0,1},{1,0},{2,3},{3,2},{4,5},{5,4},{6,7},{7,6},{8,9},{9,8},{10,11... | collective-permute-start | bytes 786440 | tf_op jit(solution)/shard_map/ppermute | solution.py:388
  43.2 6.7 %collective-permute-start.20 = (bf16[1024,128]{1,0:T(8,128)(2,1)S(1)}, bf16[1024,128]{1,0:T(8,128)(2,1)S(1)}, u32[]{:S(2)}, u32[]{:S(2)}) collective-permute-start(bf16[1024,128]{1,0:T(8,128)(2,1)S(1)} %get-tuple-element.81), channel_id=1, source_target_pairs={{0,5},{1,2},{2,7},{3,0},{4,1},{5,6},{6,3},{7,4},{8,13},{9,10},{10,... | collective-permute-start | bytes 786440 | tf_op jit(solution)/shard_map/ppermute | solution.py:388

commit v7 on v6

--- a/solution.py
+++ b/solution.py
@@ -16,6 +16,7 @@
 VMEM_LIMIT = 24 * 1024 * 1024
 FORWARD_PIECES = 2
 BACKWARD_PIECES = 1
+RETURN_PIECES = 2
 
 VMEM = pl.BlockSpec(memory_space=pltpu.VMEM)
 SMEM = pl.BlockSpec(memory_space=pltpu.SMEM)
@@ -169,13 +170,13 @@
     write_halves(full, outs, my_place(grid)[2], grid[2])
 
 
-def mix_kernel(sources, weights, *refs):
+def mix_kernel(sources, first, weights, *refs):
     blocks, outs = refs[:sources], refs[-sources:]
-    rows = blocks[0].shape[0]
+    rows = outs[0].shape[0]
     chunk = min(rows, 64)
     for start in range(0, rows, chunk):
         part = slice(start, start + chunk)
-        loaded = [block[part, :].astype(F32) for block in blocks]
+        loaded = [block[first + start : first + start + chunk, :].astype(F32) for block in blocks]
         for out_step, out in enumerate(outs):
             at = out_step * sources
             total = weights[at : at + 1, :] * loaded[0]
@@ -210,19 +211,23 @@
     return pieces[head // per_piece], head_cols(head % per_piece)
 
 
-def local_kernel(heads, length, queries_hbm, keys, values, *rest):
-    queries, local, sems = rest[-3:]
-    group = 4 if heads % 4 == 0 else 1
+def fetch_kernel(source, _, out, sems):
+    rows = out.shape[0]
+    chunk = rows // 4 if rows % 64 == 0 else rows
     copies = []
-    for at in range(0, heads, group):
-        cols = slice(at * HD, (at + group) * HD)
-        copies.append(pltpu.make_async_copy(queries_hbm.at[:, cols], queries.at[:, cols], sems.at[at // group]))
+    for step in range(rows // chunk):
+        part = pl.ds(step * chunk, chunk)
+        copies.append(pltpu.make_async_copy(source.at[part, :], out.at[part, :], sems.at[step]))
     for copy in copies:
         copy.start()
+    for copy in copies:
+        copy.wait()
+
+
+def local_kernel(heads, length, queries, keys, values, *rest):
+    local = rest[-1]
     keep = keep_mask(length, False)
     for head in range(heads):
-        if head % group == 0:
-            copies[head // group].wait()
         cols = head_cols(head)
         scores = jnp.where(keep, nt(queries[:, cols], keys[:, cols]), 0.0).astype(BF16)
         local[:, cols] = nn(scores, values[:, cols])
@@ -331,21 +336,24 @@
 def final_kernel(piece, grid, counts, length, keys, values, key_part, value_part, *rest):
     received, rest = rest[: sum(counts)], rest[sum(counts) :]
     key_hbm, value_hbm, key_grad, value_grad, below, sems = rest[-6:]
-    join_halves(split_refs(received, *counts), below, my_place(grid)[2], grid[2])
+    pair = grid[2]
+    join_halves(split_refs(received, *counts), below, my_place(grid)[2], pair)
     rows, width = key_grad.shape
     live = jnp.where(live_rows(length, rows), 1.0, 0.0)
-    heads = width // HD
-    group = 2 if heads % 2 == 0 else 1
+    per_half = width // HD // pair
+    group = 2 if per_half % 2 == 0 else 1
     copies = []
-    for head in range(heads):
-        cols = head_cols(head)
-        whole = head_cols(piece * heads + head)
+    for head in range(width // HD):
+        half, within = head // per_half, head % per_half
+        cols = head_cols(head)
+        place = half * (keys.shape[1] // HD // pair) + piece * per_half + within
+        whole = head_cols(place)
         state = below[head * HD : (head + 1) * HD, :]
         key_grad[:, cols] = (key_part[:, whole] + live * nt(values[:, whole], state)).astype(BF16)
         value_grad[:, cols] = (value_part[:, whole] + live * nn(keys[:, whole], state)).astype(BF16)
         if (head + 1) % group == 0:
             done = slice((head + 1 - group) * HD, (head + 1) * HD)
-            there = slice(piece * width + done.start, piece * width + done.stop)
+            there = slice((place + 1 - group) * HD, (place + 1) * HD)
             for j, (src, dst) in enumerate(((key_grad, key_hbm), (value_grad, value_hbm))):
                 copy = pltpu.make_async_copy(src.at[:, done], dst.at[:, there], sems.at[j, head // group])
                 copy.start()
@@ -414,7 +422,7 @@
 
 def token_sums(sums, groups):
     parts = [sums]
-    for step in range(1, groups):
+    for step in [j for j in range(1, groups) if j != 2] + [2] * (groups > 2):
         moves = [(j, target_of(j, step, groups)) for j in range(groups)]
         parts.append(lax.ppermute(sums, "head", moves))
     return parts
@@ -441,9 +449,10 @@
     def halves(pieces):
         return [shape((features // (pair * pieces), HD), BF16)] * pair
 
-    def mix(arrived, weights, after=()):
-        like = [shape(arrived[0].shape, BF16)] * members
-        return call(functools.partial(mix_kernel, members), like, (weights, *arrived), after=after)
+    def mix(arrived, weights, piece, pieces, after=()):
+        tall = arrived[0].shape[0] // pieces
+        like = [shape((tall, HD), BF16)] * members
+        return call(functools.partial(mix_kernel, members, piece * tall), like, (weights, *arrived), after=after)
 
     def flat(parts):
         return [block for part in parts for block in part]
@@ -455,12 +464,13 @@
         [pltpu.VMEM((features, HD), BF16), sems, pltpu.SMEM((1, segs), jnp.int32), pltpu.SemaphoreType.DMA(())],
         unit * HD, (1, 2, 3), (0,),
     )
-    mixed = [mix(gather_line(part, grid), up) for part in split_refs(own, *[pair] * FORWARD_PIECES)]
-    query, local = call(
+    (query,) = call(fetch_kernel, [narrow], (queries[0],), [pltpu.SemaphoreType.DMA((4,))], 0, (0,), after=(own[0],))
+    mixed = []
+    for part in split_refs(own, *[pair] * FORWARD_PIECES):
+        mixed.append(mix(gather_line(part, grid), up, 0, 1, () if mixed else (query,)))
+    (local,) = call(
         functools.partial(local_kernel, heads),
-        [narrow, wide],
-        (length, queries[0], key, value), [pltpu.SemaphoreType.DMA((heads,))], unit * rows * 2, (1,),
-        after=(mixed[0][0],),
+        [wide], (length, query, key, value), (), unit * rows * 2, after=(mixed[0][0],),
     )
     attention, prefix, sums = [], [], []
     width = features // FORWARD_PIECES
@@ -493,15 +503,18 @@
         [pltpu.VMEM(narrow.shape, BF16)] * 2 + [sems], unit * (2 * rows + HD),
         out_specs=[HBM, HBM, VMEM],
     )
+    (part,) = state_grad
+    arrived = gather_line(part, grid)
     mixed = []
-    for part in state_grad:
-        mixed.append(mix(gather_line(part, grid), down, (token,) if len(mixed) == BACKWARD_PIECES - 1 else ()))
+    for piece in range(RETURN_PIECES):
+        mixed.append(mix(arrived, down, piece, RETURN_PIECES, (token, *mixed[-1][:1]) if mixed else (token,)))
     key_part, value_part = call(
         functools.partial(back_kernel, heads, scale),
         [wide, wide], (length, query, key, value, *grads), (), unit * 4 * rows, after=(mixed[-1][0],),
     )
     results = []
-    for piece in range(BACKWARD_PIECES):
+    width = features // RETURN_PIECES
+    for piece in range(RETURN_PIECES):
         below = flat(scatter_line(mixed[piece], grid))
         operands = (length, key, value, key_part, value_part, *below, *results)
         first = len(operands) - len(results)
@@ -509,7 +522,7 @@
             functools.partial(final_kernel, piece, grid, counts),
             [narrow, narrow], operands,
             [pltpu.VMEM((rows, width), BF16)] * 2 + [pltpu.VMEM((width, HD), BF16), sems],
-            2 * unit * HD // BACKWARD_PIECES,
+            2 * unit * HD // RETURN_PIECES,
             range(first, len(operands)), out_specs=[HBM, HBM],
             aliases={first + j: j for j in range(len(results))},
         )

time: 52.7 us -> 52.1 us (0.989)
  waiting for transfers between devices: 13.4 us -> 10.5 us
  starting transfers between devices: 18.8 us -> 20.7 us
    ppermute x18 -> x21, waiting for transfers between devices: 9.58 us -> 6.67 us  [line_send(): return lax.ppermute(block, 'seg', moves)]
    ppermute x18 -> x21, starting transfers between devices: 14.3 us -> 16.4 us  [line_send(): return lax.ppermute(block, 'seg', moves)]
    pallas_call x11 -> x14, Pallas kernels: 18.4 us -> 18.7 us  [call(): pl.pallas_call(kernel, out_shape=out_shape, in_specs=specs + [ANY] * len(...]
  transfers between devices with their start and end apart: 21 -> 24, of which waited for: 9 -> 11; matrix products, arithmetic and copies ran while one was open for 0% -> 0% of each run, Pallas kernels for 22% -> 25%
where the time goes in v7:
time: 52.1 us; the launch traced here: 51.5 us
  starting transfers between devices  20.7 us (40%)
  Pallas kernels  18.7 us (36%)
  waiting for transfers between devices  10.5 us (20%)
  between operations  1.61 us (3%)
    pallas_call x14, Pallas kernels, call(): pl.pallas_call(kernel, out_shape=out_shape, in_specs=specs + [ANY] * len(...  18.7 us
    ppermute x21, starting transfers between devices, line_send(): return lax.ppermute(block, 'seg', moves)  16.4 us
    ppermute x21, waiting for transfers between devices, line_send(): return lax.ppermute(block, 'seg', moves)  6.67 us
    ppermute x3, starting transfers between devices, token_sums(): parts.append(lax.ppermute(sums, 'head', moves))  4.23 us
    ppermute x3, waiting for transfers between devices, token_sums(): parts.append(lax.ppermute(sums, 'head', moves))  3.81 us
  transfers between devices with their start and end apart: 24, of which 11 were waited for; matrix products, arithmetic and copies ran while one was open for 0% of the time, Pallas kernels for 25%

profile of v7, /device:TPU:0, one launch (start us, length us, event | category | flops | bytes accessed | tf_op | source)
XLA Modules:
  0.0 51.5 jit_solution(13101642145829450518)
XLA Ops:
  1.3 2.3 %shard_map.102 = (bf16[256,2048]{1,0:T(8,128)(2,1)S(1)}, bf16[256,2048]{1,0:T(8,128)(2,1)S(1)}, s32[1,256]{1,0:T(1,128)S(1)}, f32[16,128]{1,0:T(8,128)S(1)}, f32...) custom-call(s32[1]{0:T(128)S(6)} %copy.15.seg_len, ...), custom_call_target="tpu_custom_call" | custom-call | flops 134217728 | bytes 4736036 | tf_op jit(solution)/shard_map/pallas_call | solution.py:374
  3.6 2.5 %collective-permute-start.2 = (bf16[512,128]{1,0:T(8,128)(2,1)S(1)}, bf16[512,128]{1,0:T(8,128)(2,1)S(1)}, u32[]{:S(2)}, u32[]{:S(2)}) collective-permute-start(bf16[512,128]{1,0:T(8,128)(2,1)S(1)} %get-tuple-element.53), channel_id=1, source_target_pairs={{0,5},{1,2},{2,7},{3,0},{4,1},{5,6},{6,3},{7,4},{8,13},{9,10},{10,... | collective-permute-start | bytes 393224 | tf_op jit(solution)/shard_map/ppermute | solution.py:396
  6.1 0.6 %collective-permute-start = (bf16[512,128]{1,0:T(8,128)(2,1)S(1)}, bf16[512,128]{1,0:T(8,128)(2,1)S(1)}, u32[]{:S(2)}, u32[]{:S(2)}) collective-permute-start(bf16[512,128]{1,0:T(8,128)(2,1)S(1)} %get-tuple-element.53), channel_id=1, source_target_pairs={{0,1},{1,0},{2,3},{3,2},{4,5},{5,4},{6,7},{7,6},{8,9},{9,8},{10,11... | collective-permute-start | bytes 393224 | tf_op jit(solution)/shard_map/ppermute | solution.py:396
  6.7 0.9 %collective-permute-start.1 = (bf16[512,128]{1,0:T(8,128)(2,1)S(1)}, bf16[512,128]{1,0:T(8,128)(2,1)S(1)}, u32[]{:S(2)}, u32[]{:S(2)}) collective-permute-start(bf16[512,128]{1,0:T(8,128)(2,1)S(1)} %get-tuple-element.49._.refs_0_), channel_id=1, source_target_pairs={{0,2},{1,5},{2,0},{3,7},{4,6},{5,1},{6,4},{7,3},{8,10},{9,13},{10,... | collective-permute-start | bytes 393224 | tf_op jit(solution)/shard_map/ppermute | solution.py:396
  7.6 1.1 %collective-permute-start.4 = (bf16[512,128]{1,0:T(8,128)(2,1)S(1)}, bf16[512,128]{1,0:T(8,128)(2,1)S(1)}, u32[]{:S(2)}, u32[]{:S(2)}) collective-permute-start(bf16[512,128]{1,0:T(8,128)(2,1)S(1)} %get-tuple-element.55.refs_0_), channel_id=1, source_target_pairs={{0,2},{1,5},{2,0},{3,7},{4,6},{5,1},{6,4},{7,3},{8,10},{9,13},{10,... | collective-permute-start | bytes 393224 | tf_op jit(solution)/shard_map/ppermute | solution.py:396
  8.8 0.6 %collective-permute-start.5 = (bf16[512,128]{1,0:T(8,128)(2,1)S(1)}, bf16[512,128]{1,0:T(8,128)(2,1)S(1)}, u32[]{:S(2)}, u32[]{:S(2)}) collective-permute-start(bf16[512,128]{1,0:T(8,128)(2,1)S(1)} %get-tuple-element.56), channel_id=1, source_target_pairs={{0,5},{1,2},{2,7},{3,0},{4,1},{5,6},{6,3},{7,4},{8,13},{9,10},{10,... | collective-permute-start | bytes 393224 | tf_op jit(solution)/shard_map/ppermute | solution.py:396
  9.3 1.2 %shard_map.103.refs_4_.queries = bf16[256,2048]{1,0:T(8,128)(2,1)S(1)} custom-call(bf16[256,2048]{1,0:T(8,128)(2,1)} %bitcast.19, bf16[512,128]{1,0:T(8,128)(2,1)S(1)} %get-tuple-element.49._.refs_0_), custom_call_target="tpu_custom_call" | custom-call | bytes 2097152 | tf_op jit(solution)/shard_map/pallas_call | solution.py:374
  10.6 0.0 collective-permute-done.2.refs_3_
  10.6 0.5 collective-permute-start.3
  11.1 0.0 collective-permute-done.refs_1_
  11.1 0.6 %collective-permute-done.1.refs_2_ = bf16[512,128]{1,0:T(8,128)(2,1)S(1)} collective-permute-done((bf16[512,128]{1,0:T(8,128)(2,1)S(1)}, bf16[512,128]{1,0:T(8,128)(2,1)S(1)}, u32[]{:S(2)}, u32[]{:S(2)}) %collective-permute-start.1) | collective-permute-done | bytes 131104 | tf_op jit(solution)/shard_map/ppermute | solution.py:396
  11.7 0.3 shard_map.104
  12.0 1.6 %collective-permute-start.9 = (bf16[512,128]{1,0:T(8,128)(2,1)S(1)}, bf16[512,128]{1,0:T(8,128)(2,1)S(1)}, u32[]{:S(2)}, u32[]{:S(2)}) collective-permute-start(bf16[512,128]{1,0:T(8,128)(2,1)S(1)} %get-tuple-element.61), channel_id=1, source_target_pairs={{0,4},{1,3},{2,6},{3,1},{4,0},{5,7},{6,2},{7,5},{8,12},{9,11},{10,... | collective-permute-start | bytes 393224 | tf_op jit(solution)/shard_map/ppermute | solution.py:396
  13.6 0.0 collective-permute-start.10
  13.6 0.8 %collective-permute-done.4.refs_2_ = bf16[512,128]{1,0:T(8,128)(2,1)S(1)} collective-permute-done((bf16[512,128]{1,0:T(8,128)(2,1)S(1)}, bf16[512,128]{1,0:T(8,128)(2,1)S(1)}, u32[]{:S(2)}, u32[]{:S(2)}) %collective-permute-start.4) | collective-permute-done | bytes 131104 | tf_op jit(solution)/shard_map/ppermute | solution.py:396
  14.4 0.2 collective-permute-start.11
  14.6 0.0 collective-permute-done.5.refs_3_
  14.6 0.0 collective-permute-done.3.refs_1_
  14.6 0.3 shard_map.106
  14.9 1.5 %collective-permute-start.6 = (bf16[512,128]{1,0:T(8,128)(2,1)S(1)}, bf16[512,128]{1,0:T(8,128)(2,1)S(1)}, u32[]{:S(2)}, u32[]{:S(2)}) collective-permute-start(bf16[512,128]{1,0:T(8,128)(2,1)S(1)} %get-tuple-element.58), channel_id=1, source_target_pairs={{0,4},{1,3},{2,6},{3,1},{4,0},{5,7},{6,2},{7,5},{8,12},{9,11},{10,... | collective-permute-start | bytes 393224 | tf_op jit(solution)/shard_map/ppermute | solution.py:396
  16.4 0.2 collective-permute-start.7
  16.6 0.4 collective-permute-done.9.rest_1_
  17.0 0.7 %collective-permute-start.8 = (bf16[512,128]{1,0:T(8,128)(2,1)S(1)}, bf16[512,128]{1,0:T(8,128)(2,1)S(1)}, u32[]{:S(2)}, u32[]{:S(2)}) collective-permute-start(bf16[512,128]{1,0:T(8,128)(2,1)S(1)} %get-tuple-element.60), channel_id=1, source_target_pairs={{0,5},{1,2},{2,7},{3,0},{4,1},{5,6},{6,3},{7,4},{8,13},{9,10},{10,... | collective-permute-start | bytes 393224 | tf_op jit(solution)/shard_map/ppermute | solution.py:396
  17.8 1.5 %shard_map.105.local = f32[256,2048]{1,0:T(8,128)S(1)} custom-call(s32[1,256]{1,0:T(1,128)S(1)} %get-tuple-element.48.length, bf16[256,2048]{1,0:T(8,128)(2,1)S(1)} %shard_map.103.refs_4_.queries, bf16[256,2048]{1,0:T(8,128)(2,1)S(1)} %get-tuple-element.50.keys, bf16[256,2048]{1,0:T(8,128)(2,1)S(1)} %get-tuple-element.51.values, ...), custom_call_target="tpu_custom_call" | custom-call | flops 536870912 | bytes 5243904 | tf_op jit(solution)/shard_map/pallas_call | solution.py:374
  19.2 0.0 collective-permute-done.10.rest_2_
  19.3 0.0 collective-permute-done.11.rest_3_
  19.3 0.0 copy-done
  19.3 0.0 copy-done.1
  19.3 0.7 %shard_map.107 = (f32[256,1024]{1,0:T(8,128)S(1)}, f32[2,256]{1,0:T(2,128)S(1)}, bf16[1024,128]{1,0:T(8,128)(2,1)S(1)}) custom-call(s32[1,256]{1,0:T(1,128)S(1)} %get-tuple-element.48.length, bf16[256,2048]{1,0:T(8,128)(2,1)S(1)} %shard_map.103.refs_4_.queries, f32[256,2048]{1,0:T(8,128)S(1)} %shard_map.105.local, bf16[256,2048]{1,0:T(8,128)(2,1)S(1)} %bitcast.10, ...), custom_call_target="tpu_custom_call" | custom-call | flops 67108864 | bytes 6040576 | tf_op jit(solution)/shard_map/pallas_call | solution.py:374
  20.0 0.3 collective-permute-done.6.rest_1_
  20.3 0.0 collective-permute-done.7.rest_2_
  20.3 1.3 %collective-permute-done.8.rest_3_ = bf16[512,128]{1,0:T(8,128)(2,1)S(1)} collective-permute-done((bf16[512,128]{1,0:T(8,128)(2,1)S(1)}, bf16[512,128]{1,0:T(8,128)(2,1)S(1)}, u32[]{:S(2)}, u32[]{:S(2)}) %collective-permute-start.8) | collective-permute-done | bytes 131104 | tf_op jit(solution)/shard_map/ppermute | solution.py:396
  21.6 0.7 %shard_map.108 = (f32[256,1024]{1,0:T(8,128)S(1)}, f32[2,256]{1,0:T(2,128)S(1)}, bf16[1024,128]{1,0:T(8,128)(2,1)S(1)}) custom-call(s32[1,256]{1,0:T(1,128)S(1)} %get-tuple-element.48.length, bf16[256,2048]{1,0:T(8,128)(2,1)S(1)} %shard_map.103.refs_4_.queries, f32[256,2048]{1,0:T(8,128)S(1)} %shard_map.105.local, bf16[256,2048]{1,0:T(8,128)(2,1)S(1)} %bitcast.11, ...), custom_call_target="tpu_custom_call" | custom-call | flops 67108864 | bytes 6042624 | tf_op jit(solution)/shard_map/pallas_call | solution.py:374
  22.3 2.7 %collective-permute-start.14 = (f32[2,256]{1,0:T(2,128)S(1)}, f32[2,256]{1,0:T(2,128)S(1)}, u32[]{:S(2)}, u32[]{:S(2)}) collective-permute-start(f32[2,256]{1,0:T(2,128)S(1)} %get-tuple-element.65.rest_0_), channel_id=1, source_target_pairs={{0,16},{8,24},{16,0},{24,8},{1,17},{9,25},{17,1},{25,9},{2,18},{10... | collective-permute-start | bytes 6152 | tf_op jit(solution)/shard_map/ppermute | solution.py:427
  24.9 1.4 %collective-permute-start.13 = (f32[2,256]{1,0:T(2,128)S(1)}, f32[2,256]{1,0:T(2,128)S(1)}, u32[]{:S(2)}, u32[]{:S(2)}) collective-permute-start(f32[2,256]{1,0:T(2,128)S(1)} %get-tuple-element.65.rest_0_), channel_id=1, source_target_pairs={{0,24},{8,16},{16,8},{24,0},{1,25},{9,17},{17,9},{25,1},{2,26},{10... | collective-permute-start | bytes 6152 | tf_op jit(solution)/shard_map/ppermute | solution.py:427
  26.3 0.2 collective-permute-start.12
  26.5 0.3 collective-permute-done.14.rest_3_
  26.8 3.5 %collective-permute-done.13.rest_2_ = f32[2,256]{1,0:T(2,128)S(1)} collective-permute-done((f32[2,256]{1,0:T(2,128)S(1)}, f32[2,256]{1,0:T(2,128)S(1)}, u32[]{:S(2)}, u32[]{:S(2)}) %collective-permute-start.13) | collective-permute-done | bytes 2080 | tf_op jit(solution)/shard_map/ppermute | solution.py:427
  30.3 0.0 collective-permute-done.12.rest_1_
  30.3 1.0 %shard_map.109 = (bf16[256,2048]{1,0:T(8,128)(2,1)S(1)}, f32[1,256]{1,0:T(1,128)S(1)}, bf16[1024,128]{1,0:T(8,128)(2,1)S(1)}, bf16[1024,128]{1,0:T(8,128)(2,1)S(1)}) custom-call(s32[1,256]{1,0:T(1,128)S(1)} %get-tuple-element.48.length, bf16[256,2048]{1,0:T(8,128)(2,1)S(1)} %shard_map.103.refs_4_.queries, bf16[256,2048]{1,0:T(8,128)(2,1)S(1)} %bitcast.12, ...), custom_call_target="tpu_custom_call" | custom-call | flops 134217728 | bytes 5785600 | tf_op jit(solution)/shard_map/pallas_call | solution.py:374
  31.4 0.1 collective-permute-start.17
  31.4 1.0 %collective-permute-start.15 = (bf16[1024,128]{1,0:T(8,128)(2,1)S(1)}, bf16[1024,128]{1,0:T(8,128)(2,1)S(1)}, u32[]{:S(2)}, u32[]{:S(2)}) collective-permute-start(bf16[1024,128]{1,0:T(8,128)(2,1)S(1)} %get-tuple-element.76), channel_id=1, source_target_pairs={{0,1},{1,0},{2,3},{3,2},{4,5},{5,4},{6,7},{7,6},{8,9},{9,8},{10,11... | collective-permute-start | bytes 786440 | tf_op jit(solution)/shard_map/ppermute | solution.py:396
  32.4 1.1 %collective-permute-start.16 = (bf16[1024,128]{1,0:T(8,128)(2,1)S(1)}, bf16[1024,128]{1,0:T(8,128)(2,1)S(1)}, u32[]{:S(2)}, u32[]{:S(2)}) collective-permute-start(bf16[1024,128]{1,0:T(8,128)(2,1)S(1)} %get-tuple-element.75.refs_0_), channel_id=1, source_target_pairs={{0,2},{1,5},{2,0},{3,7},{4,6},{5,1},{6,4},{7,3},{8,10},{9,13},{10,... | collective-permute-start | bytes 786440 | tf_op jit(solution)/shard_map/ppermute | solution.py:396
  33.6 4.4 %shard_map.110 = (bf16[256,2048]{1,0:T(8,128)(2,1)}, bf16[256,2048]{1,0:T(8,128)(2,1)}, f32[8,128]{1,0:T(8,128)S(1)}) custom-call(s32[1,256]{1,0:T(1,128)S(1)} %get-tuple-element.48.length, f32[1,256]{1,0:T(1,128)S(1)} %get-tuple-element.68.inverse_rms, f32[1,2048]{1,0:T(1,128)S(1)} %bitcast.16, bf16[256,2048]{1,0:T(8,128)(2,1)S(1)} %get-tuple-element.50.keys, ...), custom_call_target="tpu_custom_call" | custom-call | flops 671088640 | bytes 7878656 | tf_op jit(solution)/shard_map/pallas_call | solution.py:374
  38.0 0.4 collective-permute-done.17.refs_3_
  38.4 0.0 collective-permute-done.15.refs_1_
  38.4 1.7 %collective-permute-done.16.refs_2_ = bf16[1024,128]{1,0:T(8,128)(2,1)S(1)} collective-permute-done((bf16[1024,128]{1,0:T(8,128)(2,1)S(1)}, bf16[1024,128]{1,0:T(8,128)(2,1)S(1)}, u32[]{:S(2)}, u32[]{:S(2)}) %collective-permute-start.16) | collective-permute-done | bytes 262176 | tf_op jit(solution)/shard_map/ppermute | solution.py:396
  40.0 0.3 shard_map.111
  40.3 1.6 %collective-permute-start.21 = (bf16[512,128]{1,0:T(8,128)(2,1)S(1)}, bf16[512,128]{1,0:T(8,128)(2,1)S(1)}, u32[]{:S(2)}, u32[]{:S(2)}) collective-permute-start(bf16[512,128]{1,0:T(8,128)(2,1)S(1)} %get-tuple-element.85), channel_id=1, source_target_pairs={{0,4},{1,3},{2,6},{3,1},{4,0},{5,7},{6,2},{7,5},{8,12},{9,11},{10,... | collective-permute-start | bytes 393224 | tf_op jit(solution)/shard_map/ppermute | solution.py:396
  41.9 0.0 collective-permute-start.22
  41.9 0.6 %collective-permute-start.23 = (bf16[512,128]{1,0:T(8,128)(2,1)S(1)}, bf16[512,128]{1,0:T(8,128)(2,1)S(1)}, u32[]{:S(2)}, u32[]{:S(2)}) collective-permute-start(bf16[512,128]{1,0:T(8,128)(2,1)S(1)} %get-tuple-element.87), channel_id=1, source_target_pairs={{0,5},{1,2},{2,7},{3,0},{4,1},{5,6},{6,3},{7,4},{8,13},{9,10},{10,... | collective-permute-start | bytes 393224 | tf_op jit(solution)/shard_map/ppermute | solution.py:396
  42.5 0.3 shard_map.112
  42.8 1.6 %collective-permute-start.18 = (bf16[512,128]{1,0:T(8,128)(2,1)S(1)}, bf16[512,128]{1,0:T(8,128)(2,1)S(1)}, u32[]{:S(2)}, u32[]{:S(2)}) collective-permute-start(bf16[512,128]{1,0:T(8,128)(2,1)S(1)} %get-tuple-element.82), channel_id=1, source_target_pairs={{0,4},{1,3},{2,6},{3,1},{4,0},{5,7},{6,2},{7,5},{8,12},{9,11},{10,... | collective-permute-start | bytes 393224 | tf_op jit(solution)/shard_map/ppermute | solution.py:396
  44.4 0.0 collective-permute-start.19
  44.4 0.9 %collective-permute-done.21.rest_1_ = bf16[512,128]{1,0:T(8,128)(2,1)S(1)} collective-permute-done((bf16[512,128]{1,0:T(8,128)(2,1)S(1)}, bf16[512,128]{1,0:T(8,128)(2,1)S(1)}, u32[]{:S(2)}, u32[]{:S(2)}) %collective-permute-start.21) | collective-permute-done | bytes 131104 | tf_op jit(solution)/shard_map/ppermute | solution.py:396
  45.4 0.0 collective-permute-start.20
  45.4 2.6 %shard_map.113 = (f32[256,2048]{1,0:T(8,128)S(1)}, f32[256,2048]{1,0:T(8,128)S(1)}) custom-call(s32[1,256]{1,0:T(1,128)S(1)} %get-tuple-element.48.length, bf16[256,2048]{1,0:T(8,128)(2,1)S(1)} %shard_map.103.refs_4_.queries, bf16[256,2048]{1,0:T(8,128)(2,1)S(1)} %get-tuple-element.50.keys, bf16[256,2048]{1,0:T(8,128)(2,1)S(1)} %get-tuple-element.51.values, ...), custom_call_target="tpu_custom_call" | custom-call | flops 1073741824 | bytes 8389632 | tf_op jit(solution)/shard_map/pallas_call | solution.py:374
  47.9 0.0 collective-permute-done.22.rest_2_
  47.9 0.0 collective-permute-done.23.rest_3_
  48.0 1.6 %shard_map.114 = (bf16[256,2048]{1,0:T(8,128)(2,1)}, bf16[256,2048]{1,0:T(8,128)(2,1)}) custom-call(s32[1,256]{1,0:T(1,128)S(1)} %get-tuple-element.48.length, bf16[256,2048]{1,0:T(8,128)(2,1)S(1)} %get-tuple-element.50.keys, bf16[256,2048]{1,0:T(8,128)(2,1)S(1)} %get-tuple-element.51.values, f32[256,2048]{1,0:T(8,128)S(1)} %get-tuple-element.80.key_part, ...), custom_call_target="tpu_custom_call" | custom-call | flops 134217728 | bytes 8913920 | tf_op jit(solution)/shard_map/pallas_call | solution.py:374
  49.6 0.0 collective-permute-done.18.rest_1_
  49.6 0.0 collective-permute-done.19.rest_2_
  49.6 0.2 collective-permute-done.20.rest_3_
  49.7 1.6 %shard_map.115 = (bf16[256,2048]{1,0:T(8,128)(2,1)}, bf16[256,2048]{1,0:T(8,128)(2,1)}) custom-call(s32[1,256]{1,0:T(1,128)S(1)} %get-tuple-element.48.length, bf16[256,2048]{1,0:T(8,128)(2,1)S(1)} %get-tuple-element.50.keys, bf16[256,2048]{1,0:T(8,128)(2,1)S(1)} %get-tuple-element.51.values, ...), custom_call_target="tpu_custom_call", output_to_operand_aliasing={{0}: (9, {}), {1}: (10, {})} | custom-call | flops 134217728 | bytes 11011072 | tf_op jit(solution)/shard_map/pallas_call | solution.py:374
  (2 shorter events, 0.0 us)
Async XLA Ops:
  3.6 6.9 %collective-permute-start.2 = (bf16[512,128]{1,0:T(8,128)(2,1)S(1)}, bf16[512,128]{1,0:T(8,128)(2,1)S(1)}, u32[]{:S(2)}, u32[]{:S(2)}) collective-permute-start(bf16[512,128]{1,0:T(8,128)(2,1)S(1)} %get-tuple-element.53), channel_id=1, source_target_pairs={{0,5},{1,2},{2,7},{3,0},{4,1},{5,6},{6,3},{7,4},{8,13},{9,10},{10,... | collective-permute-start | bytes 393224 | tf_op jit(solution)/shard_map/ppermute | solution.py:396
  6.1 4.9 %collective-permute-start = (bf16[512,128]{1,0:T(8,128)(2,1)S(1)}, bf16[512,128]{1,0:T(8,128)(2,1)S(1)}, u32[]{:S(2)}, u32[]{:S(2)}) collective-permute-start(bf16[512,128]{1,0:T(8,128)(2,1)S(1)} %get-tuple-element.53), channel_id=1, source_target_pairs={{0,1},{1,0},{2,3},{3,2},{4,5},{5,4},{6,7},{7,6},{8,9},{9,8},{10,11... | collective-permute-start | bytes 393224 | tf_op jit(solution)/shard_map/ppermute | solution.py:396
  6.7 5.0 %collective-permute-start.1 = (bf16[512,128]{1,0:T(8,128)(2,1)S(1)}, bf16[512,128]{1,0:T(8,128)(2,1)S(1)}, u32[]{:S(2)}, u32[]{:S(2)}) collective-permute-start(bf16[512,128]{1,0:T(8,128)(2,1)S(1)} %get-tuple-element.49._.refs_0_), channel_id=1, source_target_pairs={{0,2},{1,5},{2,0},{3,7},{4,6},{5,1},{6,4},{7,3},{8,10},{9,13},{10,... | collective-permute-start | bytes 393224 | tf_op jit(solution)/shard_map/ppermute | solution.py:396
  7.6 6.8 %collective-permute-start.4 = (bf16[512,128]{1,0:T(8,128)(2,1)S(1)}, bf16[512,128]{1,0:T(8,128)(2,1)S(1)}, u32[]{:S(2)}, u32[]{:S(2)}) collective-permute-start(bf16[512,128]{1,0:T(8,128)(2,1)S(1)} %get-tuple-element.55.refs_0_), channel_id=1, source_target_pairs={{0,2},{1,5},{2,0},{3,7},{4,6},{5,1},{6,4},{7,3},{8,10},{9,13},{10,... | collective-permute-start | bytes 393224 | tf_op jit(solution)/shard_map/ppermute | solution.py:396
  8.8 5.8 %collective-permute-start.5 = (bf16[512,128]{1,0:T(8,128)(2,1)S(1)}, bf16[512,128]{1,0:T(8,128)(2,1)S(1)}, u32[]{:S(2)}, u32[]{:S(2)}) collective-permute-start(bf16[512,128]{1,0:T(8,128)(2,1)S(1)} %get-tuple-element.56), channel_id=1, source_target_pairs={{0,5},{1,2},{2,7},{3,0},{4,1},{5,6},{6,3},{7,4},{8,13},{9,10},{10,... | collective-permute-start | bytes 393224 | tf_op jit(solution)/shard_map/ppermute | solution.py:396
  10.6 4.0 %collective-permute-start.3 = (bf16[512,128]{1,0:T(8,128)(2,1)S(1)}, bf16[512,128]{1,0:T(8,128)(2,1)S(1)}, u32[]{:S(2)}, u32[]{:S(2)}) collective-permute-start(bf16[512,128]{1,0:T(8,128)(2,1)S(1)} %get-tuple-element.56), channel_id=1, source_target_pairs={{0,1},{1,0},{2,3},{3,2},{4,5},{5,4},{6,7},{7,6},{8,9},{9,8},{10,11... | collective-permute-start | bytes 393224 | tf_op jit(solution)/shard_map/ppermute | solution.py:396
  12.0 5.0 %collective-permute-start.9 = (bf16[512,128]{1,0:T(8,128)(2,1)S(1)}, bf16[512,128]{1,0:T(8,128)(2,1)S(1)}, u32[]{:S(2)}, u32[]{:S(2)}) collective-permute-start(bf16[512,128]{1,0:T(8,128)(2,1)S(1)} %get-tuple-element.61), channel_id=1, source_target_pairs={{0,4},{1,3},{2,6},{3,1},{4,0},{5,7},{6,2},{7,5},{8,12},{9,11},{10,... | collective-permute-start | bytes 393224 | tf_op jit(solution)/shard_map/ppermute | solution.py:396
  13.6 5.7 %collective-permute-start.10 = (bf16[512,128]{1,0:T(8,128)(2,1)S(1)}, bf16[512,128]{1,0:T(8,128)(2,1)S(1)}, u32[]{:S(2)}, u32[]{:S(2)}) collective-permute-start(bf16[512,128]{1,0:T(8,128)(2,1)S(1)} %get-tuple-element.62), channel_id=1, source_target_pairs={{0,1},{1,0},{2,3},{3,2},{4,5},{5,4},{6,7},{7,6},{8,9},{9,8},{10,11... | collective-permute-start | bytes 393224 | tf_op jit(solution)/shard_map/ppermute | solution.py:396
  14.4 4.9 %collective-permute-start.11 = (bf16[512,128]{1,0:T(8,128)(2,1)S(1)}, bf16[512,128]{1,0:T(8,128)(2,1)S(1)}, u32[]{:S(2)}, u32[]{:S(2)}) collective-permute-start(bf16[512,128]{1,0:T(8,128)(2,1)S(1)} %get-tuple-element.63), channel_id=1, source_target_pairs={{0,5},{1,2},{2,7},{3,0},{4,1},{5,6},{6,3},{7,4},{8,13},{9,10},{10,... | collective-permute-start | bytes 393224 | tf_op jit(solution)/shard_map/ppermute | solution.py:396
  14.9 5.4 %collective-permute-start.6 = (bf16[512,128]{1,0:T(8,128)(2,1)S(1)}, bf16[512,128]{1,0:T(8,128)(2,1)S(1)}, u32[]{:S(2)}, u32[]{:S(2)}) collective-permute-start(bf16[512,128]{1,0:T(8,128)(2,1)S(1)} %get-tuple-element.58), channel_id=1, source_target_pairs={{0,4},{1,3},{2,6},{3,1},{4,0},{5,7},{6,2},{7,5},{8,12},{9,11},{10,... | collective-permute-start | bytes 393224 | tf_op jit(solution)/shard_map/ppermute | solution.py:396
  16.4 3.9 %collective-permute-start.7 = (bf16[512,128]{1,0:T(8,128)(2,1)S(1)}, bf16[512,128]{1,0:T(8,128)(2,1)S(1)}, u32[]{:S(2)}, u32[]{:S(2)}) collective-permute-start(bf16[512,128]{1,0:T(8,128)(2,1)S(1)} %get-tuple-element.59), channel_id=1, source_target_pairs={{0,1},{1,0},{2,3},{3,2},{4,5},{5,4},{6,7},{7,6},{8,9},{9,8},{10,11... | collective-permute-start | bytes 393224 | tf_op jit(solution)/shard_map/ppermute | solution.py:396
  17.0 4.6 %collective-permute-start.8 = (bf16[512,128]{1,0:T(8,128)(2,1)S(1)}, bf16[512,128]{1,0:T(8,128)(2,1)S(1)}, u32[]{:S(2)}, u32[]{:S(2)}) collective-permute-start(bf16[512,128]{1,0:T(8,128)(2,1)S(1)} %get-tuple-element.60), channel_id=1, source_target_pairs={{0,5},{1,2},{2,7},{3,0},{4,1},{5,6},{6,3},{7,4},{8,13},{9,10},{10,... | collective-permute-start | bytes 393224 | tf_op jit(solution)/shard_map/ppermute | solution.py:396
  17.8 1.5 %copy-start = (bf16[1,256,2048]{2,1,0:T(8,128)(2,1)S(1)}, bf16[1,256,2048]{2,1,0:T(8,128)(2,1)}, u32[]{:S(2)}) copy-start(bf16[1,256,2048]{2,1,0:T(8,128)(2,1)} %param.10) | copy-start | bytes 3145732
  17.8 1.5 %copy-start.1 = (f32[2048]{0:T(1024)S(1)}, f32[2048]{0:T(1024)}, u32[]{:S(2)}) copy-start(f32[2048]{0:T(1024)} %param.11) | copy-start | bytes 24580
  22.3 4.5 %collective-permute-start.14 = (f32[2,256]{1,0:T(2,128)S(1)}, f32[2,256]{1,0:T(2,128)S(1)}, u32[]{:S(2)}, u32[]{:S(2)}) collective-permute-start(f32[2,256]{1,0:T(2,128)S(1)} %get-tuple-element.65.rest_0_), channel_id=1, source_target_pairs={{0,16},{8,24},{16,0},{24,8},{1,17},{9,25},{17,1},{25,9},{2,18},{10... | collective-permute-start | bytes 6152 | tf_op jit(solution)/shard_map/ppermute | solution.py:427
  24.9 5.4 %collective-permute-start.13 = (f32[2,256]{1,0:T(2,128)S(1)}, f32[2,256]{1,0:T(2,128)S(1)}, u32[]{:S(2)}, u32[]{:S(2)}) collective-permute-start(f32[2,256]{1,0:T(2,128)S(1)} %get-tuple-element.65.rest_0_), channel_id=1, source_target_pairs={{0,24},{8,16},{16,8},{24,0},{1,25},{9,17},{17,9},{25,1},{2,26},{10... | collective-permute-start | bytes 6152 | tf_op jit(solution)/shard_map/ppermute | solution.py:427
  26.3 4.0 %collective-permute-start.12 = (f32[2,256]{1,0:T(2,128)S(1)}, f32[2,256]{1,0:T(2,128)S(1)}, u32[]{:S(2)}, u32[]{:S(2)}) collective-permute-start(f32[2,256]{1,0:T(2,128)S(1)} %get-tuple-element.65.rest_0_), channel_id=1, source_target_pairs={{0,8},{8,0},{16,24},{24,16},{1,9},{9,1},{17,25},{25,17},{2,10},{10... | collective-permute-start | bytes 6152 | tf_op jit(solution)/shard_map/ppermute | solution.py:427
  31.4 7.0 %collective-permute-start.17 = (bf16[1024,128]{1,0:T(8,128)(2,1)S(1)}, bf16[1024,128]{1,0:T(8,128)(2,1)S(1)}, u32[]{:S(2)}, u32[]{:S(2)}) collective-permute-start(bf16[1024,128]{1,0:T(8,128)(2,1)S(1)} %get-tuple-element.76), channel_id=1, source_target_pairs={{0,5},{1,2},{2,7},{3,0},{4,1},{5,6},{6,3},{7,4},{8,13},{9,10},{10,... | collective-permute-start | bytes 786440 | tf_op jit(solution)/shard_map/ppermute | solution.py:396
  31.4 6.9 %collective-permute-start.15 = (bf16[1024,128]{1,0:T(8,128)(2,1)S(1)}, bf16[1024,128]{1,0:T(8,128)(2,1)S(1)}, u32[]{:S(2)}, u32[]{:S(2)}) collective-permute-start(bf16[1024,128]{1,0:T(8,128)(2,1)S(1)} %get-tuple-element.76), channel_id=1, source_target_pairs={{0,1},{1,0},{2,3},{3,2},{4,5},{5,4},{6,7},{7,6},{8,9},{9,8},{10,11... | collective-permute-start | bytes 786440 | tf_op jit(solution)/shard_map/ppermute | solution.py:396
  32.4 7.6 %collective-permute-start.16 = (bf16[1024,128]{1,0:T(8,128)(2,1)S(1)}, bf16[1024,128]{1,0:T(8,128)(2,1)S(1)}, u32[]{:S(2)}, u32[]{:S(2)}) collective-permute-start(bf16[1024,128]{1,0:T(8,128)(2,1)S(1)} %get-tuple-element.75.refs_0_), channel_id=1, source_target_pairs={{0,2},{1,5},{2,0},{3,7},{4,6},{5,1},{6,4},{7,3},{8,10},{9,13},{10,... | collective-permute-start | bytes 786440 | tf_op jit(solution)/shard_map/ppermute | solution.py:396
  40.3 5.0 %collective-permute-start.21 = (bf16[512,128]{1,0:T(8,128)(2,1)S(1)}, bf16[512,128]{1,0:T(8,128)(2,1)S(1)}, u32[]{:S(2)}, u32[]{:S(2)}) collective-permute-start(bf16[512,128]{1,0:T(8,128)(2,1)S(1)} %get-tuple-element.85), channel_id=1, source_target_pairs={{0,4},{1,3},{2,6},{3,1},{4,0},{5,7},{6,2},{7,5},{8,12},{9,11},{10,... | collective-permute-start | bytes 393224 | tf_op jit(solution)/shard_map/ppermute | solution.py:396
  41.9 6.0 %collective-permute-start.22 = (bf16[512,128]{1,0:T(8,128)(2,1)S(1)}, bf16[512,128]{1,0:T(8,128)(2,1)S(1)}, u32[]{:S(2)}, u32[]{:S(2)}) collective-permute-start(bf16[512,128]{1,0:T(8,128)(2,1)S(1)} %get-tuple-element.86), channel_id=1, source_target_pairs={{0,1},{1,0},{2,3},{3,2},{4,5},{5,4},{6,7},{7,6},{8,9},{9,8},{10,11... | collective-permute-start | bytes 393224 | tf_op jit(solution)/shard_map/ppermute | solution.py:396
  41.9 6.0 %collective-permute-start.23 = (bf16[512,128]{1,0:T(8,128)(2,1)S(1)}, bf16[512,128]{1,0:T(8,128)(2,1)S(1)}, u32[]{:S(2)}, u32[]{:S(2)}) collective-permute-start(bf16[512,128]{1,0:T(8,128)(2,1)S(1)} %get-tuple-element.87), channel_id=1, source_target_pairs={{0,5},{1,2},{2,7},{3,0},{4,1},{5,6},{6,3},{7,4},{8,13},{9,10},{10,... | collective-permute-start | bytes 393224 | tf_op jit(solution)/shard_map/ppermute | solution.py:396
  42.8 6.7 %collective-permute-start.18 = (bf16[512,128]{1,0:T(8,128)(2,1)S(1)}, bf16[512,128]{1,0:T(8,128)(2,1)S(1)}, u32[]{:S(2)}, u32[]{:S(2)}) collective-permute-start(bf16[512,128]{1,0:T(8,128)(2,1)S(1)} %get-tuple-element.82), channel_id=1, source_target_pairs={{0,4},{1,3},{2,6},{3,1},{4,0},{5,7},{6,2},{7,5},{8,12},{9,11},{10,... | collective-permute-start | bytes 393224 | tf_op jit(solution)/shard_map/ppermute | solution.py:396
  44.4 5.2 %collective-permute-start.19 = (bf16[512,128]{1,0:T(8,128)(2,1)S(1)}, bf16[512,128]{1,0:T(8,128)(2,1)S(1)}, u32[]{:S(2)}, u32[]{:S(2)}) collective-permute-start(bf16[512,128]{1,0:T(8,128)(2,1)S(1)} %get-tuple-element.83), channel_id=1, source_target_pairs={{0,1},{1,0},{2,3},{3,2},{4,5},{5,4},{6,7},{7,6},{8,9},{9,8},{10,11... | collective-permute-start | bytes 393224 | tf_op jit(solution)/shard_map/ppermute | solution.py:396
  45.4 4.4 %collective-permute-start.20 = (bf16[512,128]{1,0:T(8,128)(2,1)S(1)}, bf16[512,128]{1,0:T(8,128)(2,1)S(1)}, u32[]{:S(2)}, u32[]{:S(2)}) collective-permute-start(bf16[512,128]{1,0:T(8,128)(2,1)S(1)} %get-tuple-element.84), channel_id=1, source_target_pairs={{0,5},{1,2},{2,7},{3,0},{4,1},{5,6},{6,3},{7,4},{8,13},{9,10},{10,... | collective-permute-start | bytes 393224 | tf_op jit(solution)/shard_map/ppermute | solution.py:396

commit v8 on v7

--- a/solution.py
+++ b/solution.py
@@ -148,11 +148,15 @@
     outs, (full, sems, parent, parent_sem) = rest[:-4], rest[-4:]
     rows, width = keys.shape
     chunk = rows // 4 if rows % 64 == 0 else rows
+    steps = rows // chunk
+    spans = 2 if width % (2 * HD) == 0 else 1
     copies = []
-    for step in range(rows // chunk):
-        part = slice(step * chunk, (step + 1) * chunk)
-        for j, (src, dst) in enumerate(((keys_hbm, keys), (values_hbm, values))):
-            copies.append(pltpu.make_async_copy(src.at[part, :], dst.at[part, :], sems.at[j, step]))
+    for span in range(spans):
+        cols = slice(span * width // spans, (span + 1) * width // spans)
+        for step in range(steps):
+            part = slice(step * chunk, (step + 1) * chunk)
+            for j, (src, dst) in enumerate(((keys_hbm, keys), (values_hbm, values))):
+                copies.append(pltpu.make_async_copy(src.at[part, cols], dst.at[part, cols], sems.at[j, span * steps + step]))
     few = pltpu.make_async_copy(parent_hbm, parent, parent_sem)
     few.start()
     for copy in copies:
@@ -161,17 +165,20 @@
     few.wait()
     write_weights(grid, parent, up, down)
     live = lax.broadcasted_iota(jnp.int32, (rows, HD), 0) < seg_len[0]
-    for copy in copies:
-        copy.wait()
     for head in range(width // HD):
+        if head % (width // HD // spans) == 0:
+            span = head // (width // HD // spans)
+            for copy in copies[span * 2 * steps : (span + 1) * 2 * steps]:
+                copy.wait()
         cols = head_cols(head)
         masked = jnp.where(live, keys[:, cols], jnp.zeros((), BF16))
         full[head * HD : (head + 1) * HD, :] = tn(masked, values[:, cols]).astype(BF16)
     write_halves(full, outs, my_place(grid)[2], grid[2])
 
 
-def mix_kernel(sources, first, weights, *refs):
+def mix_kernel(sources, pair, first, weights, *refs):
     blocks, outs = refs[:sources], refs[-sources:]
+    blocks = blocks[:1] + blocks[sources - pair + 1 :] + blocks[1 : sources - pair + 1]
     rows = outs[0].shape[0]
     chunk = min(rows, 64)
     for start in range(0, rows, chunk):
@@ -212,12 +219,7 @@
 
 
 def fetch_kernel(source, _, out, sems):
-    rows = out.shape[0]
-    chunk = rows // 4 if rows % 64 == 0 else rows
-    copies = []
-    for step in range(rows // chunk):
-        part = pl.ds(step * chunk, chunk)
-        copies.append(pltpu.make_async_copy(source.at[part, :], out.at[part, :], sems.at[step]))
+    copies = row_copies(source, out, sems)
     for copy in copies:
         copy.start()
     for copy in copies:
@@ -293,12 +295,9 @@
 def query_kernel(heads, scale, length, inverse_rms, gain, keys, values, *rest):
     sizes = (BACKWARD_PIECES, FORWARD_PIECES, FORWARD_PIECES)
     grads, attention, prefix, rest = split_refs(rest, *sizes, len(rest) - sum(sizes))
-    attended_hbm, query_hbm, token, attended, query_grad, sems = rest[-6:]
-    token[...] = jnp.zeros_like(token)
+    attended, query_grad = rest[-2:]
     keep = keep_mask(length, False)
     inverse = token_columns(inverse_rms[...])
-    group = 8 if heads % 8 == 0 else 1
-    copies = []
     for head in range(heads):
         cols = head_cols(head)
         grad_piece, at = head_of(grads, head)
@@ -310,18 +309,21 @@
         carried = nt(grad, prefix_piece[state * HD : (state + 1) * HD, :])
         query_grad[:, cols] = (scale * (carried + nn(grad_scores, keys[:, cols]))).astype(BF16)
         attended[:, cols] = (out_piece[:, at] * inverse * gain[:, cols]).astype(BF16)
-        if (head + 1) % group == 0:
-            done = slice((head + 1 - group) * HD, (head + 1) * HD)
-            for j, (src, dst) in enumerate(((attended, attended_hbm), (query_grad, query_hbm))):
-                copy = pltpu.make_async_copy(src.at[:, done], dst.at[:, done], sems.at[j, head // group])
-                copy.start()
-                copies.append(copy)
+
+
+def row_copies(source, target, sems):
+    rows = target.shape[0]
+    chunk = rows // 4 if rows % 64 == 0 else rows
+    parts = [pl.ds(step * chunk, chunk) for step in range(rows // chunk)]
+    return [pltpu.make_async_copy(source.at[p, :], target.at[p, :], sems.at[j]) for j, p in enumerate(parts)]
+
+
+def back_kernel(heads, scale, length, queries, keys, values, attended, query_grad, *rest):
+    grads, (attended_hbm, query_hbm, key_part, value_part, token, sems) = rest[:BACKWARD_PIECES], rest[-6:]
+    copies = row_copies(attended, attended_hbm, sems.at[0]) + row_copies(query_grad, query_hbm, sems.at[1])
     for copy in copies:
-        copy.wait()
-
-
-def back_kernel(heads, scale, length, queries, keys, values, *rest):
-    grads, (key_part, value_part) = rest[:BACKWARD_PIECES], rest[-2:]
+        copy.start()
+    token[...] = jnp.zeros_like(token)
     keep = keep_mask(length, True)
     for head in range(heads):
         cols = head_cols(head)
@@ -331,6 +333,8 @@
         key_part[:, cols] = scale * nn(turned, query)
         turned = jnp.where(keep, nt(keys[:, cols], query), 0.0).astype(BF16)
         value_part[:, cols] = scale * nn(turned, grad)
+    for copy in copies:
+        copy.wait()
 
 
 def final_kernel(piece, grid, counts, length, keys, values, key_part, value_part, *rest):
@@ -397,26 +401,22 @@
 
 
 def gather_line(halves, grid):
-    arrived = []
+    pair = grid[2]
+    arrived = {0: halves[0]}
     for step in range(line_length(grid)):
-        for flip in range(grid[2]):
-            if step == 0 and flip == 0:
-                arrived.append(halves[0])
-            else:
-                arrived.append(line_send(halves[flip], grid, step, flip, True))
-    return arrived
+        for flip in range(pair):
+            if step or flip:
+                arrived[step * pair + flip] = line_send(halves[flip], grid, step, flip, True)
+    return [arrived[j] for j in range(len(arrived))]
 
 
 def scatter_line(sums, grid):
     pair = grid[2]
     parts = [[] for _ in range(pair)]
-    for step in range(line_length(grid)):
+    for step in reversed(range(line_length(grid))):
         for flip in range(pair):
             block = sums[step * pair + flip]
-            if step == 0 and flip == 0:
-                parts[0].append(block)
-            else:
-                parts[flip].append(line_send(block, grid, step, flip, False))
+            parts[flip].append(line_send(block, grid, step, flip, False) if step or flip else block)
     return parts
 
 
@@ -452,7 +452,8 @@
     def mix(arrived, weights, piece, pieces, after=()):
         tall = arrived[0].shape[0] // pieces
         like = [shape((tall, HD), BF16)] * members
-        return call(functools.partial(mix_kernel, members, piece * tall), like, (weights, *arrived), after=after)
+        arrived = arrived[:1] + arrived[pair:] + arrived[1:pair]
+        return call(functools.partial(mix_kernel, members, pair, piece * tall), like, (weights, *arrived), after=after)
 
     def flat(parts):
         return [block for part in parts for block in part]
@@ -496,22 +497,23 @@
         )
         grads.append(grad_out)
         state_grad.append(parts)
-    attended, query_grad, token = call(
+    attended, query_grad = call(
         functools.partial(query_kernel, heads, scale),
-        [narrow, narrow, shape((8, HD), F32)],
+        [narrow, narrow],
         (length, inverse_rms, gain, key, value, *grads, *attention, *prefix),
-        [pltpu.VMEM(narrow.shape, BF16)] * 2 + [sems], unit * (2 * rows + HD),
-        out_specs=[HBM, HBM, VMEM],
+        (), unit * (2 * rows + HD),
+    )
+    attended, query_grad, key_part, value_part, token = call(
+        functools.partial(back_kernel, heads, scale),
+        [narrow, narrow, wide, wide, shape((8, HD), F32)],
+        (length, query, key, value, attended, query_grad, *grads), [pltpu.SemaphoreType.DMA((2, 4))],
+        unit * 4 * rows, out_specs=[HBM, HBM, VMEM, VMEM, VMEM],
     )
     (part,) = state_grad
     arrived = gather_line(part, grid)
     mixed = []
     for piece in range(RETURN_PIECES):
         mixed.append(mix(arrived, down, piece, RETURN_PIECES, (token, *mixed[-1][:1]) if mixed else (token,)))
-    key_part, value_part = call(
-        functools.partial(back_kernel, heads, scale),
-        [wide, wide], (length, query, key, value, *grads), (), unit * 4 * rows, after=(mixed[-1][0],),
-    )
     results = []
     width = features // RETURN_PIECES
     for piece in range(RETURN_PIECES):

time: 52.1 us -> 52.2 us (level)
    ppermute x21, waiting for transfers between devices: 6.67 us -> 6.08 us  [line_send(): return lax.ppermute(block, 'seg', moves)]
    ppermute x3, waiting for transfers between devices: 3.81 us -> 4.36 us  [token_sums(): parts.append(lax.ppermute(sums, 'head', moves))]
where the time goes in v8:
time: 52.2 us; the launch traced here: 51.7 us
  starting transfers between devices  21 us (40%)
  Pallas kernels  18.7 us (36%)
  waiting for transfers between devices  10.4 us (20%)
  between operations  1.57 us (3%)
    pallas_call x14, Pallas kernels, call(): pl.pallas_call(kernel, out_shape=out_shape, in_specs=specs + [ANY] * len(...  18.7 us
    ppermute x21, starting transfers between devices, line_send(): return lax.ppermute(block, 'seg', moves)  16.6 us
    ppermute x21, waiting for transfers between devices, line_send(): return lax.ppermute(block, 'seg', moves)  6.08 us
    ppermute x3, waiting for transfers between devices, token_sums(): parts.append(lax.ppermute(sums, 'head', moves))  4.36 us
    ppermute x3, starting transfers between devices, token_sums(): parts.append(lax.ppermute(sums, 'head', moves))  4.35 us
  transfers between devices with their start and end apart: 24, of which 11 were waited for; matrix products, arithmetic and copies ran while one was open for 0% of the time, Pallas kernels for 25%

profile of v8, /device:TPU:0, one launch (start us, length us, event | category | flops | bytes accessed | tf_op | source)
XLA Modules:
  0.0 51.7 jit_solution(14499174736174355302)
XLA Ops:
  1.3 2.3 %shard_map.102 = (bf16[256,2048]{1,0:T(8,128)(2,1)S(1)}, bf16[256,2048]{1,0:T(8,128)(2,1)S(1)}, s32[1,256]{1,0:T(1,128)S(1)}, f32[16,128]{1,0:T(8,128)S(1)}, f32...) custom-call(s32[1]{0:T(128)S(6)} %copy.15.seg_len, ...), custom_call_target="tpu_custom_call" | custom-call | flops 134217728 | bytes 4736036 | tf_op jit(solution)/shard_map/pallas_call | solution.py:378
  3.6 3.0 %collective-permute-start = (bf16[512,128]{1,0:T(8,128)(2,1)S(1)}, bf16[512,128]{1,0:T(8,128)(2,1)S(1)}, u32[]{:S(2)}, u32[]{:S(2)}) collective-permute-start(bf16[512,128]{1,0:T(8,128)(2,1)S(1)} %get-tuple-element.51._.refs_0_), channel_id=1, source_target_pairs={{0,2},{1,5},{2,0},{3,7},{4,6},{5,1},{6,4},{7,3},{8,10},{9,13},{10,... | collective-permute-start | bytes 393224 | tf_op jit(solution)/shard_map/ppermute | solution.py:400
  6.6 0.0 collective-permute-start.1
  6.6 0.2 collective-permute-start.2
  6.8 2.0 %collective-permute-start.3 = (bf16[512,128]{1,0:T(8,128)(2,1)S(1)}, bf16[512,128]{1,0:T(8,128)(2,1)S(1)}, u32[]{:S(2)}, u32[]{:S(2)}) collective-permute-start(bf16[512,128]{1,0:T(8,128)(2,1)S(1)} %get-tuple-element.57.refs_0_), channel_id=1, source_target_pairs={{0,2},{1,5},{2,0},{3,7},{4,6},{5,1},{6,4},{7,3},{8,10},{9,13},{10,... | collective-permute-start | bytes 393224 | tf_op jit(solution)/shard_map/ppermute | solution.py:400
  8.8 0.0 collective-permute-start.4
  8.8 1.2 %shard_map.103.refs_4_.queries = bf16[256,2048]{1,0:T(8,128)(2,1)S(1)} custom-call(bf16[256,2048]{1,0:T(8,128)(2,1)} %bitcast.19, bf16[512,128]{1,0:T(8,128)(2,1)S(1)} %get-tuple-element.51._.refs_0_), custom_call_target="tpu_custom_call" | custom-call | bytes 2097152 | tf_op jit(solution)/shard_map/pallas_call | solution.py:378
  10.0 0.4 collective-permute-done.refs_1_
  10.4 0.0 collective-permute-start.5
  10.4 1.3 %collective-permute-done.1.refs_2_ = bf16[512,128]{1,0:T(8,128)(2,1)S(1)} collective-permute-done((bf16[512,128]{1,0:T(8,128)(2,1)S(1)}, bf16[512,128]{1,0:T(8,128)(2,1)S(1)}, u32[]{:S(2)}, u32[]{:S(2)}) %collective-permute-start.1) | collective-permute-done | bytes 131104 | tf_op jit(solution)/shard_map/ppermute | solution.py:400
  11.7 0.0 collective-permute-done.2.refs_3_
  11.7 0.3 shard_map.104
  12.0 0.6 %collective-permute-start.10 = (bf16[512,128]{1,0:T(8,128)(2,1)S(1)}, bf16[512,128]{1,0:T(8,128)(2,1)S(1)}, u32[]{:S(2)}, u32[]{:S(2)}) collective-permute-start(bf16[512,128]{1,0:T(8,128)(2,1)S(1)} %get-tuple-element.64), channel_id=1, source_target_pairs={{0,5},{1,2},{2,7},{3,0},{4,1},{5,6},{6,3},{7,4},{8,13},{9,10},{10,... | collective-permute-start | bytes 393224 | tf_op jit(solution)/shard_map/ppermute | solution.py:400
  12.6 0.8 %collective-permute-start.11 = (bf16[512,128]{1,0:T(8,128)(2,1)S(1)}, bf16[512,128]{1,0:T(8,128)(2,1)S(1)}, u32[]{:S(2)}, u32[]{:S(2)}) collective-permute-start(bf16[512,128]{1,0:T(8,128)(2,1)S(1)} %get-tuple-element.65), channel_id=1, source_target_pairs={{0,1},{1,0},{2,3},{3,2},{4,5},{5,4},{6,7},{7,6},{8,9},{9,8},{10,11... | collective-permute-start | bytes 393224 | tf_op jit(solution)/shard_map/ppermute | solution.py:400
  13.4 0.0 collective-permute-done.3.refs_1_
  13.4 1.8 %collective-permute-start.9 = (bf16[512,128]{1,0:T(8,128)(2,1)S(1)}, bf16[512,128]{1,0:T(8,128)(2,1)S(1)}, u32[]{:S(2)}, u32[]{:S(2)}) collective-permute-start(bf16[512,128]{1,0:T(8,128)(2,1)S(1)} %get-tuple-element.63), channel_id=1, source_target_pairs={{0,4},{1,3},{2,6},{3,1},{4,0},{5,7},{6,2},{7,5},{8,12},{9,11},{10,... | collective-permute-start | bytes 393224 | tf_op jit(solution)/shard_map/ppermute | solution.py:400
  15.2 0.0 collective-permute-done.4.refs_2_
  15.2 0.0 collective-permute-done.5.refs_3_
  15.2 0.3 shard_map.106
  15.5 0.7 %collective-permute-start.6 = (bf16[512,128]{1,0:T(8,128)(2,1)S(1)}, bf16[512,128]{1,0:T(8,128)(2,1)S(1)}, u32[]{:S(2)}, u32[]{:S(2)}) collective-permute-start(bf16[512,128]{1,0:T(8,128)(2,1)S(1)} %get-tuple-element.59), channel_id=1, source_target_pairs={{0,4},{1,3},{2,6},{3,1},{4,0},{5,7},{6,2},{7,5},{8,12},{9,11},{10,... | collective-permute-start | bytes 393224 | tf_op jit(solution)/shard_map/ppermute | solution.py:400
  16.2 0.3 collective-permute-start.7
  16.5 0.0 collective-permute-done.10.rest_2_
  16.5 1.3 %collective-permute-start.8 = (bf16[512,128]{1,0:T(8,128)(2,1)S(1)}, bf16[512,128]{1,0:T(8,128)(2,1)S(1)}, u32[]{:S(2)}, u32[]{:S(2)}) collective-permute-start(bf16[512,128]{1,0:T(8,128)(2,1)S(1)} %get-tuple-element.62), channel_id=1, source_target_pairs={{0,1},{1,0},{2,3},{3,2},{4,5},{5,4},{6,7},{7,6},{8,9},{9,8},{10,11... | collective-permute-start | bytes 393224 | tf_op jit(solution)/shard_map/ppermute | solution.py:400
  17.8 1.5 %shard_map.105.local = f32[256,2048]{1,0:T(8,128)S(1)} custom-call(s32[1,256]{1,0:T(1,128)S(1)} %get-tuple-element.50.length, bf16[256,2048]{1,0:T(8,128)(2,1)S(1)} %shard_map.103.refs_4_.queries, bf16[256,2048]{1,0:T(8,128)(2,1)S(1)} %get-tuple-element.52.keys, bf16[256,2048]{1,0:T(8,128)(2,1)S(1)} %get-tuple-element.53.values, ...), custom_call_target="tpu_custom_call" | custom-call | flops 536870912 | bytes 5243904 | tf_op jit(solution)/shard_map/pallas_call | solution.py:378
  19.3 0.0 collective-permute-done.11.rest_3_
  19.3 0.0 collective-permute-done.9.rest_0_
  19.3 0.0 copy-done
  19.4 0.0 copy-done.1
  19.4 0.7 %shard_map.107 = (f32[256,1024]{1,0:T(8,128)S(1)}, f32[2,256]{1,0:T(2,128)S(1)}, bf16[1024,128]{1,0:T(8,128)(2,1)S(1)}) custom-call(s32[1,256]{1,0:T(1,128)S(1)} %get-tuple-element.50.length, bf16[256,2048]{1,0:T(8,128)(2,1)S(1)} %shard_map.103.refs_4_.queries, f32[256,2048]{1,0:T(8,128)S(1)} %shard_map.105.local, bf16[256,2048]{1,0:T(8,128)(2,1)S(1)} %bitcast.10, ...), custom_call_target="tpu_custom_call" | custom-call | flops 67108864 | bytes 6040576 | tf_op jit(solution)/shard_map/pallas_call | solution.py:378
  20.0 0.5 collective-permute-done.6.rest_0_
  20.5 0.5 collective-permute-done.7.rest_2_
  21.0 0.0 collective-permute-done.8.rest_3_
  21.0 0.7 %shard_map.108 = (f32[256,1024]{1,0:T(8,128)S(1)}, f32[2,256]{1,0:T(2,128)S(1)}, bf16[1024,128]{1,0:T(8,128)(2,1)S(1)}) custom-call(s32[1,256]{1,0:T(1,128)S(1)} %get-tuple-element.50.length, bf16[256,2048]{1,0:T(8,128)(2,1)S(1)} %shard_map.103.refs_4_.queries, f32[256,2048]{1,0:T(8,128)S(1)} %shard_map.105.local, bf16[256,2048]{1,0:T(8,128)(2,1)S(1)} %bitcast.11, ...), custom_call_target="tpu_custom_call" | custom-call | flops 67108864 | bytes 6042624 | tf_op jit(solution)/shard_map/pallas_call | solution.py:378
  21.7 1.7 %collective-permute-start.12 = (f32[2,256]{1,0:T(2,128)S(1)}, f32[2,256]{1,0:T(2,128)S(1)}, u32[]{:S(2)}, u32[]{:S(2)}) collective-permute-start(f32[2,256]{1,0:T(2,128)S(1)} %get-tuple-element.67.rest_0_), channel_id=1, source_target_pairs={{0,8},{8,0},{16,24},{24,16},{1,9},{9,1},{17,25},{25,17},{2,10},{10... | collective-permute-start | bytes 6152 | tf_op jit(solution)/shard_map/ppermute | solution.py:427
  23.4 2.5 %collective-permute-start.13 = (f32[2,256]{1,0:T(2,128)S(1)}, f32[2,256]{1,0:T(2,128)S(1)}, u32[]{:S(2)}, u32[]{:S(2)}) collective-permute-start(f32[2,256]{1,0:T(2,128)S(1)} %get-tuple-element.67.rest_0_), channel_id=1, source_target_pairs={{0,24},{8,16},{16,8},{24,0},{1,25},{9,17},{17,9},{25,1},{2,26},{10... | collective-permute-start | bytes 6152 | tf_op jit(solution)/shard_map/ppermute | solution.py:427
  25.9 0.1 collective-permute-start.14
  26.0 0.0 collective-permute-done.12.rest_1_
  26.0 2.8 %collective-permute-done.13.rest_2_ = f32[2,256]{1,0:T(2,128)S(1)} collective-permute-done((f32[2,256]{1,0:T(2,128)S(1)}, f32[2,256]{1,0:T(2,128)S(1)}, u32[]{:S(2)}, u32[]{:S(2)}) %collective-permute-start.13) | collective-permute-done | bytes 2080 | tf_op jit(solution)/shard_map/ppermute | solution.py:427
  28.8 1.6 %collective-permute-done.14.rest_3_ = f32[2,256]{1,0:T(2,128)S(1)} collective-permute-done((f32[2,256]{1,0:T(2,128)S(1)}, f32[2,256]{1,0:T(2,128)S(1)}, u32[]{:S(2)}, u32[]{:S(2)}) %collective-permute-start.14) | collective-permute-done | bytes 2080 | tf_op jit(solution)/shard_map/ppermute | solution.py:427
  30.4 1.1 %shard_map.109 = (bf16[256,2048]{1,0:T(8,128)(2,1)S(1)}, f32[1,256]{1,0:T(1,128)S(1)}, bf16[1024,128]{1,0:T(8,128)(2,1)S(1)}, bf16[1024,128]{1,0:T(8,128)(2,1)S(1)}) custom-call(s32[1,256]{1,0:T(1,128)S(1)} %get-tuple-element.50.length, bf16[256,2048]{1,0:T(8,128)(2,1)S(1)} %shard_map.103.refs_4_.queries, bf16[256,2048]{1,0:T(8,128)(2,1)S(1)} %bitcast.12, ...), custom_call_target="tpu_custom_call" | custom-call | flops 134217728 | bytes 5785600 | tf_op jit(solution)/shard_map/pallas_call | solution.py:378
  31.5 1.6 %collective-permute-start.15 = (bf16[1024,128]{1,0:T(8,128)(2,1)S(1)}, bf16[1024,128]{1,0:T(8,128)(2,1)S(1)}, u32[]{:S(2)}, u32[]{:S(2)}) collective-permute-start(bf16[1024,128]{1,0:T(8,128)(2,1)S(1)} %get-tuple-element.81.refs_0_), channel_id=1, source_target_pairs={{0,2},{1,5},{2,0},{3,7},{4,6},{5,1},{6,4},{7,3},{8,10},{9,13},{10,... | collective-permute-start | bytes 786440 | tf_op jit(solution)/shard_map/ppermute | solution.py:400
  33.0 0.0 collective-permute-start.16
  33.0 0.6 %collective-permute-start.17 = (bf16[1024,128]{1,0:T(8,128)(2,1)S(1)}, bf16[1024,128]{1,0:T(8,128)(2,1)S(1)}, u32[]{:S(2)}, u32[]{:S(2)}) collective-permute-start(bf16[1024,128]{1,0:T(8,128)(2,1)S(1)} %get-tuple-element.82), channel_id=1, source_target_pairs={{0,1},{1,0},{2,3},{3,2},{4,5},{5,4},{6,7},{7,6},{8,9},{9,8},{10,11... | collective-permute-start | bytes 786440 | tf_op jit(solution)/shard_map/ppermute | solution.py:400
  33.7 3.2 %shard_map.110 = (bf16[256,2048]{1,0:T(8,128)(2,1)S(1)}, bf16[256,2048]{1,0:T(8,128)(2,1)S(1)}) custom-call(s32[1,256]{1,0:T(1,128)S(1)} %get-tuple-element.50.length, f32[1,256]{1,0:T(1,128)S(1)} %get-tuple-element.70.inverse_rms, f32[1,2048]{1,0:T(1,128)S(1)} %bitcast.16, bf16[256,2048]{1,0:T(8,128)(2,1)S(1)} %get-tuple-element.52.keys, ...), custom_call_target="tpu_custom_call" | custom-call | flops 671088640 | bytes 7874560 | tf_op jit(solution)/shard_map/pallas_call | solution.py:378
  36.9 3.7 %shard_map.111 = (bf16[256,2048]{1,0:T(8,128)(2,1)}, bf16[256,2048]{1,0:T(8,128)(2,1)}, f32[256,2048]{1,0:T(8,128)S(1)}, f32[256,2048]{1,0:T(8,128)S(1)}, f32[8,128]{1,0:T(8,128)S(1)}) custom-call(s32[1,256]{1,0:T(1,128)S(1)} %get-tuple-element.50.length, bf16[256,2048]{1,0:T(8,128)(2,1)S(1)} %shard_map.103.refs_4_.queries, ...), custom_call_target="tpu_custom_call" | custom-call | flops 1073741824 | bytes 12588032 | tf_op jit(solution)/shard_map/pallas_call | solution.py:378
  40.6 0.0 collective-permute-done.15.refs_1_
  40.6 0.1 collective-permute-done.16.refs_2_
  40.7 0.0 collective-permute-done.17.refs_3_
  40.7 0.3 shard_map.112
  41.0 1.6 %collective-permute-start.21 = (bf16[512,128]{1,0:T(8,128)(2,1)S(1)}, bf16[512,128]{1,0:T(8,128)(2,1)S(1)}, u32[]{:S(2)}, u32[]{:S(2)}) collective-permute-start(bf16[512,128]{1,0:T(8,128)(2,1)S(1)} %get-tuple-element.89), channel_id=1, source_target_pairs={{0,4},{1,3},{2,6},{3,1},{4,0},{5,7},{6,2},{7,5},{8,12},{9,11},{10,... | collective-permute-start | bytes 393224 | tf_op jit(solution)/shard_map/ppermute | solution.py:400
  42.6 0.7 %collective-permute-start.22 = (bf16[512,128]{1,0:T(8,128)(2,1)S(1)}, bf16[512,128]{1,0:T(8,128)(2,1)S(1)}, u32[]{:S(2)}, u32[]{:S(2)}) collective-permute-start(bf16[512,128]{1,0:T(8,128)(2,1)S(1)} %get-tuple-element.90), channel_id=1, source_target_pairs={{0,5},{1,2},{2,7},{3,0},{4,1},{5,6},{6,3},{7,4},{8,13},{9,10},{10,... | collective-permute-start | bytes 393224 | tf_op jit(solution)/shard_map/ppermute | solution.py:400
  43.2 0.9 %collective-permute-start.23 = (bf16[512,128]{1,0:T(8,128)(2,1)S(1)}, bf16[512,128]{1,0:T(8,128)(2,1)S(1)}, u32[]{:S(2)}, u32[]{:S(2)}) collective-permute-start(bf16[512,128]{1,0:T(8,128)(2,1)S(1)} %get-tuple-element.91), channel_id=1, source_target_pairs={{0,1},{1,0},{2,3},{3,2},{4,5},{5,4},{6,7},{7,6},{8,9},{9,8},{10,11... | collective-permute-start | bytes 393224 | tf_op jit(solution)/shard_map/ppermute | solution.py:400
  44.1 0.3 shard_map.113
  44.4 0.6 %collective-permute-start.18 = (bf16[512,128]{1,0:T(8,128)(2,1)S(1)}, bf16[512,128]{1,0:T(8,128)(2,1)S(1)}, u32[]{:S(2)}, u32[]{:S(2)}) collective-permute-start(bf16[512,128]{1,0:T(8,128)(2,1)S(1)} %get-tuple-element.85), channel_id=1, source_target_pairs={{0,4},{1,3},{2,6},{3,1},{4,0},{5,7},{6,2},{7,5},{8,12},{9,11},{10,... | collective-permute-start | bytes 393224 | tf_op jit(solution)/shard_map/ppermute | solution.py:400
  45.0 0.0 collective-permute-start.19
  45.0 1.0 %collective-permute-done.21.rest_0_ = bf16[512,128]{1,0:T(8,128)(2,1)S(1)} collective-permute-done((bf16[512,128]{1,0:T(8,128)(2,1)S(1)}, bf16[512,128]{1,0:T(8,128)(2,1)S(1)}, u32[]{:S(2)}, u32[]{:S(2)}) %collective-permute-start.21) | collective-permute-done | bytes 131104 | tf_op jit(solution)/shard_map/ppermute | solution.py:400
  46.0 0.0 collective-permute-start.20
  46.0 0.9 %collective-permute-done.22.rest_2_ = bf16[512,128]{1,0:T(8,128)(2,1)S(1)} collective-permute-done((bf16[512,128]{1,0:T(8,128)(2,1)S(1)}, bf16[512,128]{1,0:T(8,128)(2,1)S(1)}, u32[]{:S(2)}, u32[]{:S(2)}) %collective-permute-start.22) | collective-permute-done | bytes 131104 | tf_op jit(solution)/shard_map/ppermute | solution.py:400
  47.0 0.0 collective-permute-done.23.rest_3_
  47.0 1.6 %shard_map.114 = (bf16[256,2048]{1,0:T(8,128)(2,1)}, bf16[256,2048]{1,0:T(8,128)(2,1)}) custom-call(s32[1,256]{1,0:T(1,128)S(1)} %get-tuple-element.50.length, bf16[256,2048]{1,0:T(8,128)(2,1)S(1)} %get-tuple-element.52.keys, bf16[256,2048]{1,0:T(8,128)(2,1)S(1)} %get-tuple-element.53.values, f32[256,2048]{1,0:T(8,128)S(1)} %get-tuple-element.78.key_part, ...), custom_call_target="tpu_custom_call" | custom-call | flops 134217728 | bytes 8913920 | tf_op jit(solution)/shard_map/pallas_call | solution.py:378
  48.6 0.9 %collective-permute-done.18.rest_0_ = bf16[512,128]{1,0:T(8,128)(2,1)S(1)} collective-permute-done((bf16[512,128]{1,0:T(8,128)(2,1)S(1)}, bf16[512,128]{1,0:T(8,128)(2,1)S(1)}, u32[]{:S(2)}, u32[]{:S(2)}) %collective-permute-start.18) | collective-permute-done | bytes 131104 | tf_op jit(solution)/shard_map/ppermute | solution.py:400
  49.5 0.4 collective-permute-done.19.rest_2_
  49.9 0.0 collective-permute-done.20.rest_3_
  49.9 1.6 %shard_map.115 = (bf16[256,2048]{1,0:T(8,128)(2,1)}, bf16[256,2048]{1,0:T(8,128)(2,1)}) custom-call(s32[1,256]{1,0:T(1,128)S(1)} %get-tuple-element.50.length, bf16[256,2048]{1,0:T(8,128)(2,1)S(1)} %get-tuple-element.52.keys, bf16[256,2048]{1,0:T(8,128)(2,1)S(1)} %get-tuple-element.53.values, ...), custom_call_target="tpu_custom_call", output_to_operand_aliasing={{0}: (9, {}), {1}: (10, {})} | custom-call | flops 134217728 | bytes 11011072 | tf_op jit(solution)/shard_map/pallas_call | solution.py:378
  (2 shorter events, 0.0 us)
Async XLA Ops:
  3.6 6.8 %collective-permute-start = (bf16[512,128]{1,0:T(8,128)(2,1)S(1)}, bf16[512,128]{1,0:T(8,128)(2,1)S(1)}, u32[]{:S(2)}, u32[]{:S(2)}) collective-permute-start(bf16[512,128]{1,0:T(8,128)(2,1)S(1)} %get-tuple-element.51._.refs_0_), channel_id=1, source_target_pairs={{0,2},{1,5},{2,0},{3,7},{4,6},{5,1},{6,4},{7,3},{8,10},{9,13},{10,... | collective-permute-start | bytes 393224 | tf_op jit(solution)/shard_map/ppermute | solution.py:400
  6.6 5.1 %collective-permute-start.1 = (bf16[512,128]{1,0:T(8,128)(2,1)S(1)}, bf16[512,128]{1,0:T(8,128)(2,1)S(1)}, u32[]{:S(2)}, u32[]{:S(2)}) collective-permute-start(bf16[512,128]{1,0:T(8,128)(2,1)S(1)} %get-tuple-element.55), channel_id=1, source_target_pairs={{0,5},{1,2},{2,7},{3,0},{4,1},{5,6},{6,3},{7,4},{8,13},{9,10},{10,... | collective-permute-start | bytes 393224 | tf_op jit(solution)/shard_map/ppermute | solution.py:400
  6.6 5.1 %collective-permute-start.2 = (bf16[512,128]{1,0:T(8,128)(2,1)S(1)}, bf16[512,128]{1,0:T(8,128)(2,1)S(1)}, u32[]{:S(2)}, u32[]{:S(2)}) collective-permute-start(bf16[512,128]{1,0:T(8,128)(2,1)S(1)} %get-tuple-element.55), channel_id=1, source_target_pairs={{0,1},{1,0},{2,3},{3,2},{4,5},{5,4},{6,7},{7,6},{8,9},{9,8},{10,11... | collective-permute-start | bytes 393224 | tf_op jit(solution)/shard_map/ppermute | solution.py:400
  6.8 6.6 %collective-permute-start.3 = (bf16[512,128]{1,0:T(8,128)(2,1)S(1)}, bf16[512,128]{1,0:T(8,128)(2,1)S(1)}, u32[]{:S(2)}, u32[]{:S(2)}) collective-permute-start(bf16[512,128]{1,0:T(8,128)(2,1)S(1)} %get-tuple-element.57.refs_0_), channel_id=1, source_target_pairs={{0,2},{1,5},{2,0},{3,7},{4,6},{5,1},{6,4},{7,3},{8,10},{9,13},{10,... | collective-permute-start | bytes 393224 | tf_op jit(solution)/shard_map/ppermute | solution.py:400
  8.8 6.4 %collective-permute-start.4 = (bf16[512,128]{1,0:T(8,128)(2,1)S(1)}, bf16[512,128]{1,0:T(8,128)(2,1)S(1)}, u32[]{:S(2)}, u32[]{:S(2)}) collective-permute-start(bf16[512,128]{1,0:T(8,128)(2,1)S(1)} %get-tuple-element.58), channel_id=1, source_target_pairs={{0,5},{1,2},{2,7},{3,0},{4,1},{5,6},{6,3},{7,4},{8,13},{9,10},{10,... | collective-permute-start | bytes 393224 | tf_op jit(solution)/shard_map/ppermute | solution.py:400
  10.4 4.8 %collective-permute-start.5 = (bf16[512,128]{1,0:T(8,128)(2,1)S(1)}, bf16[512,128]{1,0:T(8,128)(2,1)S(1)}, u32[]{:S(2)}, u32[]{:S(2)}) collective-permute-start(bf16[512,128]{1,0:T(8,128)(2,1)S(1)} %get-tuple-element.58), channel_id=1, source_target_pairs={{0,1},{1,0},{2,3},{3,2},{4,5},{5,4},{6,7},{7,6},{8,9},{9,8},{10,11... | collective-permute-start | bytes 393224 | tf_op jit(solution)/shard_map/ppermute | solution.py:400
  12.0 4.5 %collective-permute-start.10 = (bf16[512,128]{1,0:T(8,128)(2,1)S(1)}, bf16[512,128]{1,0:T(8,128)(2,1)S(1)}, u32[]{:S(2)}, u32[]{:S(2)}) collective-permute-start(bf16[512,128]{1,0:T(8,128)(2,1)S(1)} %get-tuple-element.64), channel_id=1, source_target_pairs={{0,5},{1,2},{2,7},{3,0},{4,1},{5,6},{6,3},{7,4},{8,13},{9,10},{10,... | collective-permute-start | bytes 393224 | tf_op jit(solution)/shard_map/ppermute | solution.py:400
  12.6 6.7 %collective-permute-start.11 = (bf16[512,128]{1,0:T(8,128)(2,1)S(1)}, bf16[512,128]{1,0:T(8,128)(2,1)S(1)}, u32[]{:S(2)}, u32[]{:S(2)}) collective-permute-start(bf16[512,128]{1,0:T(8,128)(2,1)S(1)} %get-tuple-element.65), channel_id=1, source_target_pairs={{0,1},{1,0},{2,3},{3,2},{4,5},{5,4},{6,7},{7,6},{8,9},{9,8},{10,11... | collective-permute-start | bytes 393224 | tf_op jit(solution)/shard_map/ppermute | solution.py:400
  13.4 5.9 %collective-permute-start.9 = (bf16[512,128]{1,0:T(8,128)(2,1)S(1)}, bf16[512,128]{1,0:T(8,128)(2,1)S(1)}, u32[]{:S(2)}, u32[]{:S(2)}) collective-permute-start(bf16[512,128]{1,0:T(8,128)(2,1)S(1)} %get-tuple-element.63), channel_id=1, source_target_pairs={{0,4},{1,3},{2,6},{3,1},{4,0},{5,7},{6,2},{7,5},{8,12},{9,11},{10,... | collective-permute-start | bytes 393224 | tf_op jit(solution)/shard_map/ppermute | solution.py:400
  15.5 5.0 %collective-permute-start.6 = (bf16[512,128]{1,0:T(8,128)(2,1)S(1)}, bf16[512,128]{1,0:T(8,128)(2,1)S(1)}, u32[]{:S(2)}, u32[]{:S(2)}) collective-permute-start(bf16[512,128]{1,0:T(8,128)(2,1)S(1)} %get-tuple-element.59), channel_id=1, source_target_pairs={{0,4},{1,3},{2,6},{3,1},{4,0},{5,7},{6,2},{7,5},{8,12},{9,11},{10,... | collective-permute-start | bytes 393224 | tf_op jit(solution)/shard_map/ppermute | solution.py:400
  16.2 4.8 %collective-permute-start.7 = (bf16[512,128]{1,0:T(8,128)(2,1)S(1)}, bf16[512,128]{1,0:T(8,128)(2,1)S(1)}, u32[]{:S(2)}, u32[]{:S(2)}) collective-permute-start(bf16[512,128]{1,0:T(8,128)(2,1)S(1)} %get-tuple-element.61), channel_id=1, source_target_pairs={{0,5},{1,2},{2,7},{3,0},{4,1},{5,6},{6,3},{7,4},{8,13},{9,10},{10,... | collective-permute-start | bytes 393224 | tf_op jit(solution)/shard_map/ppermute | solution.py:400
  16.5 4.5 %collective-permute-start.8 = (bf16[512,128]{1,0:T(8,128)(2,1)S(1)}, bf16[512,128]{1,0:T(8,128)(2,1)S(1)}, u32[]{:S(2)}, u32[]{:S(2)}) collective-permute-start(bf16[512,128]{1,0:T(8,128)(2,1)S(1)} %get-tuple-element.62), channel_id=1, source_target_pairs={{0,1},{1,0},{2,3},{3,2},{4,5},{5,4},{6,7},{7,6},{8,9},{9,8},{10,11... | collective-permute-start | bytes 393224 | tf_op jit(solution)/shard_map/ppermute | solution.py:400
  17.8 1.5 %copy-start = (bf16[1,256,2048]{2,1,0:T(8,128)(2,1)S(1)}, bf16[1,256,2048]{2,1,0:T(8,128)(2,1)}, u32[]{:S(2)}) copy-start(bf16[1,256,2048]{2,1,0:T(8,128)(2,1)} %param.10) | copy-start | bytes 3145732
  17.8 1.5 %copy-start.1 = (f32[2048]{0:T(1024)S(1)}, f32[2048]{0:T(1024)}, u32[]{:S(2)}) copy-start(f32[2048]{0:T(1024)} %param.11) | copy-start | bytes 24580
  21.7 4.4 %collective-permute-start.12 = (f32[2,256]{1,0:T(2,128)S(1)}, f32[2,256]{1,0:T(2,128)S(1)}, u32[]{:S(2)}, u32[]{:S(2)}) collective-permute-start(f32[2,256]{1,0:T(2,128)S(1)} %get-tuple-element.67.rest_0_), channel_id=1, source_target_pairs={{0,8},{8,0},{16,24},{24,16},{1,9},{9,1},{17,25},{25,17},{2,10},{10... | collective-permute-start | bytes 6152 | tf_op jit(solution)/shard_map/ppermute | solution.py:427
  23.4 5.4 %collective-permute-start.13 = (f32[2,256]{1,0:T(2,128)S(1)}, f32[2,256]{1,0:T(2,128)S(1)}, u32[]{:S(2)}, u32[]{:S(2)}) collective-permute-start(f32[2,256]{1,0:T(2,128)S(1)} %get-tuple-element.67.rest_0_), channel_id=1, source_target_pairs={{0,24},{8,16},{16,8},{24,0},{1,25},{9,17},{17,9},{25,1},{2,26},{10... | collective-permute-start | bytes 6152 | tf_op jit(solution)/shard_map/ppermute | solution.py:427
  25.9 4.5 %collective-permute-start.14 = (f32[2,256]{1,0:T(2,128)S(1)}, f32[2,256]{1,0:T(2,128)S(1)}, u32[]{:S(2)}, u32[]{:S(2)}) collective-permute-start(f32[2,256]{1,0:T(2,128)S(1)} %get-tuple-element.67.rest_0_), channel_id=1, source_target_pairs={{0,16},{8,24},{16,0},{24,8},{1,17},{9,25},{17,1},{25,9},{2,18},{10... | collective-permute-start | bytes 6152 | tf_op jit(solution)/shard_map/ppermute | solution.py:427
  31.5 9.1 %collective-permute-start.15 = (bf16[1024,128]{1,0:T(8,128)(2,1)S(1)}, bf16[1024,128]{1,0:T(8,128)(2,1)S(1)}, u32[]{:S(2)}, u32[]{:S(2)}) collective-permute-start(bf16[1024,128]{1,0:T(8,128)(2,1)S(1)} %get-tuple-element.81.refs_0_), channel_id=1, source_target_pairs={{0,2},{1,5},{2,0},{3,7},{4,6},{5,1},{6,4},{7,3},{8,10},{9,13},{10,... | collective-permute-start | bytes 786440 | tf_op jit(solution)/shard_map/ppermute | solution.py:400
  33.0 7.7 %collective-permute-start.16 = (bf16[1024,128]{1,0:T(8,128)(2,1)S(1)}, bf16[1024,128]{1,0:T(8,128)(2,1)S(1)}, u32[]{:S(2)}, u32[]{:S(2)}) collective-permute-start(bf16[1024,128]{1,0:T(8,128)(2,1)S(1)} %get-tuple-element.82), channel_id=1, source_target_pairs={{0,5},{1,2},{2,7},{3,0},{4,1},{5,6},{6,3},{7,4},{8,13},{9,10},{10,... | collective-permute-start | bytes 786440 | tf_op jit(solution)/shard_map/ppermute | solution.py:400
  33.0 7.7 %collective-permute-start.17 = (bf16[1024,128]{1,0:T(8,128)(2,1)S(1)}, bf16[1024,128]{1,0:T(8,128)(2,1)S(1)}, u32[]{:S(2)}, u32[]{:S(2)}) collective-permute-start(bf16[1024,128]{1,0:T(8,128)(2,1)S(1)} %get-tuple-element.82), channel_id=1, source_target_pairs={{0,1},{1,0},{2,3},{3,2},{4,5},{5,4},{6,7},{7,6},{8,9},{9,8},{10,11... | collective-permute-start | bytes 786440 | tf_op jit(solution)/shard_map/ppermute | solution.py:400
  41.0 5.0 %collective-permute-start.21 = (bf16[512,128]{1,0:T(8,128)(2,1)S(1)}, bf16[512,128]{1,0:T(8,128)(2,1)S(1)}, u32[]{:S(2)}, u32[]{:S(2)}) collective-permute-start(bf16[512,128]{1,0:T(8,128)(2,1)S(1)} %get-tuple-element.89), channel_id=1, source_target_pairs={{0,4},{1,3},{2,6},{3,1},{4,0},{5,7},{6,2},{7,5},{8,12},{9,11},{10,... | collective-permute-start | bytes 393224 | tf_op jit(solution)/shard_map/ppermute | solution.py:400
  42.6 4.4 %collective-permute-start.22 = (bf16[512,128]{1,0:T(8,128)(2,1)S(1)}, bf16[512,128]{1,0:T(8,128)(2,1)S(1)}, u32[]{:S(2)}, u32[]{:S(2)}) collective-permute-start(bf16[512,128]{1,0:T(8,128)(2,1)S(1)} %get-tuple-element.90), channel_id=1, source_target_pairs={{0,5},{1,2},{2,7},{3,0},{4,1},{5,6},{6,3},{7,4},{8,13},{9,10},{10,... | collective-permute-start | bytes 393224 | tf_op jit(solution)/shard_map/ppermute | solution.py:400
  43.2 3.7 %collective-permute-start.23 = (bf16[512,128]{1,0:T(8,128)(2,1)S(1)}, bf16[512,128]{1,0:T(8,128)(2,1)S(1)}, u32[]{:S(2)}, u32[]{:S(2)}) collective-permute-start(bf16[512,128]{1,0:T(8,128)(2,1)S(1)} %get-tuple-element.91), channel_id=1, source_target_pairs={{0,1},{1,0},{2,3},{3,2},{4,5},{5,4},{6,7},{7,6},{8,9},{9,8},{10,11... | collective-permute-start | bytes 393224 | tf_op jit(solution)/shard_map/ppermute | solution.py:400
  44.4 5.0 %collective-permute-start.18 = (bf16[512,128]{1,0:T(8,128)(2,1)S(1)}, bf16[512,128]{1,0:T(8,128)(2,1)S(1)}, u32[]{:S(2)}, u32[]{:S(2)}) collective-permute-start(bf16[512,128]{1,0:T(8,128)(2,1)S(1)} %get-tuple-element.85), channel_id=1, source_target_pairs={{0,4},{1,3},{2,6},{3,1},{4,0},{5,7},{6,2},{7,5},{8,12},{9,11},{10,... | collective-permute-start | bytes 393224 | tf_op jit(solution)/shard_map/ppermute | solution.py:400
  45.0 4.9 %collective-permute-start.19 = (bf16[512,128]{1,0:T(8,128)(2,1)S(1)}, bf16[512,128]{1,0:T(8,128)(2,1)S(1)}, u32[]{:S(2)}, u32[]{:S(2)}) collective-permute-start(bf16[512,128]{1,0:T(8,128)(2,1)S(1)} %get-tuple-element.87), channel_id=1, source_target_pairs={{0,5},{1,2},{2,7},{3,0},{4,1},{5,6},{6,3},{7,4},{8,13},{9,10},{10,... | collective-permute-start | bytes 393224 | tf_op jit(solution)/shard_map/ppermute | solution.py:400
  46.0 3.9 %collective-permute-start.20 = (bf16[512,128]{1,0:T(8,128)(2,1)S(1)}, bf16[512,128]{1,0:T(8,128)(2,1)S(1)}, u32[]{:S(2)}, u32[]{:S(2)}) collective-permute-start(bf16[512,128]{1,0:T(8,128)(2,1)S(1)} %get-tuple-element.88), channel_id=1, source_target_pairs={{0,1},{1,0},{2,3},{3,2},{4,5},{5,4},{6,7},{7,6},{8,9},{9,8},{10,11... | collective-permute-start | bytes 393224 | tf_op jit(solution)/shard_map/ppermute | solution.py:400

commit v9 on v8

--- a/solution.py
+++ b/solution.py
@@ -176,9 +176,8 @@
     write_halves(full, outs, my_place(grid)[2], grid[2])
 
 
-def mix_kernel(sources, pair, first, weights, *refs):
+def mix_kernel(sources, first, weights, *refs):
     blocks, outs = refs[:sources], refs[-sources:]
-    blocks = blocks[:1] + blocks[sources - pair + 1 :] + blocks[1 : sources - pair + 1]
     rows = outs[0].shape[0]
     chunk = min(rows, 64)
     for start in range(0, rows, chunk):
@@ -292,12 +291,29 @@
     write_halves(full, halves, my_place(grid)[2], grid[2])
 
 
-def query_kernel(heads, scale, length, inverse_rms, gain, keys, values, *rest):
+def row_copies(source, target, sems):
+    rows = target.shape[0]
+    chunk = rows // 4 if rows % 64 == 0 else rows
+    parts = [pl.ds(step * chunk, chunk) for step in range(rows // chunk)]
+    return [pltpu.make_async_copy(source.at[p, :], target.at[p, :], sems.at[j]) for j, p in enumerate(parts)]
+
+
+def column_copies(sources, targets, first, count, sems):
+    cols = slice(first * HD, (first + count) * HD)
+    return [
+        pltpu.make_async_copy(src.at[:, cols], dst.at[:, cols], sems.at[j])
+        for j, (src, dst) in enumerate(zip(sources, targets))
+    ]
+
+
+def query_kernel(heads, group, scale, length, inverse_rms, gain, queries, keys, values, *rest):
     sizes = (BACKWARD_PIECES, FORWARD_PIECES, FORWARD_PIECES)
     grads, attention, prefix, rest = split_refs(rest, *sizes, len(rest) - sum(sizes))
-    attended, query_grad = rest[-2:]
+    attended_hbm, query_hbm, attended, query_grad, key_part, token, sems = rest
+    token[...] = jnp.zeros_like(token)
     keep = keep_mask(length, False)
     inverse = token_columns(inverse_rms[...])
+    copies = []
     for head in range(heads):
         cols = head_cols(head)
         grad_piece, at = head_of(grads, head)
@@ -308,31 +324,31 @@
         grad_scores = jnp.where(keep, nt(grad, values[:, cols]), 0.0).astype(BF16)
         carried = nt(grad, prefix_piece[state * HD : (state + 1) * HD, :])
         query_grad[:, cols] = (scale * (carried + nn(grad_scores, keys[:, cols]))).astype(BF16)
+        key_part[:, cols] = scale * tn(grad_scores, queries[:, cols])
         attended[:, cols] = (out_piece[:, at] * inverse * gain[:, cols]).astype(BF16)
-
-
-def row_copies(source, target, sems):
-    rows = target.shape[0]
-    chunk = rows // 4 if rows % 64 == 0 else rows
-    parts = [pl.ds(step * chunk, chunk) for step in range(rows // chunk)]
-    return [pltpu.make_async_copy(source.at[p, :], target.at[p, :], sems.at[j]) for j, p in enumerate(parts)]
-
-
-def back_kernel(heads, scale, length, queries, keys, values, attended, query_grad, *rest):
-    grads, (attended_hbm, query_hbm, key_part, value_part, token, sems) = rest[:BACKWARD_PIECES], rest[-6:]
-    copies = row_copies(attended, attended_hbm, sems.at[0]) + row_copies(query_grad, query_hbm, sems.at[1])
+        if (head + 1) % group == 0 and head + 1 < heads:
+            step = head // group
+            some = column_copies(
+                (attended, query_grad), (attended_hbm, query_hbm), step * group, group, sems.at[step]
+            )
+            for copy in some:
+                copy.start()
+            copies += some
+    for copy in copies:
+        copy.wait()
+
+
+def value_kernel(heads, group, scale, length, queries, keys, attended, query_grad, *rest):
+    grads, (attended_hbm, query_hbm, value_part, sems) = rest[:BACKWARD_PIECES], rest[-4:]
+    copies = column_copies((attended, query_grad), (attended_hbm, query_hbm), heads - group, group, sems)
     for copy in copies:
         copy.start()
-    token[...] = jnp.zeros_like(token)
     keep = keep_mask(length, True)
     for head in range(heads):
         cols = head_cols(head)
         grad_piece, at = head_of(grads, head)
-        query, grad = queries[:, cols], grad_piece[:, at]
-        turned = jnp.where(keep, nt(values[:, cols], grad), 0.0).astype(BF16)
-        key_part[:, cols] = scale * nn(turned, query)
-        turned = jnp.where(keep, nt(keys[:, cols], query), 0.0).astype(BF16)
-        value_part[:, cols] = scale * nn(turned, grad)
+        turned = jnp.where(keep, nt(keys[:, cols], queries[:, cols]), 0.0).astype(BF16)
+        value_part[:, cols] = scale * nn(turned, grad_piece[:, at])
     for copy in copies:
         copy.wait()
 
@@ -452,8 +468,7 @@
     def mix(arrived, weights, piece, pieces, after=()):
         tall = arrived[0].shape[0] // pieces
         like = [shape((tall, HD), BF16)] * members
-        arrived = arrived[:1] + arrived[pair:] + arrived[1:pair]
-        return call(functools.partial(mix_kernel, members, pair, piece * tall), like, (weights, *arrived), after=after)
+        return call(functools.partial(mix_kernel, members, piece * tall), like, (weights, *arrived), after=after)
 
     def flat(parts):
         return [block for part in parts for block in part]
@@ -497,23 +512,26 @@
         )
         grads.append(grad_out)
         state_grad.append(parts)
-    attended, query_grad = call(
-        functools.partial(query_kernel, heads, scale),
-        [narrow, narrow],
-        (length, inverse_rms, gain, key, value, *grads, *attention, *prefix),
-        (), unit * (2 * rows + HD),
-    )
-    attended, query_grad, key_part, value_part, token = call(
-        functools.partial(back_kernel, heads, scale),
-        [narrow, narrow, wide, wide, shape((8, HD), F32)],
-        (length, query, key, value, attended, query_grad, *grads), [pltpu.SemaphoreType.DMA((2, 4))],
-        unit * 4 * rows, out_specs=[HBM, HBM, VMEM, VMEM, VMEM],
+    group = 4 if heads % 4 == 0 else 1
+    attended, query_grad, attended_rest, query_rest, key_part, token = call(
+        functools.partial(query_kernel, heads, group, scale),
+        [narrow, narrow, narrow, narrow, wide, shape((8, HD), F32)],
+        (length, inverse_rms, gain, query, key, value, *grads, *attention, *prefix),
+        [pltpu.SemaphoreType.DMA((heads // group, 2))], unit * (3 * rows + HD),
+        out_specs=[HBM, HBM] + [VMEM] * 4,
     )
     (part,) = state_grad
     arrived = gather_line(part, grid)
     mixed = []
     for piece in range(RETURN_PIECES):
         mixed.append(mix(arrived, down, piece, RETURN_PIECES, (token, *mixed[-1][:1]) if mixed else (token,)))
+    operands = (length, query, key, attended_rest, query_rest, *grads, attended, query_grad)
+    last = len(operands) - 2
+    attended, query_grad, value_part = call(
+        functools.partial(value_kernel, heads, group, scale),
+        [narrow, narrow, wide], operands, [pltpu.SemaphoreType.DMA((2,))], unit * 2 * rows, (last, last + 1),
+        after=(mixed[-1][0],), out_specs=[HBM, HBM, VMEM], aliases={last: 0, last + 1: 1},
+    )
     results = []
     width = features // RETURN_PIECES
     for piece in range(RETURN_PIECES):

time: 52.2 us -> 50.2 us (0.962)
  waiting for transfers between devices: 10.4 us -> 9.2 us
    ppermute x21, waiting for transfers between devices: 6.08 us -> 5.39 us  [line_send(): return lax.ppermute(block, 'seg', moves)]
    ppermute x3, waiting for transfers between devices: 4.36 us -> 3.8 us  [token_sums(): parts.append(lax.ppermute(sums, 'head', moves))]
  transfers between devices with their start and end apart: 24 -> 24, of which waited for: 11 -> 10; matrix products, arithmetic and copies ran while one was open for 0% -> 0% of each run, Pallas kernels for 25% -> 25%
where the time goes in v9:
time: 50.2 us; the launch traced here: 50 us
  starting transfers between devices  20.8 us (41%)
  Pallas kernels  18.4 us (37%)
  waiting for transfers between devices  9.2 us (18%)
  between operations  1.61 us (3%)
    pallas_call x14, Pallas kernels, call(): pl.pallas_call(kernel, out_shape=out_shape, in_specs=specs + [ANY] * len(...  18.4 us
    ppermute x21, starting transfers between devices, line_send(): return lax.ppermute(block, 'seg', moves)  16.5 us
    ppermute x21, waiting for transfers between devices, line_send(): return lax.ppermute(block, 'seg', moves)  5.39 us
    ppermute x3, starting transfers between devices, token_sums(): parts.append(lax.ppermute(sums, 'head', moves))  4.23 us
    ppermute x3, waiting for transfers between devices, token_sums(): parts.append(lax.ppermute(sums, 'head', moves))  3.8 us
  transfers between devices with their start and end apart: 24, of which 10 were waited for; matrix products, arithmetic and copies ran while one was open for 0% of the time, Pallas kernels for 25%

profile of v9, /device:TPU:0, one launch (start us, length us, event | category | flops | bytes accessed | tf_op | source)
XLA Modules:
  0.0 50.0 jit_solution(2376375288443982367)
XLA Ops:
  1.3 2.3 %shard_map.102 = (bf16[256,2048]{1,0:T(8,128)(2,1)S(1)}, bf16[256,2048]{1,0:T(8,128)(2,1)S(1)}, s32[1,256]{1,0:T(1,128)S(1)}, f32[16,128]{1,0:T(8,128)S(1)}, f32...) custom-call(s32[1]{0:T(128)S(6)} %copy.19.seg_len, ...), custom_call_target="tpu_custom_call" | custom-call | flops 134217728 | bytes 4736036 | tf_op jit(solution)/shard_map/pallas_call | solution.py:394
  3.6 2.5 %collective-permute-start.2 = (bf16[512,128]{1,0:T(8,128)(2,1)S(1)}, bf16[512,128]{1,0:T(8,128)(2,1)S(1)}, u32[]{:S(2)}, u32[]{:S(2)}) collective-permute-start(bf16[512,128]{1,0:T(8,128)(2,1)S(1)} %get-tuple-element.57), channel_id=1, source_target_pairs={{0,5},{1,2},{2,7},{3,0},{4,1},{5,6},{6,3},{7,4},{8,13},{9,10},{10,... | collective-permute-start | bytes 393224 | tf_op jit(solution)/shard_map/ppermute | solution.py:416
  6.1 0.6 %collective-permute-start = (bf16[512,128]{1,0:T(8,128)(2,1)S(1)}, bf16[512,128]{1,0:T(8,128)(2,1)S(1)}, u32[]{:S(2)}, u32[]{:S(2)}) collective-permute-start(bf16[512,128]{1,0:T(8,128)(2,1)S(1)} %get-tuple-element.57), channel_id=1, source_target_pairs={{0,1},{1,0},{2,3},{3,2},{4,5},{5,4},{6,7},{7,6},{8,9},{9,8},{10,11... | collective-permute-start | bytes 393224 | tf_op jit(solution)/shard_map/ppermute | solution.py:416
  6.7 0.9 %collective-permute-start.1 = (bf16[512,128]{1,0:T(8,128)(2,1)S(1)}, bf16[512,128]{1,0:T(8,128)(2,1)S(1)}, u32[]{:S(2)}, u32[]{:S(2)}) collective-permute-start(bf16[512,128]{1,0:T(8,128)(2,1)S(1)} %get-tuple-element.53._.refs_0_), channel_id=1, source_target_pairs={{0,2},{1,5},{2,0},{3,7},{4,6},{5,1},{6,4},{7,3},{8,10},{9,13},{10,... | collective-permute-start | bytes 393224 | tf_op jit(solution)/shard_map/ppermute | solution.py:416
  7.6 1.2 %collective-permute-start.4 = (bf16[512,128]{1,0:T(8,128)(2,1)S(1)}, bf16[512,128]{1,0:T(8,128)(2,1)S(1)}, u32[]{:S(2)}, u32[]{:S(2)}) collective-permute-start(bf16[512,128]{1,0:T(8,128)(2,1)S(1)} %get-tuple-element.59.refs_0_), channel_id=1, source_target_pairs={{0,2},{1,5},{2,0},{3,7},{4,6},{5,1},{6,4},{7,3},{8,10},{9,13},{10,... | collective-permute-start | bytes 393224 | tf_op jit(solution)/shard_map/ppermute | solution.py:416
  8.8 0.6 %collective-permute-start.5 = (bf16[512,128]{1,0:T(8,128)(2,1)S(1)}, bf16[512,128]{1,0:T(8,128)(2,1)S(1)}, u32[]{:S(2)}, u32[]{:S(2)}) collective-permute-start(bf16[512,128]{1,0:T(8,128)(2,1)S(1)} %get-tuple-element.60), channel_id=1, source_target_pairs={{0,5},{1,2},{2,7},{3,0},{4,1},{5,6},{6,3},{7,4},{8,13},{9,10},{10,... | collective-permute-start | bytes 393224 | tf_op jit(solution)/shard_map/ppermute | solution.py:416
  9.3 1.2 %shard_map.103.refs_4_.queries = bf16[256,2048]{1,0:T(8,128)(2,1)S(1)} custom-call(bf16[256,2048]{1,0:T(8,128)(2,1)} %bitcast.19, bf16[512,128]{1,0:T(8,128)(2,1)S(1)} %get-tuple-element.53._.refs_0_), custom_call_target="tpu_custom_call" | custom-call | bytes 2097152 | tf_op jit(solution)/shard_map/pallas_call | solution.py:394
  10.6 0.0 collective-permute-done.2.refs_3_
  10.6 0.5 collective-permute-start.3
  11.1 0.0 collective-permute-done.refs_1_
  11.1 0.6 %collective-permute-done.1.refs_2_ = bf16[512,128]{1,0:T(8,128)(2,1)S(1)} collective-permute-done((bf16[512,128]{1,0:T(8,128)(2,1)S(1)}, bf16[512,128]{1,0:T(8,128)(2,1)S(1)}, u32[]{:S(2)}, u32[]{:S(2)}) %collective-permute-start.1) | collective-permute-done | bytes 131104 | tf_op jit(solution)/shard_map/ppermute | solution.py:416
  11.7 0.3 shard_map.104
  12.0 1.6 %collective-permute-start.9 = (bf16[512,128]{1,0:T(8,128)(2,1)S(1)}, bf16[512,128]{1,0:T(8,128)(2,1)S(1)}, u32[]{:S(2)}, u32[]{:S(2)}) collective-permute-start(bf16[512,128]{1,0:T(8,128)(2,1)S(1)} %get-tuple-element.65), channel_id=1, source_target_pairs={{0,4},{1,3},{2,6},{3,1},{4,0},{5,7},{6,2},{7,5},{8,12},{9,11},{10,... | collective-permute-start | bytes 393224 | tf_op jit(solution)/shard_map/ppermute | solution.py:416
  13.6 0.4 collective-permute-start.10
  14.0 0.4 collective-permute-done.4.refs_2_
  14.4 0.1 collective-permute-start.11
  14.5 0.0 collective-permute-done.5.refs_3_
  14.5 0.0 collective-permute-done.3.refs_1_
  14.5 0.3 shard_map.106
  14.8 1.6 %collective-permute-start.6 = (bf16[512,128]{1,0:T(8,128)(2,1)S(1)}, bf16[512,128]{1,0:T(8,128)(2,1)S(1)}, u32[]{:S(2)}, u32[]{:S(2)}) collective-permute-start(bf16[512,128]{1,0:T(8,128)(2,1)S(1)} %get-tuple-element.61), channel_id=1, source_target_pairs={{0,4},{1,3},{2,6},{3,1},{4,0},{5,7},{6,2},{7,5},{8,12},{9,11},{10,... | collective-permute-start | bytes 393224 | tf_op jit(solution)/shard_map/ppermute | solution.py:416
  16.4 0.6 %collective-permute-start.7 = (bf16[512,128]{1,0:T(8,128)(2,1)S(1)}, bf16[512,128]{1,0:T(8,128)(2,1)S(1)}, u32[]{:S(2)}, u32[]{:S(2)}) collective-permute-start(bf16[512,128]{1,0:T(8,128)(2,1)S(1)} %get-tuple-element.63), channel_id=1, source_target_pairs={{0,5},{1,2},{2,7},{3,0},{4,1},{5,6},{6,3},{7,4},{8,13},{9,10},{10,... | collective-permute-start | bytes 393224 | tf_op jit(solution)/shard_map/ppermute | solution.py:416
  16.9 0.1 collective-permute-done.9.rest_0_
  17.0 0.3 collective-permute-start.8
  17.3 1.5 %shard_map.105.local = f32[256,2048]{1,0:T(8,128)S(1)} custom-call(s32[1,256]{1,0:T(1,128)S(1)} %get-tuple-element.52.length, bf16[256,2048]{1,0:T(8,128)(2,1)S(1)} %shard_map.103.refs_4_.queries, bf16[256,2048]{1,0:T(8,128)(2,1)S(1)} %get-tuple-element.54.keys, bf16[256,2048]{1,0:T(8,128)(2,1)S(1)} %get-tuple-element.55.values, ...), custom_call_target="tpu_custom_call" | custom-call | flops 536870912 | bytes 5243904 | tf_op jit(solution)/shard_map/pallas_call | solution.py:394
  18.8 0.0 collective-permute-done.10.rest_2_
  18.8 0.0 collective-permute-done.11.rest_3_
  18.9 0.0 copy-done
  18.9 0.0 copy-done.1
  18.9 0.7 %shard_map.107 = (f32[256,1024]{1,0:T(8,128)S(1)}, f32[2,256]{1,0:T(2,128)S(1)}, bf16[1024,128]{1,0:T(8,128)(2,1)S(1)}) custom-call(s32[1,256]{1,0:T(1,128)S(1)} %get-tuple-element.52.length, bf16[256,2048]{1,0:T(8,128)(2,1)S(1)} %shard_map.103.refs_4_.queries, f32[256,2048]{1,0:T(8,128)S(1)} %shard_map.105.local, bf16[256,2048]{1,0:T(8,128)(2,1)S(1)} %bitcast.10, ...), custom_call_target="tpu_custom_call" | custom-call | flops 67108864 | bytes 6040576 | tf_op jit(solution)/shard_map/pallas_call | solution.py:394
  19.5 0.3 collective-permute-done.6.rest_0_
  19.8 0.9 %collective-permute-done.7.rest_2_ = bf16[512,128]{1,0:T(8,128)(2,1)S(1)} collective-permute-done((bf16[512,128]{1,0:T(8,128)(2,1)S(1)}, bf16[512,128]{1,0:T(8,128)(2,1)S(1)}, u32[]{:S(2)}, u32[]{:S(2)}) %collective-permute-start.7) | collective-permute-done | bytes 131104 | tf_op jit(solution)/shard_map/ppermute | solution.py:416
  20.8 0.0 collective-permute-done.8.rest_3_
  20.8 0.7 %shard_map.108 = (f32[256,1024]{1,0:T(8,128)S(1)}, f32[2,256]{1,0:T(2,128)S(1)}, bf16[1024,128]{1,0:T(8,128)(2,1)S(1)}) custom-call(s32[1,256]{1,0:T(1,128)S(1)} %get-tuple-element.52.length, bf16[256,2048]{1,0:T(8,128)(2,1)S(1)} %shard_map.103.refs_4_.queries, f32[256,2048]{1,0:T(8,128)S(1)} %shard_map.105.local, bf16[256,2048]{1,0:T(8,128)(2,1)S(1)} %bitcast.11, ...), custom_call_target="tpu_custom_call" | custom-call | flops 67108864 | bytes 6042624 | tf_op jit(solution)/shard_map/pallas_call | solution.py:394
  21.5 2.7 %collective-permute-start.14 = (f32[2,256]{1,0:T(2,128)S(1)}, f32[2,256]{1,0:T(2,128)S(1)}, u32[]{:S(2)}, u32[]{:S(2)}) collective-permute-start(f32[2,256]{1,0:T(2,128)S(1)} %get-tuple-element.69.rest_0_), channel_id=1, source_target_pairs={{0,16},{8,24},{16,0},{24,8},{1,17},{9,25},{17,1},{25,9},{2,18},{10... | collective-permute-start | bytes 6152 | tf_op jit(solution)/shard_map/ppermute | solution.py:443
  24.1 1.3 %collective-permute-start.13 = (f32[2,256]{1,0:T(2,128)S(1)}, f32[2,256]{1,0:T(2,128)S(1)}, u32[]{:S(2)}, u32[]{:S(2)}) collective-permute-start(f32[2,256]{1,0:T(2,128)S(1)} %get-tuple-element.69.rest_0_), channel_id=1, source_target_pairs={{0,24},{8,16},{16,8},{24,0},{1,25},{9,17},{17,9},{25,1},{2,26},{10... | collective-permute-start | bytes 6152 | tf_op jit(solution)/shard_map/ppermute | solution.py:443
  25.5 0.2 collective-permute-start.12
  25.7 0.3 collective-permute-done.14.rest_3_
  26.0 3.5 %collective-permute-done.13.rest_2_ = f32[2,256]{1,0:T(2,128)S(1)} collective-permute-done((f32[2,256]{1,0:T(2,128)S(1)}, f32[2,256]{1,0:T(2,128)S(1)}, u32[]{:S(2)}, u32[]{:S(2)}) %collective-permute-start.13) | collective-permute-done | bytes 2080 | tf_op jit(solution)/shard_map/ppermute | solution.py:443
  29.5 0.0 collective-permute-done.12.rest_1_
  29.5 1.0 %shard_map.109 = (bf16[256,2048]{1,0:T(8,128)(2,1)S(1)}, f32[1,256]{1,0:T(1,128)S(1)}, bf16[1024,128]{1,0:T(8,128)(2,1)S(1)}, bf16[1024,128]{1,0:T(8,128)(2,1)S(1)}) custom-call(s32[1,256]{1,0:T(1,128)S(1)} %get-tuple-element.52.length, bf16[256,2048]{1,0:T(8,128)(2,1)S(1)} %shard_map.103.refs_4_.queries, bf16[256,2048]{1,0:T(8,128)(2,1)S(1)} %bitcast.12, ...), custom_call_target="tpu_custom_call" | custom-call | flops 134217728 | bytes 5785600 | tf_op jit(solution)/shard_map/pallas_call | solution.py:394
  30.6 0.1 collective-permute-start.17
  30.6 1.0 %collective-permute-start.15 = (bf16[1024,128]{1,0:T(8,128)(2,1)S(1)}, bf16[1024,128]{1,0:T(8,128)(2,1)S(1)}, u32[]{:S(2)}, u32[]{:S(2)}) collective-permute-start(bf16[1024,128]{1,0:T(8,128)(2,1)S(1)} %get-tuple-element.82), channel_id=1, source_target_pairs={{0,1},{1,0},{2,3},{3,2},{4,5},{5,4},{6,7},{7,6},{8,9},{9,8},{10,11... | collective-permute-start | bytes 786440 | tf_op jit(solution)/shard_map/ppermute | solution.py:416
  31.6 1.2 %collective-permute-start.16 = (bf16[1024,128]{1,0:T(8,128)(2,1)S(1)}, bf16[1024,128]{1,0:T(8,128)(2,1)S(1)}, u32[]{:S(2)}, u32[]{:S(2)}) collective-permute-start(bf16[1024,128]{1,0:T(8,128)(2,1)S(1)} %get-tuple-element.81.refs_0_), channel_id=1, source_target_pairs={{0,2},{1,5},{2,0},{3,7},{4,6},{5,1},{6,4},{7,3},{8,10},{9,13},{10,... | collective-permute-start | bytes 786440 | tf_op jit(solution)/shard_map/ppermute | solution.py:416
  32.7 4.6 %shard_map.110 = (bf16[256,2048]{1,0:T(8,128)(2,1)}, bf16[256,2048]{1,0:T(8,128)(2,1)}, bf16[256,2048]{1,0:T(8,128)(2,1)S(1)}, bf16[256,2048]{1,0:T(8,128)(2,1)S...) custom-call(s32[1,256]{1,0:T(1,128)S(1)} %get-tuple-element.52.length, f32[1,256]{1,0:T(1,128)S(1)} %get-tuple-element.72.inverse_rms, ...), custom_call_target="tpu_custom_call" | custom-call | flops 939524096 | bytes 13121536 | tf_op jit(solution)/shard_map/pallas_call | solution.py:394
  37.3 0.2 collective-permute-done.17.refs_3_
  37.6 0.0 collective-permute-done.15.refs_1_
  37.6 1.6 %collective-permute-done.16.refs_2_ = bf16[1024,128]{1,0:T(8,128)(2,1)S(1)} collective-permute-done((bf16[1024,128]{1,0:T(8,128)(2,1)S(1)}, bf16[1024,128]{1,0:T(8,128)(2,1)S(1)}, u32[]{:S(2)}, u32[]{:S(2)}) %collective-permute-start.16) | collective-permute-done | bytes 262176 | tf_op jit(solution)/shard_map/ppermute | solution.py:416
  39.2 0.3 shard_map.111
  39.5 1.5 %collective-permute-start.21 = (bf16[512,128]{1,0:T(8,128)(2,1)S(1)}, bf16[512,128]{1,0:T(8,128)(2,1)S(1)}, u32[]{:S(2)}, u32[]{:S(2)}) collective-permute-start(bf16[512,128]{1,0:T(8,128)(2,1)S(1)} %get-tuple-element.93), channel_id=1, source_target_pairs={{0,4},{1,3},{2,6},{3,1},{4,0},{5,7},{6,2},{7,5},{8,12},{9,11},{10,... | collective-permute-start | bytes 393224 | tf_op jit(solution)/shard_map/ppermute | solution.py:416
  41.0 0.0 collective-permute-start.22
  41.0 0.9 %collective-permute-start.23 = (bf16[512,128]{1,0:T(8,128)(2,1)S(1)}, bf16[512,128]{1,0:T(8,128)(2,1)S(1)}, u32[]{:S(2)}, u32[]{:S(2)}) collective-permute-start(bf16[512,128]{1,0:T(8,128)(2,1)S(1)} %get-tuple-element.95), channel_id=1, source_target_pairs={{0,1},{1,0},{2,3},{3,2},{4,5},{5,4},{6,7},{7,6},{8,9},{9,8},{10,11... | collective-permute-start | bytes 393224 | tf_op jit(solution)/shard_map/ppermute | solution.py:416
  41.9 0.3 shard_map.112
  42.2 0.7 %collective-permute-start.18 = (bf16[512,128]{1,0:T(8,128)(2,1)S(1)}, bf16[512,128]{1,0:T(8,128)(2,1)S(1)}, u32[]{:S(2)}, u32[]{:S(2)}) collective-permute-start(bf16[512,128]{1,0:T(8,128)(2,1)S(1)} %get-tuple-element.90), channel_id=1, source_target_pairs={{0,4},{1,3},{2,6},{3,1},{4,0},{5,7},{6,2},{7,5},{8,12},{9,11},{10,... | collective-permute-start | bytes 393224 | tf_op jit(solution)/shard_map/ppermute | solution.py:416
  42.9 0.5 collective-permute-start.19
  43.4 1.1 %collective-permute-done.21.rest_0_ = bf16[512,128]{1,0:T(8,128)(2,1)S(1)} collective-permute-done((bf16[512,128]{1,0:T(8,128)(2,1)S(1)}, bf16[512,128]{1,0:T(8,128)(2,1)S(1)}, u32[]{:S(2)}, u32[]{:S(2)}) %collective-permute-start.21) | collective-permute-done | bytes 131104 | tf_op jit(solution)/shard_map/ppermute | solution.py:416
  44.5 0.0 collective-permute-start.20
  44.5 2.0 %shard_map.113 = (bf16[256,2048]{1,0:T(8,128)(2,1)}, bf16[256,2048]{1,0:T(8,128)(2,1)}, f32[256,2048]{1,0:T(8,128)S(1)}) custom-call(s32[1,256]{1,0:T(1,128)S(1)} %get-tuple-element.52.length, bf16[256,2048]{1,0:T(8,128)(2,1)S(1)} %shard_map.103.refs_4_.queries, ...), custom_call_target="tpu_custom_call", output_to_operand_aliasing={{0}: (6, {}), {1}: (7, {})} | custom-call | flops 536870912 | bytes 11535360 | tf_op jit(solution)/shard_map/pallas_call | solution.py:394
  46.6 0.0 collective-permute-done.22.rest_2_
  46.6 0.0 collective-permute-done.23.rest_3_
  46.6 1.6 %shard_map.114 = (bf16[256,2048]{1,0:T(8,128)(2,1)}, bf16[256,2048]{1,0:T(8,128)(2,1)}) custom-call(s32[1,256]{1,0:T(1,128)S(1)} %get-tuple-element.52.length, bf16[256,2048]{1,0:T(8,128)(2,1)S(1)} %get-tuple-element.54.keys, bf16[256,2048]{1,0:T(8,128)(2,1)S(1)} %get-tuple-element.55.values, f32[256,2048]{1,0:T(8,128)S(1)} %get-tuple-element.88.key_part, ...), custom_call_target="tpu_custom_call" | custom-call | flops 134217728 | bytes 8913920 | tf_op jit(solution)/shard_map/pallas_call | solution.py:394
  48.2 0.0 collective-permute-done.18.rest_0_
  48.2 0.0 collective-permute-done.19.rest_2_
  48.2 0.0 collective-permute-done.20.rest_3_
  48.2 1.6 %shard_map.115 = (bf16[256,2048]{1,0:T(8,128)(2,1)}, bf16[256,2048]{1,0:T(8,128)(2,1)}) custom-call(s32[1,256]{1,0:T(1,128)S(1)} %get-tuple-element.52.length, bf16[256,2048]{1,0:T(8,128)(2,1)S(1)} %get-tuple-element.54.keys, bf16[256,2048]{1,0:T(8,128)(2,1)S(1)} %get-tuple-element.55.values, ...), custom_call_target="tpu_custom_call", output_to_operand_aliasing={{0}: (9, {}), {1}: (10, {})} | custom-call | flops 134217728 | bytes 11011072 | tf_op jit(solution)/shard_map/pallas_call | solution.py:394
  (2 shorter events, 0.0 us)
Async XLA Ops:
  3.6 6.9 %collective-permute-start.2 = (bf16[512,128]{1,0:T(8,128)(2,1)S(1)}, bf16[512,128]{1,0:T(8,128)(2,1)S(1)}, u32[]{:S(2)}, u32[]{:S(2)}) collective-permute-start(bf16[512,128]{1,0:T(8,128)(2,1)S(1)} %get-tuple-element.57), channel_id=1, source_target_pairs={{0,5},{1,2},{2,7},{3,0},{4,1},{5,6},{6,3},{7,4},{8,13},{9,10},{10,... | collective-permute-start | bytes 393224 | tf_op jit(solution)/shard_map/ppermute | solution.py:416
  6.1 4.9 %collective-permute-start = (bf16[512,128]{1,0:T(8,128)(2,1)S(1)}, bf16[512,128]{1,0:T(8,128)(2,1)S(1)}, u32[]{:S(2)}, u32[]{:S(2)}) collective-permute-start(bf16[512,128]{1,0:T(8,128)(2,1)S(1)} %get-tuple-element.57), channel_id=1, source_target_pairs={{0,1},{1,0},{2,3},{3,2},{4,5},{5,4},{6,7},{7,6},{8,9},{9,8},{10,11... | collective-permute-start | bytes 393224 | tf_op jit(solution)/shard_map/ppermute | solution.py:416
  6.7 5.0 %collective-permute-start.1 = (bf16[512,128]{1,0:T(8,128)(2,1)S(1)}, bf16[512,128]{1,0:T(8,128)(2,1)S(1)}, u32[]{:S(2)}, u32[]{:S(2)}) collective-permute-start(bf16[512,128]{1,0:T(8,128)(2,1)S(1)} %get-tuple-element.53._.refs_0_), channel_id=1, source_target_pairs={{0,2},{1,5},{2,0},{3,7},{4,6},{5,1},{6,4},{7,3},{8,10},{9,13},{10,... | collective-permute-start | bytes 393224 | tf_op jit(solution)/shard_map/ppermute | solution.py:416
  7.6 6.8 %collective-permute-start.4 = (bf16[512,128]{1,0:T(8,128)(2,1)S(1)}, bf16[512,128]{1,0:T(8,128)(2,1)S(1)}, u32[]{:S(2)}, u32[]{:S(2)}) collective-permute-start(bf16[512,128]{1,0:T(8,128)(2,1)S(1)} %get-tuple-element.59.refs_0_), channel_id=1, source_target_pairs={{0,2},{1,5},{2,0},{3,7},{4,6},{5,1},{6,4},{7,3},{8,10},{9,13},{10,... | collective-permute-start | bytes 393224 | tf_op jit(solution)/shard_map/ppermute | solution.py:416
  8.8 5.8 %collective-permute-start.5 = (bf16[512,128]{1,0:T(8,128)(2,1)S(1)}, bf16[512,128]{1,0:T(8,128)(2,1)S(1)}, u32[]{:S(2)}, u32[]{:S(2)}) collective-permute-start(bf16[512,128]{1,0:T(8,128)(2,1)S(1)} %get-tuple-element.60), channel_id=1, source_target_pairs={{0,5},{1,2},{2,7},{3,0},{4,1},{5,6},{6,3},{7,4},{8,13},{9,10},{10,... | collective-permute-start | bytes 393224 | tf_op jit(solution)/shard_map/ppermute | solution.py:416
  10.6 3.9 %collective-permute-start.3 = (bf16[512,128]{1,0:T(8,128)(2,1)S(1)}, bf16[512,128]{1,0:T(8,128)(2,1)S(1)}, u32[]{:S(2)}, u32[]{:S(2)}) collective-permute-start(bf16[512,128]{1,0:T(8,128)(2,1)S(1)} %get-tuple-element.60), channel_id=1, source_target_pairs={{0,1},{1,0},{2,3},{3,2},{4,5},{5,4},{6,7},{7,6},{8,9},{9,8},{10,11... | collective-permute-start | bytes 393224 | tf_op jit(solution)/shard_map/ppermute | solution.py:416
  12.0 5.0 %collective-permute-start.9 = (bf16[512,128]{1,0:T(8,128)(2,1)S(1)}, bf16[512,128]{1,0:T(8,128)(2,1)S(1)}, u32[]{:S(2)}, u32[]{:S(2)}) collective-permute-start(bf16[512,128]{1,0:T(8,128)(2,1)S(1)} %get-tuple-element.65), channel_id=1, source_target_pairs={{0,4},{1,3},{2,6},{3,1},{4,0},{5,7},{6,2},{7,5},{8,12},{9,11},{10,... | collective-permute-start | bytes 393224 | tf_op jit(solution)/shard_map/ppermute | solution.py:416
  13.6 5.3 %collective-permute-start.10 = (bf16[512,128]{1,0:T(8,128)(2,1)S(1)}, bf16[512,128]{1,0:T(8,128)(2,1)S(1)}, u32[]{:S(2)}, u32[]{:S(2)}) collective-permute-start(bf16[512,128]{1,0:T(8,128)(2,1)S(1)} %get-tuple-element.66), channel_id=1, source_target_pairs={{0,5},{1,2},{2,7},{3,0},{4,1},{5,6},{6,3},{7,4},{8,13},{9,10},{10,... | collective-permute-start | bytes 393224 | tf_op jit(solution)/shard_map/ppermute | solution.py:416
  14.4 4.4 %collective-permute-start.11 = (bf16[512,128]{1,0:T(8,128)(2,1)S(1)}, bf16[512,128]{1,0:T(8,128)(2,1)S(1)}, u32[]{:S(2)}, u32[]{:S(2)}) collective-permute-start(bf16[512,128]{1,0:T(8,128)(2,1)S(1)} %get-tuple-element.67), channel_id=1, source_target_pairs={{0,1},{1,0},{2,3},{3,2},{4,5},{5,4},{6,7},{7,6},{8,9},{9,8},{10,11... | collective-permute-start | bytes 393224 | tf_op jit(solution)/shard_map/ppermute | solution.py:416
  14.8 5.0 %collective-permute-start.6 = (bf16[512,128]{1,0:T(8,128)(2,1)S(1)}, bf16[512,128]{1,0:T(8,128)(2,1)S(1)}, u32[]{:S(2)}, u32[]{:S(2)}) collective-permute-start(bf16[512,128]{1,0:T(8,128)(2,1)S(1)} %get-tuple-element.61), channel_id=1, source_target_pairs={{0,4},{1,3},{2,6},{3,1},{4,0},{5,7},{6,2},{7,5},{8,12},{9,11},{10,... | collective-permute-start | bytes 393224 | tf_op jit(solution)/shard_map/ppermute | solution.py:416
  16.4 4.4 %collective-permute-start.7 = (bf16[512,128]{1,0:T(8,128)(2,1)S(1)}, bf16[512,128]{1,0:T(8,128)(2,1)S(1)}, u32[]{:S(2)}, u32[]{:S(2)}) collective-permute-start(bf16[512,128]{1,0:T(8,128)(2,1)S(1)} %get-tuple-element.63), channel_id=1, source_target_pairs={{0,5},{1,2},{2,7},{3,0},{4,1},{5,6},{6,3},{7,4},{8,13},{9,10},{10,... | collective-permute-start | bytes 393224 | tf_op jit(solution)/shard_map/ppermute | solution.py:416
  17.0 3.8 %collective-permute-start.8 = (bf16[512,128]{1,0:T(8,128)(2,1)S(1)}, bf16[512,128]{1,0:T(8,128)(2,1)S(1)}, u32[]{:S(2)}, u32[]{:S(2)}) collective-permute-start(bf16[512,128]{1,0:T(8,128)(2,1)S(1)} %get-tuple-element.64), channel_id=1, source_target_pairs={{0,1},{1,0},{2,3},{3,2},{4,5},{5,4},{6,7},{7,6},{8,9},{9,8},{10,11... | collective-permute-start | bytes 393224 | tf_op jit(solution)/shard_map/ppermute | solution.py:416
  17.3 1.5 %copy-start = (bf16[1,256,2048]{2,1,0:T(8,128)(2,1)S(1)}, bf16[1,256,2048]{2,1,0:T(8,128)(2,1)}, u32[]{:S(2)}) copy-start(bf16[1,256,2048]{2,1,0:T(8,128)(2,1)} %param.10) | copy-start | bytes 3145732
  17.3 1.5 %copy-start.1 = (f32[2048]{0:T(1024)S(1)}, f32[2048]{0:T(1024)}, u32[]{:S(2)}) copy-start(f32[2048]{0:T(1024)} %param.11) | copy-start | bytes 24580
  21.5 4.5 %collective-permute-start.14 = (f32[2,256]{1,0:T(2,128)S(1)}, f32[2,256]{1,0:T(2,128)S(1)}, u32[]{:S(2)}, u32[]{:S(2)}) collective-permute-start(f32[2,256]{1,0:T(2,128)S(1)} %get-tuple-element.69.rest_0_), channel_id=1, source_target_pairs={{0,16},{8,24},{16,0},{24,8},{1,17},{9,25},{17,1},{25,9},{2,18},{10... | collective-permute-start | bytes 6152 | tf_op jit(solution)/shard_map/ppermute | solution.py:443
  24.1 5.4 %collective-permute-start.13 = (f32[2,256]{1,0:T(2,128)S(1)}, f32[2,256]{1,0:T(2,128)S(1)}, u32[]{:S(2)}, u32[]{:S(2)}) collective-permute-start(f32[2,256]{1,0:T(2,128)S(1)} %get-tuple-element.69.rest_0_), channel_id=1, source_target_pairs={{0,24},{8,16},{16,8},{24,0},{1,25},{9,17},{17,9},{25,1},{2,26},{10... | collective-permute-start | bytes 6152 | tf_op jit(solution)/shard_map/ppermute | solution.py:443
  25.5 4.0 %collective-permute-start.12 = (f32[2,256]{1,0:T(2,128)S(1)}, f32[2,256]{1,0:T(2,128)S(1)}, u32[]{:S(2)}, u32[]{:S(2)}) collective-permute-start(f32[2,256]{1,0:T(2,128)S(1)} %get-tuple-element.69.rest_0_), channel_id=1, source_target_pairs={{0,8},{8,0},{16,24},{24,16},{1,9},{9,1},{17,25},{25,17},{2,10},{10... | collective-permute-start | bytes 6152 | tf_op jit(solution)/shard_map/ppermute | solution.py:443
  30.6 7.0 %collective-permute-start.17 = (bf16[1024,128]{1,0:T(8,128)(2,1)S(1)}, bf16[1024,128]{1,0:T(8,128)(2,1)S(1)}, u32[]{:S(2)}, u32[]{:S(2)}) collective-permute-start(bf16[1024,128]{1,0:T(8,128)(2,1)S(1)} %get-tuple-element.82), channel_id=1, source_target_pairs={{0,5},{1,2},{2,7},{3,0},{4,1},{5,6},{6,3},{7,4},{8,13},{9,10},{10,... | collective-permute-start | bytes 786440 | tf_op jit(solution)/shard_map/ppermute | solution.py:416
  30.6 7.0 %collective-permute-start.15 = (bf16[1024,128]{1,0:T(8,128)(2,1)S(1)}, bf16[1024,128]{1,0:T(8,128)(2,1)S(1)}, u32[]{:S(2)}, u32[]{:S(2)}) collective-permute-start(bf16[1024,128]{1,0:T(8,128)(2,1)S(1)} %get-tuple-element.82), channel_id=1, source_target_pairs={{0,1},{1,0},{2,3},{3,2},{4,5},{5,4},{6,7},{7,6},{8,9},{9,8},{10,11... | collective-permute-start | bytes 786440 | tf_op jit(solution)/shard_map/ppermute | solution.py:416
  31.6 7.6 %collective-permute-start.16 = (bf16[1024,128]{1,0:T(8,128)(2,1)S(1)}, bf16[1024,128]{1,0:T(8,128)(2,1)S(1)}, u32[]{:S(2)}, u32[]{:S(2)}) collective-permute-start(bf16[1024,128]{1,0:T(8,128)(2,1)S(1)} %get-tuple-element.81.refs_0_), channel_id=1, source_target_pairs={{0,2},{1,5},{2,0},{3,7},{4,6},{5,1},{6,4},{7,3},{8,10},{9,13},{10,... | collective-permute-start | bytes 786440 | tf_op jit(solution)/shard_map/ppermute | solution.py:416
  39.5 5.0 %collective-permute-start.21 = (bf16[512,128]{1,0:T(8,128)(2,1)S(1)}, bf16[512,128]{1,0:T(8,128)(2,1)S(1)}, u32[]{:S(2)}, u32[]{:S(2)}) collective-permute-start(bf16[512,128]{1,0:T(8,128)(2,1)S(1)} %get-tuple-element.93), channel_id=1, source_target_pairs={{0,4},{1,3},{2,6},{3,1},{4,0},{5,7},{6,2},{7,5},{8,12},{9,11},{10,... | collective-permute-start | bytes 393224 | tf_op jit(solution)/shard_map/ppermute | solution.py:416
  41.0 5.6 %collective-permute-start.22 = (bf16[512,128]{1,0:T(8,128)(2,1)S(1)}, bf16[512,128]{1,0:T(8,128)(2,1)S(1)}, u32[]{:S(2)}, u32[]{:S(2)}) collective-permute-start(bf16[512,128]{1,0:T(8,128)(2,1)S(1)} %get-tuple-element.94), channel_id=1, source_target_pairs={{0,5},{1,2},{2,7},{3,0},{4,1},{5,6},{6,3},{7,4},{8,13},{9,10},{10,... | collective-permute-start | bytes 393224 | tf_op jit(solution)/shard_map/ppermute | solution.py:416
  41.0 5.6 %collective-permute-start.23 = (bf16[512,128]{1,0:T(8,128)(2,1)S(1)}, bf16[512,128]{1,0:T(8,128)(2,1)S(1)}, u32[]{:S(2)}, u32[]{:S(2)}) collective-permute-start(bf16[512,128]{1,0:T(8,128)(2,1)S(1)} %get-tuple-element.95), channel_id=1, source_target_pairs={{0,1},{1,0},{2,3},{3,2},{4,5},{5,4},{6,7},{7,6},{8,9},{9,8},{10,11... | collective-permute-start | bytes 393224 | tf_op jit(solution)/shard_map/ppermute | solution.py:416
  42.2 6.0 %collective-permute-start.18 = (bf16[512,128]{1,0:T(8,128)(2,1)S(1)}, bf16[512,128]{1,0:T(8,128)(2,1)S(1)}, u32[]{:S(2)}, u32[]{:S(2)}) collective-permute-start(bf16[512,128]{1,0:T(8,128)(2,1)S(1)} %get-tuple-element.90), channel_id=1, source_target_pairs={{0,4},{1,3},{2,6},{3,1},{4,0},{5,7},{6,2},{7,5},{8,12},{9,11},{10,... | collective-permute-start | bytes 393224 | tf_op jit(solution)/shard_map/ppermute | solution.py:416
  42.9 5.3 %collective-permute-start.19 = (bf16[512,128]{1,0:T(8,128)(2,1)S(1)}, bf16[512,128]{1,0:T(8,128)(2,1)S(1)}, u32[]{:S(2)}, u32[]{:S(2)}) collective-permute-start(bf16[512,128]{1,0:T(8,128)(2,1)S(1)} %get-tuple-element.91), channel_id=1, source_target_pairs={{0,5},{1,2},{2,7},{3,0},{4,1},{5,6},{6,3},{7,4},{8,13},{9,10},{10,... | collective-permute-start | bytes 393224 | tf_op jit(solution)/shard_map/ppermute | solution.py:416
  44.5 3.7 %collective-permute-start.20 = (bf16[512,128]{1,0:T(8,128)(2,1)S(1)}, bf16[512,128]{1,0:T(8,128)(2,1)S(1)}, u32[]{:S(2)}, u32[]{:S(2)}) collective-permute-start(bf16[512,128]{1,0:T(8,128)(2,1)S(1)} %get-tuple-element.92), channel_id=1, source_target_pairs={{0,1},{1,0},{2,3},{3,2},{4,5},{5,4},{6,7},{7,6},{8,9},{9,8},{10,11... | collective-permute-start | bytes 393224 | tf_op jit(solution)/shard_map/ppermute | solution.py:416

commit v10 on v9

--- a/solution.py
+++ b/solution.py
@@ -102,12 +102,12 @@
     return [full.at[pl.ds(pl.multiple_of((core ^ j) * half, half), half), :] for j in range(pair)]
 
 
-def join_halves(parts, full, core, pair):
-    for half, terms in zip(row_halves(full, core, pair), parts):
-        total = terms[0][...].astype(F32)
-        for term in terms[1:]:
-            total += term[...].astype(F32)
-        half[...] = total.astype(BF16)
+def join_halves(refs, layout, full, core, pair):
+    refs = iter(refs)
+    for half, firsts in zip(row_halves(full, core, pair), layout):
+        rows = half.shape[0]
+        terms = [next(refs)[first : first + rows, :].astype(F32) for first in firsts]
+        half[...] = sum(terms[1:], terms[0]).astype(BF16)
 
 
 def line_length(grid):
@@ -173,22 +173,34 @@
         cols = head_cols(head)
         masked = jnp.where(live, keys[:, cols], jnp.zeros((), BF16))
         full[head * HD : (head + 1) * HD, :] = tn(masked, values[:, cols]).astype(BF16)
-    write_halves(full, outs, my_place(grid)[2], grid[2])
-
-
-def mix_kernel(sources, first, weights, *refs):
-    blocks, outs = refs[:sources], refs[-sources:]
+    core, pair = my_place(grid)[2], grid[2]
+    parts = FORWARD_PIECES * pair
+    write_halves(full, outs[:parts], core, pair)
+    if pair > 1:
+        tall = outs[1].shape[0]
+        for piece in range(FORWARD_PIECES):
+            outs[parts][piece * tall : (piece + 1) * tall, :] = outs[piece * pair + 1][...]
+
+
+def mix_kernel(firsts, pair, pieces, weights, *refs):
+    sources = len(firsts)
+    blocks, outs = refs[:sources], refs[-pair - (sources - pair) * pieces :]
     rows = outs[0].shape[0]
-    chunk = min(rows, 64)
+    chunk = min(rows // pieces, 64)
     for start in range(0, rows, chunk):
         part = slice(start, start + chunk)
-        loaded = [block[first + start : first + start + chunk, :].astype(F32) for block in blocks]
-        for out_step, out in enumerate(outs):
-            at = out_step * sources
+        loaded = [block[first + start : first + start + chunk, :].astype(F32) for block, first in zip(blocks, firsts)]
+        for target in range(sources):
+            at = target * sources
             total = weights[at : at + 1, :] * loaded[0]
-            for in_step in range(1, sources):
-                total += weights[at + in_step : at + in_step + 1, :] * loaded[in_step]
-            out[part, :] = total.astype(BF16)
+            for source in range(1, sources):
+                total += weights[at + source : at + source + 1, :] * loaded[source]
+            if target < pair:
+                outs[target][part, :] = total.astype(BF16)
+            else:
+                piece, inner = divmod(start, rows // pieces)
+                out = outs[pair + piece * (sources - pair) + target - pair]
+                out[inner : inner + chunk, :] = total.astype(BF16)
 
 
 def live_rows(length, rows):
@@ -242,10 +254,11 @@
     return jnp.transpose(jnp.broadcast_to(row, (HD, row.shape[1])))
 
 
-def carry_kernel(piece, grid, counts, scale, length, queries, local, cotangent, gain, *rest):
-    received, rest = rest[: sum(counts)], rest[sum(counts) :]
+def carry_kernel(piece, grid, layout, scale, length, queries, local, cotangent, gain, *rest):
+    count = sum(map(len, layout))
+    received, rest = rest[:count], rest[count:]
     before, (attention, sums, prefix) = rest[:-3], rest[-3:]
-    join_halves(split_refs(received, *counts), prefix, my_place(grid)[2], grid[2])
+    join_halves(received, layout, prefix, my_place(grid)[2], grid[2])
     rows, width = attention.shape
     factor = jnp.where(live_rows(length, rows), scale, 0.0)
     squares = jnp.zeros((rows, HD), F32)
@@ -309,7 +322,7 @@
 def query_kernel(heads, group, scale, length, inverse_rms, gain, queries, keys, values, *rest):
     sizes = (BACKWARD_PIECES, FORWARD_PIECES, FORWARD_PIECES)
     grads, attention, prefix, rest = split_refs(rest, *sizes, len(rest) - sum(sizes))
-    attended_hbm, query_hbm, attended, query_grad, key_part, token, sems = rest
+    attended_hbm, query_hbm, key_part, token, attended, query_grad, sems = rest
     token[...] = jnp.zeros_like(token)
     keep = keep_mask(length, False)
     inverse = token_columns(inverse_rms[...])
@@ -326,7 +339,7 @@
         query_grad[:, cols] = (scale * (carried + nn(grad_scores, keys[:, cols]))).astype(BF16)
         key_part[:, cols] = scale * tn(grad_scores, queries[:, cols])
         attended[:, cols] = (out_piece[:, at] * inverse * gain[:, cols]).astype(BF16)
-        if (head + 1) % group == 0 and head + 1 < heads:
+        if (head + 1) % group == 0:
             step = head // group
             some = column_copies(
                 (attended, query_grad), (attended_hbm, query_hbm), step * group, group, sems.at[step]
@@ -338,26 +351,21 @@
         copy.wait()
 
 
-def value_kernel(heads, group, scale, length, queries, keys, attended, query_grad, *rest):
-    grads, (attended_hbm, query_hbm, value_part, sems) = rest[:BACKWARD_PIECES], rest[-4:]
-    copies = column_copies((attended, query_grad), (attended_hbm, query_hbm), heads - group, group, sems)
-    for copy in copies:
-        copy.start()
+def value_kernel(heads, scale, length, queries, keys, *rest):
+    grads, value_part = rest[:BACKWARD_PIECES], rest[-1]
     keep = keep_mask(length, True)
     for head in range(heads):
         cols = head_cols(head)
         grad_piece, at = head_of(grads, head)
         turned = jnp.where(keep, nt(keys[:, cols], queries[:, cols]), 0.0).astype(BF16)
         value_part[:, cols] = scale * nn(turned, grad_piece[:, at])
-    for copy in copies:
-        copy.wait()
-
-
-def final_kernel(piece, grid, counts, length, keys, values, key_part, value_part, *rest):
-    received, rest = rest[: sum(counts)], rest[sum(counts) :]
+
+
+def final_kernel(piece, grid, layout, length, keys, values, key_part, value_part, *rest):
+    received, rest = rest[: sum(map(len, layout))], rest[sum(map(len, layout)) :]
     key_hbm, value_hbm, key_grad, value_grad, below, sems = rest[-6:]
     pair = grid[2]
-    join_halves(split_refs(received, *counts), below, my_place(grid)[2], pair)
+    join_halves(received, layout, below, my_place(grid)[2], pair)
     rows, width = key_grad.shape
     live = jnp.where(live_rows(length, rows), 1.0, 0.0)
     per_half = width // HD // pair
@@ -416,24 +424,35 @@
     return lax.ppermute(block, "seg", moves)
 
 
-def gather_line(halves, grid):
+def gather_line(pieces, whole, grid):
     pair = grid[2]
-    arrived = {0: halves[0]}
-    for step in range(line_length(grid)):
-        for flip in range(pair):
-            if step or flip:
-                arrived[step * pair + flip] = line_send(halves[flip], grid, step, flip, True)
-    return [arrived[j] for j in range(len(arrived))]
-
-
-def scatter_line(sums, grid):
+    swapped = [line_send(whole, grid, 0, flip, True) for flip in range(1, pair)]
+    found = []
+    for number, halves in enumerate(pieces):
+        first = number * halves[0].shape[0]
+        blocks = [(halves[0], 0)] + [(block, first) for block in swapped]
+        for step in range(1, line_length(grid)):
+            blocks += [(line_send(halves[flip], grid, step, flip, True), 0) for flip in range(pair)]
+        found.append(blocks)
+    return found
+
+
+def scatter_line(sums, grid, pieces):
     pair = grid[2]
-    parts = [[] for _ in range(pair)]
-    for step in reversed(range(line_length(grid))):
-        for flip in range(pair):
-            block = sums[step * pair + flip]
-            parts[flip].append(line_send(block, grid, step, flip, False) if step or flip else block)
-    return parts
+    others = (line_length(grid) - 1) * pair
+    swapped = [line_send(sums[flip], grid, 0, flip, False) for flip in range(1, pair)]
+    found = []
+    for piece in range(pieces):
+        first = piece * (sums[0].shape[0] // pieces)
+        parts = [[] for _ in range(pair)]
+        for step in range(1, line_length(grid)):
+            for flip in range(pair):
+                block = sums[pair + piece * others + (step - 1) * pair + flip]
+                parts[flip].append((line_send(block, grid, step, flip, False), 0))
+        for flip, block in enumerate([sums[0]] + swapped):
+            parts[flip].append((block, first))
+        found.append(parts)
+    return found
 
 
 def token_sums(sums, groups):
@@ -459,31 +478,33 @@
     members = line_length(grid) * pair
     weight_rows = shape((members * members, HD), F32)
     sems = pltpu.SemaphoreType.DMA((2, heads))
-    counts = [line_length(grid)] * pair
     unit = 2 * heads * rows * HD
 
     def halves(pieces):
         return [shape((features // (pair * pieces), HD), BF16)] * pair
 
-    def mix(arrived, weights, piece, pieces, after=()):
-        tall = arrived[0].shape[0] // pieces
-        like = [shape((tall, HD), BF16)] * members
-        return call(functools.partial(mix_kernel, members, piece * tall), like, (weights, *arrived), after=after)
-
-    def flat(parts):
-        return [block for part in parts for block in part]
+    def mix(arrived, weights, pieces, after=()):
+        blocks, firsts = zip(*arrived)
+        tall = blocks[0].shape[0]
+        like = [shape((tall, HD), BF16)] * pair + [shape((tall // pieces, HD), BF16)] * ((members - pair) * pieces)
+        return call(functools.partial(mix_kernel, firsts, pair, pieces), like, (weights, *blocks), after=after)
+
+    def unzip(parts):
+        blocks = [block for part in parts for block, _ in part]
+        return blocks, [[first for _, first in part] for part in parts]
 
     key, value, length, up, down, *own = call(
         functools.partial(state_kernel, grid),
-        [narrow, narrow, shape((1, rows), jnp.int32), weight_rows, weight_rows] + halves(FORWARD_PIECES) * FORWARD_PIECES,
+        [narrow, narrow, shape((1, rows), jnp.int32), weight_rows, weight_rows] + halves(FORWARD_PIECES) * FORWARD_PIECES + halves(1)[1:],
         (seg_len, key_rows[0], values[0], parent[None]),
         [pltpu.VMEM((features, HD), BF16), sems, pltpu.SMEM((1, segs), jnp.int32), pltpu.SemaphoreType.DMA(())],
         unit * HD, (1, 2, 3), (0,),
     )
     (query,) = call(fetch_kernel, [narrow], (queries[0],), [pltpu.SemaphoreType.DMA((4,))], 0, (0,), after=(own[0],))
+    *parts, whole = split_refs(own, *[pair] * FORWARD_PIECES, pair - 1)
     mixed = []
-    for part in split_refs(own, *[pair] * FORWARD_PIECES):
-        mixed.append(mix(gather_line(part, grid), up, 0, 1, () if mixed else (query,)))
+    for arrived in gather_line(parts, whole[0] if whole else None, grid):
+        mixed.append(mix(arrived, up, 1, () if mixed else (query,)))
     (local,) = call(
         functools.partial(local_kernel, heads),
         [wide], (length, query, key, value), (), unit * rows * 2, after=(mixed[0][0],),
@@ -491,10 +512,11 @@
     attention, prefix, sums = [], [], []
     width = features // FORWARD_PIECES
     for piece in range(FORWARD_PIECES):
+        blocks, layout = unzip(scatter_line(mixed[piece], grid, 1)[0])
         out, total, joined = call(
-            functools.partial(carry_kernel, piece, grid, counts, scale),
+            functools.partial(carry_kernel, piece, grid, layout, scale),
             [shape((rows, width), F32), shape((2, rows), F32), shape((width, HD), BF16)],
-            (length, query, local, cot, gain, *flat(scatter_line(mixed[piece], grid)), *sums),
+            (length, query, local, cot, gain, *blocks, *sums),
             (), unit * HD // FORWARD_PIECES,
         )
         attention.append(out)
@@ -513,33 +535,28 @@
         grads.append(grad_out)
         state_grad.append(parts)
     group = 4 if heads % 4 == 0 else 1
-    attended, query_grad, attended_rest, query_rest, key_part, token = call(
+    attended, query_grad, key_part, token = call(
         functools.partial(query_kernel, heads, group, scale),
-        [narrow, narrow, narrow, narrow, wide, shape((8, HD), F32)],
+        [narrow, narrow, wide, shape((8, HD), F32)],
         (length, inverse_rms, gain, query, key, value, *grads, *attention, *prefix),
-        [pltpu.SemaphoreType.DMA((heads // group, 2))], unit * (3 * rows + HD),
-        out_specs=[HBM, HBM] + [VMEM] * 4,
+        [pltpu.VMEM(narrow.shape, BF16)] * 2 + [pltpu.SemaphoreType.DMA((heads // group, 2))], unit * (3 * rows + HD),
+        out_specs=[HBM, HBM, VMEM, VMEM],
     )
-    (part,) = state_grad
-    arrived = gather_line(part, grid)
-    mixed = []
-    for piece in range(RETURN_PIECES):
-        mixed.append(mix(arrived, down, piece, RETURN_PIECES, (token, *mixed[-1][:1]) if mixed else (token,)))
-    operands = (length, query, key, attended_rest, query_rest, *grads, attended, query_grad)
-    last = len(operands) - 2
-    attended, query_grad, value_part = call(
-        functools.partial(value_kernel, heads, group, scale),
-        [narrow, narrow, wide], operands, [pltpu.SemaphoreType.DMA((2,))], unit * 2 * rows, (last, last + 1),
-        after=(mixed[-1][0],), out_specs=[HBM, HBM, VMEM], aliases={last: 0, last + 1: 1},
+    (arrived,) = gather_line(state_grad, state_grad[0][-1], grid)
+    mixed = mix(arrived, down, RETURN_PIECES, (token,))
+    (value_part,) = call(
+        functools.partial(value_kernel, heads, scale),
+        [wide], (length, query, key, *grads), (), unit * 2 * rows, after=(mixed[0],),
     )
+    returned = scatter_line(mixed, grid, RETURN_PIECES)
     results = []
     width = features // RETURN_PIECES
     for piece in range(RETURN_PIECES):
-        below = flat(scatter_line(mixed[piece], grid))
+        below, layout = unzip(returned[piece])
         operands = (length, key, value, key_part, value_part, *below, *results)
         first = len(operands) - len(results)
         results = call(
-            functools.partial(final_kernel, piece, grid, counts),
+            functools.partial(final_kernel, piece, grid, layout),
             [narrow, narrow], operands,
             [pltpu.VMEM((rows, width), BF16)] * 2 + [pltpu.VMEM((width, HD), BF16), sems],
             2 * unit * HD // RETURN_PIECES,

time: 50.2 us -> 52.2 us (1.040)
  waiting for transfers between devices: 9.2 us -> 12.5 us
  starting transfers between devices: 20.8 us -> 19.9 us
    ppermute x21 -> x19, waiting for transfers between devices: 5.39 us -> 8.75 us  [line_send(): return lax.ppermute(block, 'seg', moves)]
    ppermute x21 -> x19, starting transfers between devices: 16.5 us -> 15.7 us  [line_send(): return lax.ppermute(block, 'seg', moves)]
    pallas_call x14 -> x13, Pallas kernels: 18.4 us -> 18 us  [call(): pl.pallas_call(kernel, out_shape=out_shape, in_specs=specs + [ANY] * len(...]
  transfers between devices with their start and end apart: 24 -> 22, of which waited for: 10 -> 12; matrix products, arithmetic and copies ran while one was open for 0% -> 0% of each run, Pallas kernels for 25% -> 23%
where the time goes in v10:
time: 52.2 us; the launch traced here: 52 us
  starting transfers between devices  19.9 us (38%)
  Pallas kernels  18 us (34%)
  waiting for transfers between devices  12.5 us (24%)
  between operations  1.57 us (3%)
    pallas_call x13, Pallas kernels, call(): pl.pallas_call(kernel, out_shape=out_shape, in_specs=specs + [ANY] * len(...  18 us
    ppermute x19, starting transfers between devices, line_send(): return lax.ppermute(block, 'seg', moves)  15.7 us
    ppermute x19, waiting for transfers between devices, line_send(): return lax.ppermute(block, 'seg', moves)  8.75 us
    ppermute x3, starting transfers between devices, token_sums(): parts.append(lax.ppermute(sums, 'head', moves))  4.24 us
    ppermute x3, waiting for transfers between devices, token_sums(): parts.append(lax.ppermute(sums, 'head', moves))  3.8 us
  transfers between devices with their start and end apart: 22, of which 12 were waited for; matrix products, arithmetic and copies ran while one was open for 0% of the time, Pallas kernels for 23%

profile of v10, /device:TPU:0, one launch (start us, length us, event | category | flops | bytes accessed | tf_op | source)
XLA Modules:
  0.0 52.0 jit_solution(10748984684369721648)
XLA Ops:
  1.3 2.4 %shard_map.102 = (bf16[256,2048]{1,0:T(8,128)(2,1)S(1)}, bf16[256,2048]{1,0:T(8,128)(2,1)S(1)}, s32[1,256]{1,0:T(1,128)S(1)}, f32[16,128]{1,0:T(8,128)S(1)}, f32...) custom-call(s32[1]{0:T(128)S(6)} %copy.15.seg_len, ...), custom_call_target="tpu_custom_call" | custom-call | flops 134217728 | bytes 4998180 | tf_op jit(solution)/shard_map/pallas_call | solution.py:402
  3.6 0.5 %collective-permute-start = (bf16[1024,128]{1,0:T(8,128)(2,1)S(1)}, bf16[1024,128]{1,0:T(8,128)(2,1)S(1)}, u32[]{:S(2)}, u32[]{:S(2)}) collective-permute-start(bf16[1024,128]{1,0:T(8,128)(2,1)S(1)} %get-tuple-element.51), channel_id=1, source_target_pairs={{0,1},{1,0},{2,3},{3,2},{4,5},{5,4},{6,7},{7,6},{8,9},{9,8},{10,11... | collective-permute-start | bytes 786440 | tf_op jit(solution)/shard_map/ppermute | solution.py:424
  4.2 2.6 %collective-permute-start.2 = (bf16[512,128]{1,0:T(8,128)(2,1)S(1)}, bf16[512,128]{1,0:T(8,128)(2,1)S(1)}, u32[]{:S(2)}, u32[]{:S(2)}) collective-permute-start(bf16[512,128]{1,0:T(8,128)(2,1)S(1)} %get-tuple-element.52), channel_id=1, source_target_pairs={{0,5},{1,2},{2,7},{3,0},{4,1},{5,6},{6,3},{7,4},{8,13},{9,10},{10,... | collective-permute-start | bytes 393224 | tf_op jit(solution)/shard_map/ppermute | solution.py:424
  6.8 1.5 %collective-permute-start.1 = (bf16[512,128]{1,0:T(8,128)(2,1)S(1)}, bf16[512,128]{1,0:T(8,128)(2,1)S(1)}, u32[]{:S(2)}, u32[]{:S(2)}) collective-permute-start(bf16[512,128]{1,0:T(8,128)(2,1)S(1)} %get-tuple-element.47._.refs_0_), channel_id=1, source_target_pairs={{0,2},{1,5},{2,0},{3,7},{4,6},{5,1},{6,4},{7,3},{8,10},{9,13},{10,... | collective-permute-start | bytes 393224 | tf_op jit(solution)/shard_map/ppermute | solution.py:424
  8.3 0.0 collective-permute-start.4
  8.3 0.6 %collective-permute-start.3 = (bf16[512,128]{1,0:T(8,128)(2,1)S(1)}, bf16[512,128]{1,0:T(8,128)(2,1)S(1)}, u32[]{:S(2)}, u32[]{:S(2)}) collective-permute-start(bf16[512,128]{1,0:T(8,128)(2,1)S(1)} %get-tuple-element.54.refs_0_), channel_id=1, source_target_pairs={{0,2},{1,5},{2,0},{3,7},{4,6},{5,1},{6,4},{7,3},{8,10},{9,13},{10,... | collective-permute-start | bytes 393224 | tf_op jit(solution)/shard_map/ppermute | solution.py:424
  8.9 1.2 %shard_map.103.refs_4_.queries = bf16[256,2048]{1,0:T(8,128)(2,1)S(1)} custom-call(bf16[256,2048]{1,0:T(8,128)(2,1)} %bitcast.19, bf16[512,128]{1,0:T(8,128)(2,1)S(1)} %get-tuple-element.47._.refs_0_), custom_call_target="tpu_custom_call" | custom-call | bytes 2097152 | tf_op jit(solution)/shard_map/pallas_call | solution.py:402
  10.1 0.1 collective-permute-done.2.refs_3_
  10.2 2.1 %collective-permute-done.1.refs_2_ = bf16[512,128]{1,0:T(8,128)(2,1)S(1)} collective-permute-done((bf16[512,128]{1,0:T(8,128)(2,1)S(1)}, bf16[512,128]{1,0:T(8,128)(2,1)S(1)}, u32[]{:S(2)}, u32[]{:S(2)}) %collective-permute-start.1) | collective-permute-done | bytes 131104 | tf_op jit(solution)/shard_map/ppermute | solution.py:424
  12.3 0.0 collective-permute-done.refs_1_
  12.3 0.3 shard_map.104
  12.6 0.9 %collective-permute-start.8 = (bf16[512,128]{1,0:T(8,128)(2,1)S(1)}, bf16[512,128]{1,0:T(8,128)(2,1)S(1)}, u32[]{:S(2)}, u32[]{:S(2)}) collective-permute-start(bf16[512,128]{1,0:T(8,128)(2,1)S(1)} %get-tuple-element.60), channel_id=1, source_target_pairs={{0,4},{1,3},{2,6},{3,1},{4,0},{5,7},{6,2},{7,5},{8,12},{9,11},{10,... | collective-permute-start | bytes 393224 | tf_op jit(solution)/shard_map/ppermute | solution.py:424
  13.5 0.9 %collective-permute-start.9 = (bf16[512,128]{1,0:T(8,128)(2,1)S(1)}, bf16[512,128]{1,0:T(8,128)(2,1)S(1)}, u32[]{:S(2)}, u32[]{:S(2)}) collective-permute-start(bf16[512,128]{1,0:T(8,128)(2,1)S(1)} %get-tuple-element.61), channel_id=1, source_target_pairs={{0,5},{1,2},{2,7},{3,0},{4,1},{5,6},{6,3},{7,4},{8,13},{9,10},{10,... | collective-permute-start | bytes 393224 | tf_op jit(solution)/shard_map/ppermute | solution.py:424
  14.4 1.3 %collective-permute-start.10 = (bf16[512,128]{1,0:T(8,128)(2,1)S(1)}, bf16[512,128]{1,0:T(8,128)(2,1)S(1)}, u32[]{:S(2)}, u32[]{:S(2)}) collective-permute-start(bf16[512,128]{1,0:T(8,128)(2,1)S(1)} %get-tuple-element.62), channel_id=1, source_target_pairs={{0,1},{1,0},{2,3},{3,2},{4,5},{5,4},{6,7},{7,6},{8,9},{9,8},{10,11... | collective-permute-start | bytes 393224 | tf_op jit(solution)/shard_map/ppermute | solution.py:424
  15.7 0.0 collective-permute-done.4.refs_3_
  15.7 0.0 collective-permute-done.3.refs_2_
  15.7 0.3 shard_map.106
  16.0 1.5 %collective-permute-start.5 = (bf16[512,128]{1,0:T(8,128)(2,1)S(1)}, bf16[512,128]{1,0:T(8,128)(2,1)S(1)}, u32[]{:S(2)}, u32[]{:S(2)}) collective-permute-start(bf16[512,128]{1,0:T(8,128)(2,1)S(1)} %get-tuple-element.56), channel_id=1, source_target_pairs={{0,4},{1,3},{2,6},{3,1},{4,0},{5,7},{6,2},{7,5},{8,12},{9,11},{10,... | collective-permute-start | bytes 393224 | tf_op jit(solution)/shard_map/ppermute | solution.py:424
  17.5 0.0 collective-permute-start.6
  17.5 0.1 collective-permute-done.8.rest_0_
  17.6 0.0 collective-permute-start.7
  17.6 0.0 copy-start
  17.6 0.0 copy-start.1
  17.6 1.5 %shard_map.105.local = f32[256,2048]{1,0:T(8,128)S(1)} custom-call(s32[1,256]{1,0:T(1,128)S(1)} %get-tuple-element.46.length, bf16[256,2048]{1,0:T(8,128)(2,1)S(1)} %shard_map.103.refs_4_.queries, bf16[256,2048]{1,0:T(8,128)(2,1)S(1)} %get-tuple-element.48.keys, bf16[256,2048]{1,0:T(8,128)(2,1)S(1)} %get-tuple-element.49.values, ...), custom_call_target="tpu_custom_call" | custom-call | flops 536870912 | bytes 5243904 | tf_op jit(solution)/shard_map/pallas_call | solution.py:402
  19.1 0.0 collective-permute-done.9.rest_2_
  19.1 0.0 collective-permute-done.10.rest_3_
  19.1 0.0 copy-done
  19.1 0.0 copy-done.1
  19.1 0.7 %shard_map.107 = (f32[256,1024]{1,0:T(8,128)S(1)}, f32[2,256]{1,0:T(2,128)S(1)}, bf16[1024,128]{1,0:T(8,128)(2,1)S(1)}) custom-call(s32[1,256]{1,0:T(1,128)S(1)} %get-tuple-element.46.length, bf16[256,2048]{1,0:T(8,128)(2,1)S(1)} %shard_map.103.refs_4_.queries, f32[256,2048]{1,0:T(8,128)S(1)} %shard_map.105.local, bf16[256,2048]{1,0:T(8,128)(2,1)S(1)} %bitcast.10, ...), custom_call_target="tpu_custom_call" | custom-call | flops 67108864 | bytes 6040576 | tf_op jit(solution)/shard_map/pallas_call | solution.py:402
  19.8 1.2 %collective-permute-done.5.rest_0_ = bf16[512,128]{1,0:T(8,128)(2,1)S(1)} collective-permute-done((bf16[512,128]{1,0:T(8,128)(2,1)S(1)}, bf16[512,128]{1,0:T(8,128)(2,1)S(1)}, u32[]{:S(2)}, u32[]{:S(2)}) %collective-permute-start.5) | collective-permute-done | bytes 131104 | tf_op jit(solution)/shard_map/ppermute | solution.py:424
  21.0 0.9 %collective-permute-done.6.rest_2_ = bf16[512,128]{1,0:T(8,128)(2,1)S(1)} collective-permute-done((bf16[512,128]{1,0:T(8,128)(2,1)S(1)}, bf16[512,128]{1,0:T(8,128)(2,1)S(1)}, u32[]{:S(2)}, u32[]{:S(2)}) %collective-permute-start.6) | collective-permute-done | bytes 131104 | tf_op jit(solution)/shard_map/ppermute | solution.py:424
  21.9 0.0 collective-permute-done.7.rest_3_
  21.9 0.7 %shard_map.108 = (f32[256,1024]{1,0:T(8,128)S(1)}, f32[2,256]{1,0:T(2,128)S(1)}, bf16[1024,128]{1,0:T(8,128)(2,1)S(1)}) custom-call(s32[1,256]{1,0:T(1,128)S(1)} %get-tuple-element.46.length, bf16[256,2048]{1,0:T(8,128)(2,1)S(1)} %shard_map.103.refs_4_.queries, f32[256,2048]{1,0:T(8,128)S(1)} %shard_map.105.local, bf16[256,2048]{1,0:T(8,128)(2,1)S(1)} %bitcast.11, ...), custom_call_target="tpu_custom_call" | custom-call | flops 67108864 | bytes 6042624 | tf_op jit(solution)/shard_map/pallas_call | solution.py:402
  22.6 2.7 %collective-permute-start.13 = (f32[2,256]{1,0:T(2,128)S(1)}, f32[2,256]{1,0:T(2,128)S(1)}, u32[]{:S(2)}, u32[]{:S(2)}) collective-permute-start(f32[2,256]{1,0:T(2,128)S(1)} %get-tuple-element.64.rest_0_), channel_id=1, source_target_pairs={{0,16},{8,24},{16,0},{24,8},{1,17},{9,25},{17,1},{25,9},{2,18},{10... | collective-permute-start | bytes 6152 | tf_op jit(solution)/shard_map/ppermute | solution.py:462
  25.2 1.3 %collective-permute-start.12 = (f32[2,256]{1,0:T(2,128)S(1)}, f32[2,256]{1,0:T(2,128)S(1)}, u32[]{:S(2)}, u32[]{:S(2)}) collective-permute-start(f32[2,256]{1,0:T(2,128)S(1)} %get-tuple-element.64.rest_0_), channel_id=1, source_target_pairs={{0,24},{8,16},{16,8},{24,0},{1,25},{9,17},{17,9},{25,1},{2,26},{10... | collective-permute-start | bytes 6152 | tf_op jit(solution)/shard_map/ppermute | solution.py:462
  26.6 0.2 collective-permute-start.11
  26.8 0.3 collective-permute-done.13.rest_3_
  27.1 3.5 %collective-permute-done.12.rest_2_ = f32[2,256]{1,0:T(2,128)S(1)} collective-permute-done((f32[2,256]{1,0:T(2,128)S(1)}, f32[2,256]{1,0:T(2,128)S(1)}, u32[]{:S(2)}, u32[]{:S(2)}) %collective-permute-start.12) | collective-permute-done | bytes 2080 | tf_op jit(solution)/shard_map/ppermute | solution.py:462
  30.6 0.0 collective-permute-done.11.rest_1_
  30.6 1.0 %shard_map.109 = (bf16[256,2048]{1,0:T(8,128)(2,1)S(1)}, f32[1,256]{1,0:T(1,128)S(1)}, bf16[1024,128]{1,0:T(8,128)(2,1)S(1)}, bf16[1024,128]{1,0:T(8,128)(2,1)S(1)}) custom-call(s32[1,256]{1,0:T(1,128)S(1)} %get-tuple-element.46.length, bf16[256,2048]{1,0:T(8,128)(2,1)S(1)} %shard_map.103.refs_4_.queries, bf16[256,2048]{1,0:T(8,128)(2,1)S(1)} %bitcast.12, ...), custom_call_target="tpu_custom_call" | custom-call | flops 134217728 | bytes 5785600 | tf_op jit(solution)/shard_map/pallas_call | solution.py:402
  31.7 0.9 %collective-permute-start.15 = (bf16[1024,128]{1,0:T(8,128)(2,1)S(1)}, bf16[1024,128]{1,0:T(8,128)(2,1)S(1)}, u32[]{:S(2)}, u32[]{:S(2)}) collective-permute-start(bf16[1024,128]{1,0:T(8,128)(2,1)S(1)} %get-tuple-element.75.refs_0_), channel_id=1, source_target_pairs={{0,2},{1,5},{2,0},{3,7},{4,6},{5,1},{6,4},{7,3},{8,10},{9,13},{10,... | collective-permute-start | bytes 786440 | tf_op jit(solution)/shard_map/ppermute | solution.py:424
  32.6 0.0 collective-permute-start.16
  32.6 1.3 %collective-permute-start.14 = (bf16[1024,128]{1,0:T(8,128)(2,1)S(1)}, bf16[1024,128]{1,0:T(8,128)(2,1)S(1)}, u32[]{:S(2)}, u32[]{:S(2)}) collective-permute-start(bf16[1024,128]{1,0:T(8,128)(2,1)S(1)} %get-tuple-element.76), channel_id=1, source_target_pairs={{0,1},{1,0},{2,3},{3,2},{4,5},{5,4},{6,7},{7,6},{8,9},{9,8},{10,11... | collective-permute-start | bytes 786440 | tf_op jit(solution)/shard_map/ppermute | solution.py:424
  33.9 4.8 %shard_map.110 = (bf16[256,2048]{1,0:T(8,128)(2,1)}, bf16[256,2048]{1,0:T(8,128)(2,1)}, f32[256,2048]{1,0:T(8,128)S(1)}, f32[8,128]{1,0:T(8,128)S(1)}) custom-call(s32[1,256]{1,0:T(1,128)S(1)} %get-tuple-element.46.length, f32[1,256]{1,0:T(1,128)S(1)} %get-tuple-element.67.inverse_rms, f32[1,2048]{1,0:T(1,128)S(1)} %bitcast.16, ...), custom_call_target="tpu_custom_call" | custom-call | flops 939524096 | bytes 11024384 | tf_op jit(solution)/shard_map/pallas_call | solution.py:402
  38.6 2.0 %collective-permute-done.15.refs_2_ = bf16[1024,128]{1,0:T(8,128)(2,1)S(1)} collective-permute-done((bf16[1024,128]{1,0:T(8,128)(2,1)S(1)}, bf16[1024,128]{1,0:T(8,128)(2,1)S(1)}, u32[]{:S(2)}, u32[]{:S(2)}) %collective-permute-start.15) | collective-permute-done | bytes 262176 | tf_op jit(solution)/shard_map/ppermute | solution.py:424
  40.6 0.3 collective-permute-done.16.refs_3_
  40.9 0.0 collective-permute-done.14.refs_1_
  40.9 0.6 %shard_map.111 = (bf16[1024,128]{1,0:T(8,128)(2,1)S(1)}, bf16[1024,128]{1,0:T(8,128)(2,1)S(1)}, bf16[512,128]{1,0:T(8,128)(2,1)S(1)}, bf16[512,128]{1,0:T(8,128)...) custom-call(f32[16,128]{1,0:T(8,128)S(1)} %get-tuple-element.74.weights, ...), custom_call_target="tpu_custom_call" | custom-call | bytes 2105344 | tf_op jit(solution)/shard_map/pallas_call | solution.py:402
  41.5 0.1 collective-permute-start.19
  41.6 1.1 %collective-permute-start.20 = (bf16[512,128]{1,0:T(8,128)(2,1)S(1)}, bf16[512,128]{1,0:T(8,128)(2,1)S(1)}, u32[]{:S(2)}, u32[]{:S(2)}) collective-permute-start(bf16[512,128]{1,0:T(8,128)(2,1)S(1)} %get-tuple-element.82), channel_id=1, source_target_pairs={{0,4},{1,3},{2,6},{3,1},{4,0},{5,7},{6,2},{7,5},{8,12},{9,11},{10,... | collective-permute-start | bytes 393224 | tf_op jit(solution)/shard_map/ppermute | solution.py:424
  42.7 1.1 %collective-permute-start.21 = (bf16[512,128]{1,0:T(8,128)(2,1)S(1)}, bf16[512,128]{1,0:T(8,128)(2,1)S(1)}, u32[]{:S(2)}, u32[]{:S(2)}) collective-permute-start(bf16[512,128]{1,0:T(8,128)(2,1)S(1)} %get-tuple-element.83), channel_id=1, source_target_pairs={{0,5},{1,2},{2,7},{3,0},{4,1},{5,6},{6,3},{7,4},{8,13},{9,10},{10,... | collective-permute-start | bytes 393224 | tf_op jit(solution)/shard_map/ppermute | solution.py:424
  43.7 0.6 %collective-permute-start.17 = (bf16[512,128]{1,0:T(8,128)(2,1)S(1)}, bf16[512,128]{1,0:T(8,128)(2,1)S(1)}, u32[]{:S(2)}, u32[]{:S(2)}) collective-permute-start(bf16[512,128]{1,0:T(8,128)(2,1)S(1)} %get-tuple-element.79), channel_id=1, source_target_pairs={{0,4},{1,3},{2,6},{3,1},{4,0},{5,7},{6,2},{7,5},{8,12},{9,11},{10,... | collective-permute-start | bytes 393224 | tf_op jit(solution)/shard_map/ppermute | solution.py:424
  44.3 0.8 %collective-permute-start.18 = (bf16[512,128]{1,0:T(8,128)(2,1)S(1)}, bf16[512,128]{1,0:T(8,128)(2,1)S(1)}, u32[]{:S(2)}, u32[]{:S(2)}) collective-permute-start(bf16[512,128]{1,0:T(8,128)(2,1)S(1)} %get-tuple-element.80), channel_id=1, source_target_pairs={{0,5},{1,2},{2,7},{3,0},{4,1},{5,6},{6,3},{7,4},{8,13},{9,10},{10,... | collective-permute-start | bytes 393224 | tf_op jit(solution)/shard_map/ppermute | solution.py:424
  45.1 1.5 %shard_map.112.value_part = f32[256,2048]{1,0:T(8,128)S(1)} custom-call(s32[1,256]{1,0:T(1,128)S(1)} %get-tuple-element.46.length, bf16[256,2048]{1,0:T(8,128)(2,1)S(1)} %shard_map.103.refs_4_.queries, bf16[256,2048]{1,0:T(8,128)(2,1)S(1)} %get-tuple-element.48.keys, bf16[256,2048]{1,0:T(8,128)(2,1)S(1)} %get-tuple-element.68.rest_0_, ...), custom_call_target="tpu_custom_call" | custom-call | flops 536870912 | bytes 5243904 | tf_op jit(solution)/shard_map/pallas_call | solution.py:402
  46.6 0.0 collective-permute-done.20.rest_0_
  46.6 0.8 %collective-permute-done.21.rest_2_ = bf16[512,128]{1,0:T(8,128)(2,1)S(1)} collective-permute-done((bf16[512,128]{1,0:T(8,128)(2,1)S(1)}, bf16[512,128]{1,0:T(8,128)(2,1)S(1)}, u32[]{:S(2)}, u32[]{:S(2)}) %collective-permute-start.21) | collective-permute-done | bytes 131104 | tf_op jit(solution)/shard_map/ppermute | solution.py:424
  47.5 0.0 collective-permute-done.19.rest_3_
  47.5 1.6 %shard_map.113 = (bf16[256,2048]{1,0:T(8,128)(2,1)}, bf16[256,2048]{1,0:T(8,128)(2,1)}) custom-call(s32[1,256]{1,0:T(1,128)S(1)} %get-tuple-element.46.length, bf16[256,2048]{1,0:T(8,128)(2,1)S(1)} %get-tuple-element.48.keys, bf16[256,2048]{1,0:T(8,128)(2,1)S(1)} %get-tuple-element.49.values, f32[256,2048]{1,0:T(8,128)S(1)} %get-tuple-element.73.key_part, ...), custom_call_target="tpu_custom_call" | custom-call | flops 134217728 | bytes 9176064 | tf_op jit(solution)/shard_map/pallas_call | solution.py:402
  49.1 0.4 collective-permute-done.17.rest_0_
  49.4 0.9 %collective-permute-done.18.rest_2_ = bf16[512,128]{1,0:T(8,128)(2,1)S(1)} collective-permute-done((bf16[512,128]{1,0:T(8,128)(2,1)S(1)}, bf16[512,128]{1,0:T(8,128)(2,1)S(1)}, u32[]{:S(2)}, u32[]{:S(2)}) %collective-permute-start.18) | collective-permute-done | bytes 131104 | tf_op jit(solution)/shard_map/ppermute | solution.py:424
  50.3 1.6 %shard_map.114 = (bf16[256,2048]{1,0:T(8,128)(2,1)}, bf16[256,2048]{1,0:T(8,128)(2,1)}) custom-call(s32[1,256]{1,0:T(1,128)S(1)} %get-tuple-element.46.length, bf16[256,2048]{1,0:T(8,128)(2,1)S(1)} %get-tuple-element.48.keys, bf16[256,2048]{1,0:T(8,128)(2,1)S(1)} %get-tuple-element.49.values, ...), custom_call_target="tpu_custom_call", output_to_operand_aliasing={{0}: (9, {}), {1}: (10, {})} | custom-call | flops 134217728 | bytes 11273216 | tf_op jit(solution)/shard_map/pallas_call | solution.py:402
Async XLA Ops:
  3.6 8.6 %collective-permute-start = (bf16[1024,128]{1,0:T(8,128)(2,1)S(1)}, bf16[1024,128]{1,0:T(8,128)(2,1)S(1)}, u32[]{:S(2)}, u32[]{:S(2)}) collective-permute-start(bf16[1024,128]{1,0:T(8,128)(2,1)S(1)} %get-tuple-element.51), channel_id=1, source_target_pairs={{0,1},{1,0},{2,3},{3,2},{4,5},{5,4},{6,7},{7,6},{8,9},{9,8},{10,11... | collective-permute-start | bytes 786440 | tf_op jit(solution)/shard_map/ppermute | solution.py:424
  4.2 6.0 %collective-permute-start.2 = (bf16[512,128]{1,0:T(8,128)(2,1)S(1)}, bf16[512,128]{1,0:T(8,128)(2,1)S(1)}, u32[]{:S(2)}, u32[]{:S(2)}) collective-permute-start(bf16[512,128]{1,0:T(8,128)(2,1)S(1)} %get-tuple-element.52), channel_id=1, source_target_pairs={{0,5},{1,2},{2,7},{3,0},{4,1},{5,6},{6,3},{7,4},{8,13},{9,10},{10,... | collective-permute-start | bytes 393224 | tf_op jit(solution)/shard_map/ppermute | solution.py:424
  6.8 5.5 %collective-permute-start.1 = (bf16[512,128]{1,0:T(8,128)(2,1)S(1)}, bf16[512,128]{1,0:T(8,128)(2,1)S(1)}, u32[]{:S(2)}, u32[]{:S(2)}) collective-permute-start(bf16[512,128]{1,0:T(8,128)(2,1)S(1)} %get-tuple-element.47._.refs_0_), channel_id=1, source_target_pairs={{0,2},{1,5},{2,0},{3,7},{4,6},{5,1},{6,4},{7,3},{8,10},{9,13},{10,... | collective-permute-start | bytes 393224 | tf_op jit(solution)/shard_map/ppermute | solution.py:424
  8.3 7.4 %collective-permute-start.4 = (bf16[512,128]{1,0:T(8,128)(2,1)S(1)}, bf16[512,128]{1,0:T(8,128)(2,1)S(1)}, u32[]{:S(2)}, u32[]{:S(2)}) collective-permute-start(bf16[512,128]{1,0:T(8,128)(2,1)S(1)} %get-tuple-element.55), channel_id=1, source_target_pairs={{0,5},{1,2},{2,7},{3,0},{4,1},{5,6},{6,3},{7,4},{8,13},{9,10},{10,... | collective-permute-start | bytes 393224 | tf_op jit(solution)/shard_map/ppermute | solution.py:424
  8.3 7.4 %collective-permute-start.3 = (bf16[512,128]{1,0:T(8,128)(2,1)S(1)}, bf16[512,128]{1,0:T(8,128)(2,1)S(1)}, u32[]{:S(2)}, u32[]{:S(2)}) collective-permute-start(bf16[512,128]{1,0:T(8,128)(2,1)S(1)} %get-tuple-element.54.refs_0_), channel_id=1, source_target_pairs={{0,2},{1,5},{2,0},{3,7},{4,6},{5,1},{6,4},{7,3},{8,10},{9,13},{10,... | collective-permute-start | bytes 393224 | tf_op jit(solution)/shard_map/ppermute | solution.py:424
  12.6 5.0 %collective-permute-start.8 = (bf16[512,128]{1,0:T(8,128)(2,1)S(1)}, bf16[512,128]{1,0:T(8,128)(2,1)S(1)}, u32[]{:S(2)}, u32[]{:S(2)}) collective-permute-start(bf16[512,128]{1,0:T(8,128)(2,1)S(1)} %get-tuple-element.60), channel_id=1, source_target_pairs={{0,4},{1,3},{2,6},{3,1},{4,0},{5,7},{6,2},{7,5},{8,12},{9,11},{10,... | collective-permute-start | bytes 393224 | tf_op jit(solution)/shard_map/ppermute | solution.py:424
  13.5 5.6 %collective-permute-start.9 = (bf16[512,128]{1,0:T(8,128)(2,1)S(1)}, bf16[512,128]{1,0:T(8,128)(2,1)S(1)}, u32[]{:S(2)}, u32[]{:S(2)}) collective-permute-start(bf16[512,128]{1,0:T(8,128)(2,1)S(1)} %get-tuple-element.61), channel_id=1, source_target_pairs={{0,5},{1,2},{2,7},{3,0},{4,1},{5,6},{6,3},{7,4},{8,13},{9,10},{10,... | collective-permute-start | bytes 393224 | tf_op jit(solution)/shard_map/ppermute | solution.py:424
  14.4 4.7 %collective-permute-start.10 = (bf16[512,128]{1,0:T(8,128)(2,1)S(1)}, bf16[512,128]{1,0:T(8,128)(2,1)S(1)}, u32[]{:S(2)}, u32[]{:S(2)}) collective-permute-start(bf16[512,128]{1,0:T(8,128)(2,1)S(1)} %get-tuple-element.62), channel_id=1, source_target_pairs={{0,1},{1,0},{2,3},{3,2},{4,5},{5,4},{6,7},{7,6},{8,9},{9,8},{10,11... | collective-permute-start | bytes 393224 | tf_op jit(solution)/shard_map/ppermute | solution.py:424
  16.0 5.0 %collective-permute-start.5 = (bf16[512,128]{1,0:T(8,128)(2,1)S(1)}, bf16[512,128]{1,0:T(8,128)(2,1)S(1)}, u32[]{:S(2)}, u32[]{:S(2)}) collective-permute-start(bf16[512,128]{1,0:T(8,128)(2,1)S(1)} %get-tuple-element.56), channel_id=1, source_target_pairs={{0,4},{1,3},{2,6},{3,1},{4,0},{5,7},{6,2},{7,5},{8,12},{9,11},{10,... | collective-permute-start | bytes 393224 | tf_op jit(solution)/shard_map/ppermute | solution.py:424
  17.5 4.4 %collective-permute-start.6 = (bf16[512,128]{1,0:T(8,128)(2,1)S(1)}, bf16[512,128]{1,0:T(8,128)(2,1)S(1)}, u32[]{:S(2)}, u32[]{:S(2)}) collective-permute-start(bf16[512,128]{1,0:T(8,128)(2,1)S(1)} %get-tuple-element.58), channel_id=1, source_target_pairs={{0,5},{1,2},{2,7},{3,0},{4,1},{5,6},{6,3},{7,4},{8,13},{9,10},{10,... | collective-permute-start | bytes 393224 | tf_op jit(solution)/shard_map/ppermute | solution.py:424
  17.6 4.3 %collective-permute-start.7 = (bf16[512,128]{1,0:T(8,128)(2,1)S(1)}, bf16[512,128]{1,0:T(8,128)(2,1)S(1)}, u32[]{:S(2)}, u32[]{:S(2)}) collective-permute-start(bf16[512,128]{1,0:T(8,128)(2,1)S(1)} %get-tuple-element.59), channel_id=1, source_target_pairs={{0,1},{1,0},{2,3},{3,2},{4,5},{5,4},{6,7},{7,6},{8,9},{9,8},{10,11... | collective-permute-start | bytes 393224 | tf_op jit(solution)/shard_map/ppermute | solution.py:424
  17.6 1.5 %copy-start = (bf16[1,256,2048]{2,1,0:T(8,128)(2,1)S(1)}, bf16[1,256,2048]{2,1,0:T(8,128)(2,1)}, u32[]{:S(2)}) copy-start(bf16[1,256,2048]{2,1,0:T(8,128)(2,1)} %param.10) | copy-start | bytes 3145732
  17.6 1.5 %copy-start.1 = (f32[2048]{0:T(1024)S(1)}, f32[2048]{0:T(1024)}, u32[]{:S(2)}) copy-start(f32[2048]{0:T(1024)} %param.11) | copy-start | bytes 24580
  22.6 4.5 %collective-permute-start.13 = (f32[2,256]{1,0:T(2,128)S(1)}, f32[2,256]{1,0:T(2,128)S(1)}, u32[]{:S(2)}, u32[]{:S(2)}) collective-permute-start(f32[2,256]{1,0:T(2,128)S(1)} %get-tuple-element.64.rest_0_), channel_id=1, source_target_pairs={{0,16},{8,24},{16,0},{24,8},{1,17},{9,25},{17,1},{25,9},{2,18},{10... | collective-permute-start | bytes 6152 | tf_op jit(solution)/shard_map/ppermute | solution.py:462
  25.2 5.4 %collective-permute-start.12 = (f32[2,256]{1,0:T(2,128)S(1)}, f32[2,256]{1,0:T(2,128)S(1)}, u32[]{:S(2)}, u32[]{:S(2)}) collective-permute-start(f32[2,256]{1,0:T(2,128)S(1)} %get-tuple-element.64.rest_0_), channel_id=1, source_target_pairs={{0,24},{8,16},{16,8},{24,0},{1,25},{9,17},{17,9},{25,1},{2,26},{10... | collective-permute-start | bytes 6152 | tf_op jit(solution)/shard_map/ppermute | solution.py:462
  26.6 4.0 %collective-permute-start.11 = (f32[2,256]{1,0:T(2,128)S(1)}, f32[2,256]{1,0:T(2,128)S(1)}, u32[]{:S(2)}, u32[]{:S(2)}) collective-permute-start(f32[2,256]{1,0:T(2,128)S(1)} %get-tuple-element.64.rest_0_), channel_id=1, source_target_pairs={{0,8},{8,0},{16,24},{24,16},{1,9},{9,1},{17,25},{25,17},{2,10},{10... | collective-permute-start | bytes 6152 | tf_op jit(solution)/shard_map/ppermute | solution.py:462
  31.7 8.9 %collective-permute-start.15 = (bf16[1024,128]{1,0:T(8,128)(2,1)S(1)}, bf16[1024,128]{1,0:T(8,128)(2,1)S(1)}, u32[]{:S(2)}, u32[]{:S(2)}) collective-permute-start(bf16[1024,128]{1,0:T(8,128)(2,1)S(1)} %get-tuple-element.75.refs_0_), channel_id=1, source_target_pairs={{0,2},{1,5},{2,0},{3,7},{4,6},{5,1},{6,4},{7,3},{8,10},{9,13},{10,... | collective-permute-start | bytes 786440 | tf_op jit(solution)/shard_map/ppermute | solution.py:424
  32.6 8.3 %collective-permute-start.16 = (bf16[1024,128]{1,0:T(8,128)(2,1)S(1)}, bf16[1024,128]{1,0:T(8,128)(2,1)S(1)}, u32[]{:S(2)}, u32[]{:S(2)}) collective-permute-start(bf16[1024,128]{1,0:T(8,128)(2,1)S(1)} %get-tuple-element.76), channel_id=1, source_target_pairs={{0,5},{1,2},{2,7},{3,0},{4,1},{5,6},{6,3},{7,4},{8,13},{9,10},{10,... | collective-permute-start | bytes 786440 | tf_op jit(solution)/shard_map/ppermute | solution.py:424
  32.6 8.3 %collective-permute-start.14 = (bf16[1024,128]{1,0:T(8,128)(2,1)S(1)}, bf16[1024,128]{1,0:T(8,128)(2,1)S(1)}, u32[]{:S(2)}, u32[]{:S(2)}) collective-permute-start(bf16[1024,128]{1,0:T(8,128)(2,1)S(1)} %get-tuple-element.76), channel_id=1, source_target_pairs={{0,1},{1,0},{2,3},{3,2},{4,5},{5,4},{6,7},{7,6},{8,9},{9,8},{10,11... | collective-permute-start | bytes 786440 | tf_op jit(solution)/shard_map/ppermute | solution.py:424
  41.5 6.0 %collective-permute-start.19 = (bf16[1024,128]{1,0:T(8,128)(2,1)S(1)}, bf16[1024,128]{1,0:T(8,128)(2,1)S(1)}, u32[]{:S(2)}, u32[]{:S(2)}) collective-permute-start(bf16[1024,128]{1,0:T(8,128)(2,1)S(1)} %get-tuple-element.81), channel_id=1, source_target_pairs={{0,1},{1,0},{2,3},{3,2},{4,5},{5,4},{6,7},{7,6},{8,9},{9,8},{10,11... | collective-permute-start | bytes 786440 | tf_op jit(solution)/shard_map/ppermute | solution.py:424
  41.6 5.0 %collective-permute-start.20 = (bf16[512,128]{1,0:T(8,128)(2,1)S(1)}, bf16[512,128]{1,0:T(8,128)(2,1)S(1)}, u32[]{:S(2)}, u32[]{:S(2)}) collective-permute-start(bf16[512,128]{1,0:T(8,128)(2,1)S(1)} %get-tuple-element.82), channel_id=1, source_target_pairs={{0,4},{1,3},{2,6},{3,1},{4,0},{5,7},{6,2},{7,5},{8,12},{9,11},{10,... | collective-permute-start | bytes 393224 | tf_op jit(solution)/shard_map/ppermute | solution.py:424
  42.7 4.8 %collective-permute-start.21 = (bf16[512,128]{1,0:T(8,128)(2,1)S(1)}, bf16[512,128]{1,0:T(8,128)(2,1)S(1)}, u32[]{:S(2)}, u32[]{:S(2)}) collective-permute-start(bf16[512,128]{1,0:T(8,128)(2,1)S(1)} %get-tuple-element.83), channel_id=1, source_target_pairs={{0,5},{1,2},{2,7},{3,0},{4,1},{5,6},{6,3},{7,4},{8,13},{9,10},{10,... | collective-permute-start | bytes 393224 | tf_op jit(solution)/shard_map/ppermute | solution.py:424
  43.7 5.7 %collective-permute-start.17 = (bf16[512,128]{1,0:T(8,128)(2,1)S(1)}, bf16[512,128]{1,0:T(8,128)(2,1)S(1)}, u32[]{:S(2)}, u32[]{:S(2)}) collective-permute-start(bf16[512,128]{1,0:T(8,128)(2,1)S(1)} %get-tuple-element.79), channel_id=1, source_target_pairs={{0,4},{1,3},{2,6},{3,1},{4,0},{5,7},{6,2},{7,5},{8,12},{9,11},{10,... | collective-permute-start | bytes 393224 | tf_op jit(solution)/shard_map/ppermute | solution.py:424
  44.3 6.0 %collective-permute-start.18 = (bf16[512,128]{1,0:T(8,128)(2,1)S(1)}, bf16[512,128]{1,0:T(8,128)(2,1)S(1)}, u32[]{:S(2)}, u32[]{:S(2)}) collective-permute-start(bf16[512,128]{1,0:T(8,128)(2,1)S(1)} %get-tuple-element.80), channel_id=1, source_target_pairs={{0,5},{1,2},{2,7},{3,0},{4,1},{5,6},{6,3},{7,4},{8,13},{9,10},{10,... | collective-permute-start | bytes 393224 | tf_op jit(solution)/shard_map/ppermute | solution.py:424

commit v11 on v9

--- a/solution.py
+++ b/solution.py
@@ -195,13 +195,15 @@
     return lax.broadcasted_iota(jnp.int32, (rows, HD), 0) < length[:, :HD]
 
 
-def keep_mask(length, turned):
+def write_mask(length, keep, turned):
     rows = length.shape[1]
     first = lax.broadcasted_iota(jnp.int32, (rows, rows), 0)
     second = lax.broadcasted_iota(jnp.int32, (rows, rows), 1)
     if turned:
-        return (first <= second) & (first < length[...])
-    return (second <= first) & (second < length[...])
+        used = (first <= second) & (first < length[...])
+    else:
+        used = (second <= first) & (second < length[...])
+    keep[...] = jnp.where(used, 1.0, 0.0).astype(BF16)
 
 
 def split_refs(refs, *counts):
@@ -226,11 +228,11 @@
 
 
 def local_kernel(heads, length, queries, keys, values, *rest):
-    local = rest[-1]
-    keep = keep_mask(length, False)
+    local, keep = rest[-2:]
+    write_mask(length, keep, False)
     for head in range(heads):
         cols = head_cols(head)
-        scores = jnp.where(keep, nt(queries[:, cols], keys[:, cols]), 0.0).astype(BF16)
+        scores = nt(queries[:, cols], keys[:, cols]).astype(BF16) * keep[...]
         local[:, cols] = nn(scores, values[:, cols])
 
 
@@ -309,9 +311,10 @@
 def query_kernel(heads, group, scale, length, inverse_rms, gain, queries, keys, values, *rest):
     sizes = (BACKWARD_PIECES, FORWARD_PIECES, FORWARD_PIECES)
     grads, attention, prefix, rest = split_refs(rest, *sizes, len(rest) - sum(sizes))
-    attended_hbm, query_hbm, attended, query_grad, key_part, token, sems = rest
+    attended_hbm, query_hbm, key_part, token, attended, query_grad, keep, keep_turned, sems = rest
     token[...] = jnp.zeros_like(token)
-    keep = keep_mask(length, False)
+    write_mask(length, keep, False)
+    write_mask(length, keep_turned, True)
     inverse = token_columns(inverse_rms[...])
     copies = []
     for head in range(heads):
@@ -321,12 +324,13 @@
         out_piece, at = head_of(attention, head)
         per_piece = heads // FORWARD_PIECES
         prefix_piece, state = prefix[head // per_piece], head % per_piece
-        grad_scores = jnp.where(keep, nt(grad, values[:, cols]), 0.0).astype(BF16)
+        grad_scores = nt(grad, values[:, cols]).astype(BF16) * keep[...]
         carried = nt(grad, prefix_piece[state * HD : (state + 1) * HD, :])
         query_grad[:, cols] = (scale * (carried + nn(grad_scores, keys[:, cols]))).astype(BF16)
-        key_part[:, cols] = scale * tn(grad_scores, queries[:, cols])
+        turned = nt(values[:, cols], grad).astype(BF16) * keep_turned[...]
+        key_part[:, cols] = scale * nn(turned, queries[:, cols])
         attended[:, cols] = (out_piece[:, at] * inverse * gain[:, cols]).astype(BF16)
-        if (head + 1) % group == 0 and head + 1 < heads:
+        if (head + 1) % group == 0:
             step = head // group
             some = column_copies(
                 (attended, query_grad), (attended_hbm, query_hbm), step * group, group, sems.at[step]
@@ -338,19 +342,14 @@
         copy.wait()
 
 
-def value_kernel(heads, group, scale, length, queries, keys, attended, query_grad, *rest):
-    grads, (attended_hbm, query_hbm, value_part, sems) = rest[:BACKWARD_PIECES], rest[-4:]
-    copies = column_copies((attended, query_grad), (attended_hbm, query_hbm), heads - group, group, sems)
-    for copy in copies:
-        copy.start()
-    keep = keep_mask(length, True)
+def value_kernel(heads, scale, length, queries, keys, *rest):
+    grads, (value_part, keep) = rest[:BACKWARD_PIECES], rest[-2:]
+    write_mask(length, keep, True)
     for head in range(heads):
         cols = head_cols(head)
         grad_piece, at = head_of(grads, head)
-        turned = jnp.where(keep, nt(keys[:, cols], queries[:, cols]), 0.0).astype(BF16)
+        turned = nt(keys[:, cols], queries[:, cols]).astype(BF16) * keep[...]
         value_part[:, cols] = scale * nn(turned, grad_piece[:, at])
-    for copy in copies:
-        copy.wait()
 
 
 def final_kernel(piece, grid, counts, length, keys, values, key_part, value_part, *rest):
@@ -459,6 +458,7 @@
     members = line_length(grid) * pair
     weight_rows = shape((members * members, HD), F32)
     sems = pltpu.SemaphoreType.DMA((2, heads))
+    mask = pltpu.VMEM((rows, rows), BF16)
     counts = [line_length(grid)] * pair
     unit = 2 * heads * rows * HD
 
@@ -486,7 +486,7 @@
         mixed.append(mix(gather_line(part, grid), up, 0, 1, () if mixed else (query,)))
     (local,) = call(
         functools.partial(local_kernel, heads),
-        [wide], (length, query, key, value), (), unit * rows * 2, after=(mixed[0][0],),
+        [wide], (length, query, key, value), [mask], unit * rows * 2, after=(mixed[0][0],),
     )
     attention, prefix, sums = [], [], []
     width = features // FORWARD_PIECES
@@ -513,24 +513,21 @@
         grads.append(grad_out)
         state_grad.append(parts)
     group = 4 if heads % 4 == 0 else 1
-    attended, query_grad, attended_rest, query_rest, key_part, token = call(
+    attended, query_grad, key_part, token = call(
         functools.partial(query_kernel, heads, group, scale),
-        [narrow, narrow, narrow, narrow, wide, shape((8, HD), F32)],
+        [narrow, narrow, wide, shape((8, HD), F32)],
         (length, inverse_rms, gain, query, key, value, *grads, *attention, *prefix),
-        [pltpu.SemaphoreType.DMA((heads // group, 2))], unit * (3 * rows + HD),
-        out_specs=[HBM, HBM] + [VMEM] * 4,
+        [pltpu.VMEM(narrow.shape, BF16)] * 2 + [mask] * 2 + [pltpu.SemaphoreType.DMA((heads // group, 2))],
+        unit * (4 * rows + HD), out_specs=[HBM, HBM, VMEM, VMEM],
     )
     (part,) = state_grad
     arrived = gather_line(part, grid)
     mixed = []
     for piece in range(RETURN_PIECES):
         mixed.append(mix(arrived, down, piece, RETURN_PIECES, (token, *mixed[-1][:1]) if mixed else (token,)))
-    operands = (length, query, key, attended_rest, query_rest, *grads, attended, query_grad)
-    last = len(operands) - 2
-    attended, query_grad, value_part = call(
-        functools.partial(value_kernel, heads, group, scale),
-        [narrow, narrow, wide], operands, [pltpu.SemaphoreType.DMA((2,))], unit * 2 * rows, (last, last + 1),
-        after=(mixed[-1][0],), out_specs=[HBM, HBM, VMEM], aliases={last: 0, last + 1: 1},
+    (value_part,) = call(
+        functools.partial(value_kernel, heads, scale),
+        [wide], (length, query, key, *grads), [mask], unit * 2 * rows, after=(mixed[-1][0],),
     )
     results = []
     width = features // RETURN_PIECES

time: 50.2 us -> 50.1 us (level)
  no operation moved by 1% of the time
where the time goes in v11:
time: 50.1 us; the launch traced here: 50 us
  starting transfers between devices  20.8 us (42%)
  Pallas kernels  18.4 us (37%)
  waiting for transfers between devices  9.15 us (18%)
  between operations  1.61 us (3%)
    pallas_call x14, Pallas kernels, call(): pl.pallas_call(kernel, out_shape=out_shape, in_specs=specs + [ANY] * len(...  18.4 us
    ppermute x21, starting transfers between devices, line_send(): return lax.ppermute(block, 'seg', moves)  16.5 us
    ppermute x21, waiting for transfers between devices, line_send(): return lax.ppermute(block, 'seg', moves)  5.35 us
    ppermute x3, starting transfers between devices, token_sums(): parts.append(lax.ppermute(sums, 'head', moves))  4.23 us
    ppermute x3, waiting for transfers between devices, token_sums(): parts.append(lax.ppermute(sums, 'head', moves))  3.8 us
  transfers between devices with their start and end apart: 24, of which 10 were waited for; matrix products, arithmetic and copies ran while one was open for 0% of the time, Pallas kernels for 25%

profile of v11, /device:TPU:0, one launch (start us, length us, event | category | flops | bytes accessed | tf_op | source)
XLA Modules:
  0.0 50.0 jit_solution(3961948730813517849)
XLA Ops:
  1.3 2.3 %shard_map.102 = (bf16[256,2048]{1,0:T(8,128)(2,1)S(1)}, bf16[256,2048]{1,0:T(8,128)(2,1)S(1)}, s32[1,256]{1,0:T(1,128)S(1)}, f32[16,128]{1,0:T(8,128)S(1)}, f32...) custom-call(s32[1]{0:T(128)S(6)} %copy.15.seg_len, ...), custom_call_target="tpu_custom_call" | custom-call | flops 134217728 | bytes 4736036 | tf_op jit(solution)/shard_map/pallas_call | solution.py:393
  3.6 2.5 %collective-permute-start.2 = (bf16[512,128]{1,0:T(8,128)(2,1)S(1)}, bf16[512,128]{1,0:T(8,128)(2,1)S(1)}, u32[]{:S(2)}, u32[]{:S(2)}) collective-permute-start(bf16[512,128]{1,0:T(8,128)(2,1)S(1)} %get-tuple-element.52), channel_id=1, source_target_pairs={{0,5},{1,2},{2,7},{3,0},{4,1},{5,6},{6,3},{7,4},{8,13},{9,10},{10,... | collective-permute-start | bytes 393224 | tf_op jit(solution)/shard_map/ppermute | solution.py:415
  6.1 0.6 %collective-permute-start = (bf16[512,128]{1,0:T(8,128)(2,1)S(1)}, bf16[512,128]{1,0:T(8,128)(2,1)S(1)}, u32[]{:S(2)}, u32[]{:S(2)}) collective-permute-start(bf16[512,128]{1,0:T(8,128)(2,1)S(1)} %get-tuple-element.52), channel_id=1, source_target_pairs={{0,1},{1,0},{2,3},{3,2},{4,5},{5,4},{6,7},{7,6},{8,9},{9,8},{10,11... | collective-permute-start | bytes 393224 | tf_op jit(solution)/shard_map/ppermute | solution.py:415
  6.7 0.9 %collective-permute-start.1 = (bf16[512,128]{1,0:T(8,128)(2,1)S(1)}, bf16[512,128]{1,0:T(8,128)(2,1)S(1)}, u32[]{:S(2)}, u32[]{:S(2)}) collective-permute-start(bf16[512,128]{1,0:T(8,128)(2,1)S(1)} %get-tuple-element.48._.refs_0_), channel_id=1, source_target_pairs={{0,2},{1,5},{2,0},{3,7},{4,6},{5,1},{6,4},{7,3},{8,10},{9,13},{10,... | collective-permute-start | bytes 393224 | tf_op jit(solution)/shard_map/ppermute | solution.py:415
  7.6 1.2 %collective-permute-start.4 = (bf16[512,128]{1,0:T(8,128)(2,1)S(1)}, bf16[512,128]{1,0:T(8,128)(2,1)S(1)}, u32[]{:S(2)}, u32[]{:S(2)}) collective-permute-start(bf16[512,128]{1,0:T(8,128)(2,1)S(1)} %get-tuple-element.54.refs_0_), channel_id=1, source_target_pairs={{0,2},{1,5},{2,0},{3,7},{4,6},{5,1},{6,4},{7,3},{8,10},{9,13},{10,... | collective-permute-start | bytes 393224 | tf_op jit(solution)/shard_map/ppermute | solution.py:415
  8.8 0.6 %collective-permute-start.5 = (bf16[512,128]{1,0:T(8,128)(2,1)S(1)}, bf16[512,128]{1,0:T(8,128)(2,1)S(1)}, u32[]{:S(2)}, u32[]{:S(2)}) collective-permute-start(bf16[512,128]{1,0:T(8,128)(2,1)S(1)} %get-tuple-element.55), channel_id=1, source_target_pairs={{0,5},{1,2},{2,7},{3,0},{4,1},{5,6},{6,3},{7,4},{8,13},{9,10},{10,... | collective-permute-start | bytes 393224 | tf_op jit(solution)/shard_map/ppermute | solution.py:415
  9.3 1.2 %shard_map.103.refs_4_.queries = bf16[256,2048]{1,0:T(8,128)(2,1)S(1)} custom-call(bf16[256,2048]{1,0:T(8,128)(2,1)} %bitcast.19, bf16[512,128]{1,0:T(8,128)(2,1)S(1)} %get-tuple-element.48._.refs_0_), custom_call_target="tpu_custom_call" | custom-call | bytes 2097152 | tf_op jit(solution)/shard_map/pallas_call | solution.py:393
  10.6 0.0 collective-permute-done.2.refs_3_
  10.6 0.5 collective-permute-start.3
  11.1 0.0 collective-permute-done.refs_1_
  11.1 0.6 %collective-permute-done.1.refs_2_ = bf16[512,128]{1,0:T(8,128)(2,1)S(1)} collective-permute-done((bf16[512,128]{1,0:T(8,128)(2,1)S(1)}, bf16[512,128]{1,0:T(8,128)(2,1)S(1)}, u32[]{:S(2)}, u32[]{:S(2)}) %collective-permute-start.1) | collective-permute-done | bytes 131104 | tf_op jit(solution)/shard_map/ppermute | solution.py:415
  11.7 0.3 shard_map.104
  12.0 1.6 %collective-permute-start.9 = (bf16[512,128]{1,0:T(8,128)(2,1)S(1)}, bf16[512,128]{1,0:T(8,128)(2,1)S(1)}, u32[]{:S(2)}, u32[]{:S(2)}) collective-permute-start(bf16[512,128]{1,0:T(8,128)(2,1)S(1)} %get-tuple-element.60), channel_id=1, source_target_pairs={{0,4},{1,3},{2,6},{3,1},{4,0},{5,7},{6,2},{7,5},{8,12},{9,11},{10,... | collective-permute-start | bytes 393224 | tf_op jit(solution)/shard_map/ppermute | solution.py:415
  13.6 0.4 collective-permute-start.10
  14.0 0.4 collective-permute-done.4.refs_2_
  14.4 0.1 collective-permute-start.11
  14.5 0.0 collective-permute-done.5.refs_3_
  14.5 0.0 collective-permute-done.3.refs_1_
  14.5 0.3 shard_map.106
  14.8 1.6 %collective-permute-start.6 = (bf16[512,128]{1,0:T(8,128)(2,1)S(1)}, bf16[512,128]{1,0:T(8,128)(2,1)S(1)}, u32[]{:S(2)}, u32[]{:S(2)}) collective-permute-start(bf16[512,128]{1,0:T(8,128)(2,1)S(1)} %get-tuple-element.56), channel_id=1, source_target_pairs={{0,4},{1,3},{2,6},{3,1},{4,0},{5,7},{6,2},{7,5},{8,12},{9,11},{10,... | collective-permute-start | bytes 393224 | tf_op jit(solution)/shard_map/ppermute | solution.py:415
  16.4 0.6 %collective-permute-start.7 = (bf16[512,128]{1,0:T(8,128)(2,1)S(1)}, bf16[512,128]{1,0:T(8,128)(2,1)S(1)}, u32[]{:S(2)}, u32[]{:S(2)}) collective-permute-start(bf16[512,128]{1,0:T(8,128)(2,1)S(1)} %get-tuple-element.58), channel_id=1, source_target_pairs={{0,5},{1,2},{2,7},{3,0},{4,1},{5,6},{6,3},{7,4},{8,13},{9,10},{10,... | collective-permute-start | bytes 393224 | tf_op jit(solution)/shard_map/ppermute | solution.py:415
  16.9 0.1 collective-permute-done.9.rest_0_
  17.0 0.3 collective-permute-start.8
  17.3 1.5 %shard_map.105.local = f32[256,2048]{1,0:T(8,128)S(1)} custom-call(s32[1,256]{1,0:T(1,128)S(1)} %get-tuple-element.47.length, bf16[256,2048]{1,0:T(8,128)(2,1)S(1)} %shard_map.103.refs_4_.queries, bf16[256,2048]{1,0:T(8,128)(2,1)S(1)} %get-tuple-element.49.keys, bf16[256,2048]{1,0:T(8,128)(2,1)S(1)} %get-tuple-element.50.values, ...), custom_call_target="tpu_custom_call" | custom-call | flops 536870912 | bytes 5243904 | tf_op jit(solution)/shard_map/pallas_call | solution.py:393
  18.8 0.0 collective-permute-done.10.rest_2_
  18.8 0.0 collective-permute-done.11.rest_3_
  18.9 0.0 copy-done
  18.9 0.0 copy-done.1
  18.9 0.7 %shard_map.107 = (f32[256,1024]{1,0:T(8,128)S(1)}, f32[2,256]{1,0:T(2,128)S(1)}, bf16[1024,128]{1,0:T(8,128)(2,1)S(1)}) custom-call(s32[1,256]{1,0:T(1,128)S(1)} %get-tuple-element.47.length, bf16[256,2048]{1,0:T(8,128)(2,1)S(1)} %shard_map.103.refs_4_.queries, f32[256,2048]{1,0:T(8,128)S(1)} %shard_map.105.local, bf16[256,2048]{1,0:T(8,128)(2,1)S(1)} %bitcast.10, ...), custom_call_target="tpu_custom_call" | custom-call | flops 67108864 | bytes 6040576 | tf_op jit(solution)/shard_map/pallas_call | solution.py:393
  19.5 0.3 collective-permute-done.6.rest_0_
  19.8 0.9 %collective-permute-done.7.rest_2_ = bf16[512,128]{1,0:T(8,128)(2,1)S(1)} collective-permute-done((bf16[512,128]{1,0:T(8,128)(2,1)S(1)}, bf16[512,128]{1,0:T(8,128)(2,1)S(1)}, u32[]{:S(2)}, u32[]{:S(2)}) %collective-permute-start.7) | collective-permute-done | bytes 131104 | tf_op jit(solution)/shard_map/ppermute | solution.py:415
  20.8 0.0 collective-permute-done.8.rest_3_
  20.8 0.7 %shard_map.108 = (f32[256,1024]{1,0:T(8,128)S(1)}, f32[2,256]{1,0:T(2,128)S(1)}, bf16[1024,128]{1,0:T(8,128)(2,1)S(1)}) custom-call(s32[1,256]{1,0:T(1,128)S(1)} %get-tuple-element.47.length, bf16[256,2048]{1,0:T(8,128)(2,1)S(1)} %shard_map.103.refs_4_.queries, f32[256,2048]{1,0:T(8,128)S(1)} %shard_map.105.local, bf16[256,2048]{1,0:T(8,128)(2,1)S(1)} %bitcast.11, ...), custom_call_target="tpu_custom_call" | custom-call | flops 67108864 | bytes 6042624 | tf_op jit(solution)/shard_map/pallas_call | solution.py:393
  21.5 2.7 %collective-permute-start.14 = (f32[2,256]{1,0:T(2,128)S(1)}, f32[2,256]{1,0:T(2,128)S(1)}, u32[]{:S(2)}, u32[]{:S(2)}) collective-permute-start(f32[2,256]{1,0:T(2,128)S(1)} %get-tuple-element.64.rest_0_), channel_id=1, source_target_pairs={{0,16},{8,24},{16,0},{24,8},{1,17},{9,25},{17,1},{25,9},{2,18},{10... | collective-permute-start | bytes 6152 | tf_op jit(solution)/shard_map/ppermute | solution.py:442
  24.1 1.3 %collective-permute-start.13 = (f32[2,256]{1,0:T(2,128)S(1)}, f32[2,256]{1,0:T(2,128)S(1)}, u32[]{:S(2)}, u32[]{:S(2)}) collective-permute-start(f32[2,256]{1,0:T(2,128)S(1)} %get-tuple-element.64.rest_0_), channel_id=1, source_target_pairs={{0,24},{8,16},{16,8},{24,0},{1,25},{9,17},{17,9},{25,1},{2,26},{10... | collective-permute-start | bytes 6152 | tf_op jit(solution)/shard_map/ppermute | solution.py:442
  25.5 0.2 collective-permute-start.12
  25.7 0.3 collective-permute-done.14.rest_3_
  26.0 3.5 %collective-permute-done.13.rest_2_ = f32[2,256]{1,0:T(2,128)S(1)} collective-permute-done((f32[2,256]{1,0:T(2,128)S(1)}, f32[2,256]{1,0:T(2,128)S(1)}, u32[]{:S(2)}, u32[]{:S(2)}) %collective-permute-start.13) | collective-permute-done | bytes 2080 | tf_op jit(solution)/shard_map/ppermute | solution.py:442
  29.5 0.0 collective-permute-done.12.rest_1_
  29.5 1.0 %shard_map.109 = (bf16[256,2048]{1,0:T(8,128)(2,1)S(1)}, f32[1,256]{1,0:T(1,128)S(1)}, bf16[1024,128]{1,0:T(8,128)(2,1)S(1)}, bf16[1024,128]{1,0:T(8,128)(2,1)S(1)}) custom-call(s32[1,256]{1,0:T(1,128)S(1)} %get-tuple-element.47.length, bf16[256,2048]{1,0:T(8,128)(2,1)S(1)} %shard_map.103.refs_4_.queries, bf16[256,2048]{1,0:T(8,128)(2,1)S(1)} %bitcast.12, ...), custom_call_target="tpu_custom_call" | custom-call | flops 134217728 | bytes 5785600 | tf_op jit(solution)/shard_map/pallas_call | solution.py:393
  30.6 0.1 collective-permute-start.17
  30.6 1.0 %collective-permute-start.15 = (bf16[1024,128]{1,0:T(8,128)(2,1)S(1)}, bf16[1024,128]{1,0:T(8,128)(2,1)S(1)}, u32[]{:S(2)}, u32[]{:S(2)}) collective-permute-start(bf16[1024,128]{1,0:T(8,128)(2,1)S(1)} %get-tuple-element.76), channel_id=1, source_target_pairs={{0,1},{1,0},{2,3},{3,2},{4,5},{5,4},{6,7},{7,6},{8,9},{9,8},{10,11... | collective-permute-start | bytes 786440 | tf_op jit(solution)/shard_map/ppermute | solution.py:415
  31.6 1.2 %collective-permute-start.16 = (bf16[1024,128]{1,0:T(8,128)(2,1)S(1)}, bf16[1024,128]{1,0:T(8,128)(2,1)S(1)}, u32[]{:S(2)}, u32[]{:S(2)}) collective-permute-start(bf16[1024,128]{1,0:T(8,128)(2,1)S(1)} %get-tuple-element.75.refs_0_), channel_id=1, source_target_pairs={{0,2},{1,5},{2,0},{3,7},{4,6},{5,1},{6,4},{7,3},{8,10},{9,13},{10,... | collective-permute-start | bytes 786440 | tf_op jit(solution)/shard_map/ppermute | solution.py:415
  32.7 5.2 %shard_map.110 = (bf16[256,2048]{1,0:T(8,128)(2,1)}, bf16[256,2048]{1,0:T(8,128)(2,1)}, f32[256,2048]{1,0:T(8,128)S(1)}, f32[8,128]{1,0:T(8,128)S(1)}) custom-call(s32[1,256]{1,0:T(1,128)S(1)} %get-tuple-element.47.length, f32[1,256]{1,0:T(1,128)S(1)} %get-tuple-element.67.inverse_rms, f32[1,2048]{1,0:T(1,128)S(1)} %bitcast.16, ...), custom_call_target="tpu_custom_call" | custom-call | flops 1207959552 | bytes 11024384 | tf_op jit(solution)/shard_map/pallas_call | solution.py:393
  37.9 0.0 collective-permute-done.17.refs_3_
  38.0 0.0 collective-permute-done.15.refs_1_
  38.0 1.2 %collective-permute-done.16.refs_2_ = bf16[1024,128]{1,0:T(8,128)(2,1)S(1)} collective-permute-done((bf16[1024,128]{1,0:T(8,128)(2,1)S(1)}, bf16[1024,128]{1,0:T(8,128)(2,1)S(1)}, u32[]{:S(2)}, u32[]{:S(2)}) %collective-permute-start.16) | collective-permute-done | bytes 262176 | tf_op jit(solution)/shard_map/ppermute | solution.py:415
  39.2 0.3 shard_map.111
  39.5 1.5 %collective-permute-start.21 = (bf16[512,128]{1,0:T(8,128)(2,1)S(1)}, bf16[512,128]{1,0:T(8,128)(2,1)S(1)}, u32[]{:S(2)}, u32[]{:S(2)}) collective-permute-start(bf16[512,128]{1,0:T(8,128)(2,1)S(1)} %get-tuple-element.83), channel_id=1, source_target_pairs={{0,4},{1,3},{2,6},{3,1},{4,0},{5,7},{6,2},{7,5},{8,12},{9,11},{10,... | collective-permute-start | bytes 393224 | tf_op jit(solution)/shard_map/ppermute | solution.py:415
  41.0 0.0 collective-permute-start.22
  41.0 0.9 %collective-permute-start.23 = (bf16[512,128]{1,0:T(8,128)(2,1)S(1)}, bf16[512,128]{1,0:T(8,128)(2,1)S(1)}, u32[]{:S(2)}, u32[]{:S(2)}) collective-permute-start(bf16[512,128]{1,0:T(8,128)(2,1)S(1)} %get-tuple-element.85), channel_id=1, source_target_pairs={{0,1},{1,0},{2,3},{3,2},{4,5},{5,4},{6,7},{7,6},{8,9},{9,8},{10,11... | collective-permute-start | bytes 393224 | tf_op jit(solution)/shard_map/ppermute | solution.py:415
  41.9 0.3 shard_map.112
  42.2 0.7 %collective-permute-start.18 = (bf16[512,128]{1,0:T(8,128)(2,1)S(1)}, bf16[512,128]{1,0:T(8,128)(2,1)S(1)}, u32[]{:S(2)}, u32[]{:S(2)}) collective-permute-start(bf16[512,128]{1,0:T(8,128)(2,1)S(1)} %get-tuple-element.80), channel_id=1, source_target_pairs={{0,4},{1,3},{2,6},{3,1},{4,0},{5,7},{6,2},{7,5},{8,12},{9,11},{10,... | collective-permute-start | bytes 393224 | tf_op jit(solution)/shard_map/ppermute | solution.py:415
  42.9 0.5 collective-permute-start.19
  43.4 1.1 %collective-permute-done.21.rest_0_ = bf16[512,128]{1,0:T(8,128)(2,1)S(1)} collective-permute-done((bf16[512,128]{1,0:T(8,128)(2,1)S(1)}, bf16[512,128]{1,0:T(8,128)(2,1)S(1)}, u32[]{:S(2)}, u32[]{:S(2)}) %collective-permute-start.21) | collective-permute-done | bytes 131104 | tf_op jit(solution)/shard_map/ppermute | solution.py:415
  44.5 0.0 collective-permute-start.20
  44.5 1.5 %shard_map.113.value_part = f32[256,2048]{1,0:T(8,128)S(1)} custom-call(s32[1,256]{1,0:T(1,128)S(1)} %get-tuple-element.47.length, bf16[256,2048]{1,0:T(8,128)(2,1)S(1)} %shard_map.103.refs_4_.queries, bf16[256,2048]{1,0:T(8,128)(2,1)S(1)} %get-tuple-element.49.keys, bf16[256,2048]{1,0:T(8,128)(2,1)S(1)} %get-tuple-element.68.rest_0_, ...), custom_call_target="tpu_custom_call" | custom-call | flops 536870912 | bytes 5243904 | tf_op jit(solution)/shard_map/pallas_call | solution.py:393
  46.0 0.0 collective-permute-done.22.rest_2_
  46.0 0.0 collective-permute-done.23.rest_3_
  46.1 1.6 %shard_map.114 = (bf16[256,2048]{1,0:T(8,128)(2,1)}, bf16[256,2048]{1,0:T(8,128)(2,1)}) custom-call(s32[1,256]{1,0:T(1,128)S(1)} %get-tuple-element.47.length, bf16[256,2048]{1,0:T(8,128)(2,1)S(1)} %get-tuple-element.49.keys, bf16[256,2048]{1,0:T(8,128)(2,1)S(1)} %get-tuple-element.50.values, f32[256,2048]{1,0:T(8,128)S(1)} %get-tuple-element.73.key_part, ...), custom_call_target="tpu_custom_call" | custom-call | flops 134217728 | bytes 8913920 | tf_op jit(solution)/shard_map/pallas_call | solution.py:393
  47.6 0.0 collective-permute-done.18.rest_0_
  47.6 0.6 %collective-permute-done.19.rest_2_ = bf16[512,128]{1,0:T(8,128)(2,1)S(1)} collective-permute-done((bf16[512,128]{1,0:T(8,128)(2,1)S(1)}, bf16[512,128]{1,0:T(8,128)(2,1)S(1)}, u32[]{:S(2)}, u32[]{:S(2)}) %collective-permute-start.19) | collective-permute-done | bytes 131104 | tf_op jit(solution)/shard_map/ppermute | solution.py:415
  48.2 0.0 collective-permute-done.20.rest_3_
  48.2 1.6 %shard_map.115 = (bf16[256,2048]{1,0:T(8,128)(2,1)}, bf16[256,2048]{1,0:T(8,128)(2,1)}) custom-call(s32[1,256]{1,0:T(1,128)S(1)} %get-tuple-element.47.length, bf16[256,2048]{1,0:T(8,128)(2,1)S(1)} %get-tuple-element.49.keys, bf16[256,2048]{1,0:T(8,128)(2,1)S(1)} %get-tuple-element.50.values, ...), custom_call_target="tpu_custom_call", output_to_operand_aliasing={{0}: (9, {}), {1}: (10, {})} | custom-call | flops 134217728 | bytes 11011072 | tf_op jit(solution)/shard_map/pallas_call | solution.py:393
  (2 shorter events, 0.0 us)
Async XLA Ops:
  3.6 6.9 %collective-permute-start.2 = (bf16[512,128]{1,0:T(8,128)(2,1)S(1)}, bf16[512,128]{1,0:T(8,128)(2,1)S(1)}, u32[]{:S(2)}, u32[]{:S(2)}) collective-permute-start(bf16[512,128]{1,0:T(8,128)(2,1)S(1)} %get-tuple-element.52), channel_id=1, source_target_pairs={{0,5},{1,2},{2,7},{3,0},{4,1},{5,6},{6,3},{7,4},{8,13},{9,10},{10,... | collective-permute-start | bytes 393224 | tf_op jit(solution)/shard_map/ppermute | solution.py:415
  6.1 4.9 %collective-permute-start = (bf16[512,128]{1,0:T(8,128)(2,1)S(1)}, bf16[512,128]{1,0:T(8,128)(2,1)S(1)}, u32[]{:S(2)}, u32[]{:S(2)}) collective-permute-start(bf16[512,128]{1,0:T(8,128)(2,1)S(1)} %get-tuple-element.52), channel_id=1, source_target_pairs={{0,1},{1,0},{2,3},{3,2},{4,5},{5,4},{6,7},{7,6},{8,9},{9,8},{10,11... | collective-permute-start | bytes 393224 | tf_op jit(solution)/shard_map/ppermute | solution.py:415
  6.7 5.0 %collective-permute-start.1 = (bf16[512,128]{1,0:T(8,128)(2,1)S(1)}, bf16[512,128]{1,0:T(8,128)(2,1)S(1)}, u32[]{:S(2)}, u32[]{:S(2)}) collective-permute-start(bf16[512,128]{1,0:T(8,128)(2,1)S(1)} %get-tuple-element.48._.refs_0_), channel_id=1, source_target_pairs={{0,2},{1,5},{2,0},{3,7},{4,6},{5,1},{6,4},{7,3},{8,10},{9,13},{10,... | collective-permute-start | bytes 393224 | tf_op jit(solution)/shard_map/ppermute | solution.py:415
  7.6 6.8 %collective-permute-start.4 = (bf16[512,128]{1,0:T(8,128)(2,1)S(1)}, bf16[512,128]{1,0:T(8,128)(2,1)S(1)}, u32[]{:S(2)}, u32[]{:S(2)}) collective-permute-start(bf16[512,128]{1,0:T(8,128)(2,1)S(1)} %get-tuple-element.54.refs_0_), channel_id=1, source_target_pairs={{0,2},{1,5},{2,0},{3,7},{4,6},{5,1},{6,4},{7,3},{8,10},{9,13},{10,... | collective-permute-start | bytes 393224 | tf_op jit(solution)/shard_map/ppermute | solution.py:415
  8.8 5.8 %collective-permute-start.5 = (bf16[512,128]{1,0:T(8,128)(2,1)S(1)}, bf16[512,128]{1,0:T(8,128)(2,1)S(1)}, u32[]{:S(2)}, u32[]{:S(2)}) collective-permute-start(bf16[512,128]{1,0:T(8,128)(2,1)S(1)} %get-tuple-element.55), channel_id=1, source_target_pairs={{0,5},{1,2},{2,7},{3,0},{4,1},{5,6},{6,3},{7,4},{8,13},{9,10},{10,... | collective-permute-start | bytes 393224 | tf_op jit(solution)/shard_map/ppermute | solution.py:415
  10.6 3.9 %collective-permute-start.3 = (bf16[512,128]{1,0:T(8,128)(2,1)S(1)}, bf16[512,128]{1,0:T(8,128)(2,1)S(1)}, u32[]{:S(2)}, u32[]{:S(2)}) collective-permute-start(bf16[512,128]{1,0:T(8,128)(2,1)S(1)} %get-tuple-element.55), channel_id=1, source_target_pairs={{0,1},{1,0},{2,3},{3,2},{4,5},{5,4},{6,7},{7,6},{8,9},{9,8},{10,11... | collective-permute-start | bytes 393224 | tf_op jit(solution)/shard_map/ppermute | solution.py:415
  12.0 5.0 %collective-permute-start.9 = (bf16[512,128]{1,0:T(8,128)(2,1)S(1)}, bf16[512,128]{1,0:T(8,128)(2,1)S(1)}, u32[]{:S(2)}, u32[]{:S(2)}) collective-permute-start(bf16[512,128]{1,0:T(8,128)(2,1)S(1)} %get-tuple-element.60), channel_id=1, source_target_pairs={{0,4},{1,3},{2,6},{3,1},{4,0},{5,7},{6,2},{7,5},{8,12},{9,11},{10,... | collective-permute-start | bytes 393224 | tf_op jit(solution)/shard_map/ppermute | solution.py:415
  13.6 5.3 %collective-permute-start.10 = (bf16[512,128]{1,0:T(8,128)(2,1)S(1)}, bf16[512,128]{1,0:T(8,128)(2,1)S(1)}, u32[]{:S(2)}, u32[]{:S(2)}) collective-permute-start(bf16[512,128]{1,0:T(8,128)(2,1)S(1)} %get-tuple-element.61), channel_id=1, source_target_pairs={{0,5},{1,2},{2,7},{3,0},{4,1},{5,6},{6,3},{7,4},{8,13},{9,10},{10,... | collective-permute-start | bytes 393224 | tf_op jit(solution)/shard_map/ppermute | solution.py:415
  14.4 4.4 %collective-permute-start.11 = (bf16[512,128]{1,0:T(8,128)(2,1)S(1)}, bf16[512,128]{1,0:T(8,128)(2,1)S(1)}, u32[]{:S(2)}, u32[]{:S(2)}) collective-permute-start(bf16[512,128]{1,0:T(8,128)(2,1)S(1)} %get-tuple-element.62), channel_id=1, source_target_pairs={{0,1},{1,0},{2,3},{3,2},{4,5},{5,4},{6,7},{7,6},{8,9},{9,8},{10,11... | collective-permute-start | bytes 393224 | tf_op jit(solution)/shard_map/ppermute | solution.py:415
  14.8 5.0 %collective-permute-start.6 = (bf16[512,128]{1,0:T(8,128)(2,1)S(1)}, bf16[512,128]{1,0:T(8,128)(2,1)S(1)}, u32[]{:S(2)}, u32[]{:S(2)}) collective-permute-start(bf16[512,128]{1,0:T(8,128)(2,1)S(1)} %get-tuple-element.56), channel_id=1, source_target_pairs={{0,4},{1,3},{2,6},{3,1},{4,0},{5,7},{6,2},{7,5},{8,12},{9,11},{10,... | collective-permute-start | bytes 393224 | tf_op jit(solution)/shard_map/ppermute | solution.py:415
  16.4 4.4 %collective-permute-start.7 = (bf16[512,128]{1,0:T(8,128)(2,1)S(1)}, bf16[512,128]{1,0:T(8,128)(2,1)S(1)}, u32[]{:S(2)}, u32[]{:S(2)}) collective-permute-start(bf16[512,128]{1,0:T(8,128)(2,1)S(1)} %get-tuple-element.58), channel_id=1, source_target_pairs={{0,5},{1,2},{2,7},{3,0},{4,1},{5,6},{6,3},{7,4},{8,13},{9,10},{10,... | collective-permute-start | bytes 393224 | tf_op jit(solution)/shard_map/ppermute | solution.py:415
  17.0 3.8 %collective-permute-start.8 = (bf16[512,128]{1,0:T(8,128)(2,1)S(1)}, bf16[512,128]{1,0:T(8,128)(2,1)S(1)}, u32[]{:S(2)}, u32[]{:S(2)}) collective-permute-start(bf16[512,128]{1,0:T(8,128)(2,1)S(1)} %get-tuple-element.59), channel_id=1, source_target_pairs={{0,1},{1,0},{2,3},{3,2},{4,5},{5,4},{6,7},{7,6},{8,9},{9,8},{10,11... | collective-permute-start | bytes 393224 | tf_op jit(solution)/shard_map/ppermute | solution.py:415
  17.3 1.5 %copy-start = (bf16[1,256,2048]{2,1,0:T(8,128)(2,1)S(1)}, bf16[1,256,2048]{2,1,0:T(8,128)(2,1)}, u32[]{:S(2)}) copy-start(bf16[1,256,2048]{2,1,0:T(8,128)(2,1)} %param.10) | copy-start | bytes 3145732
  17.3 1.5 %copy-start.1 = (f32[2048]{0:T(1024)S(1)}, f32[2048]{0:T(1024)}, u32[]{:S(2)}) copy-start(f32[2048]{0:T(1024)} %param.11) | copy-start | bytes 24580
  21.5 4.5 %collective-permute-start.14 = (f32[2,256]{1,0:T(2,128)S(1)}, f32[2,256]{1,0:T(2,128)S(1)}, u32[]{:S(2)}, u32[]{:S(2)}) collective-permute-start(f32[2,256]{1,0:T(2,128)S(1)} %get-tuple-element.64.rest_0_), channel_id=1, source_target_pairs={{0,16},{8,24},{16,0},{24,8},{1,17},{9,25},{17,1},{25,9},{2,18},{10... | collective-permute-start | bytes 6152 | tf_op jit(solution)/shard_map/ppermute | solution.py:442
  24.1 5.4 %collective-permute-start.13 = (f32[2,256]{1,0:T(2,128)S(1)}, f32[2,256]{1,0:T(2,128)S(1)}, u32[]{:S(2)}, u32[]{:S(2)}) collective-permute-start(f32[2,256]{1,0:T(2,128)S(1)} %get-tuple-element.64.rest_0_), channel_id=1, source_target_pairs={{0,24},{8,16},{16,8},{24,0},{1,25},{9,17},{17,9},{25,1},{2,26},{10... | collective-permute-start | bytes 6152 | tf_op jit(solution)/shard_map/ppermute | solution.py:442
  25.5 4.0 %collective-permute-start.12 = (f32[2,256]{1,0:T(2,128)S(1)}, f32[2,256]{1,0:T(2,128)S(1)}, u32[]{:S(2)}, u32[]{:S(2)}) collective-permute-start(f32[2,256]{1,0:T(2,128)S(1)} %get-tuple-element.64.rest_0_), channel_id=1, source_target_pairs={{0,8},{8,0},{16,24},{24,16},{1,9},{9,1},{17,25},{25,17},{2,10},{10... | collective-permute-start | bytes 6152 | tf_op jit(solution)/shard_map/ppermute | solution.py:442
  30.6 7.4 %collective-permute-start.17 = (bf16[1024,128]{1,0:T(8,128)(2,1)S(1)}, bf16[1024,128]{1,0:T(8,128)(2,1)S(1)}, u32[]{:S(2)}, u32[]{:S(2)}) collective-permute-start(bf16[1024,128]{1,0:T(8,128)(2,1)S(1)} %get-tuple-element.76), channel_id=1, source_target_pairs={{0,5},{1,2},{2,7},{3,0},{4,1},{5,6},{6,3},{7,4},{8,13},{9,10},{10,... | collective-permute-start | bytes 786440 | tf_op jit(solution)/shard_map/ppermute | solution.py:415
  30.6 7.3 %collective-permute-start.15 = (bf16[1024,128]{1,0:T(8,128)(2,1)S(1)}, bf16[1024,128]{1,0:T(8,128)(2,1)S(1)}, u32[]{:S(2)}, u32[]{:S(2)}) collective-permute-start(bf16[1024,128]{1,0:T(8,128)(2,1)S(1)} %get-tuple-element.76), channel_id=1, source_target_pairs={{0,1},{1,0},{2,3},{3,2},{4,5},{5,4},{6,7},{7,6},{8,9},{9,8},{10,11... | collective-permute-start | bytes 786440 | tf_op jit(solution)/shard_map/ppermute | solution.py:415
  31.6 7.6 %collective-permute-start.16 = (bf16[1024,128]{1,0:T(8,128)(2,1)S(1)}, bf16[1024,128]{1,0:T(8,128)(2,1)S(1)}, u32[]{:S(2)}, u32[]{:S(2)}) collective-permute-start(bf16[1024,128]{1,0:T(8,128)(2,1)S(1)} %get-tuple-element.75.refs_0_), channel_id=1, source_target_pairs={{0,2},{1,5},{2,0},{3,7},{4,6},{5,1},{6,4},{7,3},{8,10},{9,13},{10,... | collective-permute-start | bytes 786440 | tf_op jit(solution)/shard_map/ppermute | solution.py:415
  39.5 5.0 %collective-permute-start.21 = (bf16[512,128]{1,0:T(8,128)(2,1)S(1)}, bf16[512,128]{1,0:T(8,128)(2,1)S(1)}, u32[]{:S(2)}, u32[]{:S(2)}) collective-permute-start(bf16[512,128]{1,0:T(8,128)(2,1)S(1)} %get-tuple-element.83), channel_id=1, source_target_pairs={{0,4},{1,3},{2,6},{3,1},{4,0},{5,7},{6,2},{7,5},{8,12},{9,11},{10,... | collective-permute-start | bytes 393224 | tf_op jit(solution)/shard_map/ppermute | solution.py:415
  41.0 5.0 %collective-permute-start.22 = (bf16[512,128]{1,0:T(8,128)(2,1)S(1)}, bf16[512,128]{1,0:T(8,128)(2,1)S(1)}, u32[]{:S(2)}, u32[]{:S(2)}) collective-permute-start(bf16[512,128]{1,0:T(8,128)(2,1)S(1)} %get-tuple-element.84), channel_id=1, source_target_pairs={{0,5},{1,2},{2,7},{3,0},{4,1},{5,6},{6,3},{7,4},{8,13},{9,10},{10,... | collective-permute-start | bytes 393224 | tf_op jit(solution)/shard_map/ppermute | solution.py:415
  41.0 5.0 %collective-permute-start.23 = (bf16[512,128]{1,0:T(8,128)(2,1)S(1)}, bf16[512,128]{1,0:T(8,128)(2,1)S(1)}, u32[]{:S(2)}, u32[]{:S(2)}) collective-permute-start(bf16[512,128]{1,0:T(8,128)(2,1)S(1)} %get-tuple-element.85), channel_id=1, source_target_pairs={{0,1},{1,0},{2,3},{3,2},{4,5},{5,4},{6,7},{7,6},{8,9},{9,8},{10,11... | collective-permute-start | bytes 393224 | tf_op jit(solution)/shard_map/ppermute | solution.py:415
  42.2 5.4 %collective-permute-start.18 = (bf16[512,128]{1,0:T(8,128)(2,1)S(1)}, bf16[512,128]{1,0:T(8,128)(2,1)S(1)}, u32[]{:S(2)}, u32[]{:S(2)}) collective-permute-start(bf16[512,128]{1,0:T(8,128)(2,1)S(1)} %get-tuple-element.80), channel_id=1, source_target_pairs={{0,4},{1,3},{2,6},{3,1},{4,0},{5,7},{6,2},{7,5},{8,12},{9,11},{10,... | collective-permute-start | bytes 393224 | tf_op jit(solution)/shard_map/ppermute | solution.py:415
  42.9 5.3 %collective-permute-start.19 = (bf16[512,128]{1,0:T(8,128)(2,1)S(1)}, bf16[512,128]{1,0:T(8,128)(2,1)S(1)}, u32[]{:S(2)}, u32[]{:S(2)}) collective-permute-start(bf16[512,128]{1,0:T(8,128)(2,1)S(1)} %get-tuple-element.81), channel_id=1, source_target_pairs={{0,5},{1,2},{2,7},{3,0},{4,1},{5,6},{6,3},{7,4},{8,13},{9,10},{10,... | collective-permute-start | bytes 393224 | tf_op jit(solution)/shard_map/ppermute | solution.py:415
  44.5 3.7 %collective-permute-start.20 = (bf16[512,128]{1,0:T(8,128)(2,1)S(1)}, bf16[512,128]{1,0:T(8,128)(2,1)S(1)}, u32[]{:S(2)}, u32[]{:S(2)}) collective-permute-start(bf16[512,128]{1,0:T(8,128)(2,1)S(1)} %get-tuple-element.82), channel_id=1, source_target_pairs={{0,1},{1,0},{2,3},{3,2},{4,5},{5,4},{6,7},{7,6},{8,9},{9,8},{10,11... | collective-permute-start | bytes 393224 | tf_op jit(solution)/shard_map/ppermute | solution.py:415

commit v12 on v11

--- a/solution.py
+++ b/solution.py
@@ -15,8 +15,7 @@
 BF16 = jnp.bfloat16
 VMEM_LIMIT = 24 * 1024 * 1024
 FORWARD_PIECES = 2
-BACKWARD_PIECES = 1
-RETURN_PIECES = 2
+BACKWARD_PIECES = 2
 
 VMEM = pl.BlockSpec(memory_space=pltpu.VMEM)
 SMEM = pl.BlockSpec(memory_space=pltpu.SMEM)
@@ -268,14 +267,15 @@
 
 def grad_kernel(piece, groups, grid, scale, length, queries, cotangent, gain, *rest):
     all_sums, attention, rest = split_refs(rest, groups, FORWARD_PIECES, len(rest) - groups - FORWARD_PIECES)
-    (grad_out, inverse_rms), halves, full = rest[:2], rest[2:-1], rest[-1]
+    grad_out, halves, full = rest[0], rest[1 : 1 + grid[2]], rest[-1]
     rows, width = grad_out.shape
     features = HEADS * HD
     total = all_sums[0][...]
     for other in all_sums[1:]:
         total = total + other[...]
     inverse = lax.rsqrt(total[0:1, :] / features + EPSILON)
-    inverse_rms[...] = inverse
+    if piece == 0:
+        rest[1 + grid[2]][...] = inverse
     live = lax.broadcasted_iota(jnp.int32, (1, rows), 1) < length[...]
     live_inverse = jnp.where(live, inverse, 0.0)
     shrink = live_inverse * inverse * (inverse * total[1:2, :]) / features
@@ -300,44 +300,35 @@
     return [pltpu.make_async_copy(source.at[p, :], target.at[p, :], sems.at[j]) for j, p in enumerate(parts)]
 
 
-def column_copies(sources, targets, first, count, sems):
-    cols = slice(first * HD, (first + count) * HD)
-    return [
-        pltpu.make_async_copy(src.at[:, cols], dst.at[:, cols], sems.at[j])
-        for j, (src, dst) in enumerate(zip(sources, targets))
-    ]
-
-
-def query_kernel(heads, group, scale, length, inverse_rms, gain, queries, keys, values, *rest):
-    sizes = (BACKWARD_PIECES, FORWARD_PIECES, FORWARD_PIECES)
-    grads, attention, prefix, rest = split_refs(rest, *sizes, len(rest) - sum(sizes))
-    attended_hbm, query_hbm, key_part, token, attended, query_grad, keep, keep_turned, sems = rest
+def query_kernel(piece, scale, length, inverse_rms, gain, queries, keys, values, grads, *rest):
+    attention, prefix, rest = split_refs(rest, FORWARD_PIECES, FORWARD_PIECES, len(rest) - 2 * FORWARD_PIECES)
+    attended_hbm, query_hbm, key_part, token, attended, query_grad, keep, sems = rest[-8:]
     token[...] = jnp.zeros_like(token)
     write_mask(length, keep, False)
-    write_mask(length, keep_turned, True)
     inverse = token_columns(inverse_rms[...])
+    heads = grads.shape[1] // HD
+    group = 4 if heads % 4 == 0 else 1
     copies = []
     for head in range(heads):
         cols = head_cols(head)
-        grad_piece, at = head_of(grads, head)
-        grad = grad_piece[:, at]
-        out_piece, at = head_of(attention, head)
-        per_piece = heads // FORWARD_PIECES
-        prefix_piece, state = prefix[head // per_piece], head % per_piece
-        grad_scores = nt(grad, values[:, cols]).astype(BF16) * keep[...]
+        place = piece * heads + head
+        whole = head_cols(place)
+        out_piece, at = head_of(attention, place)
+        per_piece = prefix[0].shape[0] // HD
+        prefix_piece, state = prefix[place // per_piece], place % per_piece
+        grad = grads[:, cols]
+        grad_scores = nt(grad, values[:, whole]).astype(BF16) * keep[...]
         carried = nt(grad, prefix_piece[state * HD : (state + 1) * HD, :])
-        query_grad[:, cols] = (scale * (carried + nn(grad_scores, keys[:, cols]))).astype(BF16)
-        turned = nt(values[:, cols], grad).astype(BF16) * keep_turned[...]
-        key_part[:, cols] = scale * nn(turned, queries[:, cols])
-        attended[:, cols] = (out_piece[:, at] * inverse * gain[:, cols]).astype(BF16)
+        query_grad[:, cols] = (scale * (carried + nn(grad_scores, keys[:, whole]))).astype(BF16)
+        key_part[:, cols] = scale * tn(grad_scores, queries[:, whole])
+        attended[:, cols] = (out_piece[:, at] * inverse * gain[:, whole]).astype(BF16)
         if (head + 1) % group == 0:
-            step = head // group
-            some = column_copies(
-                (attended, query_grad), (attended_hbm, query_hbm), step * group, group, sems.at[step]
-            )
-            for copy in some:
+            here = slice((head + 1 - group) * HD, (head + 1) * HD)
+            there = slice((place + 1 - group) * HD, (place + 1) * HD)
+            for j, (src, dst) in enumerate(((attended, attended_hbm), (query_grad, query_hbm))):
+                copy = pltpu.make_async_copy(src.at[:, here], dst.at[:, there], sems.at[head // group, j])
                 copy.start()
-            copies += some
+                copies.append(copy)
     for copy in copies:
         copy.wait()
 
@@ -352,29 +343,29 @@
         value_part[:, cols] = scale * nn(turned, grad_piece[:, at])
 
 
-def final_kernel(piece, grid, counts, length, keys, values, key_part, value_part, *rest):
-    received, rest = rest[: sum(counts)], rest[sum(counts) :]
+def final_kernel(grid, counts, length, keys, values, value_part, *rest):
+    count = sum(counts) * BACKWARD_PIECES
+    key_parts, received, rest = split_refs(rest, BACKWARD_PIECES, count, len(rest) - BACKWARD_PIECES - count)
     key_hbm, value_hbm, key_grad, value_grad, below, sems = rest[-6:]
     pair = grid[2]
-    join_halves(split_refs(received, *counts), below, my_place(grid)[2], pair)
-    rows, width = key_grad.shape
+    tall = below.shape[0] // BACKWARD_PIECES
+    for piece, parts in enumerate(split_refs(received, *[sum(counts)] * BACKWARD_PIECES)):
+        full = below.at[pl.ds(piece * tall, tall), :]
+        join_halves(split_refs(parts, *counts), full, my_place(grid)[2], pair)
+    rows, width = keys.shape
     live = jnp.where(live_rows(length, rows), 1.0, 0.0)
-    per_half = width // HD // pair
-    group = 2 if per_half % 2 == 0 else 1
+    group = 2 if width // HD % 2 == 0 else 1
     copies = []
     for head in range(width // HD):
-        half, within = head // per_half, head % per_half
-        cols = head_cols(head)
-        place = half * (keys.shape[1] // HD // pair) + piece * per_half + within
-        whole = head_cols(place)
+        cols = head_cols(head)
+        key_part, at = head_of(key_parts, head)
         state = below[head * HD : (head + 1) * HD, :]
-        key_grad[:, cols] = (key_part[:, whole] + live * nt(values[:, whole], state)).astype(BF16)
-        value_grad[:, cols] = (value_part[:, whole] + live * nn(keys[:, whole], state)).astype(BF16)
+        key_grad[:, cols] = (key_part[:, at] + live * nt(values[:, cols], state)).astype(BF16)
+        value_grad[:, cols] = (value_part[:, cols] + live * nn(keys[:, cols], state)).astype(BF16)
         if (head + 1) % group == 0:
             done = slice((head + 1 - group) * HD, (head + 1) * HD)
-            there = slice((place + 1 - group) * HD, (place + 1) * HD)
             for j, (src, dst) in enumerate(((key_grad, key_hbm), (value_grad, value_hbm))):
-                copy = pltpu.make_async_copy(src.at[:, done], dst.at[:, there], sems.at[j, head // group])
+                copy = pltpu.make_async_copy(src.at[:, done], dst.at[:, done], sems.at[j, head // group])
                 copy.start()
                 copies.append(copy)
     for copy in copies:
@@ -504,46 +495,46 @@
     grads, state_grad = [], []
     width = features // BACKWARD_PIECES
     for piece in range(BACKWARD_PIECES):
-        grad_out, inverse_rms, *parts = call(
+        grad_out, *parts = call(
             functools.partial(grad_kernel, piece, len(sums), grid, scale),
-            [shape((rows, width), BF16), row] + halves(BACKWARD_PIECES),
+            [shape((rows, width), BF16)] + halves(BACKWARD_PIECES) + [row] * (piece == 0),
             (length, query, cot, gain, *sums, *attention), [pltpu.VMEM((width, HD), BF16)],
             unit * HD // BACKWARD_PIECES,
         )
         grads.append(grad_out)
-        state_grad.append(parts)
-    group = 4 if heads % 4 == 0 else 1
-    attended, query_grad, key_part, token = call(
-        functools.partial(query_kernel, heads, group, scale),
-        [narrow, narrow, wide, shape((8, HD), F32)],
-        (length, inverse_rms, gain, query, key, value, *grads, *attention, *prefix),
-        [pltpu.VMEM(narrow.shape, BF16)] * 2 + [mask] * 2 + [pltpu.SemaphoreType.DMA((heads // group, 2))],
-        unit * (4 * rows + HD), out_specs=[HBM, HBM, VMEM, VMEM],
-    )
-    (part,) = state_grad
-    arrived = gather_line(part, grid)
-    mixed = []
-    for piece in range(RETURN_PIECES):
-        mixed.append(mix(arrived, down, piece, RETURN_PIECES, (token, *mixed[-1][:1]) if mixed else (token,)))
+        state_grad.append(parts[:pair])
+        if piece == 0:
+            inverse_rms = parts[pair]
+    group = 4 if heads // BACKWARD_PIECES % 4 == 0 else 1
+    narrow_piece, wide_piece = shape((rows, width), BF16), shape((rows, width), F32)
+    mixed, key_parts, results = [], [], []
+    for piece in range(BACKWARD_PIECES):
+        operands = (length, inverse_rms, gain, query, key, value, grads[piece], *attention, *prefix, *results)
+        last = len(operands) - len(results)
+        *results, key_part, token = call(
+            functools.partial(query_kernel, piece, scale),
+            [narrow, narrow, wide_piece, shape((8, HD), F32)], operands,
+            [pltpu.VMEM(narrow_piece.shape, BF16)] * 2 + [mask, pltpu.SemaphoreType.DMA((heads // group, 2))],
+            unit * (3 * rows + HD) // BACKWARD_PIECES, range(last, len(operands)),
+            after=tuple(sums[0] for sums in mixed), out_specs=[HBM, HBM, VMEM, VMEM],
+            aliases={last + j: j for j in range(len(results))},
+        )
+        key_parts.append(key_part)
+        if piece == 0:
+            for part in state_grad:
+                mixed.append(mix(gather_line(part, grid), down, 0, 1, (token,)))
+    attended, query_grad = results
     (value_part,) = call(
         functools.partial(value_kernel, heads, scale),
         [wide], (length, query, key, *grads), [mask], unit * 2 * rows, after=(mixed[-1][0],),
     )
-    results = []
-    width = features // RETURN_PIECES
-    for piece in range(RETURN_PIECES):
-        below = flat(scatter_line(mixed[piece], grid))
-        operands = (length, key, value, key_part, value_part, *below, *results)
-        first = len(operands) - len(results)
-        results = call(
-            functools.partial(final_kernel, piece, grid, counts),
-            [narrow, narrow], operands,
-            [pltpu.VMEM((rows, width), BF16)] * 2 + [pltpu.VMEM((width, HD), BF16), sems],
-            2 * unit * HD // RETURN_PIECES,
-            range(first, len(operands)), out_specs=[HBM, HBM],
-            aliases={first + j: j for j in range(len(results))},
-        )
-    key_grad, value_grad = results
+    below = [block for sums in mixed for block in flat(scatter_line(sums, grid))]
+    key_grad, value_grad = call(
+        functools.partial(final_kernel, grid, counts),
+        [narrow, narrow], (length, key, value, value_part, *key_parts, *below),
+        [pltpu.VMEM(narrow.shape, BF16)] * 2 + [pltpu.VMEM((features, HD), BF16), sems],
+        2 * unit * HD, out_specs=[HBM, HBM],
+    )
     return attended[None], query_grad[None], key_grad[None], value_grad[None]
 
 

time: 50.1 us -> 50.8 us (1.014)
  starting transfers between devices: 20.8 us -> 23.1 us
  waiting for transfers between devices: 9.15 us -> 7.32 us
    ppermute x21 -> x24, starting transfers between devices: 16.5 us -> 18.9 us  [line_send(): return lax.ppermute(block, 'seg', moves)]
    ppermute x21 -> x24, waiting for transfers between devices: 5.35 us -> 3.52 us  [line_send(): return lax.ppermute(block, 'seg', moves)]
    pallas_call x14 -> x15, Pallas kernels: 18.4 us -> 18.5 us  [call(): pl.pallas_call(kernel, out_shape=out_shape, in_specs=specs + [ANY] * len(...]
  transfers between devices with their start and end apart: 24 -> 27, of which waited for: 10 -> 8; matrix products, arithmetic and copies ran while one was open for 0% -> 0% of each run, Pallas kernels for 25% -> 25%
where the time goes in v12:
time: 50.8 us; the launch traced here: 50.6 us
  starting transfers between devices  23.1 us (45%)
  Pallas kernels  18.5 us (36%)
  waiting for transfers between devices  7.32 us (14%)
  between operations  1.63 us (3%)
    ppermute x24, starting transfers between devices, line_send(): return lax.ppermute(block, 'seg', moves)  18.9 us
    pallas_call x15, Pallas kernels, call(): pl.pallas_call(kernel, out_shape=out_shape, in_specs=specs + [ANY] * len(...  18.5 us
    ppermute x3, starting transfers between devices, token_sums(): parts.append(lax.ppermute(sums, 'head', moves))  4.23 us
    ppermute x3, waiting for transfers between devices, token_sums(): parts.append(lax.ppermute(sums, 'head', moves))  3.8 us
    ppermute x24, waiting for transfers between devices, line_send(): return lax.ppermute(block, 'seg', moves)  3.52 us
  transfers between devices with their start and end apart: 27, of which 8 were waited for; matrix products, arithmetic and copies ran while one was open for 0% of the time, Pallas kernels for 25%

profile of v12, /device:TPU:0, one launch (start us, length us, event | category | flops | bytes accessed | tf_op | source)
XLA Modules:
  0.0 50.6 jit_solution(8099381344466556986)
XLA Ops:
  1.3 2.3 %shard_map.102 = (bf16[256,2048]{1,0:T(8,128)(2,1)S(1)}, bf16[256,2048]{1,0:T(8,128)(2,1)S(1)}, s32[1,256]{1,0:T(1,128)S(1)}, f32[16,128]{1,0:T(8,128)S(1)}, f32...) custom-call(s32[1]{0:T(128)S(6)} %copy.15.seg_len, ...), custom_call_target="tpu_custom_call" | custom-call | flops 134217728 | bytes 4736036 | tf_op jit(solution)/shard_map/pallas_call | solution.py:384
  3.6 2.5 %collective-permute-start.2 = (bf16[512,128]{1,0:T(8,128)(2,1)S(1)}, bf16[512,128]{1,0:T(8,128)(2,1)S(1)}, u32[]{:S(2)}, u32[]{:S(2)}) collective-permute-start(bf16[512,128]{1,0:T(8,128)(2,1)S(1)} %get-tuple-element.56), channel_id=1, source_target_pairs={{0,5},{1,2},{2,7},{3,0},{4,1},{5,6},{6,3},{7,4},{8,13},{9,10},{10,... | collective-permute-start | bytes 393224 | tf_op jit(solution)/shard_map/ppermute | solution.py:406
  6.1 0.6 %collective-permute-start = (bf16[512,128]{1,0:T(8,128)(2,1)S(1)}, bf16[512,128]{1,0:T(8,128)(2,1)S(1)}, u32[]{:S(2)}, u32[]{:S(2)}) collective-permute-start(bf16[512,128]{1,0:T(8,128)(2,1)S(1)} %get-tuple-element.56), channel_id=1, source_target_pairs={{0,1},{1,0},{2,3},{3,2},{4,5},{5,4},{6,7},{7,6},{8,9},{9,8},{10,11... | collective-permute-start | bytes 393224 | tf_op jit(solution)/shard_map/ppermute | solution.py:406
  6.7 0.9 %collective-permute-start.1 = (bf16[512,128]{1,0:T(8,128)(2,1)S(1)}, bf16[512,128]{1,0:T(8,128)(2,1)S(1)}, u32[]{:S(2)}, u32[]{:S(2)}) collective-permute-start(bf16[512,128]{1,0:T(8,128)(2,1)S(1)} %get-tuple-element.52._.refs_0_), channel_id=1, source_target_pairs={{0,2},{1,5},{2,0},{3,7},{4,6},{5,1},{6,4},{7,3},{8,10},{9,13},{10,... | collective-permute-start | bytes 393224 | tf_op jit(solution)/shard_map/ppermute | solution.py:406
  7.6 1.1 %collective-permute-start.4 = (bf16[512,128]{1,0:T(8,128)(2,1)S(1)}, bf16[512,128]{1,0:T(8,128)(2,1)S(1)}, u32[]{:S(2)}, u32[]{:S(2)}) collective-permute-start(bf16[512,128]{1,0:T(8,128)(2,1)S(1)} %get-tuple-element.58.refs_0_), channel_id=1, source_target_pairs={{0,2},{1,5},{2,0},{3,7},{4,6},{5,1},{6,4},{7,3},{8,10},{9,13},{10,... | collective-permute-start | bytes 393224 | tf_op jit(solution)/shard_map/ppermute | solution.py:406
  8.8 0.6 %collective-permute-start.5 = (bf16[512,128]{1,0:T(8,128)(2,1)S(1)}, bf16[512,128]{1,0:T(8,128)(2,1)S(1)}, u32[]{:S(2)}, u32[]{:S(2)}) collective-permute-start(bf16[512,128]{1,0:T(8,128)(2,1)S(1)} %get-tuple-element.59), channel_id=1, source_target_pairs={{0,5},{1,2},{2,7},{3,0},{4,1},{5,6},{6,3},{7,4},{8,13},{9,10},{10,... | collective-permute-start | bytes 393224 | tf_op jit(solution)/shard_map/ppermute | solution.py:406
  9.3 1.2 %shard_map.103.refs_4_.queries = bf16[256,2048]{1,0:T(8,128)(2,1)S(1)} custom-call(bf16[256,2048]{1,0:T(8,128)(2,1)} %bitcast.20, bf16[512,128]{1,0:T(8,128)(2,1)S(1)} %get-tuple-element.52._.refs_0_), custom_call_target="tpu_custom_call" | custom-call | bytes 2097152 | tf_op jit(solution)/shard_map/pallas_call | solution.py:384
  10.6 0.0 collective-permute-done.2.refs_3_
  10.6 0.5 collective-permute-start.3
  11.1 0.0 collective-permute-done.refs_1_
  11.1 0.6 %collective-permute-done.1.refs_2_ = bf16[512,128]{1,0:T(8,128)(2,1)S(1)} collective-permute-done((bf16[512,128]{1,0:T(8,128)(2,1)S(1)}, bf16[512,128]{1,0:T(8,128)(2,1)S(1)}, u32[]{:S(2)}, u32[]{:S(2)}) %collective-permute-start.1) | collective-permute-done | bytes 131104 | tf_op jit(solution)/shard_map/ppermute | solution.py:406
  11.7 0.3 shard_map.104
  12.0 1.6 %collective-permute-start.9 = (bf16[512,128]{1,0:T(8,128)(2,1)S(1)}, bf16[512,128]{1,0:T(8,128)(2,1)S(1)}, u32[]{:S(2)}, u32[]{:S(2)}) collective-permute-start(bf16[512,128]{1,0:T(8,128)(2,1)S(1)} %get-tuple-element.64), channel_id=1, source_target_pairs={{0,4},{1,3},{2,6},{3,1},{4,0},{5,7},{6,2},{7,5},{8,12},{9,11},{10,... | collective-permute-start | bytes 393224 | tf_op jit(solution)/shard_map/ppermute | solution.py:406
  13.6 0.4 collective-permute-start.10
  14.0 0.4 collective-permute-done.4.refs_2_
  14.4 0.1 collective-permute-start.11
  14.5 0.0 collective-permute-done.5.refs_3_
  14.5 0.0 collective-permute-done.3.refs_1_
  14.5 0.3 shard_map.106
  14.8 1.6 %collective-permute-start.6 = (bf16[512,128]{1,0:T(8,128)(2,1)S(1)}, bf16[512,128]{1,0:T(8,128)(2,1)S(1)}, u32[]{:S(2)}, u32[]{:S(2)}) collective-permute-start(bf16[512,128]{1,0:T(8,128)(2,1)S(1)} %get-tuple-element.60), channel_id=1, source_target_pairs={{0,4},{1,3},{2,6},{3,1},{4,0},{5,7},{6,2},{7,5},{8,12},{9,11},{10,... | collective-permute-start | bytes 393224 | tf_op jit(solution)/shard_map/ppermute | solution.py:406
  16.4 0.6 %collective-permute-start.7 = (bf16[512,128]{1,0:T(8,128)(2,1)S(1)}, bf16[512,128]{1,0:T(8,128)(2,1)S(1)}, u32[]{:S(2)}, u32[]{:S(2)}) collective-permute-start(bf16[512,128]{1,0:T(8,128)(2,1)S(1)} %get-tuple-element.62), channel_id=1, source_target_pairs={{0,5},{1,2},{2,7},{3,0},{4,1},{5,6},{6,3},{7,4},{8,13},{9,10},{10,... | collective-permute-start | bytes 393224 | tf_op jit(solution)/shard_map/ppermute | solution.py:406
  16.9 0.1 collective-permute-done.9.rest_0_
  17.0 0.3 collective-permute-start.8
  17.4 1.5 %shard_map.105.local = f32[256,2048]{1,0:T(8,128)S(1)} custom-call(s32[1,256]{1,0:T(1,128)S(1)} %get-tuple-element.51.length, bf16[256,2048]{1,0:T(8,128)(2,1)S(1)} %shard_map.103.refs_4_.queries, bf16[256,2048]{1,0:T(8,128)(2,1)S(1)} %get-tuple-element.53.keys, bf16[256,2048]{1,0:T(8,128)(2,1)S(1)} %get-tuple-element.54.values, ...), custom_call_target="tpu_custom_call" | custom-call | flops 536870912 | bytes 5243904 | tf_op jit(solution)/shard_map/pallas_call | solution.py:384
  18.8 0.0 collective-permute-done.10.rest_2_
  18.8 0.0 collective-permute-done.11.rest_3_
  18.9 0.7 %shard_map.107 = (f32[256,1024]{1,0:T(8,128)S(1)}, f32[2,256]{1,0:T(2,128)S(1)}, bf16[1024,128]{1,0:T(8,128)(2,1)S(1)}) custom-call(s32[1,256]{1,0:T(1,128)S(1)} %get-tuple-element.51.length, bf16[256,2048]{1,0:T(8,128)(2,1)S(1)} %shard_map.103.refs_4_.queries, f32[256,2048]{1,0:T(8,128)S(1)} %shard_map.105.local, bf16[256,2048]{1,0:T(8,128)(2,1)S(1)} %bitcast.10, ...), custom_call_target="tpu_custom_call" | custom-call | flops 67108864 | bytes 6040576 | tf_op jit(solution)/shard_map/pallas_call | solution.py:384
  19.5 0.3 collective-permute-done.6.rest_0_
  19.8 0.9 %collective-permute-done.7.rest_2_ = bf16[512,128]{1,0:T(8,128)(2,1)S(1)} collective-permute-done((bf16[512,128]{1,0:T(8,128)(2,1)S(1)}, bf16[512,128]{1,0:T(8,128)(2,1)S(1)}, u32[]{:S(2)}, u32[]{:S(2)}) %collective-permute-start.7) | collective-permute-done | bytes 131104 | tf_op jit(solution)/shard_map/ppermute | solution.py:406
  20.8 0.0 collective-permute-done.8.rest_3_
  20.8 0.7 %shard_map.108 = (f32[256,1024]{1,0:T(8,128)S(1)}, f32[2,256]{1,0:T(2,128)S(1)}, bf16[1024,128]{1,0:T(8,128)(2,1)S(1)}) custom-call(s32[1,256]{1,0:T(1,128)S(1)} %get-tuple-element.51.length, bf16[256,2048]{1,0:T(8,128)(2,1)S(1)} %shard_map.103.refs_4_.queries, f32[256,2048]{1,0:T(8,128)S(1)} %shard_map.105.local, bf16[256,2048]{1,0:T(8,128)(2,1)S(1)} %bitcast.11, ...), custom_call_target="tpu_custom_call" | custom-call | flops 67108864 | bytes 6042624 | tf_op jit(solution)/shard_map/pallas_call | solution.py:384
  21.5 2.7 %collective-permute-start.14 = (f32[2,256]{1,0:T(2,128)S(1)}, f32[2,256]{1,0:T(2,128)S(1)}, u32[]{:S(2)}, u32[]{:S(2)}) collective-permute-start(f32[2,256]{1,0:T(2,128)S(1)} %get-tuple-element.68.rest_0_), channel_id=1, source_target_pairs={{0,16},{8,24},{16,0},{24,8},{1,17},{9,25},{17,1},{25,9},{2,18},{10... | collective-permute-start | bytes 6152 | tf_op jit(solution)/shard_map/ppermute | solution.py:433
  24.1 1.3 %collective-permute-start.13 = (f32[2,256]{1,0:T(2,128)S(1)}, f32[2,256]{1,0:T(2,128)S(1)}, u32[]{:S(2)}, u32[]{:S(2)}) collective-permute-start(f32[2,256]{1,0:T(2,128)S(1)} %get-tuple-element.68.rest_0_), channel_id=1, source_target_pairs={{0,24},{8,16},{16,8},{24,0},{1,25},{9,17},{17,9},{25,1},{2,26},{10... | collective-permute-start | bytes 6152 | tf_op jit(solution)/shard_map/ppermute | solution.py:433
  25.5 0.2 collective-permute-start.12
  25.7 0.3 collective-permute-done.14.rest_3_
  26.0 3.5 %collective-permute-done.13.rest_2_ = f32[2,256]{1,0:T(2,128)S(1)} collective-permute-done((f32[2,256]{1,0:T(2,128)S(1)}, f32[2,256]{1,0:T(2,128)S(1)}, u32[]{:S(2)}, u32[]{:S(2)}) %collective-permute-start.13) | collective-permute-done | bytes 2080 | tf_op jit(solution)/shard_map/ppermute | solution.py:433
  29.5 0.0 collective-permute-done.12.rest_1_
  29.5 0.6 %shard_map.110 = (bf16[256,1024]{1,0:T(8,128)(2,1)S(1)}, bf16[512,128]{1,0:T(8,128)(2,1)S(1)}, bf16[512,128]{1,0:T(8,128)(2,1)S(1)}) custom-call(s32[1,256]{1,0:T(1,128)S(1)} %get-tuple-element.51.length, bf16[256,2048]{1,0:T(8,128)(2,1)S(1)} %shard_map.103.refs_4_.queries, bf16[256,2048]{1,0:T(8,128)(2,1)S(1)} %bitcast.12, f32[1,2048]{1,0:T(1,128)S(1)} %bitcast.16, ...), custom_call_target="tpu_custom_call" | custom-call | flops 67108864 | bytes 4998144 | tf_op jit(solution)/shard_map/pallas_call | solution.py:384
  30.1 0.9 %collective-permute-start.19 = (bf16[512,128]{1,0:T(8,128)(2,1)S(1)}, bf16[512,128]{1,0:T(8,128)(2,1)S(1)}, u32[]{:S(2)}, u32[]{:S(2)}) collective-permute-start(bf16[512,128]{1,0:T(8,128)(2,1)S(1)} %get-tuple-element.83.refs_0_), channel_id=1, source_target_pairs={{0,2},{1,5},{2,0},{3,7},{4,6},{5,1},{6,4},{7,3},{8,10},{9,13},{10,... | collective-permute-start | bytes 393224 | tf_op jit(solution)/shard_map/ppermute | solution.py:406
  31.0 0.0 collective-permute-start.20
  31.0 1.3 %collective-permute-start.18 = (bf16[512,128]{1,0:T(8,128)(2,1)S(1)}, bf16[512,128]{1,0:T(8,128)(2,1)S(1)}, u32[]{:S(2)}, u32[]{:S(2)}) collective-permute-start(bf16[512,128]{1,0:T(8,128)(2,1)S(1)} %get-tuple-element.84), channel_id=1, source_target_pairs={{0,1},{1,0},{2,3},{3,2},{4,5},{5,4},{6,7},{7,6},{8,9},{9,8},{10,11... | collective-permute-start | bytes 393224 | tf_op jit(solution)/shard_map/ppermute | solution.py:406
  32.3 0.6 %shard_map.109 = (bf16[256,1024]{1,0:T(8,128)(2,1)S(1)}, bf16[512,128]{1,0:T(8,128)(2,1)S(1)}, bf16[512,128]{1,0:T(8,128)(2,1)S(1)}, f32[1,256]{1,0:T(1,128)S(1)}) custom-call(s32[1,256]{1,0:T(1,128)S(1)} %get-tuple-element.51.length, bf16[256,2048]{1,0:T(8,128)(2,1)S(1)} %shard_map.103.refs_4_.queries, bf16[256,2048]{1,0:T(8,128)(2,1)S(1)} %bitcast.13, ...), custom_call_target="tpu_custom_call" | custom-call | flops 67108864 | bytes 4999168 | tf_op jit(solution)/shard_map/pallas_call | solution.py:384
  32.9 0.9 %collective-permute-start.16 = (bf16[512,128]{1,0:T(8,128)(2,1)S(1)}, bf16[512,128]{1,0:T(8,128)(2,1)S(1)}, u32[]{:S(2)}, u32[]{:S(2)}) collective-permute-start(bf16[512,128]{1,0:T(8,128)(2,1)S(1)} %get-tuple-element.79.refs_0_), channel_id=1, source_target_pairs={{0,2},{1,5},{2,0},{3,7},{4,6},{5,1},{6,4},{7,3},{8,10},{9,13},{10,... | collective-permute-start | bytes 393224 | tf_op jit(solution)/shard_map/ppermute | solution.py:406
  33.8 0.5 %collective-permute-start.17 = (bf16[512,128]{1,0:T(8,128)(2,1)S(1)}, bf16[512,128]{1,0:T(8,128)(2,1)S(1)}, u32[]{:S(2)}, u32[]{:S(2)}) collective-permute-start(bf16[512,128]{1,0:T(8,128)(2,1)S(1)} %get-tuple-element.80), channel_id=1, source_target_pairs={{0,5},{1,2},{2,7},{3,0},{4,1},{5,6},{6,3},{7,4},{8,13},{9,10},{10,... | collective-permute-start | bytes 393224 | tf_op jit(solution)/shard_map/ppermute | solution.py:406
  34.4 2.8 %shard_map.111 = (bf16[256,2048]{1,0:T(8,128)(2,1)}, bf16[256,2048]{1,0:T(8,128)(2,1)}, f32[256,1024]{1,0:T(8,128)S(1)}, f32[8,128]{1,0:T(8,128)S(1)}) custom-call(s32[1,256]{1,0:T(1,128)S(1)} %get-tuple-element.51.length, f32[1,256]{1,0:T(1,128)S(1)} %get-tuple-element.71.inverse_rms, f32[1,2048]{1,0:T(1,128)S(1)} %bitcast.18, ...), custom_call_target="tpu_custom_call" | custom-call | flops 469762048 | bytes 9451520 | tf_op jit(solution)/shard_map/pallas_call | solution.py:384
  37.2 0.0 collective-permute-done.19.refs_2_
  37.2 0.8 %collective-permute-start.15 = (bf16[512,128]{1,0:T(8,128)(2,1)S(1)}, bf16[512,128]{1,0:T(8,128)(2,1)S(1)}, u32[]{:S(2)}, u32[]{:S(2)}) collective-permute-start(bf16[512,128]{1,0:T(8,128)(2,1)S(1)} %get-tuple-element.80), channel_id=1, source_target_pairs={{0,1},{1,0},{2,3},{3,2},{4,5},{5,4},{6,7},{7,6},{8,9},{9,8},{10,11... | collective-permute-start | bytes 393224 | tf_op jit(solution)/shard_map/ppermute | solution.py:406
  38.0 0.0 collective-permute-done.20.refs_3_
  38.0 0.3 shard_map.113
  38.3 1.5 %collective-permute-start.24 = (bf16[512,128]{1,0:T(8,128)(2,1)S(1)}, bf16[512,128]{1,0:T(8,128)(2,1)S(1)}, u32[]{:S(2)}, u32[]{:S(2)}) collective-permute-start(bf16[512,128]{1,0:T(8,128)(2,1)S(1)} %get-tuple-element.93), channel_id=1, source_target_pairs={{0,4},{1,3},{2,6},{3,1},{4,0},{5,7},{6,2},{7,5},{8,12},{9,11},{10,... | collective-permute-start | bytes 393224 | tf_op jit(solution)/shard_map/ppermute | solution.py:406
  39.8 0.1 collective-permute-start.25
  40.0 0.8 %collective-permute-start.26 = (bf16[512,128]{1,0:T(8,128)(2,1)S(1)}, bf16[512,128]{1,0:T(8,128)(2,1)S(1)}, u32[]{:S(2)}, u32[]{:S(2)}) collective-permute-start(bf16[512,128]{1,0:T(8,128)(2,1)S(1)} %get-tuple-element.95), channel_id=1, source_target_pairs={{0,1},{1,0},{2,3},{3,2},{4,5},{5,4},{6,7},{7,6},{8,9},{9,8},{10,11... | collective-permute-start | bytes 393224 | tf_op jit(solution)/shard_map/ppermute | solution.py:406
  40.7 0.0 collective-permute-done.17.refs_3_
  40.7 0.0 collective-permute-done.15.refs_1_
  40.7 0.3 shard_map.112
  41.0 0.7 %collective-permute-start.21 = (bf16[512,128]{1,0:T(8,128)(2,1)S(1)}, bf16[512,128]{1,0:T(8,128)(2,1)S(1)}, u32[]{:S(2)}, u32[]{:S(2)}) collective-permute-start(bf16[512,128]{1,0:T(8,128)(2,1)S(1)} %get-tuple-element.90), channel_id=1, source_target_pairs={{0,4},{1,3},{2,6},{3,1},{4,0},{5,7},{6,2},{7,5},{8,12},{9,11},{10,... | collective-permute-start | bytes 393224 | tf_op jit(solution)/shard_map/ppermute | solution.py:406
  41.8 0.5 %collective-permute-start.22 = (bf16[512,128]{1,0:T(8,128)(2,1)S(1)}, bf16[512,128]{1,0:T(8,128)(2,1)S(1)}, u32[]{:S(2)}, u32[]{:S(2)}) collective-permute-start(bf16[512,128]{1,0:T(8,128)(2,1)S(1)} %get-tuple-element.91), channel_id=1, source_target_pairs={{0,5},{1,2},{2,7},{3,0},{4,1},{5,6},{6,3},{7,4},{8,13},{9,10},{10,... | collective-permute-start | bytes 393224 | tf_op jit(solution)/shard_map/ppermute | solution.py:406
  42.3 1.1 %collective-permute-done.24.rest_6_ = bf16[512,128]{1,0:T(8,128)(2,1)S(1)} collective-permute-done((bf16[512,128]{1,0:T(8,128)(2,1)S(1)}, bf16[512,128]{1,0:T(8,128)(2,1)S(1)}, u32[]{:S(2)}, u32[]{:S(2)}) %collective-permute-start.24) | collective-permute-done | bytes 131104 | tf_op jit(solution)/shard_map/ppermute | solution.py:406
  43.4 3.4 %shard_map.114 = (bf16[256,2048]{1,0:T(8,128)(2,1)}, bf16[256,2048]{1,0:T(8,128)(2,1)}, f32[256,1024]{1,0:T(8,128)S(1)}, f32[8,128]{1,0:T(8,128)}) custom-call(s32[1,256]{1,0:T(1,128)S(1)} %get-tuple-element.51.length, f32[1,256]{1,0:T(1,128)S(1)} %get-tuple-element.71.inverse_rms, ...), custom_call_target="tpu_custom_call", output_to_operand_aliasing={{0}: (11, {}), {1}: (12, {})} | custom-call | flops 469762048 | bytes 11548672 | tf_op jit(solution)/shard_map/pallas_call | solution.py:384
  46.8 1.5 %shard_map.115.value_part = f32[256,2048]{1,0:T(8,128)S(1)} custom-call(s32[1,256]{1,0:T(1,128)S(1)} %get-tuple-element.51.length, bf16[256,2048]{1,0:T(8,128)(2,1)S(1)} %shard_map.103.refs_4_.queries, bf16[256,2048]{1,0:T(8,128)(2,1)S(1)} %get-tuple-element.53.keys, bf16[256,1024]{1,0:T(8,128)(2,1)S(1)} %get-tuple-element.75.grads.rest_0_, ...), custom_call_target="tpu_custom_call" | custom-call | flops 536870912 | bytes 5243904 | tf_op jit(solution)/shard_map/pallas_call | solution.py:384
  48.3 0.0 collective-permute-done.26.rest_9_
  48.3 0.0 collective-permute-done.21.rest_2_
  48.3 0.0 collective-permute-done.23.rest_5_
  48.3 2.1 %shard_map.116 = (bf16[256,2048]{1,0:T(8,128)(2,1)}, bf16[256,2048]{1,0:T(8,128)(2,1)}) custom-call(s32[1,256]{1,0:T(1,128)S(1)} %get-tuple-element.51.length, bf16[256,2048]{1,0:T(8,128)(2,1)S(1)} %get-tuple-element.53.keys, bf16[256,2048]{1,0:T(8,128)(2,1)S(1)} %get-tuple-element.54.values, f32[256,2048]{1,0:T(8,128)S(1)} %shard_map.115.value_part, ...), custom_call_target="tpu_custom_call" | custom-call | flops 268435456 | bytes 9438208 | tf_op jit(solution)/shard_map/pallas_call | solution.py:384
  (9 shorter events, 0.0 us)
Async XLA Ops:
  3.6 6.9 %collective-permute-start.2 = (bf16[512,128]{1,0:T(8,128)(2,1)S(1)}, bf16[512,128]{1,0:T(8,128)(2,1)S(1)}, u32[]{:S(2)}, u32[]{:S(2)}) collective-permute-start(bf16[512,128]{1,0:T(8,128)(2,1)S(1)} %get-tuple-element.56), channel_id=1, source_target_pairs={{0,5},{1,2},{2,7},{3,0},{4,1},{5,6},{6,3},{7,4},{8,13},{9,10},{10,... | collective-permute-start | bytes 393224 | tf_op jit(solution)/shard_map/ppermute | solution.py:406
  6.1 4.9 %collective-permute-start = (bf16[512,128]{1,0:T(8,128)(2,1)S(1)}, bf16[512,128]{1,0:T(8,128)(2,1)S(1)}, u32[]{:S(2)}, u32[]{:S(2)}) collective-permute-start(bf16[512,128]{1,0:T(8,128)(2,1)S(1)} %get-tuple-element.56), channel_id=1, source_target_pairs={{0,1},{1,0},{2,3},{3,2},{4,5},{5,4},{6,7},{7,6},{8,9},{9,8},{10,11... | collective-permute-start | bytes 393224 | tf_op jit(solution)/shard_map/ppermute | solution.py:406
  6.7 5.0 %collective-permute-start.1 = (bf16[512,128]{1,0:T(8,128)(2,1)S(1)}, bf16[512,128]{1,0:T(8,128)(2,1)S(1)}, u32[]{:S(2)}, u32[]{:S(2)}) collective-permute-start(bf16[512,128]{1,0:T(8,128)(2,1)S(1)} %get-tuple-element.52._.refs_0_), channel_id=1, source_target_pairs={{0,2},{1,5},{2,0},{3,7},{4,6},{5,1},{6,4},{7,3},{8,10},{9,13},{10,... | collective-permute-start | bytes 393224 | tf_op jit(solution)/shard_map/ppermute | solution.py:406
  7.6 6.8 %collective-permute-start.4 = (bf16[512,128]{1,0:T(8,128)(2,1)S(1)}, bf16[512,128]{1,0:T(8,128)(2,1)S(1)}, u32[]{:S(2)}, u32[]{:S(2)}) collective-permute-start(bf16[512,128]{1,0:T(8,128)(2,1)S(1)} %get-tuple-element.58.refs_0_), channel_id=1, source_target_pairs={{0,2},{1,5},{2,0},{3,7},{4,6},{5,1},{6,4},{7,3},{8,10},{9,13},{10,... | collective-permute-start | bytes 393224 | tf_op jit(solution)/shard_map/ppermute | solution.py:406
  8.8 5.8 %collective-permute-start.5 = (bf16[512,128]{1,0:T(8,128)(2,1)S(1)}, bf16[512,128]{1,0:T(8,128)(2,1)S(1)}, u32[]{:S(2)}, u32[]{:S(2)}) collective-permute-start(bf16[512,128]{1,0:T(8,128)(2,1)S(1)} %get-tuple-element.59), channel_id=1, source_target_pairs={{0,5},{1,2},{2,7},{3,0},{4,1},{5,6},{6,3},{7,4},{8,13},{9,10},{10,... | collective-permute-start | bytes 393224 | tf_op jit(solution)/shard_map/ppermute | solution.py:406
  10.6 3.9 %collective-permute-start.3 = (bf16[512,128]{1,0:T(8,128)(2,1)S(1)}, bf16[512,128]{1,0:T(8,128)(2,1)S(1)}, u32[]{:S(2)}, u32[]{:S(2)}) collective-permute-start(bf16[512,128]{1,0:T(8,128)(2,1)S(1)} %get-tuple-element.59), channel_id=1, source_target_pairs={{0,1},{1,0},{2,3},{3,2},{4,5},{5,4},{6,7},{7,6},{8,9},{9,8},{10,11... | collective-permute-start | bytes 393224 | tf_op jit(solution)/shard_map/ppermute | solution.py:406
  12.0 5.0 %collective-permute-start.9 = (bf16[512,128]{1,0:T(8,128)(2,1)S(1)}, bf16[512,128]{1,0:T(8,128)(2,1)S(1)}, u32[]{:S(2)}, u32[]{:S(2)}) collective-permute-start(bf16[512,128]{1,0:T(8,128)(2,1)S(1)} %get-tuple-element.64), channel_id=1, source_target_pairs={{0,4},{1,3},{2,6},{3,1},{4,0},{5,7},{6,2},{7,5},{8,12},{9,11},{10,... | collective-permute-start | bytes 393224 | tf_op jit(solution)/shard_map/ppermute | solution.py:406
  13.6 5.3 %collective-permute-start.10 = (bf16[512,128]{1,0:T(8,128)(2,1)S(1)}, bf16[512,128]{1,0:T(8,128)(2,1)S(1)}, u32[]{:S(2)}, u32[]{:S(2)}) collective-permute-start(bf16[512,128]{1,0:T(8,128)(2,1)S(1)} %get-tuple-element.65), channel_id=1, source_target_pairs={{0,5},{1,2},{2,7},{3,0},{4,1},{5,6},{6,3},{7,4},{8,13},{9,10},{10,... | collective-permute-start | bytes 393224 | tf_op jit(solution)/shard_map/ppermute | solution.py:406
  14.4 4.4 %collective-permute-start.11 = (bf16[512,128]{1,0:T(8,128)(2,1)S(1)}, bf16[512,128]{1,0:T(8,128)(2,1)S(1)}, u32[]{:S(2)}, u32[]{:S(2)}) collective-permute-start(bf16[512,128]{1,0:T(8,128)(2,1)S(1)} %get-tuple-element.66), channel_id=1, source_target_pairs={{0,1},{1,0},{2,3},{3,2},{4,5},{5,4},{6,7},{7,6},{8,9},{9,8},{10,11... | collective-permute-start | bytes 393224 | tf_op jit(solution)/shard_map/ppermute | solution.py:406
  14.8 5.0 %collective-permute-start.6 = (bf16[512,128]{1,0:T(8,128)(2,1)S(1)}, bf16[512,128]{1,0:T(8,128)(2,1)S(1)}, u32[]{:S(2)}, u32[]{:S(2)}) collective-permute-start(bf16[512,128]{1,0:T(8,128)(2,1)S(1)} %get-tuple-element.60), channel_id=1, source_target_pairs={{0,4},{1,3},{2,6},{3,1},{4,0},{5,7},{6,2},{7,5},{8,12},{9,11},{10,... | collective-permute-start | bytes 393224 | tf_op jit(solution)/shard_map/ppermute | solution.py:406
  16.4 4.4 %collective-permute-start.7 = (bf16[512,128]{1,0:T(8,128)(2,1)S(1)}, bf16[512,128]{1,0:T(8,128)(2,1)S(1)}, u32[]{:S(2)}, u32[]{:S(2)}) collective-permute-start(bf16[512,128]{1,0:T(8,128)(2,1)S(1)} %get-tuple-element.62), channel_id=1, source_target_pairs={{0,5},{1,2},{2,7},{3,0},{4,1},{5,6},{6,3},{7,4},{8,13},{9,10},{10,... | collective-permute-start | bytes 393224 | tf_op jit(solution)/shard_map/ppermute | solution.py:406
  17.0 3.8 %collective-permute-start.8 = (bf16[512,128]{1,0:T(8,128)(2,1)S(1)}, bf16[512,128]{1,0:T(8,128)(2,1)S(1)}, u32[]{:S(2)}, u32[]{:S(2)}) collective-permute-start(bf16[512,128]{1,0:T(8,128)(2,1)S(1)} %get-tuple-element.63), channel_id=1, source_target_pairs={{0,1},{1,0},{2,3},{3,2},{4,5},{5,4},{6,7},{7,6},{8,9},{9,8},{10,11... | collective-permute-start | bytes 393224 | tf_op jit(solution)/shard_map/ppermute | solution.py:406
  17.3 1.5 %copy-start = (bf16[1,256,2048]{2,1,0:T(8,128)(2,1)S(1)}, bf16[1,256,2048]{2,1,0:T(8,128)(2,1)}, u32[]{:S(2)}) copy-start(bf16[1,256,2048]{2,1,0:T(8,128)(2,1)} %param.10) | copy-start | bytes 3145732
  17.3 1.5 %copy-start.1 = (f32[2048]{0:T(1024)S(1)}, f32[2048]{0:T(1024)}, u32[]{:S(2)}) copy-start(f32[2048]{0:T(1024)} %param.11) | copy-start | bytes 24580
  21.5 4.5 %collective-permute-start.14 = (f32[2,256]{1,0:T(2,128)S(1)}, f32[2,256]{1,0:T(2,128)S(1)}, u32[]{:S(2)}, u32[]{:S(2)}) collective-permute-start(f32[2,256]{1,0:T(2,128)S(1)} %get-tuple-element.68.rest_0_), channel_id=1, source_target_pairs={{0,16},{8,24},{16,0},{24,8},{1,17},{9,25},{17,1},{25,9},{2,18},{10... | collective-permute-start | bytes 6152 | tf_op jit(solution)/shard_map/ppermute | solution.py:433
  24.1 5.4 %collective-permute-start.13 = (f32[2,256]{1,0:T(2,128)S(1)}, f32[2,256]{1,0:T(2,128)S(1)}, u32[]{:S(2)}, u32[]{:S(2)}) collective-permute-start(f32[2,256]{1,0:T(2,128)S(1)} %get-tuple-element.68.rest_0_), channel_id=1, source_target_pairs={{0,24},{8,16},{16,8},{24,0},{1,25},{9,17},{17,9},{25,1},{2,26},{10... | collective-permute-start | bytes 6152 | tf_op jit(solution)/shard_map/ppermute | solution.py:433
  25.5 4.0 %collective-permute-start.12 = (f32[2,256]{1,0:T(2,128)S(1)}, f32[2,256]{1,0:T(2,128)S(1)}, u32[]{:S(2)}, u32[]{:S(2)}) collective-permute-start(f32[2,256]{1,0:T(2,128)S(1)} %get-tuple-element.68.rest_0_), channel_id=1, source_target_pairs={{0,8},{8,0},{16,24},{24,16},{1,9},{9,1},{17,25},{25,17},{2,10},{10... | collective-permute-start | bytes 6152 | tf_op jit(solution)/shard_map/ppermute | solution.py:433
  30.1 7.1 %collective-permute-start.19 = (bf16[512,128]{1,0:T(8,128)(2,1)S(1)}, bf16[512,128]{1,0:T(8,128)(2,1)S(1)}, u32[]{:S(2)}, u32[]{:S(2)}) collective-permute-start(bf16[512,128]{1,0:T(8,128)(2,1)S(1)} %get-tuple-element.83.refs_0_), channel_id=1, source_target_pairs={{0,2},{1,5},{2,0},{3,7},{4,6},{5,1},{6,4},{7,3},{8,10},{9,13},{10,... | collective-permute-start | bytes 393224 | tf_op jit(solution)/shard_map/ppermute | solution.py:406
  31.0 7.0 %collective-permute-start.20 = (bf16[512,128]{1,0:T(8,128)(2,1)S(1)}, bf16[512,128]{1,0:T(8,128)(2,1)S(1)}, u32[]{:S(2)}, u32[]{:S(2)}) collective-permute-start(bf16[512,128]{1,0:T(8,128)(2,1)S(1)} %get-tuple-element.84), channel_id=1, source_target_pairs={{0,5},{1,2},{2,7},{3,0},{4,1},{5,6},{6,3},{7,4},{8,13},{9,10},{10,... | collective-permute-start | bytes 393224 | tf_op jit(solution)/shard_map/ppermute | solution.py:406
  31.0 7.0 %collective-permute-start.18 = (bf16[512,128]{1,0:T(8,128)(2,1)S(1)}, bf16[512,128]{1,0:T(8,128)(2,1)S(1)}, u32[]{:S(2)}, u32[]{:S(2)}) collective-permute-start(bf16[512,128]{1,0:T(8,128)(2,1)S(1)} %get-tuple-element.84), channel_id=1, source_target_pairs={{0,1},{1,0},{2,3},{3,2},{4,5},{5,4},{6,7},{7,6},{8,9},{9,8},{10,11... | collective-permute-start | bytes 393224 | tf_op jit(solution)/shard_map/ppermute | solution.py:406
  32.9 7.0 %collective-permute-start.16 = (bf16[512,128]{1,0:T(8,128)(2,1)S(1)}, bf16[512,128]{1,0:T(8,128)(2,1)S(1)}, u32[]{:S(2)}, u32[]{:S(2)}) collective-permute-start(bf16[512,128]{1,0:T(8,128)(2,1)S(1)} %get-tuple-element.79.refs_0_), channel_id=1, source_target_pairs={{0,2},{1,5},{2,0},{3,7},{4,6},{5,1},{6,4},{7,3},{8,10},{9,13},{10,... | collective-permute-start | bytes 393224 | tf_op jit(solution)/shard_map/ppermute | solution.py:406
  33.8 6.9 %collective-permute-start.17 = (bf16[512,128]{1,0:T(8,128)(2,1)S(1)}, bf16[512,128]{1,0:T(8,128)(2,1)S(1)}, u32[]{:S(2)}, u32[]{:S(2)}) collective-permute-start(bf16[512,128]{1,0:T(8,128)(2,1)S(1)} %get-tuple-element.80), channel_id=1, source_target_pairs={{0,5},{1,2},{2,7},{3,0},{4,1},{5,6},{6,3},{7,4},{8,13},{9,10},{10,... | collective-permute-start | bytes 393224 | tf_op jit(solution)/shard_map/ppermute | solution.py:406
  37.2 3.6 %collective-permute-start.15 = (bf16[512,128]{1,0:T(8,128)(2,1)S(1)}, bf16[512,128]{1,0:T(8,128)(2,1)S(1)}, u32[]{:S(2)}, u32[]{:S(2)}) collective-permute-start(bf16[512,128]{1,0:T(8,128)(2,1)S(1)} %get-tuple-element.80), channel_id=1, source_target_pairs={{0,1},{1,0},{2,3},{3,2},{4,5},{5,4},{6,7},{7,6},{8,9},{9,8},{10,11... | collective-permute-start | bytes 393224 | tf_op jit(solution)/shard_map/ppermute | solution.py:406
  38.3 5.0 %collective-permute-start.24 = (bf16[512,128]{1,0:T(8,128)(2,1)S(1)}, bf16[512,128]{1,0:T(8,128)(2,1)S(1)}, u32[]{:S(2)}, u32[]{:S(2)}) collective-permute-start(bf16[512,128]{1,0:T(8,128)(2,1)S(1)} %get-tuple-element.93), channel_id=1, source_target_pairs={{0,4},{1,3},{2,6},{3,1},{4,0},{5,7},{6,2},{7,5},{8,12},{9,11},{10,... | collective-permute-start | bytes 393224 | tf_op jit(solution)/shard_map/ppermute | solution.py:406
  39.8 8.4 %collective-permute-start.25 = (bf16[512,128]{1,0:T(8,128)(2,1)S(1)}, bf16[512,128]{1,0:T(8,128)(2,1)S(1)}, u32[]{:S(2)}, u32[]{:S(2)}) collective-permute-start(bf16[512,128]{1,0:T(8,128)(2,1)S(1)} %get-tuple-element.94), channel_id=1, source_target_pairs={{0,5},{1,2},{2,7},{3,0},{4,1},{5,6},{6,3},{7,4},{8,13},{9,10},{10,... | collective-permute-start | bytes 393224 | tf_op jit(solution)/shard_map/ppermute | solution.py:406
  40.0 8.3 %collective-permute-start.26 = (bf16[512,128]{1,0:T(8,128)(2,1)S(1)}, bf16[512,128]{1,0:T(8,128)(2,1)S(1)}, u32[]{:S(2)}, u32[]{:S(2)}) collective-permute-start(bf16[512,128]{1,0:T(8,128)(2,1)S(1)} %get-tuple-element.95), channel_id=1, source_target_pairs={{0,1},{1,0},{2,3},{3,2},{4,5},{5,4},{6,7},{7,6},{8,9},{9,8},{10,11... | collective-permute-start | bytes 393224 | tf_op jit(solution)/shard_map/ppermute | solution.py:406
  41.0 7.2 %collective-permute-start.21 = (bf16[512,128]{1,0:T(8,128)(2,1)S(1)}, bf16[512,128]{1,0:T(8,128)(2,1)S(1)}, u32[]{:S(2)}, u32[]{:S(2)}) collective-permute-start(bf16[512,128]{1,0:T(8,128)(2,1)S(1)} %get-tuple-element.90), channel_id=1, source_target_pairs={{0,4},{1,3},{2,6},{3,1},{4,0},{5,7},{6,2},{7,5},{8,12},{9,11},{10,... | collective-permute-start | bytes 393224 | tf_op jit(solution)/shard_map/ppermute | solution.py:406
  41.8 6.5 %collective-permute-start.22 = (bf16[512,128]{1,0:T(8,128)(2,1)S(1)}, bf16[512,128]{1,0:T(8,128)(2,1)S(1)}, u32[]{:S(2)}, u32[]{:S(2)}) collective-permute-start(bf16[512,128]{1,0:T(8,128)(2,1)S(1)} %get-tuple-element.91), channel_id=1, source_target_pairs={{0,5},{1,2},{2,7},{3,0},{4,1},{5,6},{6,3},{7,4},{8,13},{9,10},{10,... | collective-permute-start | bytes 393224 | tf_op jit(solution)/shard_map/ppermute | solution.py:406
  43.4 4.9 %collective-permute-start.23 = (bf16[512,128]{1,0:T(8,128)(2,1)S(1)}, bf16[512,128]{1,0:T(8,128)(2,1)S(1)}, u32[]{:S(2)}, u32[]{:S(2)}) collective-permute-start(bf16[512,128]{1,0:T(8,128)(2,1)S(1)} %get-tuple-element.92), channel_id=1, source_target_pairs={{0,1},{1,0},{2,3},{3,2},{4,5},{5,4},{6,7},{7,6},{8,9},{9,8},{10,11... | collective-permute-start | bytes 393224 | tf_op jit(solution)/shard_map/ppermute | solution.py:406

commit v13 on v12

--- a/solution.py
+++ b/solution.py
@@ -326,9 +326,10 @@
             here = slice((head + 1 - group) * HD, (head + 1) * HD)
             there = slice((place + 1 - group) * HD, (place + 1) * HD)
             for j, (src, dst) in enumerate(((attended, attended_hbm), (query_grad, query_hbm))):
-                copy = pltpu.make_async_copy(src.at[:, here], dst.at[:, there], sems.at[head // group, j])
-                copy.start()
-                copies.append(copy)
+                some = row_copies(src.at[:, here], dst.at[:, there], sems.at[head // group, j])
+                for copy in some:
+                    copy.start()
+                copies += some
     for copy in copies:
         copy.wait()
 
@@ -365,9 +366,10 @@
         if (head + 1) % group == 0:
             done = slice((head + 1 - group) * HD, (head + 1) * HD)
             for j, (src, dst) in enumerate(((key_grad, key_hbm), (value_grad, value_hbm))):
-                copy = pltpu.make_async_copy(src.at[:, done], dst.at[:, done], sems.at[j, head // group])
-                copy.start()
-                copies.append(copy)
+                some = row_copies(src.at[:, done], dst.at[:, done], sems.at[head // group, j])
+                for copy in some:
+                    copy.start()
+                copies += some
     for copy in copies:
         copy.wait()
 
@@ -514,7 +516,7 @@
         *results, key_part, token = call(
             functools.partial(query_kernel, piece, scale),
             [narrow, narrow, wide_piece, shape((8, HD), F32)], operands,
-            [pltpu.VMEM(narrow_piece.shape, BF16)] * 2 + [mask, pltpu.SemaphoreType.DMA((heads // group, 2))],
+            [pltpu.VMEM(narrow_piece.shape, BF16)] * 2 + [mask, pltpu.SemaphoreType.DMA((heads // group, 2, 4))],
             unit * (3 * rows + HD) // BACKWARD_PIECES, range(last, len(operands)),
             after=tuple(sums[0] for sums in mixed), out_specs=[HBM, HBM, VMEM, VMEM],
             aliases={last + j: j for j in range(len(results))},
@@ -532,7 +534,7 @@
     key_grad, value_grad = call(
         functools.partial(final_kernel, grid, counts),
         [narrow, narrow], (length, key, value, value_part, *key_parts, *below),
-        [pltpu.VMEM(narrow.shape, BF16)] * 2 + [pltpu.VMEM((features, HD), BF16), sems],
+        [pltpu.VMEM(narrow.shape, BF16)] * 2 + [pltpu.VMEM((features, HD), BF16), pltpu.SemaphoreType.DMA((heads, 2, 4))],
         2 * unit * HD, out_specs=[HBM, HBM],
     )
     return attended[None], query_grad[None], key_grad[None], value_grad[None]

time: 50.8 us -> 52 us (1.024)
  Pallas kernels: 18.5 us -> 19.8 us
    pallas_call x15, Pallas kernels: 18.5 us -> 19.8 us  [call(): pl.pallas_call(kernel, out_shape=out_shape, in_specs=specs + [ANY] * len(...]
where the time goes in v13:
time: 52 us; the launch traced here: 51.8 us
  starting transfers between devices  23.1 us (44%)
  Pallas kernels  19.8 us (38%)
  waiting for transfers between devices  7.32 us (14%)
  between operations  1.63 us (3%)
    pallas_call x15, Pallas kernels, call(): pl.pallas_call(kernel, out_shape=out_shape, in_specs=specs + [ANY] * len(...  19.8 us
    ppermute x24, starting transfers between devices, line_send(): return lax.ppermute(block, 'seg', moves)  18.9 us
    ppermute x3, starting transfers between devices, token_sums(): parts.append(lax.ppermute(sums, 'head', moves))  4.23 us
    ppermute x3, waiting for transfers between devices, token_sums(): parts.append(lax.ppermute(sums, 'head', moves))  3.8 us
    ppermute x24, waiting for transfers between devices, line_send(): return lax.ppermute(block, 'seg', moves)  3.52 us
  transfers between devices with their start and end apart: 27, of which 8 were waited for; matrix products, arithmetic and copies ran while one was open for 0% of the time, Pallas kernels for 25%

profile of v13, /device:TPU:0, one launch (start us, length us, event | category | flops | bytes accessed | tf_op | source)
XLA Modules:
  0.0 51.8 jit_solution(15897834025945167993)
XLA Ops:
  1.3 2.3 %shard_map.102 = (bf16[256,2048]{1,0:T(8,128)(2,1)S(1)}, bf16[256,2048]{1,0:T(8,128)(2,1)S(1)}, s32[1,256]{1,0:T(1,128)S(1)}, f32[16,128]{1,0:T(8,128)S(1)}, f32...) custom-call(s32[1]{0:T(128)S(6)} %copy.15.seg_len, ...), custom_call_target="tpu_custom_call" | custom-call | flops 134217728 | bytes 4736036 | tf_op jit(solution)/shard_map/pallas_call | solution.py:386
  3.6 2.5 %collective-permute-start.2 = (bf16[512,128]{1,0:T(8,128)(2,1)S(1)}, bf16[512,128]{1,0:T(8,128)(2,1)S(1)}, u32[]{:S(2)}, u32[]{:S(2)}) collective-permute-start(bf16[512,128]{1,0:T(8,128)(2,1)S(1)} %get-tuple-element.56), channel_id=1, source_target_pairs={{0,5},{1,2},{2,7},{3,0},{4,1},{5,6},{6,3},{7,4},{8,13},{9,10},{10,... | collective-permute-start | bytes 393224 | tf_op jit(solution)/shard_map/ppermute | solution.py:408
  6.1 0.6 %collective-permute-start = (bf16[512,128]{1,0:T(8,128)(2,1)S(1)}, bf16[512,128]{1,0:T(8,128)(2,1)S(1)}, u32[]{:S(2)}, u32[]{:S(2)}) collective-permute-start(bf16[512,128]{1,0:T(8,128)(2,1)S(1)} %get-tuple-element.56), channel_id=1, source_target_pairs={{0,1},{1,0},{2,3},{3,2},{4,5},{5,4},{6,7},{7,6},{8,9},{9,8},{10,11... | collective-permute-start | bytes 393224 | tf_op jit(solution)/shard_map/ppermute | solution.py:408
  6.7 0.9 %collective-permute-start.1 = (bf16[512,128]{1,0:T(8,128)(2,1)S(1)}, bf16[512,128]{1,0:T(8,128)(2,1)S(1)}, u32[]{:S(2)}, u32[]{:S(2)}) collective-permute-start(bf16[512,128]{1,0:T(8,128)(2,1)S(1)} %get-tuple-element.52._.refs_0_), channel_id=1, source_target_pairs={{0,2},{1,5},{2,0},{3,7},{4,6},{5,1},{6,4},{7,3},{8,10},{9,13},{10,... | collective-permute-start | bytes 393224 | tf_op jit(solution)/shard_map/ppermute | solution.py:408
  7.6 1.1 %collective-permute-start.4 = (bf16[512,128]{1,0:T(8,128)(2,1)S(1)}, bf16[512,128]{1,0:T(8,128)(2,1)S(1)}, u32[]{:S(2)}, u32[]{:S(2)}) collective-permute-start(bf16[512,128]{1,0:T(8,128)(2,1)S(1)} %get-tuple-element.58.refs_0_), channel_id=1, source_target_pairs={{0,2},{1,5},{2,0},{3,7},{4,6},{5,1},{6,4},{7,3},{8,10},{9,13},{10,... | collective-permute-start | bytes 393224 | tf_op jit(solution)/shard_map/ppermute | solution.py:408
  8.8 0.6 %collective-permute-start.5 = (bf16[512,128]{1,0:T(8,128)(2,1)S(1)}, bf16[512,128]{1,0:T(8,128)(2,1)S(1)}, u32[]{:S(2)}, u32[]{:S(2)}) collective-permute-start(bf16[512,128]{1,0:T(8,128)(2,1)S(1)} %get-tuple-element.59), channel_id=1, source_target_pairs={{0,5},{1,2},{2,7},{3,0},{4,1},{5,6},{6,3},{7,4},{8,13},{9,10},{10,... | collective-permute-start | bytes 393224 | tf_op jit(solution)/shard_map/ppermute | solution.py:408
  9.3 1.2 %shard_map.103.refs_4_.queries = bf16[256,2048]{1,0:T(8,128)(2,1)S(1)} custom-call(bf16[256,2048]{1,0:T(8,128)(2,1)} %bitcast.20, bf16[512,128]{1,0:T(8,128)(2,1)S(1)} %get-tuple-element.52._.refs_0_), custom_call_target="tpu_custom_call" | custom-call | bytes 2097152 | tf_op jit(solution)/shard_map/pallas_call | solution.py:386
  10.6 0.0 collective-permute-done.2.refs_3_
  10.6 0.5 collective-permute-start.3
  11.1 0.0 collective-permute-done.refs_1_
  11.1 0.6 %collective-permute-done.1.refs_2_ = bf16[512,128]{1,0:T(8,128)(2,1)S(1)} collective-permute-done((bf16[512,128]{1,0:T(8,128)(2,1)S(1)}, bf16[512,128]{1,0:T(8,128)(2,1)S(1)}, u32[]{:S(2)}, u32[]{:S(2)}) %collective-permute-start.1) | collective-permute-done | bytes 131104 | tf_op jit(solution)/shard_map/ppermute | solution.py:408
  11.7 0.3 shard_map.104
  12.0 1.6 %collective-permute-start.9 = (bf16[512,128]{1,0:T(8,128)(2,1)S(1)}, bf16[512,128]{1,0:T(8,128)(2,1)S(1)}, u32[]{:S(2)}, u32[]{:S(2)}) collective-permute-start(bf16[512,128]{1,0:T(8,128)(2,1)S(1)} %get-tuple-element.64), channel_id=1, source_target_pairs={{0,4},{1,3},{2,6},{3,1},{4,0},{5,7},{6,2},{7,5},{8,12},{9,11},{10,... | collective-permute-start | bytes 393224 | tf_op jit(solution)/shard_map/ppermute | solution.py:408
  13.6 0.4 collective-permute-start.10
  14.0 0.4 collective-permute-done.4.refs_2_
  14.4 0.1 collective-permute-start.11
  14.5 0.0 collective-permute-done.5.refs_3_
  14.5 0.0 collective-permute-done.3.refs_1_
  14.5 0.3 shard_map.106
  14.8 1.6 %collective-permute-start.6 = (bf16[512,128]{1,0:T(8,128)(2,1)S(1)}, bf16[512,128]{1,0:T(8,128)(2,1)S(1)}, u32[]{:S(2)}, u32[]{:S(2)}) collective-permute-start(bf16[512,128]{1,0:T(8,128)(2,1)S(1)} %get-tuple-element.60), channel_id=1, source_target_pairs={{0,4},{1,3},{2,6},{3,1},{4,0},{5,7},{6,2},{7,5},{8,12},{9,11},{10,... | collective-permute-start | bytes 393224 | tf_op jit(solution)/shard_map/ppermute | solution.py:408
  16.4 0.6 %collective-permute-start.7 = (bf16[512,128]{1,0:T(8,128)(2,1)S(1)}, bf16[512,128]{1,0:T(8,128)(2,1)S(1)}, u32[]{:S(2)}, u32[]{:S(2)}) collective-permute-start(bf16[512,128]{1,0:T(8,128)(2,1)S(1)} %get-tuple-element.62), channel_id=1, source_target_pairs={{0,5},{1,2},{2,7},{3,0},{4,1},{5,6},{6,3},{7,4},{8,13},{9,10},{10,... | collective-permute-start | bytes 393224 | tf_op jit(solution)/shard_map/ppermute | solution.py:408
  16.9 0.1 collective-permute-done.9.rest_0_
  17.0 0.3 collective-permute-start.8
  17.4 1.5 %shard_map.105.local = f32[256,2048]{1,0:T(8,128)S(1)} custom-call(s32[1,256]{1,0:T(1,128)S(1)} %get-tuple-element.51.length, bf16[256,2048]{1,0:T(8,128)(2,1)S(1)} %shard_map.103.refs_4_.queries, bf16[256,2048]{1,0:T(8,128)(2,1)S(1)} %get-tuple-element.53.keys, bf16[256,2048]{1,0:T(8,128)(2,1)S(1)} %get-tuple-element.54.values, ...), custom_call_target="tpu_custom_call" | custom-call | flops 536870912 | bytes 5243904 | tf_op jit(solution)/shard_map/pallas_call | solution.py:386
  18.8 0.0 collective-permute-done.10.rest_2_
  18.9 0.7 %shard_map.107 = (f32[256,1024]{1,0:T(8,128)S(1)}, f32[2,256]{1,0:T(2,128)S(1)}, bf16[1024,128]{1,0:T(8,128)(2,1)S(1)}) custom-call(s32[1,256]{1,0:T(1,128)S(1)} %get-tuple-element.51.length, bf16[256,2048]{1,0:T(8,128)(2,1)S(1)} %shard_map.103.refs_4_.queries, f32[256,2048]{1,0:T(8,128)S(1)} %shard_map.105.local, bf16[256,2048]{1,0:T(8,128)(2,1)S(1)} %bitcast.10, ...), custom_call_target="tpu_custom_call" | custom-call | flops 67108864 | bytes 6040576 | tf_op jit(solution)/shard_map/pallas_call | solution.py:386
  19.5 0.3 collective-permute-done.6.rest_0_
  19.8 0.9 %collective-permute-done.7.rest_2_ = bf16[512,128]{1,0:T(8,128)(2,1)S(1)} collective-permute-done((bf16[512,128]{1,0:T(8,128)(2,1)S(1)}, bf16[512,128]{1,0:T(8,128)(2,1)S(1)}, u32[]{:S(2)}, u32[]{:S(2)}) %collective-permute-start.7) | collective-permute-done | bytes 131104 | tf_op jit(solution)/shard_map/ppermute | solution.py:408
  20.8 0.0 collective-permute-done.8.rest_3_
  20.8 0.7 %shard_map.108 = (f32[256,1024]{1,0:T(8,128)S(1)}, f32[2,256]{1,0:T(2,128)S(1)}, bf16[1024,128]{1,0:T(8,128)(2,1)S(1)}) custom-call(s32[1,256]{1,0:T(1,128)S(1)} %get-tuple-element.51.length, bf16[256,2048]{1,0:T(8,128)(2,1)S(1)} %shard_map.103.refs_4_.queries, f32[256,2048]{1,0:T(8,128)S(1)} %shard_map.105.local, bf16[256,2048]{1,0:T(8,128)(2,1)S(1)} %bitcast.11, ...), custom_call_target="tpu_custom_call" | custom-call | flops 67108864 | bytes 6042624 | tf_op jit(solution)/shard_map/pallas_call | solution.py:386
  21.5 2.7 %collective-permute-start.14 = (f32[2,256]{1,0:T(2,128)S(1)}, f32[2,256]{1,0:T(2,128)S(1)}, u32[]{:S(2)}, u32[]{:S(2)}) collective-permute-start(f32[2,256]{1,0:T(2,128)S(1)} %get-tuple-element.68.rest_0_), channel_id=1, source_target_pairs={{0,16},{8,24},{16,0},{24,8},{1,17},{9,25},{17,1},{25,9},{2,18},{10... | collective-permute-start | bytes 6152 | tf_op jit(solution)/shard_map/ppermute | solution.py:435
  24.1 1.3 %collective-permute-start.13 = (f32[2,256]{1,0:T(2,128)S(1)}, f32[2,256]{1,0:T(2,128)S(1)}, u32[]{:S(2)}, u32[]{:S(2)}) collective-permute-start(f32[2,256]{1,0:T(2,128)S(1)} %get-tuple-element.68.rest_0_), channel_id=1, source_target_pairs={{0,24},{8,16},{16,8},{24,0},{1,25},{9,17},{17,9},{25,1},{2,26},{10... | collective-permute-start | bytes 6152 | tf_op jit(solution)/shard_map/ppermute | solution.py:435
  25.5 0.2 collective-permute-start.12
  25.7 0.3 collective-permute-done.14.rest_3_
  26.0 3.5 %collective-permute-done.13.rest_2_ = f32[2,256]{1,0:T(2,128)S(1)} collective-permute-done((f32[2,256]{1,0:T(2,128)S(1)}, f32[2,256]{1,0:T(2,128)S(1)}, u32[]{:S(2)}, u32[]{:S(2)}) %collective-permute-start.13) | collective-permute-done | bytes 2080 | tf_op jit(solution)/shard_map/ppermute | solution.py:435
  29.5 0.6 %shard_map.110 = (bf16[256,1024]{1,0:T(8,128)(2,1)S(1)}, bf16[512,128]{1,0:T(8,128)(2,1)S(1)}, bf16[512,128]{1,0:T(8,128)(2,1)S(1)}) custom-call(s32[1,256]{1,0:T(1,128)S(1)} %get-tuple-element.51.length, bf16[256,2048]{1,0:T(8,128)(2,1)S(1)} %shard_map.103.refs_4_.queries, bf16[256,2048]{1,0:T(8,128)(2,1)S(1)} %bitcast.12, f32[1,2048]{1,0:T(1,128)S(1)} %bitcast.16, ...), custom_call_target="tpu_custom_call" | custom-call | flops 67108864 | bytes 4998144 | tf_op jit(solution)/shard_map/pallas_call | solution.py:386
  30.1 0.9 %collective-permute-start.19 = (bf16[512,128]{1,0:T(8,128)(2,1)S(1)}, bf16[512,128]{1,0:T(8,128)(2,1)S(1)}, u32[]{:S(2)}, u32[]{:S(2)}) collective-permute-start(bf16[512,128]{1,0:T(8,128)(2,1)S(1)} %get-tuple-element.83.refs_0_), channel_id=1, source_target_pairs={{0,2},{1,5},{2,0},{3,7},{4,6},{5,1},{6,4},{7,3},{8,10},{9,13},{10,... | collective-permute-start | bytes 393224 | tf_op jit(solution)/shard_map/ppermute | solution.py:408
  31.0 0.0 collective-permute-start.20
  31.0 1.3 %collective-permute-start.18 = (bf16[512,128]{1,0:T(8,128)(2,1)S(1)}, bf16[512,128]{1,0:T(8,128)(2,1)S(1)}, u32[]{:S(2)}, u32[]{:S(2)}) collective-permute-start(bf16[512,128]{1,0:T(8,128)(2,1)S(1)} %get-tuple-element.84), channel_id=1, source_target_pairs={{0,1},{1,0},{2,3},{3,2},{4,5},{5,4},{6,7},{7,6},{8,9},{9,8},{10,11... | collective-permute-start | bytes 393224 | tf_op jit(solution)/shard_map/ppermute | solution.py:408
  32.3 0.6 %shard_map.109 = (bf16[256,1024]{1,0:T(8,128)(2,1)S(1)}, bf16[512,128]{1,0:T(8,128)(2,1)S(1)}, bf16[512,128]{1,0:T(8,128)(2,1)S(1)}, f32[1,256]{1,0:T(1,128)S(1)}) custom-call(s32[1,256]{1,0:T(1,128)S(1)} %get-tuple-element.51.length, bf16[256,2048]{1,0:T(8,128)(2,1)S(1)} %shard_map.103.refs_4_.queries, bf16[256,2048]{1,0:T(8,128)(2,1)S(1)} %bitcast.13, ...), custom_call_target="tpu_custom_call" | custom-call | flops 67108864 | bytes 4999168 | tf_op jit(solution)/shard_map/pallas_call | solution.py:386
  32.9 0.9 %collective-permute-start.16 = (bf16[512,128]{1,0:T(8,128)(2,1)S(1)}, bf16[512,128]{1,0:T(8,128)(2,1)S(1)}, u32[]{:S(2)}, u32[]{:S(2)}) collective-permute-start(bf16[512,128]{1,0:T(8,128)(2,1)S(1)} %get-tuple-element.79.refs_0_), channel_id=1, source_target_pairs={{0,2},{1,5},{2,0},{3,7},{4,6},{5,1},{6,4},{7,3},{8,10},{9,13},{10,... | collective-permute-start | bytes 393224 | tf_op jit(solution)/shard_map/ppermute | solution.py:408
  33.8 0.5 %collective-permute-start.17 = (bf16[512,128]{1,0:T(8,128)(2,1)S(1)}, bf16[512,128]{1,0:T(8,128)(2,1)S(1)}, u32[]{:S(2)}, u32[]{:S(2)}) collective-permute-start(bf16[512,128]{1,0:T(8,128)(2,1)S(1)} %get-tuple-element.80), channel_id=1, source_target_pairs={{0,5},{1,2},{2,7},{3,0},{4,1},{5,6},{6,3},{7,4},{8,13},{9,10},{10,... | collective-permute-start | bytes 393224 | tf_op jit(solution)/shard_map/ppermute | solution.py:408
  34.4 3.0 %shard_map.111 = (bf16[256,2048]{1,0:T(8,128)(2,1)}, bf16[256,2048]{1,0:T(8,128)(2,1)}, f32[256,1024]{1,0:T(8,128)S(1)}, f32[8,128]{1,0:T(8,128)S(1)}) custom-call(s32[1,256]{1,0:T(1,128)S(1)} %get-tuple-element.51.length, f32[1,256]{1,0:T(1,128)S(1)} %get-tuple-element.71.inverse_rms, f32[1,2048]{1,0:T(1,128)S(1)} %bitcast.18, ...), custom_call_target="tpu_custom_call" | custom-call | flops 469762048 | bytes 9451520 | tf_op jit(solution)/shard_map/pallas_call | solution.py:386
  37.4 0.0 collective-permute-done.19.refs_2_
  37.4 0.8 %collective-permute-start.15 = (bf16[512,128]{1,0:T(8,128)(2,1)S(1)}, bf16[512,128]{1,0:T(8,128)(2,1)S(1)}, u32[]{:S(2)}, u32[]{:S(2)}) collective-permute-start(bf16[512,128]{1,0:T(8,128)(2,1)S(1)} %get-tuple-element.80), channel_id=1, source_target_pairs={{0,1},{1,0},{2,3},{3,2},{4,5},{5,4},{6,7},{7,6},{8,9},{9,8},{10,11... | collective-permute-start | bytes 393224 | tf_op jit(solution)/shard_map/ppermute | solution.py:408
  38.2 0.0 collective-permute-done.20.refs_3_
  38.2 0.0 collective-permute-done.18.refs_1_
  38.2 0.3 shard_map.113
  38.5 1.5 %collective-permute-start.24 = (bf16[512,128]{1,0:T(8,128)(2,1)S(1)}, bf16[512,128]{1,0:T(8,128)(2,1)S(1)}, u32[]{:S(2)}, u32[]{:S(2)}) collective-permute-start(bf16[512,128]{1,0:T(8,128)(2,1)S(1)} %get-tuple-element.93), channel_id=1, source_target_pairs={{0,4},{1,3},{2,6},{3,1},{4,0},{5,7},{6,2},{7,5},{8,12},{9,11},{10,... | collective-permute-start | bytes 393224 | tf_op jit(solution)/shard_map/ppermute | solution.py:408
  40.0 0.1 collective-permute-start.25
  40.2 0.0 collective-permute-done.16.refs_2_
  40.2 0.8 %collective-permute-start.26 = (bf16[512,128]{1,0:T(8,128)(2,1)S(1)}, bf16[512,128]{1,0:T(8,128)(2,1)S(1)}, u32[]{:S(2)}, u32[]{:S(2)}) collective-permute-start(bf16[512,128]{1,0:T(8,128)(2,1)S(1)} %get-tuple-element.95), channel_id=1, source_target_pairs={{0,1},{1,0},{2,3},{3,2},{4,5},{5,4},{6,7},{7,6},{8,9},{9,8},{10,11... | collective-permute-start | bytes 393224 | tf_op jit(solution)/shard_map/ppermute | solution.py:408
  40.9 0.0 collective-permute-done.15.refs_1_
  40.9 0.3 shard_map.112
  41.2 0.7 %collective-permute-start.21 = (bf16[512,128]{1,0:T(8,128)(2,1)S(1)}, bf16[512,128]{1,0:T(8,128)(2,1)S(1)}, u32[]{:S(2)}, u32[]{:S(2)}) collective-permute-start(bf16[512,128]{1,0:T(8,128)(2,1)S(1)} %get-tuple-element.90), channel_id=1, source_target_pairs={{0,4},{1,3},{2,6},{3,1},{4,0},{5,7},{6,2},{7,5},{8,12},{9,11},{10,... | collective-permute-start | bytes 393224 | tf_op jit(solution)/shard_map/ppermute | solution.py:408
  41.9 0.5 %collective-permute-start.22 = (bf16[512,128]{1,0:T(8,128)(2,1)S(1)}, bf16[512,128]{1,0:T(8,128)(2,1)S(1)}, u32[]{:S(2)}, u32[]{:S(2)}) collective-permute-start(bf16[512,128]{1,0:T(8,128)(2,1)S(1)} %get-tuple-element.91), channel_id=1, source_target_pairs={{0,5},{1,2},{2,7},{3,0},{4,1},{5,6},{6,3},{7,4},{8,13},{9,10},{10,... | collective-permute-start | bytes 393224 | tf_op jit(solution)/shard_map/ppermute | solution.py:408
  42.5 1.1 %collective-permute-done.24.rest_6_ = bf16[512,128]{1,0:T(8,128)(2,1)S(1)} collective-permute-done((bf16[512,128]{1,0:T(8,128)(2,1)S(1)}, bf16[512,128]{1,0:T(8,128)(2,1)S(1)}, u32[]{:S(2)}, u32[]{:S(2)}) %collective-permute-start.24) | collective-permute-done | bytes 131104 | tf_op jit(solution)/shard_map/ppermute | solution.py:408
  43.6 0.0 collective-permute-start.23
  43.6 3.6 %shard_map.114 = (bf16[256,2048]{1,0:T(8,128)(2,1)}, bf16[256,2048]{1,0:T(8,128)(2,1)}, f32[256,1024]{1,0:T(8,128)S(1)}, f32[8,128]{1,0:T(8,128)}) custom-call(s32[1,256]{1,0:T(1,128)S(1)} %get-tuple-element.51.length, f32[1,256]{1,0:T(1,128)S(1)} %get-tuple-element.71.inverse_rms, ...), custom_call_target="tpu_custom_call", output_to_operand_aliasing={{0}: (11, {}), {1}: (12, {})} | custom-call | flops 469762048 | bytes 11548672 | tf_op jit(solution)/shard_map/pallas_call | solution.py:386
  47.1 1.5 %shard_map.115.value_part = f32[256,2048]{1,0:T(8,128)S(1)} custom-call(s32[1,256]{1,0:T(1,128)S(1)} %get-tuple-element.51.length, bf16[256,2048]{1,0:T(8,128)(2,1)S(1)} %shard_map.103.refs_4_.queries, bf16[256,2048]{1,0:T(8,128)(2,1)S(1)} %get-tuple-element.53.keys, bf16[256,1024]{1,0:T(8,128)(2,1)S(1)} %get-tuple-element.75.grads.rest_0_, ...), custom_call_target="tpu_custom_call" | custom-call | flops 536870912 | bytes 5243904 | tf_op jit(solution)/shard_map/pallas_call | solution.py:386
  48.6 0.0 collective-permute-done.26.rest_9_
  48.7 0.0 collective-permute-done.21.rest_2_
  48.7 0.0 collective-permute-done.23.rest_5_
  48.7 3.0 %shard_map.116 = (bf16[256,2048]{1,0:T(8,128)(2,1)}, bf16[256,2048]{1,0:T(8,128)(2,1)}) custom-call(s32[1,256]{1,0:T(1,128)S(1)} %get-tuple-element.51.length, bf16[256,2048]{1,0:T(8,128)(2,1)S(1)} %get-tuple-element.53.keys, bf16[256,2048]{1,0:T(8,128)(2,1)S(1)} %get-tuple-element.54.values, f32[256,2048]{1,0:T(8,128)S(1)} %shard_map.115.value_part, ...), custom_call_target="tpu_custom_call" | custom-call | flops 268435456 | bytes 9438208 | tf_op jit(solution)/shard_map/pallas_call | solution.py:386
  (9 shorter events, 0.0 us)
Async XLA Ops:
  3.6 6.9 %collective-permute-start.2 = (bf16[512,128]{1,0:T(8,128)(2,1)S(1)}, bf16[512,128]{1,0:T(8,128)(2,1)S(1)}, u32[]{:S(2)}, u32[]{:S(2)}) collective-permute-start(bf16[512,128]{1,0:T(8,128)(2,1)S(1)} %get-tuple-element.56), channel_id=1, source_target_pairs={{0,5},{1,2},{2,7},{3,0},{4,1},{5,6},{6,3},{7,4},{8,13},{9,10},{10,... | collective-permute-start | bytes 393224 | tf_op jit(solution)/shard_map/ppermute | solution.py:408
  6.1 4.9 %collective-permute-start = (bf16[512,128]{1,0:T(8,128)(2,1)S(1)}, bf16[512,128]{1,0:T(8,128)(2,1)S(1)}, u32[]{:S(2)}, u32[]{:S(2)}) collective-permute-start(bf16[512,128]{1,0:T(8,128)(2,1)S(1)} %get-tuple-element.56), channel_id=1, source_target_pairs={{0,1},{1,0},{2,3},{3,2},{4,5},{5,4},{6,7},{7,6},{8,9},{9,8},{10,11... | collective-permute-start | bytes 393224 | tf_op jit(solution)/shard_map/ppermute | solution.py:408
  6.7 5.0 %collective-permute-start.1 = (bf16[512,128]{1,0:T(8,128)(2,1)S(1)}, bf16[512,128]{1,0:T(8,128)(2,1)S(1)}, u32[]{:S(2)}, u32[]{:S(2)}) collective-permute-start(bf16[512,128]{1,0:T(8,128)(2,1)S(1)} %get-tuple-element.52._.refs_0_), channel_id=1, source_target_pairs={{0,2},{1,5},{2,0},{3,7},{4,6},{5,1},{6,4},{7,3},{8,10},{9,13},{10,... | collective-permute-start | bytes 393224 | tf_op jit(solution)/shard_map/ppermute | solution.py:408
  7.6 6.8 %collective-permute-start.4 = (bf16[512,128]{1,0:T(8,128)(2,1)S(1)}, bf16[512,128]{1,0:T(8,128)(2,1)S(1)}, u32[]{:S(2)}, u32[]{:S(2)}) collective-permute-start(bf16[512,128]{1,0:T(8,128)(2,1)S(1)} %get-tuple-element.58.refs_0_), channel_id=1, source_target_pairs={{0,2},{1,5},{2,0},{3,7},{4,6},{5,1},{6,4},{7,3},{8,10},{9,13},{10,... | collective-permute-start | bytes 393224 | tf_op jit(solution)/shard_map/ppermute | solution.py:408
  8.8 5.8 %collective-permute-start.5 = (bf16[512,128]{1,0:T(8,128)(2,1)S(1)}, bf16[512,128]{1,0:T(8,128)(2,1)S(1)}, u32[]{:S(2)}, u32[]{:S(2)}) collective-permute-start(bf16[512,128]{1,0:T(8,128)(2,1)S(1)} %get-tuple-element.59), channel_id=1, source_target_pairs={{0,5},{1,2},{2,7},{3,0},{4,1},{5,6},{6,3},{7,4},{8,13},{9,10},{10,... | collective-permute-start | bytes 393224 | tf_op jit(solution)/shard_map/ppermute | solution.py:408
  10.6 3.9 %collective-permute-start.3 = (bf16[512,128]{1,0:T(8,128)(2,1)S(1)}, bf16[512,128]{1,0:T(8,128)(2,1)S(1)}, u32[]{:S(2)}, u32[]{:S(2)}) collective-permute-start(bf16[512,128]{1,0:T(8,128)(2,1)S(1)} %get-tuple-element.59), channel_id=1, source_target_pairs={{0,1},{1,0},{2,3},{3,2},{4,5},{5,4},{6,7},{7,6},{8,9},{9,8},{10,11... | collective-permute-start | bytes 393224 | tf_op jit(solution)/shard_map/ppermute | solution.py:408
  12.0 5.0 %collective-permute-start.9 = (bf16[512,128]{1,0:T(8,128)(2,1)S(1)}, bf16[512,128]{1,0:T(8,128)(2,1)S(1)}, u32[]{:S(2)}, u32[]{:S(2)}) collective-permute-start(bf16[512,128]{1,0:T(8,128)(2,1)S(1)} %get-tuple-element.64), channel_id=1, source_target_pairs={{0,4},{1,3},{2,6},{3,1},{4,0},{5,7},{6,2},{7,5},{8,12},{9,11},{10,... | collective-permute-start | bytes 393224 | tf_op jit(solution)/shard_map/ppermute | solution.py:408
  13.6 5.3 %collective-permute-start.10 = (bf16[512,128]{1,0:T(8,128)(2,1)S(1)}, bf16[512,128]{1,0:T(8,128)(2,1)S(1)}, u32[]{:S(2)}, u32[]{:S(2)}) collective-permute-start(bf16[512,128]{1,0:T(8,128)(2,1)S(1)} %get-tuple-element.65), channel_id=1, source_target_pairs={{0,5},{1,2},{2,7},{3,0},{4,1},{5,6},{6,3},{7,4},{8,13},{9,10},{10,... | collective-permute-start | bytes 393224 | tf_op jit(solution)/shard_map/ppermute | solution.py:408
  14.4 4.4 %collective-permute-start.11 = (bf16[512,128]{1,0:T(8,128)(2,1)S(1)}, bf16[512,128]{1,0:T(8,128)(2,1)S(1)}, u32[]{:S(2)}, u32[]{:S(2)}) collective-permute-start(bf16[512,128]{1,0:T(8,128)(2,1)S(1)} %get-tuple-element.66), channel_id=1, source_target_pairs={{0,1},{1,0},{2,3},{3,2},{4,5},{5,4},{6,7},{7,6},{8,9},{9,8},{10,11... | collective-permute-start | bytes 393224 | tf_op jit(solution)/shard_map/ppermute | solution.py:408
  14.8 5.0 %collective-permute-start.6 = (bf16[512,128]{1,0:T(8,128)(2,1)S(1)}, bf16[512,128]{1,0:T(8,128)(2,1)S(1)}, u32[]{:S(2)}, u32[]{:S(2)}) collective-permute-start(bf16[512,128]{1,0:T(8,128)(2,1)S(1)} %get-tuple-element.60), channel_id=1, source_target_pairs={{0,4},{1,3},{2,6},{3,1},{4,0},{5,7},{6,2},{7,5},{8,12},{9,11},{10,... | collective-permute-start | bytes 393224 | tf_op jit(solution)/shard_map/ppermute | solution.py:408
  16.4 4.4 %collective-permute-start.7 = (bf16[512,128]{1,0:T(8,128)(2,1)S(1)}, bf16[512,128]{1,0:T(8,128)(2,1)S(1)}, u32[]{:S(2)}, u32[]{:S(2)}) collective-permute-start(bf16[512,128]{1,0:T(8,128)(2,1)S(1)} %get-tuple-element.62), channel_id=1, source_target_pairs={{0,5},{1,2},{2,7},{3,0},{4,1},{5,6},{6,3},{7,4},{8,13},{9,10},{10,... | collective-permute-start | bytes 393224 | tf_op jit(solution)/shard_map/ppermute | solution.py:408
  17.0 3.8 %collective-permute-start.8 = (bf16[512,128]{1,0:T(8,128)(2,1)S(1)}, bf16[512,128]{1,0:T(8,128)(2,1)S(1)}, u32[]{:S(2)}, u32[]{:S(2)}) collective-permute-start(bf16[512,128]{1,0:T(8,128)(2,1)S(1)} %get-tuple-element.63), channel_id=1, source_target_pairs={{0,1},{1,0},{2,3},{3,2},{4,5},{5,4},{6,7},{7,6},{8,9},{9,8},{10,11... | collective-permute-start | bytes 393224 | tf_op jit(solution)/shard_map/ppermute | solution.py:408
  17.3 1.5 %copy-start = (bf16[1,256,2048]{2,1,0:T(8,128)(2,1)S(1)}, bf16[1,256,2048]{2,1,0:T(8,128)(2,1)}, u32[]{:S(2)}) copy-start(bf16[1,256,2048]{2,1,0:T(8,128)(2,1)} %param.10) | copy-start | bytes 3145732
  17.3 1.5 %copy-start.1 = (f32[2048]{0:T(1024)S(1)}, f32[2048]{0:T(1024)}, u32[]{:S(2)}) copy-start(f32[2048]{0:T(1024)} %param.11) | copy-start | bytes 24580
  21.5 4.5 %collective-permute-start.14 = (f32[2,256]{1,0:T(2,128)S(1)}, f32[2,256]{1,0:T(2,128)S(1)}, u32[]{:S(2)}, u32[]{:S(2)}) collective-permute-start(f32[2,256]{1,0:T(2,128)S(1)} %get-tuple-element.68.rest_0_), channel_id=1, source_target_pairs={{0,16},{8,24},{16,0},{24,8},{1,17},{9,25},{17,1},{25,9},{2,18},{10... | collective-permute-start | bytes 6152 | tf_op jit(solution)/shard_map/ppermute | solution.py:435
  24.1 5.4 %collective-permute-start.13 = (f32[2,256]{1,0:T(2,128)S(1)}, f32[2,256]{1,0:T(2,128)S(1)}, u32[]{:S(2)}, u32[]{:S(2)}) collective-permute-start(f32[2,256]{1,0:T(2,128)S(1)} %get-tuple-element.68.rest_0_), channel_id=1, source_target_pairs={{0,24},{8,16},{16,8},{24,0},{1,25},{9,17},{17,9},{25,1},{2,26},{10... | collective-permute-start | bytes 6152 | tf_op jit(solution)/shard_map/ppermute | solution.py:435
  25.5 4.0 %collective-permute-start.12 = (f32[2,256]{1,0:T(2,128)S(1)}, f32[2,256]{1,0:T(2,128)S(1)}, u32[]{:S(2)}, u32[]{:S(2)}) collective-permute-start(f32[2,256]{1,0:T(2,128)S(1)} %get-tuple-element.68.rest_0_), channel_id=1, source_target_pairs={{0,8},{8,0},{16,24},{24,16},{1,9},{9,1},{17,25},{25,17},{2,10},{10... | collective-permute-start | bytes 6152 | tf_op jit(solution)/shard_map/ppermute | solution.py:435
  30.1 7.3 %collective-permute-start.19 = (bf16[512,128]{1,0:T(8,128)(2,1)S(1)}, bf16[512,128]{1,0:T(8,128)(2,1)S(1)}, u32[]{:S(2)}, u32[]{:S(2)}) collective-permute-start(bf16[512,128]{1,0:T(8,128)(2,1)S(1)} %get-tuple-element.83.refs_0_), channel_id=1, source_target_pairs={{0,2},{1,5},{2,0},{3,7},{4,6},{5,1},{6,4},{7,3},{8,10},{9,13},{10,... | collective-permute-start | bytes 393224 | tf_op jit(solution)/shard_map/ppermute | solution.py:408
  31.0 7.2 %collective-permute-start.20 = (bf16[512,128]{1,0:T(8,128)(2,1)S(1)}, bf16[512,128]{1,0:T(8,128)(2,1)S(1)}, u32[]{:S(2)}, u32[]{:S(2)}) collective-permute-start(bf16[512,128]{1,0:T(8,128)(2,1)S(1)} %get-tuple-element.84), channel_id=1, source_target_pairs={{0,5},{1,2},{2,7},{3,0},{4,1},{5,6},{6,3},{7,4},{8,13},{9,10},{10,... | collective-permute-start | bytes 393224 | tf_op jit(solution)/shard_map/ppermute | solution.py:408
  31.0 7.2 %collective-permute-start.18 = (bf16[512,128]{1,0:T(8,128)(2,1)S(1)}, bf16[512,128]{1,0:T(8,128)(2,1)S(1)}, u32[]{:S(2)}, u32[]{:S(2)}) collective-permute-start(bf16[512,128]{1,0:T(8,128)(2,1)S(1)} %get-tuple-element.84), channel_id=1, source_target_pairs={{0,1},{1,0},{2,3},{3,2},{4,5},{5,4},{6,7},{7,6},{8,9},{9,8},{10,11... | collective-permute-start | bytes 393224 | tf_op jit(solution)/shard_map/ppermute | solution.py:408
  32.9 7.2 %collective-permute-start.16 = (bf16[512,128]{1,0:T(8,128)(2,1)S(1)}, bf16[512,128]{1,0:T(8,128)(2,1)S(1)}, u32[]{:S(2)}, u32[]{:S(2)}) collective-permute-start(bf16[512,128]{1,0:T(8,128)(2,1)S(1)} %get-tuple-element.79.refs_0_), channel_id=1, source_target_pairs={{0,2},{1,5},{2,0},{3,7},{4,6},{5,1},{6,4},{7,3},{8,10},{9,13},{10,... | collective-permute-start | bytes 393224 | tf_op jit(solution)/shard_map/ppermute | solution.py:408
  33.8 7.1 %collective-permute-start.17 = (bf16[512,128]{1,0:T(8,128)(2,1)S(1)}, bf16[512,128]{1,0:T(8,128)(2,1)S(1)}, u32[]{:S(2)}, u32[]{:S(2)}) collective-permute-start(bf16[512,128]{1,0:T(8,128)(2,1)S(1)} %get-tuple-element.80), channel_id=1, source_target_pairs={{0,5},{1,2},{2,7},{3,0},{4,1},{5,6},{6,3},{7,4},{8,13},{9,10},{10,... | collective-permute-start | bytes 393224 | tf_op jit(solution)/shard_map/ppermute | solution.py:408
  37.4 3.6 %collective-permute-start.15 = (bf16[512,128]{1,0:T(8,128)(2,1)S(1)}, bf16[512,128]{1,0:T(8,128)(2,1)S(1)}, u32[]{:S(2)}, u32[]{:S(2)}) collective-permute-start(bf16[512,128]{1,0:T(8,128)(2,1)S(1)} %get-tuple-element.80), channel_id=1, source_target_pairs={{0,1},{1,0},{2,3},{3,2},{4,5},{5,4},{6,7},{7,6},{8,9},{9,8},{10,11... | collective-permute-start | bytes 393224 | tf_op jit(solution)/shard_map/ppermute | solution.py:408
  38.5 5.0 %collective-permute-start.24 = (bf16[512,128]{1,0:T(8,128)(2,1)S(1)}, bf16[512,128]{1,0:T(8,128)(2,1)S(1)}, u32[]{:S(2)}, u32[]{:S(2)}) collective-permute-start(bf16[512,128]{1,0:T(8,128)(2,1)S(1)} %get-tuple-element.93), channel_id=1, source_target_pairs={{0,4},{1,3},{2,6},{3,1},{4,0},{5,7},{6,2},{7,5},{8,12},{9,11},{10,... | collective-permute-start | bytes 393224 | tf_op jit(solution)/shard_map/ppermute | solution.py:408
  40.0 8.6 %collective-permute-start.25 = (bf16[512,128]{1,0:T(8,128)(2,1)S(1)}, bf16[512,128]{1,0:T(8,128)(2,1)S(1)}, u32[]{:S(2)}, u32[]{:S(2)}) collective-permute-start(bf16[512,128]{1,0:T(8,128)(2,1)S(1)} %get-tuple-element.94), channel_id=1, source_target_pairs={{0,5},{1,2},{2,7},{3,0},{4,1},{5,6},{6,3},{7,4},{8,13},{9,10},{10,... | collective-permute-start | bytes 393224 | tf_op jit(solution)/shard_map/ppermute | solution.py:408
  40.2 8.5 %collective-permute-start.26 = (bf16[512,128]{1,0:T(8,128)(2,1)S(1)}, bf16[512,128]{1,0:T(8,128)(2,1)S(1)}, u32[]{:S(2)}, u32[]{:S(2)}) collective-permute-start(bf16[512,128]{1,0:T(8,128)(2,1)S(1)} %get-tuple-element.95), channel_id=1, source_target_pairs={{0,1},{1,0},{2,3},{3,2},{4,5},{5,4},{6,7},{7,6},{8,9},{9,8},{10,11... | collective-permute-start | bytes 393224 | tf_op jit(solution)/shard_map/ppermute | solution.py:408
  41.2 7.4 %collective-permute-start.21 = (bf16[512,128]{1,0:T(8,128)(2,1)S(1)}, bf16[512,128]{1,0:T(8,128)(2,1)S(1)}, u32[]{:S(2)}, u32[]{:S(2)}) collective-permute-start(bf16[512,128]{1,0:T(8,128)(2,1)S(1)} %get-tuple-element.90), channel_id=1, source_target_pairs={{0,4},{1,3},{2,6},{3,1},{4,0},{5,7},{6,2},{7,5},{8,12},{9,11},{10,... | collective-permute-start | bytes 393224 | tf_op jit(solution)/shard_map/ppermute | solution.py:408
  41.9 6.7 %collective-permute-start.22 = (bf16[512,128]{1,0:T(8,128)(2,1)S(1)}, bf16[512,128]{1,0:T(8,128)(2,1)S(1)}, u32[]{:S(2)}, u32[]{:S(2)}) collective-permute-start(bf16[512,128]{1,0:T(8,128)(2,1)S(1)} %get-tuple-element.91), channel_id=1, source_target_pairs={{0,5},{1,2},{2,7},{3,0},{4,1},{5,6},{6,3},{7,4},{8,13},{9,10},{10,... | collective-permute-start | bytes 393224 | tf_op jit(solution)/shard_map/ppermute | solution.py:408
  43.6 5.1 %collective-permute-start.23 = (bf16[512,128]{1,0:T(8,128)(2,1)S(1)}, bf16[512,128]{1,0:T(8,128)(2,1)S(1)}, u32[]{:S(2)}, u32[]{:S(2)}) collective-permute-start(bf16[512,128]{1,0:T(8,128)(2,1)S(1)} %get-tuple-element.92), channel_id=1, source_target_pairs={{0,1},{1,0},{2,3},{3,2},{4,5},{5,4},{6,7},{7,6},{8,9},{9,8},{10,11... | collective-permute-start | bytes 393224 | tf_op jit(solution)/shard_map/ppermute | solution.py:408

commit v14 on v12

--- a/solution.py
+++ b/solution.py
@@ -300,15 +300,25 @@
     return [pltpu.make_async_copy(source.at[p, :], target.at[p, :], sems.at[j]) for j, p in enumerate(parts)]
 
 
+def write_out(piece, sources, targets, sems):
+    copies = []
+    for j, (source, target) in enumerate(zip(sources, targets)):
+        width = source.shape[1]
+        copies += row_copies(source, target.at[:, pl.ds(piece * width, width)], sems.at[j])
+    for copy in copies:
+        copy.start()
+    return copies
+
+
 def query_kernel(piece, scale, length, inverse_rms, gain, queries, keys, values, grads, *rest):
     attention, prefix, rest = split_refs(rest, FORWARD_PIECES, FORWARD_PIECES, len(rest) - 2 * FORWARD_PIECES)
-    attended_hbm, query_hbm, key_part, token, attended, query_grad, keep, sems = rest[-8:]
+    attended, query_grad, key_part, token = rest[-8:-4] if piece else rest[-6:-2]
+    keep, sems = rest[-2:]
+    copies = write_out(piece - 1, rest[:2], rest[-4:-2], sems) if piece else []
     token[...] = jnp.zeros_like(token)
     write_mask(length, keep, False)
     inverse = token_columns(inverse_rms[...])
     heads = grads.shape[1] // HD
-    group = 4 if heads % 4 == 0 else 1
-    copies = []
     for head in range(heads):
         cols = head_cols(head)
         place = piece * heads + head
@@ -322,25 +332,22 @@
         query_grad[:, cols] = (scale * (carried + nn(grad_scores, keys[:, whole]))).astype(BF16)
         key_part[:, cols] = scale * tn(grad_scores, queries[:, whole])
         attended[:, cols] = (out_piece[:, at] * inverse * gain[:, whole]).astype(BF16)
-        if (head + 1) % group == 0:
-            here = slice((head + 1 - group) * HD, (head + 1) * HD)
-            there = slice((place + 1 - group) * HD, (place + 1) * HD)
-            for j, (src, dst) in enumerate(((attended, attended_hbm), (query_grad, query_hbm))):
-                copy = pltpu.make_async_copy(src.at[:, here], dst.at[:, there], sems.at[head // group, j])
-                copy.start()
-                copies.append(copy)
     for copy in copies:
         copy.wait()
 
 
 def value_kernel(heads, scale, length, queries, keys, *rest):
-    grads, (value_part, keep) = rest[:BACKWARD_PIECES], rest[-2:]
+    grads, rest = rest[:BACKWARD_PIECES], rest[BACKWARD_PIECES:]
+    value_part, attended_hbm, query_hbm, keep, sems = rest[-5:]
+    copies = write_out(BACKWARD_PIECES - 1, rest[:2], (attended_hbm, query_hbm), sems)
     write_mask(length, keep, True)
     for head in range(heads):
         cols = head_cols(head)
         grad_piece, at = head_of(grads, head)
         turned = nt(keys[:, cols], queries[:, cols]).astype(BF16) * keep[...]
         value_part[:, cols] = scale * nn(turned, grad_piece[:, at])
+    for copy in copies:
+        copy.wait()
 
 
 def final_kernel(grid, counts, length, keys, values, value_part, *rest):
@@ -505,28 +512,39 @@
         state_grad.append(parts[:pair])
         if piece == 0:
             inverse_rms = parts[pair]
-    group = 4 if heads // BACKWARD_PIECES % 4 == 0 else 1
     narrow_piece, wide_piece = shape((rows, width), BF16), shape((rows, width), F32)
-    mixed, key_parts, results = [], [], []
+    copy_sems = pltpu.SemaphoreType.DMA((2, 4))
+    mixed, key_parts, left, results = [], [], [], []
+
+    def with_results(kernel, out_shape, operands, scratch, flops, after):
+        operands = (*operands, *left, *results)
+        last = len(operands) - len(results)
+        outs = [narrow] * 2 if left else []
+        return call(
+            kernel, out_shape + outs, operands, [*scratch, copy_sems], flops, range(last, len(operands)), after=after,
+            out_specs=[VMEM] * len(out_shape) + [HBM] * len(outs),
+            aliases={last + j: len(out_shape) + j for j in range(len(results))},
+        )
+
     for piece in range(BACKWARD_PIECES):
-        operands = (length, inverse_rms, gain, query, key, value, grads[piece], *attention, *prefix, *results)
-        last = len(operands) - len(results)
-        *results, key_part, token = call(
-            functools.partial(query_kernel, piece, scale),
-            [narrow, narrow, wide_piece, shape((8, HD), F32)], operands,
-            [pltpu.VMEM(narrow_piece.shape, BF16)] * 2 + [mask, pltpu.SemaphoreType.DMA((heads // group, 2))],
-            unit * (3 * rows + HD) // BACKWARD_PIECES, range(last, len(operands)),
-            after=tuple(sums[0] for sums in mixed), out_specs=[HBM, HBM, VMEM, VMEM],
-            aliases={last + j: j for j in range(len(results))},
-        )
+        *left, key_part, token, first, second = [
+            *with_results(
+                functools.partial(query_kernel, piece, scale),
+                [narrow_piece, narrow_piece, wide_piece, shape((8, HD), F32)],
+                (length, inverse_rms, gain, query, key, value, grads[piece], *attention, *prefix),
+                [mask], unit * (3 * rows + HD) // BACKWARD_PIECES, tuple(sums[0] for sums in mixed),
+            ),
+            None,
+            None,
+        ][:6]
+        results = [] if first is None else [first, second]
         key_parts.append(key_part)
         if piece == 0:
             for part in state_grad:
                 mixed.append(mix(gather_line(part, grid), down, 0, 1, (token,)))
-    attended, query_grad = results
-    (value_part,) = call(
+    value_part, attended, query_grad = with_results(
         functools.partial(value_kernel, heads, scale),
-        [wide], (length, query, key, *grads), [mask], unit * 2 * rows, after=(mixed[-1][0],),
+        [wide], (length, query, key, *grads), [mask], unit * 2 * rows, (mixed[-1][0],),
     )
     below = [block for sums in mixed for block in flat(scatter_line(sums, grid))]
     key_grad, value_grad = call(

time: 50.8 us -> 50.4 us (level)
  no operation moved by 1% of the time
where the time goes in v14:
time: 50.4 us; the launch traced here: 50.2 us
  starting transfers between devices  23.1 us (46%)
  Pallas kernels  18.2 us (36%)
  waiting for transfers between devices  7.32 us (15%)
  between operations  1.63 us (3%)
    ppermute x24, starting transfers between devices, line_send(): return lax.ppermute(block, 'seg', moves)  18.8 us
    pallas_call x15, Pallas kernels, call(): pl.pallas_call(kernel, out_shape=out_shape, in_specs=specs + [ANY] * len(...  18.2 us
    ppermute x3, starting transfers between devices, token_sums(): parts.append(lax.ppermute(sums, 'head', moves))  4.23 us
    ppermute x3, waiting for transfers between devices, token_sums(): parts.append(lax.ppermute(sums, 'head', moves))  3.8 us
    ppermute x24, waiting for transfers between devices, line_send(): return lax.ppermute(block, 'seg', moves)  3.51 us
  transfers between devices with their start and end apart: 27, of which 8 were waited for; matrix products, arithmetic and copies ran while one was open for 0% of the time, Pallas kernels for 25%

profile of v14, /device:TPU:0, one launch (start us, length us, event | category | flops | bytes accessed | tf_op | source)
XLA Modules:
  0.0 50.2 jit_solution(5931087631746750393)
XLA Ops:
  1.3 2.3 %shard_map.102 = (bf16[256,2048]{1,0:T(8,128)(2,1)S(1)}, bf16[256,2048]{1,0:T(8,128)(2,1)S(1)}, s32[1,256]{1,0:T(1,128)S(1)}, f32[16,128]{1,0:T(8,128)S(1)}, f32...) custom-call(s32[1]{0:T(128)S(6)} %copy.15.seg_len, ...), custom_call_target="tpu_custom_call" | custom-call | flops 134217728 | bytes 4736036 | tf_op jit(solution)/shard_map/pallas_call | solution.py:391
  3.6 2.5 %collective-permute-start.2 = (bf16[512,128]{1,0:T(8,128)(2,1)S(1)}, bf16[512,128]{1,0:T(8,128)(2,1)S(1)}, u32[]{:S(2)}, u32[]{:S(2)}) collective-permute-start(bf16[512,128]{1,0:T(8,128)(2,1)S(1)} %get-tuple-element.61), channel_id=1, source_target_pairs={{0,5},{1,2},{2,7},{3,0},{4,1},{5,6},{6,3},{7,4},{8,13},{9,10},{10,... | collective-permute-start | bytes 393224 | tf_op jit(solution)/shard_map/ppermute | solution.py:413
  6.1 0.6 %collective-permute-start = (bf16[512,128]{1,0:T(8,128)(2,1)S(1)}, bf16[512,128]{1,0:T(8,128)(2,1)S(1)}, u32[]{:S(2)}, u32[]{:S(2)}) collective-permute-start(bf16[512,128]{1,0:T(8,128)(2,1)S(1)} %get-tuple-element.61), channel_id=1, source_target_pairs={{0,1},{1,0},{2,3},{3,2},{4,5},{5,4},{6,7},{7,6},{8,9},{9,8},{10,11... | collective-permute-start | bytes 393224 | tf_op jit(solution)/shard_map/ppermute | solution.py:413
  6.7 0.9 %collective-permute-start.1 = (bf16[512,128]{1,0:T(8,128)(2,1)S(1)}, bf16[512,128]{1,0:T(8,128)(2,1)S(1)}, u32[]{:S(2)}, u32[]{:S(2)}) collective-permute-start(bf16[512,128]{1,0:T(8,128)(2,1)S(1)} %get-tuple-element.57._.refs_0_), channel_id=1, source_target_pairs={{0,2},{1,5},{2,0},{3,7},{4,6},{5,1},{6,4},{7,3},{8,10},{9,13},{10,... | collective-permute-start | bytes 393224 | tf_op jit(solution)/shard_map/ppermute | solution.py:413
  7.6 1.1 %collective-permute-start.4 = (bf16[512,128]{1,0:T(8,128)(2,1)S(1)}, bf16[512,128]{1,0:T(8,128)(2,1)S(1)}, u32[]{:S(2)}, u32[]{:S(2)}) collective-permute-start(bf16[512,128]{1,0:T(8,128)(2,1)S(1)} %get-tuple-element.63.refs_0_), channel_id=1, source_target_pairs={{0,2},{1,5},{2,0},{3,7},{4,6},{5,1},{6,4},{7,3},{8,10},{9,13},{10,... | collective-permute-start | bytes 393224 | tf_op jit(solution)/shard_map/ppermute | solution.py:413
  8.8 0.6 %collective-permute-start.5 = (bf16[512,128]{1,0:T(8,128)(2,1)S(1)}, bf16[512,128]{1,0:T(8,128)(2,1)S(1)}, u32[]{:S(2)}, u32[]{:S(2)}) collective-permute-start(bf16[512,128]{1,0:T(8,128)(2,1)S(1)} %get-tuple-element.64), channel_id=1, source_target_pairs={{0,5},{1,2},{2,7},{3,0},{4,1},{5,6},{6,3},{7,4},{8,13},{9,10},{10,... | collective-permute-start | bytes 393224 | tf_op jit(solution)/shard_map/ppermute | solution.py:413
  9.3 1.2 %shard_map.103.refs_4_.queries = bf16[256,2048]{1,0:T(8,128)(2,1)S(1)} custom-call(bf16[256,2048]{1,0:T(8,128)(2,1)} %bitcast.20, bf16[512,128]{1,0:T(8,128)(2,1)S(1)} %get-tuple-element.57._.refs_0_), custom_call_target="tpu_custom_call" | custom-call | bytes 2097152 | tf_op jit(solution)/shard_map/pallas_call | solution.py:391
  10.6 0.0 collective-permute-done.2.refs_3_
  10.6 0.5 collective-permute-start.3
  11.1 0.0 collective-permute-done.refs_1_
  11.1 0.6 %collective-permute-done.1.refs_2_ = bf16[512,128]{1,0:T(8,128)(2,1)S(1)} collective-permute-done((bf16[512,128]{1,0:T(8,128)(2,1)S(1)}, bf16[512,128]{1,0:T(8,128)(2,1)S(1)}, u32[]{:S(2)}, u32[]{:S(2)}) %collective-permute-start.1) | collective-permute-done | bytes 131104 | tf_op jit(solution)/shard_map/ppermute | solution.py:413
  11.7 0.3 shard_map.104
  12.0 1.6 %collective-permute-start.9 = (bf16[512,128]{1,0:T(8,128)(2,1)S(1)}, bf16[512,128]{1,0:T(8,128)(2,1)S(1)}, u32[]{:S(2)}, u32[]{:S(2)}) collective-permute-start(bf16[512,128]{1,0:T(8,128)(2,1)S(1)} %get-tuple-element.69), channel_id=1, source_target_pairs={{0,4},{1,3},{2,6},{3,1},{4,0},{5,7},{6,2},{7,5},{8,12},{9,11},{10,... | collective-permute-start | bytes 393224 | tf_op jit(solution)/shard_map/ppermute | solution.py:413
  13.6 0.4 collective-permute-start.10
  14.0 0.4 collective-permute-done.4.refs_2_
  14.4 0.1 collective-permute-start.11
  14.5 0.0 collective-permute-done.5.refs_3_
  14.5 0.0 collective-permute-done.3.refs_1_
  14.5 0.3 shard_map.106
  14.8 1.6 %collective-permute-start.6 = (bf16[512,128]{1,0:T(8,128)(2,1)S(1)}, bf16[512,128]{1,0:T(8,128)(2,1)S(1)}, u32[]{:S(2)}, u32[]{:S(2)}) collective-permute-start(bf16[512,128]{1,0:T(8,128)(2,1)S(1)} %get-tuple-element.65), channel_id=1, source_target_pairs={{0,4},{1,3},{2,6},{3,1},{4,0},{5,7},{6,2},{7,5},{8,12},{9,11},{10,... | collective-permute-start | bytes 393224 | tf_op jit(solution)/shard_map/ppermute | solution.py:413
  16.4 0.6 %collective-permute-start.7 = (bf16[512,128]{1,0:T(8,128)(2,1)S(1)}, bf16[512,128]{1,0:T(8,128)(2,1)S(1)}, u32[]{:S(2)}, u32[]{:S(2)}) collective-permute-start(bf16[512,128]{1,0:T(8,128)(2,1)S(1)} %get-tuple-element.67), channel_id=1, source_target_pairs={{0,5},{1,2},{2,7},{3,0},{4,1},{5,6},{6,3},{7,4},{8,13},{9,10},{10,... | collective-permute-start | bytes 393224 | tf_op jit(solution)/shard_map/ppermute | solution.py:413
  16.9 0.1 collective-permute-done.9.rest_0_
  17.0 0.3 collective-permute-start.8
  17.4 1.5 %shard_map.105.local = f32[256,2048]{1,0:T(8,128)S(1)} custom-call(s32[1,256]{1,0:T(1,128)S(1)} %get-tuple-element.56.length, bf16[256,2048]{1,0:T(8,128)(2,1)S(1)} %shard_map.103.refs_4_.queries, bf16[256,2048]{1,0:T(8,128)(2,1)S(1)} %get-tuple-element.58.keys, bf16[256,2048]{1,0:T(8,128)(2,1)S(1)} %get-tuple-element.59.values, ...), custom_call_target="tpu_custom_call" | custom-call | flops 536870912 | bytes 5243904 | tf_op jit(solution)/shard_map/pallas_call | solution.py:391
  18.8 0.0 collective-permute-done.11.rest_3_
  18.9 0.7 %shard_map.107 = (f32[256,1024]{1,0:T(8,128)S(1)}, f32[2,256]{1,0:T(2,128)S(1)}, bf16[1024,128]{1,0:T(8,128)(2,1)S(1)}) custom-call(s32[1,256]{1,0:T(1,128)S(1)} %get-tuple-element.56.length, bf16[256,2048]{1,0:T(8,128)(2,1)S(1)} %shard_map.103.refs_4_.queries, f32[256,2048]{1,0:T(8,128)S(1)} %shard_map.105.local, bf16[256,2048]{1,0:T(8,128)(2,1)S(1)} %bitcast.10, ...), custom_call_target="tpu_custom_call" | custom-call | flops 67108864 | bytes 6040576 | tf_op jit(solution)/shard_map/pallas_call | solution.py:391
  19.5 0.3 collective-permute-done.6.rest_0_
  19.8 0.9 %collective-permute-done.7.rest_2_ = bf16[512,128]{1,0:T(8,128)(2,1)S(1)} collective-permute-done((bf16[512,128]{1,0:T(8,128)(2,1)S(1)}, bf16[512,128]{1,0:T(8,128)(2,1)S(1)}, u32[]{:S(2)}, u32[]{:S(2)}) %collective-permute-start.7) | collective-permute-done | bytes 131104 | tf_op jit(solution)/shard_map/ppermute | solution.py:413
  20.8 0.7 %shard_map.108 = (f32[256,1024]{1,0:T(8,128)S(1)}, f32[2,256]{1,0:T(2,128)S(1)}, bf16[1024,128]{1,0:T(8,128)(2,1)S(1)}) custom-call(s32[1,256]{1,0:T(1,128)S(1)} %get-tuple-element.56.length, bf16[256,2048]{1,0:T(8,128)(2,1)S(1)} %shard_map.103.refs_4_.queries, f32[256,2048]{1,0:T(8,128)S(1)} %shard_map.105.local, bf16[256,2048]{1,0:T(8,128)(2,1)S(1)} %bitcast.11, ...), custom_call_target="tpu_custom_call" | custom-call | flops 67108864 | bytes 6042624 | tf_op jit(solution)/shard_map/pallas_call | solution.py:391
  21.5 2.7 %collective-permute-start.14 = (f32[2,256]{1,0:T(2,128)S(1)}, f32[2,256]{1,0:T(2,128)S(1)}, u32[]{:S(2)}, u32[]{:S(2)}) collective-permute-start(f32[2,256]{1,0:T(2,128)S(1)} %get-tuple-element.73.rest_0_), channel_id=1, source_target_pairs={{0,16},{8,24},{16,0},{24,8},{1,17},{9,25},{17,1},{25,9},{2,18},{10... | collective-permute-start | bytes 6152 | tf_op jit(solution)/shard_map/ppermute | solution.py:440
  24.1 1.3 %collective-permute-start.13 = (f32[2,256]{1,0:T(2,128)S(1)}, f32[2,256]{1,0:T(2,128)S(1)}, u32[]{:S(2)}, u32[]{:S(2)}) collective-permute-start(f32[2,256]{1,0:T(2,128)S(1)} %get-tuple-element.73.rest_0_), channel_id=1, source_target_pairs={{0,24},{8,16},{16,8},{24,0},{1,25},{9,17},{17,9},{25,1},{2,26},{10... | collective-permute-start | bytes 6152 | tf_op jit(solution)/shard_map/ppermute | solution.py:440
  25.5 0.2 collective-permute-start.12
  25.7 0.3 collective-permute-done.14.rest_3_
  26.0 3.5 %collective-permute-done.13.rest_2_ = f32[2,256]{1,0:T(2,128)S(1)} collective-permute-done((f32[2,256]{1,0:T(2,128)S(1)}, f32[2,256]{1,0:T(2,128)S(1)}, u32[]{:S(2)}, u32[]{:S(2)}) %collective-permute-start.13) | collective-permute-done | bytes 2080 | tf_op jit(solution)/shard_map/ppermute | solution.py:440
  29.5 0.0 collective-permute-done.12.rest_1_
  29.5 0.6 %shard_map.110 = (bf16[256,1024]{1,0:T(8,128)(2,1)S(1)}, bf16[512,128]{1,0:T(8,128)(2,1)S(1)}, bf16[512,128]{1,0:T(8,128)(2,1)S(1)}) custom-call(s32[1,256]{1,0:T(1,128)S(1)} %get-tuple-element.56.length, bf16[256,2048]{1,0:T(8,128)(2,1)S(1)} %shard_map.103.refs_4_.queries, bf16[256,2048]{1,0:T(8,128)(2,1)S(1)} %bitcast.12, f32[1,2048]{1,0:T(1,128)S(1)} %bitcast.16, ...), custom_call_target="tpu_custom_call" | custom-call | flops 67108864 | bytes 4998144 | tf_op jit(solution)/shard_map/pallas_call | solution.py:391
  30.1 0.9 %collective-permute-start.19 = (bf16[512,128]{1,0:T(8,128)(2,1)S(1)}, bf16[512,128]{1,0:T(8,128)(2,1)S(1)}, u32[]{:S(2)}, u32[]{:S(2)}) collective-permute-start(bf16[512,128]{1,0:T(8,128)(2,1)S(1)} %get-tuple-element.88.refs_0_), channel_id=1, source_target_pairs={{0,2},{1,5},{2,0},{3,7},{4,6},{5,1},{6,4},{7,3},{8,10},{9,13},{10,... | collective-permute-start | bytes 393224 | tf_op jit(solution)/shard_map/ppermute | solution.py:413
  31.0 0.0 collective-permute-start.20
  31.0 1.3 %collective-permute-start.18 = (bf16[512,128]{1,0:T(8,128)(2,1)S(1)}, bf16[512,128]{1,0:T(8,128)(2,1)S(1)}, u32[]{:S(2)}, u32[]{:S(2)}) collective-permute-start(bf16[512,128]{1,0:T(8,128)(2,1)S(1)} %get-tuple-element.89), channel_id=1, source_target_pairs={{0,1},{1,0},{2,3},{3,2},{4,5},{5,4},{6,7},{7,6},{8,9},{9,8},{10,11... | collective-permute-start | bytes 393224 | tf_op jit(solution)/shard_map/ppermute | solution.py:413
  32.3 0.6 %shard_map.109 = (bf16[256,1024]{1,0:T(8,128)(2,1)S(1)}, bf16[512,128]{1,0:T(8,128)(2,1)S(1)}, bf16[512,128]{1,0:T(8,128)(2,1)S(1)}, f32[1,256]{1,0:T(1,128)S(1)}) custom-call(s32[1,256]{1,0:T(1,128)S(1)} %get-tuple-element.56.length, bf16[256,2048]{1,0:T(8,128)(2,1)S(1)} %shard_map.103.refs_4_.queries, bf16[256,2048]{1,0:T(8,128)(2,1)S(1)} %bitcast.13, ...), custom_call_target="tpu_custom_call" | custom-call | flops 67108864 | bytes 4999168 | tf_op jit(solution)/shard_map/pallas_call | solution.py:391
  32.9 0.9 %collective-permute-start.16 = (bf16[512,128]{1,0:T(8,128)(2,1)S(1)}, bf16[512,128]{1,0:T(8,128)(2,1)S(1)}, u32[]{:S(2)}, u32[]{:S(2)}) collective-permute-start(bf16[512,128]{1,0:T(8,128)(2,1)S(1)} %get-tuple-element.84.refs_0_), channel_id=1, source_target_pairs={{0,2},{1,5},{2,0},{3,7},{4,6},{5,1},{6,4},{7,3},{8,10},{9,13},{10,... | collective-permute-start | bytes 393224 | tf_op jit(solution)/shard_map/ppermute | solution.py:413
  33.8 0.5 %collective-permute-start.17 = (bf16[512,128]{1,0:T(8,128)(2,1)S(1)}, bf16[512,128]{1,0:T(8,128)(2,1)S(1)}, u32[]{:S(2)}, u32[]{:S(2)}) collective-permute-start(bf16[512,128]{1,0:T(8,128)(2,1)S(1)} %get-tuple-element.85), channel_id=1, source_target_pairs={{0,5},{1,2},{2,7},{3,0},{4,1},{5,6},{6,3},{7,4},{8,13},{9,10},{10,... | collective-permute-start | bytes 393224 | tf_op jit(solution)/shard_map/ppermute | solution.py:413
  34.4 1.9 %shard_map.111 = (bf16[256,1024]{1,0:T(8,128)(2,1)S(1)}, bf16[256,1024]{1,0:T(8,128)(2,1)S(1)}, f32[256,1024]{1,0:T(8,128)S(1)}, f32[8,128]{1,0:T(8,128)S(1)}) custom-call(s32[1,256]{1,0:T(1,128)S(1)} %get-tuple-element.56.length, f32[1,256]{1,0:T(1,128)S(1)} %get-tuple-element.78.inverse_rms, f32[1,2048]{1,0:T(1,128)S(1)} %bitcast.18, ...), custom_call_target="tpu_custom_call" | custom-call | flops 469762048 | bytes 8402944 | tf_op jit(solution)/shard_map/pallas_call | solution.py:391
  36.3 0.0 collective-permute-done.19.refs_2_
  36.3 0.8 %collective-permute-start.15 = (bf16[512,128]{1,0:T(8,128)(2,1)S(1)}, bf16[512,128]{1,0:T(8,128)(2,1)S(1)}, u32[]{:S(2)}, u32[]{:S(2)}) collective-permute-start(bf16[512,128]{1,0:T(8,128)(2,1)S(1)} %get-tuple-element.85), channel_id=1, source_target_pairs={{0,1},{1,0},{2,3},{3,2},{4,5},{5,4},{6,7},{7,6},{8,9},{9,8},{10,11... | collective-permute-start | bytes 393224 | tf_op jit(solution)/shard_map/ppermute | solution.py:413
  37.1 0.0 collective-permute-done.20.refs_3_
  37.1 0.3 shard_map.113
  37.4 1.5 %collective-permute-start.24 = (bf16[512,128]{1,0:T(8,128)(2,1)S(1)}, bf16[512,128]{1,0:T(8,128)(2,1)S(1)}, u32[]{:S(2)}, u32[]{:S(2)}) collective-permute-start(bf16[512,128]{1,0:T(8,128)(2,1)S(1)} %get-tuple-element.103), channel_id=1, source_target_pairs={{0,4},{1,3},{2,6},{3,1},{4,0},{5,7},{6,2},{7,5},{8,12},{9,11},{10,... | collective-permute-start | bytes 393224 | tf_op jit(solution)/shard_map/ppermute | solution.py:413
  38.9 0.2 collective-permute-start.25
  39.1 0.0 collective-permute-done.16.refs_2_
  39.1 0.8 %collective-permute-start.26 = (bf16[512,128]{1,0:T(8,128)(2,1)S(1)}, bf16[512,128]{1,0:T(8,128)(2,1)S(1)}, u32[]{:S(2)}, u32[]{:S(2)}) collective-permute-start(bf16[512,128]{1,0:T(8,128)(2,1)S(1)} %get-tuple-element.105), channel_id=1, source_target_pairs={{0,1},{1,0},{2,3},{3,2},{4,5},{5,4},{6,7},{7,6},{8,9},{9,8},{10,11... | collective-permute-start | bytes 393224 | tf_op jit(solution)/shard_map/ppermute | solution.py:413
  39.8 0.0 collective-permute-done.17.refs_3_
  39.8 0.0 collective-permute-done.15.refs_1_
  39.8 0.3 shard_map.112
  40.1 1.0 %collective-permute-start.21 = (bf16[512,128]{1,0:T(8,128)(2,1)S(1)}, bf16[512,128]{1,0:T(8,128)(2,1)S(1)}, u32[]{:S(2)}, u32[]{:S(2)}) collective-permute-start(bf16[512,128]{1,0:T(8,128)(2,1)S(1)} %get-tuple-element.100), channel_id=1, source_target_pairs={{0,4},{1,3},{2,6},{3,1},{4,0},{5,7},{6,2},{7,5},{8,12},{9,11},{10,... | collective-permute-start | bytes 393224 | tf_op jit(solution)/shard_map/ppermute | solution.py:413
  41.2 0.2 collective-permute-start.22
  41.4 1.1 %collective-permute-done.24.rest_6_ = bf16[512,128]{1,0:T(8,128)(2,1)S(1)} collective-permute-done((bf16[512,128]{1,0:T(8,128)(2,1)S(1)}, bf16[512,128]{1,0:T(8,128)(2,1)S(1)}, u32[]{:S(2)}, u32[]{:S(2)}) %collective-permute-start.24) | collective-permute-done | bytes 131104 | tf_op jit(solution)/shard_map/ppermute | solution.py:413
  42.4 0.0 collective-permute-start.23
  42.4 3.2 %shard_map.114 = (bf16[256,1024]{1,0:T(8,128)(2,1)S(1)}, bf16[256,1024]{1,0:T(8,128)(2,1)S(1)}, f32[256,1024]{1,0:T(8,128)S(1)}, f32[8,128]{1,0:T(8,128)}, bf16[...) custom-call(s32[1,256]{1,0:T(1,128)S(1)} %get-tuple-element.56.length, f32[1,256]{1,0:T(1,128)S(1)} %get-tuple-element.78.inverse_rms, ...), custom_call_target="tpu_custom_call" | custom-call | flops 469762048 | bytes 11548672 | tf_op jit(solution)/shard_map/pallas_call | solution.py:391
  45.7 2.2 %shard_map.115 = (f32[256,2048]{1,0:T(8,128)S(1)}, bf16[256,2048]{1,0:T(8,128)(2,1)}, bf16[256,2048]{1,0:T(8,128)(2,1)}) custom-call(s32[1,256]{1,0:T(1,128)S(1)} %get-tuple-element.56.length, bf16[256,2048]{1,0:T(8,128)(2,1)S(1)} %shard_map.103.refs_4_.queries, ...), custom_call_target="tpu_custom_call", output_to_operand_aliasing={{1}: (7, {}), {2}: (8, {})} | custom-call | flops 536870912 | bytes 10486784 | tf_op jit(solution)/shard_map/pallas_call | solution.py:391
  47.9 0.0 collective-permute-done.25.rest_8_
  47.9 0.0 collective-permute-done.21.rest_2_
  47.9 0.0 collective-permute-done.22.rest_4_
  47.9 2.1 %shard_map.116 = (bf16[256,2048]{1,0:T(8,128)(2,1)}, bf16[256,2048]{1,0:T(8,128)(2,1)}) custom-call(s32[1,256]{1,0:T(1,128)S(1)} %get-tuple-element.56.length, bf16[256,2048]{1,0:T(8,128)(2,1)S(1)} %get-tuple-element.58.keys, bf16[256,2048]{1,0:T(8,128)(2,1)S(1)} %get-tuple-element.59.values, f32[256,2048]{1,0:T(8,128)S(1)} %get-tuple-element.97.value_part, ...), custom_call_target="tpu_custom_call" | custom-call | flops 268435456 | bytes 9438208 | tf_op jit(solution)/shard_map/pallas_call | solution.py:391
  (9 shorter events, 0.0 us)
Async XLA Ops:
  3.6 6.9 %collective-permute-start.2 = (bf16[512,128]{1,0:T(8,128)(2,1)S(1)}, bf16[512,128]{1,0:T(8,128)(2,1)S(1)}, u32[]{:S(2)}, u32[]{:S(2)}) collective-permute-start(bf16[512,128]{1,0:T(8,128)(2,1)S(1)} %get-tuple-element.61), channel_id=1, source_target_pairs={{0,5},{1,2},{2,7},{3,0},{4,1},{5,6},{6,3},{7,4},{8,13},{9,10},{10,... | collective-permute-start | bytes 393224 | tf_op jit(solution)/shard_map/ppermute | solution.py:413
  6.1 4.9 %collective-permute-start = (bf16[512,128]{1,0:T(8,128)(2,1)S(1)}, bf16[512,128]{1,0:T(8,128)(2,1)S(1)}, u32[]{:S(2)}, u32[]{:S(2)}) collective-permute-start(bf16[512,128]{1,0:T(8,128)(2,1)S(1)} %get-tuple-element.61), channel_id=1, source_target_pairs={{0,1},{1,0},{2,3},{3,2},{4,5},{5,4},{6,7},{7,6},{8,9},{9,8},{10,11... | collective-permute-start | bytes 393224 | tf_op jit(solution)/shard_map/ppermute | solution.py:413
  6.7 5.0 %collective-permute-start.1 = (bf16[512,128]{1,0:T(8,128)(2,1)S(1)}, bf16[512,128]{1,0:T(8,128)(2,1)S(1)}, u32[]{:S(2)}, u32[]{:S(2)}) collective-permute-start(bf16[512,128]{1,0:T(8,128)(2,1)S(1)} %get-tuple-element.57._.refs_0_), channel_id=1, source_target_pairs={{0,2},{1,5},{2,0},{3,7},{4,6},{5,1},{6,4},{7,3},{8,10},{9,13},{10,... | collective-permute-start | bytes 393224 | tf_op jit(solution)/shard_map/ppermute | solution.py:413
  7.6 6.8 %collective-permute-start.4 = (bf16[512,128]{1,0:T(8,128)(2,1)S(1)}, bf16[512,128]{1,0:T(8,128)(2,1)S(1)}, u32[]{:S(2)}, u32[]{:S(2)}) collective-permute-start(bf16[512,128]{1,0:T(8,128)(2,1)S(1)} %get-tuple-element.63.refs_0_), channel_id=1, source_target_pairs={{0,2},{1,5},{2,0},{3,7},{4,6},{5,1},{6,4},{7,3},{8,10},{9,13},{10,... | collective-permute-start | bytes 393224 | tf_op jit(solution)/shard_map/ppermute | solution.py:413
  8.8 5.8 %collective-permute-start.5 = (bf16[512,128]{1,0:T(8,128)(2,1)S(1)}, bf16[512,128]{1,0:T(8,128)(2,1)S(1)}, u32[]{:S(2)}, u32[]{:S(2)}) collective-permute-start(bf16[512,128]{1,0:T(8,128)(2,1)S(1)} %get-tuple-element.64), channel_id=1, source_target_pairs={{0,5},{1,2},{2,7},{3,0},{4,1},{5,6},{6,3},{7,4},{8,13},{9,10},{10,... | collective-permute-start | bytes 393224 | tf_op jit(solution)/shard_map/ppermute | solution.py:413
  10.6 3.9 %collective-permute-start.3 = (bf16[512,128]{1,0:T(8,128)(2,1)S(1)}, bf16[512,128]{1,0:T(8,128)(2,1)S(1)}, u32[]{:S(2)}, u32[]{:S(2)}) collective-permute-start(bf16[512,128]{1,0:T(8,128)(2,1)S(1)} %get-tuple-element.64), channel_id=1, source_target_pairs={{0,1},{1,0},{2,3},{3,2},{4,5},{5,4},{6,7},{7,6},{8,9},{9,8},{10,11... | collective-permute-start | bytes 393224 | tf_op jit(solution)/shard_map/ppermute | solution.py:413
  12.0 5.0 %collective-permute-start.9 = (bf16[512,128]{1,0:T(8,128)(2,1)S(1)}, bf16[512,128]{1,0:T(8,128)(2,1)S(1)}, u32[]{:S(2)}, u32[]{:S(2)}) collective-permute-start(bf16[512,128]{1,0:T(8,128)(2,1)S(1)} %get-tuple-element.69), channel_id=1, source_target_pairs={{0,4},{1,3},{2,6},{3,1},{4,0},{5,7},{6,2},{7,5},{8,12},{9,11},{10,... | collective-permute-start | bytes 393224 | tf_op jit(solution)/shard_map/ppermute | solution.py:413
  13.6 5.3 %collective-permute-start.10 = (bf16[512,128]{1,0:T(8,128)(2,1)S(1)}, bf16[512,128]{1,0:T(8,128)(2,1)S(1)}, u32[]{:S(2)}, u32[]{:S(2)}) collective-permute-start(bf16[512,128]{1,0:T(8,128)(2,1)S(1)} %get-tuple-element.70), channel_id=1, source_target_pairs={{0,5},{1,2},{2,7},{3,0},{4,1},{5,6},{6,3},{7,4},{8,13},{9,10},{10,... | collective-permute-start | bytes 393224 | tf_op jit(solution)/shard_map/ppermute | solution.py:413
  14.4 4.4 %collective-permute-start.11 = (bf16[512,128]{1,0:T(8,128)(2,1)S(1)}, bf16[512,128]{1,0:T(8,128)(2,1)S(1)}, u32[]{:S(2)}, u32[]{:S(2)}) collective-permute-start(bf16[512,128]{1,0:T(8,128)(2,1)S(1)} %get-tuple-element.71), channel_id=1, source_target_pairs={{0,1},{1,0},{2,3},{3,2},{4,5},{5,4},{6,7},{7,6},{8,9},{9,8},{10,11... | collective-permute-start | bytes 393224 | tf_op jit(solution)/shard_map/ppermute | solution.py:413
  14.8 5.0 %collective-permute-start.6 = (bf16[512,128]{1,0:T(8,128)(2,1)S(1)}, bf16[512,128]{1,0:T(8,128)(2,1)S(1)}, u32[]{:S(2)}, u32[]{:S(2)}) collective-permute-start(bf16[512,128]{1,0:T(8,128)(2,1)S(1)} %get-tuple-element.65), channel_id=1, source_target_pairs={{0,4},{1,3},{2,6},{3,1},{4,0},{5,7},{6,2},{7,5},{8,12},{9,11},{10,... | collective-permute-start | bytes 393224 | tf_op jit(solution)/shard_map/ppermute | solution.py:413
  16.4 4.4 %collective-permute-start.7 = (bf16[512,128]{1,0:T(8,128)(2,1)S(1)}, bf16[512,128]{1,0:T(8,128)(2,1)S(1)}, u32[]{:S(2)}, u32[]{:S(2)}) collective-permute-start(bf16[512,128]{1,0:T(8,128)(2,1)S(1)} %get-tuple-element.67), channel_id=1, source_target_pairs={{0,5},{1,2},{2,7},{3,0},{4,1},{5,6},{6,3},{7,4},{8,13},{9,10},{10,... | collective-permute-start | bytes 393224 | tf_op jit(solution)/shard_map/ppermute | solution.py:413
  17.0 3.8 %collective-permute-start.8 = (bf16[512,128]{1,0:T(8,128)(2,1)S(1)}, bf16[512,128]{1,0:T(8,128)(2,1)S(1)}, u32[]{:S(2)}, u32[]{:S(2)}) collective-permute-start(bf16[512,128]{1,0:T(8,128)(2,1)S(1)} %get-tuple-element.68), channel_id=1, source_target_pairs={{0,1},{1,0},{2,3},{3,2},{4,5},{5,4},{6,7},{7,6},{8,9},{9,8},{10,11... | collective-permute-start | bytes 393224 | tf_op jit(solution)/shard_map/ppermute | solution.py:413
  17.3 1.5 %copy-start = (bf16[1,256,2048]{2,1,0:T(8,128)(2,1)S(1)}, bf16[1,256,2048]{2,1,0:T(8,128)(2,1)}, u32[]{:S(2)}) copy-start(bf16[1,256,2048]{2,1,0:T(8,128)(2,1)} %param.10) | copy-start | bytes 3145732
  17.3 1.5 %copy-start.1 = (f32[2048]{0:T(1024)S(1)}, f32[2048]{0:T(1024)}, u32[]{:S(2)}) copy-start(f32[2048]{0:T(1024)} %param.11) | copy-start | bytes 24580
  21.5 4.5 %collective-permute-start.14 = (f32[2,256]{1,0:T(2,128)S(1)}, f32[2,256]{1,0:T(2,128)S(1)}, u32[]{:S(2)}, u32[]{:S(2)}) collective-permute-start(f32[2,256]{1,0:T(2,128)S(1)} %get-tuple-element.73.rest_0_), channel_id=1, source_target_pairs={{0,16},{8,24},{16,0},{24,8},{1,17},{9,25},{17,1},{25,9},{2,18},{10... | collective-permute-start | bytes 6152 | tf_op jit(solution)/shard_map/ppermute | solution.py:440
  24.1 5.4 %collective-permute-start.13 = (f32[2,256]{1,0:T(2,128)S(1)}, f32[2,256]{1,0:T(2,128)S(1)}, u32[]{:S(2)}, u32[]{:S(2)}) collective-permute-start(f32[2,256]{1,0:T(2,128)S(1)} %get-tuple-element.73.rest_0_), channel_id=1, source_target_pairs={{0,24},{8,16},{16,8},{24,0},{1,25},{9,17},{17,9},{25,1},{2,26},{10... | collective-permute-start | bytes 6152 | tf_op jit(solution)/shard_map/ppermute | solution.py:440
  25.5 4.0 %collective-permute-start.12 = (f32[2,256]{1,0:T(2,128)S(1)}, f32[2,256]{1,0:T(2,128)S(1)}, u32[]{:S(2)}, u32[]{:S(2)}) collective-permute-start(f32[2,256]{1,0:T(2,128)S(1)} %get-tuple-element.73.rest_0_), channel_id=1, source_target_pairs={{0,8},{8,0},{16,24},{24,16},{1,9},{9,1},{17,25},{25,17},{2,10},{10... | collective-permute-start | bytes 6152 | tf_op jit(solution)/shard_map/ppermute | solution.py:440
  30.1 6.2 %collective-permute-start.19 = (bf16[512,128]{1,0:T(8,128)(2,1)S(1)}, bf16[512,128]{1,0:T(8,128)(2,1)S(1)}, u32[]{:S(2)}, u32[]{:S(2)}) collective-permute-start(bf16[512,128]{1,0:T(8,128)(2,1)S(1)} %get-tuple-element.88.refs_0_), channel_id=1, source_target_pairs={{0,2},{1,5},{2,0},{3,7},{4,6},{5,1},{6,4},{7,3},{8,10},{9,13},{10,... | collective-permute-start | bytes 393224 | tf_op jit(solution)/shard_map/ppermute | solution.py:413
  31.0 6.1 %collective-permute-start.20 = (bf16[512,128]{1,0:T(8,128)(2,1)S(1)}, bf16[512,128]{1,0:T(8,128)(2,1)S(1)}, u32[]{:S(2)}, u32[]{:S(2)}) collective-permute-start(bf16[512,128]{1,0:T(8,128)(2,1)S(1)} %get-tuple-element.89), channel_id=1, source_target_pairs={{0,5},{1,2},{2,7},{3,0},{4,1},{5,6},{6,3},{7,4},{8,13},{9,10},{10,... | collective-permute-start | bytes 393224 | tf_op jit(solution)/shard_map/ppermute | solution.py:413
  31.0 6.1 %collective-permute-start.18 = (bf16[512,128]{1,0:T(8,128)(2,1)S(1)}, bf16[512,128]{1,0:T(8,128)(2,1)S(1)}, u32[]{:S(2)}, u32[]{:S(2)}) collective-permute-start(bf16[512,128]{1,0:T(8,128)(2,1)S(1)} %get-tuple-element.89), channel_id=1, source_target_pairs={{0,1},{1,0},{2,3},{3,2},{4,5},{5,4},{6,7},{7,6},{8,9},{9,8},{10,11... | collective-permute-start | bytes 393224 | tf_op jit(solution)/shard_map/ppermute | solution.py:413
  32.9 6.2 %collective-permute-start.16 = (bf16[512,128]{1,0:T(8,128)(2,1)S(1)}, bf16[512,128]{1,0:T(8,128)(2,1)S(1)}, u32[]{:S(2)}, u32[]{:S(2)}) collective-permute-start(bf16[512,128]{1,0:T(8,128)(2,1)S(1)} %get-tuple-element.84.refs_0_), channel_id=1, source_target_pairs={{0,2},{1,5},{2,0},{3,7},{4,6},{5,1},{6,4},{7,3},{8,10},{9,13},{10,... | collective-permute-start | bytes 393224 | tf_op jit(solution)/shard_map/ppermute | solution.py:413
  33.8 6.0 %collective-permute-start.17 = (bf16[512,128]{1,0:T(8,128)(2,1)S(1)}, bf16[512,128]{1,0:T(8,128)(2,1)S(1)}, u32[]{:S(2)}, u32[]{:S(2)}) collective-permute-start(bf16[512,128]{1,0:T(8,128)(2,1)S(1)} %get-tuple-element.85), channel_id=1, source_target_pairs={{0,5},{1,2},{2,7},{3,0},{4,1},{5,6},{6,3},{7,4},{8,13},{9,10},{10,... | collective-permute-start | bytes 393224 | tf_op jit(solution)/shard_map/ppermute | solution.py:413
  36.3 3.6 %collective-permute-start.15 = (bf16[512,128]{1,0:T(8,128)(2,1)S(1)}, bf16[512,128]{1,0:T(8,128)(2,1)S(1)}, u32[]{:S(2)}, u32[]{:S(2)}) collective-permute-start(bf16[512,128]{1,0:T(8,128)(2,1)S(1)} %get-tuple-element.85), channel_id=1, source_target_pairs={{0,1},{1,0},{2,3},{3,2},{4,5},{5,4},{6,7},{7,6},{8,9},{9,8},{10,11... | collective-permute-start | bytes 393224 | tf_op jit(solution)/shard_map/ppermute | solution.py:413
  37.4 5.0 %collective-permute-start.24 = (bf16[512,128]{1,0:T(8,128)(2,1)S(1)}, bf16[512,128]{1,0:T(8,128)(2,1)S(1)}, u32[]{:S(2)}, u32[]{:S(2)}) collective-permute-start(bf16[512,128]{1,0:T(8,128)(2,1)S(1)} %get-tuple-element.103), channel_id=1, source_target_pairs={{0,4},{1,3},{2,6},{3,1},{4,0},{5,7},{6,2},{7,5},{8,12},{9,11},{10,... | collective-permute-start | bytes 393224 | tf_op jit(solution)/shard_map/ppermute | solution.py:413
  38.9 9.0 %collective-permute-start.25 = (bf16[512,128]{1,0:T(8,128)(2,1)S(1)}, bf16[512,128]{1,0:T(8,128)(2,1)S(1)}, u32[]{:S(2)}, u32[]{:S(2)}) collective-permute-start(bf16[512,128]{1,0:T(8,128)(2,1)S(1)} %get-tuple-element.104), channel_id=1, source_target_pairs={{0,5},{1,2},{2,7},{3,0},{4,1},{5,6},{6,3},{7,4},{8,13},{9,10},{10,... | collective-permute-start | bytes 393224 | tf_op jit(solution)/shard_map/ppermute | solution.py:413
  39.1 8.8 %collective-permute-start.26 = (bf16[512,128]{1,0:T(8,128)(2,1)S(1)}, bf16[512,128]{1,0:T(8,128)(2,1)S(1)}, u32[]{:S(2)}, u32[]{:S(2)}) collective-permute-start(bf16[512,128]{1,0:T(8,128)(2,1)S(1)} %get-tuple-element.105), channel_id=1, source_target_pairs={{0,1},{1,0},{2,3},{3,2},{4,5},{5,4},{6,7},{7,6},{8,9},{9,8},{10,11... | collective-permute-start | bytes 393224 | tf_op jit(solution)/shard_map/ppermute | solution.py:413
  40.1 7.8 %collective-permute-start.21 = (bf16[512,128]{1,0:T(8,128)(2,1)S(1)}, bf16[512,128]{1,0:T(8,128)(2,1)S(1)}, u32[]{:S(2)}, u32[]{:S(2)}) collective-permute-start(bf16[512,128]{1,0:T(8,128)(2,1)S(1)} %get-tuple-element.100), channel_id=1, source_target_pairs={{0,4},{1,3},{2,6},{3,1},{4,0},{5,7},{6,2},{7,5},{8,12},{9,11},{10,... | collective-permute-start | bytes 393224 | tf_op jit(solution)/shard_map/ppermute | solution.py:413
  41.2 6.8 %collective-permute-start.22 = (bf16[512,128]{1,0:T(8,128)(2,1)S(1)}, bf16[512,128]{1,0:T(8,128)(2,1)S(1)}, u32[]{:S(2)}, u32[]{:S(2)}) collective-permute-start(bf16[512,128]{1,0:T(8,128)(2,1)S(1)} %get-tuple-element.101), channel_id=1, source_target_pairs={{0,5},{1,2},{2,7},{3,0},{4,1},{5,6},{6,3},{7,4},{8,13},{9,10},{10,... | collective-permute-start | bytes 393224 | tf_op jit(solution)/shard_map/ppermute | solution.py:413
  42.4 5.5 %collective-permute-start.23 = (bf16[512,128]{1,0:T(8,128)(2,1)S(1)}, bf16[512,128]{1,0:T(8,128)(2,1)S(1)}, u32[]{:S(2)}, u32[]{:S(2)}) collective-permute-start(bf16[512,128]{1,0:T(8,128)(2,1)S(1)} %get-tuple-element.102), channel_id=1, source_target_pairs={{0,1},{1,0},{2,3},{3,2},{4,5},{5,4},{6,7},{7,6},{8,9},{9,8},{10,11... | collective-permute-start | bytes 393224 | tf_op jit(solution)/shard_map/ppermute | solution.py:413

commit v15 on v14

--- a/solution.py
+++ b/solution.py
@@ -159,7 +159,7 @@
     few = pltpu.make_async_copy(parent_hbm, parent, parent_sem)
     few.start()
     for copy in copies:
-        copy.start()
+        copy.start(priority=1)
     length[...] = jnp.full(length.shape, seg_len[0], jnp.int32)
     few.wait()
     write_weights(grid, parent, up, down)
@@ -221,7 +221,7 @@
 def fetch_kernel(source, _, out, sems):
     copies = row_copies(source, out, sems)
     for copy in copies:
-        copy.start()
+        copy.start(priority=1)
     for copy in copies:
         copy.wait()
 
@@ -306,7 +306,7 @@
         width = source.shape[1]
         copies += row_copies(source, target.at[:, pl.ds(piece * width, width)], sems.at[j])
     for copy in copies:
-        copy.start()
+        copy.start(priority=1)
     return copies
 
 
@@ -373,7 +373,7 @@
             done = slice((head + 1 - group) * HD, (head + 1) * HD)
             for j, (src, dst) in enumerate(((key_grad, key_hbm), (value_grad, value_hbm))):
                 copy = pltpu.make_async_copy(src.at[:, done], dst.at[:, done], sems.at[j, head // group])
-                copy.start()
+                copy.start(priority=1)
                 copies.append(copy)
     for copy in copies:
         copy.wait()

time: 50.4 us -> 50.4 us (level)
  no operation moved by 1% of the time
where the time goes in v15:
time: 50.4 us; the launch traced here: 50.2 us
  starting transfers between devices  23.1 us (46%)
  Pallas kernels  18.2 us (36%)
  waiting for transfers between devices  7.32 us (15%)
  between operations  1.63 us (3%)
    ppermute x24, starting transfers between devices, line_send(): return lax.ppermute(block, 'seg', moves)  18.8 us
    pallas_call x15, Pallas kernels, call(): pl.pallas_call(kernel, out_shape=out_shape, in_specs=specs + [ANY] * len(...  18.2 us
    ppermute x3, starting transfers between devices, token_sums(): parts.append(lax.ppermute(sums, 'head', moves))  4.23 us
    ppermute x3, waiting for transfers between devices, token_sums(): parts.append(lax.ppermute(sums, 'head', moves))  3.8 us
    ppermute x24, waiting for transfers between devices, line_send(): return lax.ppermute(block, 'seg', moves)  3.51 us
  transfers between devices with their start and end apart: 27, of which 8 were waited for; matrix products, arithmetic and copies ran while one was open for 0% of the time, Pallas kernels for 25%

profile of v15, /device:TPU:0, one launch (start us, length us, event | category | flops | bytes accessed | tf_op | source)
XLA Modules:
  0.0 50.2 jit_solution(6610493431354642715)
XLA Ops:
  1.3 2.3 %shard_map.102 = (bf16[256,2048]{1,0:T(8,128)(2,1)S(1)}, bf16[256,2048]{1,0:T(8,128)(2,1)S(1)}, s32[1,256]{1,0:T(1,128)S(1)}, f32[16,128]{1,0:T(8,128)S(1)}, f32...) custom-call(s32[1]{0:T(128)S(6)} %copy.15.seg_len, ...), custom_call_target="tpu_custom_call" | custom-call | flops 134217728 | bytes 4736036 | tf_op jit(solution)/shard_map/pallas_call | solution.py:391
  3.6 2.5 %collective-permute-start.2 = (bf16[512,128]{1,0:T(8,128)(2,1)S(1)}, bf16[512,128]{1,0:T(8,128)(2,1)S(1)}, u32[]{:S(2)}, u32[]{:S(2)}) collective-permute-start(bf16[512,128]{1,0:T(8,128)(2,1)S(1)} %get-tuple-element.61), channel_id=1, source_target_pairs={{0,5},{1,2},{2,7},{3,0},{4,1},{5,6},{6,3},{7,4},{8,13},{9,10},{10,... | collective-permute-start | bytes 393224 | tf_op jit(solution)/shard_map/ppermute | solution.py:413
  6.1 0.6 %collective-permute-start = (bf16[512,128]{1,0:T(8,128)(2,1)S(1)}, bf16[512,128]{1,0:T(8,128)(2,1)S(1)}, u32[]{:S(2)}, u32[]{:S(2)}) collective-permute-start(bf16[512,128]{1,0:T(8,128)(2,1)S(1)} %get-tuple-element.61), channel_id=1, source_target_pairs={{0,1},{1,0},{2,3},{3,2},{4,5},{5,4},{6,7},{7,6},{8,9},{9,8},{10,11... | collective-permute-start | bytes 393224 | tf_op jit(solution)/shard_map/ppermute | solution.py:413
  6.7 0.9 %collective-permute-start.1 = (bf16[512,128]{1,0:T(8,128)(2,1)S(1)}, bf16[512,128]{1,0:T(8,128)(2,1)S(1)}, u32[]{:S(2)}, u32[]{:S(2)}) collective-permute-start(bf16[512,128]{1,0:T(8,128)(2,1)S(1)} %get-tuple-element.57._.refs_0_), channel_id=1, source_target_pairs={{0,2},{1,5},{2,0},{3,7},{4,6},{5,1},{6,4},{7,3},{8,10},{9,13},{10,... | collective-permute-start | bytes 393224 | tf_op jit(solution)/shard_map/ppermute | solution.py:413
  7.6 1.1 %collective-permute-start.4 = (bf16[512,128]{1,0:T(8,128)(2,1)S(1)}, bf16[512,128]{1,0:T(8,128)(2,1)S(1)}, u32[]{:S(2)}, u32[]{:S(2)}) collective-permute-start(bf16[512,128]{1,0:T(8,128)(2,1)S(1)} %get-tuple-element.63.refs_0_), channel_id=1, source_target_pairs={{0,2},{1,5},{2,0},{3,7},{4,6},{5,1},{6,4},{7,3},{8,10},{9,13},{10,... | collective-permute-start | bytes 393224 | tf_op jit(solution)/shard_map/ppermute | solution.py:413
  8.8 0.6 %collective-permute-start.5 = (bf16[512,128]{1,0:T(8,128)(2,1)S(1)}, bf16[512,128]{1,0:T(8,128)(2,1)S(1)}, u32[]{:S(2)}, u32[]{:S(2)}) collective-permute-start(bf16[512,128]{1,0:T(8,128)(2,1)S(1)} %get-tuple-element.64), channel_id=1, source_target_pairs={{0,5},{1,2},{2,7},{3,0},{4,1},{5,6},{6,3},{7,4},{8,13},{9,10},{10,... | collective-permute-start | bytes 393224 | tf_op jit(solution)/shard_map/ppermute | solution.py:413
  9.3 1.2 %shard_map.103.refs_4_.queries = bf16[256,2048]{1,0:T(8,128)(2,1)S(1)} custom-call(bf16[256,2048]{1,0:T(8,128)(2,1)} %bitcast.20, bf16[512,128]{1,0:T(8,128)(2,1)S(1)} %get-tuple-element.57._.refs_0_), custom_call_target="tpu_custom_call" | custom-call | bytes 2097152 | tf_op jit(solution)/shard_map/pallas_call | solution.py:391
  10.6 0.0 collective-permute-done.2.refs_3_
  10.6 0.5 collective-permute-start.3
  11.1 0.0 collective-permute-done.refs_1_
  11.1 0.6 %collective-permute-done.1.refs_2_ = bf16[512,128]{1,0:T(8,128)(2,1)S(1)} collective-permute-done((bf16[512,128]{1,0:T(8,128)(2,1)S(1)}, bf16[512,128]{1,0:T(8,128)(2,1)S(1)}, u32[]{:S(2)}, u32[]{:S(2)}) %collective-permute-start.1) | collective-permute-done | bytes 131104 | tf_op jit(solution)/shard_map/ppermute | solution.py:413
  11.7 0.3 shard_map.104
  12.0 1.6 %collective-permute-start.9 = (bf16[512,128]{1,0:T(8,128)(2,1)S(1)}, bf16[512,128]{1,0:T(8,128)(2,1)S(1)}, u32[]{:S(2)}, u32[]{:S(2)}) collective-permute-start(bf16[512,128]{1,0:T(8,128)(2,1)S(1)} %get-tuple-element.69), channel_id=1, source_target_pairs={{0,4},{1,3},{2,6},{3,1},{4,0},{5,7},{6,2},{7,5},{8,12},{9,11},{10,... | collective-permute-start | bytes 393224 | tf_op jit(solution)/shard_map/ppermute | solution.py:413
  13.6 0.4 collective-permute-start.10
  14.0 0.4 collective-permute-done.4.refs_2_
  14.4 0.1 collective-permute-start.11
  14.5 0.0 collective-permute-done.5.refs_3_
  14.5 0.0 collective-permute-done.3.refs_1_
  14.5 0.3 shard_map.106
  14.8 1.6 %collective-permute-start.6 = (bf16[512,128]{1,0:T(8,128)(2,1)S(1)}, bf16[512,128]{1,0:T(8,128)(2,1)S(1)}, u32[]{:S(2)}, u32[]{:S(2)}) collective-permute-start(bf16[512,128]{1,0:T(8,128)(2,1)S(1)} %get-tuple-element.65), channel_id=1, source_target_pairs={{0,4},{1,3},{2,6},{3,1},{4,0},{5,7},{6,2},{7,5},{8,12},{9,11},{10,... | collective-permute-start | bytes 393224 | tf_op jit(solution)/shard_map/ppermute | solution.py:413
  16.4 0.6 %collective-permute-start.7 = (bf16[512,128]{1,0:T(8,128)(2,1)S(1)}, bf16[512,128]{1,0:T(8,128)(2,1)S(1)}, u32[]{:S(2)}, u32[]{:S(2)}) collective-permute-start(bf16[512,128]{1,0:T(8,128)(2,1)S(1)} %get-tuple-element.67), channel_id=1, source_target_pairs={{0,5},{1,2},{2,7},{3,0},{4,1},{5,6},{6,3},{7,4},{8,13},{9,10},{10,... | collective-permute-start | bytes 393224 | tf_op jit(solution)/shard_map/ppermute | solution.py:413
  16.9 0.1 collective-permute-done.9.rest_0_
  17.0 0.3 collective-permute-start.8
  17.4 1.5 %shard_map.105.local = f32[256,2048]{1,0:T(8,128)S(1)} custom-call(s32[1,256]{1,0:T(1,128)S(1)} %get-tuple-element.56.length, bf16[256,2048]{1,0:T(8,128)(2,1)S(1)} %shard_map.103.refs_4_.queries, bf16[256,2048]{1,0:T(8,128)(2,1)S(1)} %get-tuple-element.58.keys, bf16[256,2048]{1,0:T(8,128)(2,1)S(1)} %get-tuple-element.59.values, ...), custom_call_target="tpu_custom_call" | custom-call | flops 536870912 | bytes 5243904 | tf_op jit(solution)/shard_map/pallas_call | solution.py:391
  18.8 0.0 collective-permute-done.11.rest_3_
  18.9 0.7 %shard_map.107 = (f32[256,1024]{1,0:T(8,128)S(1)}, f32[2,256]{1,0:T(2,128)S(1)}, bf16[1024,128]{1,0:T(8,128)(2,1)S(1)}) custom-call(s32[1,256]{1,0:T(1,128)S(1)} %get-tuple-element.56.length, bf16[256,2048]{1,0:T(8,128)(2,1)S(1)} %shard_map.103.refs_4_.queries, f32[256,2048]{1,0:T(8,128)S(1)} %shard_map.105.local, bf16[256,2048]{1,0:T(8,128)(2,1)S(1)} %bitcast.10, ...), custom_call_target="tpu_custom_call" | custom-call | flops 67108864 | bytes 6040576 | tf_op jit(solution)/shard_map/pallas_call | solution.py:391
  19.5 0.3 collective-permute-done.6.rest_0_
  19.8 0.9 %collective-permute-done.7.rest_2_ = bf16[512,128]{1,0:T(8,128)(2,1)S(1)} collective-permute-done((bf16[512,128]{1,0:T(8,128)(2,1)S(1)}, bf16[512,128]{1,0:T(8,128)(2,1)S(1)}, u32[]{:S(2)}, u32[]{:S(2)}) %collective-permute-start.7) | collective-permute-done | bytes 131104 | tf_op jit(solution)/shard_map/ppermute | solution.py:413
  20.8 0.7 %shard_map.108 = (f32[256,1024]{1,0:T(8,128)S(1)}, f32[2,256]{1,0:T(2,128)S(1)}, bf16[1024,128]{1,0:T(8,128)(2,1)S(1)}) custom-call(s32[1,256]{1,0:T(1,128)S(1)} %get-tuple-element.56.length, bf16[256,2048]{1,0:T(8,128)(2,1)S(1)} %shard_map.103.refs_4_.queries, f32[256,2048]{1,0:T(8,128)S(1)} %shard_map.105.local, bf16[256,2048]{1,0:T(8,128)(2,1)S(1)} %bitcast.11, ...), custom_call_target="tpu_custom_call" | custom-call | flops 67108864 | bytes 6042624 | tf_op jit(solution)/shard_map/pallas_call | solution.py:391
  21.5 2.7 %collective-permute-start.14 = (f32[2,256]{1,0:T(2,128)S(1)}, f32[2,256]{1,0:T(2,128)S(1)}, u32[]{:S(2)}, u32[]{:S(2)}) collective-permute-start(f32[2,256]{1,0:T(2,128)S(1)} %get-tuple-element.73.rest_0_), channel_id=1, source_target_pairs={{0,16},{8,24},{16,0},{24,8},{1,17},{9,25},{17,1},{25,9},{2,18},{10... | collective-permute-start | bytes 6152 | tf_op jit(solution)/shard_map/ppermute | solution.py:440
  24.1 1.3 %collective-permute-start.13 = (f32[2,256]{1,0:T(2,128)S(1)}, f32[2,256]{1,0:T(2,128)S(1)}, u32[]{:S(2)}, u32[]{:S(2)}) collective-permute-start(f32[2,256]{1,0:T(2,128)S(1)} %get-tuple-element.73.rest_0_), channel_id=1, source_target_pairs={{0,24},{8,16},{16,8},{24,0},{1,25},{9,17},{17,9},{25,1},{2,26},{10... | collective-permute-start | bytes 6152 | tf_op jit(solution)/shard_map/ppermute | solution.py:440
  25.5 0.2 collective-permute-start.12
  25.7 0.3 collective-permute-done.14.rest_3_
  26.0 3.5 %collective-permute-done.13.rest_2_ = f32[2,256]{1,0:T(2,128)S(1)} collective-permute-done((f32[2,256]{1,0:T(2,128)S(1)}, f32[2,256]{1,0:T(2,128)S(1)}, u32[]{:S(2)}, u32[]{:S(2)}) %collective-permute-start.13) | collective-permute-done | bytes 2080 | tf_op jit(solution)/shard_map/ppermute | solution.py:440
  29.5 0.0 collective-permute-done.12.rest_1_
  29.5 0.6 %shard_map.110 = (bf16[256,1024]{1,0:T(8,128)(2,1)S(1)}, bf16[512,128]{1,0:T(8,128)(2,1)S(1)}, bf16[512,128]{1,0:T(8,128)(2,1)S(1)}) custom-call(s32[1,256]{1,0:T(1,128)S(1)} %get-tuple-element.56.length, bf16[256,2048]{1,0:T(8,128)(2,1)S(1)} %shard_map.103.refs_4_.queries, bf16[256,2048]{1,0:T(8,128)(2,1)S(1)} %bitcast.12, f32[1,2048]{1,0:T(1,128)S(1)} %bitcast.16, ...), custom_call_target="tpu_custom_call" | custom-call | flops 67108864 | bytes 4998144 | tf_op jit(solution)/shard_map/pallas_call | solution.py:391
  30.1 0.9 %collective-permute-start.19 = (bf16[512,128]{1,0:T(8,128)(2,1)S(1)}, bf16[512,128]{1,0:T(8,128)(2,1)S(1)}, u32[]{:S(2)}, u32[]{:S(2)}) collective-permute-start(bf16[512,128]{1,0:T(8,128)(2,1)S(1)} %get-tuple-element.88.refs_0_), channel_id=1, source_target_pairs={{0,2},{1,5},{2,0},{3,7},{4,6},{5,1},{6,4},{7,3},{8,10},{9,13},{10,... | collective-permute-start | bytes 393224 | tf_op jit(solution)/shard_map/ppermute | solution.py:413
  31.0 0.0 collective-permute-start.20
  31.0 1.3 %collective-permute-start.18 = (bf16[512,128]{1,0:T(8,128)(2,1)S(1)}, bf16[512,128]{1,0:T(8,128)(2,1)S(1)}, u32[]{:S(2)}, u32[]{:S(2)}) collective-permute-start(bf16[512,128]{1,0:T(8,128)(2,1)S(1)} %get-tuple-element.89), channel_id=1, source_target_pairs={{0,1},{1,0},{2,3},{3,2},{4,5},{5,4},{6,7},{7,6},{8,9},{9,8},{10,11... | collective-permute-start | bytes 393224 | tf_op jit(solution)/shard_map/ppermute | solution.py:413
  32.3 0.6 %shard_map.109 = (bf16[256,1024]{1,0:T(8,128)(2,1)S(1)}, bf16[512,128]{1,0:T(8,128)(2,1)S(1)}, bf16[512,128]{1,0:T(8,128)(2,1)S(1)}, f32[1,256]{1,0:T(1,128)S(1)}) custom-call(s32[1,256]{1,0:T(1,128)S(1)} %get-tuple-element.56.length, bf16[256,2048]{1,0:T(8,128)(2,1)S(1)} %shard_map.103.refs_4_.queries, bf16[256,2048]{1,0:T(8,128)(2,1)S(1)} %bitcast.13, ...), custom_call_target="tpu_custom_call" | custom-call | flops 67108864 | bytes 4999168 | tf_op jit(solution)/shard_map/pallas_call | solution.py:391
  32.9 0.9 %collective-permute-start.16 = (bf16[512,128]{1,0:T(8,128)(2,1)S(1)}, bf16[512,128]{1,0:T(8,128)(2,1)S(1)}, u32[]{:S(2)}, u32[]{:S(2)}) collective-permute-start(bf16[512,128]{1,0:T(8,128)(2,1)S(1)} %get-tuple-element.84.refs_0_), channel_id=1, source_target_pairs={{0,2},{1,5},{2,0},{3,7},{4,6},{5,1},{6,4},{7,3},{8,10},{9,13},{10,... | collective-permute-start | bytes 393224 | tf_op jit(solution)/shard_map/ppermute | solution.py:413
  33.8 0.5 %collective-permute-start.17 = (bf16[512,128]{1,0:T(8,128)(2,1)S(1)}, bf16[512,128]{1,0:T(8,128)(2,1)S(1)}, u32[]{:S(2)}, u32[]{:S(2)}) collective-permute-start(bf16[512,128]{1,0:T(8,128)(2,1)S(1)} %get-tuple-element.85), channel_id=1, source_target_pairs={{0,5},{1,2},{2,7},{3,0},{4,1},{5,6},{6,3},{7,4},{8,13},{9,10},{10,... | collective-permute-start | bytes 393224 | tf_op jit(solution)/shard_map/ppermute | solution.py:413
  34.4 1.9 %shard_map.111 = (bf16[256,1024]{1,0:T(8,128)(2,1)S(1)}, bf16[256,1024]{1,0:T(8,128)(2,1)S(1)}, f32[256,1024]{1,0:T(8,128)S(1)}, f32[8,128]{1,0:T(8,128)S(1)}) custom-call(s32[1,256]{1,0:T(1,128)S(1)} %get-tuple-element.56.length, f32[1,256]{1,0:T(1,128)S(1)} %get-tuple-element.78.inverse_rms, f32[1,2048]{1,0:T(1,128)S(1)} %bitcast.18, ...), custom_call_target="tpu_custom_call" | custom-call | flops 469762048 | bytes 8402944 | tf_op jit(solution)/shard_map/pallas_call | solution.py:391
  36.3 0.0 collective-permute-done.19.refs_2_
  36.3 0.8 %collective-permute-start.15 = (bf16[512,128]{1,0:T(8,128)(2,1)S(1)}, bf16[512,128]{1,0:T(8,128)(2,1)S(1)}, u32[]{:S(2)}, u32[]{:S(2)}) collective-permute-start(bf16[512,128]{1,0:T(8,128)(2,1)S(1)} %get-tuple-element.85), channel_id=1, source_target_pairs={{0,1},{1,0},{2,3},{3,2},{4,5},{5,4},{6,7},{7,6},{8,9},{9,8},{10,11... | collective-permute-start | bytes 393224 | tf_op jit(solution)/shard_map/ppermute | solution.py:413
  37.1 0.0 collective-permute-done.20.refs_3_
  37.1 0.3 shard_map.113
  37.4 1.5 %collective-permute-start.24 = (bf16[512,128]{1,0:T(8,128)(2,1)S(1)}, bf16[512,128]{1,0:T(8,128)(2,1)S(1)}, u32[]{:S(2)}, u32[]{:S(2)}) collective-permute-start(bf16[512,128]{1,0:T(8,128)(2,1)S(1)} %get-tuple-element.103), channel_id=1, source_target_pairs={{0,4},{1,3},{2,6},{3,1},{4,0},{5,7},{6,2},{7,5},{8,12},{9,11},{10,... | collective-permute-start | bytes 393224 | tf_op jit(solution)/shard_map/ppermute | solution.py:413
  38.9 0.2 collective-permute-start.25
  39.1 0.0 collective-permute-done.16.refs_2_
  39.1 0.8 %collective-permute-start.26 = (bf16[512,128]{1,0:T(8,128)(2,1)S(1)}, bf16[512,128]{1,0:T(8,128)(2,1)S(1)}, u32[]{:S(2)}, u32[]{:S(2)}) collective-permute-start(bf16[512,128]{1,0:T(8,128)(2,1)S(1)} %get-tuple-element.105), channel_id=1, source_target_pairs={{0,1},{1,0},{2,3},{3,2},{4,5},{5,4},{6,7},{7,6},{8,9},{9,8},{10,11... | collective-permute-start | bytes 393224 | tf_op jit(solution)/shard_map/ppermute | solution.py:413
  39.8 0.0 collective-permute-done.17.refs_3_
  39.8 0.0 collective-permute-done.15.refs_1_
  39.8 0.3 shard_map.112
  40.1 1.0 %collective-permute-start.21 = (bf16[512,128]{1,0:T(8,128)(2,1)S(1)}, bf16[512,128]{1,0:T(8,128)(2,1)S(1)}, u32[]{:S(2)}, u32[]{:S(2)}) collective-permute-start(bf16[512,128]{1,0:T(8,128)(2,1)S(1)} %get-tuple-element.100), channel_id=1, source_target_pairs={{0,4},{1,3},{2,6},{3,1},{4,0},{5,7},{6,2},{7,5},{8,12},{9,11},{10,... | collective-permute-start | bytes 393224 | tf_op jit(solution)/shard_map/ppermute | solution.py:413
  41.2 0.2 collective-permute-start.22
  41.4 1.1 %collective-permute-done.24.rest_6_ = bf16[512,128]{1,0:T(8,128)(2,1)S(1)} collective-permute-done((bf16[512,128]{1,0:T(8,128)(2,1)S(1)}, bf16[512,128]{1,0:T(8,128)(2,1)S(1)}, u32[]{:S(2)}, u32[]{:S(2)}) %collective-permute-start.24) | collective-permute-done | bytes 131104 | tf_op jit(solution)/shard_map/ppermute | solution.py:413
  42.4 0.0 collective-permute-start.23
  42.4 3.2 %shard_map.114 = (bf16[256,1024]{1,0:T(8,128)(2,1)S(1)}, bf16[256,1024]{1,0:T(8,128)(2,1)S(1)}, f32[256,1024]{1,0:T(8,128)S(1)}, f32[8,128]{1,0:T(8,128)}, bf16[...) custom-call(s32[1,256]{1,0:T(1,128)S(1)} %get-tuple-element.56.length, f32[1,256]{1,0:T(1,128)S(1)} %get-tuple-element.78.inverse_rms, ...), custom_call_target="tpu_custom_call" | custom-call | flops 469762048 | bytes 11548672 | tf_op jit(solution)/shard_map/pallas_call | solution.py:391
  45.7 2.2 %shard_map.115 = (f32[256,2048]{1,0:T(8,128)S(1)}, bf16[256,2048]{1,0:T(8,128)(2,1)}, bf16[256,2048]{1,0:T(8,128)(2,1)}) custom-call(s32[1,256]{1,0:T(1,128)S(1)} %get-tuple-element.56.length, bf16[256,2048]{1,0:T(8,128)(2,1)S(1)} %shard_map.103.refs_4_.queries, ...), custom_call_target="tpu_custom_call", output_to_operand_aliasing={{1}: (7, {}), {2}: (8, {})} | custom-call | flops 536870912 | bytes 10486784 | tf_op jit(solution)/shard_map/pallas_call | solution.py:391
  47.9 0.0 collective-permute-done.25.rest_8_
  47.9 0.0 collective-permute-done.21.rest_2_
  47.9 0.0 collective-permute-done.22.rest_4_
  47.9 2.1 %shard_map.116 = (bf16[256,2048]{1,0:T(8,128)(2,1)}, bf16[256,2048]{1,0:T(8,128)(2,1)}) custom-call(s32[1,256]{1,0:T(1,128)S(1)} %get-tuple-element.56.length, bf16[256,2048]{1,0:T(8,128)(2,1)S(1)} %get-tuple-element.58.keys, bf16[256,2048]{1,0:T(8,128)(2,1)S(1)} %get-tuple-element.59.values, f32[256,2048]{1,0:T(8,128)S(1)} %get-tuple-element.97.value_part, ...), custom_call_target="tpu_custom_call" | custom-call | flops 268435456 | bytes 9438208 | tf_op jit(solution)/shard_map/pallas_call | solution.py:391
  (9 shorter events, 0.0 us)
Async XLA Ops:
  3.6 6.9 %collective-permute-start.2 = (bf16[512,128]{1,0:T(8,128)(2,1)S(1)}, bf16[512,128]{1,0:T(8,128)(2,1)S(1)}, u32[]{:S(2)}, u32[]{:S(2)}) collective-permute-start(bf16[512,128]{1,0:T(8,128)(2,1)S(1)} %get-tuple-element.61), channel_id=1, source_target_pairs={{0,5},{1,2},{2,7},{3,0},{4,1},{5,6},{6,3},{7,4},{8,13},{9,10},{10,... | collective-permute-start | bytes 393224 | tf_op jit(solution)/shard_map/ppermute | solution.py:413
  6.1 4.9 %collective-permute-start = (bf16[512,128]{1,0:T(8,128)(2,1)S(1)}, bf16[512,128]{1,0:T(8,128)(2,1)S(1)}, u32[]{:S(2)}, u32[]{:S(2)}) collective-permute-start(bf16[512,128]{1,0:T(8,128)(2,1)S(1)} %get-tuple-element.61), channel_id=1, source_target_pairs={{0,1},{1,0},{2,3},{3,2},{4,5},{5,4},{6,7},{7,6},{8,9},{9,8},{10,11... | collective-permute-start | bytes 393224 | tf_op jit(solution)/shard_map/ppermute | solution.py:413
  6.7 5.0 %collective-permute-start.1 = (bf16[512,128]{1,0:T(8,128)(2,1)S(1)}, bf16[512,128]{1,0:T(8,128)(2,1)S(1)}, u32[]{:S(2)}, u32[]{:S(2)}) collective-permute-start(bf16[512,128]{1,0:T(8,128)(2,1)S(1)} %get-tuple-element.57._.refs_0_), channel_id=1, source_target_pairs={{0,2},{1,5},{2,0},{3,7},{4,6},{5,1},{6,4},{7,3},{8,10},{9,13},{10,... | collective-permute-start | bytes 393224 | tf_op jit(solution)/shard_map/ppermute | solution.py:413
  7.6 6.8 %collective-permute-start.4 = (bf16[512,128]{1,0:T(8,128)(2,1)S(1)}, bf16[512,128]{1,0:T(8,128)(2,1)S(1)}, u32[]{:S(2)}, u32[]{:S(2)}) collective-permute-start(bf16[512,128]{1,0:T(8,128)(2,1)S(1)} %get-tuple-element.63.refs_0_), channel_id=1, source_target_pairs={{0,2},{1,5},{2,0},{3,7},{4,6},{5,1},{6,4},{7,3},{8,10},{9,13},{10,... | collective-permute-start | bytes 393224 | tf_op jit(solution)/shard_map/ppermute | solution.py:413
  8.8 5.8 %collective-permute-start.5 = (bf16[512,128]{1,0:T(8,128)(2,1)S(1)}, bf16[512,128]{1,0:T(8,128)(2,1)S(1)}, u32[]{:S(2)}, u32[]{:S(2)}) collective-permute-start(bf16[512,128]{1,0:T(8,128)(2,1)S(1)} %get-tuple-element.64), channel_id=1, source_target_pairs={{0,5},{1,2},{2,7},{3,0},{4,1},{5,6},{6,3},{7,4},{8,13},{9,10},{10,... | collective-permute-start | bytes 393224 | tf_op jit(solution)/shard_map/ppermute | solution.py:413
  10.6 3.9 %collective-permute-start.3 = (bf16[512,128]{1,0:T(8,128)(2,1)S(1)}, bf16[512,128]{1,0:T(8,128)(2,1)S(1)}, u32[]{:S(2)}, u32[]{:S(2)}) collective-permute-start(bf16[512,128]{1,0:T(8,128)(2,1)S(1)} %get-tuple-element.64), channel_id=1, source_target_pairs={{0,1},{1,0},{2,3},{3,2},{4,5},{5,4},{6,7},{7,6},{8,9},{9,8},{10,11... | collective-permute-start | bytes 393224 | tf_op jit(solution)/shard_map/ppermute | solution.py:413
  12.0 5.0 %collective-permute-start.9 = (bf16[512,128]{1,0:T(8,128)(2,1)S(1)}, bf16[512,128]{1,0:T(8,128)(2,1)S(1)}, u32[]{:S(2)}, u32[]{:S(2)}) collective-permute-start(bf16[512,128]{1,0:T(8,128)(2,1)S(1)} %get-tuple-element.69), channel_id=1, source_target_pairs={{0,4},{1,3},{2,6},{3,1},{4,0},{5,7},{6,2},{7,5},{8,12},{9,11},{10,... | collective-permute-start | bytes 393224 | tf_op jit(solution)/shard_map/ppermute | solution.py:413
  13.6 5.3 %collective-permute-start.10 = (bf16[512,128]{1,0:T(8,128)(2,1)S(1)}, bf16[512,128]{1,0:T(8,128)(2,1)S(1)}, u32[]{:S(2)}, u32[]{:S(2)}) collective-permute-start(bf16[512,128]{1,0:T(8,128)(2,1)S(1)} %get-tuple-element.70), channel_id=1, source_target_pairs={{0,5},{1,2},{2,7},{3,0},{4,1},{5,6},{6,3},{7,4},{8,13},{9,10},{10,... | collective-permute-start | bytes 393224 | tf_op jit(solution)/shard_map/ppermute | solution.py:413
  14.4 4.4 %collective-permute-start.11 = (bf16[512,128]{1,0:T(8,128)(2,1)S(1)}, bf16[512,128]{1,0:T(8,128)(2,1)S(1)}, u32[]{:S(2)}, u32[]{:S(2)}) collective-permute-start(bf16[512,128]{1,0:T(8,128)(2,1)S(1)} %get-tuple-element.71), channel_id=1, source_target_pairs={{0,1},{1,0},{2,3},{3,2},{4,5},{5,4},{6,7},{7,6},{8,9},{9,8},{10,11... | collective-permute-start | bytes 393224 | tf_op jit(solution)/shard_map/ppermute | solution.py:413
  14.8 5.0 %collective-permute-start.6 = (bf16[512,128]{1,0:T(8,128)(2,1)S(1)}, bf16[512,128]{1,0:T(8,128)(2,1)S(1)}, u32[]{:S(2)}, u32[]{:S(2)}) collective-permute-start(bf16[512,128]{1,0:T(8,128)(2,1)S(1)} %get-tuple-element.65), channel_id=1, source_target_pairs={{0,4},{1,3},{2,6},{3,1},{4,0},{5,7},{6,2},{7,5},{8,12},{9,11},{10,... | collective-permute-start | bytes 393224 | tf_op jit(solution)/shard_map/ppermute | solution.py:413
  16.4 4.4 %collective-permute-start.7 = (bf16[512,128]{1,0:T(8,128)(2,1)S(1)}, bf16[512,128]{1,0:T(8,128)(2,1)S(1)}, u32[]{:S(2)}, u32[]{:S(2)}) collective-permute-start(bf16[512,128]{1,0:T(8,128)(2,1)S(1)} %get-tuple-element.67), channel_id=1, source_target_pairs={{0,5},{1,2},{2,7},{3,0},{4,1},{5,6},{6,3},{7,4},{8,13},{9,10},{10,... | collective-permute-start | bytes 393224 | tf_op jit(solution)/shard_map/ppermute | solution.py:413
  17.0 3.8 %collective-permute-start.8 = (bf16[512,128]{1,0:T(8,128)(2,1)S(1)}, bf16[512,128]{1,0:T(8,128)(2,1)S(1)}, u32[]{:S(2)}, u32[]{:S(2)}) collective-permute-start(bf16[512,128]{1,0:T(8,128)(2,1)S(1)} %get-tuple-element.68), channel_id=1, source_target_pairs={{0,1},{1,0},{2,3},{3,2},{4,5},{5,4},{6,7},{7,6},{8,9},{9,8},{10,11... | collective-permute-start | bytes 393224 | tf_op jit(solution)/shard_map/ppermute | solution.py:413
  17.3 1.5 %copy-start = (bf16[1,256,2048]{2,1,0:T(8,128)(2,1)S(1)}, bf16[1,256,2048]{2,1,0:T(8,128)(2,1)}, u32[]{:S(2)}) copy-start(bf16[1,256,2048]{2,1,0:T(8,128)(2,1)} %param.10) | copy-start | bytes 3145732
  17.3 1.5 %copy-start.1 = (f32[2048]{0:T(1024)S(1)}, f32[2048]{0:T(1024)}, u32[]{:S(2)}) copy-start(f32[2048]{0:T(1024)} %param.11) | copy-start | bytes 24580
  21.5 4.5 %collective-permute-start.14 = (f32[2,256]{1,0:T(2,128)S(1)}, f32[2,256]{1,0:T(2,128)S(1)}, u32[]{:S(2)}, u32[]{:S(2)}) collective-permute-start(f32[2,256]{1,0:T(2,128)S(1)} %get-tuple-element.73.rest_0_), channel_id=1, source_target_pairs={{0,16},{8,24},{16,0},{24,8},{1,17},{9,25},{17,1},{25,9},{2,18},{10... | collective-permute-start | bytes 6152 | tf_op jit(solution)/shard_map/ppermute | solution.py:440
  24.1 5.4 %collective-permute-start.13 = (f32[2,256]{1,0:T(2,128)S(1)}, f32[2,256]{1,0:T(2,128)S(1)}, u32[]{:S(2)}, u32[]{:S(2)}) collective-permute-start(f32[2,256]{1,0:T(2,128)S(1)} %get-tuple-element.73.rest_0_), channel_id=1, source_target_pairs={{0,24},{8,16},{16,8},{24,0},{1,25},{9,17},{17,9},{25,1},{2,26},{10... | collective-permute-start | bytes 6152 | tf_op jit(solution)/shard_map/ppermute | solution.py:440
  25.5 4.0 %collective-permute-start.12 = (f32[2,256]{1,0:T(2,128)S(1)}, f32[2,256]{1,0:T(2,128)S(1)}, u32[]{:S(2)}, u32[]{:S(2)}) collective-permute-start(f32[2,256]{1,0:T(2,128)S(1)} %get-tuple-element.73.rest_0_), channel_id=1, source_target_pairs={{0,8},{8,0},{16,24},{24,16},{1,9},{9,1},{17,25},{25,17},{2,10},{10... | collective-permute-start | bytes 6152 | tf_op jit(solution)/shard_map/ppermute | solution.py:440
  30.1 6.2 %collective-permute-start.19 = (bf16[512,128]{1,0:T(8,128)(2,1)S(1)}, bf16[512,128]{1,0:T(8,128)(2,1)S(1)}, u32[]{:S(2)}, u32[]{:S(2)}) collective-permute-start(bf16[512,128]{1,0:T(8,128)(2,1)S(1)} %get-tuple-element.88.refs_0_), channel_id=1, source_target_pairs={{0,2},{1,5},{2,0},{3,7},{4,6},{5,1},{6,4},{7,3},{8,10},{9,13},{10,... | collective-permute-start | bytes 393224 | tf_op jit(solution)/shard_map/ppermute | solution.py:413
  31.0 6.1 %collective-permute-start.20 = (bf16[512,128]{1,0:T(8,128)(2,1)S(1)}, bf16[512,128]{1,0:T(8,128)(2,1)S(1)}, u32[]{:S(2)}, u32[]{:S(2)}) collective-permute-start(bf16[512,128]{1,0:T(8,128)(2,1)S(1)} %get-tuple-element.89), channel_id=1, source_target_pairs={{0,5},{1,2},{2,7},{3,0},{4,1},{5,6},{6,3},{7,4},{8,13},{9,10},{10,... | collective-permute-start | bytes 393224 | tf_op jit(solution)/shard_map/ppermute | solution.py:413
  31.0 6.1 %collective-permute-start.18 = (bf16[512,128]{1,0:T(8,128)(2,1)S(1)}, bf16[512,128]{1,0:T(8,128)(2,1)S(1)}, u32[]{:S(2)}, u32[]{:S(2)}) collective-permute-start(bf16[512,128]{1,0:T(8,128)(2,1)S(1)} %get-tuple-element.89), channel_id=1, source_target_pairs={{0,1},{1,0},{2,3},{3,2},{4,5},{5,4},{6,7},{7,6},{8,9},{9,8},{10,11... | collective-permute-start | bytes 393224 | tf_op jit(solution)/shard_map/ppermute | solution.py:413
  32.9 6.2 %collective-permute-start.16 = (bf16[512,128]{1,0:T(8,128)(2,1)S(1)}, bf16[512,128]{1,0:T(8,128)(2,1)S(1)}, u32[]{:S(2)}, u32[]{:S(2)}) collective-permute-start(bf16[512,128]{1,0:T(8,128)(2,1)S(1)} %get-tuple-element.84.refs_0_), channel_id=1, source_target_pairs={{0,2},{1,5},{2,0},{3,7},{4,6},{5,1},{6,4},{7,3},{8,10},{9,13},{10,... | collective-permute-start | bytes 393224 | tf_op jit(solution)/shard_map/ppermute | solution.py:413
  33.8 6.0 %collective-permute-start.17 = (bf16[512,128]{1,0:T(8,128)(2,1)S(1)}, bf16[512,128]{1,0:T(8,128)(2,1)S(1)}, u32[]{:S(2)}, u32[]{:S(2)}) collective-permute-start(bf16[512,128]{1,0:T(8,128)(2,1)S(1)} %get-tuple-element.85), channel_id=1, source_target_pairs={{0,5},{1,2},{2,7},{3,0},{4,1},{5,6},{6,3},{7,4},{8,13},{9,10},{10,... | collective-permute-start | bytes 393224 | tf_op jit(solution)/shard_map/ppermute | solution.py:413
  36.3 3.6 %collective-permute-start.15 = (bf16[512,128]{1,0:T(8,128)(2,1)S(1)}, bf16[512,128]{1,0:T(8,128)(2,1)S(1)}, u32[]{:S(2)}, u32[]{:S(2)}) collective-permute-start(bf16[512,128]{1,0:T(8,128)(2,1)S(1)} %get-tuple-element.85), channel_id=1, source_target_pairs={{0,1},{1,0},{2,3},{3,2},{4,5},{5,4},{6,7},{7,6},{8,9},{9,8},{10,11... | collective-permute-start | bytes 393224 | tf_op jit(solution)/shard_map/ppermute | solution.py:413
  37.4 5.0 %collective-permute-start.24 = (bf16[512,128]{1,0:T(8,128)(2,1)S(1)}, bf16[512,128]{1,0:T(8,128)(2,1)S(1)}, u32[]{:S(2)}, u32[]{:S(2)}) collective-permute-start(bf16[512,128]{1,0:T(8,128)(2,1)S(1)} %get-tuple-element.103), channel_id=1, source_target_pairs={{0,4},{1,3},{2,6},{3,1},{4,0},{5,7},{6,2},{7,5},{8,12},{9,11},{10,... | collective-permute-start | bytes 393224 | tf_op jit(solution)/shard_map/ppermute | solution.py:413
  38.9 9.0 %collective-permute-start.25 = (bf16[512,128]{1,0:T(8,128)(2,1)S(1)}, bf16[512,128]{1,0:T(8,128)(2,1)S(1)}, u32[]{:S(2)}, u32[]{:S(2)}) collective-permute-start(bf16[512,128]{1,0:T(8,128)(2,1)S(1)} %get-tuple-element.104), channel_id=1, source_target_pairs={{0,5},{1,2},{2,7},{3,0},{4,1},{5,6},{6,3},{7,4},{8,13},{9,10},{10,... | collective-permute-start | bytes 393224 | tf_op jit(solution)/shard_map/ppermute | solution.py:413
  39.1 8.8 %collective-permute-start.26 = (bf16[512,128]{1,0:T(8,128)(2,1)S(1)}, bf16[512,128]{1,0:T(8,128)(2,1)S(1)}, u32[]{:S(2)}, u32[]{:S(2)}) collective-permute-start(bf16[512,128]{1,0:T(8,128)(2,1)S(1)} %get-tuple-element.105), channel_id=1, source_target_pairs={{0,1},{1,0},{2,3},{3,2},{4,5},{5,4},{6,7},{7,6},{8,9},{9,8},{10,11... | collective-permute-start | bytes 393224 | tf_op jit(solution)/shard_map/ppermute | solution.py:413
  40.1 7.8 %collective-permute-start.21 = (bf16[512,128]{1,0:T(8,128)(2,1)S(1)}, bf16[512,128]{1,0:T(8,128)(2,1)S(1)}, u32[]{:S(2)}, u32[]{:S(2)}) collective-permute-start(bf16[512,128]{1,0:T(8,128)(2,1)S(1)} %get-tuple-element.100), channel_id=1, source_target_pairs={{0,4},{1,3},{2,6},{3,1},{4,0},{5,7},{6,2},{7,5},{8,12},{9,11},{10,... | collective-permute-start | bytes 393224 | tf_op jit(solution)/shard_map/ppermute | solution.py:413
  41.2 6.8 %collective-permute-start.22 = (bf16[512,128]{1,0:T(8,128)(2,1)S(1)}, bf16[512,128]{1,0:T(8,128)(2,1)S(1)}, u32[]{:S(2)}, u32[]{:S(2)}) collective-permute-start(bf16[512,128]{1,0:T(8,128)(2,1)S(1)} %get-tuple-element.101), channel_id=1, source_target_pairs={{0,5},{1,2},{2,7},{3,0},{4,1},{5,6},{6,3},{7,4},{8,13},{9,10},{10,... | collective-permute-start | bytes 393224 | tf_op jit(solution)/shard_map/ppermute | solution.py:413
  42.4 5.5 %collective-permute-start.23 = (bf16[512,128]{1,0:T(8,128)(2,1)S(1)}, bf16[512,128]{1,0:T(8,128)(2,1)S(1)}, u32[]{:S(2)}, u32[]{:S(2)}) collective-permute-start(bf16[512,128]{1,0:T(8,128)(2,1)S(1)} %get-tuple-element.102), channel_id=1, source_target_pairs={{0,1},{1,0},{2,3},{3,2},{4,5},{5,4},{6,7},{7,6},{8,9},{9,8},{10,11... | collective-permute-start | bytes 393224 | tf_op jit(solution)/shard_map/ppermute | solution.py:413

commit v16 on v11

--- a/solution.py
+++ b/solution.py
@@ -15,8 +15,6 @@
 BF16 = jnp.bfloat16
 VMEM_LIMIT = 24 * 1024 * 1024
 FORWARD_PIECES = 2
-BACKWARD_PIECES = 1
-RETURN_PIECES = 2
 
 VMEM = pl.BlockSpec(memory_space=pltpu.VMEM)
 SMEM = pl.BlockSpec(memory_space=pltpu.SMEM)
@@ -136,27 +134,30 @@
                 rows[at : at + 1, :] = jnp.full((1, HD), weight, F32)
 
 
-def write_halves(full, outs, core, pair):
-    rows = full.shape[0] * pair // len(outs)
-    for piece in range(len(outs) // pair):
-        halves = row_halves(full.at[pl.ds(piece * rows, rows), :], core, pair)
-        for half, out in zip(halves, outs[piece * pair : (piece + 1) * pair]):
-            out[...] = half[...]
+def own_states(piece, grid, keys, values, live, full, outs):
+    heads = full.shape[0] // HD
+    for head in range(heads):
+        cols = head_cols(piece * heads + head)
+        masked = jnp.where(live, keys[:, cols], jnp.zeros((), BF16))
+        full[head * HD : (head + 1) * HD, :] = tn(masked, values[:, cols]).astype(BF16)
+    for half, out in zip(row_halves(full, my_place(grid)[2], grid[2]), outs):
+        out[...] = half[...]
 
 
 def state_kernel(grid, seg_len, keys_hbm, values_hbm, parent_hbm, keys, values, length, up, down, *rest):
     outs, (full, sems, parent, parent_sem) = rest[:-4], rest[-4:]
     rows, width = keys.shape
-    chunk = rows // 4 if rows % 64 == 0 else rows
+    chunk = rows // 2 if rows % 32 == 0 else rows
     steps = rows // chunk
-    spans = 2 if width % (2 * HD) == 0 else 1
+    spans = [slice(0, full.shape[0]), slice(full.shape[0], width)][:FORWARD_PIECES]
     copies = []
-    for span in range(spans):
-        cols = slice(span * width // spans, (span + 1) * width // spans)
+    for number, cols in enumerate(spans):
         for step in range(steps):
             part = slice(step * chunk, (step + 1) * chunk)
             for j, (src, dst) in enumerate(((keys_hbm, keys), (values_hbm, values))):
-                copies.append(pltpu.make_async_copy(src.at[part, cols], dst.at[part, cols], sems.at[j, span * steps + step]))
+                copies.append(
+                    pltpu.make_async_copy(src.at[part, cols], dst.at[part, cols], sems.at[j, number * steps + step])
+                )
     few = pltpu.make_async_copy(parent_hbm, parent, parent_sem)
     few.start()
     for copy in copies:
@@ -165,15 +166,16 @@
     few.wait()
     write_weights(grid, parent, up, down)
     live = lax.broadcasted_iota(jnp.int32, (rows, HD), 0) < seg_len[0]
-    for head in range(width // HD):
-        if head % (width // HD // spans) == 0:
-            span = head // (width // HD // spans)
-            for copy in copies[span * 2 * steps : (span + 1) * 2 * steps]:
-                copy.wait()
-        cols = head_cols(head)
-        masked = jnp.where(live, keys[:, cols], jnp.zeros((), BF16))
-        full[head * HD : (head + 1) * HD, :] = tn(masked, values[:, cols]).astype(BF16)
-    write_halves(full, outs, my_place(grid)[2], grid[2])
+    for copy in copies[: 2 * steps]:
+        copy.wait()
+    own_states(0, grid, keys, values, live, full, outs)
+    for copy in copies[2 * steps :]:
+        copy.wait()
+
+
+def next_state_kernel(piece, grid, length, keys, values, *rest):
+    outs, full = rest[:-1], rest[-1]
+    own_states(piece, grid, keys, values, live_rows(length, keys.shape[0]), full, outs)
 
 
 def mix_kernel(sources, first, weights, *refs):
@@ -214,11 +216,6 @@
     return parts
 
 
-def head_of(pieces, head):
-    per_piece = pieces[0].shape[1] // HD
-    return pieces[head // per_piece], head_cols(head % per_piece)
-
-
 def fetch_kernel(source, _, out, sems):
     copies = row_copies(source, out, sems)
     for copy in copies:
@@ -246,18 +243,17 @@
 
 def carry_kernel(piece, grid, counts, scale, length, queries, local, cotangent, gain, *rest):
     received, rest = rest[: sum(counts)], rest[sum(counts) :]
-    before, (attention, sums, prefix) = rest[:-3], rest[-3:]
+    before, (attention, sums, prefix) = rest[: (piece > 0)], rest[-3:]
     join_halves(split_refs(received, *counts), prefix, my_place(grid)[2], grid[2])
-    rows, width = attention.shape
+    rows, width = queries.shape[0], prefix.shape[0]
     factor = jnp.where(live_rows(length, rows), scale, 0.0)
     squares = jnp.zeros((rows, HD), F32)
     products = jnp.zeros((rows, HD), F32)
     for head in range(width // HD):
-        cols = head_cols(head)
         whole = head_cols(piece * width // HD + head)
         carried = nn(queries[:, whole], prefix[head * HD : (head + 1) * HD, :])
         out = factor * (carried + local[:, whole])
-        attention[:, cols] = out
+        attention[:, whole] = out
         squares += out * out
         products += out * (cotangent[:, whole].astype(F32) * gain[:, whole])
     both = jnp.concatenate([token_rows(squares), token_rows(products)], axis=0)
@@ -266,10 +262,9 @@
     sums[...] = both
 
 
-def grad_kernel(piece, groups, grid, scale, length, queries, cotangent, gain, *rest):
-    all_sums, attention, rest = split_refs(rest, groups, FORWARD_PIECES, len(rest) - groups - FORWARD_PIECES)
-    (grad_out, inverse_rms), halves, full = rest[:2], rest[2:-1], rest[-1]
-    rows, width = grad_out.shape
+def grad_kernel(groups, grid, scale, length, queries, cotangent, gain, attention, *rest):
+    all_sums, (grad_out, inverse_rms, *halves, full) = rest[:groups], rest[groups:]
+    rows = queries.shape[0]
     features = HEADS * HD
     total = all_sums[0][...]
     for other in all_sums[1:]:
@@ -281,16 +276,14 @@
     shrink = live_inverse * inverse * (inverse * total[1:2, :]) / features
     live_inverse = token_columns(live_inverse)
     shrink = token_columns(shrink)
-    for head in range(width // HD):
+    for head in range(queries.shape[1] // HD):
         cols = head_cols(head)
-        place = piece * width // HD + head
-        whole = head_cols(place)
-        out_piece, at = head_of(attention, place)
-        gain_grad = cotangent[:, whole].astype(F32) * gain[:, whole]
-        grad = (live_inverse * gain_grad - out_piece[:, at] * shrink).astype(BF16)
+        gain_grad = cotangent[:, cols].astype(F32) * gain[:, cols]
+        grad = (live_inverse * gain_grad - attention[:, cols] * shrink).astype(BF16)
         grad_out[:, cols] = grad
-        full[head * HD : (head + 1) * HD, :] = (scale * tn(queries[:, whole], grad)).astype(BF16)
-    write_halves(full, halves, my_place(grid)[2], grid[2])
+        full[head * HD : (head + 1) * HD, :] = (scale * tn(queries[:, cols], grad)).astype(BF16)
+    for half, out in zip(row_halves(full, my_place(grid)[2], grid[2]), halves):
+        out[...] = half[...]
 
 
 def row_copies(source, target, sems):
@@ -300,81 +293,66 @@
     return [pltpu.make_async_copy(source.at[p, :], target.at[p, :], sems.at[j]) for j, p in enumerate(parts)]
 
 
-def column_copies(sources, targets, first, count, sems):
-    cols = slice(first * HD, (first + count) * HD)
-    return [
-        pltpu.make_async_copy(src.at[:, cols], dst.at[:, cols], sems.at[j])
-        for j, (src, dst) in enumerate(zip(sources, targets))
-    ]
-
-
-def query_kernel(heads, group, scale, length, inverse_rms, gain, queries, keys, values, *rest):
-    sizes = (BACKWARD_PIECES, FORWARD_PIECES, FORWARD_PIECES)
-    grads, attention, prefix, rest = split_refs(rest, *sizes, len(rest) - sum(sizes))
-    attended_hbm, query_hbm, key_part, token, attended, query_grad, keep, keep_turned, sems = rest
+def query_kernel(heads, group, scale, length, inverse_rms, gain, queries, keys, values, grads, attention, *rest):
+    prefix, rest = split_refs(rest, FORWARD_PIECES, len(rest) - FORWARD_PIECES)
+    attended_hbm, query_hbm, key_part, token, attended, query_grad, keep, sems = rest
     token[...] = jnp.zeros_like(token)
     write_mask(length, keep, False)
-    write_mask(length, keep_turned, True)
     inverse = token_columns(inverse_rms[...])
     copies = []
     for head in range(heads):
         cols = head_cols(head)
-        grad_piece, at = head_of(grads, head)
-        grad = grad_piece[:, at]
-        out_piece, at = head_of(attention, head)
+        grad = grads[:, cols]
         per_piece = heads // FORWARD_PIECES
         prefix_piece, state = prefix[head // per_piece], head % per_piece
         grad_scores = nt(grad, values[:, cols]).astype(BF16) * keep[...]
         carried = nt(grad, prefix_piece[state * HD : (state + 1) * HD, :])
         query_grad[:, cols] = (scale * (carried + nn(grad_scores, keys[:, cols]))).astype(BF16)
-        turned = nt(values[:, cols], grad).astype(BF16) * keep_turned[...]
-        key_part[:, cols] = scale * nn(turned, queries[:, cols])
-        attended[:, cols] = (out_piece[:, at] * inverse * gain[:, cols]).astype(BF16)
+        key_part[:, cols] = scale * tn(grad_scores, queries[:, cols])
+        attended[:, cols] = (attention[:, cols] * inverse * gain[:, cols]).astype(BF16)
         if (head + 1) % group == 0:
             step = head // group
-            some = column_copies(
-                (attended, query_grad), (attended_hbm, query_hbm), step * group, group, sems.at[step]
-            )
-            for copy in some:
+            done = slice(step * group * HD, (head + 1) * HD)
+            for j, (src, dst) in enumerate(((attended, attended_hbm), (query_grad, query_hbm))):
+                copy = pltpu.make_async_copy(src.at[:, done], dst.at[:, done], sems.at[step, j])
                 copy.start()
-            copies += some
+                copies.append(copy)
     for copy in copies:
         copy.wait()
 
 
-def value_kernel(heads, scale, length, queries, keys, *rest):
-    grads, (value_part, keep) = rest[:BACKWARD_PIECES], rest[-2:]
+def value_kernel(heads, scale, length, queries, keys, grads, *rest):
+    value_part, keep = rest[-2:]
     write_mask(length, keep, True)
     for head in range(heads):
         cols = head_cols(head)
-        grad_piece, at = head_of(grads, head)
         turned = nt(keys[:, cols], queries[:, cols]).astype(BF16) * keep[...]
-        value_part[:, cols] = scale * nn(turned, grad_piece[:, at])
-
-
-def final_kernel(piece, grid, counts, length, keys, values, key_part, value_part, *rest):
+        value_part[:, cols] = scale * nn(turned, grads[:, cols])
+
+
+def final_kernel(begin, count, grid, counts, length, keys, values, key_part, value_part, *rest):
     received, rest = rest[: sum(counts)], rest[sum(counts) :]
     key_hbm, value_hbm, key_grad, value_grad, below, sems = rest[-6:]
     pair = grid[2]
     join_halves(split_refs(received, *counts), below, my_place(grid)[2], pair)
-    rows, width = key_grad.shape
+    rows = keys.shape[0]
     live = jnp.where(live_rows(length, rows), 1.0, 0.0)
-    per_half = width // HD // pair
-    group = 2 if per_half % 2 == 0 else 1
-    copies = []
-    for head in range(width // HD):
-        half, within = head // per_half, head % per_half
+    copies, pending = [], 0
+    for head in range(pair * count):
+        half, within = divmod(head, count)
         cols = head_cols(head)
-        place = half * (keys.shape[1] // HD // pair) + piece * per_half + within
+        place = half * (keys.shape[1] // HD // pair) + begin + within
         whole = head_cols(place)
         state = below[head * HD : (head + 1) * HD, :]
         key_grad[:, cols] = (key_part[:, whole] + live * nt(values[:, whole], state)).astype(BF16)
         value_grad[:, cols] = (value_part[:, whole] + live * nn(keys[:, whole], state)).astype(BF16)
-        if (head + 1) % group == 0:
-            done = slice((head + 1 - group) * HD, (head + 1) * HD)
-            there = slice((place + 1 - group) * HD, (place + 1) * HD)
+        pending += 1
+        if pending == 2 or within == count - 1:
+            done = slice((head + 1 - pending) * HD, (head + 1) * HD)
+            there = slice((place + 1 - pending) * HD, (place + 1) * HD)
+            pending = 0
             for j, (src, dst) in enumerate(((key_grad, key_hbm), (value_grad, value_hbm))):
-                copy = pltpu.make_async_copy(src.at[:, done], dst.at[:, there], sems.at[j, head // group])
+                copy = pltpu.make_async_copy(src.at[:, done], dst.at[:, there], sems.at[j, head])
                 copy.start()
                 copies.append(copy)
     for copy in copies:
@@ -465,25 +443,30 @@
     def halves(pieces):
         return [shape((features // (pair * pieces), HD), BF16)] * pair
 
-    def mix(arrived, weights, piece, pieces, after=()):
-        tall = arrived[0].shape[0] // pieces
+    def mix(arrived, weights, first, tall, after=()):
         like = [shape((tall, HD), BF16)] * members
-        return call(functools.partial(mix_kernel, members, piece * tall), like, (weights, *arrived), after=after)
+        return call(functools.partial(mix_kernel, members, first), like, (weights, *arrived), after=after)
 
     def flat(parts):
         return [block for part in parts for block in part]
 
+    state_scratch = pltpu.VMEM((features // FORWARD_PIECES, HD), BF16)
     key, value, length, up, down, *own = call(
         functools.partial(state_kernel, grid),
-        [narrow, narrow, shape((1, rows), jnp.int32), weight_rows, weight_rows] + halves(FORWARD_PIECES) * FORWARD_PIECES,
+        [narrow, narrow, shape((1, rows), jnp.int32), weight_rows, weight_rows] + halves(FORWARD_PIECES),
         (seg_len, key_rows[0], values[0], parent[None]),
-        [pltpu.VMEM((features, HD), BF16), sems, pltpu.SMEM((1, segs), jnp.int32), pltpu.SemaphoreType.DMA(())],
-        unit * HD, (1, 2, 3), (0,),
-    )
+        [state_scratch, sems, pltpu.SMEM((1, segs), jnp.int32), pltpu.SemaphoreType.DMA(())],
+        unit * HD // FORWARD_PIECES, (1, 2, 3), (0,),
+    )
+    for piece in range(1, FORWARD_PIECES):
+        own += call(
+            functools.partial(next_state_kernel, piece, grid), halves(FORWARD_PIECES),
+            (length, key, value), [state_scratch], unit * HD // FORWARD_PIECES,
+        )
     (query,) = call(fetch_kernel, [narrow], (queries[0],), [pltpu.SemaphoreType.DMA((4,))], 0, (0,), after=(own[0],))
     mixed = []
     for part in split_refs(own, *[pair] * FORWARD_PIECES):
-        mixed.append(mix(gather_line(part, grid), up, 0, 1, () if mixed else (query,)))
+        mixed.append(mix(gather_line(part, grid), up, 0, part[0].shape[0], () if mixed else (query,)))
     (local,) = call(
         functools.partial(local_kernel, heads),
         [wide], (length, query, key, value), [mask], unit * rows * 2, after=(mixed[0][0],),
@@ -491,55 +474,53 @@
     attention, prefix, sums = [], [], []
     width = features // FORWARD_PIECES
     for piece in range(FORWARD_PIECES):
+        blocks = flat(scatter_line(mixed[piece], grid))
+        operands = (length, query, local, cot, gain, *blocks, *sums, *attention)
         out, total, joined = call(
             functools.partial(carry_kernel, piece, grid, counts, scale),
-            [shape((rows, width), F32), shape((2, rows), F32), shape((width, HD), BF16)],
-            (length, query, local, cot, gain, *flat(scatter_line(mixed[piece], grid)), *sums),
-            (), unit * HD // FORWARD_PIECES,
+            [wide, shape((2, rows), F32), shape((width, HD), BF16)], operands,
+            (), unit * HD // FORWARD_PIECES, aliases={len(operands) - 1: 0} if attention else None,
         )
-        attention.append(out)
+        attention, sums = [out], [total]
         prefix.append(joined)
-        sums = [total]
+    (attention,) = attention
     sums = token_sums(sums[0], groups)
-    grads, state_grad = [], []
-    width = features // BACKWARD_PIECES
-    for piece in range(BACKWARD_PIECES):
-        grad_out, inverse_rms, *parts = call(
-            functools.partial(grad_kernel, piece, len(sums), grid, scale),
-            [shape((rows, width), BF16), row] + halves(BACKWARD_PIECES),
-            (length, query, cot, gain, *sums, *attention), [pltpu.VMEM((width, HD), BF16)],
-            unit * HD // BACKWARD_PIECES,
-        )
-        grads.append(grad_out)
-        state_grad.append(parts)
+    grads, inverse_rms, *state_grad = call(
+        functools.partial(grad_kernel, len(sums), grid, scale),
+        [narrow, row] + halves(1), (length, query, cot, gain, attention, *sums),
+        [pltpu.VMEM((features, HD), BF16)], unit * HD,
+    )
     group = 4 if heads % 4 == 0 else 1
     attended, query_grad, key_part, token = call(
         functools.partial(query_kernel, heads, group, scale),
         [narrow, narrow, wide, shape((8, HD), F32)],
-        (length, inverse_rms, gain, query, key, value, *grads, *attention, *prefix),
-        [pltpu.VMEM(narrow.shape, BF16)] * 2 + [mask] * 2 + [pltpu.SemaphoreType.DMA((heads // group, 2))],
-        unit * (4 * rows + HD), out_specs=[HBM, HBM, VMEM, VMEM],
-    )
-    (part,) = state_grad
-    arrived = gather_line(part, grid)
+        (length, inverse_rms, gain, query, key, value, grads, attention, *prefix),
+        [pltpu.VMEM(narrow.shape, BF16)] * 2 + [mask, pltpu.SemaphoreType.DMA((heads // group, 2))],
+        unit * (3 * rows + HD), out_specs=[HBM, HBM, VMEM, VMEM],
+    )
+    arrived = gather_line(state_grad, grid)
+    half_heads = heads // pair
+    last = max(half_heads * 3 // 8, min(half_heads - 1, 1))
+    pieces = [(0, half_heads - last), (half_heads - last, last)] if last else [(0, half_heads)]
     mixed = []
-    for piece in range(RETURN_PIECES):
-        mixed.append(mix(arrived, down, piece, RETURN_PIECES, (token, *mixed[-1][:1]) if mixed else (token,)))
+    for begin, count in pieces:
+        before = (token, *mixed[-1][:1]) if mixed else (token,)
+        mixed.append(mix(arrived, down, begin * HD, count * HD, before))
     (value_part,) = call(
         functools.partial(value_kernel, heads, scale),
-        [wide], (length, query, key, *grads), [mask], unit * 2 * rows, after=(mixed[-1][0],),
+        [wide], (length, query, key, grads), [mask], unit * 2 * rows, after=(mixed[-1][0],),
     )
     results = []
-    width = features // RETURN_PIECES
-    for piece in range(RETURN_PIECES):
-        below = flat(scatter_line(mixed[piece], grid))
+    for (begin, count), sums in zip(pieces, mixed):
+        below = flat(scatter_line(sums, grid))
         operands = (length, key, value, key_part, value_part, *below, *results)
         first = len(operands) - len(results)
+        width = pair * count * HD
         results = call(
-            functools.partial(final_kernel, piece, grid, counts),
+            functools.partial(final_kernel, begin, count, grid, counts),
             [narrow, narrow], operands,
             [pltpu.VMEM((rows, width), BF16)] * 2 + [pltpu.VMEM((width, HD), BF16), sems],
-            2 * unit * HD // RETURN_PIECES,
+            2 * unit * HD * pair * count // heads,
             range(first, len(operands)), out_specs=[HBM, HBM],
             aliases={first + j: j for j in range(len(results))},
         )

time: 50.1 us -> 49.6 us (0.990)
  waiting for transfers between devices: 9.15 us -> 8.3 us
  starting transfers between devices: 20.8 us -> 21.5 us
    ppermute x21, waiting for transfers between devices: 5.35 us -> 4.49 us  [line_send(): return lax.ppermute(block, 'seg', moves)]
    ppermute x21, starting transfers between devices: 16.5 us -> 17.3 us  [line_send(): return lax.ppermute(block, 'seg', moves)]
    pallas_call x14 -> x15, Pallas kernels: 18.4 us -> 17.9 us  [call(): pl.pallas_call(kernel, out_shape=out_shape, in_specs=specs + [ANY] * len(...]
  transfers between devices with their start and end apart: 24 -> 24, of which waited for: 10 -> 7; matrix products, arithmetic and copies ran while one was open for 0% -> 0% of each run, Pallas kernels for 25% -> 25%
where the time goes in v16:
time: 49.6 us; the launch traced here: 49.3 us
  starting transfers between devices  21.5 us (43%)
  Pallas kernels  17.9 us (36%)
  waiting for transfers between devices  8.3 us (17%)
  between operations  1.64 us (3%)
    pallas_call x15, Pallas kernels, call(): pl.pallas_call(kernel, out_shape=out_shape, in_specs=specs + [ANY] * len(...  17.9 us
    ppermute x21, starting transfers between devices, line_send(): return lax.ppermute(block, 'seg', moves)  17.3 us
    ppermute x21, waiting for transfers between devices, line_send(): return lax.ppermute(block, 'seg', moves)  4.49 us
    ppermute x3, starting transfers between devices, token_sums(): parts.append(lax.ppermute(sums, 'head', moves))  4.22 us
    ppermute x3, waiting for transfers between devices, token_sums(): parts.append(lax.ppermute(sums, 'head', moves))  3.82 us
  transfers between devices with their start and end apart: 24, of which 7 were waited for; matrix products, arithmetic and copies ran while one was open for 0% of the time, Pallas kernels for 25%

profile of v16, /device:TPU:0, one launch (start us, length us, event | category | flops | bytes accessed | tf_op | source)
XLA Modules:
  0.0 49.3 jit_solution(16372849509512046831)
XLA Ops:
  1.3 1.9 %shard_map.102 = (bf16[256,2048]{1,0:T(8,128)(2,1)S(1)}, bf16[256,2048]{1,0:T(8,128)(2,1)S(1)}, s32[1,256]{1,0:T(1,128)S(1)}, f32[16,128]{1,0:T(8,128)S(1)}, f32...) custom-call(s32[1]{0:T(128)S(6)} %copy.17.seg_len, bf16[256,2048]{1,0:T(8,128)(2,1)} %bitcast.20, ...), custom_call_target="tpu_custom_call" | custom-call | flops 67108864 | bytes 4473892 | tf_op jit(solution)/shard_map/pallas_call | solution.py:371
  3.2 2.5 %collective-permute-start.2 = (bf16[512,128]{1,0:T(8,128)(2,1)S(1)}, bf16[512,128]{1,0:T(8,128)(2,1)S(1)}, u32[]{:S(2)}, u32[]{:S(2)}) collective-permute-start(bf16[512,128]{1,0:T(8,128)(2,1)S(1)} %get-tuple-element.52), channel_id=1, source_target_pairs={{0,5},{1,2},{2,7},{3,0},{4,1},{5,6},{6,3},{7,4},{8,13},{9,10},{10,... | collective-permute-start | bytes 393224 | tf_op jit(solution)/shard_map/ppermute | solution.py:393
  5.6 0.6 %collective-permute-start = (bf16[512,128]{1,0:T(8,128)(2,1)S(1)}, bf16[512,128]{1,0:T(8,128)(2,1)S(1)}, u32[]{:S(2)}, u32[]{:S(2)}) collective-permute-start(bf16[512,128]{1,0:T(8,128)(2,1)S(1)} %get-tuple-element.52), channel_id=1, source_target_pairs={{0,1},{1,0},{2,3},{3,2},{4,5},{5,4},{6,7},{7,6},{8,9},{9,8},{10,11... | collective-permute-start | bytes 393224 | tf_op jit(solution)/shard_map/ppermute | solution.py:393
  6.3 0.9 %collective-permute-start.1 = (bf16[512,128]{1,0:T(8,128)(2,1)S(1)}, bf16[512,128]{1,0:T(8,128)(2,1)S(1)}, u32[]{:S(2)}, u32[]{:S(2)}) collective-permute-start(bf16[512,128]{1,0:T(8,128)(2,1)S(1)} %get-tuple-element.48._.refs_0_), channel_id=1, source_target_pairs={{0,2},{1,5},{2,0},{3,7},{4,6},{5,1},{6,4},{7,3},{8,10},{9,13},{10,... | collective-permute-start | bytes 393224 | tf_op jit(solution)/shard_map/ppermute | solution.py:393
  7.1 0.4 shard_map.106
  7.5 1.2 %collective-permute-start.4 = (bf16[512,128]{1,0:T(8,128)(2,1)S(1)}, bf16[512,128]{1,0:T(8,128)(2,1)S(1)}, u32[]{:S(2)}, u32[]{:S(2)}) collective-permute-start(bf16[512,128]{1,0:T(8,128)(2,1)S(1)} %get-tuple-element.54.refs_0_), channel_id=1, source_target_pairs={{0,2},{1,5},{2,0},{3,7},{4,6},{5,1},{6,4},{7,3},{8,10},{9,13},{10,... | collective-permute-start | bytes 393224 | tf_op jit(solution)/shard_map/ppermute | solution.py:393
  8.7 0.6 %collective-permute-start.5 = (bf16[512,128]{1,0:T(8,128)(2,1)S(1)}, bf16[512,128]{1,0:T(8,128)(2,1)S(1)}, u32[]{:S(2)}, u32[]{:S(2)}) collective-permute-start(bf16[512,128]{1,0:T(8,128)(2,1)S(1)} %get-tuple-element.55), channel_id=1, source_target_pairs={{0,5},{1,2},{2,7},{3,0},{4,1},{5,6},{6,3},{7,4},{8,13},{9,10},{10,... | collective-permute-start | bytes 393224 | tf_op jit(solution)/shard_map/ppermute | solution.py:393
  9.3 1.2 %shard_map.103.refs_4_.queries = bf16[256,2048]{1,0:T(8,128)(2,1)S(1)} custom-call(bf16[256,2048]{1,0:T(8,128)(2,1)} %bitcast.19, bf16[512,128]{1,0:T(8,128)(2,1)S(1)} %get-tuple-element.48._.refs_0_), custom_call_target="tpu_custom_call" | custom-call | bytes 2097152 | tf_op jit(solution)/shard_map/pallas_call | solution.py:371
  10.6 0.0 collective-permute-done.2.refs_3_
  10.6 0.5 collective-permute-start.3
  11.0 0.0 collective-permute-done.refs_1_
  11.0 0.2 collective-permute-done.1.refs_2_
  11.2 0.3 shard_map.104
  11.5 1.6 %collective-permute-start.9 = (bf16[512,128]{1,0:T(8,128)(2,1)S(1)}, bf16[512,128]{1,0:T(8,128)(2,1)S(1)}, u32[]{:S(2)}, u32[]{:S(2)}) collective-permute-start(bf16[512,128]{1,0:T(8,128)(2,1)S(1)} %get-tuple-element.60), channel_id=1, source_target_pairs={{0,4},{1,3},{2,6},{3,1},{4,0},{5,7},{6,2},{7,5},{8,12},{9,11},{10,... | collective-permute-start | bytes 393224 | tf_op jit(solution)/shard_map/ppermute | solution.py:393
  13.1 0.3 collective-permute-start.10
  13.4 0.0 collective-permute-done.4.refs_2_
  13.5 0.7 %collective-permute-start.11 = (bf16[512,128]{1,0:T(8,128)(2,1)S(1)}, bf16[512,128]{1,0:T(8,128)(2,1)S(1)}, u32[]{:S(2)}, u32[]{:S(2)}) collective-permute-start(bf16[512,128]{1,0:T(8,128)(2,1)S(1)} %get-tuple-element.62), channel_id=1, source_target_pairs={{0,1},{1,0},{2,3},{3,2},{4,5},{5,4},{6,7},{7,6},{8,9},{9,8},{10,11... | collective-permute-start | bytes 393224 | tf_op jit(solution)/shard_map/ppermute | solution.py:393
  14.2 0.0 collective-permute-done.5.refs_3_
  14.2 0.0 collective-permute-done.3.refs_1_
  14.2 0.3 shard_map.107
  14.5 1.4 %collective-permute-start.6 = (bf16[512,128]{1,0:T(8,128)(2,1)S(1)}, bf16[512,128]{1,0:T(8,128)(2,1)S(1)}, u32[]{:S(2)}, u32[]{:S(2)}) collective-permute-start(bf16[512,128]{1,0:T(8,128)(2,1)S(1)} %get-tuple-element.56), channel_id=1, source_target_pairs={{0,4},{1,3},{2,6},{3,1},{4,0},{5,7},{6,2},{7,5},{8,12},{9,11},{10,... | collective-permute-start | bytes 393224 | tf_op jit(solution)/shard_map/ppermute | solution.py:393
  15.9 0.9 %collective-permute-start.7 = (bf16[512,128]{1,0:T(8,128)(2,1)S(1)}, bf16[512,128]{1,0:T(8,128)(2,1)S(1)}, u32[]{:S(2)}, u32[]{:S(2)}) collective-permute-start(bf16[512,128]{1,0:T(8,128)(2,1)S(1)} %get-tuple-element.58), channel_id=1, source_target_pairs={{0,5},{1,2},{2,7},{3,0},{4,1},{5,6},{6,3},{7,4},{8,13},{9,10},{10,... | collective-permute-start | bytes 393224 | tf_op jit(solution)/shard_map/ppermute | solution.py:393
  16.8 0.0 collective-permute-done.9.rest_0_
  16.8 0.3 collective-permute-start.8
  17.1 1.5 %shard_map.105.local = f32[256,2048]{1,0:T(8,128)S(1)} custom-call(s32[1,256]{1,0:T(1,128)S(1)} %get-tuple-element.47.length, bf16[256,2048]{1,0:T(8,128)(2,1)S(1)} %shard_map.103.refs_4_.queries, bf16[256,2048]{1,0:T(8,128)(2,1)S(1)} %get-tuple-element.49.keys, bf16[256,2048]{1,0:T(8,128)(2,1)S(1)} %get-tuple-element.50.values, ...), custom_call_target="tpu_custom_call" | custom-call | flops 536870912 | bytes 5243904 | tf_op jit(solution)/shard_map/pallas_call | solution.py:371
  18.6 0.0 collective-permute-done.10.rest_2_
  18.6 0.0 collective-permute-done.11.rest_3_
  18.6 0.0 copy-done
  18.6 0.7 %shard_map.108 = (f32[256,2048]{1,0:T(8,128)S(1)}, f32[2,256]{1,0:T(2,128)S(1)}, bf16[1024,128]{1,0:T(8,128)(2,1)S(1)}) custom-call(s32[1,256]{1,0:T(1,128)S(1)} %get-tuple-element.47.length, bf16[256,2048]{1,0:T(8,128)(2,1)S(1)} %shard_map.103.refs_4_.queries, f32[256,2048]{1,0:T(8,128)S(1)} %shard_map.105.local, bf16[256,2048]{1,0:T(8,128)(2,1)S(1)} %bitcast.10, ...), custom_call_target="tpu_custom_call" | custom-call | flops 67108864 | bytes 7089152 | tf_op jit(solution)/shard_map/pallas_call | solution.py:371
  19.3 0.2 collective-permute-done.6.rest_0_
  19.5 0.8 %collective-permute-done.7.rest_2_ = bf16[512,128]{1,0:T(8,128)(2,1)S(1)} collective-permute-done((bf16[512,128]{1,0:T(8,128)(2,1)S(1)}, bf16[512,128]{1,0:T(8,128)(2,1)S(1)}, u32[]{:S(2)}, u32[]{:S(2)}) %collective-permute-start.7) | collective-permute-done | bytes 131104 | tf_op jit(solution)/shard_map/ppermute | solution.py:393
  20.3 0.0 collective-permute-done.8.rest_3_
  20.3 0.7 %shard_map.109 = (f32[256,2048]{1,0:T(8,128)S(1)}, f32[2,256]{1,0:T(2,128)S(1)}, bf16[1024,128]{1,0:T(8,128)(2,1)S(1)}) custom-call(s32[1,256]{1,0:T(1,128)S(1)} %get-tuple-element.47.length, bf16[256,2048]{1,0:T(8,128)(2,1)S(1)} %shard_map.103.refs_4_.queries, f32[256,2048]{1,0:T(8,128)S(1)} %shard_map.105.local, ...), custom_call_target="tpu_custom_call", output_to_operand_aliasing={{0}: (10, {})} | custom-call | flops 67108864 | bytes 9188352 | tf_op jit(solution)/shard_map/pallas_call | solution.py:371
  21.0 2.7 %collective-permute-start.14 = (f32[2,256]{1,0:T(2,128)S(1)}, f32[2,256]{1,0:T(2,128)S(1)}, u32[]{:S(2)}, u32[]{:S(2)}) collective-permute-start(f32[2,256]{1,0:T(2,128)S(1)} %get-tuple-element.66.rest_0_), channel_id=1, source_target_pairs={{0,16},{8,24},{16,0},{24,8},{1,17},{9,25},{17,1},{25,9},{2,18},{10... | collective-permute-start | bytes 6152 | tf_op jit(solution)/shard_map/ppermute | solution.py:420
  23.6 1.3 %collective-permute-start.13 = (f32[2,256]{1,0:T(2,128)S(1)}, f32[2,256]{1,0:T(2,128)S(1)}, u32[]{:S(2)}, u32[]{:S(2)}) collective-permute-start(f32[2,256]{1,0:T(2,128)S(1)} %get-tuple-element.66.rest_0_), channel_id=1, source_target_pairs={{0,24},{8,16},{16,8},{24,0},{1,25},{9,17},{17,9},{25,1},{2,26},{10... | collective-permute-start | bytes 6152 | tf_op jit(solution)/shard_map/ppermute | solution.py:420
  25.0 0.2 collective-permute-start.12
  25.2 0.3 collective-permute-done.14.rest_3_
  25.5 3.5 %collective-permute-done.13.rest_2_ = f32[2,256]{1,0:T(2,128)S(1)} collective-permute-done((f32[2,256]{1,0:T(2,128)S(1)}, f32[2,256]{1,0:T(2,128)S(1)}, u32[]{:S(2)}, u32[]{:S(2)}) %collective-permute-start.13) | collective-permute-done | bytes 2080 | tf_op jit(solution)/shard_map/ppermute | solution.py:420
  29.0 0.0 collective-permute-done.12.rest_1_
  29.0 1.0 %shard_map.110 = (bf16[256,2048]{1,0:T(8,128)(2,1)S(1)}, f32[1,256]{1,0:T(1,128)S(1)}, bf16[1024,128]{1,0:T(8,128)(2,1)S(1)}, bf16[1024,128]{1,0:T(8,128)(2,1)S(1)}) custom-call(s32[1,256]{1,0:T(1,128)S(1)} %get-tuple-element.47.length, bf16[256,2048]{1,0:T(8,128)(2,1)S(1)} %shard_map.103.refs_4_.queries, bf16[256,2048]{1,0:T(8,128)(2,1)S(1)} %bitcast.12, ...), custom_call_target="tpu_custom_call" | custom-call | flops 134217728 | bytes 5785600 | tf_op jit(solution)/shard_map/pallas_call | solution.py:371
  30.1 0.1 collective-permute-start.17
  30.2 1.1 %collective-permute-start.15 = (bf16[1024,128]{1,0:T(8,128)(2,1)S(1)}, bf16[1024,128]{1,0:T(8,128)(2,1)S(1)}, u32[]{:S(2)}, u32[]{:S(2)}) collective-permute-start(bf16[1024,128]{1,0:T(8,128)(2,1)S(1)} %get-tuple-element.76), channel_id=1, source_target_pairs={{0,1},{1,0},{2,3},{3,2},{4,5},{5,4},{6,7},{7,6},{8,9},{9,8},{10,11... | collective-permute-start | bytes 786440 | tf_op jit(solution)/shard_map/ppermute | solution.py:393
  31.3 1.0 %collective-permute-start.16 = (bf16[1024,128]{1,0:T(8,128)(2,1)S(1)}, bf16[1024,128]{1,0:T(8,128)(2,1)S(1)}, u32[]{:S(2)}, u32[]{:S(2)}) collective-permute-start(bf16[1024,128]{1,0:T(8,128)(2,1)S(1)} %get-tuple-element.75.refs_0_), channel_id=1, source_target_pairs={{0,2},{1,5},{2,0},{3,7},{4,6},{5,1},{6,4},{7,3},{8,10},{9,13},{10,... | collective-permute-start | bytes 786440 | tf_op jit(solution)/shard_map/ppermute | solution.py:393
  32.3 4.8 %shard_map.111 = (bf16[256,2048]{1,0:T(8,128)(2,1)}, bf16[256,2048]{1,0:T(8,128)(2,1)}, f32[256,2048]{1,0:T(8,128)S(1)}, f32[8,128]{1,0:T(8,128)S(1)}) custom-call(s32[1,256]{1,0:T(1,128)S(1)} %get-tuple-element.47.length, f32[1,256]{1,0:T(1,128)S(1)} %get-tuple-element.67.inverse_rms, f32[1,2048]{1,0:T(1,128)S(1)} %bitcast.16, ...), custom_call_target="tpu_custom_call" | custom-call | flops 939524096 | bytes 11024384 | tf_op jit(solution)/shard_map/pallas_call | solution.py:371
  37.1 0.0 collective-permute-done.17.refs_3_
  37.1 0.0 collective-permute-done.15.refs_1_
  37.1 1.6 %collective-permute-done.16.refs_2_ = bf16[1024,128]{1,0:T(8,128)(2,1)S(1)} collective-permute-done((bf16[1024,128]{1,0:T(8,128)(2,1)S(1)}, bf16[1024,128]{1,0:T(8,128)(2,1)S(1)}, u32[]{:S(2)}, u32[]{:S(2)}) %collective-permute-start.16) | collective-permute-done | bytes 262176 | tf_op jit(solution)/shard_map/ppermute | solution.py:393
  38.7 0.4 shard_map.112
  39.1 1.0 %collective-permute-start.21 = (bf16[640,128]{1,0:T(8,128)(2,1)S(1)}, bf16[640,128]{1,0:T(8,128)(2,1)S(1)}, u32[]{:S(2)}, u32[]{:S(2)}) collective-permute-start(bf16[640,128]{1,0:T(8,128)(2,1)S(1)} %get-tuple-element.83), channel_id=1, source_target_pairs={{0,4},{1,3},{2,6},{3,1},{4,0},{5,7},{6,2},{7,5},{8,12},{9,11},{10,... | collective-permute-start | bytes 491528 | tf_op jit(solution)/shard_map/ppermute | solution.py:393
  40.1 0.1 collective-permute-start.22
  40.2 1.6 %collective-permute-start.23 = (bf16[640,128]{1,0:T(8,128)(2,1)S(1)}, bf16[640,128]{1,0:T(8,128)(2,1)S(1)}, u32[]{:S(2)}, u32[]{:S(2)}) collective-permute-start(bf16[640,128]{1,0:T(8,128)(2,1)S(1)} %get-tuple-element.85), channel_id=1, source_target_pairs={{0,1},{1,0},{2,3},{3,2},{4,5},{5,4},{6,7},{7,6},{8,9},{9,8},{10,11... | collective-permute-start | bytes 491528 | tf_op jit(solution)/shard_map/ppermute | solution.py:393
  41.8 0.2 shard_map.113
  42.1 0.6 %collective-permute-start.18 = (bf16[384,128]{1,0:T(8,128)(2,1)S(1)}, bf16[384,128]{1,0:T(8,128)(2,1)S(1)}, u32[]{:S(2)}, u32[]{:S(2)}) collective-permute-start(bf16[384,128]{1,0:T(8,128)(2,1)S(1)} %get-tuple-element.80), channel_id=1, source_target_pairs={{0,4},{1,3},{2,6},{3,1},{4,0},{5,7},{6,2},{7,5},{8,12},{9,11},{10,... | collective-permute-start | bytes 294920 | tf_op jit(solution)/shard_map/ppermute | solution.py:393
  42.6 0.3 collective-permute-start.19
  43.0 1.5 %collective-permute-done.21.rest_0_ = bf16[640,128]{1,0:T(8,128)(2,1)S(1)} collective-permute-done((bf16[640,128]{1,0:T(8,128)(2,1)S(1)}, bf16[640,128]{1,0:T(8,128)(2,1)S(1)}, u32[]{:S(2)}, u32[]{:S(2)}) %collective-permute-start.21) | collective-permute-done | bytes 163872 | tf_op jit(solution)/shard_map/ppermute | solution.py:393
  44.5 0.0 collective-permute-start.20
  44.5 1.5 %shard_map.114.value_part = f32[256,2048]{1,0:T(8,128)S(1)} custom-call(s32[1,256]{1,0:T(1,128)S(1)} %get-tuple-element.47.length, bf16[256,2048]{1,0:T(8,128)(2,1)S(1)} %shard_map.103.refs_4_.queries, bf16[256,2048]{1,0:T(8,128)(2,1)S(1)} %get-tuple-element.49.keys, bf16[256,2048]{1,0:T(8,128)(2,1)S(1)} %get-tuple-element.68.grads, ...), custom_call_target="tpu_custom_call" | custom-call | flops 536870912 | bytes 5243904 | tf_op jit(solution)/shard_map/pallas_call | solution.py:371
  46.0 0.0 collective-permute-done.22.rest_2_
  46.0 0.0 collective-permute-done.23.rest_3_
  46.0 1.7 %shard_map.115 = (bf16[256,2048]{1,0:T(8,128)(2,1)}, bf16[256,2048]{1,0:T(8,128)(2,1)}) custom-call(s32[1,256]{1,0:T(1,128)S(1)} %get-tuple-element.47.length, bf16[256,2048]{1,0:T(8,128)(2,1)S(1)} %get-tuple-element.49.keys, bf16[256,2048]{1,0:T(8,128)(2,1)S(1)} %get-tuple-element.50.values, f32[256,2048]{1,0:T(8,128)S(1)} %get-tuple-element.73.key_part, ...), custom_call_target="tpu_custom_call" | custom-call | flops 167772160 | bytes 9044992 | tf_op jit(solution)/shard_map/pallas_call | solution.py:371
  47.7 0.0 collective-permute-done.18.rest_0_
  47.7 0.0 collective-permute-done.19.rest_2_
  47.7 0.0 collective-permute-done.20.rest_3_
  47.7 1.4 %shard_map.116 = (bf16[256,2048]{1,0:T(8,128)(2,1)}, bf16[256,2048]{1,0:T(8,128)(2,1)}) custom-call(s32[1,256]{1,0:T(1,128)S(1)} %get-tuple-element.47.length, bf16[256,2048]{1,0:T(8,128)(2,1)S(1)} %get-tuple-element.49.keys, bf16[256,2048]{1,0:T(8,128)(2,1)S(1)} %get-tuple-element.50.values, ...), custom_call_target="tpu_custom_call", output_to_operand_aliasing={{0}: (9, {}), {1}: (10, {})} | custom-call | flops 100663296 | bytes 10880000 | tf_op jit(solution)/shard_map/pallas_call | solution.py:371
  (3 shorter events, 0.0 us)
Async XLA Ops:
  3.2 7.4 %collective-permute-start.2 = (bf16[512,128]{1,0:T(8,128)(2,1)S(1)}, bf16[512,128]{1,0:T(8,128)(2,1)S(1)}, u32[]{:S(2)}, u32[]{:S(2)}) collective-permute-start(bf16[512,128]{1,0:T(8,128)(2,1)S(1)} %get-tuple-element.52), channel_id=1, source_target_pairs={{0,5},{1,2},{2,7},{3,0},{4,1},{5,6},{6,3},{7,4},{8,13},{9,10},{10,... | collective-permute-start | bytes 393224 | tf_op jit(solution)/shard_map/ppermute | solution.py:393
  5.6 5.4 %collective-permute-start = (bf16[512,128]{1,0:T(8,128)(2,1)S(1)}, bf16[512,128]{1,0:T(8,128)(2,1)S(1)}, u32[]{:S(2)}, u32[]{:S(2)}) collective-permute-start(bf16[512,128]{1,0:T(8,128)(2,1)S(1)} %get-tuple-element.52), channel_id=1, source_target_pairs={{0,1},{1,0},{2,3},{3,2},{4,5},{5,4},{6,7},{7,6},{8,9},{9,8},{10,11... | collective-permute-start | bytes 393224 | tf_op jit(solution)/shard_map/ppermute | solution.py:393
  6.3 5.0 %collective-permute-start.1 = (bf16[512,128]{1,0:T(8,128)(2,1)S(1)}, bf16[512,128]{1,0:T(8,128)(2,1)S(1)}, u32[]{:S(2)}, u32[]{:S(2)}) collective-permute-start(bf16[512,128]{1,0:T(8,128)(2,1)S(1)} %get-tuple-element.48._.refs_0_), channel_id=1, source_target_pairs={{0,2},{1,5},{2,0},{3,7},{4,6},{5,1},{6,4},{7,3},{8,10},{9,13},{10,... | collective-permute-start | bytes 393224 | tf_op jit(solution)/shard_map/ppermute | solution.py:393
  7.5 6.0 %collective-permute-start.4 = (bf16[512,128]{1,0:T(8,128)(2,1)S(1)}, bf16[512,128]{1,0:T(8,128)(2,1)S(1)}, u32[]{:S(2)}, u32[]{:S(2)}) collective-permute-start(bf16[512,128]{1,0:T(8,128)(2,1)S(1)} %get-tuple-element.54.refs_0_), channel_id=1, source_target_pairs={{0,2},{1,5},{2,0},{3,7},{4,6},{5,1},{6,4},{7,3},{8,10},{9,13},{10,... | collective-permute-start | bytes 393224 | tf_op jit(solution)/shard_map/ppermute | solution.py:393
  8.7 5.5 %collective-permute-start.5 = (bf16[512,128]{1,0:T(8,128)(2,1)S(1)}, bf16[512,128]{1,0:T(8,128)(2,1)S(1)}, u32[]{:S(2)}, u32[]{:S(2)}) collective-permute-start(bf16[512,128]{1,0:T(8,128)(2,1)S(1)} %get-tuple-element.55), channel_id=1, source_target_pairs={{0,5},{1,2},{2,7},{3,0},{4,1},{5,6},{6,3},{7,4},{8,13},{9,10},{10,... | collective-permute-start | bytes 393224 | tf_op jit(solution)/shard_map/ppermute | solution.py:393
  10.6 3.6 %collective-permute-start.3 = (bf16[512,128]{1,0:T(8,128)(2,1)S(1)}, bf16[512,128]{1,0:T(8,128)(2,1)S(1)}, u32[]{:S(2)}, u32[]{:S(2)}) collective-permute-start(bf16[512,128]{1,0:T(8,128)(2,1)S(1)} %get-tuple-element.55), channel_id=1, source_target_pairs={{0,1},{1,0},{2,3},{3,2},{4,5},{5,4},{6,7},{7,6},{8,9},{9,8},{10,11... | collective-permute-start | bytes 393224 | tf_op jit(solution)/shard_map/ppermute | solution.py:393
  11.5 5.3 %collective-permute-start.9 = (bf16[512,128]{1,0:T(8,128)(2,1)S(1)}, bf16[512,128]{1,0:T(8,128)(2,1)S(1)}, u32[]{:S(2)}, u32[]{:S(2)}) collective-permute-start(bf16[512,128]{1,0:T(8,128)(2,1)S(1)} %get-tuple-element.60), channel_id=1, source_target_pairs={{0,4},{1,3},{2,6},{3,1},{4,0},{5,7},{6,2},{7,5},{8,12},{9,11},{10,... | collective-permute-start | bytes 393224 | tf_op jit(solution)/shard_map/ppermute | solution.py:393
  13.1 5.5 %collective-permute-start.10 = (bf16[512,128]{1,0:T(8,128)(2,1)S(1)}, bf16[512,128]{1,0:T(8,128)(2,1)S(1)}, u32[]{:S(2)}, u32[]{:S(2)}) collective-permute-start(bf16[512,128]{1,0:T(8,128)(2,1)S(1)} %get-tuple-element.61), channel_id=1, source_target_pairs={{0,5},{1,2},{2,7},{3,0},{4,1},{5,6},{6,3},{7,4},{8,13},{9,10},{10,... | collective-permute-start | bytes 393224 | tf_op jit(solution)/shard_map/ppermute | solution.py:393
  13.5 5.1 %collective-permute-start.11 = (bf16[512,128]{1,0:T(8,128)(2,1)S(1)}, bf16[512,128]{1,0:T(8,128)(2,1)S(1)}, u32[]{:S(2)}, u32[]{:S(2)}) collective-permute-start(bf16[512,128]{1,0:T(8,128)(2,1)S(1)} %get-tuple-element.62), channel_id=1, source_target_pairs={{0,1},{1,0},{2,3},{3,2},{4,5},{5,4},{6,7},{7,6},{8,9},{9,8},{10,11... | collective-permute-start | bytes 393224 | tf_op jit(solution)/shard_map/ppermute | solution.py:393
  14.5 5.0 %collective-permute-start.6 = (bf16[512,128]{1,0:T(8,128)(2,1)S(1)}, bf16[512,128]{1,0:T(8,128)(2,1)S(1)}, u32[]{:S(2)}, u32[]{:S(2)}) collective-permute-start(bf16[512,128]{1,0:T(8,128)(2,1)S(1)} %get-tuple-element.56), channel_id=1, source_target_pairs={{0,4},{1,3},{2,6},{3,1},{4,0},{5,7},{6,2},{7,5},{8,12},{9,11},{10,... | collective-permute-start | bytes 393224 | tf_op jit(solution)/shard_map/ppermute | solution.py:393
  15.9 4.4 %collective-permute-start.7 = (bf16[512,128]{1,0:T(8,128)(2,1)S(1)}, bf16[512,128]{1,0:T(8,128)(2,1)S(1)}, u32[]{:S(2)}, u32[]{:S(2)}) collective-permute-start(bf16[512,128]{1,0:T(8,128)(2,1)S(1)} %get-tuple-element.58), channel_id=1, source_target_pairs={{0,5},{1,2},{2,7},{3,0},{4,1},{5,6},{6,3},{7,4},{8,13},{9,10},{10,... | collective-permute-start | bytes 393224 | tf_op jit(solution)/shard_map/ppermute | solution.py:393
  16.8 3.5 %collective-permute-start.8 = (bf16[512,128]{1,0:T(8,128)(2,1)S(1)}, bf16[512,128]{1,0:T(8,128)(2,1)S(1)}, u32[]{:S(2)}, u32[]{:S(2)}) collective-permute-start(bf16[512,128]{1,0:T(8,128)(2,1)S(1)} %get-tuple-element.59), channel_id=1, source_target_pairs={{0,1},{1,0},{2,3},{3,2},{4,5},{5,4},{6,7},{7,6},{8,9},{9,8},{10,11... | collective-permute-start | bytes 393224 | tf_op jit(solution)/shard_map/ppermute | solution.py:393
  17.1 1.5 %copy-start = (bf16[1,256,2048]{2,1,0:T(8,128)(2,1)S(1)}, bf16[1,256,2048]{2,1,0:T(8,128)(2,1)}, u32[]{:S(2)}) copy-start(bf16[1,256,2048]{2,1,0:T(8,128)(2,1)} %param.10) | copy-start | bytes 3145732
  17.1 1.5 %copy-start.1 = (f32[2048]{0:T(1024)S(1)}, f32[2048]{0:T(1024)}, u32[]{:S(2)}) copy-start(f32[2048]{0:T(1024)} %param.11) | copy-start | bytes 24580
  21.0 4.5 %collective-permute-start.14 = (f32[2,256]{1,0:T(2,128)S(1)}, f32[2,256]{1,0:T(2,128)S(1)}, u32[]{:S(2)}, u32[]{:S(2)}) collective-permute-start(f32[2,256]{1,0:T(2,128)S(1)} %get-tuple-element.66.rest_0_), channel_id=1, source_target_pairs={{0,16},{8,24},{16,0},{24,8},{1,17},{9,25},{17,1},{25,9},{2,18},{10... | collective-permute-start | bytes 6152 | tf_op jit(solution)/shard_map/ppermute | solution.py:420
  23.6 5.4 %collective-permute-start.13 = (f32[2,256]{1,0:T(2,128)S(1)}, f32[2,256]{1,0:T(2,128)S(1)}, u32[]{:S(2)}, u32[]{:S(2)}) collective-permute-start(f32[2,256]{1,0:T(2,128)S(1)} %get-tuple-element.66.rest_0_), channel_id=1, source_target_pairs={{0,24},{8,16},{16,8},{24,0},{1,25},{9,17},{17,9},{25,1},{2,26},{10... | collective-permute-start | bytes 6152 | tf_op jit(solution)/shard_map/ppermute | solution.py:420
  25.0 4.0 %collective-permute-start.12 = (f32[2,256]{1,0:T(2,128)S(1)}, f32[2,256]{1,0:T(2,128)S(1)}, u32[]{:S(2)}, u32[]{:S(2)}) collective-permute-start(f32[2,256]{1,0:T(2,128)S(1)} %get-tuple-element.66.rest_0_), channel_id=1, source_target_pairs={{0,8},{8,0},{16,24},{24,16},{1,9},{9,1},{17,25},{25,17},{2,10},{10... | collective-permute-start | bytes 6152 | tf_op jit(solution)/shard_map/ppermute | solution.py:420
  30.1 7.0 %collective-permute-start.17 = (bf16[1024,128]{1,0:T(8,128)(2,1)S(1)}, bf16[1024,128]{1,0:T(8,128)(2,1)S(1)}, u32[]{:S(2)}, u32[]{:S(2)}) collective-permute-start(bf16[1024,128]{1,0:T(8,128)(2,1)S(1)} %get-tuple-element.76), channel_id=1, source_target_pairs={{0,5},{1,2},{2,7},{3,0},{4,1},{5,6},{6,3},{7,4},{8,13},{9,10},{10,... | collective-permute-start | bytes 786440 | tf_op jit(solution)/shard_map/ppermute | solution.py:393
  30.2 6.9 %collective-permute-start.15 = (bf16[1024,128]{1,0:T(8,128)(2,1)S(1)}, bf16[1024,128]{1,0:T(8,128)(2,1)S(1)}, u32[]{:S(2)}, u32[]{:S(2)}) collective-permute-start(bf16[1024,128]{1,0:T(8,128)(2,1)S(1)} %get-tuple-element.76), channel_id=1, source_target_pairs={{0,1},{1,0},{2,3},{3,2},{4,5},{5,4},{6,7},{7,6},{8,9},{9,8},{10,11... | collective-permute-start | bytes 786440 | tf_op jit(solution)/shard_map/ppermute | solution.py:393
  31.3 7.5 %collective-permute-start.16 = (bf16[1024,128]{1,0:T(8,128)(2,1)S(1)}, bf16[1024,128]{1,0:T(8,128)(2,1)S(1)}, u32[]{:S(2)}, u32[]{:S(2)}) collective-permute-start(bf16[1024,128]{1,0:T(8,128)(2,1)S(1)} %get-tuple-element.75.refs_0_), channel_id=1, source_target_pairs={{0,2},{1,5},{2,0},{3,7},{4,6},{5,1},{6,4},{7,3},{8,10},{9,13},{10,... | collective-permute-start | bytes 786440 | tf_op jit(solution)/shard_map/ppermute | solution.py:393
  39.1 5.4 %collective-permute-start.21 = (bf16[640,128]{1,0:T(8,128)(2,1)S(1)}, bf16[640,128]{1,0:T(8,128)(2,1)S(1)}, u32[]{:S(2)}, u32[]{:S(2)}) collective-permute-start(bf16[640,128]{1,0:T(8,128)(2,1)S(1)} %get-tuple-element.83), channel_id=1, source_target_pairs={{0,4},{1,3},{2,6},{3,1},{4,0},{5,7},{6,2},{7,5},{8,12},{9,11},{10,... | collective-permute-start | bytes 491528 | tf_op jit(solution)/shard_map/ppermute | solution.py:393
  40.1 5.9 %collective-permute-start.22 = (bf16[640,128]{1,0:T(8,128)(2,1)S(1)}, bf16[640,128]{1,0:T(8,128)(2,1)S(1)}, u32[]{:S(2)}, u32[]{:S(2)}) collective-permute-start(bf16[640,128]{1,0:T(8,128)(2,1)S(1)} %get-tuple-element.84), channel_id=1, source_target_pairs={{0,5},{1,2},{2,7},{3,0},{4,1},{5,6},{6,3},{7,4},{8,13},{9,10},{10,... | collective-permute-start | bytes 491528 | tf_op jit(solution)/shard_map/ppermute | solution.py:393
  40.2 5.8 %collective-permute-start.23 = (bf16[640,128]{1,0:T(8,128)(2,1)S(1)}, bf16[640,128]{1,0:T(8,128)(2,1)S(1)}, u32[]{:S(2)}, u32[]{:S(2)}) collective-permute-start(bf16[640,128]{1,0:T(8,128)(2,1)S(1)} %get-tuple-element.85), channel_id=1, source_target_pairs={{0,1},{1,0},{2,3},{3,2},{4,5},{5,4},{6,7},{7,6},{8,9},{9,8},{10,11... | collective-permute-start | bytes 491528 | tf_op jit(solution)/shard_map/ppermute | solution.py:393
  42.1 5.6 %collective-permute-start.18 = (bf16[384,128]{1,0:T(8,128)(2,1)S(1)}, bf16[384,128]{1,0:T(8,128)(2,1)S(1)}, u32[]{:S(2)}, u32[]{:S(2)}) collective-permute-start(bf16[384,128]{1,0:T(8,128)(2,1)S(1)} %get-tuple-element.80), channel_id=1, source_target_pairs={{0,4},{1,3},{2,6},{3,1},{4,0},{5,7},{6,2},{7,5},{8,12},{9,11},{10,... | collective-permute-start | bytes 294920 | tf_op jit(solution)/shard_map/ppermute | solution.py:393
  42.6 5.1 %collective-permute-start.19 = (bf16[384,128]{1,0:T(8,128)(2,1)S(1)}, bf16[384,128]{1,0:T(8,128)(2,1)S(1)}, u32[]{:S(2)}, u32[]{:S(2)}) collective-permute-start(bf16[384,128]{1,0:T(8,128)(2,1)S(1)} %get-tuple-element.81), channel_id=1, source_target_pairs={{0,5},{1,2},{2,7},{3,0},{4,1},{5,6},{6,3},{7,4},{8,13},{9,10},{10,... | collective-permute-start | bytes 294920 | tf_op jit(solution)/shard_map/ppermute | solution.py:393
  44.5 3.2 %collective-permute-start.20 = (bf16[384,128]{1,0:T(8,128)(2,1)S(1)}, bf16[384,128]{1,0:T(8,128)(2,1)S(1)}, u32[]{:S(2)}, u32[]{:S(2)}) collective-permute-start(bf16[384,128]{1,0:T(8,128)(2,1)S(1)} %get-tuple-element.82), channel_id=1, source_target_pairs={{0,1},{1,0},{2,3},{3,2},{4,5},{5,4},{6,7},{7,6},{8,9},{9,8},{10,11... | collective-permute-start | bytes 294920 | tf_op jit(solution)/shard_map/ppermute | solution.py:393

commit v17 on v16

--- a/solution.py
+++ b/solution.py
@@ -263,7 +263,7 @@
 
 
 def grad_kernel(groups, grid, scale, length, queries, cotangent, gain, attention, *rest):
-    all_sums, (grad_out, inverse_rms, *halves, full) = rest[:groups], rest[groups:]
+    all_sums, (grad_out, inverse_rms, *halves) = rest[:groups], rest[groups:]
     rows = queries.shape[0]
     features = HEADS * HD
     total = all_sums[0][...]
@@ -276,14 +276,16 @@
     shrink = live_inverse * inverse * (inverse * total[1:2, :]) / features
     live_inverse = token_columns(live_inverse)
     shrink = token_columns(shrink)
-    for head in range(queries.shape[1] // HD):
-        cols = head_cols(head)
-        gain_grad = cotangent[:, cols].astype(F32) * gain[:, cols]
-        grad = (live_inverse * gain_grad - attention[:, cols] * shrink).astype(BF16)
-        grad_out[:, cols] = grad
-        full[head * HD : (head + 1) * HD, :] = (scale * tn(queries[:, cols], grad)).astype(BF16)
-    for half, out in zip(row_halves(full, my_place(grid)[2], grid[2]), halves):
-        out[...] = half[...]
+    core = my_place(grid)[2]
+    for flip, half in enumerate(halves):
+        height = half.shape[0]
+        first = (core ^ flip) * height
+        for head in range(height // HD):
+            cols = pl.ds(pl.multiple_of(first + head * HD, HD), HD)
+            gain_grad = cotangent[:, cols].astype(F32) * gain[:, cols]
+            grad = (live_inverse * gain_grad - attention[:, cols] * shrink).astype(BF16)
+            grad_out[:, cols] = grad
+            half[head * HD : (head + 1) * HD, :] = (scale * tn(queries[:, cols], grad)).astype(BF16)
 
 
 def row_copies(source, target, sems):
@@ -463,10 +465,13 @@
             functools.partial(next_state_kernel, piece, grid), halves(FORWARD_PIECES),
             (length, key, value), [state_scratch], unit * HD // FORWARD_PIECES,
         )
-    (query,) = call(fetch_kernel, [narrow], (queries[0],), [pltpu.SemaphoreType.DMA((4,))], 0, (0,), after=(own[0],))
     mixed = []
     for part in split_refs(own, *[pair] * FORWARD_PIECES):
-        mixed.append(mix(gather_line(part, grid), up, 0, part[0].shape[0], () if mixed else (query,)))
+        mixed.append(mix(gather_line(part, grid), up, 0, part[0].shape[0], () if len(mixed) != 1 else (query,)))
+        if len(mixed) == 1:
+            (query,) = call(
+                fetch_kernel, [narrow], (queries[0],), [pltpu.SemaphoreType.DMA((4,))], 0, (0,), after=(mixed[0][0],)
+            )
     (local,) = call(
         functools.partial(local_kernel, heads),
         [wide], (length, query, key, value), [mask], unit * rows * 2, after=(mixed[0][0],),
@@ -488,7 +493,7 @@
     grads, inverse_rms, *state_grad = call(
         functools.partial(grad_kernel, len(sums), grid, scale),
         [narrow, row] + halves(1), (length, query, cot, gain, attention, *sums),
-        [pltpu.VMEM((features, HD), BF16)], unit * HD,
+        (), unit * HD,
     )
     group = 4 if heads % 4 == 0 else 1
     attended, query_grad, key_part, token = call(

time: 49.6 us -> 51.4 us (1.036)
  waiting for transfers between devices: 8.3 us -> 10 us
    ppermute x21, waiting for transfers between devices: 4.49 us -> 6.21 us  [line_send(): return lax.ppermute(block, 'seg', moves)]
  transfers between devices with their start and end apart: 24 -> 24, of which waited for: 7 -> 8; matrix products, arithmetic and copies ran while one was open for 0% -> 0% of each run, Pallas kernels for 25% -> 24%
where the time goes in v17:
time: 51.4 us; the launch traced here: 51.2 us
  starting transfers between devices  21.2 us (41%)
  Pallas kernels  18.3 us (36%)
  waiting for transfers between devices  10 us (19%)
  between operations  1.64 us (3%)
    pallas_call x15, Pallas kernels, call(): pl.pallas_call(kernel, out_shape=out_shape, in_specs=specs + [ANY] * len(...  18.3 us
    ppermute x21, starting transfers between devices, line_send(): return lax.ppermute(block, 'seg', moves)  17 us
    ppermute x21, waiting for transfers between devices, line_send(): return lax.ppermute(block, 'seg', moves)  6.21 us
    ppermute x3, starting transfers between devices, token_sums(): parts.append(lax.ppermute(sums, 'head', moves))  4.22 us
    ppermute x3, waiting for transfers between devices, token_sums(): parts.append(lax.ppermute(sums, 'head', moves))  3.81 us
  transfers between devices with their start and end apart: 24, of which 8 were waited for; matrix products, arithmetic and copies ran while one was open for 0% of the time, Pallas kernels for 24%

profile of v17, /device:TPU:0, one launch (start us, length us, event | category | flops | bytes accessed | tf_op | source)
XLA Modules:
  0.0 51.2 jit_solution(17860336941362344174)
XLA Ops:
  1.3 1.9 %shard_map.102 = (bf16[256,2048]{1,0:T(8,128)(2,1)S(1)}, bf16[256,2048]{1,0:T(8,128)(2,1)S(1)}, s32[1,256]{1,0:T(1,128)S(1)}, f32[16,128]{1,0:T(8,128)S(1)}, f32...) custom-call(s32[1]{0:T(128)S(6)} %copy.17.seg_len, bf16[256,2048]{1,0:T(8,128)(2,1)} %bitcast.20, ...), custom_call_target="tpu_custom_call" | custom-call | flops 67108864 | bytes 4473892 | tf_op jit(solution)/shard_map/pallas_call | solution.py:373
  3.2 3.0 %collective-permute-start.1 = (bf16[512,128]{1,0:T(8,128)(2,1)S(1)}, bf16[512,128]{1,0:T(8,128)(2,1)S(1)}, u32[]{:S(2)}, u32[]{:S(2)}) collective-permute-start(bf16[512,128]{1,0:T(8,128)(2,1)S(1)} %get-tuple-element.49.refs_0_), channel_id=1, source_target_pairs={{0,2},{1,5},{2,0},{3,7},{4,6},{5,1},{6,4},{7,3},{8,10},{9,13},{10,... | collective-permute-start | bytes 393224 | tf_op jit(solution)/shard_map/ppermute | solution.py:395
  6.2 0.0 collective-permute-start.2
  6.2 0.2 collective-permute-start
  6.3 0.4 shard_map.106
  6.7 2.0 %collective-permute-start.4 = (bf16[512,128]{1,0:T(8,128)(2,1)S(1)}, bf16[512,128]{1,0:T(8,128)(2,1)S(1)}, u32[]{:S(2)}, u32[]{:S(2)}) collective-permute-start(bf16[512,128]{1,0:T(8,128)(2,1)S(1)} %get-tuple-element.54.refs_0_), channel_id=1, source_target_pairs={{0,2},{1,5},{2,0},{3,7},{4,6},{5,1},{6,4},{7,3},{8,10},{9,13},{10,... | collective-permute-start | bytes 393224 | tf_op jit(solution)/shard_map/ppermute | solution.py:395
  8.7 0.0 collective-permute-start.5
  8.7 0.9 %collective-permute-done.1.refs_2_ = bf16[512,128]{1,0:T(8,128)(2,1)S(1)} collective-permute-done((bf16[512,128]{1,0:T(8,128)(2,1)S(1)}, bf16[512,128]{1,0:T(8,128)(2,1)S(1)}, u32[]{:S(2)}, u32[]{:S(2)}) %collective-permute-start.1) | collective-permute-done | bytes 131104 | tf_op jit(solution)/shard_map/ppermute | solution.py:395
  9.7 0.0 collective-permute-start.3
  9.7 1.0 %collective-permute-done.2.refs_3_ = bf16[512,128]{1,0:T(8,128)(2,1)S(1)} collective-permute-done((bf16[512,128]{1,0:T(8,128)(2,1)S(1)}, bf16[512,128]{1,0:T(8,128)(2,1)S(1)}, u32[]{:S(2)}, u32[]{:S(2)}) %collective-permute-start.2) | collective-permute-done | bytes 131104 | tf_op jit(solution)/shard_map/ppermute | solution.py:395
  10.7 0.0 collective-permute-done.refs_1_
  10.7 0.3 shard_map.103
  11.0 2.1 %collective-permute-start.9 = (bf16[512,128]{1,0:T(8,128)(2,1)S(1)}, bf16[512,128]{1,0:T(8,128)(2,1)S(1)}, u32[]{:S(2)}, u32[]{:S(2)}) collective-permute-start(bf16[512,128]{1,0:T(8,128)(2,1)S(1)} %get-tuple-element.60), channel_id=1, source_target_pairs={{0,4},{1,3},{2,6},{3,1},{4,0},{5,7},{6,2},{7,5},{8,12},{9,11},{10,... | collective-permute-start | bytes 393224 | tf_op jit(solution)/shard_map/ppermute | solution.py:395
  13.1 1.2 %collective-permute-start.10 = (bf16[512,128]{1,0:T(8,128)(2,1)S(1)}, bf16[512,128]{1,0:T(8,128)(2,1)S(1)}, u32[]{:S(2)}, u32[]{:S(2)}) collective-permute-start(bf16[512,128]{1,0:T(8,128)(2,1)S(1)} %get-tuple-element.61), channel_id=1, source_target_pairs={{0,5},{1,2},{2,7},{3,0},{4,1},{5,6},{6,3},{7,4},{8,13},{9,10},{10,... | collective-permute-start | bytes 393224 | tf_op jit(solution)/shard_map/ppermute | solution.py:395
  14.3 0.0 collective-permute-done.4.refs_2_
  14.3 0.3 collective-permute-start.11
  14.5 1.2 %shard_map.104.queries.refs_4_ = bf16[256,2048]{1,0:T(8,128)(2,1)S(1)} custom-call(bf16[256,2048]{1,0:T(8,128)(2,1)} %bitcast.19, bf16[512,128]{1,0:T(8,128)(2,1)S(1)} %get-tuple-element.51._.rest_0_.rest_1_), custom_call_target="tpu_custom_call" | custom-call | bytes 2097152 | tf_op jit(solution)/shard_map/pallas_call | solution.py:373
  15.8 0.0 collective-permute-done.5.refs_3_
  15.8 0.0 collective-permute-done.3.refs_1_
  15.8 0.3 shard_map.107
  16.1 0.2 collective-permute-start.6
  16.3 2.0 %collective-permute-start.7 = (bf16[512,128]{1,0:T(8,128)(2,1)S(1)}, bf16[512,128]{1,0:T(8,128)(2,1)S(1)}, u32[]{:S(2)}, u32[]{:S(2)}) collective-permute-start(bf16[512,128]{1,0:T(8,128)(2,1)S(1)} %get-tuple-element.58), channel_id=1, source_target_pairs={{0,5},{1,2},{2,7},{3,0},{4,1},{5,6},{6,3},{7,4},{8,13},{9,10},{10,... | collective-permute-start | bytes 393224 | tf_op jit(solution)/shard_map/ppermute | solution.py:395
  18.3 0.0 collective-permute-done.9.rest_0_
  18.3 0.3 collective-permute-start.8
  18.6 1.5 %shard_map.105.local = f32[256,2048]{1,0:T(8,128)S(1)} custom-call(s32[1,256]{1,0:T(1,128)S(1)} %get-tuple-element.47.length, bf16[256,2048]{1,0:T(8,128)(2,1)S(1)} %shard_map.104.queries.refs_4_, bf16[256,2048]{1,0:T(8,128)(2,1)S(1)} %get-tuple-element.52.keys, bf16[256,2048]{1,0:T(8,128)(2,1)S(1)} %get-tuple-element.53.values, ...), custom_call_target="tpu_custom_call" | custom-call | flops 536870912 | bytes 5243904 | tf_op jit(solution)/shard_map/pallas_call | solution.py:373
  20.0 0.0 collective-permute-done.10.rest_2_
  20.1 0.0 collective-permute-done.11.rest_3_
  20.1 0.0 copy-done
  20.1 0.7 %shard_map.108 = (f32[256,2048]{1,0:T(8,128)S(1)}, f32[2,256]{1,0:T(2,128)S(1)}, bf16[1024,128]{1,0:T(8,128)(2,1)S(1)}) custom-call(s32[1,256]{1,0:T(1,128)S(1)} %get-tuple-element.47.length, bf16[256,2048]{1,0:T(8,128)(2,1)S(1)} %shard_map.104.queries.refs_4_, f32[256,2048]{1,0:T(8,128)S(1)} %shard_map.105.local, bf16[256,2048]{1,0:T(8,128)(2,1)S(1)} %bitcast.10, ...), custom_call_target="tpu_custom_call" | custom-call | flops 67108864 | bytes 7089152 | tf_op jit(solution)/shard_map/pallas_call | solution.py:373
  20.8 0.4 collective-permute-done.6.rest_0_
  21.1 0.7 %collective-permute-done.7.rest_2_ = bf16[512,128]{1,0:T(8,128)(2,1)S(1)} collective-permute-done((bf16[512,128]{1,0:T(8,128)(2,1)S(1)}, bf16[512,128]{1,0:T(8,128)(2,1)S(1)}, u32[]{:S(2)}, u32[]{:S(2)}) %collective-permute-start.7) | collective-permute-done | bytes 131104 | tf_op jit(solution)/shard_map/ppermute | solution.py:395
  21.8 0.0 collective-permute-done.8.rest_3_
  21.8 0.7 %shard_map.109 = (f32[256,2048]{1,0:T(8,128)S(1)}, f32[2,256]{1,0:T(2,128)S(1)}, bf16[1024,128]{1,0:T(8,128)(2,1)S(1)}) custom-call(s32[1,256]{1,0:T(1,128)S(1)} %get-tuple-element.47.length, bf16[256,2048]{1,0:T(8,128)(2,1)S(1)} %shard_map.104.queries.refs_4_, f32[256,2048]{1,0:T(8,128)S(1)} %shard_map.105.local, ...), custom_call_target="tpu_custom_call", output_to_operand_aliasing={{0}: (10, {})} | custom-call | flops 67108864 | bytes 9188352 | tf_op jit(solution)/shard_map/pallas_call | solution.py:373
  22.5 2.7 %collective-permute-start.14 = (f32[2,256]{1,0:T(2,128)S(1)}, f32[2,256]{1,0:T(2,128)S(1)}, u32[]{:S(2)}, u32[]{:S(2)}) collective-permute-start(f32[2,256]{1,0:T(2,128)S(1)} %get-tuple-element.66.rest_0_), channel_id=1, source_target_pairs={{0,16},{8,24},{16,0},{24,8},{1,17},{9,25},{17,1},{25,9},{2,18},{10... | collective-permute-start | bytes 6152 | tf_op jit(solution)/shard_map/ppermute | solution.py:422
  25.1 1.3 %collective-permute-start.13 = (f32[2,256]{1,0:T(2,128)S(1)}, f32[2,256]{1,0:T(2,128)S(1)}, u32[]{:S(2)}, u32[]{:S(2)}) collective-permute-start(f32[2,256]{1,0:T(2,128)S(1)} %get-tuple-element.66.rest_0_), channel_id=1, source_target_pairs={{0,24},{8,16},{16,8},{24,0},{1,25},{9,17},{17,9},{25,1},{2,26},{10... | collective-permute-start | bytes 6152 | tf_op jit(solution)/shard_map/ppermute | solution.py:422
  26.5 0.2 collective-permute-start.12
  26.7 0.3 collective-permute-done.14.rest_3_
  27.0 3.5 %collective-permute-done.13.rest_2_ = f32[2,256]{1,0:T(2,128)S(1)} collective-permute-done((f32[2,256]{1,0:T(2,128)S(1)}, f32[2,256]{1,0:T(2,128)S(1)}, u32[]{:S(2)}, u32[]{:S(2)}) %collective-permute-start.13) | collective-permute-done | bytes 2080 | tf_op jit(solution)/shard_map/ppermute | solution.py:422
  30.5 0.0 collective-permute-done.12.rest_1_
  30.5 1.4 %shard_map.110 = (bf16[256,2048]{1,0:T(8,128)(2,1)S(1)}, f32[1,256]{1,0:T(1,128)S(1)}, bf16[1024,128]{1,0:T(8,128)(2,1)S(1)}, bf16[1024,128]{1,0:T(8,128)(2,1)S(1)}) custom-call(s32[1,256]{1,0:T(1,128)S(1)} %get-tuple-element.47.length, bf16[256,2048]{1,0:T(8,128)(2,1)S(1)} %shard_map.104.queries.refs_4_, bf16[256,2048]{1,0:T(8,128)(2,1)S(1)} %bitcast.12, ...), custom_call_target="tpu_custom_call" | custom-call | flops 134217728 | bytes 5785600 | tf_op jit(solution)/shard_map/pallas_call | solution.py:373
  31.9 0.1 collective-permute-start.17
  32.0 1.1 %collective-permute-start.15 = (bf16[1024,128]{1,0:T(8,128)(2,1)S(1)}, bf16[1024,128]{1,0:T(8,128)(2,1)S(1)}, u32[]{:S(2)}, u32[]{:S(2)}) collective-permute-start(bf16[1024,128]{1,0:T(8,128)(2,1)S(1)} %get-tuple-element.76), channel_id=1, source_target_pairs={{0,1},{1,0},{2,3},{3,2},{4,5},{5,4},{6,7},{7,6},{8,9},{9,8},{10,11... | collective-permute-start | bytes 786440 | tf_op jit(solution)/shard_map/ppermute | solution.py:395
  33.1 1.0 %collective-permute-start.16 = (bf16[1024,128]{1,0:T(8,128)(2,1)S(1)}, bf16[1024,128]{1,0:T(8,128)(2,1)S(1)}, u32[]{:S(2)}, u32[]{:S(2)}) collective-permute-start(bf16[1024,128]{1,0:T(8,128)(2,1)S(1)} %get-tuple-element.75.refs_0_), channel_id=1, source_target_pairs={{0,2},{1,5},{2,0},{3,7},{4,6},{5,1},{6,4},{7,3},{8,10},{9,13},{10,... | collective-permute-start | bytes 786440 | tf_op jit(solution)/shard_map/ppermute | solution.py:395
  34.1 4.8 %shard_map.111 = (bf16[256,2048]{1,0:T(8,128)(2,1)}, bf16[256,2048]{1,0:T(8,128)(2,1)}, f32[256,2048]{1,0:T(8,128)S(1)}, f32[8,128]{1,0:T(8,128)S(1)}) custom-call(s32[1,256]{1,0:T(1,128)S(1)} %get-tuple-element.47.length, f32[1,256]{1,0:T(1,128)S(1)} %get-tuple-element.67.inverse_rms, f32[1,2048]{1,0:T(1,128)S(1)} %bitcast.16, ...), custom_call_target="tpu_custom_call" | custom-call | flops 939524096 | bytes 11024384 | tf_op jit(solution)/shard_map/pallas_call | solution.py:373
  38.9 0.0 collective-permute-done.17.refs_3_
  38.9 0.0 collective-permute-done.15.refs_1_
  39.0 1.6 %collective-permute-done.16.refs_2_ = bf16[1024,128]{1,0:T(8,128)(2,1)S(1)} collective-permute-done((bf16[1024,128]{1,0:T(8,128)(2,1)S(1)}, bf16[1024,128]{1,0:T(8,128)(2,1)S(1)}, u32[]{:S(2)}, u32[]{:S(2)}) %collective-permute-start.16) | collective-permute-done | bytes 262176 | tf_op jit(solution)/shard_map/ppermute | solution.py:395
  40.6 0.4 shard_map.112
  41.0 0.9 %collective-permute-start.21 = (bf16[640,128]{1,0:T(8,128)(2,1)S(1)}, bf16[640,128]{1,0:T(8,128)(2,1)S(1)}, u32[]{:S(2)}, u32[]{:S(2)}) collective-permute-start(bf16[640,128]{1,0:T(8,128)(2,1)S(1)} %get-tuple-element.83), channel_id=1, source_target_pairs={{0,4},{1,3},{2,6},{3,1},{4,0},{5,7},{6,2},{7,5},{8,12},{9,11},{10,... | collective-permute-start | bytes 491528 | tf_op jit(solution)/shard_map/ppermute | solution.py:395
  41.8 0.2 collective-permute-start.22
  42.1 1.6 %collective-permute-start.23 = (bf16[640,128]{1,0:T(8,128)(2,1)S(1)}, bf16[640,128]{1,0:T(8,128)(2,1)S(1)}, u32[]{:S(2)}, u32[]{:S(2)}) collective-permute-start(bf16[640,128]{1,0:T(8,128)(2,1)S(1)} %get-tuple-element.85), channel_id=1, source_target_pairs={{0,1},{1,0},{2,3},{3,2},{4,5},{5,4},{6,7},{7,6},{8,9},{9,8},{10,11... | collective-permute-start | bytes 491528 | tf_op jit(solution)/shard_map/ppermute | solution.py:395
  43.7 0.2 shard_map.113
  43.9 0.6 %collective-permute-start.18 = (bf16[384,128]{1,0:T(8,128)(2,1)S(1)}, bf16[384,128]{1,0:T(8,128)(2,1)S(1)}, u32[]{:S(2)}, u32[]{:S(2)}) collective-permute-start(bf16[384,128]{1,0:T(8,128)(2,1)S(1)} %get-tuple-element.80), channel_id=1, source_target_pairs={{0,4},{1,3},{2,6},{3,1},{4,0},{5,7},{6,2},{7,5},{8,12},{9,11},{10,... | collective-permute-start | bytes 294920 | tf_op jit(solution)/shard_map/ppermute | solution.py:395
  44.5 0.3 collective-permute-start.19
  44.8 1.5 %collective-permute-done.21.rest_0_ = bf16[640,128]{1,0:T(8,128)(2,1)S(1)} collective-permute-done((bf16[640,128]{1,0:T(8,128)(2,1)S(1)}, bf16[640,128]{1,0:T(8,128)(2,1)S(1)}, u32[]{:S(2)}, u32[]{:S(2)}) %collective-permute-start.21) | collective-permute-done | bytes 163872 | tf_op jit(solution)/shard_map/ppermute | solution.py:395
  46.4 0.0 collective-permute-start.20
  46.4 1.5 %shard_map.114.value_part = f32[256,2048]{1,0:T(8,128)S(1)} custom-call(s32[1,256]{1,0:T(1,128)S(1)} %get-tuple-element.47.length, bf16[256,2048]{1,0:T(8,128)(2,1)S(1)} %shard_map.104.queries.refs_4_, bf16[256,2048]{1,0:T(8,128)(2,1)S(1)} %get-tuple-element.52.keys, bf16[256,2048]{1,0:T(8,128)(2,1)S(1)} %get-tuple-element.68.grads, ...), custom_call_target="tpu_custom_call" | custom-call | flops 536870912 | bytes 5243904 | tf_op jit(solution)/shard_map/pallas_call | solution.py:373
  47.8 0.0 collective-permute-done.22.rest_2_
  47.9 0.0 collective-permute-done.23.rest_3_
  47.9 1.7 %shard_map.115 = (bf16[256,2048]{1,0:T(8,128)(2,1)}, bf16[256,2048]{1,0:T(8,128)(2,1)}) custom-call(s32[1,256]{1,0:T(1,128)S(1)} %get-tuple-element.47.length, bf16[256,2048]{1,0:T(8,128)(2,1)S(1)} %get-tuple-element.52.keys, bf16[256,2048]{1,0:T(8,128)(2,1)S(1)} %get-tuple-element.53.values, f32[256,2048]{1,0:T(8,128)S(1)} %get-tuple-element.73.key_part, ...), custom_call_target="tpu_custom_call" | custom-call | flops 167772160 | bytes 9044992 | tf_op jit(solution)/shard_map/pallas_call | solution.py:373
  49.5 0.0 collective-permute-done.18.rest_0_
  49.6 0.0 collective-permute-done.19.rest_2_
  49.6 0.0 collective-permute-done.20.rest_3_
  49.6 1.4 %shard_map.116 = (bf16[256,2048]{1,0:T(8,128)(2,1)}, bf16[256,2048]{1,0:T(8,128)(2,1)}) custom-call(s32[1,256]{1,0:T(1,128)S(1)} %get-tuple-element.47.length, bf16[256,2048]{1,0:T(8,128)(2,1)S(1)} %get-tuple-element.52.keys, bf16[256,2048]{1,0:T(8,128)(2,1)S(1)} %get-tuple-element.53.values, ...), custom_call_target="tpu_custom_call", output_to_operand_aliasing={{0}: (9, {}), {1}: (10, {})} | custom-call | flops 100663296 | bytes 10880000 | tf_op jit(solution)/shard_map/pallas_call | solution.py:373
  (3 shorter events, 0.0 us)
Async XLA Ops:
  3.2 6.5 %collective-permute-start.1 = (bf16[512,128]{1,0:T(8,128)(2,1)S(1)}, bf16[512,128]{1,0:T(8,128)(2,1)S(1)}, u32[]{:S(2)}, u32[]{:S(2)}) collective-permute-start(bf16[512,128]{1,0:T(8,128)(2,1)S(1)} %get-tuple-element.49.refs_0_), channel_id=1, source_target_pairs={{0,2},{1,5},{2,0},{3,7},{4,6},{5,1},{6,4},{7,3},{8,10},{9,13},{10,... | collective-permute-start | bytes 393224 | tf_op jit(solution)/shard_map/ppermute | solution.py:395
  6.2 4.6 %collective-permute-start.2 = (bf16[512,128]{1,0:T(8,128)(2,1)S(1)}, bf16[512,128]{1,0:T(8,128)(2,1)S(1)}, u32[]{:S(2)}, u32[]{:S(2)}) collective-permute-start(bf16[512,128]{1,0:T(8,128)(2,1)S(1)} %get-tuple-element.50), channel_id=1, source_target_pairs={{0,5},{1,2},{2,7},{3,0},{4,1},{5,6},{6,3},{7,4},{8,13},{9,10},{10,... | collective-permute-start | bytes 393224 | tf_op jit(solution)/shard_map/ppermute | solution.py:395
  6.2 4.6 %collective-permute-start = (bf16[512,128]{1,0:T(8,128)(2,1)S(1)}, bf16[512,128]{1,0:T(8,128)(2,1)S(1)}, u32[]{:S(2)}, u32[]{:S(2)}) collective-permute-start(bf16[512,128]{1,0:T(8,128)(2,1)S(1)} %get-tuple-element.50), channel_id=1, source_target_pairs={{0,1},{1,0},{2,3},{3,2},{4,5},{5,4},{6,7},{7,6},{8,9},{9,8},{10,11... | collective-permute-start | bytes 393224 | tf_op jit(solution)/shard_map/ppermute | solution.py:395
  6.7 7.5 %collective-permute-start.4 = (bf16[512,128]{1,0:T(8,128)(2,1)S(1)}, bf16[512,128]{1,0:T(8,128)(2,1)S(1)}, u32[]{:S(2)}, u32[]{:S(2)}) collective-permute-start(bf16[512,128]{1,0:T(8,128)(2,1)S(1)} %get-tuple-element.54.refs_0_), channel_id=1, source_target_pairs={{0,2},{1,5},{2,0},{3,7},{4,6},{5,1},{6,4},{7,3},{8,10},{9,13},{10,... | collective-permute-start | bytes 393224 | tf_op jit(solution)/shard_map/ppermute | solution.py:395
  8.7 7.0 %collective-permute-start.5 = (bf16[512,128]{1,0:T(8,128)(2,1)S(1)}, bf16[512,128]{1,0:T(8,128)(2,1)S(1)}, u32[]{:S(2)}, u32[]{:S(2)}) collective-permute-start(bf16[512,128]{1,0:T(8,128)(2,1)S(1)} %get-tuple-element.55), channel_id=1, source_target_pairs={{0,5},{1,2},{2,7},{3,0},{4,1},{5,6},{6,3},{7,4},{8,13},{9,10},{10,... | collective-permute-start | bytes 393224 | tf_op jit(solution)/shard_map/ppermute | solution.py:395
  9.7 6.1 %collective-permute-start.3 = (bf16[512,128]{1,0:T(8,128)(2,1)S(1)}, bf16[512,128]{1,0:T(8,128)(2,1)S(1)}, u32[]{:S(2)}, u32[]{:S(2)}) collective-permute-start(bf16[512,128]{1,0:T(8,128)(2,1)S(1)} %get-tuple-element.55), channel_id=1, source_target_pairs={{0,1},{1,0},{2,3},{3,2},{4,5},{5,4},{6,7},{7,6},{8,9},{9,8},{10,11... | collective-permute-start | bytes 393224 | tf_op jit(solution)/shard_map/ppermute | solution.py:395
  11.0 7.3 %collective-permute-start.9 = (bf16[512,128]{1,0:T(8,128)(2,1)S(1)}, bf16[512,128]{1,0:T(8,128)(2,1)S(1)}, u32[]{:S(2)}, u32[]{:S(2)}) collective-permute-start(bf16[512,128]{1,0:T(8,128)(2,1)S(1)} %get-tuple-element.60), channel_id=1, source_target_pairs={{0,4},{1,3},{2,6},{3,1},{4,0},{5,7},{6,2},{7,5},{8,12},{9,11},{10,... | collective-permute-start | bytes 393224 | tf_op jit(solution)/shard_map/ppermute | solution.py:395
  13.1 7.0 %collective-permute-start.10 = (bf16[512,128]{1,0:T(8,128)(2,1)S(1)}, bf16[512,128]{1,0:T(8,128)(2,1)S(1)}, u32[]{:S(2)}, u32[]{:S(2)}) collective-permute-start(bf16[512,128]{1,0:T(8,128)(2,1)S(1)} %get-tuple-element.61), channel_id=1, source_target_pairs={{0,5},{1,2},{2,7},{3,0},{4,1},{5,6},{6,3},{7,4},{8,13},{9,10},{10,... | collective-permute-start | bytes 393224 | tf_op jit(solution)/shard_map/ppermute | solution.py:395
  14.3 5.8 %collective-permute-start.11 = (bf16[512,128]{1,0:T(8,128)(2,1)S(1)}, bf16[512,128]{1,0:T(8,128)(2,1)S(1)}, u32[]{:S(2)}, u32[]{:S(2)}) collective-permute-start(bf16[512,128]{1,0:T(8,128)(2,1)S(1)} %get-tuple-element.62), channel_id=1, source_target_pairs={{0,1},{1,0},{2,3},{3,2},{4,5},{5,4},{6,7},{7,6},{8,9},{9,8},{10,11... | collective-permute-start | bytes 393224 | tf_op jit(solution)/shard_map/ppermute | solution.py:395
  16.1 5.0 %collective-permute-start.6 = (bf16[512,128]{1,0:T(8,128)(2,1)S(1)}, bf16[512,128]{1,0:T(8,128)(2,1)S(1)}, u32[]{:S(2)}, u32[]{:S(2)}) collective-permute-start(bf16[512,128]{1,0:T(8,128)(2,1)S(1)} %get-tuple-element.56), channel_id=1, source_target_pairs={{0,4},{1,3},{2,6},{3,1},{4,0},{5,7},{6,2},{7,5},{8,12},{9,11},{10,... | collective-permute-start | bytes 393224 | tf_op jit(solution)/shard_map/ppermute | solution.py:395
  16.3 5.5 %collective-permute-start.7 = (bf16[512,128]{1,0:T(8,128)(2,1)S(1)}, bf16[512,128]{1,0:T(8,128)(2,1)S(1)}, u32[]{:S(2)}, u32[]{:S(2)}) collective-permute-start(bf16[512,128]{1,0:T(8,128)(2,1)S(1)} %get-tuple-element.58), channel_id=1, source_target_pairs={{0,5},{1,2},{2,7},{3,0},{4,1},{5,6},{6,3},{7,4},{8,13},{9,10},{10,... | collective-permute-start | bytes 393224 | tf_op jit(solution)/shard_map/ppermute | solution.py:395
  18.3 1.8 %copy-start = (bf16[1,256,2048]{2,1,0:T(8,128)(2,1)S(1)}, bf16[1,256,2048]{2,1,0:T(8,128)(2,1)}, u32[]{:S(2)}) copy-start(bf16[1,256,2048]{2,1,0:T(8,128)(2,1)} %param.10) | copy-start | bytes 3145732
  18.3 1.8 %copy-start.1 = (f32[2048]{0:T(1024)S(1)}, f32[2048]{0:T(1024)}, u32[]{:S(2)}) copy-start(f32[2048]{0:T(1024)} %param.11) | copy-start | bytes 24580
  18.3 3.5 %collective-permute-start.8 = (bf16[512,128]{1,0:T(8,128)(2,1)S(1)}, bf16[512,128]{1,0:T(8,128)(2,1)S(1)}, u32[]{:S(2)}, u32[]{:S(2)}) collective-permute-start(bf16[512,128]{1,0:T(8,128)(2,1)S(1)} %get-tuple-element.59), channel_id=1, source_target_pairs={{0,1},{1,0},{2,3},{3,2},{4,5},{5,4},{6,7},{7,6},{8,9},{9,8},{10,11... | collective-permute-start | bytes 393224 | tf_op jit(solution)/shard_map/ppermute | solution.py:395
  22.5 4.5 %collective-permute-start.14 = (f32[2,256]{1,0:T(2,128)S(1)}, f32[2,256]{1,0:T(2,128)S(1)}, u32[]{:S(2)}, u32[]{:S(2)}) collective-permute-start(f32[2,256]{1,0:T(2,128)S(1)} %get-tuple-element.66.rest_0_), channel_id=1, source_target_pairs={{0,16},{8,24},{16,0},{24,8},{1,17},{9,25},{17,1},{25,9},{2,18},{10... | collective-permute-start | bytes 6152 | tf_op jit(solution)/shard_map/ppermute | solution.py:422
  25.1 5.4 %collective-permute-start.13 = (f32[2,256]{1,0:T(2,128)S(1)}, f32[2,256]{1,0:T(2,128)S(1)}, u32[]{:S(2)}, u32[]{:S(2)}) collective-permute-start(f32[2,256]{1,0:T(2,128)S(1)} %get-tuple-element.66.rest_0_), channel_id=1, source_target_pairs={{0,24},{8,16},{16,8},{24,0},{1,25},{9,17},{17,9},{25,1},{2,26},{10... | collective-permute-start | bytes 6152 | tf_op jit(solution)/shard_map/ppermute | solution.py:422
  26.5 4.0 %collective-permute-start.12 = (f32[2,256]{1,0:T(2,128)S(1)}, f32[2,256]{1,0:T(2,128)S(1)}, u32[]{:S(2)}, u32[]{:S(2)}) collective-permute-start(f32[2,256]{1,0:T(2,128)S(1)} %get-tuple-element.66.rest_0_), channel_id=1, source_target_pairs={{0,8},{8,0},{16,24},{24,16},{1,9},{9,1},{17,25},{25,17},{2,10},{10... | collective-permute-start | bytes 6152 | tf_op jit(solution)/shard_map/ppermute | solution.py:422
  31.9 7.0 %collective-permute-start.17 = (bf16[1024,128]{1,0:T(8,128)(2,1)S(1)}, bf16[1024,128]{1,0:T(8,128)(2,1)S(1)}, u32[]{:S(2)}, u32[]{:S(2)}) collective-permute-start(bf16[1024,128]{1,0:T(8,128)(2,1)S(1)} %get-tuple-element.76), channel_id=1, source_target_pairs={{0,5},{1,2},{2,7},{3,0},{4,1},{5,6},{6,3},{7,4},{8,13},{9,10},{10,... | collective-permute-start | bytes 786440 | tf_op jit(solution)/shard_map/ppermute | solution.py:395
  32.0 6.9 %collective-permute-start.15 = (bf16[1024,128]{1,0:T(8,128)(2,1)S(1)}, bf16[1024,128]{1,0:T(8,128)(2,1)S(1)}, u32[]{:S(2)}, u32[]{:S(2)}) collective-permute-start(bf16[1024,128]{1,0:T(8,128)(2,1)S(1)} %get-tuple-element.76), channel_id=1, source_target_pairs={{0,1},{1,0},{2,3},{3,2},{4,5},{5,4},{6,7},{7,6},{8,9},{9,8},{10,11... | collective-permute-start | bytes 786440 | tf_op jit(solution)/shard_map/ppermute | solution.py:395
  33.1 7.5 %collective-permute-start.16 = (bf16[1024,128]{1,0:T(8,128)(2,1)S(1)}, bf16[1024,128]{1,0:T(8,128)(2,1)S(1)}, u32[]{:S(2)}, u32[]{:S(2)}) collective-permute-start(bf16[1024,128]{1,0:T(8,128)(2,1)S(1)} %get-tuple-element.75.refs_0_), channel_id=1, source_target_pairs={{0,2},{1,5},{2,0},{3,7},{4,6},{5,1},{6,4},{7,3},{8,10},{9,13},{10,... | collective-permute-start | bytes 786440 | tf_op jit(solution)/shard_map/ppermute | solution.py:395
  41.0 5.4 %collective-permute-start.21 = (bf16[640,128]{1,0:T(8,128)(2,1)S(1)}, bf16[640,128]{1,0:T(8,128)(2,1)S(1)}, u32[]{:S(2)}, u32[]{:S(2)}) collective-permute-start(bf16[640,128]{1,0:T(8,128)(2,1)S(1)} %get-tuple-element.83), channel_id=1, source_target_pairs={{0,4},{1,3},{2,6},{3,1},{4,0},{5,7},{6,2},{7,5},{8,12},{9,11},{10,... | collective-permute-start | bytes 491528 | tf_op jit(solution)/shard_map/ppermute | solution.py:395
  41.8 6.0 %collective-permute-start.22 = (bf16[640,128]{1,0:T(8,128)(2,1)S(1)}, bf16[640,128]{1,0:T(8,128)(2,1)S(1)}, u32[]{:S(2)}, u32[]{:S(2)}) collective-permute-start(bf16[640,128]{1,0:T(8,128)(2,1)S(1)} %get-tuple-element.84), channel_id=1, source_target_pairs={{0,5},{1,2},{2,7},{3,0},{4,1},{5,6},{6,3},{7,4},{8,13},{9,10},{10,... | collective-permute-start | bytes 491528 | tf_op jit(solution)/shard_map/ppermute | solution.py:395
  42.1 5.8 %collective-permute-start.23 = (bf16[640,128]{1,0:T(8,128)(2,1)S(1)}, bf16[640,128]{1,0:T(8,128)(2,1)S(1)}, u32[]{:S(2)}, u32[]{:S(2)}) collective-permute-start(bf16[640,128]{1,0:T(8,128)(2,1)S(1)} %get-tuple-element.85), channel_id=1, source_target_pairs={{0,1},{1,0},{2,3},{3,2},{4,5},{5,4},{6,7},{7,6},{8,9},{9,8},{10,11... | collective-permute-start | bytes 491528 | tf_op jit(solution)/shard_map/ppermute | solution.py:395
  43.9 5.6 %collective-permute-start.18 = (bf16[384,128]{1,0:T(8,128)(2,1)S(1)}, bf16[384,128]{1,0:T(8,128)(2,1)S(1)}, u32[]{:S(2)}, u32[]{:S(2)}) collective-permute-start(bf16[384,128]{1,0:T(8,128)(2,1)S(1)} %get-tuple-element.80), channel_id=1, source_target_pairs={{0,4},{1,3},{2,6},{3,1},{4,0},{5,7},{6,2},{7,5},{8,12},{9,11},{10,... | collective-permute-start | bytes 294920 | tf_op jit(solution)/shard_map/ppermute | solution.py:395
  44.5 5.1 %collective-permute-start.19 = (bf16[384,128]{1,0:T(8,128)(2,1)S(1)}, bf16[384,128]{1,0:T(8,128)(2,1)S(1)}, u32[]{:S(2)}, u32[]{:S(2)}) collective-permute-start(bf16[384,128]{1,0:T(8,128)(2,1)S(1)} %get-tuple-element.81), channel_id=1, source_target_pairs={{0,5},{1,2},{2,7},{3,0},{4,1},{5,6},{6,3},{7,4},{8,13},{9,10},{10,... | collective-permute-start | bytes 294920 | tf_op jit(solution)/shard_map/ppermute | solution.py:395
  46.4 3.2 %collective-permute-start.20 = (bf16[384,128]{1,0:T(8,128)(2,1)S(1)}, bf16[384,128]{1,0:T(8,128)(2,1)S(1)}, u32[]{:S(2)}, u32[]{:S(2)}) collective-permute-start(bf16[384,128]{1,0:T(8,128)(2,1)S(1)} %get-tuple-element.82), channel_id=1, source_target_pairs={{0,1},{1,0},{2,3},{3,2},{4,5},{5,4},{6,7},{7,6},{8,9},{9,8},{10,11... | collective-permute-start | bytes 294920 | tf_op jit(solution)/shard_map/ppermute | solution.py:395

commit v18 on v17

--- a/solution.py
+++ b/solution.py
@@ -95,17 +95,16 @@
     return lax.div(chip, grid[1]), lax.rem(chip, grid[1]), lax.rem(me, grid[2])
 
 
-def row_halves(full, core, pair):
-    half = full.shape[0] // pair
-    return [full.at[pl.ds(pl.multiple_of((core ^ j) * half, half), half), :] for j in range(pair)]
-
-
-def join_halves(parts, full, core, pair):
-    for half, terms in zip(row_halves(full, core, pair), parts):
-        total = terms[0][...].astype(F32)
-        for term in terms[1:]:
-            total += term[...].astype(F32)
-        half[...] = total.astype(BF16)
+def for_each_core(grid, body):
+    core = my_place(grid)[2]
+    for number in range(grid[2]):
+        pl.when(core == number)(functools.partial(body, number))
+
+
+def arrived_state(parts, core, head, count):
+    half, within = divmod(head, count)
+    terms = [term[within * HD : (within + 1) * HD, :].astype(F32) for term in parts[half ^ core]]
+    return sum(terms[1:], terms[0]).astype(BF16)
 
 
 def line_length(grid):
@@ -134,22 +133,25 @@
                 rows[at : at + 1, :] = jnp.full((1, HD), weight, F32)
 
 
-def own_states(piece, grid, keys, values, live, full, outs):
-    heads = full.shape[0] // HD
-    for head in range(heads):
-        cols = head_cols(piece * heads + head)
-        masked = jnp.where(live, keys[:, cols], jnp.zeros((), BF16))
-        full[head * HD : (head + 1) * HD, :] = tn(masked, values[:, cols]).astype(BF16)
-    for half, out in zip(row_halves(full, my_place(grid)[2], grid[2]), outs):
-        out[...] = half[...]
+def own_states(piece, grid, keys, values, live, outs):
+    def body(core):
+        count = outs[0].shape[0] // HD
+        for head in range(count * len(outs)):
+            half, within = divmod(head, count)
+            cols = head_cols(piece * count * len(outs) + head)
+            masked = jnp.where(live, keys[:, cols], jnp.zeros((), BF16))
+            outs[half ^ core][within * HD : (within + 1) * HD, :] = tn(masked, values[:, cols]).astype(BF16)
+
+    for_each_core(grid, body)
 
 
 def state_kernel(grid, seg_len, keys_hbm, values_hbm, parent_hbm, keys, values, length, up, down, *rest):
-    outs, (full, sems, parent, parent_sem) = rest[:-4], rest[-4:]
+    outs, (sems, parent, parent_sem) = rest[:-3], rest[-3:]
     rows, width = keys.shape
     chunk = rows // 2 if rows % 32 == 0 else rows
     steps = rows // chunk
-    spans = [slice(0, full.shape[0]), slice(full.shape[0], width)][:FORWARD_PIECES]
+    first = width // FORWARD_PIECES
+    spans = [slice(0, first), slice(first, width)][:FORWARD_PIECES]
     copies = []
     for number, cols in enumerate(spans):
         for step in range(steps):
@@ -168,14 +170,13 @@
     live = lax.broadcasted_iota(jnp.int32, (rows, HD), 0) < seg_len[0]
     for copy in copies[: 2 * steps]:
         copy.wait()
-    own_states(0, grid, keys, values, live, full, outs)
+    own_states(0, grid, keys, values, live, outs)
     for copy in copies[2 * steps :]:
         copy.wait()
 
 
-def next_state_kernel(piece, grid, length, keys, values, *rest):
-    outs, full = rest[:-1], rest[-1]
-    own_states(piece, grid, keys, values, live_rows(length, keys.shape[0]), full, outs)
+def next_state_kernel(piece, grid, length, keys, values, *outs):
+    own_states(piece, grid, keys, values, live_rows(length, keys.shape[0]), outs)
 
 
 def mix_kernel(sources, first, weights, *refs):
@@ -244,22 +245,27 @@
 def carry_kernel(piece, grid, counts, scale, length, queries, local, cotangent, gain, *rest):
     received, rest = rest[: sum(counts)], rest[sum(counts) :]
     before, (attention, sums, prefix) = rest[: (piece > 0)], rest[-3:]
-    join_halves(split_refs(received, *counts), prefix, my_place(grid)[2], grid[2])
-    rows, width = queries.shape[0], prefix.shape[0]
+    parts = split_refs(received, *counts)
+    rows, heads = queries.shape[0], prefix.shape[0] // HD
     factor = jnp.where(live_rows(length, rows), scale, 0.0)
-    squares = jnp.zeros((rows, HD), F32)
-    products = jnp.zeros((rows, HD), F32)
-    for head in range(width // HD):
-        whole = head_cols(piece * width // HD + head)
-        carried = nn(queries[:, whole], prefix[head * HD : (head + 1) * HD, :])
-        out = factor * (carried + local[:, whole])
-        attention[:, whole] = out
-        squares += out * out
-        products += out * (cotangent[:, whole].astype(F32) * gain[:, whole])
-    both = jnp.concatenate([token_rows(squares), token_rows(products)], axis=0)
-    for other in before:
-        both += other[...]
-    sums[...] = both
+
+    def body(core):
+        squares = jnp.zeros((rows, HD), F32)
+        products = jnp.zeros((rows, HD), F32)
+        for head in range(heads):
+            whole = head_cols(piece * heads + head)
+            state = arrived_state(parts, core, head, heads // grid[2])
+            prefix[head * HD : (head + 1) * HD, :] = state
+            out = factor * (nn(queries[:, whole], state) + local[:, whole])
+            attention[:, whole] = out
+            squares += out * out
+            products += out * (cotangent[:, whole].astype(F32) * gain[:, whole])
+        both = jnp.concatenate([token_rows(squares), token_rows(products)], axis=0)
+        for other in before:
+            both += other[...]
+        sums[...] = both
+
+    for_each_core(grid, body)
 
 
 def grad_kernel(groups, grid, scale, length, queries, cotangent, gain, attention, *rest):
@@ -276,16 +282,19 @@
     shrink = live_inverse * inverse * (inverse * total[1:2, :]) / features
     live_inverse = token_columns(live_inverse)
     shrink = token_columns(shrink)
-    core = my_place(grid)[2]
-    for flip, half in enumerate(halves):
-        height = half.shape[0]
-        first = (core ^ flip) * height
-        for head in range(height // HD):
-            cols = pl.ds(pl.multiple_of(first + head * HD, HD), HD)
+
+    def body(core):
+        count = halves[0].shape[0] // HD
+        for head in range(queries.shape[1] // HD):
+            cols = head_cols(head)
+            half, within = divmod(head, count)
             gain_grad = cotangent[:, cols].astype(F32) * gain[:, cols]
             grad = (live_inverse * gain_grad - attention[:, cols] * shrink).astype(BF16)
             grad_out[:, cols] = grad
-            half[head * HD : (head + 1) * HD, :] = (scale * tn(queries[:, cols], grad)).astype(BF16)
+            state = (scale * tn(queries[:, cols], grad)).astype(BF16)
+            halves[half ^ core][within * HD : (within + 1) * HD, :] = state
+
+    for_each_core(grid, body)
 
 
 def row_copies(source, target, sems):
@@ -334,31 +343,35 @@
 
 def final_kernel(begin, count, grid, counts, length, keys, values, key_part, value_part, *rest):
     received, rest = rest[: sum(counts)], rest[sum(counts) :]
-    key_hbm, value_hbm, key_grad, value_grad, below, sems = rest[-6:]
+    key_hbm, value_hbm, key_grad, value_grad, sems = rest[-5:]
+    parts = split_refs(received, *counts)
     pair = grid[2]
-    join_halves(split_refs(received, *counts), below, my_place(grid)[2], pair)
     rows = keys.shape[0]
     live = jnp.where(live_rows(length, rows), 1.0, 0.0)
-    copies, pending = [], 0
-    for head in range(pair * count):
-        half, within = divmod(head, count)
-        cols = head_cols(head)
-        place = half * (keys.shape[1] // HD // pair) + begin + within
-        whole = head_cols(place)
-        state = below[head * HD : (head + 1) * HD, :]
-        key_grad[:, cols] = (key_part[:, whole] + live * nt(values[:, whole], state)).astype(BF16)
-        value_grad[:, cols] = (value_part[:, whole] + live * nn(keys[:, whole], state)).astype(BF16)
-        pending += 1
-        if pending == 2 or within == count - 1:
-            done = slice((head + 1 - pending) * HD, (head + 1) * HD)
-            there = slice((place + 1 - pending) * HD, (place + 1) * HD)
-            pending = 0
-            for j, (src, dst) in enumerate(((key_grad, key_hbm), (value_grad, value_hbm))):
-                copy = pltpu.make_async_copy(src.at[:, done], dst.at[:, there], sems.at[j, head])
-                copy.start()
-                copies.append(copy)
-    for copy in copies:
-        copy.wait()
+
+    def body(core):
+        copies, pending = [], 0
+        for head in range(pair * count):
+            half, within = divmod(head, count)
+            cols = head_cols(head)
+            place = half * (keys.shape[1] // HD // pair) + begin + within
+            whole = head_cols(place)
+            state = arrived_state(parts, core, head, count)
+            key_grad[:, cols] = (key_part[:, whole] + live * nt(values[:, whole], state)).astype(BF16)
+            value_grad[:, cols] = (value_part[:, whole] + live * nn(keys[:, whole], state)).astype(BF16)
+            pending += 1
+            if pending == 2 or within == count - 1:
+                done = slice((head + 1 - pending) * HD, (head + 1) * HD)
+                there = slice((place + 1 - pending) * HD, (place + 1) * HD)
+                pending = 0
+                for j, (src, dst) in enumerate(((key_grad, key_hbm), (value_grad, value_hbm))):
+                    copy = pltpu.make_async_copy(src.at[:, done], dst.at[:, there], sems.at[j, head])
+                    copy.start()
+                    copies.append(copy)
+        for copy in copies:
+            copy.wait()
+
+    for_each_core(grid, body)
 
 
 def in_hbm(x):
@@ -452,26 +465,22 @@
     def flat(parts):
         return [block for part in parts for block in part]
 
-    state_scratch = pltpu.VMEM((features // FORWARD_PIECES, HD), BF16)
     key, value, length, up, down, *own = call(
         functools.partial(state_kernel, grid),
         [narrow, narrow, shape((1, rows), jnp.int32), weight_rows, weight_rows] + halves(FORWARD_PIECES),
         (seg_len, key_rows[0], values[0], parent[None]),
-        [state_scratch, sems, pltpu.SMEM((1, segs), jnp.int32), pltpu.SemaphoreType.DMA(())],
+        [sems, pltpu.SMEM((1, segs), jnp.int32), pltpu.SemaphoreType.DMA(())],
         unit * HD // FORWARD_PIECES, (1, 2, 3), (0,),
     )
     for piece in range(1, FORWARD_PIECES):
         own += call(
             functools.partial(next_state_kernel, piece, grid), halves(FORWARD_PIECES),
-            (length, key, value), [state_scratch], unit * HD // FORWARD_PIECES,
+            (length, key, value), (), unit * HD // FORWARD_PIECES,
         )
+    (query,) = call(fetch_kernel, [narrow], (queries[0],), [pltpu.SemaphoreType.DMA((4,))], 0, (0,), after=(own[0],))
     mixed = []
     for part in split_refs(own, *[pair] * FORWARD_PIECES):
-        mixed.append(mix(gather_line(part, grid), up, 0, part[0].shape[0], () if len(mixed) != 1 else (query,)))
-        if len(mixed) == 1:
-            (query,) = call(
-                fetch_kernel, [narrow], (queries[0],), [pltpu.SemaphoreType.DMA((4,))], 0, (0,), after=(mixed[0][0],)
-            )
+        mixed.append(mix(gather_line(part, grid), up, 0, part[0].shape[0], () if mixed else (query,)))
     (local,) = call(
         functools.partial(local_kernel, heads),
         [wide], (length, query, key, value), [mask], unit * rows * 2, after=(mixed[0][0],),
@@ -524,7 +533,7 @@
         results = call(
             functools.partial(final_kernel, begin, count, grid, counts),
             [narrow, narrow], operands,
-            [pltpu.VMEM((rows, width), BF16)] * 2 + [pltpu.VMEM((width, HD), BF16), sems],
+            [pltpu.VMEM((rows, width), BF16)] * 2 + [sems],
             2 * unit * HD * pair * count // heads,
             range(first, len(operands)), out_specs=[HBM, HBM],
             aliases={first + j: j for j in range(len(results))},

time: 51.4 us -> 49.7 us (0.967)
  waiting for transfers between devices: 10 us -> 8.36 us
  Pallas kernels: 18.3 us -> 17.7 us
    ppermute x21, waiting for transfers between devices: 6.21 us -> 4.56 us  [line_send(): return lax.ppermute(block, 'seg', moves)]
    pallas_call x15, Pallas kernels: 18.3 us -> 17.7 us  [call(): pl.pallas_call(kernel, out_shape=out_shape, in_specs=specs + [ANY] * len(...]
  transfers between devices with their start and end apart: 24 -> 24, of which waited for: 8 -> 7; matrix products, arithmetic and copies ran while one was open for 0% -> 0% of each run, Pallas kernels for 24% -> 25%
where the time goes in v18:
time: 49.7 us; the launch traced here: 49.4 us
  starting transfers between devices  21.7 us (44%)
  Pallas kernels  17.7 us (36%)
  waiting for transfers between devices  8.36 us (17%)
  between operations  1.65 us (3%)
    pallas_call x15, Pallas kernels, call(): pl.pallas_call(kernel, out_shape=out_shape, in_specs=specs + [ANY] * len(...  17.7 us
    ppermute x21, starting transfers between devices, line_send(): return lax.ppermute(block, 'seg', moves)  17.4 us
    ppermute x21, waiting for transfers between devices, line_send(): return lax.ppermute(block, 'seg', moves)  4.56 us
    ppermute x3, starting transfers between devices, token_sums(): parts.append(lax.ppermute(sums, 'head', moves))  4.24 us
    ppermute x3, waiting for transfers between devices, token_sums(): parts.append(lax.ppermute(sums, 'head', moves))  3.8 us
  transfers between devices with their start and end apart: 24, of which 7 were waited for; matrix products, arithmetic and copies ran while one was open for 0% of the time, Pallas kernels for 25%

profile of v18, /device:TPU:0, one launch (start us, length us, event | category | flops | bytes accessed | tf_op | source)
XLA Modules:
  0.0 49.4 jit_solution(15825056193857945199)
XLA Ops:
  1.3 1.9 %shard_map.102 = (bf16[256,2048]{1,0:T(8,128)(2,1)S(1)}, bf16[256,2048]{1,0:T(8,128)(2,1)S(1)}, s32[1,256]{1,0:T(1,128)S(1)}, f32[16,128]{1,0:T(8,128)S(1)}, f32...) custom-call(s32[1]{0:T(128)S(6)} %copy.17.seg_len, bf16[256,2048]{1,0:T(8,128)(2,1)} %bitcast.20, ...), custom_call_target="tpu_custom_call" | custom-call | flops 67108864 | bytes 4473892 | tf_op jit(solution)/shard_map/pallas_call | solution.py:386
  3.1 2.5 %collective-permute-start.2 = (bf16[512,128]{1,0:T(8,128)(2,1)S(1)}, bf16[512,128]{1,0:T(8,128)(2,1)S(1)}, u32[]{:S(2)}, u32[]{:S(2)}) collective-permute-start(bf16[512,128]{1,0:T(8,128)(2,1)S(1)} %get-tuple-element.52), channel_id=1, source_target_pairs={{0,5},{1,2},{2,7},{3,0},{4,1},{5,6},{6,3},{7,4},{8,13},{9,10},{10,... | collective-permute-start | bytes 393224 | tf_op jit(solution)/shard_map/ppermute | solution.py:408
  5.6 0.6 %collective-permute-start = (bf16[512,128]{1,0:T(8,128)(2,1)S(1)}, bf16[512,128]{1,0:T(8,128)(2,1)S(1)}, u32[]{:S(2)}, u32[]{:S(2)}) collective-permute-start(bf16[512,128]{1,0:T(8,128)(2,1)S(1)} %get-tuple-element.52), channel_id=1, source_target_pairs={{0,1},{1,0},{2,3},{3,2},{4,5},{5,4},{6,7},{7,6},{8,9},{9,8},{10,11... | collective-permute-start | bytes 393224 | tf_op jit(solution)/shard_map/ppermute | solution.py:408
  6.2 0.9 %collective-permute-start.1 = (bf16[512,128]{1,0:T(8,128)(2,1)S(1)}, bf16[512,128]{1,0:T(8,128)(2,1)S(1)}, u32[]{:S(2)}, u32[]{:S(2)}) collective-permute-start(bf16[512,128]{1,0:T(8,128)(2,1)S(1)} %get-tuple-element.48._.refs_0_), channel_id=1, source_target_pairs={{0,2},{1,5},{2,0},{3,7},{4,6},{5,1},{6,4},{7,3},{8,10},{9,13},{10,... | collective-permute-start | bytes 393224 | tf_op jit(solution)/shard_map/ppermute | solution.py:408
  7.1 0.4 shard_map.106
  7.5 1.2 %collective-permute-start.4 = (bf16[512,128]{1,0:T(8,128)(2,1)S(1)}, bf16[512,128]{1,0:T(8,128)(2,1)S(1)}, u32[]{:S(2)}, u32[]{:S(2)}) collective-permute-start(bf16[512,128]{1,0:T(8,128)(2,1)S(1)} %get-tuple-element.54.refs_0_), channel_id=1, source_target_pairs={{0,2},{1,5},{2,0},{3,7},{4,6},{5,1},{6,4},{7,3},{8,10},{9,13},{10,... | collective-permute-start | bytes 393224 | tf_op jit(solution)/shard_map/ppermute | solution.py:408
  8.7 0.6 %collective-permute-start.5 = (bf16[512,128]{1,0:T(8,128)(2,1)S(1)}, bf16[512,128]{1,0:T(8,128)(2,1)S(1)}, u32[]{:S(2)}, u32[]{:S(2)}) collective-permute-start(bf16[512,128]{1,0:T(8,128)(2,1)S(1)} %get-tuple-element.55), channel_id=1, source_target_pairs={{0,5},{1,2},{2,7},{3,0},{4,1},{5,6},{6,3},{7,4},{8,13},{9,10},{10,... | collective-permute-start | bytes 393224 | tf_op jit(solution)/shard_map/ppermute | solution.py:408
  9.3 1.2 %shard_map.103.refs_4_.queries = bf16[256,2048]{1,0:T(8,128)(2,1)S(1)} custom-call(bf16[256,2048]{1,0:T(8,128)(2,1)} %bitcast.19, bf16[512,128]{1,0:T(8,128)(2,1)S(1)} %get-tuple-element.48._.refs_0_), custom_call_target="tpu_custom_call" | custom-call | bytes 2097152 | tf_op jit(solution)/shard_map/pallas_call | solution.py:386
  10.5 0.0 collective-permute-done.2.refs_3_
  10.5 0.5 collective-permute-start.3
  11.0 0.0 collective-permute-done.refs_1_
  11.0 0.2 collective-permute-done.1.refs_2_
  11.2 0.3 shard_map.104
  11.5 1.6 %collective-permute-start.9 = (bf16[512,128]{1,0:T(8,128)(2,1)S(1)}, bf16[512,128]{1,0:T(8,128)(2,1)S(1)}, u32[]{:S(2)}, u32[]{:S(2)}) collective-permute-start(bf16[512,128]{1,0:T(8,128)(2,1)S(1)} %get-tuple-element.60), channel_id=1, source_target_pairs={{0,4},{1,3},{2,6},{3,1},{4,0},{5,7},{6,2},{7,5},{8,12},{9,11},{10,... | collective-permute-start | bytes 393224 | tf_op jit(solution)/shard_map/ppermute | solution.py:408
  13.1 0.3 collective-permute-start.10
  13.4 0.0 collective-permute-done.4.refs_2_
  13.5 0.7 %collective-permute-start.11 = (bf16[512,128]{1,0:T(8,128)(2,1)S(1)}, bf16[512,128]{1,0:T(8,128)(2,1)S(1)}, u32[]{:S(2)}, u32[]{:S(2)}) collective-permute-start(bf16[512,128]{1,0:T(8,128)(2,1)S(1)} %get-tuple-element.62), channel_id=1, source_target_pairs={{0,1},{1,0},{2,3},{3,2},{4,5},{5,4},{6,7},{7,6},{8,9},{9,8},{10,11... | collective-permute-start | bytes 393224 | tf_op jit(solution)/shard_map/ppermute | solution.py:408
  14.2 0.0 collective-permute-done.5.refs_3_
  14.2 0.0 collective-permute-done.3.refs_1_
  14.2 0.3 shard_map.107
  14.5 1.4 %collective-permute-start.6 = (bf16[512,128]{1,0:T(8,128)(2,1)S(1)}, bf16[512,128]{1,0:T(8,128)(2,1)S(1)}, u32[]{:S(2)}, u32[]{:S(2)}) collective-permute-start(bf16[512,128]{1,0:T(8,128)(2,1)S(1)} %get-tuple-element.56), channel_id=1, source_target_pairs={{0,4},{1,3},{2,6},{3,1},{4,0},{5,7},{6,2},{7,5},{8,12},{9,11},{10,... | collective-permute-start | bytes 393224 | tf_op jit(solution)/shard_map/ppermute | solution.py:408
  15.9 0.9 %collective-permute-start.7 = (bf16[512,128]{1,0:T(8,128)(2,1)S(1)}, bf16[512,128]{1,0:T(8,128)(2,1)S(1)}, u32[]{:S(2)}, u32[]{:S(2)}) collective-permute-start(bf16[512,128]{1,0:T(8,128)(2,1)S(1)} %get-tuple-element.58), channel_id=1, source_target_pairs={{0,5},{1,2},{2,7},{3,0},{4,1},{5,6},{6,3},{7,4},{8,13},{9,10},{10,... | collective-permute-start | bytes 393224 | tf_op jit(solution)/shard_map/ppermute | solution.py:408
  16.8 0.0 collective-permute-done.9.rest_0_
  16.8 0.3 collective-permute-start.8
  17.1 1.5 %shard_map.105.local = f32[256,2048]{1,0:T(8,128)S(1)} custom-call(s32[1,256]{1,0:T(1,128)S(1)} %get-tuple-element.47.length, bf16[256,2048]{1,0:T(8,128)(2,1)S(1)} %shard_map.103.refs_4_.queries, bf16[256,2048]{1,0:T(8,128)(2,1)S(1)} %get-tuple-element.49.keys, bf16[256,2048]{1,0:T(8,128)(2,1)S(1)} %get-tuple-element.50.values, ...), custom_call_target="tpu_custom_call" | custom-call | flops 536870912 | bytes 5243904 | tf_op jit(solution)/shard_map/pallas_call | solution.py:386
  18.6 0.0 collective-permute-done.10.rest_2_
  18.6 0.0 collective-permute-done.11.rest_3_
  18.6 0.0 copy-done
  18.6 0.6 %shard_map.108 = (f32[256,2048]{1,0:T(8,128)S(1)}, f32[2,256]{1,0:T(2,128)S(1)}, bf16[1024,128]{1,0:T(8,128)(2,1)S(1)}) custom-call(s32[1,256]{1,0:T(1,128)S(1)} %get-tuple-element.47.length, bf16[256,2048]{1,0:T(8,128)(2,1)S(1)} %shard_map.103.refs_4_.queries, f32[256,2048]{1,0:T(8,128)S(1)} %shard_map.105.local, bf16[256,2048]{1,0:T(8,128)(2,1)S(1)} %bitcast.10, ...), custom_call_target="tpu_custom_call" | custom-call | flops 67108864 | bytes 7089152 | tf_op jit(solution)/shard_map/pallas_call | solution.py:386
  19.2 0.3 collective-permute-done.6.rest_0_
  19.5 0.8 %collective-permute-done.7.rest_2_ = bf16[512,128]{1,0:T(8,128)(2,1)S(1)} collective-permute-done((bf16[512,128]{1,0:T(8,128)(2,1)S(1)}, bf16[512,128]{1,0:T(8,128)(2,1)S(1)}, u32[]{:S(2)}, u32[]{:S(2)}) %collective-permute-start.7) | collective-permute-done | bytes 131104 | tf_op jit(solution)/shard_map/ppermute | solution.py:408
  20.3 0.0 collective-permute-done.8.rest_3_
  20.3 0.6 %shard_map.109 = (f32[256,2048]{1,0:T(8,128)S(1)}, f32[2,256]{1,0:T(2,128)S(1)}, bf16[1024,128]{1,0:T(8,128)(2,1)S(1)}) custom-call(s32[1,256]{1,0:T(1,128)S(1)} %get-tuple-element.47.length, bf16[256,2048]{1,0:T(8,128)(2,1)S(1)} %shard_map.103.refs_4_.queries, f32[256,2048]{1,0:T(8,128)S(1)} %shard_map.105.local, ...), custom_call_target="tpu_custom_call", output_to_operand_aliasing={{0}: (10, {})} | custom-call | flops 67108864 | bytes 9188352 | tf_op jit(solution)/shard_map/pallas_call | solution.py:386
  20.9 2.7 %collective-permute-start.14 = (f32[2,256]{1,0:T(2,128)S(1)}, f32[2,256]{1,0:T(2,128)S(1)}, u32[]{:S(2)}, u32[]{:S(2)}) collective-permute-start(f32[2,256]{1,0:T(2,128)S(1)} %get-tuple-element.66.rest_0_), channel_id=1, source_target_pairs={{0,16},{8,24},{16,0},{24,8},{1,17},{9,25},{17,1},{25,9},{2,18},{10... | collective-permute-start | bytes 6152 | tf_op jit(solution)/shard_map/ppermute | solution.py:435
  23.6 1.3 %collective-permute-start.13 = (f32[2,256]{1,0:T(2,128)S(1)}, f32[2,256]{1,0:T(2,128)S(1)}, u32[]{:S(2)}, u32[]{:S(2)}) collective-permute-start(f32[2,256]{1,0:T(2,128)S(1)} %get-tuple-element.66.rest_0_), channel_id=1, source_target_pairs={{0,24},{8,16},{16,8},{24,0},{1,25},{9,17},{17,9},{25,1},{2,26},{10... | collective-permute-start | bytes 6152 | tf_op jit(solution)/shard_map/ppermute | solution.py:435
  24.9 0.2 collective-permute-start.12
  25.1 0.3 collective-permute-done.14.rest_3_
  25.4 3.5 %collective-permute-done.13.rest_2_ = f32[2,256]{1,0:T(2,128)S(1)} collective-permute-done((f32[2,256]{1,0:T(2,128)S(1)}, f32[2,256]{1,0:T(2,128)S(1)}, u32[]{:S(2)}, u32[]{:S(2)}) %collective-permute-start.13) | collective-permute-done | bytes 2080 | tf_op jit(solution)/shard_map/ppermute | solution.py:435
  28.9 0.0 collective-permute-done.12.rest_1_
  28.9 1.1 %shard_map.110 = (bf16[256,2048]{1,0:T(8,128)(2,1)S(1)}, f32[1,256]{1,0:T(1,128)S(1)}, bf16[1024,128]{1,0:T(8,128)(2,1)S(1)}, bf16[1024,128]{1,0:T(8,128)(2,1)S(1)}) custom-call(s32[1,256]{1,0:T(1,128)S(1)} %get-tuple-element.47.length, bf16[256,2048]{1,0:T(8,128)(2,1)S(1)} %shard_map.103.refs_4_.queries, bf16[256,2048]{1,0:T(8,128)(2,1)S(1)} %bitcast.12, ...), custom_call_target="tpu_custom_call" | custom-call | flops 134217728 | bytes 5785600 | tf_op jit(solution)/shard_map/pallas_call | solution.py:386
  30.0 0.2 collective-permute-start.17
  30.3 1.2 %collective-permute-start.15 = (bf16[1024,128]{1,0:T(8,128)(2,1)S(1)}, bf16[1024,128]{1,0:T(8,128)(2,1)S(1)}, u32[]{:S(2)}, u32[]{:S(2)}) collective-permute-start(bf16[1024,128]{1,0:T(8,128)(2,1)S(1)} %get-tuple-element.76), channel_id=1, source_target_pairs={{0,1},{1,0},{2,3},{3,2},{4,5},{5,4},{6,7},{7,6},{8,9},{9,8},{10,11... | collective-permute-start | bytes 786440 | tf_op jit(solution)/shard_map/ppermute | solution.py:408
  31.4 1.0 %collective-permute-start.16 = (bf16[1024,128]{1,0:T(8,128)(2,1)S(1)}, bf16[1024,128]{1,0:T(8,128)(2,1)S(1)}, u32[]{:S(2)}, u32[]{:S(2)}) collective-permute-start(bf16[1024,128]{1,0:T(8,128)(2,1)S(1)} %get-tuple-element.75.refs_0_), channel_id=1, source_target_pairs={{0,2},{1,5},{2,0},{3,7},{4,6},{5,1},{6,4},{7,3},{8,10},{9,13},{10,... | collective-permute-start | bytes 786440 | tf_op jit(solution)/shard_map/ppermute | solution.py:408
  32.4 4.8 %shard_map.111 = (bf16[256,2048]{1,0:T(8,128)(2,1)}, bf16[256,2048]{1,0:T(8,128)(2,1)}, f32[256,2048]{1,0:T(8,128)S(1)}, f32[8,128]{1,0:T(8,128)S(1)}) custom-call(s32[1,256]{1,0:T(1,128)S(1)} %get-tuple-element.47.length, f32[1,256]{1,0:T(1,128)S(1)} %get-tuple-element.67.inverse_rms, f32[1,2048]{1,0:T(1,128)S(1)} %bitcast.16, ...), custom_call_target="tpu_custom_call" | custom-call | flops 939524096 | bytes 11024384 | tf_op jit(solution)/shard_map/pallas_call | solution.py:386
  37.2 0.0 collective-permute-done.17.refs_3_
  37.2 0.0 collective-permute-done.15.refs_1_
  37.2 1.6 %collective-permute-done.16.refs_2_ = bf16[1024,128]{1,0:T(8,128)(2,1)S(1)} collective-permute-done((bf16[1024,128]{1,0:T(8,128)(2,1)S(1)}, bf16[1024,128]{1,0:T(8,128)(2,1)S(1)}, u32[]{:S(2)}, u32[]{:S(2)}) %collective-permute-start.16) | collective-permute-done | bytes 262176 | tf_op jit(solution)/shard_map/ppermute | solution.py:408
  38.9 0.4 shard_map.112
  39.2 1.0 %collective-permute-start.21 = (bf16[640,128]{1,0:T(8,128)(2,1)S(1)}, bf16[640,128]{1,0:T(8,128)(2,1)S(1)}, u32[]{:S(2)}, u32[]{:S(2)}) collective-permute-start(bf16[640,128]{1,0:T(8,128)(2,1)S(1)} %get-tuple-element.83), channel_id=1, source_target_pairs={{0,4},{1,3},{2,6},{3,1},{4,0},{5,7},{6,2},{7,5},{8,12},{9,11},{10,... | collective-permute-start | bytes 491528 | tf_op jit(solution)/shard_map/ppermute | solution.py:408
  40.3 0.1 collective-permute-start.22
  40.4 1.6 %collective-permute-start.23 = (bf16[640,128]{1,0:T(8,128)(2,1)S(1)}, bf16[640,128]{1,0:T(8,128)(2,1)S(1)}, u32[]{:S(2)}, u32[]{:S(2)}) collective-permute-start(bf16[640,128]{1,0:T(8,128)(2,1)S(1)} %get-tuple-element.85), channel_id=1, source_target_pairs={{0,1},{1,0},{2,3},{3,2},{4,5},{5,4},{6,7},{7,6},{8,9},{9,8},{10,11... | collective-permute-start | bytes 491528 | tf_op jit(solution)/shard_map/ppermute | solution.py:408
  42.0 0.2 shard_map.113
  42.2 0.6 %collective-permute-start.18 = (bf16[384,128]{1,0:T(8,128)(2,1)S(1)}, bf16[384,128]{1,0:T(8,128)(2,1)S(1)}, u32[]{:S(2)}, u32[]{:S(2)}) collective-permute-start(bf16[384,128]{1,0:T(8,128)(2,1)S(1)} %get-tuple-element.80), channel_id=1, source_target_pairs={{0,4},{1,3},{2,6},{3,1},{4,0},{5,7},{6,2},{7,5},{8,12},{9,11},{10,... | collective-permute-start | bytes 294920 | tf_op jit(solution)/shard_map/ppermute | solution.py:408
  42.8 0.3 collective-permute-start.19
  43.1 1.5 %collective-permute-done.21.rest_0_ = bf16[640,128]{1,0:T(8,128)(2,1)S(1)} collective-permute-done((bf16[640,128]{1,0:T(8,128)(2,1)S(1)}, bf16[640,128]{1,0:T(8,128)(2,1)S(1)}, u32[]{:S(2)}, u32[]{:S(2)}) %collective-permute-start.21) | collective-permute-done | bytes 163872 | tf_op jit(solution)/shard_map/ppermute | solution.py:408
  44.6 0.0 collective-permute-start.20
  44.6 1.5 %shard_map.114.value_part = f32[256,2048]{1,0:T(8,128)S(1)} custom-call(s32[1,256]{1,0:T(1,128)S(1)} %get-tuple-element.47.length, bf16[256,2048]{1,0:T(8,128)(2,1)S(1)} %shard_map.103.refs_4_.queries, bf16[256,2048]{1,0:T(8,128)(2,1)S(1)} %get-tuple-element.49.keys, bf16[256,2048]{1,0:T(8,128)(2,1)S(1)} %get-tuple-element.68.grads, ...), custom_call_target="tpu_custom_call" | custom-call | flops 536870912 | bytes 5243904 | tf_op jit(solution)/shard_map/pallas_call | solution.py:386
  46.1 0.0 collective-permute-done.22.rest_2_
  46.1 0.0 collective-permute-done.23.rest_3_
  46.1 1.7 %shard_map.115 = (bf16[256,2048]{1,0:T(8,128)(2,1)}, bf16[256,2048]{1,0:T(8,128)(2,1)}) custom-call(s32[1,256]{1,0:T(1,128)S(1)} %get-tuple-element.47.length, bf16[256,2048]{1,0:T(8,128)(2,1)S(1)} %get-tuple-element.49.keys, bf16[256,2048]{1,0:T(8,128)(2,1)S(1)} %get-tuple-element.50.values, f32[256,2048]{1,0:T(8,128)S(1)} %get-tuple-element.73.key_part, ...), custom_call_target="tpu_custom_call" | custom-call | flops 167772160 | bytes 9044992 | tf_op jit(solution)/shard_map/pallas_call | solution.py:386
  47.8 0.0 collective-permute-done.18.rest_0_
  47.8 0.0 collective-permute-done.19.rest_2_
  47.8 0.0 collective-permute-done.20.rest_3_
  47.9 1.4 %shard_map.116 = (bf16[256,2048]{1,0:T(8,128)(2,1)}, bf16[256,2048]{1,0:T(8,128)(2,1)}) custom-call(s32[1,256]{1,0:T(1,128)S(1)} %get-tuple-element.47.length, bf16[256,2048]{1,0:T(8,128)(2,1)S(1)} %get-tuple-element.49.keys, bf16[256,2048]{1,0:T(8,128)(2,1)S(1)} %get-tuple-element.50.values, ...), custom_call_target="tpu_custom_call", output_to_operand_aliasing={{0}: (9, {}), {1}: (10, {})} | custom-call | flops 100663296 | bytes 10880000 | tf_op jit(solution)/shard_map/pallas_call | solution.py:386
  (3 shorter events, 0.0 us)
Async XLA Ops:
  3.1 7.4 %collective-permute-start.2 = (bf16[512,128]{1,0:T(8,128)(2,1)S(1)}, bf16[512,128]{1,0:T(8,128)(2,1)S(1)}, u32[]{:S(2)}, u32[]{:S(2)}) collective-permute-start(bf16[512,128]{1,0:T(8,128)(2,1)S(1)} %get-tuple-element.52), channel_id=1, source_target_pairs={{0,5},{1,2},{2,7},{3,0},{4,1},{5,6},{6,3},{7,4},{8,13},{9,10},{10,... | collective-permute-start | bytes 393224 | tf_op jit(solution)/shard_map/ppermute | solution.py:408
  5.6 5.4 %collective-permute-start = (bf16[512,128]{1,0:T(8,128)(2,1)S(1)}, bf16[512,128]{1,0:T(8,128)(2,1)S(1)}, u32[]{:S(2)}, u32[]{:S(2)}) collective-permute-start(bf16[512,128]{1,0:T(8,128)(2,1)S(1)} %get-tuple-element.52), channel_id=1, source_target_pairs={{0,1},{1,0},{2,3},{3,2},{4,5},{5,4},{6,7},{7,6},{8,9},{9,8},{10,11... | collective-permute-start | bytes 393224 | tf_op jit(solution)/shard_map/ppermute | solution.py:408
  6.2 5.0 %collective-permute-start.1 = (bf16[512,128]{1,0:T(8,128)(2,1)S(1)}, bf16[512,128]{1,0:T(8,128)(2,1)S(1)}, u32[]{:S(2)}, u32[]{:S(2)}) collective-permute-start(bf16[512,128]{1,0:T(8,128)(2,1)S(1)} %get-tuple-element.48._.refs_0_), channel_id=1, source_target_pairs={{0,2},{1,5},{2,0},{3,7},{4,6},{5,1},{6,4},{7,3},{8,10},{9,13},{10,... | collective-permute-start | bytes 393224 | tf_op jit(solution)/shard_map/ppermute | solution.py:408
  7.5 6.0 %collective-permute-start.4 = (bf16[512,128]{1,0:T(8,128)(2,1)S(1)}, bf16[512,128]{1,0:T(8,128)(2,1)S(1)}, u32[]{:S(2)}, u32[]{:S(2)}) collective-permute-start(bf16[512,128]{1,0:T(8,128)(2,1)S(1)} %get-tuple-element.54.refs_0_), channel_id=1, source_target_pairs={{0,2},{1,5},{2,0},{3,7},{4,6},{5,1},{6,4},{7,3},{8,10},{9,13},{10,... | collective-permute-start | bytes 393224 | tf_op jit(solution)/shard_map/ppermute | solution.py:408
  8.7 5.5 %collective-permute-start.5 = (bf16[512,128]{1,0:T(8,128)(2,1)S(1)}, bf16[512,128]{1,0:T(8,128)(2,1)S(1)}, u32[]{:S(2)}, u32[]{:S(2)}) collective-permute-start(bf16[512,128]{1,0:T(8,128)(2,1)S(1)} %get-tuple-element.55), channel_id=1, source_target_pairs={{0,5},{1,2},{2,7},{3,0},{4,1},{5,6},{6,3},{7,4},{8,13},{9,10},{10,... | collective-permute-start | bytes 393224 | tf_op jit(solution)/shard_map/ppermute | solution.py:408
  10.5 3.7 %collective-permute-start.3 = (bf16[512,128]{1,0:T(8,128)(2,1)S(1)}, bf16[512,128]{1,0:T(8,128)(2,1)S(1)}, u32[]{:S(2)}, u32[]{:S(2)}) collective-permute-start(bf16[512,128]{1,0:T(8,128)(2,1)S(1)} %get-tuple-element.55), channel_id=1, source_target_pairs={{0,1},{1,0},{2,3},{3,2},{4,5},{5,4},{6,7},{7,6},{8,9},{9,8},{10,11... | collective-permute-start | bytes 393224 | tf_op jit(solution)/shard_map/ppermute | solution.py:408
  11.5 5.3 %collective-permute-start.9 = (bf16[512,128]{1,0:T(8,128)(2,1)S(1)}, bf16[512,128]{1,0:T(8,128)(2,1)S(1)}, u32[]{:S(2)}, u32[]{:S(2)}) collective-permute-start(bf16[512,128]{1,0:T(8,128)(2,1)S(1)} %get-tuple-element.60), channel_id=1, source_target_pairs={{0,4},{1,3},{2,6},{3,1},{4,0},{5,7},{6,2},{7,5},{8,12},{9,11},{10,... | collective-permute-start | bytes 393224 | tf_op jit(solution)/shard_map/ppermute | solution.py:408
  13.1 5.5 %collective-permute-start.10 = (bf16[512,128]{1,0:T(8,128)(2,1)S(1)}, bf16[512,128]{1,0:T(8,128)(2,1)S(1)}, u32[]{:S(2)}, u32[]{:S(2)}) collective-permute-start(bf16[512,128]{1,0:T(8,128)(2,1)S(1)} %get-tuple-element.61), channel_id=1, source_target_pairs={{0,5},{1,2},{2,7},{3,0},{4,1},{5,6},{6,3},{7,4},{8,13},{9,10},{10,... | collective-permute-start | bytes 393224 | tf_op jit(solution)/shard_map/ppermute | solution.py:408
  13.5 5.1 %collective-permute-start.11 = (bf16[512,128]{1,0:T(8,128)(2,1)S(1)}, bf16[512,128]{1,0:T(8,128)(2,1)S(1)}, u32[]{:S(2)}, u32[]{:S(2)}) collective-permute-start(bf16[512,128]{1,0:T(8,128)(2,1)S(1)} %get-tuple-element.62), channel_id=1, source_target_pairs={{0,1},{1,0},{2,3},{3,2},{4,5},{5,4},{6,7},{7,6},{8,9},{9,8},{10,11... | collective-permute-start | bytes 393224 | tf_op jit(solution)/shard_map/ppermute | solution.py:408
  14.5 5.0 %collective-permute-start.6 = (bf16[512,128]{1,0:T(8,128)(2,1)S(1)}, bf16[512,128]{1,0:T(8,128)(2,1)S(1)}, u32[]{:S(2)}, u32[]{:S(2)}) collective-permute-start(bf16[512,128]{1,0:T(8,128)(2,1)S(1)} %get-tuple-element.56), channel_id=1, source_target_pairs={{0,4},{1,3},{2,6},{3,1},{4,0},{5,7},{6,2},{7,5},{8,12},{9,11},{10,... | collective-permute-start | bytes 393224 | tf_op jit(solution)/shard_map/ppermute | solution.py:408
  15.9 4.4 %collective-permute-start.7 = (bf16[512,128]{1,0:T(8,128)(2,1)S(1)}, bf16[512,128]{1,0:T(8,128)(2,1)S(1)}, u32[]{:S(2)}, u32[]{:S(2)}) collective-permute-start(bf16[512,128]{1,0:T(8,128)(2,1)S(1)} %get-tuple-element.58), channel_id=1, source_target_pairs={{0,5},{1,2},{2,7},{3,0},{4,1},{5,6},{6,3},{7,4},{8,13},{9,10},{10,... | collective-permute-start | bytes 393224 | tf_op jit(solution)/shard_map/ppermute | solution.py:408
  16.8 3.5 %collective-permute-start.8 = (bf16[512,128]{1,0:T(8,128)(2,1)S(1)}, bf16[512,128]{1,0:T(8,128)(2,1)S(1)}, u32[]{:S(2)}, u32[]{:S(2)}) collective-permute-start(bf16[512,128]{1,0:T(8,128)(2,1)S(1)} %get-tuple-element.59), channel_id=1, source_target_pairs={{0,1},{1,0},{2,3},{3,2},{4,5},{5,4},{6,7},{7,6},{8,9},{9,8},{10,11... | collective-permute-start | bytes 393224 | tf_op jit(solution)/shard_map/ppermute | solution.py:408
  17.1 1.5 %copy-start = (bf16[1,256,2048]{2,1,0:T(8,128)(2,1)S(1)}, bf16[1,256,2048]{2,1,0:T(8,128)(2,1)}, u32[]{:S(2)}) copy-start(bf16[1,256,2048]{2,1,0:T(8,128)(2,1)} %param.10) | copy-start | bytes 3145732
  17.1 1.5 %copy-start.1 = (f32[2048]{0:T(1024)S(1)}, f32[2048]{0:T(1024)}, u32[]{:S(2)}) copy-start(f32[2048]{0:T(1024)} %param.11) | copy-start | bytes 24580
  20.9 4.5 %collective-permute-start.14 = (f32[2,256]{1,0:T(2,128)S(1)}, f32[2,256]{1,0:T(2,128)S(1)}, u32[]{:S(2)}, u32[]{:S(2)}) collective-permute-start(f32[2,256]{1,0:T(2,128)S(1)} %get-tuple-element.66.rest_0_), channel_id=1, source_target_pairs={{0,16},{8,24},{16,0},{24,8},{1,17},{9,25},{17,1},{25,9},{2,18},{10... | collective-permute-start | bytes 6152 | tf_op jit(solution)/shard_map/ppermute | solution.py:435
  23.6 5.4 %collective-permute-start.13 = (f32[2,256]{1,0:T(2,128)S(1)}, f32[2,256]{1,0:T(2,128)S(1)}, u32[]{:S(2)}, u32[]{:S(2)}) collective-permute-start(f32[2,256]{1,0:T(2,128)S(1)} %get-tuple-element.66.rest_0_), channel_id=1, source_target_pairs={{0,24},{8,16},{16,8},{24,0},{1,25},{9,17},{17,9},{25,1},{2,26},{10... | collective-permute-start | bytes 6152 | tf_op jit(solution)/shard_map/ppermute | solution.py:435
  24.9 4.0 %collective-permute-start.12 = (f32[2,256]{1,0:T(2,128)S(1)}, f32[2,256]{1,0:T(2,128)S(1)}, u32[]{:S(2)}, u32[]{:S(2)}) collective-permute-start(f32[2,256]{1,0:T(2,128)S(1)} %get-tuple-element.66.rest_0_), channel_id=1, source_target_pairs={{0,8},{8,0},{16,24},{24,16},{1,9},{9,1},{17,25},{25,17},{2,10},{10... | collective-permute-start | bytes 6152 | tf_op jit(solution)/shard_map/ppermute | solution.py:435
  30.0 7.2 %collective-permute-start.17 = (bf16[1024,128]{1,0:T(8,128)(2,1)S(1)}, bf16[1024,128]{1,0:T(8,128)(2,1)S(1)}, u32[]{:S(2)}, u32[]{:S(2)}) collective-permute-start(bf16[1024,128]{1,0:T(8,128)(2,1)S(1)} %get-tuple-element.76), channel_id=1, source_target_pairs={{0,5},{1,2},{2,7},{3,0},{4,1},{5,6},{6,3},{7,4},{8,13},{9,10},{10,... | collective-permute-start | bytes 786440 | tf_op jit(solution)/shard_map/ppermute | solution.py:408
  30.3 6.9 %collective-permute-start.15 = (bf16[1024,128]{1,0:T(8,128)(2,1)S(1)}, bf16[1024,128]{1,0:T(8,128)(2,1)S(1)}, u32[]{:S(2)}, u32[]{:S(2)}) collective-permute-start(bf16[1024,128]{1,0:T(8,128)(2,1)S(1)} %get-tuple-element.76), channel_id=1, source_target_pairs={{0,1},{1,0},{2,3},{3,2},{4,5},{5,4},{6,7},{7,6},{8,9},{9,8},{10,11... | collective-permute-start | bytes 786440 | tf_op jit(solution)/shard_map/ppermute | solution.py:408
  31.4 7.4 %collective-permute-start.16 = (bf16[1024,128]{1,0:T(8,128)(2,1)S(1)}, bf16[1024,128]{1,0:T(8,128)(2,1)S(1)}, u32[]{:S(2)}, u32[]{:S(2)}) collective-permute-start(bf16[1024,128]{1,0:T(8,128)(2,1)S(1)} %get-tuple-element.75.refs_0_), channel_id=1, source_target_pairs={{0,2},{1,5},{2,0},{3,7},{4,6},{5,1},{6,4},{7,3},{8,10},{9,13},{10,... | collective-permute-start | bytes 786440 | tf_op jit(solution)/shard_map/ppermute | solution.py:408
  39.2 5.4 %collective-permute-start.21 = (bf16[640,128]{1,0:T(8,128)(2,1)S(1)}, bf16[640,128]{1,0:T(8,128)(2,1)S(1)}, u32[]{:S(2)}, u32[]{:S(2)}) collective-permute-start(bf16[640,128]{1,0:T(8,128)(2,1)S(1)} %get-tuple-element.83), channel_id=1, source_target_pairs={{0,4},{1,3},{2,6},{3,1},{4,0},{5,7},{6,2},{7,5},{8,12},{9,11},{10,... | collective-permute-start | bytes 491528 | tf_op jit(solution)/shard_map/ppermute | solution.py:408
  40.3 5.8 %collective-permute-start.22 = (bf16[640,128]{1,0:T(8,128)(2,1)S(1)}, bf16[640,128]{1,0:T(8,128)(2,1)S(1)}, u32[]{:S(2)}, u32[]{:S(2)}) collective-permute-start(bf16[640,128]{1,0:T(8,128)(2,1)S(1)} %get-tuple-element.84), channel_id=1, source_target_pairs={{0,5},{1,2},{2,7},{3,0},{4,1},{5,6},{6,3},{7,4},{8,13},{9,10},{10,... | collective-permute-start | bytes 491528 | tf_op jit(solution)/shard_map/ppermute | solution.py:408
  40.4 5.7 %collective-permute-start.23 = (bf16[640,128]{1,0:T(8,128)(2,1)S(1)}, bf16[640,128]{1,0:T(8,128)(2,1)S(1)}, u32[]{:S(2)}, u32[]{:S(2)}) collective-permute-start(bf16[640,128]{1,0:T(8,128)(2,1)S(1)} %get-tuple-element.85), channel_id=1, source_target_pairs={{0,1},{1,0},{2,3},{3,2},{4,5},{5,4},{6,7},{7,6},{8,9},{9,8},{10,11... | collective-permute-start | bytes 491528 | tf_op jit(solution)/shard_map/ppermute | solution.py:408
  42.2 5.6 %collective-permute-start.18 = (bf16[384,128]{1,0:T(8,128)(2,1)S(1)}, bf16[384,128]{1,0:T(8,128)(2,1)S(1)}, u32[]{:S(2)}, u32[]{:S(2)}) collective-permute-start(bf16[384,128]{1,0:T(8,128)(2,1)S(1)} %get-tuple-element.80), channel_id=1, source_target_pairs={{0,4},{1,3},{2,6},{3,1},{4,0},{5,7},{6,2},{7,5},{8,12},{9,11},{10,... | collective-permute-start | bytes 294920 | tf_op jit(solution)/shard_map/ppermute | solution.py:408
  42.8 5.1 %collective-permute-start.19 = (bf16[384,128]{1,0:T(8,128)(2,1)S(1)}, bf16[384,128]{1,0:T(8,128)(2,1)S(1)}, u32[]{:S(2)}, u32[]{:S(2)}) collective-permute-start(bf16[384,128]{1,0:T(8,128)(2,1)S(1)} %get-tuple-element.81), channel_id=1, source_target_pairs={{0,5},{1,2},{2,7},{3,0},{4,1},{5,6},{6,3},{7,4},{8,13},{9,10},{10,... | collective-permute-start | bytes 294920 | tf_op jit(solution)/shard_map/ppermute | solution.py:408
  44.6 3.2 %collective-permute-start.20 = (bf16[384,128]{1,0:T(8,128)(2,1)S(1)}, bf16[384,128]{1,0:T(8,128)(2,1)S(1)}, u32[]{:S(2)}, u32[]{:S(2)}) collective-permute-start(bf16[384,128]{1,0:T(8,128)(2,1)S(1)} %get-tuple-element.82), channel_id=1, source_target_pairs={{0,1},{1,0},{2,3},{3,2},{4,5},{5,4},{6,7},{7,6},{8,9},{9,8},{10,11... | collective-permute-start | bytes 294920 | tf_op jit(solution)/shard_map/ppermute | solution.py:408

commit v19 on v18

--- a/solution.py
+++ b/solution.py
@@ -15,6 +15,7 @@
 BF16 = jnp.bfloat16
 VMEM_LIMIT = 24 * 1024 * 1024
 FORWARD_PIECES = 2
+VALUE_PIECES = 2
 
 VMEM = pl.BlockSpec(memory_space=pltpu.VMEM)
 SMEM = pl.BlockSpec(memory_space=pltpu.SMEM)
@@ -304,10 +305,10 @@
     return [pltpu.make_async_copy(source.at[p, :], target.at[p, :], sems.at[j]) for j, p in enumerate(parts)]
 
 
-def query_kernel(heads, group, scale, length, inverse_rms, gain, queries, keys, values, grads, attention, *rest):
+def query_kernel(heads, group, scale, length, inverse_rms, gain, queries, keys, values, grads, attention, block, *rest):
     prefix, rest = split_refs(rest, FORWARD_PIECES, len(rest) - FORWARD_PIECES)
     attended_hbm, query_hbm, key_part, token, attended, query_grad, keep, sems = rest
-    token[...] = jnp.zeros_like(token)
+    token[...] = block[...]
     write_mask(length, keep, False)
     inverse = token_columns(inverse_rms[...])
     copies = []
@@ -332,17 +333,17 @@
         copy.wait()
 
 
-def value_kernel(heads, scale, length, queries, keys, grads, *rest):
+def value_kernel(first, scale, length, queries, keys, grads, *rest):
     value_part, keep = rest[-2:]
     write_mask(length, keep, True)
-    for head in range(heads):
-        cols = head_cols(head)
-        turned = nt(keys[:, cols], queries[:, cols]).astype(BF16) * keep[...]
-        value_part[:, cols] = scale * nn(turned, grads[:, cols])
-
-
-def final_kernel(begin, count, grid, counts, length, keys, values, key_part, value_part, *rest):
-    received, rest = rest[: sum(counts)], rest[sum(counts) :]
+    for head in range(value_part.shape[1] // HD):
+        whole = head_cols(first + head)
+        turned = nt(keys[:, whole], queries[:, whole]).astype(BF16) * keep[...]
+        value_part[:, head_cols(head)] = scale * nn(turned, grads[:, whole])
+
+
+def final_kernel(begin, count, grid, counts, length, keys, values, key_part, *rest):
+    value_parts, received, rest = split_refs(rest, VALUE_PIECES, sum(counts), len(rest) - VALUE_PIECES - sum(counts))
     key_hbm, value_hbm, key_grad, value_grad, sems = rest[-5:]
     parts = split_refs(received, *counts)
     pair = grid[2]
@@ -358,7 +359,9 @@
             whole = head_cols(place)
             state = arrived_state(parts, core, head, count)
             key_grad[:, cols] = (key_part[:, whole] + live * nt(values[:, whole], state)).astype(BF16)
-            value_grad[:, cols] = (value_part[:, whole] + live * nn(keys[:, whole], state)).astype(BF16)
+            number, inner = divmod(place, value_parts[0].shape[1] // HD)
+            value_part = value_parts[number][:, head_cols(inner)]
+            value_grad[:, cols] = (value_part + live * nn(keys[:, whole], state)).astype(BF16)
             pending += 1
             if pending == 2 or within == count - 1:
                 done = slice((head + 1 - pending) * HD, (head + 1) * HD)
@@ -408,13 +411,13 @@
     return lax.ppermute(block, "seg", moves)
 
 
-def gather_line(halves, grid):
+def gather_line(halves, grid, swapped=None):
     pair = grid[2]
     arrived = {0: halves[0]}
     for step in range(line_length(grid)):
         for flip in range(pair):
             if step or flip:
-                arrived[step * pair + flip] = line_send(halves[flip], grid, step, flip, True)
+                arrived[step * pair + flip] = line_send(halves[flip] if step or swapped is None else swapped, grid, step, flip, True)
     return [arrived[j] for j in range(len(arrived))]
 
 
@@ -507,27 +510,34 @@
     group = 4 if heads % 4 == 0 else 1
     attended, query_grad, key_part, token = call(
         functools.partial(query_kernel, heads, group, scale),
-        [narrow, narrow, wide, shape((8, HD), F32)],
-        (length, inverse_rms, gain, query, key, value, grads, attention, *prefix),
+        [narrow, narrow, wide, shape(state_grad[-1].shape, BF16)],
+        (length, inverse_rms, gain, query, key, value, grads, attention, state_grad[-1], *prefix),
         [pltpu.VMEM(narrow.shape, BF16)] * 2 + [mask, pltpu.SemaphoreType.DMA((heads // group, 2))],
         unit * (3 * rows + HD), out_specs=[HBM, HBM, VMEM, VMEM],
     )
-    arrived = gather_line(state_grad, grid)
+    def value_piece(number, after):
+        width = features // VALUE_PIECES
+        (out,) = call(
+            functools.partial(value_kernel, number * heads // VALUE_PIECES, scale),
+            [shape((rows, width), F32)], (length, query, key, grads), [mask], unit * 2 * rows // VALUE_PIECES,
+            after=after,
+        )
+        return out
+
+    value_parts = [value_piece(0, (token,))]
+    arrived = gather_line(state_grad, grid, token)
     half_heads = heads // pair
     last = max(half_heads * 3 // 8, min(half_heads - 1, 1))
     pieces = [(0, half_heads - last), (half_heads - last, last)] if last else [(0, half_heads)]
     mixed = []
     for begin, count in pieces:
-        before = (token, *mixed[-1][:1]) if mixed else (token,)
+        before = (value_parts[0], *mixed[-1][:1]) if mixed else (value_parts[0],)
         mixed.append(mix(arrived, down, begin * HD, count * HD, before))
-    (value_part,) = call(
-        functools.partial(value_kernel, heads, scale),
-        [wide], (length, query, key, grads), [mask], unit * 2 * rows, after=(mixed[-1][0],),
-    )
+    value_parts += [value_piece(number, (mixed[-1][0],)) for number in range(1, VALUE_PIECES)]
     results = []
     for (begin, count), sums in zip(pieces, mixed):
         below = flat(scatter_line(sums, grid))
-        operands = (length, key, value, key_part, value_part, *below, *results)
+        operands = (length, key, value, key_part, *value_parts, *below, *results)
         first = len(operands) - len(results)
         width = pair * count * HD
         results = call(

time: 49.7 us -> 49.6 us (level)
  waiting for transfers between devices: 8.36 us -> 7.59 us
    ppermute x21, waiting for transfers between devices: 4.56 us -> 3.78 us  [line_send(): return lax.ppermute(block, 'seg', moves)]
    pallas_call x15 -> x16, Pallas kernels: 17.7 us -> 18.1 us  [call(): pl.pallas_call(kernel, out_shape=out_shape, in_specs=specs + [ANY] * len(...]
  transfers between devices with their start and end apart: 24 -> 24, of which waited for: 7 -> 9; matrix products, arithmetic and copies ran while one was open for 0% -> 0% of each run, Pallas kernels for 25% -> 26%
where the time goes in v19:
time: 49.6 us; the launch traced here: 49.3 us
  starting transfers between devices  22 us (44%)
  Pallas kernels  18.1 us (36%)
  waiting for transfers between devices  7.59 us (15%)
  between operations  1.61 us (3%)
    pallas_call x16, Pallas kernels, call(): pl.pallas_call(kernel, out_shape=out_shape, in_specs=specs + [ANY] * len(...  18.1 us
    ppermute x21, starting transfers between devices, line_send(): return lax.ppermute(block, 'seg', moves)  17.7 us
    ppermute x3, starting transfers between devices, token_sums(): parts.append(lax.ppermute(sums, 'head', moves))  4.23 us
    ppermute x3, waiting for transfers between devices, token_sums(): parts.append(lax.ppermute(sums, 'head', moves))  3.81 us
    ppermute x21, waiting for transfers between devices, line_send(): return lax.ppermute(block, 'seg', moves)  3.78 us
  transfers between devices with their start and end apart: 24, of which 9 were waited for; matrix products, arithmetic and copies ran while one was open for 0% of the time, Pallas kernels for 26%

profile of v19, /device:TPU:0, one launch (start us, length us, event | category | flops | bytes accessed | tf_op | source)
XLA Modules:
  0.0 49.3 jit_solution(5829743574717961676)
XLA Ops:
  1.3 1.8 %shard_map.102 = (bf16[256,2048]{1,0:T(8,128)(2,1)S(1)}, bf16[256,2048]{1,0:T(8,128)(2,1)S(1)}, s32[1,256]{1,0:T(1,128)S(1)}, f32[16,128]{1,0:T(8,128)S(1)}, f32...) custom-call(s32[1]{0:T(128)S(6)} %copy.17.seg_len, bf16[256,2048]{1,0:T(8,128)(2,1)} %bitcast.20, ...), custom_call_target="tpu_custom_call" | custom-call | flops 67108864 | bytes 4473892 | tf_op jit(solution)/shard_map/pallas_call | solution.py:389
  3.1 2.5 %collective-permute-start.2 = (bf16[512,128]{1,0:T(8,128)(2,1)S(1)}, bf16[512,128]{1,0:T(8,128)(2,1)S(1)}, u32[]{:S(2)}, u32[]{:S(2)}) collective-permute-start(bf16[512,128]{1,0:T(8,128)(2,1)S(1)} %get-tuple-element.52), channel_id=1, source_target_pairs={{0,5},{1,2},{2,7},{3,0},{4,1},{5,6},{6,3},{7,4},{8,13},{9,10},{10,... | collective-permute-start | bytes 393224 | tf_op jit(solution)/shard_map/ppermute | solution.py:411
  5.6 0.6 %collective-permute-start = (bf16[512,128]{1,0:T(8,128)(2,1)S(1)}, bf16[512,128]{1,0:T(8,128)(2,1)S(1)}, u32[]{:S(2)}, u32[]{:S(2)}) collective-permute-start(bf16[512,128]{1,0:T(8,128)(2,1)S(1)} %get-tuple-element.52), channel_id=1, source_target_pairs={{0,1},{1,0},{2,3},{3,2},{4,5},{5,4},{6,7},{7,6},{8,9},{9,8},{10,11... | collective-permute-start | bytes 393224 | tf_op jit(solution)/shard_map/ppermute | solution.py:411
  6.2 0.8 %collective-permute-start.1 = (bf16[512,128]{1,0:T(8,128)(2,1)S(1)}, bf16[512,128]{1,0:T(8,128)(2,1)S(1)}, u32[]{:S(2)}, u32[]{:S(2)}) collective-permute-start(bf16[512,128]{1,0:T(8,128)(2,1)S(1)} %get-tuple-element.48._.refs_0_), channel_id=1, source_target_pairs={{0,2},{1,5},{2,0},{3,7},{4,6},{5,1},{6,4},{7,3},{8,10},{9,13},{10,... | collective-permute-start | bytes 393224 | tf_op jit(solution)/shard_map/ppermute | solution.py:411
  7.1 0.4 shard_map.106
  7.5 1.2 %collective-permute-start.4 = (bf16[512,128]{1,0:T(8,128)(2,1)S(1)}, bf16[512,128]{1,0:T(8,128)(2,1)S(1)}, u32[]{:S(2)}, u32[]{:S(2)}) collective-permute-start(bf16[512,128]{1,0:T(8,128)(2,1)S(1)} %get-tuple-element.54.refs_0_), channel_id=1, source_target_pairs={{0,2},{1,5},{2,0},{3,7},{4,6},{5,1},{6,4},{7,3},{8,10},{9,13},{10,... | collective-permute-start | bytes 393224 | tf_op jit(solution)/shard_map/ppermute | solution.py:411
  8.7 0.6 %collective-permute-start.5 = (bf16[512,128]{1,0:T(8,128)(2,1)S(1)}, bf16[512,128]{1,0:T(8,128)(2,1)S(1)}, u32[]{:S(2)}, u32[]{:S(2)}) collective-permute-start(bf16[512,128]{1,0:T(8,128)(2,1)S(1)} %get-tuple-element.55), channel_id=1, source_target_pairs={{0,5},{1,2},{2,7},{3,0},{4,1},{5,6},{6,3},{7,4},{8,13},{9,10},{10,... | collective-permute-start | bytes 393224 | tf_op jit(solution)/shard_map/ppermute | solution.py:411
  9.3 1.2 %shard_map.103.refs_4_.queries = bf16[256,2048]{1,0:T(8,128)(2,1)S(1)} custom-call(bf16[256,2048]{1,0:T(8,128)(2,1)} %bitcast.19, bf16[512,128]{1,0:T(8,128)(2,1)S(1)} %get-tuple-element.48._.refs_0_), custom_call_target="tpu_custom_call" | custom-call | bytes 2097152 | tf_op jit(solution)/shard_map/pallas_call | solution.py:389
  10.5 0.0 collective-permute-done.2.refs_3_
  10.5 0.5 collective-permute-start.3
  11.0 0.0 collective-permute-done.refs_1_
  11.0 0.2 collective-permute-done.1.refs_2_
  11.2 0.3 shard_map.104
  11.5 1.6 %collective-permute-start.9 = (bf16[512,128]{1,0:T(8,128)(2,1)S(1)}, bf16[512,128]{1,0:T(8,128)(2,1)S(1)}, u32[]{:S(2)}, u32[]{:S(2)}) collective-permute-start(bf16[512,128]{1,0:T(8,128)(2,1)S(1)} %get-tuple-element.60), channel_id=1, source_target_pairs={{0,4},{1,3},{2,6},{3,1},{4,0},{5,7},{6,2},{7,5},{8,12},{9,11},{10,... | collective-permute-start | bytes 393224 | tf_op jit(solution)/shard_map/ppermute | solution.py:411
  13.1 0.3 collective-permute-start.10
  13.4 0.0 collective-permute-done.4.refs_2_
  13.5 0.7 %collective-permute-start.11 = (bf16[512,128]{1,0:T(8,128)(2,1)S(1)}, bf16[512,128]{1,0:T(8,128)(2,1)S(1)}, u32[]{:S(2)}, u32[]{:S(2)}) collective-permute-start(bf16[512,128]{1,0:T(8,128)(2,1)S(1)} %get-tuple-element.62), channel_id=1, source_target_pairs={{0,1},{1,0},{2,3},{3,2},{4,5},{5,4},{6,7},{7,6},{8,9},{9,8},{10,11... | collective-permute-start | bytes 393224 | tf_op jit(solution)/shard_map/ppermute | solution.py:411
  14.2 0.0 collective-permute-done.5.refs_3_
  14.2 0.0 collective-permute-done.3.refs_1_
  14.2 0.3 shard_map.107
  14.5 1.4 %collective-permute-start.6 = (bf16[512,128]{1,0:T(8,128)(2,1)S(1)}, bf16[512,128]{1,0:T(8,128)(2,1)S(1)}, u32[]{:S(2)}, u32[]{:S(2)}) collective-permute-start(bf16[512,128]{1,0:T(8,128)(2,1)S(1)} %get-tuple-element.56), channel_id=1, source_target_pairs={{0,4},{1,3},{2,6},{3,1},{4,0},{5,7},{6,2},{7,5},{8,12},{9,11},{10,... | collective-permute-start | bytes 393224 | tf_op jit(solution)/shard_map/ppermute | solution.py:411
  15.9 0.9 %collective-permute-start.7 = (bf16[512,128]{1,0:T(8,128)(2,1)S(1)}, bf16[512,128]{1,0:T(8,128)(2,1)S(1)}, u32[]{:S(2)}, u32[]{:S(2)}) collective-permute-start(bf16[512,128]{1,0:T(8,128)(2,1)S(1)} %get-tuple-element.58), channel_id=1, source_target_pairs={{0,5},{1,2},{2,7},{3,0},{4,1},{5,6},{6,3},{7,4},{8,13},{9,10},{10,... | collective-permute-start | bytes 393224 | tf_op jit(solution)/shard_map/ppermute | solution.py:411
  16.8 0.0 collective-permute-done.9.rest_0_
  16.8 0.3 collective-permute-start.8
  17.1 1.5 %shard_map.105.local = f32[256,2048]{1,0:T(8,128)S(1)} custom-call(s32[1,256]{1,0:T(1,128)S(1)} %get-tuple-element.47.length, bf16[256,2048]{1,0:T(8,128)(2,1)S(1)} %shard_map.103.refs_4_.queries, bf16[256,2048]{1,0:T(8,128)(2,1)S(1)} %get-tuple-element.49.keys, bf16[256,2048]{1,0:T(8,128)(2,1)S(1)} %get-tuple-element.50.values, ...), custom_call_target="tpu_custom_call" | custom-call | flops 536870912 | bytes 5243904 | tf_op jit(solution)/shard_map/pallas_call | solution.py:389
  18.6 0.0 collective-permute-done.10.rest_2_
  18.6 0.0 collective-permute-done.11.rest_3_
  18.6 0.6 %shard_map.108 = (f32[256,2048]{1,0:T(8,128)S(1)}, f32[2,256]{1,0:T(2,128)S(1)}, bf16[1024,128]{1,0:T(8,128)(2,1)S(1)}) custom-call(s32[1,256]{1,0:T(1,128)S(1)} %get-tuple-element.47.length, bf16[256,2048]{1,0:T(8,128)(2,1)S(1)} %shard_map.103.refs_4_.queries, f32[256,2048]{1,0:T(8,128)S(1)} %shard_map.105.local, bf16[256,2048]{1,0:T(8,128)(2,1)S(1)} %bitcast.10, ...), custom_call_target="tpu_custom_call" | custom-call | flops 67108864 | bytes 7089152 | tf_op jit(solution)/shard_map/pallas_call | solution.py:389
  19.2 0.3 collective-permute-done.6.rest_0_
  19.5 0.8 %collective-permute-done.7.rest_2_ = bf16[512,128]{1,0:T(8,128)(2,1)S(1)} collective-permute-done((bf16[512,128]{1,0:T(8,128)(2,1)S(1)}, bf16[512,128]{1,0:T(8,128)(2,1)S(1)}, u32[]{:S(2)}, u32[]{:S(2)}) %collective-permute-start.7) | collective-permute-done | bytes 131104 | tf_op jit(solution)/shard_map/ppermute | solution.py:411
  20.3 0.0 collective-permute-done.8.rest_3_
  20.3 0.6 %shard_map.109 = (f32[256,2048]{1,0:T(8,128)S(1)}, f32[2,256]{1,0:T(2,128)S(1)}, bf16[1024,128]{1,0:T(8,128)(2,1)S(1)}) custom-call(s32[1,256]{1,0:T(1,128)S(1)} %get-tuple-element.47.length, bf16[256,2048]{1,0:T(8,128)(2,1)S(1)} %shard_map.103.refs_4_.queries, f32[256,2048]{1,0:T(8,128)S(1)} %shard_map.105.local, ...), custom_call_target="tpu_custom_call", output_to_operand_aliasing={{0}: (10, {})} | custom-call | flops 67108864 | bytes 9188352 | tf_op jit(solution)/shard_map/pallas_call | solution.py:389
  20.9 2.7 %collective-permute-start.14 = (f32[2,256]{1,0:T(2,128)S(1)}, f32[2,256]{1,0:T(2,128)S(1)}, u32[]{:S(2)}, u32[]{:S(2)}) collective-permute-start(f32[2,256]{1,0:T(2,128)S(1)} %get-tuple-element.66.rest_0_), channel_id=1, source_target_pairs={{0,16},{8,24},{16,0},{24,8},{1,17},{9,25},{17,1},{25,9},{2,18},{10... | collective-permute-start | bytes 6152 | tf_op jit(solution)/shard_map/ppermute | solution.py:438
  23.6 1.3 %collective-permute-start.13 = (f32[2,256]{1,0:T(2,128)S(1)}, f32[2,256]{1,0:T(2,128)S(1)}, u32[]{:S(2)}, u32[]{:S(2)}) collective-permute-start(f32[2,256]{1,0:T(2,128)S(1)} %get-tuple-element.66.rest_0_), channel_id=1, source_target_pairs={{0,24},{8,16},{16,8},{24,0},{1,25},{9,17},{17,9},{25,1},{2,26},{10... | collective-permute-start | bytes 6152 | tf_op jit(solution)/shard_map/ppermute | solution.py:438
  24.9 0.2 collective-permute-start.12
  25.1 0.3 collective-permute-done.14.rest_3_
  25.5 3.5 %collective-permute-done.13.rest_2_ = f32[2,256]{1,0:T(2,128)S(1)} collective-permute-done((f32[2,256]{1,0:T(2,128)S(1)}, f32[2,256]{1,0:T(2,128)S(1)}, u32[]{:S(2)}, u32[]{:S(2)}) %collective-permute-start.13) | collective-permute-done | bytes 2080 | tf_op jit(solution)/shard_map/ppermute | solution.py:438
  28.9 0.0 collective-permute-done.12.rest_1_
  28.9 1.1 %shard_map.110 = (bf16[256,2048]{1,0:T(8,128)(2,1)S(1)}, f32[1,256]{1,0:T(1,128)S(1)}, bf16[1024,128]{1,0:T(8,128)(2,1)S(1)}, bf16[1024,128]{1,0:T(8,128)(2,1)S(1)}) custom-call(s32[1,256]{1,0:T(1,128)S(1)} %get-tuple-element.47.length, bf16[256,2048]{1,0:T(8,128)(2,1)S(1)} %shard_map.103.refs_4_.queries, bf16[256,2048]{1,0:T(8,128)(2,1)S(1)} %bitcast.12, ...), custom_call_target="tpu_custom_call" | custom-call | flops 134217728 | bytes 5785600 | tf_op jit(solution)/shard_map/pallas_call | solution.py:389
  30.0 0.2 collective-permute-start.17
  30.3 1.1 %collective-permute-start.16 = (bf16[1024,128]{1,0:T(8,128)(2,1)S(1)}, bf16[1024,128]{1,0:T(8,128)(2,1)S(1)}, u32[]{:S(2)}, u32[]{:S(2)}) collective-permute-start(bf16[1024,128]{1,0:T(8,128)(2,1)S(1)} %get-tuple-element.77.refs_0_), channel_id=1, source_target_pairs={{0,2},{1,5},{2,0},{3,7},{4,6},{5,1},{6,4},{7,3},{8,10},{9,13},{10,... | collective-permute-start | bytes 786440 | tf_op jit(solution)/shard_map/ppermute | solution.py:411
  31.4 4.8 %shard_map.111 = (bf16[256,2048]{1,0:T(8,128)(2,1)}, bf16[256,2048]{1,0:T(8,128)(2,1)}, f32[256,2048]{1,0:T(8,128)S(1)}, bf16[1024,128]{1,0:T(8,128)(2,1)S(1)}) custom-call(s32[1,256]{1,0:T(1,128)S(1)} %get-tuple-element.47.length, f32[1,256]{1,0:T(1,128)S(1)} %get-tuple-element.67.inverse_rms, f32[1,2048]{1,0:T(1,128)S(1)} %bitcast.16, ...), custom_call_target="tpu_custom_call" | custom-call | flops 939524096 | bytes 11544576 | tf_op jit(solution)/shard_map/pallas_call | solution.py:389
  36.2 1.3 %collective-permute-start.15 = (bf16[1024,128]{1,0:T(8,128)(2,1)S(1)}, bf16[1024,128]{1,0:T(8,128)(2,1)S(1)}, u32[]{:S(2)}, u32[]{:S(2)}) collective-permute-start(bf16[1024,128]{1,0:T(8,128)(2,1)S(1)} %get-tuple-element.75.rest_0_), channel_id=1, source_target_pairs={{0,1},{1,0},{2,3},{3,2},{4,5},{5,4},{6,7},{7,6},{8,9},{9,8},{10,11... | collective-permute-start | bytes 786440 | tf_op jit(solution)/shard_map/ppermute | solution.py:411
  37.5 0.9 %shard_map.112.refs_4_.rest_0_ = f32[256,1024]{1,0:T(8,128)S(1)} custom-call(s32[1,256]{1,0:T(1,128)S(1)} %get-tuple-element.47.length, bf16[256,2048]{1,0:T(8,128)(2,1)S(1)} %shard_map.103.refs_4_.queries, bf16[256,2048]{1,0:T(8,128)(2,1)S(1)} %get-tuple-element.49.keys, bf16[256,2048]{1,0:T(8,128)(2,1)S(1)} %get-tuple-element.68.grads, ...), custom_call_target="tpu_custom_call" | custom-call | flops 268435456 | bytes 4195328 | tf_op jit(solution)/shard_map/pallas_call | solution.py:389
  38.4 0.0 collective-permute-done.17.refs_3_
  38.4 0.4 collective-permute-done.16.refs_2_
  38.9 0.0 collective-permute-done.15.refs_1_
  38.9 0.4 shard_map.113
  39.2 1.0 %collective-permute-start.21 = (bf16[640,128]{1,0:T(8,128)(2,1)S(1)}, bf16[640,128]{1,0:T(8,128)(2,1)S(1)}, u32[]{:S(2)}, u32[]{:S(2)}) collective-permute-start(bf16[640,128]{1,0:T(8,128)(2,1)S(1)} %get-tuple-element.83), channel_id=1, source_target_pairs={{0,4},{1,3},{2,6},{3,1},{4,0},{5,7},{6,2},{7,5},{8,12},{9,11},{10,... | collective-permute-start | bytes 491528 | tf_op jit(solution)/shard_map/ppermute | solution.py:411
  40.2 0.1 collective-permute-start.22
  40.4 1.6 %collective-permute-start.23 = (bf16[640,128]{1,0:T(8,128)(2,1)S(1)}, bf16[640,128]{1,0:T(8,128)(2,1)S(1)}, u32[]{:S(2)}, u32[]{:S(2)}) collective-permute-start(bf16[640,128]{1,0:T(8,128)(2,1)S(1)} %get-tuple-element.85), channel_id=1, source_target_pairs={{0,1},{1,0},{2,3},{3,2},{4,5},{5,4},{6,7},{7,6},{8,9},{9,8},{10,11... | collective-permute-start | bytes 491528 | tf_op jit(solution)/shard_map/ppermute | solution.py:411
  42.0 0.2 shard_map.114
  42.2 0.6 %collective-permute-start.18 = (bf16[384,128]{1,0:T(8,128)(2,1)S(1)}, bf16[384,128]{1,0:T(8,128)(2,1)S(1)}, u32[]{:S(2)}, u32[]{:S(2)}) collective-permute-start(bf16[384,128]{1,0:T(8,128)(2,1)S(1)} %get-tuple-element.80), channel_id=1, source_target_pairs={{0,4},{1,3},{2,6},{3,1},{4,0},{5,7},{6,2},{7,5},{8,12},{9,11},{10,... | collective-permute-start | bytes 294920 | tf_op jit(solution)/shard_map/ppermute | solution.py:411
  42.8 0.3 collective-permute-start.19
  43.1 1.5 %collective-permute-done.21.rest_2_ = bf16[640,128]{1,0:T(8,128)(2,1)S(1)} collective-permute-done((bf16[640,128]{1,0:T(8,128)(2,1)S(1)}, bf16[640,128]{1,0:T(8,128)(2,1)S(1)}, u32[]{:S(2)}, u32[]{:S(2)}) %collective-permute-start.21) | collective-permute-done | bytes 163872 | tf_op jit(solution)/shard_map/ppermute | solution.py:411
  44.6 0.0 collective-permute-start.20
  44.6 0.9 %shard_map.115.rest_1_ = f32[256,1024]{1,0:T(8,128)S(1)} custom-call(s32[1,256]{1,0:T(1,128)S(1)} %get-tuple-element.47.length, bf16[256,2048]{1,0:T(8,128)(2,1)S(1)} %shard_map.103.refs_4_.queries, bf16[256,2048]{1,0:T(8,128)(2,1)S(1)} %get-tuple-element.49.keys, bf16[256,2048]{1,0:T(8,128)(2,1)S(1)} %get-tuple-element.68.grads, ...), custom_call_target="tpu_custom_call" | custom-call | flops 268435456 | bytes 4195328 | tf_op jit(solution)/shard_map/pallas_call | solution.py:389
  45.6 0.0 collective-permute-done.22.rest_4_
  45.6 0.0 collective-permute-done.23.rest_5_
  45.6 1.7 %shard_map.116 = (bf16[256,2048]{1,0:T(8,128)(2,1)}, bf16[256,2048]{1,0:T(8,128)(2,1)}) custom-call(s32[1,256]{1,0:T(1,128)S(1)} %get-tuple-element.47.length, bf16[256,2048]{1,0:T(8,128)(2,1)S(1)} %get-tuple-element.49.keys, bf16[256,2048]{1,0:T(8,128)(2,1)S(1)} %get-tuple-element.50.values, f32[256,2048]{1,0:T(8,128)S(1)} %get-tuple-element.74.key_part, ...), custom_call_target="tpu_custom_call" | custom-call | flops 167772160 | bytes 9044992 | tf_op jit(solution)/shard_map/pallas_call | solution.py:389
  47.3 0.2 collective-permute-done.18.rest_2_
  47.4 0.3 collective-permute-done.19.rest_4_
  47.7 0.0 collective-permute-done.20.rest_5_
  47.7 1.4 %shard_map.117 = (bf16[256,2048]{1,0:T(8,128)(2,1)}, bf16[256,2048]{1,0:T(8,128)(2,1)}) custom-call(s32[1,256]{1,0:T(1,128)S(1)} %get-tuple-element.47.length, bf16[256,2048]{1,0:T(8,128)(2,1)S(1)} %get-tuple-element.49.keys, bf16[256,2048]{1,0:T(8,128)(2,1)S(1)} %get-tuple-element.50.values, ...), custom_call_target="tpu_custom_call", output_to_operand_aliasing={{0}: (10, {}), {1}: (11, {})} | custom-call | flops 100663296 | bytes 10880000 | tf_op jit(solution)/shard_map/pallas_call | solution.py:389
  (4 shorter events, 0.0 us)
Async XLA Ops:
  3.1 7.4 %collective-permute-start.2 = (bf16[512,128]{1,0:T(8,128)(2,1)S(1)}, bf16[512,128]{1,0:T(8,128)(2,1)S(1)}, u32[]{:S(2)}, u32[]{:S(2)}) collective-permute-start(bf16[512,128]{1,0:T(8,128)(2,1)S(1)} %get-tuple-element.52), channel_id=1, source_target_pairs={{0,5},{1,2},{2,7},{3,0},{4,1},{5,6},{6,3},{7,4},{8,13},{9,10},{10,... | collective-permute-start | bytes 393224 | tf_op jit(solution)/shard_map/ppermute | solution.py:411
  5.6 5.4 %collective-permute-start = (bf16[512,128]{1,0:T(8,128)(2,1)S(1)}, bf16[512,128]{1,0:T(8,128)(2,1)S(1)}, u32[]{:S(2)}, u32[]{:S(2)}) collective-permute-start(bf16[512,128]{1,0:T(8,128)(2,1)S(1)} %get-tuple-element.52), channel_id=1, source_target_pairs={{0,1},{1,0},{2,3},{3,2},{4,5},{5,4},{6,7},{7,6},{8,9},{9,8},{10,11... | collective-permute-start | bytes 393224 | tf_op jit(solution)/shard_map/ppermute | solution.py:411
  6.2 5.0 %collective-permute-start.1 = (bf16[512,128]{1,0:T(8,128)(2,1)S(1)}, bf16[512,128]{1,0:T(8,128)(2,1)S(1)}, u32[]{:S(2)}, u32[]{:S(2)}) collective-permute-start(bf16[512,128]{1,0:T(8,128)(2,1)S(1)} %get-tuple-element.48._.refs_0_), channel_id=1, source_target_pairs={{0,2},{1,5},{2,0},{3,7},{4,6},{5,1},{6,4},{7,3},{8,10},{9,13},{10,... | collective-permute-start | bytes 393224 | tf_op jit(solution)/shard_map/ppermute | solution.py:411
  7.5 6.0 %collective-permute-start.4 = (bf16[512,128]{1,0:T(8,128)(2,1)S(1)}, bf16[512,128]{1,0:T(8,128)(2,1)S(1)}, u32[]{:S(2)}, u32[]{:S(2)}) collective-permute-start(bf16[512,128]{1,0:T(8,128)(2,1)S(1)} %get-tuple-element.54.refs_0_), channel_id=1, source_target_pairs={{0,2},{1,5},{2,0},{3,7},{4,6},{5,1},{6,4},{7,3},{8,10},{9,13},{10,... | collective-permute-start | bytes 393224 | tf_op jit(solution)/shard_map/ppermute | solution.py:411
  8.7 5.5 %collective-permute-start.5 = (bf16[512,128]{1,0:T(8,128)(2,1)S(1)}, bf16[512,128]{1,0:T(8,128)(2,1)S(1)}, u32[]{:S(2)}, u32[]{:S(2)}) collective-permute-start(bf16[512,128]{1,0:T(8,128)(2,1)S(1)} %get-tuple-element.55), channel_id=1, source_target_pairs={{0,5},{1,2},{2,7},{3,0},{4,1},{5,6},{6,3},{7,4},{8,13},{9,10},{10,... | collective-permute-start | bytes 393224 | tf_op jit(solution)/shard_map/ppermute | solution.py:411
  10.5 3.7 %collective-permute-start.3 = (bf16[512,128]{1,0:T(8,128)(2,1)S(1)}, bf16[512,128]{1,0:T(8,128)(2,1)S(1)}, u32[]{:S(2)}, u32[]{:S(2)}) collective-permute-start(bf16[512,128]{1,0:T(8,128)(2,1)S(1)} %get-tuple-element.55), channel_id=1, source_target_pairs={{0,1},{1,0},{2,3},{3,2},{4,5},{5,4},{6,7},{7,6},{8,9},{9,8},{10,11... | collective-permute-start | bytes 393224 | tf_op jit(solution)/shard_map/ppermute | solution.py:411
  11.5 5.3 %collective-permute-start.9 = (bf16[512,128]{1,0:T(8,128)(2,1)S(1)}, bf16[512,128]{1,0:T(8,128)(2,1)S(1)}, u32[]{:S(2)}, u32[]{:S(2)}) collective-permute-start(bf16[512,128]{1,0:T(8,128)(2,1)S(1)} %get-tuple-element.60), channel_id=1, source_target_pairs={{0,4},{1,3},{2,6},{3,1},{4,0},{5,7},{6,2},{7,5},{8,12},{9,11},{10,... | collective-permute-start | bytes 393224 | tf_op jit(solution)/shard_map/ppermute | solution.py:411
  13.1 5.5 %collective-permute-start.10 = (bf16[512,128]{1,0:T(8,128)(2,1)S(1)}, bf16[512,128]{1,0:T(8,128)(2,1)S(1)}, u32[]{:S(2)}, u32[]{:S(2)}) collective-permute-start(bf16[512,128]{1,0:T(8,128)(2,1)S(1)} %get-tuple-element.61), channel_id=1, source_target_pairs={{0,5},{1,2},{2,7},{3,0},{4,1},{5,6},{6,3},{7,4},{8,13},{9,10},{10,... | collective-permute-start | bytes 393224 | tf_op jit(solution)/shard_map/ppermute | solution.py:411
  13.5 5.1 %collective-permute-start.11 = (bf16[512,128]{1,0:T(8,128)(2,1)S(1)}, bf16[512,128]{1,0:T(8,128)(2,1)S(1)}, u32[]{:S(2)}, u32[]{:S(2)}) collective-permute-start(bf16[512,128]{1,0:T(8,128)(2,1)S(1)} %get-tuple-element.62), channel_id=1, source_target_pairs={{0,1},{1,0},{2,3},{3,2},{4,5},{5,4},{6,7},{7,6},{8,9},{9,8},{10,11... | collective-permute-start | bytes 393224 | tf_op jit(solution)/shard_map/ppermute | solution.py:411
  14.5 5.0 %collective-permute-start.6 = (bf16[512,128]{1,0:T(8,128)(2,1)S(1)}, bf16[512,128]{1,0:T(8,128)(2,1)S(1)}, u32[]{:S(2)}, u32[]{:S(2)}) collective-permute-start(bf16[512,128]{1,0:T(8,128)(2,1)S(1)} %get-tuple-element.56), channel_id=1, source_target_pairs={{0,4},{1,3},{2,6},{3,1},{4,0},{5,7},{6,2},{7,5},{8,12},{9,11},{10,... | collective-permute-start | bytes 393224 | tf_op jit(solution)/shard_map/ppermute | solution.py:411
  15.9 4.4 %collective-permute-start.7 = (bf16[512,128]{1,0:T(8,128)(2,1)S(1)}, bf16[512,128]{1,0:T(8,128)(2,1)S(1)}, u32[]{:S(2)}, u32[]{:S(2)}) collective-permute-start(bf16[512,128]{1,0:T(8,128)(2,1)S(1)} %get-tuple-element.58), channel_id=1, source_target_pairs={{0,5},{1,2},{2,7},{3,0},{4,1},{5,6},{6,3},{7,4},{8,13},{9,10},{10,... | collective-permute-start | bytes 393224 | tf_op jit(solution)/shard_map/ppermute | solution.py:411
  16.8 3.5 %collective-permute-start.8 = (bf16[512,128]{1,0:T(8,128)(2,1)S(1)}, bf16[512,128]{1,0:T(8,128)(2,1)S(1)}, u32[]{:S(2)}, u32[]{:S(2)}) collective-permute-start(bf16[512,128]{1,0:T(8,128)(2,1)S(1)} %get-tuple-element.59), channel_id=1, source_target_pairs={{0,1},{1,0},{2,3},{3,2},{4,5},{5,4},{6,7},{7,6},{8,9},{9,8},{10,11... | collective-permute-start | bytes 393224 | tf_op jit(solution)/shard_map/ppermute | solution.py:411
  17.1 1.5 %copy-start = (bf16[1,256,2048]{2,1,0:T(8,128)(2,1)S(1)}, bf16[1,256,2048]{2,1,0:T(8,128)(2,1)}, u32[]{:S(2)}) copy-start(bf16[1,256,2048]{2,1,0:T(8,128)(2,1)} %param.10) | copy-start | bytes 3145732
  17.1 1.5 %copy-start.1 = (f32[2048]{0:T(1024)S(1)}, f32[2048]{0:T(1024)}, u32[]{:S(2)}) copy-start(f32[2048]{0:T(1024)} %param.11) | copy-start | bytes 24580
  20.9 4.5 %collective-permute-start.14 = (f32[2,256]{1,0:T(2,128)S(1)}, f32[2,256]{1,0:T(2,128)S(1)}, u32[]{:S(2)}, u32[]{:S(2)}) collective-permute-start(f32[2,256]{1,0:T(2,128)S(1)} %get-tuple-element.66.rest_0_), channel_id=1, source_target_pairs={{0,16},{8,24},{16,0},{24,8},{1,17},{9,25},{17,1},{25,9},{2,18},{10... | collective-permute-start | bytes 6152 | tf_op jit(solution)/shard_map/ppermute | solution.py:438
  23.6 5.4 %collective-permute-start.13 = (f32[2,256]{1,0:T(2,128)S(1)}, f32[2,256]{1,0:T(2,128)S(1)}, u32[]{:S(2)}, u32[]{:S(2)}) collective-permute-start(f32[2,256]{1,0:T(2,128)S(1)} %get-tuple-element.66.rest_0_), channel_id=1, source_target_pairs={{0,24},{8,16},{16,8},{24,0},{1,25},{9,17},{17,9},{25,1},{2,26},{10... | collective-permute-start | bytes 6152 | tf_op jit(solution)/shard_map/ppermute | solution.py:438
  24.9 4.0 %collective-permute-start.12 = (f32[2,256]{1,0:T(2,128)S(1)}, f32[2,256]{1,0:T(2,128)S(1)}, u32[]{:S(2)}, u32[]{:S(2)}) collective-permute-start(f32[2,256]{1,0:T(2,128)S(1)} %get-tuple-element.66.rest_0_), channel_id=1, source_target_pairs={{0,8},{8,0},{16,24},{24,16},{1,9},{9,1},{17,25},{25,17},{2,10},{10... | collective-permute-start | bytes 6152 | tf_op jit(solution)/shard_map/ppermute | solution.py:438
  30.0 8.4 %collective-permute-start.17 = (bf16[1024,128]{1,0:T(8,128)(2,1)S(1)}, bf16[1024,128]{1,0:T(8,128)(2,1)S(1)}, u32[]{:S(2)}, u32[]{:S(2)}) collective-permute-start(bf16[1024,128]{1,0:T(8,128)(2,1)S(1)} %get-tuple-element.69.block), channel_id=1, source_target_pairs={{0,5},{1,2},{2,7},{3,0},{4,1},{5,6},{6,3},{7,4},{8,13},{9,10},{10,... | collective-permute-start | bytes 786440 | tf_op jit(solution)/shard_map/ppermute | solution.py:411
  30.3 8.6 %collective-permute-start.16 = (bf16[1024,128]{1,0:T(8,128)(2,1)S(1)}, bf16[1024,128]{1,0:T(8,128)(2,1)S(1)}, u32[]{:S(2)}, u32[]{:S(2)}) collective-permute-start(bf16[1024,128]{1,0:T(8,128)(2,1)S(1)} %get-tuple-element.77.refs_0_), channel_id=1, source_target_pairs={{0,2},{1,5},{2,0},{3,7},{4,6},{5,1},{6,4},{7,3},{8,10},{9,13},{10,... | collective-permute-start | bytes 786440 | tf_op jit(solution)/shard_map/ppermute | solution.py:411
  36.2 2.7 %collective-permute-start.15 = (bf16[1024,128]{1,0:T(8,128)(2,1)S(1)}, bf16[1024,128]{1,0:T(8,128)(2,1)S(1)}, u32[]{:S(2)}, u32[]{:S(2)}) collective-permute-start(bf16[1024,128]{1,0:T(8,128)(2,1)S(1)} %get-tuple-element.75.rest_0_), channel_id=1, source_target_pairs={{0,1},{1,0},{2,3},{3,2},{4,5},{5,4},{6,7},{7,6},{8,9},{9,8},{10,11... | collective-permute-start | bytes 786440 | tf_op jit(solution)/shard_map/ppermute | solution.py:411
  39.2 5.4 %collective-permute-start.21 = (bf16[640,128]{1,0:T(8,128)(2,1)S(1)}, bf16[640,128]{1,0:T(8,128)(2,1)S(1)}, u32[]{:S(2)}, u32[]{:S(2)}) collective-permute-start(bf16[640,128]{1,0:T(8,128)(2,1)S(1)} %get-tuple-element.83), channel_id=1, source_target_pairs={{0,4},{1,3},{2,6},{3,1},{4,0},{5,7},{6,2},{7,5},{8,12},{9,11},{10,... | collective-permute-start | bytes 491528 | tf_op jit(solution)/shard_map/ppermute | solution.py:411
  40.2 5.3 %collective-permute-start.22 = (bf16[640,128]{1,0:T(8,128)(2,1)S(1)}, bf16[640,128]{1,0:T(8,128)(2,1)S(1)}, u32[]{:S(2)}, u32[]{:S(2)}) collective-permute-start(bf16[640,128]{1,0:T(8,128)(2,1)S(1)} %get-tuple-element.84), channel_id=1, source_target_pairs={{0,5},{1,2},{2,7},{3,0},{4,1},{5,6},{6,3},{7,4},{8,13},{9,10},{10,... | collective-permute-start | bytes 491528 | tf_op jit(solution)/shard_map/ppermute | solution.py:411
  40.4 5.2 %collective-permute-start.23 = (bf16[640,128]{1,0:T(8,128)(2,1)S(1)}, bf16[640,128]{1,0:T(8,128)(2,1)S(1)}, u32[]{:S(2)}, u32[]{:S(2)}) collective-permute-start(bf16[640,128]{1,0:T(8,128)(2,1)S(1)} %get-tuple-element.85), channel_id=1, source_target_pairs={{0,1},{1,0},{2,3},{3,2},{4,5},{5,4},{6,7},{7,6},{8,9},{9,8},{10,11... | collective-permute-start | bytes 491528 | tf_op jit(solution)/shard_map/ppermute | solution.py:411
  42.2 5.2 %collective-permute-start.18 = (bf16[384,128]{1,0:T(8,128)(2,1)S(1)}, bf16[384,128]{1,0:T(8,128)(2,1)S(1)}, u32[]{:S(2)}, u32[]{:S(2)}) collective-permute-start(bf16[384,128]{1,0:T(8,128)(2,1)S(1)} %get-tuple-element.80), channel_id=1, source_target_pairs={{0,4},{1,3},{2,6},{3,1},{4,0},{5,7},{6,2},{7,5},{8,12},{9,11},{10,... | collective-permute-start | bytes 294920 | tf_op jit(solution)/shard_map/ppermute | solution.py:411
  42.8 4.9 %collective-permute-start.19 = (bf16[384,128]{1,0:T(8,128)(2,1)S(1)}, bf16[384,128]{1,0:T(8,128)(2,1)S(1)}, u32[]{:S(2)}, u32[]{:S(2)}) collective-permute-start(bf16[384,128]{1,0:T(8,128)(2,1)S(1)} %get-tuple-element.81), channel_id=1, source_target_pairs={{0,5},{1,2},{2,7},{3,0},{4,1},{5,6},{6,3},{7,4},{8,13},{9,10},{10,... | collective-permute-start | bytes 294920 | tf_op jit(solution)/shard_map/ppermute | solution.py:411
  44.6 3.1 %collective-permute-start.20 = (bf16[384,128]{1,0:T(8,128)(2,1)S(1)}, bf16[384,128]{1,0:T(8,128)(2,1)S(1)}, u32[]{:S(2)}, u32[]{:S(2)}) collective-permute-start(bf16[384,128]{1,0:T(8,128)(2,1)S(1)} %get-tuple-element.82), channel_id=1, source_target_pairs={{0,1},{1,0},{2,3},{3,2},{4,5},{5,4},{6,7},{7,6},{8,9},{9,8},{10,11... | collective-permute-start | bytes 294920 | tf_op jit(solution)/shard_map/ppermute | solution.py:411

commit v20 on v19

--- a/solution.py
+++ b/solution.py
@@ -176,7 +176,9 @@
         copy.wait()
 
 
-def next_state_kernel(piece, grid, length, keys, values, *outs):
+def next_state_kernel(piece, grid, length, keys, values, block, *outs):
+    outs, handed = outs[:-1], outs[-1]
+    handed[...] = block[...]
     own_states(piece, grid, keys, values, live_rows(length, keys.shape[0]), outs)
 
 
@@ -475,15 +477,19 @@
         [sems, pltpu.SMEM((1, segs), jnp.int32), pltpu.SemaphoreType.DMA(())],
         unit * HD // FORWARD_PIECES, (1, 2, 3), (0,),
     )
+    swapped = []
     for piece in range(1, FORWARD_PIECES):
-        own += call(
-            functools.partial(next_state_kernel, piece, grid), halves(FORWARD_PIECES),
-            (length, key, value), (), unit * HD // FORWARD_PIECES,
+        *states, handed = call(
+            functools.partial(next_state_kernel, piece, grid), halves(FORWARD_PIECES) + halves(FORWARD_PIECES)[:1],
+            (length, key, value, own[-1]), (), unit * HD // FORWARD_PIECES,
         )
+        own += states
+        swapped.append(handed)
     (query,) = call(fetch_kernel, [narrow], (queries[0],), [pltpu.SemaphoreType.DMA((4,))], 0, (0,), after=(own[0],))
     mixed = []
     for part in split_refs(own, *[pair] * FORWARD_PIECES):
-        mixed.append(mix(gather_line(part, grid), up, 0, part[0].shape[0], () if mixed else (query,)))
+        late = swapped[len(mixed)] if len(mixed) < len(swapped) else None
+        mixed.append(mix(gather_line(part, grid, late), up, 0, part[0].shape[0], () if mixed else (query,)))
     (local,) = call(
         functools.partial(local_kernel, heads),
         [wide], (length, query, key, value), [mask], unit * rows * 2, after=(mixed[0][0],),

time: 49.6 us -> 49.8 us (level)
  starting transfers between devices: 22 us -> 19.9 us
  waiting for transfers between devices: 7.59 us -> 9.59 us
    ppermute x21, starting transfers between devices: 17.7 us -> 15.7 us  [line_send(): return lax.ppermute(block, 'seg', moves)]
    ppermute x21, waiting for transfers between devices: 3.78 us -> 5.78 us  [line_send(): return lax.ppermute(block, 'seg', moves)]
  transfers between devices with their start and end apart: 24 -> 24, of which waited for: 9 -> 10; matrix products, arithmetic and copies ran while one was open for 0% -> 0% of each run, Pallas kernels for 26% -> 26%
where the time goes in v20:
time: 49.8 us; the launch traced here: 49.3 us
  starting transfers between devices  19.9 us (40%)
  Pallas kernels  18.1 us (36%)
  waiting for transfers between devices  9.59 us (19%)
  between operations  1.62 us (3%)
    pallas_call x16, Pallas kernels, call(): pl.pallas_call(kernel, out_shape=out_shape, in_specs=specs + [ANY] * len(...  18.1 us
    ppermute x21, starting transfers between devices, line_send(): return lax.ppermute(block, 'seg', moves)  15.7 us
    ppermute x21, waiting for transfers between devices, line_send(): return lax.ppermute(block, 'seg', moves)  5.78 us
    ppermute x3, starting transfers between devices, token_sums(): parts.append(lax.ppermute(sums, 'head', moves))  4.23 us
    ppermute x3, waiting for transfers between devices, token_sums(): parts.append(lax.ppermute(sums, 'head', moves))  3.8 us
  transfers between devices with their start and end apart: 24, of which 10 were waited for; matrix products, arithmetic and copies ran while one was open for 0% of the time, Pallas kernels for 26%

profile of v20, /device:TPU:0, one launch (start us, length us, event | category | flops | bytes accessed | tf_op | source)
XLA Modules:
  0.0 49.3 jit_solution(13129646566589348019)
XLA Ops:
  1.3 1.8 %shard_map.102 = (bf16[256,2048]{1,0:T(8,128)(2,1)S(1)}, bf16[256,2048]{1,0:T(8,128)(2,1)S(1)}, s32[1,256]{1,0:T(1,128)S(1)}, f32[16,128]{1,0:T(8,128)S(1)}, f32...) custom-call(s32[1]{0:T(128)S(6)} %copy.17.seg_len, bf16[256,2048]{1,0:T(8,128)(2,1)} %bitcast.20, ...), custom_call_target="tpu_custom_call" | custom-call | flops 67108864 | bytes 4473892 | tf_op jit(solution)/shard_map/pallas_call | solution.py:391
  3.1 2.5 %collective-permute-start.2 = (bf16[512,128]{1,0:T(8,128)(2,1)S(1)}, bf16[512,128]{1,0:T(8,128)(2,1)S(1)}, u32[]{:S(2)}, u32[]{:S(2)}) collective-permute-start(bf16[512,128]{1,0:T(8,128)(2,1)S(1)} %get-tuple-element.53.block), channel_id=1, source_target_pairs={{0,5},{1,2},{2,7},{3,0},{4,1},{5,6},{6,3},{7,4},{8,13},{9,10},{10,... | collective-permute-start | bytes 393224 | tf_op jit(solution)/shard_map/ppermute | solution.py:413
  5.6 1.5 %collective-permute-start.1 = (bf16[512,128]{1,0:T(8,128)(2,1)S(1)}, bf16[512,128]{1,0:T(8,128)(2,1)S(1)}, u32[]{:S(2)}, u32[]{:S(2)}) collective-permute-start(bf16[512,128]{1,0:T(8,128)(2,1)S(1)} %get-tuple-element.49._.refs_0_), channel_id=1, source_target_pairs={{0,2},{1,5},{2,0},{3,7},{4,6},{5,1},{6,4},{7,3},{8,10},{9,13},{10,... | collective-permute-start | bytes 393224 | tf_op jit(solution)/shard_map/ppermute | solution.py:413
  7.1 0.4 shard_map.104
  7.5 0.5 collective-permute-start
  7.9 0.5 %collective-permute-start.4 = (bf16[512,128]{1,0:T(8,128)(2,1)S(1)}, bf16[512,128]{1,0:T(8,128)(2,1)S(1)}, u32[]{:S(2)}, u32[]{:S(2)}) collective-permute-start(bf16[512,128]{1,0:T(8,128)(2,1)S(1)} %get-tuple-element.56.refs_0_), channel_id=1, source_target_pairs={{0,2},{1,5},{2,0},{3,7},{4,6},{5,1},{6,4},{7,3},{8,10},{9,13},{10,... | collective-permute-start | bytes 393224 | tf_op jit(solution)/shard_map/ppermute | solution.py:413
  8.5 0.9 %collective-permute-start.5 = (bf16[512,128]{1,0:T(8,128)(2,1)S(1)}, bf16[512,128]{1,0:T(8,128)(2,1)S(1)}, u32[]{:S(2)}, u32[]{:S(2)}) collective-permute-start(bf16[512,128]{1,0:T(8,128)(2,1)S(1)} %get-tuple-element.57), channel_id=1, source_target_pairs={{0,5},{1,2},{2,7},{3,0},{4,1},{5,6},{6,3},{7,4},{8,13},{9,10},{10,... | collective-permute-start | bytes 393224 | tf_op jit(solution)/shard_map/ppermute | solution.py:413
  9.4 1.2 %shard_map.103.refs_4_.queries = bf16[256,2048]{1,0:T(8,128)(2,1)S(1)} custom-call(bf16[256,2048]{1,0:T(8,128)(2,1)} %bitcast.19, bf16[512,128]{1,0:T(8,128)(2,1)S(1)} %get-tuple-element.49._.refs_0_), custom_call_target="tpu_custom_call" | custom-call | bytes 2097152 | tf_op jit(solution)/shard_map/pallas_call | solution.py:391
  10.6 0.0 collective-permute-done.2.refs_3_
  10.6 0.7 %collective-permute-start.3 = (bf16[512,128]{1,0:T(8,128)(2,1)S(1)}, bf16[512,128]{1,0:T(8,128)(2,1)S(1)}, u32[]{:S(2)}, u32[]{:S(2)}) collective-permute-start(bf16[512,128]{1,0:T(8,128)(2,1)S(1)} %get-tuple-element.57), channel_id=1, source_target_pairs={{0,1},{1,0},{2,3},{3,2},{4,5},{5,4},{6,7},{7,6},{8,9},{9,8},{10,11... | collective-permute-start | bytes 393224 | tf_op jit(solution)/shard_map/ppermute | solution.py:413
  11.4 0.0 collective-permute-done.1.refs_2_
  11.4 0.0 collective-permute-done.refs_1_
  11.4 0.3 shard_map.105
  11.7 0.7 %collective-permute-start.9 = (bf16[512,128]{1,0:T(8,128)(2,1)S(1)}, bf16[512,128]{1,0:T(8,128)(2,1)S(1)}, u32[]{:S(2)}, u32[]{:S(2)}) collective-permute-start(bf16[512,128]{1,0:T(8,128)(2,1)S(1)} %get-tuple-element.62), channel_id=1, source_target_pairs={{0,4},{1,3},{2,6},{3,1},{4,0},{5,7},{6,2},{7,5},{8,12},{9,11},{10,... | collective-permute-start | bytes 393224 | tf_op jit(solution)/shard_map/ppermute | solution.py:413
  12.4 0.8 %collective-permute-start.10 = (bf16[512,128]{1,0:T(8,128)(2,1)S(1)}, bf16[512,128]{1,0:T(8,128)(2,1)S(1)}, u32[]{:S(2)}, u32[]{:S(2)}) collective-permute-start(bf16[512,128]{1,0:T(8,128)(2,1)S(1)} %get-tuple-element.63), channel_id=1, source_target_pairs={{0,5},{1,2},{2,7},{3,0},{4,1},{5,6},{6,3},{7,4},{8,13},{9,10},{10,... | collective-permute-start | bytes 393224 | tf_op jit(solution)/shard_map/ppermute | solution.py:413
  13.3 1.0 %collective-permute-done.4.refs_2_ = bf16[512,128]{1,0:T(8,128)(2,1)S(1)} collective-permute-done((bf16[512,128]{1,0:T(8,128)(2,1)S(1)}, bf16[512,128]{1,0:T(8,128)(2,1)S(1)}, u32[]{:S(2)}, u32[]{:S(2)}) %collective-permute-start.4) | collective-permute-done | bytes 131104 | tf_op jit(solution)/shard_map/ppermute | solution.py:413
  14.3 0.0 collective-permute-start.11
  14.3 0.0 collective-permute-done.5.refs_3_
  14.3 0.0 collective-permute-done.3.refs_1_
  14.3 0.3 shard_map.107
  14.6 0.6 %collective-permute-start.6 = (bf16[512,128]{1,0:T(8,128)(2,1)S(1)}, bf16[512,128]{1,0:T(8,128)(2,1)S(1)}, u32[]{:S(2)}, u32[]{:S(2)}) collective-permute-start(bf16[512,128]{1,0:T(8,128)(2,1)S(1)} %get-tuple-element.58), channel_id=1, source_target_pairs={{0,4},{1,3},{2,6},{3,1},{4,0},{5,7},{6,2},{7,5},{8,12},{9,11},{10,... | collective-permute-start | bytes 393224 | tf_op jit(solution)/shard_map/ppermute | solution.py:413
  15.1 1.2 %collective-permute-start.7 = (bf16[512,128]{1,0:T(8,128)(2,1)S(1)}, bf16[512,128]{1,0:T(8,128)(2,1)S(1)}, u32[]{:S(2)}, u32[]{:S(2)}) collective-permute-start(bf16[512,128]{1,0:T(8,128)(2,1)S(1)} %get-tuple-element.60), channel_id=1, source_target_pairs={{0,5},{1,2},{2,7},{3,0},{4,1},{5,6},{6,3},{7,4},{8,13},{9,10},{10,... | collective-permute-start | bytes 393224 | tf_op jit(solution)/shard_map/ppermute | solution.py:413
  16.4 0.3 collective-permute-done.9.rest_0_
  16.7 0.0 collective-permute-start.8
  16.7 1.5 %shard_map.106.local = f32[256,2048]{1,0:T(8,128)S(1)} custom-call(s32[1,256]{1,0:T(1,128)S(1)} %get-tuple-element.48.length, bf16[256,2048]{1,0:T(8,128)(2,1)S(1)} %shard_map.103.refs_4_.queries, bf16[256,2048]{1,0:T(8,128)(2,1)S(1)} %get-tuple-element.50.keys, bf16[256,2048]{1,0:T(8,128)(2,1)S(1)} %get-tuple-element.51.values, ...), custom_call_target="tpu_custom_call" | custom-call | flops 536870912 | bytes 5243904 | tf_op jit(solution)/shard_map/pallas_call | solution.py:391
  18.2 0.0 collective-permute-done.10.rest_2_
  18.2 0.0 collective-permute-done.11.rest_3_
  18.3 0.6 %shard_map.108 = (f32[256,2048]{1,0:T(8,128)S(1)}, f32[2,256]{1,0:T(2,128)S(1)}, bf16[1024,128]{1,0:T(8,128)(2,1)S(1)}) custom-call(s32[1,256]{1,0:T(1,128)S(1)} %get-tuple-element.48.length, bf16[256,2048]{1,0:T(8,128)(2,1)S(1)} %shard_map.103.refs_4_.queries, f32[256,2048]{1,0:T(8,128)S(1)} %shard_map.106.local, bf16[256,2048]{1,0:T(8,128)(2,1)S(1)} %bitcast.10, ...), custom_call_target="tpu_custom_call" | custom-call | flops 67108864 | bytes 7089152 | tf_op jit(solution)/shard_map/pallas_call | solution.py:391
  18.9 0.7 %collective-permute-done.6.rest_0_ = bf16[512,128]{1,0:T(8,128)(2,1)S(1)} collective-permute-done((bf16[512,128]{1,0:T(8,128)(2,1)S(1)}, bf16[512,128]{1,0:T(8,128)(2,1)S(1)}, u32[]{:S(2)}, u32[]{:S(2)}) %collective-permute-start.6) | collective-permute-done | bytes 131104 | tf_op jit(solution)/shard_map/ppermute | solution.py:413
  19.6 0.9 %collective-permute-done.7.rest_2_ = bf16[512,128]{1,0:T(8,128)(2,1)S(1)} collective-permute-done((bf16[512,128]{1,0:T(8,128)(2,1)S(1)}, bf16[512,128]{1,0:T(8,128)(2,1)S(1)}, u32[]{:S(2)}, u32[]{:S(2)}) %collective-permute-start.7) | collective-permute-done | bytes 131104 | tf_op jit(solution)/shard_map/ppermute | solution.py:413
  20.5 0.0 collective-permute-done.8.rest_3_
  20.5 0.6 %shard_map.109 = (f32[256,2048]{1,0:T(8,128)S(1)}, f32[2,256]{1,0:T(2,128)S(1)}, bf16[1024,128]{1,0:T(8,128)(2,1)S(1)}) custom-call(s32[1,256]{1,0:T(1,128)S(1)} %get-tuple-element.48.length, bf16[256,2048]{1,0:T(8,128)(2,1)S(1)} %shard_map.103.refs_4_.queries, f32[256,2048]{1,0:T(8,128)S(1)} %shard_map.106.local, ...), custom_call_target="tpu_custom_call", output_to_operand_aliasing={{0}: (10, {})} | custom-call | flops 67108864 | bytes 9188352 | tf_op jit(solution)/shard_map/pallas_call | solution.py:391
  21.1 2.7 %collective-permute-start.14 = (f32[2,256]{1,0:T(2,128)S(1)}, f32[2,256]{1,0:T(2,128)S(1)}, u32[]{:S(2)}, u32[]{:S(2)}) collective-permute-start(f32[2,256]{1,0:T(2,128)S(1)} %get-tuple-element.68.rest_0_), channel_id=1, source_target_pairs={{0,16},{8,24},{16,0},{24,8},{1,17},{9,25},{17,1},{25,9},{2,18},{10... | collective-permute-start | bytes 6152 | tf_op jit(solution)/shard_map/ppermute | solution.py:440
  23.8 1.3 %collective-permute-start.13 = (f32[2,256]{1,0:T(2,128)S(1)}, f32[2,256]{1,0:T(2,128)S(1)}, u32[]{:S(2)}, u32[]{:S(2)}) collective-permute-start(f32[2,256]{1,0:T(2,128)S(1)} %get-tuple-element.68.rest_0_), channel_id=1, source_target_pairs={{0,24},{8,16},{16,8},{24,0},{1,25},{9,17},{17,9},{25,1},{2,26},{10... | collective-permute-start | bytes 6152 | tf_op jit(solution)/shard_map/ppermute | solution.py:440
  25.1 0.2 collective-permute-start.12
  25.4 0.3 collective-permute-done.14.rest_3_
  25.7 3.5 %collective-permute-done.13.rest_2_ = f32[2,256]{1,0:T(2,128)S(1)} collective-permute-done((f32[2,256]{1,0:T(2,128)S(1)}, f32[2,256]{1,0:T(2,128)S(1)}, u32[]{:S(2)}, u32[]{:S(2)}) %collective-permute-start.13) | collective-permute-done | bytes 2080 | tf_op jit(solution)/shard_map/ppermute | solution.py:440
  29.2 0.0 collective-permute-done.12.rest_1_
  29.2 1.1 %shard_map.110 = (bf16[256,2048]{1,0:T(8,128)(2,1)S(1)}, f32[1,256]{1,0:T(1,128)S(1)}, bf16[1024,128]{1,0:T(8,128)(2,1)S(1)}, bf16[1024,128]{1,0:T(8,128)(2,1)S(1)}) custom-call(s32[1,256]{1,0:T(1,128)S(1)} %get-tuple-element.48.length, bf16[256,2048]{1,0:T(8,128)(2,1)S(1)} %shard_map.103.refs_4_.queries, bf16[256,2048]{1,0:T(8,128)(2,1)S(1)} %bitcast.12, ...), custom_call_target="tpu_custom_call" | custom-call | flops 134217728 | bytes 5785600 | tf_op jit(solution)/shard_map/pallas_call | solution.py:391
  30.3 0.2 collective-permute-start.17
  30.5 0.6 %collective-permute-start.16 = (bf16[1024,128]{1,0:T(8,128)(2,1)S(1)}, bf16[1024,128]{1,0:T(8,128)(2,1)S(1)}, u32[]{:S(2)}, u32[]{:S(2)}) collective-permute-start(bf16[1024,128]{1,0:T(8,128)(2,1)S(1)} %get-tuple-element.79.refs_0_), channel_id=1, source_target_pairs={{0,2},{1,5},{2,0},{3,7},{4,6},{5,1},{6,4},{7,3},{8,10},{9,13},{10,... | collective-permute-start | bytes 786440 | tf_op jit(solution)/shard_map/ppermute | solution.py:413
  31.1 4.8 %shard_map.111 = (bf16[256,2048]{1,0:T(8,128)(2,1)}, bf16[256,2048]{1,0:T(8,128)(2,1)}, f32[256,2048]{1,0:T(8,128)S(1)}, bf16[1024,128]{1,0:T(8,128)(2,1)S(1)}) custom-call(s32[1,256]{1,0:T(1,128)S(1)} %get-tuple-element.48.length, f32[1,256]{1,0:T(1,128)S(1)} %get-tuple-element.69.inverse_rms, f32[1,2048]{1,0:T(1,128)S(1)} %bitcast.16, ...), custom_call_target="tpu_custom_call" | custom-call | flops 939524096 | bytes 11544576 | tf_op jit(solution)/shard_map/pallas_call | solution.py:391
  35.9 1.2 %collective-permute-start.15 = (bf16[1024,128]{1,0:T(8,128)(2,1)S(1)}, bf16[1024,128]{1,0:T(8,128)(2,1)S(1)}, u32[]{:S(2)}, u32[]{:S(2)}) collective-permute-start(bf16[1024,128]{1,0:T(8,128)(2,1)S(1)} %get-tuple-element.77.rest_0_), channel_id=1, source_target_pairs={{0,1},{1,0},{2,3},{3,2},{4,5},{5,4},{6,7},{7,6},{8,9},{9,8},{10,11... | collective-permute-start | bytes 786440 | tf_op jit(solution)/shard_map/ppermute | solution.py:413
  37.1 0.9 %shard_map.112.refs_4_.rest_0_ = f32[256,1024]{1,0:T(8,128)S(1)} custom-call(s32[1,256]{1,0:T(1,128)S(1)} %get-tuple-element.48.length, bf16[256,2048]{1,0:T(8,128)(2,1)S(1)} %shard_map.103.refs_4_.queries, bf16[256,2048]{1,0:T(8,128)(2,1)S(1)} %get-tuple-element.50.keys, bf16[256,2048]{1,0:T(8,128)(2,1)S(1)} %get-tuple-element.70.grads, ...), custom_call_target="tpu_custom_call" | custom-call | flops 268435456 | bytes 4195328 | tf_op jit(solution)/shard_map/pallas_call | solution.py:391
  38.1 0.4 collective-permute-done.17.refs_3_
  38.5 0.6 %collective-permute-done.16.refs_2_ = bf16[1024,128]{1,0:T(8,128)(2,1)S(1)} collective-permute-done((bf16[1024,128]{1,0:T(8,128)(2,1)S(1)}, bf16[1024,128]{1,0:T(8,128)(2,1)S(1)}, u32[]{:S(2)}, u32[]{:S(2)}) %collective-permute-start.16) | collective-permute-done | bytes 262176 | tf_op jit(solution)/shard_map/ppermute | solution.py:413
  39.1 0.0 collective-permute-done.15.refs_1_
  39.1 0.4 shard_map.113
  39.5 0.6 %collective-permute-start.21 = (bf16[640,128]{1,0:T(8,128)(2,1)S(1)}, bf16[640,128]{1,0:T(8,128)(2,1)S(1)}, u32[]{:S(2)}, u32[]{:S(2)}) collective-permute-start(bf16[640,128]{1,0:T(8,128)(2,1)S(1)} %get-tuple-element.85), channel_id=1, source_target_pairs={{0,4},{1,3},{2,6},{3,1},{4,0},{5,7},{6,2},{7,5},{8,12},{9,11},{10,... | collective-permute-start | bytes 491528 | tf_op jit(solution)/shard_map/ppermute | solution.py:413
  40.1 0.5 collective-permute-start.22
  40.5 1.0 %collective-permute-start.23 = (bf16[640,128]{1,0:T(8,128)(2,1)S(1)}, bf16[640,128]{1,0:T(8,128)(2,1)S(1)}, u32[]{:S(2)}, u32[]{:S(2)}) collective-permute-start(bf16[640,128]{1,0:T(8,128)(2,1)S(1)} %get-tuple-element.87), channel_id=1, source_target_pairs={{0,1},{1,0},{2,3},{3,2},{4,5},{5,4},{6,7},{7,6},{8,9},{9,8},{10,11... | collective-permute-start | bytes 491528 | tf_op jit(solution)/shard_map/ppermute | solution.py:413
  41.6 0.2 shard_map.114
  41.8 0.7 %collective-permute-start.18 = (bf16[384,128]{1,0:T(8,128)(2,1)S(1)}, bf16[384,128]{1,0:T(8,128)(2,1)S(1)}, u32[]{:S(2)}, u32[]{:S(2)}) collective-permute-start(bf16[384,128]{1,0:T(8,128)(2,1)S(1)} %get-tuple-element.82), channel_id=1, source_target_pairs={{0,4},{1,3},{2,6},{3,1},{4,0},{5,7},{6,2},{7,5},{8,12},{9,11},{10,... | collective-permute-start | bytes 294920 | tf_op jit(solution)/shard_map/ppermute | solution.py:413
  42.5 0.8 %collective-permute-start.19 = (bf16[384,128]{1,0:T(8,128)(2,1)S(1)}, bf16[384,128]{1,0:T(8,128)(2,1)S(1)}, u32[]{:S(2)}, u32[]{:S(2)}) collective-permute-start(bf16[384,128]{1,0:T(8,128)(2,1)S(1)} %get-tuple-element.83), channel_id=1, source_target_pairs={{0,5},{1,2},{2,7},{3,0},{4,1},{5,6},{6,3},{7,4},{8,13},{9,10},{10,... | collective-permute-start | bytes 294920 | tf_op jit(solution)/shard_map/ppermute | solution.py:413
  43.3 1.5 %collective-permute-done.21.rest_2_ = bf16[640,128]{1,0:T(8,128)(2,1)S(1)} collective-permute-done((bf16[640,128]{1,0:T(8,128)(2,1)S(1)}, bf16[640,128]{1,0:T(8,128)(2,1)S(1)}, u32[]{:S(2)}, u32[]{:S(2)}) %collective-permute-start.21) | collective-permute-done | bytes 163872 | tf_op jit(solution)/shard_map/ppermute | solution.py:413
  44.9 0.0 collective-permute-start.20
  44.9 0.9 %shard_map.115.rest_1_ = f32[256,1024]{1,0:T(8,128)S(1)} custom-call(s32[1,256]{1,0:T(1,128)S(1)} %get-tuple-element.48.length, bf16[256,2048]{1,0:T(8,128)(2,1)S(1)} %shard_map.103.refs_4_.queries, bf16[256,2048]{1,0:T(8,128)(2,1)S(1)} %get-tuple-element.50.keys, bf16[256,2048]{1,0:T(8,128)(2,1)S(1)} %get-tuple-element.70.grads, ...), custom_call_target="tpu_custom_call" | custom-call | flops 268435456 | bytes 4195328 | tf_op jit(solution)/shard_map/pallas_call | solution.py:391
  45.8 0.0 collective-permute-done.22.rest_4_
  45.8 0.0 collective-permute-done.23.rest_5_
  45.8 1.7 %shard_map.116 = (bf16[256,2048]{1,0:T(8,128)(2,1)}, bf16[256,2048]{1,0:T(8,128)(2,1)}) custom-call(s32[1,256]{1,0:T(1,128)S(1)} %get-tuple-element.48.length, bf16[256,2048]{1,0:T(8,128)(2,1)S(1)} %get-tuple-element.50.keys, bf16[256,2048]{1,0:T(8,128)(2,1)S(1)} %get-tuple-element.51.values, f32[256,2048]{1,0:T(8,128)S(1)} %get-tuple-element.76.key_part, ...), custom_call_target="tpu_custom_call" | custom-call | flops 167772160 | bytes 9044992 | tf_op jit(solution)/shard_map/pallas_call | solution.py:391
  47.5 0.2 collective-permute-done.18.rest_2_
  47.7 0.0 collective-permute-done.19.rest_4_
  47.7 0.0 collective-permute-done.20.rest_5_
  47.7 1.4 %shard_map.117 = (bf16[256,2048]{1,0:T(8,128)(2,1)}, bf16[256,2048]{1,0:T(8,128)(2,1)}) custom-call(s32[1,256]{1,0:T(1,128)S(1)} %get-tuple-element.48.length, bf16[256,2048]{1,0:T(8,128)(2,1)S(1)} %get-tuple-element.50.keys, bf16[256,2048]{1,0:T(8,128)(2,1)S(1)} %get-tuple-element.51.values, ...), custom_call_target="tpu_custom_call", output_to_operand_aliasing={{0}: (10, {}), {1}: (11, {})} | custom-call | flops 100663296 | bytes 10880000 | tf_op jit(solution)/shard_map/pallas_call | solution.py:391
  (4 shorter events, 0.0 us)
Async XLA Ops:
  3.1 7.5 %collective-permute-start.2 = (bf16[512,128]{1,0:T(8,128)(2,1)S(1)}, bf16[512,128]{1,0:T(8,128)(2,1)S(1)}, u32[]{:S(2)}, u32[]{:S(2)}) collective-permute-start(bf16[512,128]{1,0:T(8,128)(2,1)S(1)} %get-tuple-element.53.block), channel_id=1, source_target_pairs={{0,5},{1,2},{2,7},{3,0},{4,1},{5,6},{6,3},{7,4},{8,13},{9,10},{10,... | collective-permute-start | bytes 393224 | tf_op jit(solution)/shard_map/ppermute | solution.py:413
  5.6 5.8 %collective-permute-start.1 = (bf16[512,128]{1,0:T(8,128)(2,1)S(1)}, bf16[512,128]{1,0:T(8,128)(2,1)S(1)}, u32[]{:S(2)}, u32[]{:S(2)}) collective-permute-start(bf16[512,128]{1,0:T(8,128)(2,1)S(1)} %get-tuple-element.49._.refs_0_), channel_id=1, source_target_pairs={{0,2},{1,5},{2,0},{3,7},{4,6},{5,1},{6,4},{7,3},{8,10},{9,13},{10,... | collective-permute-start | bytes 393224 | tf_op jit(solution)/shard_map/ppermute | solution.py:413
  7.5 3.9 %collective-permute-start = (bf16[512,128]{1,0:T(8,128)(2,1)S(1)}, bf16[512,128]{1,0:T(8,128)(2,1)S(1)}, u32[]{:S(2)}, u32[]{:S(2)}) collective-permute-start(bf16[512,128]{1,0:T(8,128)(2,1)S(1)} %get-tuple-element.54), channel_id=1, source_target_pairs={{0,1},{1,0},{2,3},{3,2},{4,5},{5,4},{6,7},{7,6},{8,9},{9,8},{10,11... | collective-permute-start | bytes 393224 | tf_op jit(solution)/shard_map/ppermute | solution.py:413
  7.9 6.3 %collective-permute-start.4 = (bf16[512,128]{1,0:T(8,128)(2,1)S(1)}, bf16[512,128]{1,0:T(8,128)(2,1)S(1)}, u32[]{:S(2)}, u32[]{:S(2)}) collective-permute-start(bf16[512,128]{1,0:T(8,128)(2,1)S(1)} %get-tuple-element.56.refs_0_), channel_id=1, source_target_pairs={{0,2},{1,5},{2,0},{3,7},{4,6},{5,1},{6,4},{7,3},{8,10},{9,13},{10,... | collective-permute-start | bytes 393224 | tf_op jit(solution)/shard_map/ppermute | solution.py:413
  8.5 5.8 %collective-permute-start.5 = (bf16[512,128]{1,0:T(8,128)(2,1)S(1)}, bf16[512,128]{1,0:T(8,128)(2,1)S(1)}, u32[]{:S(2)}, u32[]{:S(2)}) collective-permute-start(bf16[512,128]{1,0:T(8,128)(2,1)S(1)} %get-tuple-element.57), channel_id=1, source_target_pairs={{0,5},{1,2},{2,7},{3,0},{4,1},{5,6},{6,3},{7,4},{8,13},{9,10},{10,... | collective-permute-start | bytes 393224 | tf_op jit(solution)/shard_map/ppermute | solution.py:413
  10.6 3.6 %collective-permute-start.3 = (bf16[512,128]{1,0:T(8,128)(2,1)S(1)}, bf16[512,128]{1,0:T(8,128)(2,1)S(1)}, u32[]{:S(2)}, u32[]{:S(2)}) collective-permute-start(bf16[512,128]{1,0:T(8,128)(2,1)S(1)} %get-tuple-element.57), channel_id=1, source_target_pairs={{0,1},{1,0},{2,3},{3,2},{4,5},{5,4},{6,7},{7,6},{8,9},{9,8},{10,11... | collective-permute-start | bytes 393224 | tf_op jit(solution)/shard_map/ppermute | solution.py:413
  11.7 5.0 %collective-permute-start.9 = (bf16[512,128]{1,0:T(8,128)(2,1)S(1)}, bf16[512,128]{1,0:T(8,128)(2,1)S(1)}, u32[]{:S(2)}, u32[]{:S(2)}) collective-permute-start(bf16[512,128]{1,0:T(8,128)(2,1)S(1)} %get-tuple-element.62), channel_id=1, source_target_pairs={{0,4},{1,3},{2,6},{3,1},{4,0},{5,7},{6,2},{7,5},{8,12},{9,11},{10,... | collective-permute-start | bytes 393224 | tf_op jit(solution)/shard_map/ppermute | solution.py:413
  12.4 5.8 %collective-permute-start.10 = (bf16[512,128]{1,0:T(8,128)(2,1)S(1)}, bf16[512,128]{1,0:T(8,128)(2,1)S(1)}, u32[]{:S(2)}, u32[]{:S(2)}) collective-permute-start(bf16[512,128]{1,0:T(8,128)(2,1)S(1)} %get-tuple-element.63), channel_id=1, source_target_pairs={{0,5},{1,2},{2,7},{3,0},{4,1},{5,6},{6,3},{7,4},{8,13},{9,10},{10,... | collective-permute-start | bytes 393224 | tf_op jit(solution)/shard_map/ppermute | solution.py:413
  14.3 4.0 %collective-permute-start.11 = (bf16[512,128]{1,0:T(8,128)(2,1)S(1)}, bf16[512,128]{1,0:T(8,128)(2,1)S(1)}, u32[]{:S(2)}, u32[]{:S(2)}) collective-permute-start(bf16[512,128]{1,0:T(8,128)(2,1)S(1)} %get-tuple-element.64), channel_id=1, source_target_pairs={{0,1},{1,0},{2,3},{3,2},{4,5},{5,4},{6,7},{7,6},{8,9},{9,8},{10,11... | collective-permute-start | bytes 393224 | tf_op jit(solution)/shard_map/ppermute | solution.py:413
  14.6 5.0 %collective-permute-start.6 = (bf16[512,128]{1,0:T(8,128)(2,1)S(1)}, bf16[512,128]{1,0:T(8,128)(2,1)S(1)}, u32[]{:S(2)}, u32[]{:S(2)}) collective-permute-start(bf16[512,128]{1,0:T(8,128)(2,1)S(1)} %get-tuple-element.58), channel_id=1, source_target_pairs={{0,4},{1,3},{2,6},{3,1},{4,0},{5,7},{6,2},{7,5},{8,12},{9,11},{10,... | collective-permute-start | bytes 393224 | tf_op jit(solution)/shard_map/ppermute | solution.py:413
  15.1 5.4 %collective-permute-start.7 = (bf16[512,128]{1,0:T(8,128)(2,1)S(1)}, bf16[512,128]{1,0:T(8,128)(2,1)S(1)}, u32[]{:S(2)}, u32[]{:S(2)}) collective-permute-start(bf16[512,128]{1,0:T(8,128)(2,1)S(1)} %get-tuple-element.60), channel_id=1, source_target_pairs={{0,5},{1,2},{2,7},{3,0},{4,1},{5,6},{6,3},{7,4},{8,13},{9,10},{10,... | collective-permute-start | bytes 393224 | tf_op jit(solution)/shard_map/ppermute | solution.py:413
  16.7 3.8 %collective-permute-start.8 = (bf16[512,128]{1,0:T(8,128)(2,1)S(1)}, bf16[512,128]{1,0:T(8,128)(2,1)S(1)}, u32[]{:S(2)}, u32[]{:S(2)}) collective-permute-start(bf16[512,128]{1,0:T(8,128)(2,1)S(1)} %get-tuple-element.61), channel_id=1, source_target_pairs={{0,1},{1,0},{2,3},{3,2},{4,5},{5,4},{6,7},{7,6},{8,9},{9,8},{10,11... | collective-permute-start | bytes 393224 | tf_op jit(solution)/shard_map/ppermute | solution.py:413
  16.7 1.5 %copy-start = (bf16[1,256,2048]{2,1,0:T(8,128)(2,1)S(1)}, bf16[1,256,2048]{2,1,0:T(8,128)(2,1)}, u32[]{:S(2)}) copy-start(bf16[1,256,2048]{2,1,0:T(8,128)(2,1)} %param.10) | copy-start | bytes 3145732
  16.7 1.5 %copy-start.1 = (f32[2048]{0:T(1024)S(1)}, f32[2048]{0:T(1024)}, u32[]{:S(2)}) copy-start(f32[2048]{0:T(1024)} %param.11) | copy-start | bytes 24580
  21.1 4.5 %collective-permute-start.14 = (f32[2,256]{1,0:T(2,128)S(1)}, f32[2,256]{1,0:T(2,128)S(1)}, u32[]{:S(2)}, u32[]{:S(2)}) collective-permute-start(f32[2,256]{1,0:T(2,128)S(1)} %get-tuple-element.68.rest_0_), channel_id=1, source_target_pairs={{0,16},{8,24},{16,0},{24,8},{1,17},{9,25},{17,1},{25,9},{2,18},{10... | collective-permute-start | bytes 6152 | tf_op jit(solution)/shard_map/ppermute | solution.py:440
  23.8 5.4 %collective-permute-start.13 = (f32[2,256]{1,0:T(2,128)S(1)}, f32[2,256]{1,0:T(2,128)S(1)}, u32[]{:S(2)}, u32[]{:S(2)}) collective-permute-start(f32[2,256]{1,0:T(2,128)S(1)} %get-tuple-element.68.rest_0_), channel_id=1, source_target_pairs={{0,24},{8,16},{16,8},{24,0},{1,25},{9,17},{17,9},{25,1},{2,26},{10... | collective-permute-start | bytes 6152 | tf_op jit(solution)/shard_map/ppermute | solution.py:440
  25.1 4.0 %collective-permute-start.12 = (f32[2,256]{1,0:T(2,128)S(1)}, f32[2,256]{1,0:T(2,128)S(1)}, u32[]{:S(2)}, u32[]{:S(2)}) collective-permute-start(f32[2,256]{1,0:T(2,128)S(1)} %get-tuple-element.68.rest_0_), channel_id=1, source_target_pairs={{0,8},{8,0},{16,24},{24,16},{1,9},{9,1},{17,25},{25,17},{2,10},{10... | collective-permute-start | bytes 6152 | tf_op jit(solution)/shard_map/ppermute | solution.py:440
  30.3 8.2 %collective-permute-start.17 = (bf16[1024,128]{1,0:T(8,128)(2,1)S(1)}, bf16[1024,128]{1,0:T(8,128)(2,1)S(1)}, u32[]{:S(2)}, u32[]{:S(2)}) collective-permute-start(bf16[1024,128]{1,0:T(8,128)(2,1)S(1)} %get-tuple-element.71.block), channel_id=1, source_target_pairs={{0,5},{1,2},{2,7},{3,0},{4,1},{5,6},{6,3},{7,4},{8,13},{9,10},{10,... | collective-permute-start | bytes 786440 | tf_op jit(solution)/shard_map/ppermute | solution.py:413
  30.5 8.6 %collective-permute-start.16 = (bf16[1024,128]{1,0:T(8,128)(2,1)S(1)}, bf16[1024,128]{1,0:T(8,128)(2,1)S(1)}, u32[]{:S(2)}, u32[]{:S(2)}) collective-permute-start(bf16[1024,128]{1,0:T(8,128)(2,1)S(1)} %get-tuple-element.79.refs_0_), channel_id=1, source_target_pairs={{0,2},{1,5},{2,0},{3,7},{4,6},{5,1},{6,4},{7,3},{8,10},{9,13},{10,... | collective-permute-start | bytes 786440 | tf_op jit(solution)/shard_map/ppermute | solution.py:413
  35.9 3.2 %collective-permute-start.15 = (bf16[1024,128]{1,0:T(8,128)(2,1)S(1)}, bf16[1024,128]{1,0:T(8,128)(2,1)S(1)}, u32[]{:S(2)}, u32[]{:S(2)}) collective-permute-start(bf16[1024,128]{1,0:T(8,128)(2,1)S(1)} %get-tuple-element.77.rest_0_), channel_id=1, source_target_pairs={{0,1},{1,0},{2,3},{3,2},{4,5},{5,4},{6,7},{7,6},{8,9},{9,8},{10,11... | collective-permute-start | bytes 786440 | tf_op jit(solution)/shard_map/ppermute | solution.py:413
  39.5 5.4 %collective-permute-start.21 = (bf16[640,128]{1,0:T(8,128)(2,1)S(1)}, bf16[640,128]{1,0:T(8,128)(2,1)S(1)}, u32[]{:S(2)}, u32[]{:S(2)}) collective-permute-start(bf16[640,128]{1,0:T(8,128)(2,1)S(1)} %get-tuple-element.85), channel_id=1, source_target_pairs={{0,4},{1,3},{2,6},{3,1},{4,0},{5,7},{6,2},{7,5},{8,12},{9,11},{10,... | collective-permute-start | bytes 491528 | tf_op jit(solution)/shard_map/ppermute | solution.py:413
  40.1 5.7 %collective-permute-start.22 = (bf16[640,128]{1,0:T(8,128)(2,1)S(1)}, bf16[640,128]{1,0:T(8,128)(2,1)S(1)}, u32[]{:S(2)}, u32[]{:S(2)}) collective-permute-start(bf16[640,128]{1,0:T(8,128)(2,1)S(1)} %get-tuple-element.86), channel_id=1, source_target_pairs={{0,5},{1,2},{2,7},{3,0},{4,1},{5,6},{6,3},{7,4},{8,13},{9,10},{10,... | collective-permute-start | bytes 491528 | tf_op jit(solution)/shard_map/ppermute | solution.py:413
  40.5 5.3 %collective-permute-start.23 = (bf16[640,128]{1,0:T(8,128)(2,1)S(1)}, bf16[640,128]{1,0:T(8,128)(2,1)S(1)}, u32[]{:S(2)}, u32[]{:S(2)}) collective-permute-start(bf16[640,128]{1,0:T(8,128)(2,1)S(1)} %get-tuple-element.87), channel_id=1, source_target_pairs={{0,1},{1,0},{2,3},{3,2},{4,5},{5,4},{6,7},{7,6},{8,9},{9,8},{10,11... | collective-permute-start | bytes 491528 | tf_op jit(solution)/shard_map/ppermute | solution.py:413
  41.8 5.9 %collective-permute-start.18 = (bf16[384,128]{1,0:T(8,128)(2,1)S(1)}, bf16[384,128]{1,0:T(8,128)(2,1)S(1)}, u32[]{:S(2)}, u32[]{:S(2)}) collective-permute-start(bf16[384,128]{1,0:T(8,128)(2,1)S(1)} %get-tuple-element.82), channel_id=1, source_target_pairs={{0,4},{1,3},{2,6},{3,1},{4,0},{5,7},{6,2},{7,5},{8,12},{9,11},{10,... | collective-permute-start | bytes 294920 | tf_op jit(solution)/shard_map/ppermute | solution.py:413
  42.5 5.2 %collective-permute-start.19 = (bf16[384,128]{1,0:T(8,128)(2,1)S(1)}, bf16[384,128]{1,0:T(8,128)(2,1)S(1)}, u32[]{:S(2)}, u32[]{:S(2)}) collective-permute-start(bf16[384,128]{1,0:T(8,128)(2,1)S(1)} %get-tuple-element.83), channel_id=1, source_target_pairs={{0,5},{1,2},{2,7},{3,0},{4,1},{5,6},{6,3},{7,4},{8,13},{9,10},{10,... | collective-permute-start | bytes 294920 | tf_op jit(solution)/shard_map/ppermute | solution.py:413
  44.9 2.8 %collective-permute-start.20 = (bf16[384,128]{1,0:T(8,128)(2,1)S(1)}, bf16[384,128]{1,0:T(8,128)(2,1)S(1)}, u32[]{:S(2)}, u32[]{:S(2)}) collective-permute-start(bf16[384,128]{1,0:T(8,128)(2,1)S(1)} %get-tuple-element.84), channel_id=1, source_target_pairs={{0,1},{1,0},{2,3},{3,2},{4,5},{5,4},{6,7},{7,6},{8,9},{9,8},{10,11... | collective-permute-start | bytes 294920 | tf_op jit(solution)/shard_map/ppermute | solution.py:413
